TPU v7x, 32 devices: a whole 2x2x4 slice. The times are simulated.
32 devices in a mesh: grp: 2 (over y), seg: 8 (over z, x), tp: 2 (over core).
Axes of the slice: x: 2, y: 2, z: 4, core: 2. Of those that a mesh axis runs over, the one named last changes fastest.
Arguments:
- queries: bfloat16 [2048, 5120], P(('grp', 'seg'), 'tp'), parts along dimension 0, may hold values from -42 to 42
- key_vectors: bfloat16 [2048, 1024], P(('grp', 'seg'), 'tp'), parts along dimension 0, may hold values from -4.5 to 4.5
- value_vectors: bfloat16 [2048, 1024], P(('grp', 'seg'), 'tp'), parts along dimension 0, may hold values from -5 to 5
- direction: bfloat16 [2048, 5120], P(('grp', 'seg'), 'tp'), parts along dimension 0, may hold values from -5 to 5
- rewards: float32 [2048], P(('grp', 'seg')), parts along dimension 0, may hold values from -4 to 4
- logprobs: float32 [2048], P(('grp', 'seg')), parts along dimension 0, may hold values from -6 to -0.05
- ref_logprobs: float32 [2048], P(('grp', 'seg')), parts along dimension 0, may hold values from -6 to -0.05
- value_est: float32 [2048], P(('grp', 'seg')), parts along dimension 0, may hold values from -4 to 4
- parents: int32 [16], P('grp'), parts along dimension 0, may hold values from -1 to 4, as said below
- seg_lengths: int32 [16], P('grp'), parts along dimension 0, may hold values from 1 to 128, 768 in all
Outputs:
- grad_queries: bfloat16 [2048, 5120], P(('grp', 'seg'), 'tp'), parts along dimension 0
- grad_keys: bfloat16 [2048, 1024], P(('grp', 'seg'), 'tp'), parts along dimension 0
- grad_values: bfloat16 [2048, 1024], P(('grp', 'seg'), 'tp'), parts along dimension 0
- advantages: float32 [2048], P(('grp', 'seg')), parts along dimension 0
There are 2 independent parts, one for each index of `grp`. A program takes and returns all parts, laid end to end along the dimension named above; each array names one. Nothing has to cross between parts.
Inputs may be any that keep to these rules, and one draw needn't show every extreme that they name: `parents`: segment 0 has parent -1 and every other segment's parent is an earlier segment; segment 0 is the root (the shared prompt segment) and an ancestor of every later segment; no segment has more than 4 ancestors, and some have exactly 4.
All inputs are finite; a program needn't handle non-finite values.
Results may differ from a plain program's by a relative error of at most 0.0091.
Values may be sent and summed in bfloat16 or wider, within the bound.
No kernel may reach another device: no remote copies, remote signals or barrier semaphores. Data moves between devices by JAX's collectives and lax.ppermute only.
A program may use at most 64 MiB of HBM per device.

v0:
```python
import math

import jax
import jax.numpy as jnp
from jax import lax
from jax.sharding import PartitionSpec as P

HD = 128
DEPTH = 5


BETA = 0.1
LAMBDA_SEG = 0.7


def lookup(table_values, lookup_ids):
    matches = lookup_ids[..., None] == jnp.arange(table_values.shape[0], dtype=jnp.int32)
    return jnp.sum(jnp.where(matches, table_values, 0), axis=-1)


def ancestors(parents, count):
    current = jnp.arange(parents.shape[0], dtype=jnp.int32)
    chain_list = []
    for depth_step in range(count):
        parent_ids = lookup(parents, current)
        current = jnp.where(current >= 0, parent_ids, -1)
        chain_list.append(current)
    return jnp.stack(chain_list, axis=1)


def local_terms(rewards, logprobs, ref_logprobs, value_est, seg_lengths, log_rate):
    length = rewards.shape[1]
    positions = jnp.arange(length, dtype=jnp.int32)
    is_valid = positions[None, :] < seg_lengths[:, None]
    next_value = jnp.concatenate([value_est[:, 1:], jnp.zeros_like(value_est[:, :1])], axis=1)
    next_value = jnp.where(positions[None, :] + 1 < seg_lengths[:, None], next_value, 0.0)
    deltas = jnp.where(
        is_valid, rewards - BETA * (logprobs - ref_logprobs) + next_value - value_est, 0.0
    )
    offset = (positions[None, :] - positions[:, None]).astype(jnp.float32)
    discount = jnp.where(offset >= 0, jnp.exp(offset * log_rate), 0.0)
    local_sum = jnp.dot(deltas, discount.T, precision=lax.Precision.HIGHEST)
    return (local_sum, is_valid)


def tree_solve(first_local, first_value, parents, seg_lengths, log_rate, sweeps):
    children = (parents[None, :] == jnp.arange(parents.shape[0], dtype=jnp.int32)[:, None]).astype(
        jnp.float32
    )
    child_count = jnp.sum(children, axis=1)
    tree_weights = children / jnp.maximum(child_count, 1.0)[:, None]
    later_value = jnp.dot(tree_weights, first_value, precision=lax.Precision.HIGHEST)
    lengths_f = seg_lengths.astype(jnp.float32)
    base_term = first_local + jnp.exp((lengths_f - 1.0) * log_rate) * later_value
    factor = jnp.exp(lengths_f * log_rate)
    head_adv = base_term
    for depth_step in range(sweeps):
        head_adv = base_term + factor * jnp.dot(
            tree_weights, head_adv, precision=lax.Precision.HIGHEST
        )
    later_head = jnp.dot(tree_weights, head_adv, precision=lax.Precision.HIGHEST)
    return (later_value, later_head)


def advantage_rows(local_sum, is_valid, seg_lengths, later_value, later_head, log_rate):
    positions = jnp.arange(local_sum.shape[1], dtype=jnp.float32)
    lengths_f = seg_lengths.astype(jnp.float32)[:, None]
    value_part = jnp.exp((lengths_f - 1.0 - positions[None, :]) * log_rate) * later_value[:, None]
    head_part = jnp.exp((lengths_f - positions[None, :]) * log_rate) * later_head[:, None]
    return jnp.where(is_valid, local_sum + value_part + head_part, 0.0)


def build_mask(slot_ids, seg_lengths, length):
    slot_lengths = lookup(seg_lengths, slot_ids)
    positions = jnp.arange(length, dtype=jnp.int32)
    key_valid = (slot_ids >= 0)[:, :, None] & (positions[None, None, :] < slot_lengths[:, :, None])
    self_slot = (jnp.arange(slot_ids.shape[1]) == 0)[None, None, :, None]
    causal = positions[None, None, None, :] <= positions[None, :, None, None]
    keymask = key_valid[:, None, :, :] & (jnp.logical_not(self_slot) | causal)
    return keymask.reshape(slot_ids.shape[0], length, -1)


def attend_group(q_group, do_group, k_group, v_group, keymask):
    score_scale = q_group.shape[-1] ** (-0.5)
    scores = (
        jnp.einsum("tjd,kd->jtk", q_group, k_group, preferred_element_type=jnp.float32)
        * score_scale
    )
    scores = jnp.where(keymask[None], scores, -1e30)
    row_max = jnp.max(scores, axis=-1, keepdims=True)
    weights = jnp.exp(scores - row_max)
    attn_prob = weights / jnp.sum(weights, axis=-1, keepdims=True)
    prob_low = attn_prob.astype(jnp.bfloat16)
    attn_out = jnp.einsum("jtk,kd->tjd", prob_low, v_group, preferred_element_type=jnp.float32)
    row_dot = jnp.sum(do_group.astype(jnp.float32) * attn_out, axis=-1)
    dprob = jnp.einsum("tjd,kd->jtk", do_group, v_group, preferred_element_type=jnp.float32)
    dscore = (attn_prob * (dprob - jnp.transpose(row_dot)[:, :, None])).astype(jnp.bfloat16)
    grad_q = (
        jnp.einsum("jtk,kd->tjd", dscore, k_group, preferred_element_type=jnp.float32) * score_scale
    ).astype(jnp.bfloat16)
    grad_k = (
        jnp.einsum("jtk,tjd->kd", dscore, q_group, preferred_element_type=jnp.float32) * score_scale
    )
    grad_v = jnp.einsum("jtk,tjd->kd", prob_low, do_group, preferred_element_type=jnp.float32)
    return (grad_q, grad_k, grad_v)


def segment_backward(q_one, do_one, kv_one, mask_one):
    length, kv_heads, group_size, head_dim = q_one.shape
    flat_kv = kv_one.reshape(-1, 2, kv_heads, head_dim)

    def per_group(inputs):
        return attend_group(inputs[0], inputs[1], inputs[2], inputs[3], mask_one)

    grad_q, grad_k, grad_v = lax.map(
        per_group,
        (
            jnp.moveaxis(q_one, 1, 0),
            jnp.moveaxis(do_one, 1, 0),
            jnp.moveaxis(flat_kv[:, 0], 1, 0),
            jnp.moveaxis(flat_kv[:, 1], 1, 0),
        ),
    )
    grad_q = jnp.moveaxis(grad_q, 0, 1).reshape(length, -1)
    grad_kv = jnp.stack([jnp.moveaxis(grad_k, 0, 1), jnp.moveaxis(grad_v, 0, 1)], axis=1)
    return (grad_q, grad_kv.reshape(kv_one.shape[0], length, -1))


def fetch_rows(spread, wanted):
    routed = jnp.take(spread, jnp.maximum(wanted, 0), axis=0)
    return lax.all_to_all(routed, "seg", split_axis=0, concat_axis=2, tiled=True)


def return_rows(grad_rows, wanted, total_segs):
    returned = lax.all_to_all(grad_rows, "seg", split_axis=2, concat_axis=0, tiled=True)
    piece_len = returned.shape[2]
    feature_len = returned.shape[3]
    routed_ids = wanted.reshape(-1)
    targets = jnp.where(routed_ids >= 0, routed_ids, total_segs)
    summed = jax.ops.segment_sum(
        returned.reshape(-1, piece_len * feature_len), targets, num_segments=total_segs + 1
    )[:total_segs]
    return lax.all_to_all(
        summed.reshape(total_segs, piece_len, feature_len),
        "seg",
        split_axis=0,
        concat_axis=1,
        tiled=True,
    )


def body(
    queries,
    key_vectors,
    value_vectors,
    direction,
    rewards,
    logprobs,
    ref_logprobs,
    value_est,
    parents,
    seg_lengths,
):
    total_segs = parents.shape[0]
    groups = lax.axis_size("seg")
    held_segs = total_segs // groups
    length = rewards.shape[0] // held_segs
    first_seg = lax.axis_index("seg") * held_segs
    log_rate = math.log(LAMBDA_SEG) / length
    held_lengths = lax.dynamic_slice_in_dim(seg_lengths, first_seg, held_segs)
    grid = (held_segs, length)
    held_values = value_est.reshape(grid)
    local_sum, is_valid = local_terms(
        rewards.reshape(grid),
        logprobs.reshape(grid),
        ref_logprobs.reshape(grid),
        held_values,
        held_lengths,
        log_rate,
    )
    all_first, all_value = (
        lax.all_gather(local_sum[:, 0], "seg", axis=0, tiled=True),
        lax.all_gather(held_values[:, 0], "seg", axis=0, tiled=True),
    )
    later_value, later_head = tree_solve(
        all_first, all_value, parents, seg_lengths, log_rate, DEPTH
    )
    advantage = advantage_rows(
        local_sum,
        is_valid,
        held_lengths,
        lax.dynamic_slice_in_dim(later_value, first_seg, held_segs),
        lax.dynamic_slice_in_dim(later_head, first_seg, held_segs),
        log_rate,
    )
    kv_width = key_vectors.shape[1]
    kv_heads = kv_width // HD
    group_size = queries.shape[1] // kv_width
    kv_local = jnp.concatenate([key_vectors, value_vectors], axis=1).reshape(
        held_segs, length, 2 * kv_width
    )
    spread = lax.all_to_all(kv_local, "seg", split_axis=1, concat_axis=0, tiled=True)
    chains = ancestors(parents, DEPTH - 1)
    held_ids = first_seg + jnp.arange(held_segs, dtype=jnp.int32)
    lead_ids = held_ids[:, None]
    lead_kv = kv_local[:, None]
    lead_count = lead_ids.shape[1]
    arrived = fetch_rows(spread, chains)
    held_wanted = lax.dynamic_slice_in_dim(chains, first_seg, held_segs)
    slot_ids = jnp.concatenate([lead_ids, held_wanted], axis=1)
    slot_kv = jnp.concatenate([lead_kv, arrived], axis=1)
    keymask = build_mask(slot_ids, seg_lengths, length)
    grad_out = (
        advantage[:, :, None] * direction.reshape(held_segs, length, -1).astype(jnp.float32)
    ).astype(jnp.bfloat16)
    head_shape = (held_segs, length, kv_heads, group_size, HD)

    def per_segment(inputs):
        return segment_backward(inputs[0], inputs[1], inputs[2], inputs[3])

    grad_q, grad_kv = lax.map(
        per_segment, (queries.reshape(head_shape), grad_out.reshape(head_shape), slot_kv, keymask)
    )
    grad_rows = grad_kv[:, lead_count:]
    kv_grads = return_rows(grad_rows, chains, total_segs) + grad_kv[:, 0]
    kv_grads = kv_grads.reshape(held_segs * length, 2 * kv_width)
    grad_keys = kv_grads[:, :kv_width].astype(jnp.bfloat16)
    grad_values = kv_grads[:, kv_width:].astype(jnp.bfloat16)
    return (
        grad_q.reshape(held_segs * length, queries.shape[1]),
        grad_keys,
        grad_values,
        advantage.reshape(held_segs * length),
    )


def solution(mesh):
    in_specs = (
        P(("grp", "seg"), "tp"),
        P(("grp", "seg"), "tp"),
        P(("grp", "seg"), "tp"),
        P(("grp", "seg"), "tp"),
        P(("grp", "seg")),
        P(("grp", "seg")),
        P(("grp", "seg")),
        P(("grp", "seg")),
        P("grp"),
        P("grp"),
    )
    out_specs = (
        P(("grp", "seg"), "tp"),
        P(("grp", "seg"), "tp"),
        P(("grp", "seg"), "tp"),
        P(("grp", "seg")),
    )
    return jax.shard_map(body, mesh=mesh, in_specs=in_specs, out_specs=out_specs, check_vma=False)
```

profile of v0, /device:TPU:0, one launch (start us, length us, event | category | flops | bytes accessed | tf_op | source)
XLA Modules:
  0.0 199.5 jit_solution(5259848497133937567)
XLA Ops:
  0.7 1.0 constant_dynamic-update-slice_fusion.1
  1.7 0.9 constant_dynamic-update-slice_fusion
  3.5 2.1 %reduce.5 = bf16[128,1024]{1,0:T(8,128)(2,1)S(1)} reduce(bf16[128,1,1024]{2,1,0:T(2,128)(2,1)S(1)} %bitcast.338, bf16[]{:T(256)} %broadcast.419), dimensions={1}, to_apply=%bitcast.281.reduce_sub_computation | reduce | bytes 524290
  5.7 0.9 reshape.539
  6.6 7.3 %all-to-all-start = ((bf16[8,2,8192]{2,1,0:T(2,128)(2,1)}), bf16[8,2,8192]{2,1,0:T(2,128)(2,1)S(1)}, u32[]{:S(2)}, u32[]{:S(2)}) async-start(bf16[8,2,8192]{2,1,0:T(2,128)(2,1)} %reshape.539), calls=%async_computation | async-start | bytes 524288 | tf_op jit(solution)/shard_map/all_to_all | solution.py:202
  14.7 0.6 dynamic_slice.38
  15.3 0.6 dynamic-slice
  15.9 0.9 fusion.72
  16.7 0.7 bitcast_dynamic-update-slice_fusion
  17.5 0.7 bitcast_dynamic-update-slice_fusion.1
  18.2 21.8 %all-reduce.2 = (f32[8]{0:T(128)S(1)}, f32[8]{0:T(128)S(1)}) all-reduce(f32[8]{0:T(128)S(1)} %bitcast_dynamic-update-slice_fusion, f32[8]{0:T(128)S(1)} %bitcast_dynamic-update-slice_fusion.1), channel_id=3, replica_groups=mesh['grp'=2,'seg'=8,'tp'=2] {'seg'}, use_global_device_ids=true, to_apply=%add.1 | all-reduce | flops 16 | bytes 128 | tf_op jit(solution)/shard_map/all_gather | solution.py:182
  42.4 0.6 gather_fusion
  43.0 1.1 broadcast_select_fusion
  44.2 3.9 %all-to-all-start.1 = ((bf16[8,4,16,1024]{3,2,1,0:T(8,128)(2,1)}), bf16[8,4,16,1024]{3,2,1,0:T(8,128)(2,1)S(1)}, u32[]{:S(2)}, u32[]{:S(2)}) async-start(bf16[8,4,16,1024]{3,2,1,0:T(8,128)(2,1)} %broadcast_select_fusion), calls=%async_computation.1 | async-start | bytes 2097152 | tf_op jit(solution)/shard_map/all_to_all | solution.py:131
  48.8 0.6 dynamic_slice.39
  49.4 0.6 dynamic_slice.40
  50.1 1.1 copy.132
  51.9 1.9 compare_select_fusion.8
  53.8 0.6 broadcast_bitcast_fusion
  54.5 0.6 fusion.82
  55.2 14.3 %all-to-all-done.1 = bf16[8,4,16,1024]{3,2,1,0:T(8,128)(2,1)S(1)} async-done(((bf16[8,4,16,1024]{3,2,1,0:T(8,128)(2,1)}), bf16[8,4,16,1024]{3,2,1,0:T(8,128)(2,1)S(1)}, u32[]{:S(2)}, u32[]{:S(2)}) %all-to-all-start.1) | async-done | bytes 1048608 | tf_op jit(solution)/shard_map/all_to_all | solution.py:131
  69.8 1.0 reshape.476
  71.3 0.9 copy.137
  72.2 0.9 copy.135
  73.1 33.3 %while.25 = (s32[]{:T(128)}, bf16[4,128,5,128]{1,3,2,0:T(8,128)(2,1)}, f32[4,640,128]{2,1,0:T(8,128)}, f32[4,640,128]{2,1,0:T(8,128)}, bf16[4,640,128]{2,1,0:T(8...) while((s32[]{:T(128)}, ...), condition=%wide.region_10.11_spmd.clone, body=%wide.region_6.10_spmd.clone.sunk | while | flops 633896960 | bytes 15603617 | solution.py:115
  73.6 1.6 exponential_reduce_fusion.2
  75.5 0.9 copy-done.1
  76.3 0.5 fusion.150
  77.3 1.1 fusion.154
  78.4 1.9 fusion.152
  80.3 1.1 fusion.153
  81.9 1.6 exponential_reduce_fusion.2
  83.8 0.9 copy-done.1
  84.6 0.5 fusion.150
  85.6 1.1 fusion.154
  86.8 1.9 fusion.152
  88.7 1.1 fusion.153
  90.2 1.6 exponential_reduce_fusion.2
  92.1 0.9 copy-done.1
  93.0 0.5 fusion.150
  94.0 1.1 fusion.154
  95.1 1.9 fusion.152
  97.0 1.1 fusion.153
  98.5 1.6 exponential_reduce_fusion.2
  100.4 0.9 copy-done.1
  101.3 0.5 fusion.150
  102.3 1.1 fusion.154
  103.4 1.9 fusion.152
  105.3 1.1 fusion.153
  106.4 1.9 pad_maximum_fusion
  108.3 3.2 %copy.140 = f32[640,2,4,128]{3,2,1,0:T(4,128)} copy(f32[640,2,4,128]{3,0,2,1:T(8,128)S(1)} %pad_maximum_fusion) | data formatting | bytes 5242880 | tf_op jit(solution)/shard_map/while/body/eval_jaxpr/stack | solution.py:125
  111.5 2.9 %broadcast_in_dim.134 = f32[1,5,128,1024]{3,2,1,0:T(8,128)S(1)} reshape(f32[640,2,4,128]{3,2,1,0:T(4,128)} %copy.140) | data formatting | bytes 5242880 | tf_op jit(solution)/shard_map/while/body/jit(dynamic_update_index_in_dim)/broadcast_in_dim | solution.py:221
  114.6 2.7 %copy.141 = f32[1,4,128,1024]{3,1,0,2:T(4,128)} copy(f32[1,4,128,1024]{3,2,1,0:T(8,128)S(1)} %slice.48) | data formatting | bytes 4194304 | tf_op jit(solution)/shard_map/slice | solution.py:224
  117.3 4.7 %all-to-all-start.2 = ((f32[1,4,128,1024]{3,1,0,2:T(4,128)}), f32[1,4,128,1024]{3,1,0,2:T(4,128)}, u32[]{:S(2)}, u32[]{:S(2)}) async-start(f32[1,4,128,1024]{3,1,0,2:T(4,128)} %copy.141), calls=%async_computation.2 | async-start | bytes 4194304 | tf_op jit(solution)/shard_map/all_to_all | solution.py:135
  122.1 46.1 %all-to-all-done.2 = f32[1,4,128,1024]{3,1,0,2:T(4,128)} async-done(((f32[1,4,128,1024]{3,1,0,2:T(4,128)}), f32[1,4,128,1024]{3,1,0,2:T(4,128)}, u32[]{:S(2)}, u32[]{:S(2)}) %all-to-all-start.2) | async-done | bytes 2097184 | tf_op jit(solution)/shard_map/all_to_all | solution.py:135
  168.2 2.8 %copy.142 = f32[1,4,8,16,1024]{4,3,1,2,0:T(8,128)S(1)} copy(f32[1,4,8,16,1024]{4,1,3,2,0:T(4,128)} %bitcast.65) | data formatting | bytes 4194304 | tf_op jit(solution)/shard_map/all_to_all | solution.py:135
  171.0 2.6 %copy.154 = f32[4,8,16,1024]{3,1,2,0:T(8,128)} copy(f32[4,8,16,1024]{3,2,1,0:T(8,128)S(1)} %bitcast.328) | data formatting | bytes 4194304
  173.6 4.9 %scatter_custom_fusion = f32[9,16384]{1,0:T(8,128)} fusion(s32[32]{0:T(128)S(1)} %fusion.88, f32[32,16384]{1,0:T(8,128)} %bitcast.336, f32[]{:T(128)} %constant.50.clone.1), kind=kCustom, calls=%fused_computation.85 | custom fusion | flops 524288 | bytes 590336 | tf_op jit(solution)/shard_map/scatter-add | solution.py:140
  178.5 1.1 slice.49
  179.6 1.1 copy.158
  180.7 3.5 %all-to-all-start.3 = ((f32[8,16,1024]{2,1,0:T(8,128)}), f32[8,16,1024]{2,1,0:T(8,128)S(1)}, u32[]{:S(2)}, u32[]{:S(2)}) async-start(f32[8,16,1024]{2,1,0:T(8,128)} %bitcast.337), calls=%async_computation.3 | async-start | bytes 1048576 | tf_op jit(solution)/shard_map/all_to_all | solution.py:143
  184.2 2.2 %copy.143 = bf16[128,2560]{1,0:T(8,128)(2,1)} copy(bf16[128,2560]{0,1:T(8,128)(2,1)} %bitcast.344) | data formatting | bytes 1310720
  186.4 12.4 %all-to-all-done.3 = f32[8,16,1024]{2,1,0:T(8,128)S(1)} async-done(((f32[8,16,1024]{2,1,0:T(8,128)}), f32[8,16,1024]{2,1,0:T(8,128)S(1)}, u32[]{:S(2)}, u32[]{:S(2)}) %all-to-all-start.3) | async-done | bytes 524320 | tf_op jit(solution)/shard_map/all_to_all | solution.py:143
  198.8 0.7 fusion.107
  (105 shorter events, 10.7 us)
Async XLA Ops:
  0.6 14.7 %copy-start.15 = (u32[32]{0:T(128)S(1)}, u32[32]{0:T(128)}, u32[]{:S(2)}) copy-start(u32[32]{0:T(128)} %constant.108) | copy-start | bytes 388
  0.6 13.2 %copy-start.13 = (s32[8]{0:T(128)S(1)}, s32[8]{0:T(128)}, u32[]{:S(2)}) copy-start(s32[8]{0:T(128)} %param.20) | copy-start | bytes 100
  0.7 14.0 %copy-start.12 = (f32[128]{0:T(128)S(1)}, f32[128]{0:T(128)}, u32[]{:S(2)}) copy-start(f32[128]{0:T(128)} %param.19) | copy-start | bytes 1540
  0.7 14.0 %copy-start.14 = (s32[8]{0:T(128)S(1)}, s32[8]{0:T(128)}, u32[]{:S(2)}) copy-start(s32[8]{0:T(128)} %param.21) | copy-start | bytes 100
  0.7 15.2 %copy-start.11 = (f32[128]{0:T(128)S(1)}, f32[128]{0:T(128)}, u32[]{:S(2)}) copy-start(f32[128]{0:T(128)} %param.18) | copy-start | bytes 1540
  0.7 15.2 %copy-start.10 = (f32[128]{0:T(128)S(1)}, f32[128]{0:T(128)}, u32[]{:S(2)}) copy-start(f32[128]{0:T(128)} %param.17) | copy-start | bytes 1540
  0.7 15.2 %copy-start.9 = (f32[128]{0:T(128)S(1)}, f32[128]{0:T(128)}, u32[]{:S(2)}) copy-start(f32[128]{0:T(128)} %param.16) | copy-start | bytes 1540
  6.6 35.5 %all-to-all-start = ((bf16[8,2,8192]{2,1,0:T(2,128)(2,1)}), bf16[8,2,8192]{2,1,0:T(2,128)(2,1)S(1)}, u32[]{:S(2)}, u32[]{:S(2)}) async-start(bf16[8,2,8192]{2,1,0:T(2,128)(2,1)} %reshape.539), calls=%async_computation | async-start | bytes 524288 | tf_op jit(solution)/shard_map/all_to_all | solution.py:202
  40.9 1.5 copy-start.6
  43.0 7.1 %copy-start.2 = (bf16[128,2560]{1,0:T(8,128)(2,1)S(1)}, bf16[128,2560]{1,0:T(8,128)(2,1)}, u32[]{:S(2)}) copy-start(bf16[128,2560]{1,0:T(8,128)(2,1)} %param.12) | copy-start | bytes 1966084
  44.2 7.0 %copy-start.3 = (bf16[128,2560]{1,0:T(8,128)(2,1)S(1)}, bf16[128,2560]{1,0:T(8,128)(2,1)}, u32[]{:S(2)}) copy-start(bf16[128,2560]{1,0:T(8,128)(2,1)} %param.15) | copy-start | bytes 1966084
  44.2 25.4 %all-to-all-start.1 = ((bf16[8,4,16,1024]{3,2,1,0:T(8,128)(2,1)}), bf16[8,4,16,1024]{3,2,1,0:T(8,128)(2,1)S(1)}, u32[]{:S(2)}, u32[]{:S(2)}) async-start(bf16[8,4,16,1024]{3,2,1,0:T(8,128)(2,1)} %broadcast_select_fusion), calls=%async_computation.1 | async-start | bytes 2097152 | tf_op jit(solution)/shard_map/all_to_all | solution.py:131
  53.8 15.9 %copy-start.8 = (f32[128]{0:T(128)}, f32[128]{0:T(128)S(1)}, u32[]{:S(2)}) copy-start(f32[128]{0:T(128)S(1)} %compare_select_fusion.8) | copy-start | bytes 1540
  71.2 1.9 copy-start
  71.2 1.9 copy-start.4
  71.3 1.9 copy-start.5
  75.2 1.1 copy-start.1
  83.5 1.1 copy-start.1
  91.9 1.1 copy-start.1
  100.2 1.1 copy-start.1
  117.3 4.7 %copy-start.7 = (s32[8,4]{0,1:T(4,128)S(1)}, s32[8,4]{0,1:T(4,128)}, u32[]{:S(2)}) copy-start(s32[8,4]{0,1:T(4,128)} %copy-done.6) | copy-start | bytes 388
  117.3 51.0 %all-to-all-start.2 = ((f32[1,4,128,1024]{3,1,0,2:T(4,128)}), f32[1,4,128,1024]{3,1,0,2:T(4,128)}, u32[]{:S(2)}, u32[]{:S(2)}) async-start(f32[1,4,128,1024]{3,1,0,2:T(4,128)} %copy.141), calls=%async_computation.2 | async-start | bytes 4194304 | tf_op jit(solution)/shard_map/all_to_all | solution.py:135
  180.7 18.0 %all-to-all-start.3 = ((f32[8,16,1024]{2,1,0:T(8,128)}), f32[8,16,1024]{2,1,0:T(8,128)S(1)}, u32[]{:S(2)}, u32[]{:S(2)}) async-start(f32[8,16,1024]{2,1,0:T(8,128)} %bitcast.337), calls=%async_computation.3 | async-start | bytes 1048576 | tf_op jit(solution)/shard_map/all_to_all | solution.py:143
where the time goes:
time: 201 us; the launch traced here: 200 us
  waiting for transfers between devices  72.8 us (36%)
  local copies, waits for them, and re-layouts  38.2 us (19%)
  matrix products  29.4 us (15%)
  blocking collectives  21.8 us (11%)
  starting transfers between devices  19.3 us (10%)
  other arithmetic  16 us (8%)
    all_to_all x1, waiting for transfers between devices, return_rows(): lax.all_to_all(grad_rows, 'seg', split_axis=2, concat_axis=0, tiled=True)  46.1 us
    all_gather x1, blocking collectives, body(): lax.all_gather(local_sum[:, 0], 'seg', axis=0, tiled=True)  21.8 us
    all_to_all x1, waiting for transfers between devices, fetch_rows(): lax.all_to_all(routed, 'seg', split_axis=0, concat_axis=2, tiled=True)  14.3 us
    unnamed x47, local copies, waits for them, and re-layouts  13.9 us
    all_to_all x1, waiting for transfers between devices, return_rows(): lax.all_to_all(summed.reshape(total_segs, piece_len, feature_len), 'seg',...  12.4 us
    dot_general x4, matrix products, attend_group(): jnp.einsum('jtk,kd->tjd', dscore, k_group, preferred_element_type=jnp.flo...  7.63 us
    all_to_all x1, starting transfers between devices, body(): lax.all_to_all(kv_local, 'seg', split_axis=1, concat_axis=0, tiled=True)  7.25 us
    sub x4, matrix products, attend_group(): weights = jnp.exp(scores - row_max)  6.59 us
  transfers between devices with their start and end apart: 4, of which 3 were waited for; matrix products, arithmetic and copies ran while one was open for 8% of the time, Pallas kernels for 0%

commit v1 on v0

v1 whole, which is shorter than its diff:
```python
import functools
import math

import jax
import jax.numpy as jnp
from jax import lax
from jax.experimental import pallas as pl
from jax.experimental.pallas import tpu as pltpu
from jax.sharding import PartitionSpec as P

HD = 128
DEPTH = 5
BETA = 0.1
LAMBDA_SEG = 0.7
GATHER_LIMIT = 16
LOG2E = math.log2(math.e)


def lookup(table_values, lookup_ids):
    matches = lookup_ids[..., None] == jnp.arange(table_values.shape[0], dtype=jnp.int32)
    return jnp.sum(jnp.where(matches, table_values, 0), axis=-1)


def ancestors(parents, count):
    current = jnp.arange(parents.shape[0], dtype=jnp.int32)
    chain_list = []
    for depth_step in range(count):
        parent_ids = lookup(parents, current)
        current = jnp.where(current >= 0, parent_ids, -1)
        chain_list.append(current)
    return jnp.stack(chain_list, axis=1)


def delta_rows(rewards, logprobs, ref_logprobs, value_est, next_value, own_len):
    positions = lax.broadcasted_iota(jnp.int32, rewards.shape, 1)
    next_value = jnp.where(positions + 1 < own_len, next_value, 0.0)
    return jnp.where(
        positions < own_len,
        rewards - BETA * (logprobs - ref_logprobs) + next_value - value_est,
        0.0,
    )


def attend_kernel(
    log_rate,
    group_size,
    depth,
    own_ref,
    src_ref,
    dst_ref,
    slot_len_ref,
    parents_ref,
    lengths_ref,
    first_ref,
    deltas_ref,
    q_ref,
    dir_ref,
    k_ref,
    v_ref,
    dq_ref,
    dk_ref,
    dv_ref,
    adv_ref,
    do_scr,
    bias_scr,
    p_scr,
    ds_scr,
):
    length = q_ref.shape[0]
    slots = src_ref.shape[0]
    kv_heads = k_ref.shape[2] // HD
    own = own_ref[0]
    own_len = slot_len_ref[0]
    count = parents_ref.shape[1]

    row_id = lax.broadcasted_iota(jnp.int32, (count, count), 0)
    col_id = lax.broadcasted_iota(jnp.int32, (count, count), 1)
    eye = row_id == col_id

    def to_row(col):
        return jnp.sum(jnp.where(eye, col, 0.0), axis=0, keepdims=True)

    children = (parents_ref[...] == row_id).astype(jnp.float32)
    weights = children / jnp.maximum(jnp.sum(children, axis=1, keepdims=True), 1.0)
    lens_col = jnp.sum(jnp.where(eye, lengths_ref[...].astype(jnp.float32), 0.0), axis=1, keepdims=True)
    first_local = first_ref[:, 0:1]
    first_value = first_ref[:, 1:2]
    later_value = jnp.sum(weights * to_row(first_value), axis=1, keepdims=True)
    base_term = first_local + jnp.exp((lens_col - 1.0) * log_rate) * later_value
    factor = jnp.exp(lens_col * log_rate)
    head = base_term
    for _ in range(depth):
        head = base_term + factor * jnp.sum(weights * to_row(head), axis=1, keepdims=True)
    later_head = jnp.sum(weights * to_row(head), axis=1, keepdims=True)
    mine = lax.broadcasted_iota(jnp.int32, (count, 1), 0) == own
    my_value = jnp.sum(jnp.where(mine, later_value, 0.0), axis=0, keepdims=True)
    my_head = jnp.sum(jnp.where(mine, later_head, 0.0), axis=0, keepdims=True)

    t_id = lax.broadcasted_iota(jnp.int32, (length, length), 0)
    j_id = lax.broadcasted_iota(jnp.int32, (length, length), 1)
    offset = (j_id - t_id).astype(jnp.float32)
    discount = jnp.where(offset >= 0, jnp.exp(offset * log_rate), 0.0)
    local_sum = jnp.sum(discount * deltas_ref[...], axis=1, keepdims=True)
    t_col = lax.broadcasted_iota(jnp.int32, (length, 1), 0)
    left = (own_len - t_col).astype(jnp.float32)
    advantage = jnp.where(
        t_col < own_len,
        local_sum
        + jnp.exp((left - 1.0) * log_rate) * my_value
        + jnp.exp(left * log_rate) * my_head,
        0.0,
    )
    adv_ref[...] = jnp.sum(jnp.where(t_id == j_id, advantage, 0.0), axis=0, keepdims=True)
    do_scr[...] = (advantage * dir_ref[...].astype(jnp.float32)).astype(jnp.bfloat16)

    for slot in range(slots):
        seen = t_id < slot_len_ref[slot]
        if slot == 0:
            seen = jnp.logical_and(seen, t_id <= j_id)
        bias_scr[slot * length : (slot + 1) * length, :] = jnp.where(seen, 0.0, -1e30)

    dk_ref[...] = jnp.zeros_like(dk_ref)
    dv_ref[...] = jnp.zeros_like(dv_ref)
    scale = HD**-0.5
    contract_last = (((1,), (1,)), ((), ()))
    contract_first = (((0,), (0,)), ((), ()))

    for g in range(kv_heads):
        kv_cols = slice(g * HD, (g + 1) * HD)
        k_all = jnp.concatenate([k_ref[src_ref[s], :, kv_cols] for s in range(slots)], axis=0)
        v_all = jnp.concatenate([v_ref[src_ref[s], :, kv_cols] for s in range(slots)], axis=0)
        heads = [
            slice((g * group_size + j) * HD, (g * group_size + j + 1) * HD)
            for j in range(group_size)
        ]
        q_all = jnp.concatenate([q_ref[:, c] for c in heads], axis=0)
        do_all = jnp.concatenate([do_scr[:, c] for c in heads], axis=0)
        for j in range(group_size):
            rows = slice(j * length, (j + 1) * length)
            scores = lax.dot_general(
                k_all, q_all[rows], contract_last, preferred_element_type=jnp.float32
            )
            scores = scores * (scale * LOG2E) + bias_scr[...]
            top = jnp.max(scores, axis=0, keepdims=True)
            unnorm = jnp.exp2(scores - top)
            prob = unnorm * (1.0 / jnp.sum(unnorm, axis=0, keepdims=True))
            prob_low = prob.astype(jnp.bfloat16)
            dprob = lax.dot_general(
                v_all, do_all[rows], contract_last, preferred_element_type=jnp.float32
            )
            row_dot = jnp.sum(prob_low.astype(jnp.float32) * dprob, axis=0, keepdims=True)
            dscore = (prob * (dprob - row_dot)).astype(jnp.bfloat16)
            p_scr[:, rows] = prob_low
            ds_scr[:, rows] = dscore
        dscore_all = ds_scr[...]
        dq_t = lax.dot_general(
            k_all, dscore_all, contract_first, preferred_element_type=jnp.float32
        )
        for j in range(group_size):
            dq_ref[:, heads[j]] = (
                jnp.transpose(dq_t[:, j * length : (j + 1) * length]) * scale
            ).astype(dq_ref.dtype)
        dk_all = jnp.dot(dscore_all, q_all, preferred_element_type=jnp.float32) * scale
        dv_all = jnp.dot(p_scr[...], do_all, preferred_element_type=jnp.float32)
        for s in range(slots):
            rows = slice(s * length, (s + 1) * length)

            @pl.when(slot_len_ref[s] > 0)
            def _():
                dk_ref[dst_ref[s], :, kv_cols] = dk_all[rows].astype(dk_ref.dtype)
                dv_ref[dst_ref[s], :, kv_cols] = dv_all[rows].astype(dv_ref.dtype)


def attend(
    own, src, dst, slot_lens, parents, lengths, first, deltas, q, direction, k, v, out_slots, log_rate
):
    length, kv_width = k.shape[1:]
    slots = src.shape[0]
    keys = slots * length
    group_size = q.shape[1] // kv_width
    smem = pl.BlockSpec(memory_space=pltpu.SMEM)
    vmem = pl.BlockSpec(memory_space=pltpu.VMEM)
    products = 5 * 2 * keys * length * q.shape[1]
    return pl.pallas_call(
        functools.partial(attend_kernel, log_rate, group_size, DEPTH),
        out_shape=(
            jax.ShapeDtypeStruct(q.shape, jnp.bfloat16),
            jax.ShapeDtypeStruct((out_slots, length, kv_width), jnp.bfloat16),
            jax.ShapeDtypeStruct((out_slots, length, kv_width), jnp.bfloat16),
            jax.ShapeDtypeStruct((1, length), jnp.float32),
        ),
        in_specs=[smem] * 4 + [vmem] * 8,
        out_specs=(vmem,) * 4,
        scratch_shapes=[
            pltpu.VMEM(q.shape, jnp.bfloat16),
            pltpu.VMEM((keys, length), jnp.float32),
            pltpu.VMEM((keys, group_size * length), jnp.bfloat16),
            pltpu.VMEM((keys, group_size * length), jnp.bfloat16),
        ],
        compiler_params=pltpu.CompilerParams(vmem_limit_bytes=40 * 1024 * 1024),
        cost_estimate=pl.CostEstimate(
            flops=products, bytes_accessed=8 * 1024 * 1024, transcendentals=keys * q.shape[1]
        ),
        name="tree_attention_backward",
    )(own, src, dst, slot_lens, parents, lengths, first, deltas, q, direction, k, v)


def fetch_rows(spread, wanted):
    routed = jnp.take(spread, jnp.maximum(wanted, 0), axis=0)
    return lax.all_to_all(routed, "seg", split_axis=0, concat_axis=2, tiled=True)


def return_rows(grad_rows, wanted, total_segs):
    returned = lax.all_to_all(grad_rows, "seg", split_axis=2, concat_axis=0, tiled=True)
    piece_len = returned.shape[2]
    feature_len = returned.shape[3]
    routed_ids = wanted.reshape(-1)
    targets = jnp.where(routed_ids >= 0, routed_ids, total_segs)
    summed = jax.ops.segment_sum(
        returned.reshape(-1, piece_len * feature_len).astype(jnp.float32),
        targets,
        num_segments=total_segs + 1,
    )[:total_segs]
    return lax.all_to_all(
        summed.reshape(total_segs, piece_len, feature_len),
        "seg",
        split_axis=0,
        concat_axis=1,
        tiled=True,
    )


def body(
    queries,
    key_vectors,
    value_vectors,
    direction,
    rewards,
    logprobs,
    ref_logprobs,
    value_est,
    parents,
    seg_lengths,
):
    total_segs = parents.shape[0]
    groups = lax.axis_size("seg")
    held_segs = total_segs // groups
    assert held_segs == 1
    length = rewards.shape[0]
    own = lax.axis_index("seg")
    log_rate = math.log(LAMBDA_SEG) / length
    kv_width = key_vectors.shape[1]
    own_len = lax.dynamic_slice_in_dim(seg_lengths, own, 1)

    next_value = jnp.concatenate([value_est[1:], jnp.zeros_like(value_est[:1])])
    deltas = delta_rows(
        rewards[None], logprobs[None], ref_logprobs[None], value_est[None], next_value[None], own_len[0]
    )
    powers = jnp.exp(jnp.arange(length, dtype=jnp.float32) * log_rate)
    first_pair = jnp.stack([jnp.sum(deltas[0] * powers), value_est[0]])[None]
    first = lax.all_gather(first_pair, "seg", axis=0, tiled=True)

    chains = ancestors(parents, DEPTH - 1)
    held_wanted = lax.dynamic_slice_in_dim(chains, own, 1)
    slot_ids = jnp.concatenate([jnp.reshape(own, (1, 1)), held_wanted], axis=1)[0]
    slot_lens = lookup(seg_lengths, slot_ids)
    args = (jnp.reshape(own, (1,)),)
    tail = (parents[None], seg_lengths[None], first, deltas, queries, direction)
    if groups <= GATHER_LIMIT:
        keys = lax.all_gather(key_vectors[None], "seg", axis=0, tiled=True)
        values = lax.all_gather(value_vectors[None], "seg", axis=0, tiled=True)
        src = jnp.maximum(slot_ids, 0)
        grad_q, grad_k, grad_v, advantage = attend(
            *args, src, src, slot_lens, *tail, keys, values, total_segs, log_rate
        )
        grad_keys = lax.psum_scatter(grad_k, "seg", scatter_dimension=0, tiled=True)[0]
        grad_values = lax.psum_scatter(grad_v, "seg", scatter_dimension=0, tiled=True)[0]
    else:
        kv_local = jnp.concatenate([key_vectors, value_vectors], axis=1)[None]
        spread = lax.all_to_all(kv_local, "seg", split_axis=1, concat_axis=0, tiled=True)
        arrived = fetch_rows(spread, chains)[0]
        slot_kv = jnp.concatenate([kv_local, arrived], axis=0)
        src = jnp.arange(DEPTH, dtype=jnp.int32)
        grad_q, grad_k, grad_v, advantage = attend(
            *args,
            src,
            src,
            slot_lens,
            *tail,
            slot_kv[:, :, :kv_width],
            slot_kv[:, :, kv_width:],
            DEPTH,
            log_rate,
        )
        grad_kv = jnp.concatenate([grad_k, grad_v], axis=2)
        summed = return_rows(grad_kv[None, 1:], chains, total_segs)[0]
        summed = summed + grad_kv[0].astype(jnp.float32)
        grad_keys = summed[:, :kv_width].astype(jnp.bfloat16)
        grad_values = summed[:, kv_width:].astype(jnp.bfloat16)
    return (grad_q, grad_keys, grad_values, advantage[0])


def solution(mesh):
    in_specs = (
        P(("grp", "seg"), "tp"),
        P(("grp", "seg"), "tp"),
        P(("grp", "seg"), "tp"),
        P(("grp", "seg"), "tp"),
        P(("grp", "seg")),
        P(("grp", "seg")),
        P(("grp", "seg")),
        P(("grp", "seg")),
        P("grp"),
        P("grp"),
    )
    out_specs = (
        P(("grp", "seg"), "tp"),
        P(("grp", "seg"), "tp"),
        P(("grp", "seg"), "tp"),
        P(("grp", "seg")),
    )
    return jax.shard_map(body, mesh=mesh, in_specs=in_specs, out_specs=out_specs, check_vma=False)
```

time: 201 us -> 246 us (1.22)
  waiting for transfers between devices: 72.8 us -> 185 us
  local copies, waits for them, and re-layouts: 38.2 us -> 8.15 us
  matrix products: 29.4 us -> 0 us
  starting transfers between devices: 19.3 us -> 0.16 us
  other arithmetic: 16 us -> 3.12 us
  between operations: 1.71 us -> 14.5 us
  Pallas kernels: 0 us -> 11 us
    reduce_scatter x0 -> x2, waiting for transfers between devices: none -> 129 us  [the longest x1 66.6 us: body(): lax.psum_scatter(grad_v, 'seg', scatter_dimension=0, tiled=True)[0]]
    all_to_all x4 -> x0, waiting for transfers between devices: 72.8 us -> none  [the longest x1 46.1 us: return_rows(): lax.all_to_all(grad_rows, 'seg', split_axis=2, concat_axis=0, tiled=True)]
    all_gather x0 -> x2, waiting for transfers between devices: none -> 54.9 us  [the longest x1 41.1 us: body(): values = lax.all_gather(value_vectors[None], 'seg', axis=0, tiled=True)]
    unnamed x0 -> x1, blocking collectives: none -> 23.2 us
    dot_general x28 -> x0, matrix products: 22.8 us -> none  [the longest x4 7.63 us: attend_group(): jnp.einsum('jtk,kd->tjd', dscore, k_group, preferred_element_type=jnp.flo...]
    all_gather x1 -> x0, blocking collectives: 21.8 us -> none  [body(): lax.all_gather(local_sum[:, 0], 'seg', axis=0, tiled=True)]
    all_to_all x4 -> x0, starting transfers between devices: 19.3 us -> none  [the longest x1 7.25 us: body(): lax.all_to_all(kv_local, 'seg', split_axis=1, concat_axis=0, tiled=True)]
    pallas_call x0 -> x1, Pallas kernels: none -> 11 us  [attend(): pl.pallas_call(functools.partial(attend_kernel, log_rate, group_size, DEP...]
  transfers between devices with their start and end apart: 4 -> 4, of which waited for: 3 -> 4; matrix products, arithmetic and copies ran while one was open for 8% -> 2% of each run, Pallas kernels for 0% -> 0%
where the time goes in v1:
time: 246 us
  waiting for transfers between devices  185 us (75%)
  blocking collectives  23.2 us (9%)
  between operations  14.5 us (6%)
  Pallas kernels  11 us (4%)
  local copies, waits for them, and re-layouts  8.15 us (3%)
  other arithmetic  3.12 us (1%)
    reduce_scatter x1, waiting for transfers between devices, body(): lax.psum_scatter(grad_v, 'seg', scatter_dimension=0, tiled=True)[0]  66.6 us
    reduce_scatter x1, waiting for transfers between devices, body(): lax.psum_scatter(grad_k, 'seg', scatter_dimension=0, tiled=True)[0]  61.9 us
    all_gather x1, waiting for transfers between devices, body(): values = lax.all_gather(value_vectors[None], 'seg', axis=0, tiled=True)  41.1 us
    unnamed x1, blocking collectives  23.2 us
    all_gather x1, waiting for transfers between devices, body(): keys = lax.all_gather(key_vectors[None], 'seg', axis=0, tiled=True)  13.8 us
    pallas_call x1, Pallas kernels, attend(): pl.pallas_call(functools.partial(attend_kernel, log_rate, group_size, DEP...  11 us
    unnamed x24, local copies, waits for them, and re-layouts  7.25 us
  transfers between devices with their start and end apart: 4, of which 4 were waited for; matrix products, arithmetic and copies ran while one was open for 2% of the time, Pallas kernels for 0%

profile of v1, /device:TPU:0, one launch (start us, length us, event | category | flops | bytes accessed | tf_op | source)
XLA Modules:
  0.0 245.6 jit_solution(18319811043843905244)
XLA Ops:
  7.2 0.0 all-gather.6.cloned.1.call-start
  7.2 0.7 all-gather.6.cloned.1.call-update
  7.9 0.0 all-gather.8.cloned.1.call-start
  7.9 0.7 all-gather.8.cloned.1.call-update
  8.6 0.0 reduce-scatter.3.cloned.1.call-start
  8.7 0.0 copy-start.6
  8.7 0.6 copy-done.6
  9.4 0.1 slice.6
  9.4 0.0 copy-start.5
  9.4 0.7 copy-done.5
  10.1 0.0 copy-start.10
  10.1 0.6 dynamic_slice.7
  10.7 0.1 copy-done.10
  10.7 0.6 dynamic-slice
  12.0 0.0 copy-start.7
  12.0 0.0 copy-start.8
  12.0 0.0 copy-start.9
  12.0 0.6 copy-done.7
  12.6 0.0 copy-done.8
  12.7 0.0 copy-done.9
  12.7 1.3 multiply_reduce_fusion
  14.0 0.8 maximum_dynamic-update-slice_fusion
  14.8 0.0 copy-start.4
  14.8 23.2 %all-reduce = f32[16]{0:T(128)S(1)} all-reduce(f32[16]{0:T(128)S(1)} %maximum_dynamic-update-slice_fusion), channel_id=2, replica_groups=mesh['grp'=2,'seg'=8,'tp'=2] {'seg'}, use_global_device_ids=true, to_apply=%add | all-reduce | flops 16 | bytes 128
  38.1 0.0 copy-done.4
  38.1 0.1 select_reduce_fusion.4
  38.2 0.2 select_reduce_fusion.3
  38.4 0.2 select_reduce_fusion.2
  38.6 0.2 select_reduce_fusion.1
  38.8 0.1 constant_dynamic-slice_fusion
  38.9 0.1 copy.15
  38.9 0.1 reshape.85.first_ref
  39.0 0.1 broadcast_maximum_fusion
  39.1 0.2 select_reduce_fusion.slot_len_ref
  39.3 13.8 %all-gather.6.cloned.1.call-done = bf16[1024,512]{1,0:T(8,128)(2,1)} async-done(((bf16[128,512]{1,0:T(8,128)(2,1)}), bf16[1024,512]{1,0:T(8,128)(2,1)}) %all-gather.6.cloned.1.call-update) | async-done | bytes 1048592 | tf_op jit(solution)/shard_map/all_gather | solution.py:270
  53.1 41.1 %all-gather.8.cloned.1.call-done = bf16[1024,512]{1,0:T(8,128)(2,1)} async-done(((bf16[128,512]{1,0:T(8,128)(2,1)}), bf16[1024,512]{1,0:T(8,128)(2,1)}) %all-gather.8.cloned.1.call-update) | async-done | bytes 1048592 | tf_op jit(solution)/shard_map/all_gather | solution.py:271
  94.2 0.0 copy-start
  94.2 1.2 copy-done
  95.4 0.0 copy-start.1
  95.4 1.2 copy-done.1
  96.6 0.0 copy-start.2
  96.6 1.1 copy-done.2
  97.7 0.0 copy-start.3
  97.7 1.1 copy-done.3
  98.8 11.0 %tree_attention_backward.1 = (bf16[128,2560]{1,0:T(8,128)(2,1)}, bf16[8,128,512]{2,1,0:T(8,128)(2,1)}, bf16[8,128,512]{2,1,0:T(8,128)(2,1)}, f32[1,128]{1,0:T(1,128)}) custom-call(s32[1]{0:T(128)} %bitcast.own_ref, s32[5]{0:T(128)S(1)} %get-tuple-element.14.src_ref.dst_ref, s32[5]{0:T(128)S(1)} %get-tuple-element.14.src_ref.dst_ref, ...), custom_call_target="tpu_custom_call" | custom-call | flops 2097152000 | bytes 8388608 | tf_op jit(solution)/shard_map/tree_attention_backward/pallas_call | solution.py:184
  109.8 0.0 reduce-scatter.3.cloned.1.call-update
  109.9 0.0 reduce-scatter.5.cloned.1.call-start
  109.9 0.5 reduce-scatter.5.cloned.1.call-update
  110.4 61.9 %reduce-scatter.3.cloned.1.call-done = bf16[1,128,512]{2,1,0:T(8,128)(2,1)} async-done(((bf16[8,128,512]{2,1,0:T(8,128)(2,1)}), bf16[1,128,512]{2,1,0:T(8,128)(2,1)}) %reduce-scatter.3.cloned.1.call-update) | async-done | bytes 131088 | tf_op jit(solution)/shard_map/reduce_scatter | solution.py:276
  172.4 66.6 %reduce-scatter.5.cloned.1.call-done = bf16[1,128,512]{2,1,0:T(8,128)(2,1)} async-done(((bf16[8,128,512]{2,1,0:T(8,128)(2,1)}), bf16[1,128,512]{2,1,0:T(8,128)(2,1)}) %reduce-scatter.5.cloned.1.call-update) | async-done | bytes 131088 | tf_op jit(solution)/shard_map/reduce_scatter | solution.py:277
  (5 shorter events, 0.0 us)
Async XLA Ops:
  7.2 45.9 %all-gather.6.cloned.1.call-start = ((), (), s32[]{:S(2)}) async-start(), calls=%async_computation.4 | async-start | bytes 1179648 | tf_op jit(solution)/shard_map/all_gather | solution.py:270
  7.9 86.3 %all-gather.8.cloned.1.call-start = ((), (), s32[]{:S(2)}) async-start(), calls=%async_computation.5 | async-start | bytes 1179648 | tf_op jit(solution)/shard_map/all_gather | solution.py:271
  8.6 163.7 %reduce-scatter.3.cloned.1.call-start = ((), (), s32[]{:S(2)}) async-start(), calls=%async_computation.2 | async-start | bytes 1179648 | tf_op jit(solution)/shard_map/reduce_scatter | solution.py:276
  8.7 0.7 copy-start.6
  9.4 0.7 copy-start.5
  10.1 0.7 copy-start.10
  12.0 0.7 copy-start.7
  12.0 0.7 copy-start.8
  12.0 0.7 copy-start.9
  14.8 23.2 %copy-start.4 = (s32[8]{0:T(128)S(1)}, s32[8]{0:T(128)}, u32[]{:S(2)}) copy-start(s32[8]{0:T(128)} %param.18) | copy-start | bytes 100
  94.2 1.2 copy-start
  95.4 1.2 copy-start.1
  96.6 1.1 copy-start.2
  97.7 1.1 copy-start.3
  109.9 129.2 %reduce-scatter.5.cloned.1.call-start = ((), (), s32[]{:S(2)}) async-start(), calls=%async_computation.3 | async-start | bytes 1179648 | tf_op jit(solution)/shard_map/reduce_scatter | solution.py:277
Sparse Core Ops, SparseCore 0:
  10.1 42.9 all-gather.5
  55.2 38.8 all-gather.7
  110.0 62.3 reduce-scatter.2
  176.6 62.3 reduce-scatter.4

commit v2 on v1

v2 whole, which is shorter than its diff:
```python
import functools
import math

import jax
import jax.numpy as jnp
from jax import lax
from jax.experimental import pallas as pl
from jax.experimental.pallas import tpu as pltpu
from jax.sharding import PartitionSpec as P

HD = 128
DEPTH = 5
BETA = 0.1
LAMBDA_SEG = 0.7
PAIRED_GROUPS = 8
LOG2E = math.log2(math.e)


def lookup(table_values, lookup_ids):
    matches = lookup_ids[..., None] == jnp.arange(table_values.shape[0], dtype=jnp.int32)
    return jnp.sum(jnp.where(matches, table_values, 0), axis=-1)


def ancestors(parents, count):
    current = jnp.arange(parents.shape[0], dtype=jnp.int32)
    chain_list = []
    for depth_step in range(count):
        parent_ids = lookup(parents, current)
        current = jnp.where(current >= 0, parent_ids, -1)
        chain_list.append(current)
    return jnp.stack(chain_list, axis=1)


def token_terms(log_rate, own_len, rewards, logprobs, ref_logprobs, values):
    positions = lax.broadcasted_iota(jnp.int32, rewards.shape, 1)
    later = jnp.concatenate([values[:, 1:], values[:, :1]], axis=1)
    later = jnp.where(positions + 1 < own_len, later, 0.0)
    deltas = jnp.where(
        positions < own_len, rewards - BETA * (logprobs - ref_logprobs) + later - values, 0.0
    )
    powers = jnp.exp(positions.astype(jnp.float32) * log_rate)
    first_local = jnp.sum(deltas * powers, axis=1, keepdims=True)
    firsts = jnp.where(positions == 0, first_local, jnp.where(positions == 1, values[:, :1], 0.0))
    return deltas, firsts


def pack_kernel(
    log_rate,
    parts,
    own_ref,
    lengths_ref,
    k_ref,
    v_ref,
    rewards_ref,
    logprobs_ref,
    ref_logprobs_ref,
    values_ref,
    *out_refs,
):
    terms_ref = out_refs[-1]
    own = own_ref[0]
    heads = k_ref.shape[1] // HD // parts
    for step, out_ref in enumerate(out_refs[:-1]):
        part = lax.rem(own + step, parts)
        for h in range(heads):
            columns = pl.ds(pl.multiple_of((part * heads + h) * HD, HD), HD)
            out_ref[h] = k_ref[:, columns]
            out_ref[heads + h] = v_ref[:, columns]
    length = k_ref.shape[0]
    deltas, firsts = token_terms(
        log_rate,
        lengths_ref[own],
        rewards_ref[...],
        logprobs_ref[...],
        ref_logprobs_ref[...],
        values_ref[...],
    )
    mine = lax.broadcasted_iota(jnp.int32, (terms_ref.shape[0], length), 0) == own
    terms_ref[:, :length] = jnp.where(mine, deltas, 0.0)
    terms_ref[:, length:] = jnp.where(mine, firsts, 0.0)


def pack(own, lengths, k, v, token_rows, parts, log_rate):
    length, width = k.shape
    smem = pl.BlockSpec(memory_space=pltpu.SMEM)
    vmem = pl.BlockSpec(memory_space=pltpu.VMEM)
    heads = width // HD // parts
    block = jax.ShapeDtypeStruct((2 * heads, length, HD), k.dtype)
    terms = jax.ShapeDtypeStruct((lengths.shape[0], 2 * length), jnp.float32)
    return pl.pallas_call(
        functools.partial(pack_kernel, log_rate, parts),
        out_shape=(block,) * parts + (terms,),
        in_specs=[smem] * 2 + [vmem] * 6,
        out_specs=(vmem,) * (parts + 1),
        cost_estimate=pl.CostEstimate(
            flops=length * 100, bytes_accessed=8 * length * width, transcendentals=length
        ),
        name="pack_keys_values",
    )(own, lengths, k, v, *token_rows)


def attend_kernel(log_rate, group_size, depth, segs, sources, *refs):
    own_ref, parents_s, lengths_s, parents_ref, lengths_ref, terms_ref = refs[:6]
    refs = refs[6:]
    q_refs, dir_refs, kv_refs = refs[:segs], refs[segs : 2 * segs], refs[2 * segs : 2 * segs + sources]
    refs = refs[2 * segs + sources :]
    adv_ref, dq_refs, dkv_refs = refs[0], refs[1 : 1 + segs], refs[1 + segs : 1 + segs + sources // segs]
    q_scr, do_scr, kv_scr, bias_scr, p_scr, ds_scr, acc_scr = refs[1 + segs + sources // segs :]

    length = q_refs[0].shape[0]
    kv_heads = kv_scr.shape[1] // 2
    count = parents_s.shape[0]
    own = own_ref[0]
    part = lax.rem(own, segs)

    row_id = lax.broadcasted_iota(jnp.int32, (count, count), 0)
    col_id = lax.broadcasted_iota(jnp.int32, (count, count), 1)
    eye = row_id == col_id

    def to_row(col):
        return jnp.sum(jnp.where(eye, col, 0.0), axis=0, keepdims=True)

    children = (parents_ref[...] == row_id).astype(jnp.float32)
    weights = children / jnp.maximum(jnp.sum(children, axis=1, keepdims=True), 1.0)
    lens_col = jnp.sum(
        jnp.where(eye, lengths_ref[...].astype(jnp.float32), 0.0), axis=1, keepdims=True
    )
    first_local = terms_ref[:, length : length + 1]
    first_value = terms_ref[:, length + 1 : length + 2]
    later_value = jnp.sum(weights * to_row(first_value), axis=1, keepdims=True)
    base_term = first_local + jnp.exp((lens_col - 1.0) * log_rate) * later_value
    factor = jnp.exp(lens_col * log_rate)
    head = base_term
    for _ in range(depth):
        head = base_term + factor * jnp.sum(weights * to_row(head), axis=1, keepdims=True)
    later_head = jnp.sum(weights * to_row(head), axis=1, keepdims=True)

    t_id = lax.broadcasted_iota(jnp.int32, (length, length), 0)
    j_id = lax.broadcasted_iota(jnp.int32, (length, length), 1)
    offset = (j_id - t_id).astype(jnp.float32)
    discount = jnp.where(offset >= 0, jnp.exp(offset * log_rate), 0.0)
    t_col = lax.broadcasted_iota(jnp.int32, (length, 1), 0)
    seg_col = lax.broadcasted_iota(jnp.int32, (count, 1), 0)

    for source in range(sources):
        kv_scr[source] = kv_refs[source][...]
    acc_scr[...] = jnp.zeros_like(acc_scr)

    slot_sources = []
    for i in range(segs):
        seg = own - part + lax.rem(part + i, segs)
        seg_len = lengths_s[seg]
        mine = seg_col == seg
        my_value = jnp.sum(jnp.where(mine, later_value, 0.0), axis=0, keepdims=True)
        my_head = jnp.sum(jnp.where(mine, later_head, 0.0), axis=0, keepdims=True)
        deltas = jnp.sum(jnp.where(mine, terms_ref[:, :length], 0.0), axis=0, keepdims=True)
        local_sum = jnp.sum(discount * deltas, axis=1, keepdims=True)
        left = (seg_len - t_col).astype(jnp.float32)
        advantage = jnp.where(
            t_col < seg_len,
            local_sum
            + jnp.exp((left - 1.0) * log_rate) * my_value
            + jnp.exp(left * log_rate) * my_head,
            0.0,
        )
        if i == 0:
            adv_ref[...] = jnp.sum(jnp.where(t_id == j_id, advantage, 0.0), axis=0, keepdims=True)
        heads = kv_heads * group_size
        first_col = part * heads * HD if q_refs[i].shape[1] > heads * HD else 0
        for h in range(heads):
            columns = pl.ds(pl.multiple_of(first_col + h * HD, HD), HD)
            q_scr[i, h] = q_refs[i][:, columns]
            grad_out = advantage * dir_refs[i][:, columns].astype(jnp.float32)
            do_scr[i, h] = grad_out.astype(jnp.bfloat16)

        ancestor = seg
        chosen = []
        for slot in range(depth):
            if slot > 0:
                ancestor = jnp.where(
                    ancestor >= 0, parents_s[jnp.maximum(ancestor, 0)], -1
                ).astype(jnp.int32)
            slot_len = jnp.where(ancestor >= 0, lengths_s[jnp.maximum(ancestor, 0)], 0)
            if segs == 1:
                chosen.append(slot)
            else:
                known = jnp.maximum(ancestor, 0)
                steps = (own - part) // segs - known // segs
                turn = lax.rem(lax.rem(known, segs) - part + segs, segs)
                chosen.append(jnp.where(ancestor >= 0, steps * segs + turn, 0))
            seen = t_id < slot_len
            if slot == 0:
                seen = jnp.logical_and(seen, t_id <= j_id)
            bias_scr[i, slot * length : (slot + 1) * length, :] = jnp.where(seen, 0.0, -1e30)
        slot_sources.append(chosen)

    scale = HD**-0.5
    contract_last = (((1,), (1,)), ((), ()))
    contract_first = (((0,), (0,)), ((), ()))
    for i in range(segs):
        chosen = slot_sources[i]
        for g in range(kv_heads):
            k_all = jnp.concatenate([kv_scr[s, g] for s in chosen], axis=0)
            v_all = jnp.concatenate([kv_scr[s, kv_heads + g] for s in chosen], axis=0)
            mine = slice(g * group_size, (g + 1) * group_size)
            q_all = q_scr[i, mine].reshape(group_size * length, HD)
            do_all = do_scr[i, mine].reshape(group_size * length, HD)
            for j in range(group_size):
                rows = slice(j * length, (j + 1) * length)
                scores = lax.dot_general(
                    k_all, q_all[rows], contract_last, preferred_element_type=jnp.float32
                )
                scores = scores * (scale * LOG2E) + bias_scr[i]
                top = jnp.max(scores, axis=0, keepdims=True)
                unnorm = jnp.exp2(scores - top)
                prob = unnorm * (1.0 / jnp.sum(unnorm, axis=0, keepdims=True))
                prob_low = prob.astype(jnp.bfloat16)
                dprob = lax.dot_general(
                    v_all, do_all[rows], contract_last, preferred_element_type=jnp.float32
                )
                row_dot = jnp.sum(prob_low.astype(jnp.float32) * dprob, axis=0, keepdims=True)
                dscore = (prob * (dprob - row_dot)).astype(jnp.bfloat16)
                p_scr[:, rows] = prob_low
                ds_scr[:, rows] = dscore
            dscore_all = ds_scr[...]
            dq_t = lax.dot_general(
                k_all, dscore_all, contract_first, preferred_element_type=jnp.float32
            )
            for j in range(group_size):
                head = g * group_size + j
                dq_refs[i][:, head * HD : (head + 1) * HD] = (
                    jnp.transpose(dq_t[:, j * length : (j + 1) * length]) * scale
                ).astype(jnp.bfloat16)
            dk_all = jnp.dot(dscore_all, q_all, preferred_element_type=jnp.float32) * scale
            dv_all = jnp.dot(p_scr[...], do_all, preferred_element_type=jnp.float32)
            for slot, s in enumerate(chosen):
                rows = slice(slot * length, (slot + 1) * length)
                acc_scr[s, g] += dk_all[rows]
                acc_scr[s, kv_heads + g] += dv_all[rows]
    for step in range(sources // segs):
        for i in range(segs):
            dkv_refs[step][i] = acc_scr[step * segs + i].astype(jnp.bfloat16)


def attend(own, parents, lengths, terms, q_list, dir_list, kv_list, log_rate):
    segs, sources = len(q_list), len(kv_list)
    planes, length, _ = kv_list[0].shape
    kv_heads = planes // 2
    width = q_list[-1].shape[1]
    group_size = width // HD // kv_heads
    keys = DEPTH * length
    smem = pl.BlockSpec(memory_space=pltpu.SMEM)
    vmem = pl.BlockSpec(memory_space=pltpu.VMEM)
    out_shape = (
        (jax.ShapeDtypeStruct((1, length), jnp.float32),)
        + (jax.ShapeDtypeStruct((length, width), jnp.bfloat16),) * segs
        + (jax.ShapeDtypeStruct((segs, planes, length, HD), jnp.bfloat16),) * (sources // segs)
    )
    outs = pl.pallas_call(
        functools.partial(attend_kernel, log_rate, group_size, DEPTH, segs, sources),
        out_shape=out_shape,
        in_specs=[smem] * 3 + [vmem] * (3 + 2 * segs + sources),
        out_specs=(vmem,) * len(out_shape),
        scratch_shapes=[
            pltpu.VMEM((segs, width // HD, length, HD), jnp.bfloat16),
            pltpu.VMEM((segs, width // HD, length, HD), jnp.bfloat16),
            pltpu.VMEM((sources, planes, length, HD), jnp.bfloat16),
            pltpu.VMEM((segs, keys, length), jnp.float32),
            pltpu.VMEM((keys, group_size * length), jnp.bfloat16),
            pltpu.VMEM((keys, group_size * length), jnp.bfloat16),
            pltpu.VMEM((sources, planes, length, HD), jnp.float32),
        ],
        compiler_params=pltpu.CompilerParams(vmem_limit_bytes=40 * 1024 * 1024),
        cost_estimate=pl.CostEstimate(
            flops=5 * 2 * keys * length * width * segs,
            bytes_accessed=8 * 1024 * 1024,
            transcendentals=keys * width * segs,
        ),
        name="tree_attention_backward",
    )(own, parents, lengths, parents[None], lengths[None], terms, *q_list, *dir_list, *kv_list)
    return outs[0], outs[1 : 1 + segs], outs[1 + segs :]


def permute(array, pairs):
    return lax.ppermute(array, "seg", pairs)


def climb(block, groups):
    two = permute(block, [(i, i + 4) for i in range(groups - 4)])
    one = permute(block, [(i, i + 2) for i in range(groups - 2)])
    three = permute(two, [(i, i + 2) for i in range(4, groups - 2)])
    return one, two, three


def descend(one, two, three, groups):
    passed = permute(three, [(i, i - 2) for i in range(6, groups)])
    from_one = permute(one, [(i, i - 2) for i in range(2, groups)])
    two = (two.astype(jnp.float32) + passed.astype(jnp.float32)).astype(two.dtype)
    from_two = permute(two, [(i, i - 4) for i in range(4, groups)])
    return from_one.astype(jnp.float32) + from_two.astype(jnp.float32)


def paired_body(own, queries, direction, key_vectors, value_vectors, token_rows, parents, lengths, log_rate):
    groups = lax.axis_size("seg")
    part = own[0] % 2
    swap = [(i, i ^ 1) for i in range(groups)]
    kept, given, terms = pack(own, lengths, key_vectors, value_vectors, token_rows, 2, log_rate)
    taken = permute(given, swap)
    kept_far = climb(kept, groups)
    half = queries.shape[1] // 2
    q_taken = permute(lax.dynamic_slice_in_dim(queries, (1 - part) * half, half, 1), swap)
    dir_taken = permute(lax.dynamic_slice_in_dim(direction, (1 - part) * half, half, 1), swap)
    taken_far = climb(taken, groups)
    for bit in (1, 2, 4):
        terms = terms + permute(terms, [(i, i ^ bit) for i in range(groups)])
    kv_list = [kept, taken]
    for pair in zip(kept_far, taken_far):
        kv_list += pair
    advantage, dq, dkv = attend(
        own, parents, lengths, terms, [queries, q_taken], [direction, dir_taken], kv_list, log_rate
    )
    dq_back = permute(dq[1], swap)
    total = dkv[0].astype(jnp.float32) + descend(dkv[1], dkv[2], dkv[3], groups)
    total = total.astype(jnp.bfloat16)
    dkv_back = permute(total[1], swap)
    first = part == 0

    def join(mine, other):
        return jnp.concatenate([jnp.where(first, mine, other), jnp.where(first, other, mine)], axis=1)

    def flat(block):
        return jnp.moveaxis(block, 0, 1).reshape(block.shape[1], -1)

    heads = total.shape[1] // 2
    grad_keys = join(flat(total[0, :heads]), flat(dkv_back[:heads]))
    grad_values = join(flat(total[0, heads:]), flat(dkv_back[heads:]))
    return join(dq[0], dq_back), grad_keys, grad_values, advantage[0]


def fetch_rows(spread, wanted):
    routed = jnp.take(spread, jnp.maximum(wanted, 0), axis=0)
    return lax.all_to_all(routed, "seg", split_axis=0, concat_axis=2, tiled=True)


def return_rows(grad_rows, wanted, total_segs):
    returned = lax.all_to_all(grad_rows, "seg", split_axis=2, concat_axis=0, tiled=True)
    piece_len = returned.shape[2]
    feature_len = returned.shape[3]
    routed_ids = wanted.reshape(-1)
    targets = jnp.where(routed_ids >= 0, routed_ids, total_segs)
    summed = jax.ops.segment_sum(
        returned.reshape(-1, piece_len * feature_len).astype(jnp.float32),
        targets,
        num_segments=total_segs + 1,
    )[:total_segs]
    return lax.all_to_all(
        summed.reshape(total_segs, piece_len, feature_len),
        "seg",
        split_axis=0,
        concat_axis=1,
        tiled=True,
    )


def routed_body(own, queries, direction, key_vectors, value_vectors, token_rows, parents, lengths, log_rate):
    total_segs = parents.shape[0]
    length = queries.shape[0]
    block, terms = pack(own, lengths, key_vectors, value_vectors, token_rows, 1, log_rate)
    planes = block.shape[0]
    mine = lax.dynamic_slice_in_dim(terms, own[0], 1)
    terms = lax.all_gather(mine, "seg", axis=0, tiled=True)
    flat = jnp.moveaxis(block, 0, 1).reshape(1, length, planes * HD)
    spread = lax.all_to_all(flat, "seg", split_axis=1, concat_axis=0, tiled=True)
    chains = ancestors(parents, DEPTH - 1)
    arrived = fetch_rows(spread, chains)[0].reshape(DEPTH - 1, length, planes, HD)
    arrived = jnp.moveaxis(arrived, 2, 1)
    kv_list = [block] + [arrived[slot] for slot in range(DEPTH - 1)]
    advantage, dq, dkv = attend(
        own, parents, lengths, terms, [queries], [direction], kv_list, log_rate
    )
    rows = jnp.moveaxis(jnp.concatenate(dkv[1:]), 1, 2).reshape(1, DEPTH - 1, length, planes * HD)
    summed = return_rows(rows, chains, total_segs)[0]
    summed = summed + jnp.moveaxis(dkv[0][0], 0, 1).reshape(length, planes * HD).astype(jnp.float32)
    width = key_vectors.shape[1]
    grad_keys = summed[:, :width].astype(jnp.bfloat16)
    grad_values = summed[:, width:].astype(jnp.bfloat16)
    return dq[0], grad_keys, grad_values, advantage[0]


def body(
    queries,
    key_vectors,
    value_vectors,
    direction,
    rewards,
    logprobs,
    ref_logprobs,
    value_est,
    parents,
    seg_lengths,
):
    groups = lax.axis_size("seg")
    assert parents.shape[0] == groups
    own = jnp.reshape(lax.axis_index("seg"), (1,))
    log_rate = math.log(LAMBDA_SEG) / rewards.shape[0]
    token_rows = [rewards[None], logprobs[None], ref_logprobs[None], value_est[None]]
    plan = paired_body if groups == PAIRED_GROUPS else routed_body
    return plan(
        own, queries, direction, key_vectors, value_vectors, token_rows, parents, seg_lengths, log_rate
    )


def solution(mesh):
    in_specs = (
        P(("grp", "seg"), "tp"),
        P(("grp", "seg"), "tp"),
        P(("grp", "seg"), "tp"),
        P(("grp", "seg"), "tp"),
        P(("grp", "seg")),
        P(("grp", "seg")),
        P(("grp", "seg")),
        P(("grp", "seg")),
        P("grp"),
        P("grp"),
    )
    out_specs = (
        P(("grp", "seg"), "tp"),
        P(("grp", "seg"), "tp"),
        P(("grp", "seg"), "tp"),
        P(("grp", "seg")),
    )
    return jax.shard_map(body, mesh=mesh, in_specs=in_specs, out_specs=out_specs, check_vma=False)
```

time: 246 us -> 90.8 us (0.37)
  waiting for transfers between devices: 185 us -> 44.9 us
  starting transfers between devices: 0.16 us -> 29.5 us
  blocking collectives: 23.2 us -> 0 us
  between operations: 14.5 us -> 0.91 us
  local copies, waits for them, and re-layouts: 8.15 us -> 3.16 us
    reduce_scatter x2 -> x0, waiting for transfers between devices: 129 us -> none  [the longest x1 66.6 us: body(): lax.psum_scatter(grad_v, 'seg', scatter_dimension=0, tiled=True)[0]]
    all_gather x2 -> x0, waiting for transfers between devices: 54.9 us -> none  [the longest x1 41.1 us: body(): values = lax.all_gather(value_vectors[None], 'seg', axis=0, tiled=True)]
    ppermute x0 -> x17, waiting for transfers between devices: none -> 44.9 us  [permute(): return lax.ppermute(array, 'seg', pairs)]
    ppermute x0 -> x17, starting transfers between devices: none -> 29.5 us  [permute(): return lax.ppermute(array, 'seg', pairs)]
    unnamed x1 -> x0, blocking collectives: 23.2 us -> none
    unnamed x24 -> x14, local copies, waits for them, and re-layouts: 7.25 us -> 1.57 us
  transfers between devices with their start and end apart: 4 -> 17, of which waited for: 4 -> 8; matrix products, arithmetic and copies ran while one was open for 2% -> 2% of each run, Pallas kernels for 0% -> 0%
where the time goes in v2:
time: 90.8 us; the launch traced here: 90.5 us
  waiting for transfers between devices  44.9 us (49%)
  starting transfers between devices  29.5 us (32%)
  Pallas kernels  10.8 us (12%)
  local copies, waits for them, and re-layouts  3.16 us (3%)
  other arithmetic  1.16 us (1%)
  between operations  0.91 us (1%)
    ppermute x17, waiting for transfers between devices, permute(): return lax.ppermute(array, 'seg', pairs)  44.9 us
    ppermute x17, starting transfers between devices, permute(): return lax.ppermute(array, 'seg', pairs)  29.5 us
    pallas_call x1, Pallas kernels, attend(): pl.pallas_call(functools.partial(attend_kernel, log_rate, group_size, DEP...  9 us
    pallas_call x1, Pallas kernels, pack(): pl.pallas_call(functools.partial(pack_kernel, log_rate, parts), out_shape...  1.84 us
  transfers between devices with their start and end apart: 17, of which 8 were waited for; matrix products, arithmetic and copies ran while one was open for 2% of the time, Pallas kernels for 0%

profile of v2, /device:TPU:0, one launch (start us, length us, event | category | flops | bytes accessed | tf_op | source)
XLA Modules:
  0.0 90.5 jit_solution(11585312331907833217)
XLA Ops:
  0.6 0.0 copy-start
  0.6 1.8 %pack_keys_values.1 = (bf16[4,128,128]{2,1,0:T(8,128)(2,1)}, bf16[4,128,128]{2,1,0:T(8,128)(2,1)}, f32[8,256]{1,0:T(8,128)}) custom-call(s32[1]{0:T(128)} %bitcast.own_ref.refs_0_, s32[8]{0:T(128)} %refs_2_.1, bf16[128,512]{1,0:T(8,128)(2,1)} %k_ref.1, bf16[128,512]{1,0:T(8,128)(2,1)} %v_ref.1, f32[1,128]{1,0:T(1,128)} %bitcast.40, f32[1,128]{1,0:T(1,128)} %bitcast.41, ...), custom_call_target="tpu_custom_call" | custom-call | flops 12800 | bytes 524288 | tf_op jit(solution)/shard_map/pack_keys_values/pallas_call | solution.py:90
  2.5 2.9 %collective-permute-start.5 = (bf16[4,128,128]{2,1,0:T(8,128)(2,1)}, bf16[4,128,128]{2,1,0:T(8,128)(2,1)S(1)}, u32[]{:S(2)}, u32[]{:S(2)}) collective-permute-start(bf16[4,128,128]{2,1,0:T(8,128)(2,1)} %get-tuple-element.16), channel_id=1, source_target_pairs={{0,2},{2,0},{4,6},{6,4},{8,10},{10,8},{12,14},{14,12},{1,3},{3,1},... | collective-permute-start | bytes 393224 | tf_op jit(solution)/shard_map/ppermute | solution.py:285
  5.4 0.0 copy-start.5
  5.4 0.0 copy-start.3
  5.4 0.0 copy-start.1
  5.4 0.0 copy-start.2
  5.4 0.0 copy-start.4
  5.4 1.1 %constant_dynamic-slice_fusion = bf16[128,1280]{1,0:T(8,128)(2,1)S(1)} fusion(bf16[128,2560]{1,0:T(8,128)(2,1)} %refs_8_.1, s32[]{:T(128)S(6)} %select_n.69), kind=kLoop, calls=%fused_computation.14 | loop fusion | bytes 655364 | tf_op jit(solution)/shard_map/dynamic_slice | solution.py:312
  6.5 0.1 collective-permute-start.4
  6.6 0.0 copy-done
  6.7 2.1 %collective-permute-start.3 = (bf16[128,1280]{1,0:T(8,128)(2,1)S(1)}, bf16[128,1280]{1,0:T(8,128)(2,1)S(1)}, u32[]{:S(2)}, u32[]{:S(2)}) collective-permute-start(bf16[128,1280]{1,0:T(8,128)(2,1)S(1)} %constant_dynamic-slice_fusion.1), channel_id=1, source_target_pairs={{0,2},{2,0},{4,6},{6,4},{8,10},{10,8},{12,14},{14,12},{1,3},{3,1},... | collective-permute-start | bytes 983048 | tf_op jit(solution)/shard_map/ppermute | solution.py:285
  8.7 0.0 copy-done.5
  8.7 0.1 collective-permute-start
  8.8 14.5 %collective-permute-done = f32[8,256]{1,0:T(8,128)S(1)} collective-permute-done((f32[8,256]{1,0:T(8,128)S(1)}, f32[8,256]{1,0:T(8,128)S(1)}, u32[]{:S(2)}, u32[]{:S(2)}) %collective-permute-start) | collective-permute-done | bytes 8224 | tf_op jit(solution)/shard_map/ppermute | solution.py:285
  23.4 1.8 %collective-permute-start.1 = (f32[8,256]{1,0:T(8,128)S(1)}, f32[8,256]{1,0:T(8,128)S(1)}, u32[]{:S(2)}, u32[]{:S(2)}) collective-permute-start(f32[8,256]{1,0:T(8,128)S(1)} %add.27), channel_id=1, source_target_pairs={{0,4},{2,6},{4,0},{6,2},{8,12},{10,14},{12,8},{14,10},{1,5},{3,7},... | collective-permute-start | bytes 24584 | tf_op jit(solution)/shard_map/ppermute | solution.py:285
  25.2 1.8 %collective-permute-done.1 = f32[8,256]{1,0:T(8,128)S(1)} collective-permute-done((f32[8,256]{1,0:T(8,128)S(1)}, f32[8,256]{1,0:T(8,128)S(1)}, u32[]{:S(2)}, u32[]{:S(2)}) %collective-permute-start.1) | collective-permute-done | bytes 8224 | tf_op jit(solution)/shard_map/ppermute | solution.py:285
  27.0 2.8 %collective-permute-start.2 = (f32[8,256]{1,0:T(8,128)S(1)}, f32[8,256]{1,0:T(8,128)S(1)}, u32[]{:S(2)}, u32[]{:S(2)}) collective-permute-start(f32[8,256]{1,0:T(8,128)S(1)} %add.28), channel_id=1, source_target_pairs={{0,8},{2,10},{4,12},{6,14},{8,0},{10,2},{12,4},{14,6},{1,9},{3,11}... | collective-permute-start | bytes 24584 | tf_op jit(solution)/shard_map/ppermute | solution.py:285
  29.9 0.0 copy-done.3
  29.9 2.0 %collective-permute-start.8 = (bf16[4,128,128]{2,1,0:T(8,128)(2,1)S(1)}, bf16[4,128,128]{2,1,0:T(8,128)(2,1)S(1)}, u32[]{:S(2)}, u32[]{:S(2)}) collective-permute-start(bf16[4,128,128]{2,1,0:T(8,128)(2,1)S(1)} %copy-done.3), channel_id=1, source_target_pairs={{0,8},{2,10},{4,12},{6,14},{1,9},{3,11},{5,13},{7,15},{16,24},{18,... | collective-permute-start | bytes 393224 | tf_op jit(solution)/shard_map/ppermute | solution.py:285
  31.8 0.0 collective-permute-done.2
  31.9 3.7 %collective-permute-start.6 = (bf16[4,128,128]{2,1,0:T(8,128)(2,1)S(1)}, bf16[4,128,128]{2,1,0:T(8,128)(2,1)S(1)}, u32[]{:S(2)}, u32[]{:S(2)}) collective-permute-start(bf16[4,128,128]{2,1,0:T(8,128)(2,1)S(1)} %copy-done.3), channel_id=1, source_target_pairs={{0,4},{2,6},{4,8},{6,10},{8,12},{10,14},{1,5},{3,7},{5,9},{7,11},{... | collective-permute-start | bytes 393224 | tf_op jit(solution)/shard_map/ppermute | solution.py:285
  35.6 0.0 collective-permute-done.5.refs_11_
  35.6 4.8 %collective-permute-start.9 = (bf16[4,128,128]{2,1,0:T(8,128)(2,1)S(1)}, bf16[4,128,128]{2,1,0:T(8,128)(2,1)S(1)}, u32[]{:S(2)}, u32[]{:S(2)}) collective-permute-start(bf16[4,128,128]{2,1,0:T(8,128)(2,1)S(1)} %collective-permute-done.5.refs_11_), channel_id=1, source_target_pairs={{0,8},{2,10},{4,12},{6,14},{1,9},{3,11},{5,13},{7,15},{16,24},{18,... | collective-permute-start | bytes 393224 | tf_op jit(solution)/shard_map/ppermute | solution.py:285
  40.4 0.0 collective-permute-done.8.refs_14_
  40.4 1.3 %collective-permute-start.7 = (bf16[4,128,128]{2,1,0:T(8,128)(2,1)S(1)}, bf16[4,128,128]{2,1,0:T(8,128)(2,1)S(1)}, u32[]{:S(2)}, u32[]{:S(2)}) collective-permute-start(bf16[4,128,128]{2,1,0:T(8,128)(2,1)S(1)} %collective-permute-done.5.refs_11_), channel_id=1, source_target_pairs={{0,4},{2,6},{4,8},{6,10},{8,12},{10,14},{1,5},{3,7},{5,9},{7,11},{... | collective-permute-start | bytes 393224 | tf_op jit(solution)/shard_map/ppermute | solution.py:285
  41.7 0.0 collective-permute-done.6.refs_12_
  41.8 0.7 collective-permute-start.10
  42.4 0.5 collective-permute-done.9.refs_15_
  42.9 0.7 collective-permute-start.11
  43.6 0.7 collective-permute-done.7.refs_13_
  44.3 0.0 collective-permute-done.10.refs_16_
  44.3 0.0 collective-permute-done.4.refs_9_
  44.3 0.0 collective-permute-done.3.refs_7_
  44.4 0.0 collective-permute-done.11.refs_17_
  44.4 0.0 copy-done.1
  44.4 0.0 copy-done.2
  44.4 0.0 copy-done.4
  44.4 9.0 %tree_attention_backward.1 = (f32[1,128]{1,0:T(1,128)}, bf16[128,1280]{1,0:T(8,128)(2,1)S(1)}, bf16[128,1280]{1,0:T(8,128)(2,1)S(1)}, bf16[2,4,128,128]{3,2,1,0:...) custom-call(s32[1]{0:T(128)} %bitcast.own_ref.refs_0_, ...), custom_call_target="tpu_custom_call" | custom-call | flops 2097152000 | bytes 8388608 | tf_op jit(solution)/shard_map/tree_attention_backward/pallas_call | solution.py:259
  53.4 0.7 collective-permute-start.14
  54.1 1.6 %collective-permute-start.12 = (bf16[128,1280]{1,0:T(8,128)(2,1)S(1)}, bf16[128,1280]{1,0:T(8,128)(2,1)S(1)}, u32[]{:S(2)}, u32[]{:S(2)}) collective-permute-start(bf16[128,1280]{1,0:T(8,128)(2,1)S(1)} %get-tuple-element.18), channel_id=1, source_target_pairs={{0,2},{2,0},{4,6},{6,4},{8,10},{10,8},{12,14},{14,12},{1,3},{3,1},... | collective-permute-start | bytes 983048 | tf_op jit(solution)/shard_map/ppermute | solution.py:285
  55.6 1.3 %collective-permute-start.13 = (bf16[2,4,128,128]{3,2,1,0:T(8,128)(2,1)S(1)}, bf16[2,4,128,128]{3,2,1,0:T(8,128)(2,1)S(1)}, u32[]{:S(2)}, u32[]{:S(2)}) collective-permute-start(bf16[2,4,128,128]{3,2,1,0:T(8,128)(2,1)S(1)} %get-tuple-element.20), channel_id=1, source_target_pairs={{4,0},{6,2},{8,4},{10,6},{12,8},{14,10},{5,1},{7,3},{9,5},{11,7},{... | collective-permute-start | bytes 786440 | tf_op jit(solution)/shard_map/ppermute | solution.py:285
  56.9 0.0 collective-permute-done.14
  56.9 0.1 add_convert_fusion.1
  57.0 1.3 %collective-permute-start.15 = (bf16[2,4,128,128]{3,2,1,0:T(8,128)(2,1)S(1)}, bf16[2,4,128,128]{3,2,1,0:T(8,128)(2,1)S(1)}, u32[]{:S(2)}, u32[]{:S(2)}) collective-permute-start(bf16[2,4,128,128]{3,2,1,0:T(8,128)(2,1)S(1)} %add_convert_fusion.1), channel_id=1, source_target_pairs={{8,0},{10,2},{12,4},{14,6},{9,1},{11,3},{13,5},{15,7},{24,16},{26,... | collective-permute-start | bytes 786440 | tf_op jit(solution)/shard_map/ppermute | solution.py:285
  58.3 2.9 %collective-permute-done.12 = bf16[128,1280]{1,0:T(8,128)(2,1)S(1)} collective-permute-done((bf16[128,1280]{1,0:T(8,128)(2,1)S(1)}, bf16[128,1280]{1,0:T(8,128)(2,1)S(1)}, u32[]{:S(2)}, u32[]{:S(2)}) %collective-permute-start.12) | collective-permute-done | bytes 327712 | tf_op jit(solution)/shard_map/ppermute | solution.py:285
  61.3 4.5 %collective-permute-done.13 = bf16[2,4,128,128]{3,2,1,0:T(8,128)(2,1)S(1)} collective-permute-done((bf16[2,4,128,128]{3,2,1,0:T(8,128)(2,1)S(1)}, bf16[2,4,128,128]{3,2,1,0:T(8,128)(2,1)S(1)}, u32[]{:S(2)}, u32[]{:S(2)}) %collective-permute-start.13) | collective-permute-done | bytes 262176 | tf_op jit(solution)/shard_map/ppermute | solution.py:285
  65.7 17.4 %collective-permute-done.15 = bf16[2,4,128,128]{3,2,1,0:T(8,128)(2,1)S(1)} collective-permute-done((bf16[2,4,128,128]{3,2,1,0:T(8,128)(2,1)S(1)}, bf16[2,4,128,128]{3,2,1,0:T(8,128)(2,1)S(1)}, u32[]{:S(2)}, u32[]{:S(2)}) %collective-permute-start.15) | collective-permute-done | bytes 262176 | tf_op jit(solution)/shard_map/ppermute | solution.py:285
  83.2 0.1 add_convert_fusion
  83.3 1.7 %collective-permute-start.16 = (bf16[4,128,128]{2,1,0:T(8,128)(2,1)S(1)}, bf16[4,128,128]{2,1,0:T(8,128)(2,1)S(1)}, u32[]{:S(2)}, u32[]{:S(2)}) collective-permute-start(bf16[4,128,128]{2,1,0:T(8,128)(2,1)S(1)} %slice_bitcast_fusion), channel_id=1, source_target_pairs={{0,2},{2,0},{4,6},{6,4},{8,10},{10,8},{12,14},{14,12},{1,3},{3,1},... | collective-permute-start | bytes 393224 | tf_op jit(solution)/shard_map/ppermute | solution.py:285
  85.0 0.9 pad_maximum_fusion
  85.9 2.5 %collective-permute-done.16 = bf16[4,128,128]{2,1,0:T(8,128)(2,1)S(1)} collective-permute-done((bf16[4,128,128]{2,1,0:T(8,128)(2,1)S(1)}, bf16[4,128,128]{2,1,0:T(8,128)(2,1)S(1)}, u32[]{:S(2)}, u32[]{:S(2)}) %collective-permute-start.16) | collective-permute-done | bytes 131104 | tf_op jit(solution)/shard_map/ppermute | solution.py:285
  88.4 0.1 copy.16
  88.5 0.1 copy.15
  88.6 0.1 copy.17
  88.8 0.8 copy.19
  89.6 0.1 copy.14
  89.7 0.8 copy.18
  (9 shorter events, 0.1 us)
Async XLA Ops:
  0.6 6.0 %copy-start = (bf16[128,2560]{1,0:T(8,128)(2,1)S(1)}, bf16[128,2560]{1,0:T(8,128)(2,1)}, u32[]{:S(2)}) copy-start(bf16[128,2560]{1,0:T(8,128)(2,1)} %refs_6_.1) | copy-start | bytes 1966084
  2.5 33.1 %collective-permute-start.5 = (bf16[4,128,128]{2,1,0:T(8,128)(2,1)}, bf16[4,128,128]{2,1,0:T(8,128)(2,1)S(1)}, u32[]{:S(2)}, u32[]{:S(2)}) collective-permute-start(bf16[4,128,128]{2,1,0:T(8,128)(2,1)} %get-tuple-element.16), channel_id=1, source_target_pairs={{0,2},{2,0},{4,6},{6,4},{8,10},{10,8},{12,14},{14,12},{1,3},{3,1},... | collective-permute-start | bytes 393224 | tf_op jit(solution)/shard_map/ppermute | solution.py:285
  5.4 3.3 %copy-start.5 = (f32[8,256]{1,0:T(8,128)S(1)}, f32[8,256]{1,0:T(8,128)}, u32[]{:S(2)}) copy-start(f32[8,256]{1,0:T(8,128)} %get-tuple-element.14) | copy-start | bytes 24580
  5.4 24.4 %copy-start.3 = (bf16[4,128,128]{2,1,0:T(8,128)(2,1)S(1)}, bf16[4,128,128]{2,1,0:T(8,128)(2,1)}, u32[]{:S(2)}) copy-start(bf16[4,128,128]{2,1,0:T(8,128)(2,1)} %get-tuple-element.15.refs_10_) | copy-start | bytes 393220
  5.4 38.9 %copy-start.1 = (bf16[128,2560]{1,0:T(8,128)(2,1)S(1)}, bf16[128,2560]{1,0:T(8,128)(2,1)}, u32[]{:S(2)}) copy-start(bf16[128,2560]{1,0:T(8,128)(2,1)} %refs_8_.1) | copy-start | bytes 1966084
  5.4 38.9 %copy-start.2 = (s32[8]{0:T(128)S(1)}, s32[8]{0:T(128)}, u32[]{:S(2)}) copy-start(s32[8]{0:T(128)} %refs_2_.1) | copy-start | bytes 100
  5.4 39.0 %copy-start.4 = (s32[8]{0:T(128)S(1)}, s32[8]{0:T(128)}, u32[]{:S(2)}) copy-start(s32[8]{0:T(128)} %refs_1_.1) | copy-start | bytes 100
  6.5 37.8 %collective-permute-start.4 = (bf16[128,1280]{1,0:T(8,128)(2,1)S(1)}, bf16[128,1280]{1,0:T(8,128)(2,1)S(1)}, u32[]{:S(2)}, u32[]{:S(2)}) collective-permute-start(bf16[128,1280]{1,0:T(8,128)(2,1)S(1)} %constant_dynamic-slice_fusion), channel_id=1, source_target_pairs={{0,2},{2,0},{4,6},{6,4},{8,10},{10,8},{12,14},{14,12},{1,3},{3,1},... | collective-permute-start | bytes 983048 | tf_op jit(solution)/shard_map/ppermute | solution.py:285
  6.7 37.7 %collective-permute-start.3 = (bf16[128,1280]{1,0:T(8,128)(2,1)S(1)}, bf16[128,1280]{1,0:T(8,128)(2,1)S(1)}, u32[]{:S(2)}, u32[]{:S(2)}) collective-permute-start(bf16[128,1280]{1,0:T(8,128)(2,1)S(1)} %constant_dynamic-slice_fusion.1), channel_id=1, source_target_pairs={{0,2},{2,0},{4,6},{6,4},{8,10},{10,8},{12,14},{14,12},{1,3},{3,1},... | collective-permute-start | bytes 983048 | tf_op jit(solution)/shard_map/ppermute | solution.py:285
  8.7 14.6 %collective-permute-start = (f32[8,256]{1,0:T(8,128)S(1)}, f32[8,256]{1,0:T(8,128)S(1)}, u32[]{:S(2)}, u32[]{:S(2)}) collective-permute-start(f32[8,256]{1,0:T(8,128)S(1)} %copy-done.5), channel_id=1, source_target_pairs={{0,2},{2,0},{4,6},{6,4},{8,10},{10,8},{12,14},{14,12},{1,3},{3,1},... | collective-permute-start | bytes 24584 | tf_op jit(solution)/shard_map/ppermute | solution.py:285
  23.4 3.7 %collective-permute-start.1 = (f32[8,256]{1,0:T(8,128)S(1)}, f32[8,256]{1,0:T(8,128)S(1)}, u32[]{:S(2)}, u32[]{:S(2)}) collective-permute-start(f32[8,256]{1,0:T(8,128)S(1)} %add.27), channel_id=1, source_target_pairs={{0,4},{2,6},{4,0},{6,2},{8,12},{10,14},{12,8},{14,10},{1,5},{3,7},... | collective-permute-start | bytes 24584 | tf_op jit(solution)/shard_map/ppermute | solution.py:285
  27.0 4.8 %collective-permute-start.2 = (f32[8,256]{1,0:T(8,128)S(1)}, f32[8,256]{1,0:T(8,128)S(1)}, u32[]{:S(2)}, u32[]{:S(2)}) collective-permute-start(f32[8,256]{1,0:T(8,128)S(1)} %add.28), channel_id=1, source_target_pairs={{0,8},{2,10},{4,12},{6,14},{8,0},{10,2},{12,4},{14,6},{1,9},{3,11}... | collective-permute-start | bytes 24584 | tf_op jit(solution)/shard_map/ppermute | solution.py:285
  29.9 10.6 %collective-permute-start.8 = (bf16[4,128,128]{2,1,0:T(8,128)(2,1)S(1)}, bf16[4,128,128]{2,1,0:T(8,128)(2,1)S(1)}, u32[]{:S(2)}, u32[]{:S(2)}) collective-permute-start(bf16[4,128,128]{2,1,0:T(8,128)(2,1)S(1)} %copy-done.3), channel_id=1, source_target_pairs={{0,8},{2,10},{4,12},{6,14},{1,9},{3,11},{5,13},{7,15},{16,24},{18,... | collective-permute-start | bytes 393224 | tf_op jit(solution)/shard_map/ppermute | solution.py:285
  31.9 9.9 %collective-permute-start.6 = (bf16[4,128,128]{2,1,0:T(8,128)(2,1)S(1)}, bf16[4,128,128]{2,1,0:T(8,128)(2,1)S(1)}, u32[]{:S(2)}, u32[]{:S(2)}) collective-permute-start(bf16[4,128,128]{2,1,0:T(8,128)(2,1)S(1)} %copy-done.3), channel_id=1, source_target_pairs={{0,4},{2,6},{4,8},{6,10},{8,12},{10,14},{1,5},{3,7},{5,9},{7,11},{... | collective-permute-start | bytes 393224 | tf_op jit(solution)/shard_map/ppermute | solution.py:285
  35.6 7.3 %collective-permute-start.9 = (bf16[4,128,128]{2,1,0:T(8,128)(2,1)S(1)}, bf16[4,128,128]{2,1,0:T(8,128)(2,1)S(1)}, u32[]{:S(2)}, u32[]{:S(2)}) collective-permute-start(bf16[4,128,128]{2,1,0:T(8,128)(2,1)S(1)} %collective-permute-done.5.refs_11_), channel_id=1, source_target_pairs={{0,8},{2,10},{4,12},{6,14},{1,9},{3,11},{5,13},{7,15},{16,24},{18,... | collective-permute-start | bytes 393224 | tf_op jit(solution)/shard_map/ppermute | solution.py:285
  40.4 3.9 %collective-permute-start.7 = (bf16[4,128,128]{2,1,0:T(8,128)(2,1)S(1)}, bf16[4,128,128]{2,1,0:T(8,128)(2,1)S(1)}, u32[]{:S(2)}, u32[]{:S(2)}) collective-permute-start(bf16[4,128,128]{2,1,0:T(8,128)(2,1)S(1)} %collective-permute-done.5.refs_11_), channel_id=1, source_target_pairs={{0,4},{2,6},{4,8},{6,10},{8,12},{10,14},{1,5},{3,7},{5,9},{7,11},{... | collective-permute-start | bytes 393224 | tf_op jit(solution)/shard_map/ppermute | solution.py:285
  41.8 2.6 %collective-permute-start.10 = (bf16[4,128,128]{2,1,0:T(8,128)(2,1)S(1)}, bf16[4,128,128]{2,1,0:T(8,128)(2,1)S(1)}, u32[]{:S(2)}, u32[]{:S(2)}) collective-permute-start(bf16[4,128,128]{2,1,0:T(8,128)(2,1)S(1)} %collective-permute-done.8.refs_14_), channel_id=1, source_target_pairs={{8,12},{10,14},{9,13},{11,15},{24,28},{26,30},{25,29},{27,31}} | collective-permute-start | bytes 393224 | tf_op jit(solution)/shard_map/ppermute | solution.py:285
  42.9 1.4 %collective-permute-start.11 = (bf16[4,128,128]{2,1,0:T(8,128)(2,1)S(1)}, bf16[4,128,128]{2,1,0:T(8,128)(2,1)S(1)}, u32[]{:S(2)}, u32[]{:S(2)}) collective-permute-start(bf16[4,128,128]{2,1,0:T(8,128)(2,1)S(1)} %collective-permute-done.9.refs_15_), channel_id=1, source_target_pairs={{8,12},{10,14},{9,13},{11,15},{24,28},{26,30},{25,29},{27,31}} | collective-permute-start | bytes 393224 | tf_op jit(solution)/shard_map/ppermute | solution.py:285
  53.4 3.5 %collective-permute-start.14 = (bf16[2,4,128,128]{3,2,1,0:T(8,128)(2,1)S(1)}, bf16[2,4,128,128]{3,2,1,0:T(8,128)(2,1)S(1)}, u32[]{:S(2)}, u32[]{:S(2)}) collective-permute-start(bf16[2,4,128,128]{3,2,1,0:T(8,128)(2,1)S(1)} %get-tuple-element.22), channel_id=1, source_target_pairs={{12,8},{14,10},{13,9},{15,11},{28,24},{30,26},{29,25},{31,27}} | collective-permute-start | bytes 786440 | tf_op jit(solution)/shard_map/ppermute | solution.py:285
  54.1 7.1 %collective-permute-start.12 = (bf16[128,1280]{1,0:T(8,128)(2,1)S(1)}, bf16[128,1280]{1,0:T(8,128)(2,1)S(1)}, u32[]{:S(2)}, u32[]{:S(2)}) collective-permute-start(bf16[128,1280]{1,0:T(8,128)(2,1)S(1)} %get-tuple-element.18), channel_id=1, source_target_pairs={{0,2},{2,0},{4,6},{6,4},{8,10},{10,8},{12,14},{14,12},{1,3},{3,1},... | collective-permute-start | bytes 983048 | tf_op jit(solution)/shard_map/ppermute | solution.py:285
  55.6 10.1 %collective-permute-start.13 = (bf16[2,4,128,128]{3,2,1,0:T(8,128)(2,1)S(1)}, bf16[2,4,128,128]{3,2,1,0:T(8,128)(2,1)S(1)}, u32[]{:S(2)}, u32[]{:S(2)}) collective-permute-start(bf16[2,4,128,128]{3,2,1,0:T(8,128)(2,1)S(1)} %get-tuple-element.20), channel_id=1, source_target_pairs={{4,0},{6,2},{8,4},{10,6},{12,8},{14,10},{5,1},{7,3},{9,5},{11,7},{... | collective-permute-start | bytes 786440 | tf_op jit(solution)/shard_map/ppermute | solution.py:285
  57.0 26.2 %collective-permute-start.15 = (bf16[2,4,128,128]{3,2,1,0:T(8,128)(2,1)S(1)}, bf16[2,4,128,128]{3,2,1,0:T(8,128)(2,1)S(1)}, u32[]{:S(2)}, u32[]{:S(2)}) collective-permute-start(bf16[2,4,128,128]{3,2,1,0:T(8,128)(2,1)S(1)} %add_convert_fusion.1), channel_id=1, source_target_pairs={{8,0},{10,2},{12,4},{14,6},{9,1},{11,3},{13,5},{15,7},{24,16},{26,... | collective-permute-start | bytes 786440 | tf_op jit(solution)/shard_map/ppermute | solution.py:285
  83.3 5.0 %collective-permute-start.16 = (bf16[4,128,128]{2,1,0:T(8,128)(2,1)S(1)}, bf16[4,128,128]{2,1,0:T(8,128)(2,1)S(1)}, u32[]{:S(2)}, u32[]{:S(2)}) collective-permute-start(bf16[4,128,128]{2,1,0:T(8,128)(2,1)S(1)} %slice_bitcast_fusion), channel_id=1, source_target_pairs={{0,2},{2,0},{4,6},{6,4},{8,10},{10,8},{12,14},{14,12},{1,3},{3,1},... | collective-permute-start | bytes 393224 | tf_op jit(solution)/shard_map/ppermute | solution.py:285

commit v3 on v2

v3 whole, which is shorter than its diff:
```python
import functools
import math

import jax
import jax.numpy as jnp
from jax import lax
from jax.experimental import pallas as pl
from jax.experimental.pallas import tpu as pltpu
from jax.sharding import PartitionSpec as P

HD = 128
DEPTH = 5
BETA = 0.1
LAMBDA_SEG = 0.7
PAIRED_GROUPS = 8
LOG2E = math.log2(math.e)


def lookup(table_values, lookup_ids):
    matches = lookup_ids[..., None] == jnp.arange(table_values.shape[0], dtype=jnp.int32)
    return jnp.sum(jnp.where(matches, table_values, 0), axis=-1)


def ancestors(parents, count):
    current = jnp.arange(parents.shape[0], dtype=jnp.int32)
    chain_list = []
    for depth_step in range(count):
        parent_ids = lookup(parents, current)
        current = jnp.where(current >= 0, parent_ids, -1)
        chain_list.append(current)
    return jnp.stack(chain_list, axis=1)


def token_terms(log_rate, own_len, rewards, logprobs, ref_logprobs, values):
    positions = lax.broadcasted_iota(jnp.int32, rewards.shape, 1)
    later = jnp.concatenate([values[:, 1:], values[:, :1]], axis=1)
    later = jnp.where(positions + 1 < own_len, later, 0.0)
    deltas = jnp.where(
        positions < own_len, rewards - BETA * (logprobs - ref_logprobs) + later - values, 0.0
    )
    powers = jnp.exp(positions.astype(jnp.float32) * log_rate)
    first_local = jnp.sum(deltas * powers, axis=1, keepdims=True)
    firsts = jnp.where(positions == 0, first_local, jnp.where(positions == 1, values[:, :1], 0.0))
    return deltas, firsts


def pack_kernel(
    log_rate,
    parts,
    own_ref,
    lengths_ref,
    k_ref,
    v_ref,
    rewards_ref,
    logprobs_ref,
    ref_logprobs_ref,
    values_ref,
    *out_refs,
):
    terms_ref = out_refs[-1]
    own = own_ref[0]
    heads = k_ref.shape[1] // HD // parts
    for step, out_ref in enumerate(out_refs[:-1]):
        part = lax.rem(own + step, parts)
        for h in range(heads):
            columns = pl.ds(pl.multiple_of((part * heads + h) * HD, HD), HD)
            out_ref[h, 0] = k_ref[:, columns]
            out_ref[h, 1] = v_ref[:, columns]
    length = k_ref.shape[0]
    deltas, firsts = token_terms(
        log_rate,
        lengths_ref[own],
        rewards_ref[...],
        logprobs_ref[...],
        ref_logprobs_ref[...],
        values_ref[...],
    )
    mine = lax.broadcasted_iota(jnp.int32, (terms_ref.shape[0], length), 0) == own
    terms_ref[:, :length] = jnp.where(mine, deltas, 0.0)
    terms_ref[:, length:] = jnp.where(mine, firsts, 0.0)


def pack(own, lengths, k, v, token_rows, parts, log_rate):
    length, width = k.shape
    smem = pl.BlockSpec(memory_space=pltpu.SMEM)
    vmem = pl.BlockSpec(memory_space=pltpu.VMEM)
    heads = width // HD // parts
    block = jax.ShapeDtypeStruct((heads, 2, length, HD), k.dtype)
    terms = jax.ShapeDtypeStruct((lengths.shape[0], 2 * length), jnp.float32)
    return pl.pallas_call(
        functools.partial(pack_kernel, log_rate, parts),
        out_shape=(block,) * parts + (terms,),
        in_specs=[smem] * 2 + [vmem] * 6,
        out_specs=(vmem,) * (parts + 1),
        cost_estimate=pl.CostEstimate(
            flops=length * 100, bytes_accessed=8 * length * width, transcendentals=length
        ),
        name="pack_keys_values",
    )(own, lengths, k, v, *token_rows)


def pack_queries_kernel(own_ref, q_ref, dir_ref, out_ref):
    other = 1 - lax.rem(own_ref[0], 2)
    heads = out_ref.shape[1]
    for h in range(heads):
        columns = pl.ds(pl.multiple_of((other * heads + h) * HD, HD), HD)
        out_ref[0, h] = q_ref[:, columns]
        out_ref[1, h] = dir_ref[:, columns]


def pack_queries(own, q, direction):
    length, width = q.shape
    smem = pl.BlockSpec(memory_space=pltpu.SMEM)
    vmem = pl.BlockSpec(memory_space=pltpu.VMEM)
    return pl.pallas_call(
        pack_queries_kernel,
        out_shape=jax.ShapeDtypeStruct((2, width // HD // 2, length, HD), q.dtype),
        in_specs=[smem, vmem, vmem],
        out_specs=vmem,
        cost_estimate=pl.CostEstimate(flops=0, bytes_accessed=6 * length * width, transcendentals=0),
        name="pack_queries",
    )(own, q, direction)


def prepare_kernel(
    log_rate,
    depth,
    segs,
    own_ref,
    parents_s,
    lengths_s,
    parents_ref,
    lengths_ref,
    terms_ref,
    row_ref,
    adv_ref,
    bias_ref,
):
    length = row_ref.shape[1]
    count = parents_s.shape[0]
    own = own_ref[0]
    part = lax.rem(own, segs)

    row_id = lax.broadcasted_iota(jnp.int32, (count, count), 0)
    col_id = lax.broadcasted_iota(jnp.int32, (count, count), 1)
    eye = row_id == col_id

    def to_row(col):
        return jnp.sum(jnp.where(eye, col, 0.0), axis=0, keepdims=True)

    children = (parents_ref[...] == row_id).astype(jnp.float32)
    weights = children / jnp.maximum(jnp.sum(children, axis=1, keepdims=True), 1.0)
    lens_col = jnp.sum(
        jnp.where(eye, lengths_ref[...].astype(jnp.float32), 0.0), axis=1, keepdims=True
    )
    first_local = terms_ref[:, length : length + 1]
    first_value = terms_ref[:, length + 1 : length + 2]
    later_value = jnp.sum(weights * to_row(first_value), axis=1, keepdims=True)
    base_term = first_local + jnp.exp((lens_col - 1.0) * log_rate) * later_value
    factor = jnp.exp(lens_col * log_rate)
    head = base_term
    for _ in range(depth):
        head = base_term + factor * jnp.sum(weights * to_row(head), axis=1, keepdims=True)
    later_head = jnp.sum(weights * to_row(head), axis=1, keepdims=True)

    t_id = lax.broadcasted_iota(jnp.int32, (length, length), 0)
    j_id = lax.broadcasted_iota(jnp.int32, (length, length), 1)
    offset = (j_id - t_id).astype(jnp.float32)
    discount = jnp.where(offset >= 0, jnp.exp(offset * log_rate), 0.0)
    t_col = lax.broadcasted_iota(jnp.int32, (length, 1), 0)
    seg_col = lax.broadcasted_iota(jnp.int32, (count, 1), 0)
    for i in range(segs):
        seg = own - part + lax.rem(part + i, segs)
        seg_len = lengths_s[seg]
        mine = seg_col == seg
        my_value = jnp.sum(jnp.where(mine, later_value, 0.0), axis=0, keepdims=True)
        my_head = jnp.sum(jnp.where(mine, later_head, 0.0), axis=0, keepdims=True)
        deltas = jnp.sum(jnp.where(mine, terms_ref[:, :length], 0.0), axis=0, keepdims=True)
        local_sum = jnp.sum(discount * deltas, axis=1, keepdims=True)
        left = (seg_len - t_col).astype(jnp.float32)
        advantage = jnp.where(
            t_col < seg_len,
            local_sum
            + jnp.exp((left - 1.0) * log_rate) * my_value
            + jnp.exp(left * log_rate) * my_head,
            0.0,
        )
        if i == 0:
            row_ref[...] = jnp.sum(jnp.where(t_id == j_id, advantage, 0.0), axis=0, keepdims=True)
        adv_ref[i] = jnp.broadcast_to(advantage, (length, HD))

        ancestor = seg
        for slot in range(depth):
            if slot > 0:
                ancestor = parent_of(ancestor, parents_s)
            slot_len = jnp.where(ancestor >= 0, lengths_s[jnp.maximum(ancestor, 0)], 0)
            seen = t_id < slot_len
            if slot == 0:
                seen = jnp.logical_and(seen, t_id <= j_id)
            bias_ref[i, slot * length : (slot + 1) * length, :] = jnp.where(seen, 0.0, -1e30)


def parent_of(segment, parents_s):
    known = parents_s[jnp.maximum(segment, 0)]
    return jnp.where(segment >= 0, known, -1).astype(jnp.int32)


def prepare(own, parents, lengths, terms, segs, log_rate):
    length = terms.shape[1] // 2
    smem = pl.BlockSpec(memory_space=pltpu.SMEM)
    vmem = pl.BlockSpec(memory_space=pltpu.VMEM)
    return pl.pallas_call(
        functools.partial(prepare_kernel, log_rate, DEPTH, segs),
        out_shape=(
            jax.ShapeDtypeStruct((1, length), jnp.float32),
            jax.ShapeDtypeStruct((segs, length, HD), jnp.float32),
            jax.ShapeDtypeStruct((segs, DEPTH * length, length), jnp.float32),
        ),
        in_specs=[smem] * 3 + [vmem] * 3,
        out_specs=(vmem,) * 3,
        cost_estimate=pl.CostEstimate(
            flops=200 * length * length,
            bytes_accessed=4 * (DEPTH + 1) * segs * length * length,
            transcendentals=length * length,
        ),
        name="prepare_advantages",
    )(own, parents, lengths, parents[None], lengths[None], terms)


def attend_kernel(group_size, depth, chunk, chunks, segs, *refs):
    own_ref, parents_s, adv_ref, bias_ref, q_ref, dir_ref = refs[:6]
    shared_refs = refs[6 : 5 + segs]
    refs = refs[5 + segs :]
    steps = (len(refs) - segs - 4) // 2
    kv_refs, dq_refs, dkv_refs = refs[:steps], refs[steps : steps + segs], refs[steps + segs : -4]
    kv_scr, p_scr, ds_scr, acc_scr = refs[-4:]

    length = q_ref.shape[0]
    own = own_ref[0]
    part = lax.rem(own, segs)
    for step in range(steps):
        for i in range(segs):
            kv_scr[step * segs + i] = kv_refs[step][i * chunks + chunk]
    acc_scr[...] = jnp.zeros_like(acc_scr)

    scale = HD**-0.5
    contract_last = (((1,), (1,)), ((), ()))
    contract_first = (((0,), (0,)), ((), ()))
    for i in range(segs):
        ancestor = own - part + lax.rem(part + i, segs)
        chosen = []
        for slot in range(depth):
            if slot > 0:
                ancestor = parent_of(ancestor, parents_s)
            if segs == 1:
                chosen.append(slot)
            else:
                known = jnp.maximum(ancestor, 0)
                step = (own - part) // segs - known // segs
                turn = lax.rem(lax.rem(known, segs) - part + segs, segs)
                chosen.append(jnp.where(ancestor >= 0, step * segs + turn, 0))
        if i == 0:
            first = (part * chunks + chunk) * group_size
            columns = [
                pl.ds(pl.multiple_of((first + j) * HD, HD), HD) for j in range(group_size)
            ]
            q_list = [q_ref[:, c] for c in columns]
            dir_list = [dir_ref[:, c] for c in columns]
        else:
            first = chunk * group_size
            q_list = [shared_refs[i - 1][0, first + j] for j in range(group_size)]
            dir_list = [shared_refs[i - 1][1, first + j] for j in range(group_size)]
        do_list = [(adv_ref[i] * d.astype(jnp.float32)).astype(jnp.bfloat16) for d in dir_list]
        k_all = jnp.concatenate([kv_scr[s, 0] for s in chosen], axis=0)
        v_all = jnp.concatenate([kv_scr[s, 1] for s in chosen], axis=0)
        for j in range(group_size):
            columns = slice(j * length, (j + 1) * length)
            scores = lax.dot_general(
                k_all, q_list[j], contract_last, preferred_element_type=jnp.float32
            )
            scores = scores * (scale * LOG2E) + bias_ref[i]
            top = jnp.max(scores, axis=0, keepdims=True)
            unnorm = jnp.exp2(scores - top)
            prob = unnorm * (1.0 / jnp.sum(unnorm, axis=0, keepdims=True))
            prob_low = prob.astype(jnp.bfloat16)
            dprob = lax.dot_general(
                v_all, do_list[j], contract_last, preferred_element_type=jnp.float32
            )
            row_dot = jnp.sum(prob_low.astype(jnp.float32) * dprob, axis=0, keepdims=True)
            dscore = (prob * (dprob - row_dot)).astype(jnp.bfloat16)
            p_scr[:, columns] = prob_low
            ds_scr[:, columns] = dscore
        dscore_all = ds_scr[...]
        dq_t = lax.dot_general(
            k_all, dscore_all, contract_first, preferred_element_type=jnp.float32
        )
        for j in range(group_size):
            dq_refs[i][:, j * HD : (j + 1) * HD] = (
                jnp.transpose(dq_t[:, j * length : (j + 1) * length]) * scale
            ).astype(jnp.bfloat16)
        q_all = jnp.concatenate(q_list, axis=0)
        do_all = jnp.concatenate(do_list, axis=0)
        dk_all = jnp.dot(dscore_all, q_all, preferred_element_type=jnp.float32) * scale
        dv_all = jnp.dot(p_scr[...], do_all, preferred_element_type=jnp.float32)
        for slot, s in enumerate(chosen):
            rows = slice(slot * length, (slot + 1) * length)
            acc_scr[s, 0] += dk_all[rows]
            acc_scr[s, 1] += dv_all[rows]
    for step in range(steps):
        for i in range(segs):
            dkv_refs[step][i] = acc_scr[step * segs + i].astype(jnp.bfloat16)


def attend(own, parents, advantages, bias, q, direction, shared, kv_list, chunk, chunks):
    segs, length = advantages.shape[:2]
    steps = len(kv_list)
    group_size = q.shape[1] // HD // chunks // segs
    width = group_size * HD
    keys = DEPTH * length
    smem = pl.BlockSpec(memory_space=pltpu.SMEM)
    vmem = pl.BlockSpec(memory_space=pltpu.VMEM)
    out_shape = (jax.ShapeDtypeStruct((length, width), jnp.bfloat16),) * segs + (
        jax.ShapeDtypeStruct((segs, 2, length, HD), jnp.bfloat16),
    ) * steps
    outs = pl.pallas_call(
        functools.partial(attend_kernel, group_size, DEPTH, chunk, chunks, segs),
        out_shape=out_shape,
        in_specs=[smem] * 2 + [vmem] * (4 + len(shared) + len(kv_list)),
        out_specs=(vmem,) * len(out_shape),
        scratch_shapes=[
            pltpu.VMEM((steps * segs, 2, length, HD), jnp.bfloat16),
            pltpu.VMEM((keys, width), jnp.bfloat16),
            pltpu.VMEM((keys, width), jnp.bfloat16),
            pltpu.VMEM((steps * segs, 2, length, HD), jnp.float32),
        ],
        compiler_params=pltpu.CompilerParams(vmem_limit_bytes=40 * 1024 * 1024),
        cost_estimate=pl.CostEstimate(
            flops=5 * 2 * keys * length * width * segs,
            bytes_accessed=8 * 1024 * 1024,
            transcendentals=keys * width * segs,
        ),
        name="tree_attention_backward",
    )(own, parents, advantages, bias, q, direction, *shared, *kv_list)
    return outs[:segs], outs[segs:]


def finish_kernel(chunks, own_ref, *refs):
    part = lax.rem(own_ref[0], 2)
    dq_refs, kv_refs = refs[: 2 * chunks], refs[2 * chunks : -3]
    dq_ref, dk_ref, dv_ref = refs[-3:]
    for side in range(2):
        where = part if side == 0 else 1 - part
        for chunk in range(chunks):
            block = dq_refs[side * chunks + chunk]
            width = block.shape[1]
            column = pl.multiple_of((where * chunks + chunk) * width, HD)
            dq_ref[:, pl.ds(column, width)] = block[...]
            columns = pl.ds(pl.multiple_of((where * chunks + chunk) * HD, HD), HD)
            block = kv_refs[side * chunks + chunk]
            dk_ref[:, columns] = block[0]
            dv_ref[:, columns] = block[1]


def finish(own, dq_list, kv_list):
    chunks = len(kv_list) // 2
    length, width = dq_list[0].shape
    smem = pl.BlockSpec(memory_space=pltpu.SMEM)
    vmem = pl.BlockSpec(memory_space=pltpu.VMEM)
    kv_out = jax.ShapeDtypeStruct((length, 2 * chunks * HD), jnp.bfloat16)
    return pl.pallas_call(
        functools.partial(finish_kernel, chunks),
        out_shape=(
            jax.ShapeDtypeStruct((length, 2 * chunks * width), jnp.bfloat16),
            kv_out,
            kv_out,
        ),
        in_specs=[smem] + [vmem] * (4 * chunks),
        out_specs=(vmem,) * 3,
        cost_estimate=pl.CostEstimate(
            flops=0, bytes_accessed=8 * length * width * chunks, transcendentals=0
        ),
        name="join_heads",
    )(own, *dq_list, *kv_list)


def permute(array, pairs):
    return lax.ppermute(array, "seg", pairs)


def after(array, *earlier):
    return lax.optimization_barrier((array, *earlier))[0]


def paired_body(own, queries, direction, key_vectors, value_vectors, token_rows, parents, lengths, log_rate):
    groups = lax.axis_size("seg")
    chunks = key_vectors.shape[1] // HD // 2
    swap = [(i, i ^ 1) for i in range(groups)]
    up = {d: [(i, i + 2 * d) for i in range(groups - 2 * d)] for d in (1, 2)}
    down = {d: [(i, i - 2 * d) for i in range(2 * d, groups)] for d in (1, 2, 3)}
    forward = [(i, i + 2) for i in range(4, groups - 2)]

    kept, given, terms = pack(own, lengths, key_vectors, value_vectors, token_rows, 2, log_rate)
    terms = terms + permute(terms, swap)
    taken = permute(given, swap)
    shares = pack_queries(own, after(queries, given), direction)
    near = jnp.concatenate([kept, taken])
    two = permute(near, up[2])
    one = permute(near, up[1])
    three = permute(two, forward)
    shared = permute(after(shares, near, terms), swap)
    for d in (1, 2):
        terms = terms + permute(terms, down[d])
    row, advantages, bias = prepare(own, parents, lengths, terms, 2, log_rate)
    blocks = [near, one, two, three]

    results = []
    for chunk in range(chunks):
        results.append(
            attend(
                own, parents, advantages, bias, queries, direction, [shared], blocks, chunk, chunks
            )
        )
    dq_own, dq_back, totals, totals_back = [], [], [], []
    for dq, dkv in results:
        arrived = [permute(dkv[d], down[d]) for d in (3, 2, 1)]
        dq_own.append(dq[0])
        dq_back.append(permute(dq[1], swap))
        near = after(dkv[0], results[-1][0][0])
        total = sum(block.astype(jnp.float32) for block in [near] + arrived).astype(jnp.bfloat16)
        totals.append(total[0])
        totals_back.append(permute(total[1], swap))
    grad_q, grad_k, grad_v = finish(own, dq_own + dq_back, totals + totals_back)
    return grad_q, grad_k, grad_v, row[0]


def fetch_rows(spread, wanted):
    routed = jnp.take(spread, jnp.maximum(wanted, 0), axis=0)
    return lax.all_to_all(routed, "seg", split_axis=0, concat_axis=2, tiled=True)


def return_rows(grad_rows, wanted, total_segs):
    returned = lax.all_to_all(grad_rows, "seg", split_axis=2, concat_axis=0, tiled=True)
    piece_len = returned.shape[2]
    feature_len = returned.shape[3]
    routed_ids = wanted.reshape(-1)
    targets = jnp.where(routed_ids >= 0, routed_ids, total_segs)
    summed = jax.ops.segment_sum(
        returned.reshape(-1, piece_len * feature_len).astype(jnp.float32),
        targets,
        num_segments=total_segs + 1,
    )[:total_segs]
    return lax.all_to_all(
        summed.reshape(total_segs, piece_len, feature_len),
        "seg",
        split_axis=0,
        concat_axis=1,
        tiled=True,
    )


def routed_body(own, queries, direction, key_vectors, value_vectors, token_rows, parents, lengths, log_rate):
    total_segs = parents.shape[0]
    length = queries.shape[0]
    block, terms = pack(own, lengths, key_vectors, value_vectors, token_rows, 1, log_rate)
    heads = block.shape[0]
    mine = lax.dynamic_slice_in_dim(terms, own[0], 1)
    terms = lax.all_gather(mine, "seg", axis=0, tiled=True)
    row, advantages, bias = prepare(own, parents, lengths, terms, 1, log_rate)
    flat = jnp.concatenate([key_vectors, value_vectors], axis=1)[None]
    spread = lax.all_to_all(flat, "seg", split_axis=1, concat_axis=0, tiled=True)
    chains = ancestors(parents, DEPTH - 1)
    arrived = fetch_rows(spread, chains)[0]
    slot_kv = jnp.concatenate([flat, arrived]).reshape(DEPTH, length, 2, heads, HD)
    slot_kv = jnp.transpose(slot_kv, (0, 3, 2, 1, 4))
    kv_list = [slot_kv[slot] for slot in range(DEPTH)]
    dq_list, dkv_list = [], []
    for head in range(heads):
        dq, dkv = attend(
            own, parents, advantages, bias, queries, direction, [], kv_list, head, heads
        )
        dq_list.append(dq[0])
        dkv_list.append(jnp.concatenate(dkv))
    rows = jnp.transpose(jnp.stack(dkv_list), (1, 3, 2, 0, 4)).reshape(1, DEPTH, length, -1)
    summed = return_rows(rows[:, 1:], chains, total_segs)[0] + rows[0, 0].astype(jnp.float32)
    width = key_vectors.shape[1]
    grad_keys = summed[:, :width].astype(jnp.bfloat16)
    grad_values = summed[:, width:].astype(jnp.bfloat16)
    return jnp.concatenate(dq_list, axis=1), grad_keys, grad_values, row[0]


def body(
    queries,
    key_vectors,
    value_vectors,
    direction,
    rewards,
    logprobs,
    ref_logprobs,
    value_est,
    parents,
    seg_lengths,
):
    groups = lax.axis_size("seg")
    assert parents.shape[0] == groups
    own = jnp.reshape(lax.axis_index("seg"), (1,))
    log_rate = math.log(LAMBDA_SEG) / rewards.shape[0]
    token_rows = [rewards[None], logprobs[None], ref_logprobs[None], value_est[None]]
    plan = paired_body if groups == PAIRED_GROUPS else routed_body
    return plan(
        own, queries, direction, key_vectors, value_vectors, token_rows, parents, seg_lengths, log_rate
    )


def solution(mesh):
    in_specs = (
        P(("grp", "seg"), "tp"),
        P(("grp", "seg"), "tp"),
        P(("grp", "seg"), "tp"),
        P(("grp", "seg"), "tp"),
        P(("grp", "seg")),
        P(("grp", "seg")),
        P(("grp", "seg")),
        P(("grp", "seg")),
        P("grp"),
        P("grp"),
    )
    out_specs = (
        P(("grp", "seg"), "tp"),
        P(("grp", "seg"), "tp"),
        P(("grp", "seg"), "tp"),
        P(("grp", "seg")),
    )
    return jax.shard_map(body, mesh=mesh, in_specs=in_specs, out_specs=out_specs, check_vma=False)
```

time: 90.8 us -> 84.8 us (0.934)
  waiting for transfers between devices: 44.9 us -> 31.6 us
  Pallas kernels: 10.8 us -> 18.1 us
  local copies, waits for them, and re-layouts: 3.16 us -> 6.13 us
  starting transfers between devices: 29.5 us -> 26.9 us
    ppermute x17 -> x18, waiting for transfers between devices: 44.9 us -> 31.6 us  [permute(): return lax.ppermute(array, 'seg', pairs)]
    pallas_call x1 -> x5, Pallas kernels: 9 us -> 16.3 us  [the longest x2 8.95 us: attend(): pl.pallas_call(functools.partial(attend_kernel, group_size, DEPTH, chunk,...]
    unnamed x14 -> x27, local copies, waits for them, and re-layouts: 1.57 us -> 4.84 us
    ppermute x17 -> x18, starting transfers between devices: 29.5 us -> 26.9 us  [permute(): return lax.ppermute(array, 'seg', pairs)]
    squeeze x1 -> x2, local copies, waits for them, and re-layouts: 0.01 us -> 1.27 us  [paired_body(): totals_back.append(permute(total[1], swap))]
    dynamic_slice x2 -> x0, local copies, waits for them, and re-layouts: 1.1 us -> none  [the longest x1 1.07 us: paired_body(): lax.dynamic_slice_in_dim(direction, (1 - part) * half, half, 1)]
  transfers between devices with their start and end apart: 17 -> 18, of which waited for: 8 -> 8; matrix products, arithmetic and copies ran while one was open for 2% -> 3% of each run, Pallas kernels for 0% -> 11%
where the time goes in v3:
time: 84.8 us; the launch traced here: 84.3 us
  waiting for transfers between devices  31.6 us (37%)
  starting transfers between devices  26.9 us (32%)
  Pallas kernels  18.1 us (21%)
  local copies, waits for them, and re-layouts  6.13 us (7%)
  between operations  0.91 us (1%)
    ppermute x18, waiting for transfers between devices, permute(): return lax.ppermute(array, 'seg', pairs)  31.6 us
    ppermute x18, starting transfers between devices, permute(): return lax.ppermute(array, 'seg', pairs)  26.9 us
    pallas_call x2, Pallas kernels, attend(): pl.pallas_call(functools.partial(attend_kernel, group_size, DEPTH, chunk,...  8.95 us
    unnamed x27, local copies, waits for them, and re-layouts  4.84 us
    pallas_call x1, Pallas kernels, prepare(): pl.pallas_call(functools.partial(prepare_kernel, log_rate, DEPTH, segs),...  2.82 us
    pallas_call x1, Pallas kernels, pack_queries(): pl.pallas_call(pack_queries_kernel, out_shape=jax.ShapeDtypeStruct((2, wi...  2.35 us
    pallas_call x1, Pallas kernels, finish(): pl.pallas_call(functools.partial(finish_kernel, chunks), out_shape=(jax.S...  2.2 us
    pallas_call x1, Pallas kernels, pack(): pl.pallas_call(functools.partial(pack_kernel, log_rate, parts), out_shape...  1.78 us
  transfers between devices with their start and end apart: 18, of which 8 were waited for; matrix products, arithmetic and copies ran while one was open for 3% of the time, Pallas kernels for 11%

profile of v3, /device:TPU:0, one launch (start us, length us, event | category | flops | bytes accessed | tf_op | source)
XLA Modules:
  0.0 84.3 jit_solution(5150417155211208752)
XLA Ops:
  0.6 1.8 %pack_keys_values.1 = (bf16[2,2,128,128]{3,2,1,0:T(8,128)(2,1)}, bf16[2,2,128,128]{3,2,1,0:T(8,128)(2,1)}, f32[8,256]{1,0:T(8,128)}) custom-call(s32[1]{0:T(128)} %bitcast.own_ref.refs_0_, s32[8]{0:T(128)} %lengths_s.1, bf16[128,512]{1,0:T(8,128)(2,1)} %k_ref.1, bf16[128,512]{1,0:T(8,128)(2,1)} %v_ref.1, f32[1,128]{1,0:T(1,128)} %bitcast.17, ...), custom_call_target="tpu_custom_call" | custom-call | flops 12800 | bytes 524288 | tf_op jit(solution)/shard_map/pack_keys_values/pallas_call | solution.py:90
  2.4 2.9 %collective-permute-start.3 = (bf16[2,2,128,128]{3,2,1,0:T(8,128)(2,1)}, bf16[2,2,128,128]{3,2,1,0:T(8,128)(2,1)S(1)}, u32[]{:S(2)}, u32[]{:S(2)}) collective-permute-start(bf16[2,2,128,128]{3,2,1,0:T(8,128)(2,1)} %get-tuple-element.32), channel_id=1, source_target_pairs={{0,2},{2,0},{4,6},{6,4},{8,10},{10,8},{12,14},{14,12},{1,3},{3,1},... | collective-permute-start | bytes 393224 | tf_op jit(solution)/shard_map/ppermute | solution.py:387
  5.4 0.0 collective-permute-start
  5.4 0.9 %constant_dynamic-update-slice_fusion.1 = bf16[4,2,128,128]{3,2,1,0:T(8,128)(2,1)S(1)} fusion(bf16[2,2,128,128]{3,2,1,0:T(8,128)(2,1)} %get-tuple-element.34), kind=kLoop, calls=%fused_computation.7 | loop fusion | bytes 262144
  6.3 0.0 copy-start.12
  6.3 0.0 copy-start
  6.3 0.0 copy-start.1
  6.3 2.3 %pack_queries.1 = bf16[2,10,128,128]{3,2,1,0:T(8,128)(2,1)} custom-call(s32[1]{0:T(128)} %bitcast.own_ref.refs_0_, bf16[128,2560]{1,0:T(8,128)(2,1)} %refs_4_.3, bf16[128,2560]{1,0:T(8,128)(2,1)} %refs_5_.3), custom_call_target="tpu_custom_call" | custom-call | bytes 1966080 | tf_op jit(solution)/shard_map/pack_queries/pallas_call | solution.py:115
  8.7 0.5 collective-permute-done
  9.2 0.0 copy-done.12
  9.2 0.0 collective-permute-done.3
  9.3 1.8 %collective-permute-start.4 = (bf16[2,10,128,128]{3,2,1,0:T(8,128)(2,1)}, bf16[2,10,128,128]{3,2,1,0:T(8,128)(2,1)S(1)}, u32[]{:S(2)}, u32[]{:S(2)}) collective-permute-start(bf16[2,10,128,128]{3,2,1,0:T(8,128)(2,1)} %pack_queries.1), channel_id=1, source_target_pairs={{0,2},{2,0},{4,6},{6,4},{8,10},{10,8},{12,14},{14,12},{1,3},{3,1},... | collective-permute-start | bytes 1966088 | tf_op jit(solution)/shard_map/ppermute | solution.py:387
  11.1 4.5 %collective-permute-start.6 = (bf16[4,2,128,128]{3,2,1,0:T(8,128)(2,1)S(1)}, bf16[4,2,128,128]{3,2,1,0:T(8,128)(2,1)S(1)}, u32[]{:S(2)}, u32[]{:S(2)}) collective-permute-start(bf16[4,2,128,128]{3,2,1,0:T(8,128)(2,1)S(1)} %constant_dynamic-update-slice_fusion.refs_7_), channel_id=1, source_target_pairs={{0,8},{2,10},{4,12},{6,14},{1,9},{3,11},{5,13},{7,15},{16,24},{18,... | collective-permute-start | bytes 786440 | tf_op jit(solution)/shard_map/ppermute | solution.py:387
  15.6 3.5 %collective-permute-start.5 = (bf16[4,2,128,128]{3,2,1,0:T(8,128)(2,1)S(1)}, bf16[4,2,128,128]{3,2,1,0:T(8,128)(2,1)S(1)}, u32[]{:S(2)}, u32[]{:S(2)}) collective-permute-start(bf16[4,2,128,128]{3,2,1,0:T(8,128)(2,1)S(1)} %constant_dynamic-update-slice_fusion.refs_7_), channel_id=1, source_target_pairs={{0,4},{2,6},{4,8},{6,10},{8,12},{10,14},{1,5},{3,7},{5,9},{7,11},{... | collective-permute-start | bytes 786440 | tf_op jit(solution)/shard_map/ppermute | solution.py:387
  19.1 3.2 %collective-permute-done.6.refs_9_ = bf16[4,2,128,128]{3,2,1,0:T(8,128)(2,1)S(1)} collective-permute-done((bf16[4,2,128,128]{3,2,1,0:T(8,128)(2,1)S(1)}, bf16[4,2,128,128]{3,2,1,0:T(8,128)(2,1)S(1)}, u32[]{:S(2)}, u32[]{:S(2)}) %collective-permute-start.6) | collective-permute-done | bytes 262176 | tf_op jit(solution)/shard_map/ppermute | solution.py:387
  22.3 0.7 collective-permute-start.7
  23.0 1.3 %collective-permute-start.1 = (f32[8,256]{1,0:T(8,128)S(1)}, f32[8,256]{1,0:T(8,128)S(1)}, u32[]{:S(2)}, u32[]{:S(2)}) collective-permute-start(f32[8,256]{1,0:T(8,128)S(1)} %add.27), channel_id=1, source_target_pairs={{4,0},{6,2},{8,4},{10,6},{12,8},{14,10},{5,1},{7,3},{9,5},{11,7},{... | collective-permute-start | bytes 24584 | tf_op jit(solution)/shard_map/ppermute | solution.py:387
  24.3 7.1 %collective-permute-done.1 = f32[8,256]{1,0:T(8,128)S(1)} collective-permute-done((f32[8,256]{1,0:T(8,128)S(1)}, f32[8,256]{1,0:T(8,128)S(1)}, u32[]{:S(2)}, u32[]{:S(2)}) %collective-permute-start.1) | collective-permute-done | bytes 8224 | tf_op jit(solution)/shard_map/ppermute | solution.py:387
  31.4 1.3 %collective-permute-start.2 = (f32[8,256]{1,0:T(8,128)S(1)}, f32[8,256]{1,0:T(8,128)S(1)}, u32[]{:S(2)}, u32[]{:S(2)}) collective-permute-start(f32[8,256]{1,0:T(8,128)S(1)} %add.28), channel_id=1, source_target_pairs={{8,0},{10,2},{12,4},{14,6},{9,1},{11,3},{13,5},{15,7},{24,16},{26,... | collective-permute-start | bytes 24584 | tf_op jit(solution)/shard_map/ppermute | solution.py:387
  32.7 8.2 %collective-permute-done.2 = f32[8,256]{1,0:T(8,128)S(1)} collective-permute-done((f32[8,256]{1,0:T(8,128)S(1)}, f32[8,256]{1,0:T(8,128)S(1)}, u32[]{:S(2)}, u32[]{:S(2)}) %collective-permute-start.2) | collective-permute-done | bytes 8224 | tf_op jit(solution)/shard_map/ppermute | solution.py:387
  41.0 0.6 add.29.terms_ref
  41.6 2.8 %prepare_advantages.1 = (f32[1,128]{1,0:T(1,128)}, f32[2,128,128]{2,1,0:T(8,128)}, f32[2,640,128]{2,1,0:T(8,128)}) custom-call(s32[1]{0:T(128)} %bitcast.own_ref.refs_0_, s32[8]{0:T(128)} %refs_1_.3, s32[8]{0:T(128)} %lengths_s.1, s32[1,8]{1,0:T(1,128)} %bitcast.16, s32[1,8]{1,0:T(1,128)} %bitcast.21, f32[8,256]{1,0:T(8,128)} %add.29.terms_ref), custom_call_target="tpu_custom_call" | custom-call | flops 3276800 | bytes 786432 | tf_op jit(solution)/shard_map/prepare_advantages/pallas_call | solution.py:212
  44.4 0.0 collective-permute-done.5.refs_8_
  44.4 0.0 collective-permute-done.7.refs_10_
  44.4 0.0 collective-permute-done.4.refs_6_
  44.4 0.0 copy-start.4
  44.4 0.0 copy-done
  44.4 0.0 copy-done.1
  44.4 0.6 copy-done.4
  45.1 1.1 %copy-done.5 = f32[2,640,128]{2,1,0:T(8,128)S(1)} copy-done((f32[2,640,128]{2,1,0:T(8,128)S(1)}, f32[2,640,128]{2,1,0:T(8,128)}, u32[]{:S(2)}) %copy-start.5) | copy-done | bytes 655384
  46.1 0.9 %copy-done.6 = f32[2,128,128]{2,1,0:T(8,128)S(1)} copy-done((f32[2,128,128]{2,1,0:T(8,128)S(1)}, f32[2,128,128]{2,1,0:T(8,128)}, u32[]{:S(2)}) %copy-start.6) | copy-done | bytes 131096
  47.1 4.5 %tree_attention_backward.3 = (bf16[128,640]{1,0:T(8,128)(2,1)S(1)}, bf16[128,640]{1,0:T(8,128)(2,1)S(1)}, bf16[2,2,128,128]{3,2,1,0:T(8,128)(2,1)S(1)}, bf16[2,2...) custom-call(s32[1]{0:T(128)} %bitcast.own_ref.refs_0_, ...), custom_call_target="tpu_custom_call" | custom-call | flops 1048576000 | bytes 8388608 | tf_op jit(solution)/shard_map/tree_attention_backward/pallas_call | solution.py:325
  51.5 0.0 copy-start.2
  51.5 0.7 copy-done.2
  52.2 1.3 %collective-permute-start.13 = (bf16[2,2,128,128]{3,2,1,0:T(8,128)(2,1)S(1)}, bf16[2,2,128,128]{3,2,1,0:T(8,128)(2,1)S(1)}, u32[]{:S(2)}, u32[]{:S(2)}) collective-permute-start(bf16[2,2,128,128]{3,2,1,0:T(8,128)(2,1)S(1)} %get-tuple-element.47), channel_id=1, source_target_pairs={{12,0},{14,2},{13,1},{15,3},{28,16},{30,18},{29,17},{31,19}} | collective-permute-start | bytes 393224 | tf_op jit(solution)/shard_map/ppermute | solution.py:387
  53.5 1.3 %collective-permute-start.14 = (bf16[2,2,128,128]{3,2,1,0:T(8,128)(2,1)S(1)}, bf16[2,2,128,128]{3,2,1,0:T(8,128)(2,1)S(1)}, u32[]{:S(2)}, u32[]{:S(2)}) collective-permute-start(bf16[2,2,128,128]{3,2,1,0:T(8,128)(2,1)S(1)} %get-tuple-element.48), channel_id=1, source_target_pairs={{8,0},{10,2},{12,4},{14,6},{9,1},{11,3},{13,5},{15,7},{24,16},{26,... | collective-permute-start | bytes 393224 | tf_op jit(solution)/shard_map/ppermute | solution.py:387
  54.8 1.3 %collective-permute-start.15 = (bf16[2,2,128,128]{3,2,1,0:T(8,128)(2,1)S(1)}, bf16[2,2,128,128]{3,2,1,0:T(8,128)(2,1)S(1)}, u32[]{:S(2)}, u32[]{:S(2)}) collective-permute-start(bf16[2,2,128,128]{3,2,1,0:T(8,128)(2,1)S(1)} %get-tuple-element.49), channel_id=1, source_target_pairs={{4,0},{6,2},{8,4},{10,6},{12,8},{14,10},{5,1},{7,3},{9,5},{11,7},{... | collective-permute-start | bytes 393224 | tf_op jit(solution)/shard_map/ppermute | solution.py:387
  56.1 0.0 copy-done.7
  56.1 4.5 %tree_attention_backward.2 = (bf16[128,640]{1,0:T(8,128)(2,1)S(1)}, bf16[128,640]{1,0:T(8,128)(2,1)S(1)}, bf16[2,2,128,128]{3,2,1,0:T(8,128)(2,1)S(1)}, bf16[2,2...) custom-call(s32[1]{0:T(128)} %bitcast.own_ref.refs_0_, ...), custom_call_target="tpu_custom_call" | custom-call | flops 1048576000 | bytes 8388608 | tf_op jit(solution)/shard_map/tree_attention_backward/pallas_call | solution.py:325
  60.6 0.0 copy-start.3
  60.6 1.3 %collective-permute-start.10 = (bf16[2,2,128,128]{3,2,1,0:T(8,128)(2,1)S(1)}, bf16[2,2,128,128]{3,2,1,0:T(8,128)(2,1)S(1)}, u32[]{:S(2)}, u32[]{:S(2)}) collective-permute-start(bf16[2,2,128,128]{3,2,1,0:T(8,128)(2,1)S(1)} %get-tuple-element.42), channel_id=1, source_target_pairs={{12,0},{14,2},{13,1},{15,3},{28,16},{30,18},{29,17},{31,19}} | collective-permute-start | bytes 393224 | tf_op jit(solution)/shard_map/ppermute | solution.py:387
  61.9 1.3 %collective-permute-start.11 = (bf16[2,2,128,128]{3,2,1,0:T(8,128)(2,1)S(1)}, bf16[2,2,128,128]{3,2,1,0:T(8,128)(2,1)S(1)}, u32[]{:S(2)}, u32[]{:S(2)}) collective-permute-start(bf16[2,2,128,128]{3,2,1,0:T(8,128)(2,1)S(1)} %get-tuple-element.43), channel_id=1, source_target_pairs={{8,0},{10,2},{12,4},{14,6},{9,1},{11,3},{13,5},{15,7},{24,16},{26,... | collective-permute-start | bytes 393224 | tf_op jit(solution)/shard_map/ppermute | solution.py:387
  63.2 0.0 collective-permute-done.13
  63.2 1.3 %collective-permute-start.12 = (bf16[2,2,128,128]{3,2,1,0:T(8,128)(2,1)S(1)}, bf16[2,2,128,128]{3,2,1,0:T(8,128)(2,1)S(1)}, u32[]{:S(2)}, u32[]{:S(2)}) collective-permute-start(bf16[2,2,128,128]{3,2,1,0:T(8,128)(2,1)S(1)} %get-tuple-element.44), channel_id=1, source_target_pairs={{4,0},{6,2},{8,4},{10,6},{12,8},{14,10},{5,1},{7,3},{9,5},{11,7},{... | collective-permute-start | bytes 393224 | tf_op jit(solution)/shard_map/ppermute | solution.py:387
  64.5 0.8 collective-permute-done.14
  65.3 0.5 collective-permute-start.9
  65.8 0.0 collective-permute-done.15
  65.8 1.5 %collective-permute-start.8 = (bf16[128,640]{1,0:T(8,128)(2,1)S(1)}, bf16[128,640]{1,0:T(8,128)(2,1)S(1)}, u32[]{:S(2)}, u32[]{:S(2)}) collective-permute-start(bf16[128,640]{1,0:T(8,128)(2,1)S(1)} %get-tuple-element.38), channel_id=1, source_target_pairs={{0,2},{2,0},{4,6},{6,4},{8,10},{10,8},{12,14},{14,12},{1,3},{3,1},... | collective-permute-start | bytes 491528 | tf_op jit(solution)/shard_map/ppermute | solution.py:387
  67.3 0.1 add_convert_fusion
  67.4 0.6 slice_bitcast_fusion
  68.0 3.2 %collective-permute-done.10 = bf16[2,2,128,128]{3,2,1,0:T(8,128)(2,1)S(1)} collective-permute-done((bf16[2,2,128,128]{3,2,1,0:T(8,128)(2,1)S(1)}, bf16[2,2,128,128]{3,2,1,0:T(8,128)(2,1)S(1)}, u32[]{:S(2)}, u32[]{:S(2)}) %collective-permute-start.10) | collective-permute-done | bytes 131104 | tf_op jit(solution)/shard_map/ppermute | solution.py:387
  71.2 0.6 collective-permute-start.17
  71.8 4.7 %collective-permute-done.11 = bf16[2,2,128,128]{3,2,1,0:T(8,128)(2,1)S(1)} collective-permute-done((bf16[2,2,128,128]{3,2,1,0:T(8,128)(2,1)S(1)}, bf16[2,2,128,128]{3,2,1,0:T(8,128)(2,1)S(1)}, u32[]{:S(2)}, u32[]{:S(2)}) %collective-permute-start.11) | collective-permute-done | bytes 131104 | tf_op jit(solution)/shard_map/ppermute | solution.py:387
  76.5 0.0 collective-permute-done.12
  76.5 0.1 add_convert_fusion.1
  76.6 0.6 slice_bitcast_fusion.1
  77.2 0.5 collective-permute-start.16
  77.8 0.0 collective-permute-done.9.refs_3_
  77.8 0.0 collective-permute-done.8.refs_2_
  77.8 0.0 collective-permute-done.17.refs_7_
  77.8 3.7 %collective-permute-done.16.refs_6_ = bf16[2,128,128]{2,1,0:T(8,128)(2,1)S(1)} collective-permute-done((bf16[2,128,128]{2,1,0:T(8,128)(2,1)S(1)}, bf16[2,128,128]{2,1,0:T(8,128)(2,1)S(1)}, u32[]{:S(2)}, u32[]{:S(2)}) %collective-permute-start.16) | collective-permute-done | bytes 65568 | tf_op jit(solution)/shard_map/ppermute | solution.py:387
  81.5 0.0 copy-done.8
  81.5 0.6 copy-done.11
  82.1 2.2 %join_heads.1 = (bf16[128,2560]{1,0:T(8,128)(2,1)}, bf16[128,512]{1,0:T(8,128)(2,1)}, bf16[128,512]{1,0:T(8,128)(2,1)}) custom-call(s32[1]{0:T(128)} %bitcast.own_ref.refs_0_, bf16[128,640]{1,0:T(8,128)(2,1)} %copy-done.3, bf16[128,640]{1,0:T(8,128)(2,1)} %copy-done.2, bf16[128,640]{1,0:T(8,128)(2,1)} %copy-done.9, bf16[128,640]{1,0:T(8,128)(2,1)} %copy-done.8, ...), custom_call_target="tpu_custom_call" | custom-call | bytes 1310720 | tf_op jit(solution)/shard_map/join_heads/pallas_call | solution.py:370
  (13 shorter events, 0.0 us)
Async XLA Ops:
  2.4 6.8 %collective-permute-start.3 = (bf16[2,2,128,128]{3,2,1,0:T(8,128)(2,1)}, bf16[2,2,128,128]{3,2,1,0:T(8,128)(2,1)S(1)}, u32[]{:S(2)}, u32[]{:S(2)}) collective-permute-start(bf16[2,2,128,128]{3,2,1,0:T(8,128)(2,1)} %get-tuple-element.32), channel_id=1, source_target_pairs={{0,2},{2,0},{4,6},{6,4},{8,10},{10,8},{12,14},{14,12},{1,3},{3,1},... | collective-permute-start | bytes 393224 | tf_op jit(solution)/shard_map/ppermute | solution.py:387
  5.4 3.9 %collective-permute-start = (f32[8,256]{1,0:T(8,128)}, f32[8,256]{1,0:T(8,128)S(1)}, u32[]{:S(2)}, u32[]{:S(2)}) collective-permute-start(f32[8,256]{1,0:T(8,128)} %get-tuple-element.29), channel_id=1, source_target_pairs={{0,2},{2,0},{4,6},{6,4},{8,10},{10,8},{12,14},{14,12},{1,3},{3,1},... | collective-permute-start | bytes 24584 | tf_op jit(solution)/shard_map/ppermute | solution.py:387
  6.3 2.9 %copy-start.12 = (f32[8,256]{1,0:T(8,128)S(1)}, f32[8,256]{1,0:T(8,128)}, u32[]{:S(2)}) copy-start(f32[8,256]{1,0:T(8,128)} %get-tuple-element.29) | copy-start | bytes 24580
  6.3 38.1 %copy-start = (bf16[128,2560]{1,0:T(8,128)(2,1)S(1)}, bf16[128,2560]{1,0:T(8,128)(2,1)}, u32[]{:S(2)}) copy-start(bf16[128,2560]{1,0:T(8,128)(2,1)} %refs_4_.3) | copy-start | bytes 1966084
  6.3 38.1 %copy-start.1 = (bf16[128,2560]{1,0:T(8,128)(2,1)S(1)}, bf16[128,2560]{1,0:T(8,128)(2,1)}, u32[]{:S(2)}) copy-start(bf16[128,2560]{1,0:T(8,128)(2,1)} %refs_5_.3) | copy-start | bytes 1966084
  9.3 35.1 %collective-permute-start.4 = (bf16[2,10,128,128]{3,2,1,0:T(8,128)(2,1)}, bf16[2,10,128,128]{3,2,1,0:T(8,128)(2,1)S(1)}, u32[]{:S(2)}, u32[]{:S(2)}) collective-permute-start(bf16[2,10,128,128]{3,2,1,0:T(8,128)(2,1)} %pack_queries.1), channel_id=1, source_target_pairs={{0,2},{2,0},{4,6},{6,4},{8,10},{10,8},{12,14},{14,12},{1,3},{3,1},... | collective-permute-start | bytes 1966088 | tf_op jit(solution)/shard_map/ppermute | solution.py:387
  11.1 11.2 %collective-permute-start.6 = (bf16[4,2,128,128]{3,2,1,0:T(8,128)(2,1)S(1)}, bf16[4,2,128,128]{3,2,1,0:T(8,128)(2,1)S(1)}, u32[]{:S(2)}, u32[]{:S(2)}) collective-permute-start(bf16[4,2,128,128]{3,2,1,0:T(8,128)(2,1)S(1)} %constant_dynamic-update-slice_fusion.refs_7_), channel_id=1, source_target_pairs={{0,8},{2,10},{4,12},{6,14},{1,9},{3,11},{5,13},{7,15},{16,24},{18,... | collective-permute-start | bytes 786440 | tf_op jit(solution)/shard_map/ppermute | solution.py:387
  15.6 28.8 %collective-permute-start.5 = (bf16[4,2,128,128]{3,2,1,0:T(8,128)(2,1)S(1)}, bf16[4,2,128,128]{3,2,1,0:T(8,128)(2,1)S(1)}, u32[]{:S(2)}, u32[]{:S(2)}) collective-permute-start(bf16[4,2,128,128]{3,2,1,0:T(8,128)(2,1)S(1)} %constant_dynamic-update-slice_fusion.refs_7_), channel_id=1, source_target_pairs={{0,4},{2,6},{4,8},{6,10},{8,12},{10,14},{1,5},{3,7},{5,9},{7,11},{... | collective-permute-start | bytes 786440 | tf_op jit(solution)/shard_map/ppermute | solution.py:387
  22.3 22.1 %collective-permute-start.7 = (bf16[4,2,128,128]{3,2,1,0:T(8,128)(2,1)S(1)}, bf16[4,2,128,128]{3,2,1,0:T(8,128)(2,1)S(1)}, u32[]{:S(2)}, u32[]{:S(2)}) collective-permute-start(bf16[4,2,128,128]{3,2,1,0:T(8,128)(2,1)S(1)} %collective-permute-done.6.refs_9_), channel_id=1, source_target_pairs={{8,12},{10,14},{9,13},{11,15},{24,28},{26,30},{25,29},{27,31}} | collective-permute-start | bytes 786440 | tf_op jit(solution)/shard_map/ppermute | solution.py:387
  23.0 8.4 %collective-permute-start.1 = (f32[8,256]{1,0:T(8,128)S(1)}, f32[8,256]{1,0:T(8,128)S(1)}, u32[]{:S(2)}, u32[]{:S(2)}) collective-permute-start(f32[8,256]{1,0:T(8,128)S(1)} %add.27), channel_id=1, source_target_pairs={{4,0},{6,2},{8,4},{10,6},{12,8},{14,10},{5,1},{7,3},{9,5},{11,7},{... | collective-permute-start | bytes 24584 | tf_op jit(solution)/shard_map/ppermute | solution.py:387
  31.4 9.5 %collective-permute-start.2 = (f32[8,256]{1,0:T(8,128)S(1)}, f32[8,256]{1,0:T(8,128)S(1)}, u32[]{:S(2)}, u32[]{:S(2)}) collective-permute-start(f32[8,256]{1,0:T(8,128)S(1)} %add.28), channel_id=1, source_target_pairs={{8,0},{10,2},{12,4},{14,6},{9,1},{11,3},{13,5},{15,7},{24,16},{26,... | collective-permute-start | bytes 24584 | tf_op jit(solution)/shard_map/ppermute | solution.py:387
  44.4 0.7 copy-start.4
  45.1 1.1 %copy-start.5 = (f32[2,640,128]{2,1,0:T(8,128)S(1)}, f32[2,640,128]{2,1,0:T(8,128)}, u32[]{:S(2)}) copy-start(f32[2,640,128]{2,1,0:T(8,128)} %get-tuple-element.31.refs_3_) | copy-start | bytes 1966084
  46.1 0.9 %copy-start.6 = (f32[2,128,128]{2,1,0:T(8,128)S(1)}, f32[2,128,128]{2,1,0:T(8,128)}, u32[]{:S(2)}) copy-start(f32[2,128,128]{2,1,0:T(8,128)} %get-tuple-element.30.refs_2_) | copy-start | bytes 393220
  47.1 9.0 %copy-start.7 = (f32[2,128,128]{2,1,0:T(8,128)S(1)}, f32[2,128,128]{2,1,0:T(8,128)}, u32[]{:S(2)}) copy-start(f32[2,128,128]{2,1,0:T(8,128)} %get-tuple-element.30.refs_2_) | copy-start | bytes 393220
  51.5 0.7 copy-start.2
  52.2 11.0 %collective-permute-start.13 = (bf16[2,2,128,128]{3,2,1,0:T(8,128)(2,1)S(1)}, bf16[2,2,128,128]{3,2,1,0:T(8,128)(2,1)S(1)}, u32[]{:S(2)}, u32[]{:S(2)}) collective-permute-start(bf16[2,2,128,128]{3,2,1,0:T(8,128)(2,1)S(1)} %get-tuple-element.47), channel_id=1, source_target_pairs={{12,0},{14,2},{13,1},{15,3},{28,16},{30,18},{29,17},{31,19}} | collective-permute-start | bytes 393224 | tf_op jit(solution)/shard_map/ppermute | solution.py:387
  53.5 11.8 %collective-permute-start.14 = (bf16[2,2,128,128]{3,2,1,0:T(8,128)(2,1)S(1)}, bf16[2,2,128,128]{3,2,1,0:T(8,128)(2,1)S(1)}, u32[]{:S(2)}, u32[]{:S(2)}) collective-permute-start(bf16[2,2,128,128]{3,2,1,0:T(8,128)(2,1)S(1)} %get-tuple-element.48), channel_id=1, source_target_pairs={{8,0},{10,2},{12,4},{14,6},{9,1},{11,3},{13,5},{15,7},{24,16},{26,... | collective-permute-start | bytes 393224 | tf_op jit(solution)/shard_map/ppermute | solution.py:387
  54.8 11.0 %collective-permute-start.15 = (bf16[2,2,128,128]{3,2,1,0:T(8,128)(2,1)S(1)}, bf16[2,2,128,128]{3,2,1,0:T(8,128)(2,1)S(1)}, u32[]{:S(2)}, u32[]{:S(2)}) collective-permute-start(bf16[2,2,128,128]{3,2,1,0:T(8,128)(2,1)S(1)} %get-tuple-element.49), channel_id=1, source_target_pairs={{4,0},{6,2},{8,4},{10,6},{12,8},{14,10},{5,1},{7,3},{9,5},{11,7},{... | collective-permute-start | bytes 393224 | tf_op jit(solution)/shard_map/ppermute | solution.py:387
  60.6 6.8 %copy-start.3 = (bf16[128,640]{1,0:T(8,128)(2,1)}, bf16[128,640]{1,0:T(8,128)(2,1)S(1)}, u32[]{:S(2)}) copy-start(bf16[128,640]{1,0:T(8,128)(2,1)S(1)} %get-tuple-element.36.refs_0_) | copy-start | bytes 491524
  60.6 10.6 %collective-permute-start.10 = (bf16[2,2,128,128]{3,2,1,0:T(8,128)(2,1)S(1)}, bf16[2,2,128,128]{3,2,1,0:T(8,128)(2,1)S(1)}, u32[]{:S(2)}, u32[]{:S(2)}) collective-permute-start(bf16[2,2,128,128]{3,2,1,0:T(8,128)(2,1)S(1)} %get-tuple-element.42), channel_id=1, source_target_pairs={{12,0},{14,2},{13,1},{15,3},{28,16},{30,18},{29,17},{31,19}} | collective-permute-start | bytes 393224 | tf_op jit(solution)/shard_map/ppermute | solution.py:387
  61.9 14.6 %collective-permute-start.11 = (bf16[2,2,128,128]{3,2,1,0:T(8,128)(2,1)S(1)}, bf16[2,2,128,128]{3,2,1,0:T(8,128)(2,1)S(1)}, u32[]{:S(2)}, u32[]{:S(2)}) collective-permute-start(bf16[2,2,128,128]{3,2,1,0:T(8,128)(2,1)S(1)} %get-tuple-element.43), channel_id=1, source_target_pairs={{8,0},{10,2},{12,4},{14,6},{9,1},{11,3},{13,5},{15,7},{24,16},{26,... | collective-permute-start | bytes 393224 | tf_op jit(solution)/shard_map/ppermute | solution.py:387
  63.2 13.3 %collective-permute-start.12 = (bf16[2,2,128,128]{3,2,1,0:T(8,128)(2,1)S(1)}, bf16[2,2,128,128]{3,2,1,0:T(8,128)(2,1)S(1)}, u32[]{:S(2)}, u32[]{:S(2)}) collective-permute-start(bf16[2,2,128,128]{3,2,1,0:T(8,128)(2,1)S(1)} %get-tuple-element.44), channel_id=1, source_target_pairs={{4,0},{6,2},{8,4},{10,6},{12,8},{14,10},{5,1},{7,3},{9,5},{11,7},{... | collective-permute-start | bytes 393224 | tf_op jit(solution)/shard_map/ppermute | solution.py:387
  65.3 12.5 %collective-permute-start.9 = (bf16[128,640]{1,0:T(8,128)(2,1)S(1)}, bf16[128,640]{1,0:T(8,128)(2,1)S(1)}, u32[]{:S(2)}, u32[]{:S(2)}) collective-permute-start(bf16[128,640]{1,0:T(8,128)(2,1)S(1)} %get-tuple-element.39), channel_id=1, source_target_pairs={{0,2},{2,0},{4,6},{6,4},{8,10},{10,8},{12,14},{14,12},{1,3},{3,1},... | collective-permute-start | bytes 491528 | tf_op jit(solution)/shard_map/ppermute | solution.py:387
  65.8 12.0 %collective-permute-start.8 = (bf16[128,640]{1,0:T(8,128)(2,1)S(1)}, bf16[128,640]{1,0:T(8,128)(2,1)S(1)}, u32[]{:S(2)}, u32[]{:S(2)}) collective-permute-start(bf16[128,640]{1,0:T(8,128)(2,1)S(1)} %get-tuple-element.38), channel_id=1, source_target_pairs={{0,2},{2,0},{4,6},{6,4},{8,10},{10,8},{12,14},{14,12},{1,3},{3,1},... | collective-permute-start | bytes 491528 | tf_op jit(solution)/shard_map/ppermute | solution.py:387
  71.2 6.6 %collective-permute-start.17 = (bf16[2,128,128]{2,1,0:T(8,128)(2,1)S(1)}, bf16[2,128,128]{2,1,0:T(8,128)(2,1)S(1)}, u32[]{:S(2)}, u32[]{:S(2)}) collective-permute-start(bf16[2,128,128]{2,1,0:T(8,128)(2,1)S(1)} %get-tuple-element.54), channel_id=1, source_target_pairs={{0,2},{2,0},{4,6},{6,4},{8,10},{10,8},{12,14},{14,12},{1,3},{3,1},... | collective-permute-start | bytes 196616 | tf_op jit(solution)/shard_map/ppermute | solution.py:387
  77.2 4.3 %collective-permute-start.16 = (bf16[2,128,128]{2,1,0:T(8,128)(2,1)S(1)}, bf16[2,128,128]{2,1,0:T(8,128)(2,1)S(1)}, u32[]{:S(2)}, u32[]{:S(2)}) collective-permute-start(bf16[2,128,128]{2,1,0:T(8,128)(2,1)S(1)} %get-tuple-element.56), channel_id=1, source_target_pairs={{0,2},{2,0},{4,6},{6,4},{8,10},{10,8},{12,14},{14,12},{1,3},{3,1},... | collective-permute-start | bytes 196616 | tf_op jit(solution)/shard_map/ppermute | solution.py:387
  77.8 3.7 %copy-start.8 = (bf16[128,640]{1,0:T(8,128)(2,1)}, bf16[128,640]{1,0:T(8,128)(2,1)S(1)}, u32[]{:S(2)}) copy-start(bf16[128,640]{1,0:T(8,128)(2,1)S(1)} %collective-permute-done.9.refs_3_) | copy-start | bytes 491524
  77.8 3.7 %copy-start.9 = (bf16[128,640]{1,0:T(8,128)(2,1)}, bf16[128,640]{1,0:T(8,128)(2,1)S(1)}, u32[]{:S(2)}) copy-start(bf16[128,640]{1,0:T(8,128)(2,1)S(1)} %collective-permute-done.8.refs_2_) | copy-start | bytes 491524
  77.8 3.7 %copy-start.10 = (bf16[2,128,128]{2,1,0:T(8,128)(2,1)}, bf16[2,128,128]{2,1,0:T(8,128)(2,1)S(1)}, u32[]{:S(2)}) copy-start(bf16[2,128,128]{2,1,0:T(8,128)(2,1)S(1)} %collective-permute-done.17.refs_7_) | copy-start | bytes 196612
  81.5 0.6 copy-start.11

commit v4 on v3

--- a/solution.py
+++ b/solution.py
@@ -99,27 +99,54 @@
     )(own, lengths, k, v, *token_rows)
 
 
-def pack_queries_kernel(own_ref, q_ref, dir_ref, out_ref):
-    other = 1 - lax.rem(own_ref[0], 2)
-    heads = out_ref.shape[1]
-    for h in range(heads):
-        columns = pl.ds(pl.multiple_of((other * heads + h) * HD, HD), HD)
-        out_ref[0, h] = q_ref[:, columns]
-        out_ref[1, h] = dir_ref[:, columns]
-
-
-def pack_queries(own, q, direction):
+def pack_queries_kernel(parts, own_ref, q_ref, dir_ref, *out_refs):
+    own = own_ref[0]
+    chunks = len(out_refs) // parts
+    heads = out_refs[0].shape[1]
+    for step in range(parts):
+        part = lax.rem(own + step, parts)
+        for chunk in range(chunks):
+            out_ref = out_refs[step * chunks + chunk]
+            for h in range(heads):
+                column = (part * chunks + chunk) * heads + h
+                columns = pl.ds(pl.multiple_of(column * HD, HD), HD)
+                out_ref[0, h] = q_ref[:, columns]
+                out_ref[1, h] = dir_ref[:, columns]
+
+
+def pack_queries(own, q, direction, parts, chunks):
     length, width = q.shape
     smem = pl.BlockSpec(memory_space=pltpu.SMEM)
     vmem = pl.BlockSpec(memory_space=pltpu.VMEM)
-    return pl.pallas_call(
-        pack_queries_kernel,
-        out_shape=jax.ShapeDtypeStruct((2, width // HD // 2, length, HD), q.dtype),
+    block = jax.ShapeDtypeStruct((2, width // HD // parts // chunks, length, HD), q.dtype)
+    outs = pl.pallas_call(
+        functools.partial(pack_queries_kernel, parts),
+        out_shape=(block,) * (parts * chunks),
         in_specs=[smem, vmem, vmem],
-        out_specs=vmem,
-        cost_estimate=pl.CostEstimate(flops=0, bytes_accessed=6 * length * width, transcendentals=0),
+        out_specs=(vmem,) * (parts * chunks),
+        cost_estimate=pl.CostEstimate(flops=0, bytes_accessed=8 * length * width, transcendentals=0),
         name="pack_queries",
     )(own, q, direction)
+    return [outs[step * chunks : (step + 1) * chunks] for step in range(parts)]
+
+
+def join_blocks_kernel(mine_ref, other_ref, *out_refs):
+    for chunk, out_ref in enumerate(out_refs):
+        out_ref[0] = mine_ref[chunk]
+        out_ref[1] = other_ref[chunk]
+
+
+def join_blocks(mine, other):
+    chunks = mine.shape[0]
+    vmem = pl.BlockSpec(memory_space=pltpu.VMEM)
+    return pl.pallas_call(
+        join_blocks_kernel,
+        out_shape=(jax.ShapeDtypeStruct((2,) + mine.shape[1:], mine.dtype),) * chunks,
+        in_specs=[vmem] * 2,
+        out_specs=(vmem,) * chunks,
+        cost_estimate=pl.CostEstimate(flops=0, bytes_accessed=8 * mine.size, transcendentals=0),
+        name="join_blocks",
+    )(mine, other)
 
 
 def prepare_kernel(
@@ -131,13 +158,15 @@
     lengths_s,
     parents_ref,
     lengths_ref,
-    terms_ref,
+    near_ref,
+    far_ref,
     row_ref,
     adv_ref,
     bias_ref,
 ):
     length = row_ref.shape[1]
     count = parents_s.shape[0]
+    terms = near_ref[...] + far_ref[...]
     own = own_ref[0]
     part = lax.rem(own, segs)
 
@@ -153,8 +182,8 @@
     lens_col = jnp.sum(
         jnp.where(eye, lengths_ref[...].astype(jnp.float32), 0.0), axis=1, keepdims=True
     )
-    first_local = terms_ref[:, length : length + 1]
-    first_value = terms_ref[:, length + 1 : length + 2]
+    first_local = terms[:, length : length + 1]
+    first_value = terms[:, length + 1 : length + 2]
     later_value = jnp.sum(weights * to_row(first_value), axis=1, keepdims=True)
     base_term = first_local + jnp.exp((lens_col - 1.0) * log_rate) * later_value
     factor = jnp.exp(lens_col * log_rate)
@@ -175,7 +204,7 @@
         mine = seg_col == seg
         my_value = jnp.sum(jnp.where(mine, later_value, 0.0), axis=0, keepdims=True)
         my_head = jnp.sum(jnp.where(mine, later_head, 0.0), axis=0, keepdims=True)
-        deltas = jnp.sum(jnp.where(mine, terms_ref[:, :length], 0.0), axis=0, keepdims=True)
+        deltas = jnp.sum(jnp.where(mine, terms[:, :length], 0.0), axis=0, keepdims=True)
         local_sum = jnp.sum(discount * deltas, axis=1, keepdims=True)
         left = (seg_len - t_col).astype(jnp.float32)
         advantage = jnp.where(
@@ -205,8 +234,8 @@
     return jnp.where(segment >= 0, known, -1).astype(jnp.int32)
 
 
-def prepare(own, parents, lengths, terms, segs, log_rate):
-    length = terms.shape[1] // 2
+def prepare(own, parents, lengths, near, far, segs, log_rate):
+    length = near.shape[1] // 2
     smem = pl.BlockSpec(memory_space=pltpu.SMEM)
     vmem = pl.BlockSpec(memory_space=pltpu.VMEM)
     return pl.pallas_call(
@@ -216,7 +245,7 @@
             jax.ShapeDtypeStruct((segs, length, HD), jnp.float32),
             jax.ShapeDtypeStruct((segs, DEPTH * length, length), jnp.float32),
         ),
-        in_specs=[smem] * 3 + [vmem] * 3,
+        in_specs=[smem] * 3 + [vmem] * 4,
         out_specs=(vmem,) * 3,
         cost_estimate=pl.CostEstimate(
             flops=200 * length * length,
@@ -224,23 +253,23 @@
             transcendentals=length * length,
         ),
         name="prepare_advantages",
-    )(own, parents, lengths, parents[None], lengths[None], terms)
-
-
-def attend_kernel(group_size, depth, chunk, chunks, segs, *refs):
-    own_ref, parents_s, adv_ref, bias_ref, q_ref, dir_ref = refs[:6]
-    shared_refs = refs[6 : 5 + segs]
-    refs = refs[5 + segs :]
+    )(own, parents, lengths, parents[None], lengths[None], near, far)
+
+
+def attend_kernel(depth, segs, *refs):
+    own_ref, parents_s, adv_ref, bias_ref = refs[:4]
+    query_refs = refs[4 : 4 + segs]
+    refs = refs[4 + segs :]
     steps = (len(refs) - segs - 4) // 2
     kv_refs, dq_refs, dkv_refs = refs[:steps], refs[steps : steps + segs], refs[steps + segs : -4]
     kv_scr, p_scr, ds_scr, acc_scr = refs[-4:]
 
-    length = q_ref.shape[0]
+    group_size, length = query_refs[0].shape[1:3]
     own = own_ref[0]
     part = lax.rem(own, segs)
     for step in range(steps):
         for i in range(segs):
-            kv_scr[step * segs + i] = kv_refs[step][i * chunks + chunk]
+            kv_scr[step * segs + i] = kv_refs[step][i]
     acc_scr[...] = jnp.zeros_like(acc_scr)
 
     scale = HD**-0.5
@@ -259,17 +288,8 @@
                 step = (own - part) // segs - known // segs
                 turn = lax.rem(lax.rem(known, segs) - part + segs, segs)
                 chosen.append(jnp.where(ancestor >= 0, step * segs + turn, 0))
-        if i == 0:
-            first = (part * chunks + chunk) * group_size
-            columns = [
-                pl.ds(pl.multiple_of((first + j) * HD, HD), HD) for j in range(group_size)
-            ]
-            q_list = [q_ref[:, c] for c in columns]
-            dir_list = [dir_ref[:, c] for c in columns]
-        else:
-            first = chunk * group_size
-            q_list = [shared_refs[i - 1][0, first + j] for j in range(group_size)]
-            dir_list = [shared_refs[i - 1][1, first + j] for j in range(group_size)]
+        q_list = [query_refs[i][0, j] for j in range(group_size)]
+        dir_list = [query_refs[i][1, j] for j in range(group_size)]
         do_list = [(adv_ref[i] * d.astype(jnp.float32)).astype(jnp.bfloat16) for d in dir_list]
         k_all = jnp.concatenate([kv_scr[s, 0] for s in chosen], axis=0)
         v_all = jnp.concatenate([kv_scr[s, 1] for s in chosen], axis=0)
@@ -311,11 +331,10 @@
             dkv_refs[step][i] = acc_scr[step * segs + i].astype(jnp.bfloat16)
 
 
-def attend(own, parents, advantages, bias, q, direction, shared, kv_list, chunk, chunks):
+def attend(own, parents, advantages, bias, query_list, kv_list):
     segs, length = advantages.shape[:2]
     steps = len(kv_list)
-    group_size = q.shape[1] // HD // chunks // segs
-    width = group_size * HD
+    width = query_list[0].shape[1] * HD
     keys = DEPTH * length
     smem = pl.BlockSpec(memory_space=pltpu.SMEM)
     vmem = pl.BlockSpec(memory_space=pltpu.VMEM)
@@ -323,9 +342,9 @@
         jax.ShapeDtypeStruct((segs, 2, length, HD), jnp.bfloat16),
     ) * steps
     outs = pl.pallas_call(
-        functools.partial(attend_kernel, group_size, DEPTH, chunk, chunks, segs),
+        functools.partial(attend_kernel, DEPTH, segs),
         out_shape=out_shape,
-        in_specs=[smem] * 2 + [vmem] * (4 + len(shared) + len(kv_list)),
+        in_specs=[smem] * 2 + [vmem] * (2 + segs + steps),
         out_specs=(vmem,) * len(out_shape),
         scratch_shapes=[
             pltpu.VMEM((steps * segs, 2, length, HD), jnp.bfloat16),
@@ -340,47 +359,70 @@
             transcendentals=keys * width * segs,
         ),
         name="tree_attention_backward",
-    )(own, parents, advantages, bias, q, direction, *shared, *kv_list)
+    )(own, parents, advantages, bias, *query_list, *kv_list)
     return outs[:segs], outs[segs:]
 
 
-def finish_kernel(chunks, own_ref, *refs):
+def join_queries_kernel(chunks, own_ref, *refs):
     part = lax.rem(own_ref[0], 2)
-    dq_refs, kv_refs = refs[: 2 * chunks], refs[2 * chunks : -3]
-    dq_ref, dk_ref, dv_ref = refs[-3:]
+    dq_ref = refs[-1]
     for side in range(2):
         where = part if side == 0 else 1 - part
         for chunk in range(chunks):
-            block = dq_refs[side * chunks + chunk]
+            block = refs[side * chunks + chunk]
             width = block.shape[1]
             column = pl.multiple_of((where * chunks + chunk) * width, HD)
             dq_ref[:, pl.ds(column, width)] = block[...]
-            columns = pl.ds(pl.multiple_of((where * chunks + chunk) * HD, HD), HD)
-            block = kv_refs[side * chunks + chunk]
-            dk_ref[:, columns] = block[0]
-            dv_ref[:, columns] = block[1]
-
-
-def finish(own, dq_list, kv_list):
-    chunks = len(kv_list) // 2
+
+
+def join_queries(own, dq_list):
     length, width = dq_list[0].shape
     smem = pl.BlockSpec(memory_space=pltpu.SMEM)
     vmem = pl.BlockSpec(memory_space=pltpu.VMEM)
-    kv_out = jax.ShapeDtypeStruct((length, 2 * chunks * HD), jnp.bfloat16)
     return pl.pallas_call(
-        functools.partial(finish_kernel, chunks),
-        out_shape=(
-            jax.ShapeDtypeStruct((length, 2 * chunks * width), jnp.bfloat16),
-            kv_out,
-            kv_out,
+        functools.partial(join_queries_kernel, len(dq_list) // 2),
+        out_shape=jax.ShapeDtypeStruct((length, len(dq_list) * width), jnp.bfloat16),
+        in_specs=[smem] + [vmem] * len(dq_list),
+        out_specs=vmem,
+        cost_estimate=pl.CostEstimate(
+            flops=0, bytes_accessed=4 * length * width * len(dq_list), transcendentals=0
         ),
-        in_specs=[smem] + [vmem] * (4 * chunks),
-        out_specs=(vmem,) * 3,
+        name="join_queries",
+    )(own, *dq_list)
+
+
+def join_keys_kernel(chunks, own_ref, *refs):
+    part = lax.rem(own_ref[0], 2)
+    other_refs, sum_refs = refs[:chunks], refs[chunks:-2]
+    many = len(sum_refs) // chunks
+    dk_ref, dv_ref = refs[-2:]
+    for chunk in range(chunks):
+        here = pl.ds(pl.multiple_of((part * chunks + chunk) * HD, HD), HD)
+        there = pl.ds(pl.multiple_of(((1 - part) * chunks + chunk) * HD, HD), HD)
+        for plane, out_ref in enumerate((dk_ref, dv_ref)):
+            blocks = [ref[0, plane] for ref in sum_refs[chunk * many : (chunk + 1) * many]]
+            total = sum(block.astype(jnp.float32) for block in blocks)
+            out_ref[:, here] = total.astype(jnp.bfloat16)
+            out_ref[:, there] = other_refs[chunk][plane]
+
+
+def join_keys(own, others, summands):
+    chunks = len(others)
+    length = others[0].shape[1]
+    smem = pl.BlockSpec(memory_space=pltpu.SMEM)
+    vmem = pl.BlockSpec(memory_space=pltpu.VMEM)
+    flat = [block for blocks in summands for block in blocks]
+    out = jax.ShapeDtypeStruct((length, 2 * chunks * HD), jnp.bfloat16)
+    return pl.pallas_call(
+        functools.partial(join_keys_kernel, chunks),
+        out_shape=(out, out),
+        in_specs=[smem] + [vmem] * (chunks + len(flat)),
+        out_specs=(vmem, vmem),
         cost_estimate=pl.CostEstimate(
-            flops=0, bytes_accessed=8 * length * width * chunks, transcendentals=0
+            flops=0, bytes_accessed=16 * length * HD * chunks, transcendentals=0
         ),
-        name="join_heads",
-    )(own, *dq_list, *kv_list)
+        name="join_keys",
+    )(own, *others, *flat)
 
 
 def permute(array, pairs):
@@ -395,41 +437,51 @@
     groups = lax.axis_size("seg")
     chunks = key_vectors.shape[1] // HD // 2
     swap = [(i, i ^ 1) for i in range(groups)]
-    up = {d: [(i, i + 2 * d) for i in range(groups - 2 * d)] for d in (1, 2)}
+    up = {d: [(i, i + 2 * d) for i in range(groups - 2 * d)] for d in (1, 2, 3)}
     down = {d: [(i, i - 2 * d) for i in range(2 * d, groups)] for d in (1, 2, 3)}
     forward = [(i, i + 2) for i in range(4, groups - 2)]
 
     kept, given, terms = pack(own, lengths, key_vectors, value_vectors, token_rows, 2, log_rate)
     terms = terms + permute(terms, swap)
     taken = permute(given, swap)
-    shares = pack_queries(own, after(queries, given), direction)
-    near = jnp.concatenate([kept, taken])
-    two = permute(near, up[2])
-    one = permute(near, up[1])
-    three = permute(two, forward)
-    shared = permute(after(shares, near, terms), swap)
-    for d in (1, 2):
-        terms = terms + permute(terms, down[d])
-    row, advantages, bias = prepare(own, parents, lengths, terms, 2, log_rate)
-    blocks = [near, one, two, three]
-
-    results = []
+    kept_q, given_q = pack_queries(own, after(queries, given), direction, 2, chunks)
+    terms = terms + permute(terms, down[1])
+    near = join_blocks(kept, after(taken, terms))
+    blocks = [[near[0]] + [permute(near[0], up[d]) for d in (3, 2, 1)][::-1]]
+    taken_q = [permute(after(given_q[0], near[0]), swap)]
+    row, advantages, bias = prepare(
+        own, parents, lengths, terms, permute(terms, down[2]), 2, log_rate
+    )
+    blocks[0][1:] = lax.optimization_barrier((*blocks[0][1:], bias))[:-1]
+    for chunk in range(1, chunks):
+        taken_q.append(permute(after(given_q[chunk], taken_q[-1], bias), swap))
+
+    dq_own, dq_back, dkv_list = [], [], []
     for chunk in range(chunks):
-        results.append(
-            attend(
-                own, parents, advantages, bias, queries, direction, [shared], blocks, chunk, chunks
-            )
-        )
-    dq_own, dq_back, totals, totals_back = [], [], [], []
-    for dq, dkv in results:
+        gate = blocks[chunk]
+        dq, dkv = attend(own, parents, advantages, bias, [kept_q[chunk], taken_q[chunk]], gate)
+        dq_own.append(dq[0])
+        dq_back.append(dq[1])
+        dkv_list.append(dkv)
+        if chunk + 1 < chunks:
+            block = near[chunk + 1]
+            two = permute(after(block, *gate[1:]), up[2])
+            one = permute(after(block, dq[0]), up[1])
+            three = permute(after(two, dq[0]), forward)
+            blocks.append([block, one, two, three])
+
+    last = dq_own[-1]
+    summands = []
+    for dkv in dkv_list:
         arrived = [permute(dkv[d], down[d]) for d in (3, 2, 1)]
-        dq_own.append(dq[0])
-        dq_back.append(permute(dq[1], swap))
-        near = after(dkv[0], results[-1][0][0])
-        total = sum(block.astype(jnp.float32) for block in [near] + arrived).astype(jnp.bfloat16)
-        totals.append(total[0])
-        totals_back.append(permute(total[1], swap))
-    grad_q, grad_k, grad_v = finish(own, dq_own + dq_back, totals + totals_back)
+        summands.append([after(dkv[0], last)] + arrived)
+    dq_back = [permute(block, swap) for block in dq_back]
+    others = []
+    for blocks in summands:
+        total = sum(block[1].astype(jnp.float32) for block in blocks)
+        others.append(permute(total.astype(jnp.bfloat16), swap))
+    grad_q = join_queries(own, dq_own + dq_back)
+    grad_k, grad_v = join_keys(own, others, summands)
     return grad_q, grad_k, grad_v, row[0]
 
 
@@ -465,19 +517,20 @@
     heads = block.shape[0]
     mine = lax.dynamic_slice_in_dim(terms, own[0], 1)
     terms = lax.all_gather(mine, "seg", axis=0, tiled=True)
-    row, advantages, bias = prepare(own, parents, lengths, terms, 1, log_rate)
+    row, advantages, bias = prepare(
+        own, parents, lengths, terms, jnp.zeros_like(terms), 1, log_rate
+    )
     flat = jnp.concatenate([key_vectors, value_vectors], axis=1)[None]
     spread = lax.all_to_all(flat, "seg", split_axis=1, concat_axis=0, tiled=True)
     chains = ancestors(parents, DEPTH - 1)
     arrived = fetch_rows(spread, chains)[0]
     slot_kv = jnp.concatenate([flat, arrived]).reshape(DEPTH, length, 2, heads, HD)
     slot_kv = jnp.transpose(slot_kv, (0, 3, 2, 1, 4))
-    kv_list = [slot_kv[slot] for slot in range(DEPTH)]
+    (kept_q,) = pack_queries(own, queries, direction, 1, heads)
     dq_list, dkv_list = [], []
     for head in range(heads):
-        dq, dkv = attend(
-            own, parents, advantages, bias, queries, direction, [], kv_list, head, heads
-        )
+        kv_list = [slot_kv[slot : slot + 1, head] for slot in range(DEPTH)]
+        dq, dkv = attend(own, parents, advantages, bias, [kept_q[head]], kv_list)
         dq_list.append(dq[0])
         dkv_list.append(jnp.concatenate(dkv))
     rows = jnp.transpose(jnp.stack(dkv_list), (1, 3, 2, 0, 4)).reshape(1, DEPTH, length, -1)

time: 84.8 us -> 84.8 us (level)
  waiting for transfers between devices: 31.6 us -> 19.5 us
  starting transfers between devices: 26.9 us -> 32.9 us
  Pallas kernels: 18.1 us -> 22 us
  local copies, waits for them, and re-layouts: 6.13 us -> 8.04 us
    ppermute x18 -> x22, waiting for transfers between devices: 31.6 us -> 19.5 us  [permute(): return lax.ppermute(array, 'seg', pairs)]
    ppermute x18 -> x22, starting transfers between devices: 26.9 us -> 32.9 us  [permute(): return lax.ppermute(array, 'seg', pairs)]
    pallas_call x4 -> x6, Pallas kernels: 13.5 us -> 17.3 us  [the longest x2 8.88 us: attend(): pl.pallas_call(functools.partial(attend_kernel, DEPTH, segs), out_shape=o...]
    unnamed x27 -> x48, local copies, waits for them, and re-layouts: 4.84 us -> 8.04 us
    squeeze x2 -> x0, local copies, waits for them, and re-layouts: 1.27 us -> none  [paired_body(): totals_back.append(permute(total[1], swap))]
  transfers between devices with their start and end apart: 18 -> 22, of which waited for: 8 -> 6; matrix products, arithmetic and copies ran while one was open for 3% -> 1% of each run, Pallas kernels for 11% -> 19%
where the time goes in v4:
time: 84.8 us; the launch traced here: 84.2 us
  starting transfers between devices  32.9 us (39%)
  Pallas kernels  22 us (26%)
  waiting for transfers between devices  19.5 us (23%)
  local copies, waits for them, and re-layouts  8.04 us (9%)
  between operations  0.99 us (1%)
    ppermute x22, starting transfers between devices, permute(): return lax.ppermute(array, 'seg', pairs)  32.9 us
    ppermute x22, waiting for transfers between devices, permute(): return lax.ppermute(array, 'seg', pairs)  19.5 us
    pallas_call x2, Pallas kernels, attend(): pl.pallas_call(functools.partial(attend_kernel, DEPTH, segs), out_shape=o...  8.88 us
    unnamed x48, local copies, waits for them, and re-layouts  8.04 us
    pallas_call x1, Pallas kernels, prepare(): pl.pallas_call(functools.partial(prepare_kernel, log_rate, DEPTH, segs),...  2.83 us
    pallas_call x1, Pallas kernels, pack_queries(): pl.pallas_call(functools.partial(pack_queries_kernel, parts), out_shape=(...  2.63 us
    pallas_call x1, Pallas kernels, join_keys(): pl.pallas_call(functools.partial(join_keys_kernel, chunks), out_shape=(ou...  2.09 us
    pallas_call x1, Pallas kernels, join_queries(): pl.pallas_call(functools.partial(join_queries_kernel, len(dq_list) // 2),...  2.06 us
  transfers between devices with their start and end apart: 22, of which 6 were waited for; matrix products, arithmetic and copies ran while one was open for 1% of the time, Pallas kernels for 19%

profile of v4, /device:TPU:0, one launch (start us, length us, event | category | flops | bytes accessed | tf_op | source)
XLA Modules:
  0.0 84.2 jit_solution(3925616780866666907)
XLA Ops:
  0.6 1.8 %pack_keys_values.1 = (bf16[2,2,128,128]{3,2,1,0:T(8,128)(2,1)}, bf16[2,2,128,128]{3,2,1,0:T(8,128)(2,1)}, f32[8,256]{1,0:T(8,128)}) custom-call(s32[1]{0:T(128)} %bitcast.own_ref.refs_0_, s32[8]{0:T(128)} %lengths_s.1, bf16[128,512]{1,0:T(8,128)(2,1)} %k_ref.1, bf16[128,512]{1,0:T(8,128)(2,1)} %v_ref.1, f32[1,128]{1,0:T(1,128)} %bitcast.13, ...), custom_call_target="tpu_custom_call" | custom-call | flops 12800 | bytes 524288 | tf_op jit(solution)/shard_map/pack_keys_values/pallas_call | solution.py:90
  2.4 2.9 %collective-permute-start.3 = (bf16[2,2,128,128]{3,2,1,0:T(8,128)(2,1)}, bf16[2,2,128,128]{3,2,1,0:T(8,128)(2,1)S(1)}, u32[]{:S(2)}, u32[]{:S(2)}) collective-permute-start(bf16[2,2,128,128]{3,2,1,0:T(8,128)(2,1)} %get-tuple-element.45), channel_id=1, source_target_pairs={{0,2},{2,0},{4,6},{6,4},{8,10},{10,8},{12,14},{14,12},{1,3},{3,1},... | collective-permute-start | bytes 393224 | tf_op jit(solution)/shard_map/ppermute | solution.py:429
  5.4 0.0 collective-permute-start
  5.4 3.8 %collective-permute-done = f32[8,256]{1,0:T(8,128)S(1)} collective-permute-done((f32[8,256]{1,0:T(8,128)}, f32[8,256]{1,0:T(8,128)S(1)}, u32[]{:S(2)}, u32[]{:S(2)}) %collective-permute-start) | collective-permute-done | bytes 8224 | tf_op jit(solution)/shard_map/ppermute | solution.py:429
  9.2 0.7 add.34
  9.9 1.3 %collective-permute-start.1 = (f32[8,256]{1,0:T(8,128)S(1)}, f32[8,256]{1,0:T(8,128)S(1)}, u32[]{:S(2)}, u32[]{:S(2)}) collective-permute-start(f32[8,256]{1,0:T(8,128)S(1)} %add.34), channel_id=1, source_target_pairs={{4,0},{6,2},{8,4},{10,6},{12,8},{14,10},{5,1},{7,3},{9,5},{11,7},{... | collective-permute-start | bytes 24584 | tf_op jit(solution)/shard_map/ppermute | solution.py:429
  11.2 2.6 %pack_queries.1 = (bf16[2,5,128,128]{3,2,1,0:T(8,128)(2,1)}, bf16[2,5,128,128]{3,2,1,0:T(8,128)(2,1)}, bf16[2,5,128,128]{3,2,1,0:T(8,128)(2,1)}, bf16[2,5,128,128]{3,2,1,0:T(8,128)(2,1)}) custom-call(s32[1]{0:T(128)} %bitcast.own_ref.refs_0_, bf16[128,2560]{1,0:T(8,128)(2,1)} %q_ref, bf16[128,2560]{1,0:T(8,128)(2,1)} %dir_ref.1), custom_call_target="tpu_custom_call" | custom-call | bytes 2621440 | tf_op jit(solution)/shard_map/pack_queries/pallas_call | solution.py:122
  13.9 1.6 %collective-permute-done.1 = f32[8,256]{1,0:T(8,128)S(1)} collective-permute-done((f32[8,256]{1,0:T(8,128)S(1)}, f32[8,256]{1,0:T(8,128)S(1)}, u32[]{:S(2)}, u32[]{:S(2)}) %collective-permute-start.1) | collective-permute-done | bytes 8224 | tf_op jit(solution)/shard_map/ppermute | solution.py:429
  15.5 0.0 collective-permute-done.3.other_ref
  15.5 0.0 copy-start.19
  15.5 0.6 copy-done.19
  16.1 1.7 %join_blocks.1 = (bf16[2,2,128,128]{3,2,1,0:T(8,128)(2,1)}, bf16[2,2,128,128]{3,2,1,0:T(8,128)(2,1)}) custom-call(bf16[2,2,128,128]{3,2,1,0:T(8,128)(2,1)} %get-tuple-element.49.mine_ref, bf16[2,2,128,128]{3,2,1,0:T(8,128)(2,1)} %copy-done.19), custom_call_target="tpu_custom_call" | custom-call | bytes 524288 | tf_op jit(solution)/shard_map/join_blocks/pallas_call | solution.py:142
  17.8 1.7 %collective-permute-start.4 = (bf16[2,5,128,128]{3,2,1,0:T(8,128)(2,1)}, bf16[2,5,128,128]{3,2,1,0:T(8,128)(2,1)S(1)}, u32[]{:S(2)}, u32[]{:S(2)}) collective-permute-start(bf16[2,5,128,128]{3,2,1,0:T(8,128)(2,1)} %get-tuple-element.52), channel_id=1, source_target_pairs={{0,2},{2,0},{4,6},{6,4},{8,10},{10,8},{12,14},{14,12},{1,3},{3,1},... | collective-permute-start | bytes 983048 | tf_op jit(solution)/shard_map/ppermute | solution.py:429
  19.6 3.5 %collective-permute-start.5 = (bf16[2,2,128,128]{3,2,1,0:T(8,128)(2,1)}, bf16[2,2,128,128]{3,2,1,0:T(8,128)(2,1)S(1)}, u32[]{:S(2)}, u32[]{:S(2)}) collective-permute-start(bf16[2,2,128,128]{3,2,1,0:T(8,128)(2,1)} %get-tuple-element.51.refs_6_), channel_id=1, source_target_pairs={{0,4},{2,6},{4,8},{6,10},{8,12},{10,14},{1,5},{3,7},{5,9},{7,11},{... | collective-permute-start | bytes 393224 | tf_op jit(solution)/shard_map/ppermute | solution.py:429
  23.0 4.0 %collective-permute-start.6 = (bf16[2,2,128,128]{3,2,1,0:T(8,128)(2,1)}, bf16[2,2,128,128]{3,2,1,0:T(8,128)(2,1)S(1)}, u32[]{:S(2)}, u32[]{:S(2)}) collective-permute-start(bf16[2,2,128,128]{3,2,1,0:T(8,128)(2,1)} %get-tuple-element.51.refs_6_), channel_id=1, source_target_pairs={{0,8},{2,10},{4,12},{6,14},{1,9},{3,11},{5,13},{7,15},{16,24},{18,... | collective-permute-start | bytes 393224 | tf_op jit(solution)/shard_map/ppermute | solution.py:429
  27.0 1.3 %collective-permute-start.7 = (bf16[2,2,128,128]{3,2,1,0:T(8,128)(2,1)}, bf16[2,2,128,128]{3,2,1,0:T(8,128)(2,1)S(1)}, u32[]{:S(2)}, u32[]{:S(2)}) collective-permute-start(bf16[2,2,128,128]{3,2,1,0:T(8,128)(2,1)} %get-tuple-element.51.refs_6_), channel_id=1, source_target_pairs={{0,12},{2,14},{1,13},{3,15},{16,28},{18,30},{17,29},{19,31}} | collective-permute-start | bytes 393224 | tf_op jit(solution)/shard_map/ppermute | solution.py:429
  28.3 1.3 %collective-permute-start.2 = (f32[8,256]{1,0:T(8,128)S(1)}, f32[8,256]{1,0:T(8,128)S(1)}, u32[]{:S(2)}, u32[]{:S(2)}) collective-permute-start(f32[8,256]{1,0:T(8,128)S(1)} %add.35.near_ref), channel_id=1, source_target_pairs={{8,0},{10,2},{12,4},{14,6},{9,1},{11,3},{13,5},{15,7},{24,16},{26,... | collective-permute-start | bytes 24584 | tf_op jit(solution)/shard_map/ppermute | solution.py:429
  29.6 5.1 %collective-permute-done.2.far_ref = f32[8,256]{1,0:T(8,128)S(1)} collective-permute-done((f32[8,256]{1,0:T(8,128)S(1)}, f32[8,256]{1,0:T(8,128)S(1)}, u32[]{:S(2)}, u32[]{:S(2)}) %collective-permute-start.2) | collective-permute-done | bytes 8224 | tf_op jit(solution)/shard_map/ppermute | solution.py:429
  34.8 0.6 copy-done.23
  35.4 2.8 %prepare_advantages.1 = (f32[1,128]{1,0:T(1,128)}, f32[2,128,128]{2,1,0:T(8,128)}, f32[2,640,128]{2,1,0:T(8,128)}) custom-call(s32[1]{0:T(128)} %bitcast.own_ref.refs_0_, s32[8]{0:T(128)} %refs_1_.3, s32[8]{0:T(128)} %lengths_s.1, s32[1,8]{1,0:T(1,128)} %bitcast.12, s32[1,8]{1,0:T(1,128)} %bitcast.17, f32[8,256]{1,0:T(8,128)} %copy-done.22, f32[8,256]{1,0:T(8,128)} %copy-done.23), custom_call_target="tpu_custom_call" | custom-call | flops 3276800 | bytes 786432 | tf_op jit(solution)/shard_map/prepare_advantages/pallas_call | solution.py:241
  38.2 0.0 collective-permute-done.4.refs_5_
  38.2 0.5 collective-permute-start.8
  38.8 0.0 collective-permute-done.5.refs_7_
  38.8 0.0 collective-permute-done.6.refs_8_
  38.8 0.0 collective-permute-done.7.refs_9_
  38.8 1.7 %collective-permute-start.10 = (bf16[2,2,128,128]{3,2,1,0:T(8,128)(2,1)}, bf16[2,2,128,128]{3,2,1,0:T(8,128)(2,1)S(1)}, u32[]{:S(2)}, u32[]{:S(2)}) collective-permute-start(bf16[2,2,128,128]{3,2,1,0:T(8,128)(2,1)} %get-tuple-element.62.refs_6_), channel_id=1, source_target_pairs={{0,8},{2,10},{4,12},{6,14},{1,9},{3,11},{5,13},{7,15},{16,24},{18,... | collective-permute-start | bytes 393224 | tf_op jit(solution)/shard_map/ppermute | solution.py:429
  40.4 0.0 copy-start.8
  40.4 0.6 copy-done.8
  41.1 0.9 %copy-done.7 = bf16[2,2,128,128]{3,2,1,0:T(8,128)(2,1)S(1)} copy-done((bf16[2,2,128,128]{3,2,1,0:T(8,128)(2,1)S(1)}, bf16[2,2,128,128]{3,2,1,0:T(8,128)(2,1)}, u32[]{:S(2)}) %copy-start.7) | copy-done | bytes 131096
  42.0 1.1 %copy-done.9 = f32[2,640,128]{2,1,0:T(8,128)S(1)} copy-done((f32[2,640,128]{2,1,0:T(8,128)S(1)}, f32[2,640,128]{2,1,0:T(8,128)}, u32[]{:S(2)}) %copy-start.9) | copy-done | bytes 655384
  43.1 0.9 %copy-done.10 = f32[2,128,128]{2,1,0:T(8,128)S(1)} copy-done((f32[2,128,128]{2,1,0:T(8,128)S(1)}, f32[2,128,128]{2,1,0:T(8,128)}, u32[]{:S(2)}) %copy-start.10) | copy-done | bytes 131096
  44.0 4.4 %tree_attention_backward.2 = (bf16[128,640]{1,0:T(8,128)(2,1)S(1)}, bf16[128,640]{1,0:T(8,128)(2,1)S(1)}, bf16[2,2,128,128]{3,2,1,0:T(8,128)(2,1)S(1)}, bf16[2,2...) custom-call(s32[1]{0:T(128)} %bitcast.own_ref.refs_0_, ...), custom_call_target="tpu_custom_call" | custom-call | flops 1048576000 | bytes 8388608 | tf_op jit(solution)/shard_map/tree_attention_backward/pallas_call | solution.py:344
  48.4 0.7 copy-done.2
  49.1 1.7 %collective-permute-start.9 = (bf16[2,2,128,128]{3,2,1,0:T(8,128)(2,1)S(1)}, bf16[2,2,128,128]{3,2,1,0:T(8,128)(2,1)S(1)}, u32[]{:S(2)}, u32[]{:S(2)}) collective-permute-start(bf16[2,2,128,128]{3,2,1,0:T(8,128)(2,1)S(1)} %copy-done.6), channel_id=1, source_target_pairs={{0,4},{2,6},{4,8},{6,10},{8,12},{10,14},{1,5},{3,7},{5,9},{7,11},{... | collective-permute-start | bytes 393224 | tf_op jit(solution)/shard_map/ppermute | solution.py:429
  50.8 0.0 collective-permute-done.10.refs_8_
  50.8 0.7 collective-permute-start.11
  51.5 1.3 %collective-permute-start.16 = (bf16[2,2,128,128]{3,2,1,0:T(8,128)(2,1)S(1)}, bf16[2,2,128,128]{3,2,1,0:T(8,128)(2,1)S(1)}, u32[]{:S(2)}, u32[]{:S(2)}) collective-permute-start(bf16[2,2,128,128]{3,2,1,0:T(8,128)(2,1)S(1)} %get-tuple-element.71), channel_id=1, source_target_pairs={{4,0},{6,2},{8,4},{10,6},{12,8},{14,10},{5,1},{7,3},{9,5},{11,7},{... | collective-permute-start | bytes 393224 | tf_op jit(solution)/shard_map/ppermute | solution.py:429
  52.8 1.3 %collective-permute-start.15 = (bf16[2,2,128,128]{3,2,1,0:T(8,128)(2,1)S(1)}, bf16[2,2,128,128]{3,2,1,0:T(8,128)(2,1)S(1)}, u32[]{:S(2)}, u32[]{:S(2)}) collective-permute-start(bf16[2,2,128,128]{3,2,1,0:T(8,128)(2,1)S(1)} %get-tuple-element.70), channel_id=1, source_target_pairs={{8,0},{10,2},{12,4},{14,6},{9,1},{11,3},{13,5},{15,7},{24,16},{26,... | collective-permute-start | bytes 393224 | tf_op jit(solution)/shard_map/ppermute | solution.py:429
  54.1 0.0 collective-permute-done.9.refs_7_
  54.1 1.3 %collective-permute-start.14 = (bf16[2,2,128,128]{3,2,1,0:T(8,128)(2,1)S(1)}, bf16[2,2,128,128]{3,2,1,0:T(8,128)(2,1)S(1)}, u32[]{:S(2)}, u32[]{:S(2)}) collective-permute-start(bf16[2,2,128,128]{3,2,1,0:T(8,128)(2,1)S(1)} %get-tuple-element.69), channel_id=1, source_target_pairs={{12,0},{14,2},{13,1},{15,3},{28,16},{30,18},{29,17},{31,19}} | collective-permute-start | bytes 393224 | tf_op jit(solution)/shard_map/ppermute | solution.py:429
  55.4 0.0 collective-permute-done.11.refs_9_
  55.4 1.1 %collective-permute-start.12 = (bf16[128,640]{1,0:T(8,128)(2,1)S(1)}, bf16[128,640]{1,0:T(8,128)(2,1)S(1)}, u32[]{:S(2)}, u32[]{:S(2)}) collective-permute-start(bf16[128,640]{1,0:T(8,128)(2,1)S(1)} %get-tuple-element.65), channel_id=1, source_target_pairs={{0,2},{2,0},{4,6},{6,4},{8,10},{10,8},{12,14},{14,12},{1,3},{3,1},... | collective-permute-start | bytes 491528 | tf_op jit(solution)/shard_map/ppermute | solution.py:429
  56.6 0.0 collective-permute-done.8.refs_5_
  56.6 4.4 %tree_attention_backward.3 = (bf16[128,640]{1,0:T(8,128)(2,1)S(1)}, bf16[128,640]{1,0:T(8,128)(2,1)S(1)}, bf16[2,2,128,128]{3,2,1,0:T(8,128)(2,1)S(1)}, bf16[2,2...) custom-call(s32[1]{0:T(128)} %bitcast.own_ref.refs_0_, ...), custom_call_target="tpu_custom_call" | custom-call | flops 1048576000 | bytes 8388608 | tf_op jit(solution)/shard_map/tree_attention_backward/pallas_call | solution.py:344
  61.0 1.0 %collective-permute-start.13 = (bf16[128,640]{1,0:T(8,128)(2,1)S(1)}, bf16[128,640]{1,0:T(8,128)(2,1)S(1)}, u32[]{:S(2)}, u32[]{:S(2)}) collective-permute-start(bf16[128,640]{1,0:T(8,128)(2,1)S(1)} %get-tuple-element.66), channel_id=1, source_target_pairs={{0,2},{2,0},{4,6},{6,4},{8,10},{10,8},{12,14},{14,12},{1,3},{3,1},... | collective-permute-start | bytes 491528 | tf_op jit(solution)/shard_map/ppermute | solution.py:429
  62.1 0.0 collective-permute-done.16.refs_5_
  62.1 1.3 %collective-permute-start.20 = (bf16[2,2,128,128]{3,2,1,0:T(8,128)(2,1)S(1)}, bf16[2,2,128,128]{3,2,1,0:T(8,128)(2,1)S(1)}, u32[]{:S(2)}, u32[]{:S(2)}) collective-permute-start(bf16[2,2,128,128]{3,2,1,0:T(8,128)(2,1)S(1)} %get-tuple-element.76), channel_id=1, source_target_pairs={{4,0},{6,2},{8,4},{10,6},{12,8},{14,10},{5,1},{7,3},{9,5},{11,7},{... | collective-permute-start | bytes 393224 | tf_op jit(solution)/shard_map/ppermute | solution.py:429
  63.3 1.3 %collective-permute-done.15.refs_4_ = bf16[2,2,128,128]{3,2,1,0:T(8,128)(2,1)S(1)} collective-permute-done((bf16[2,2,128,128]{3,2,1,0:T(8,128)(2,1)S(1)}, bf16[2,2,128,128]{3,2,1,0:T(8,128)(2,1)S(1)}, u32[]{:S(2)}, u32[]{:S(2)}) %collective-permute-start.15) | collective-permute-done | bytes 131104 | tf_op jit(solution)/shard_map/ppermute | solution.py:429
  64.7 1.3 %collective-permute-start.19 = (bf16[2,2,128,128]{3,2,1,0:T(8,128)(2,1)S(1)}, bf16[2,2,128,128]{3,2,1,0:T(8,128)(2,1)S(1)}, u32[]{:S(2)}, u32[]{:S(2)}) collective-permute-start(bf16[2,2,128,128]{3,2,1,0:T(8,128)(2,1)S(1)} %get-tuple-element.75), channel_id=1, source_target_pairs={{8,0},{10,2},{12,4},{14,6},{9,1},{11,3},{13,5},{15,7},{24,16},{26,... | collective-permute-start | bytes 393224 | tf_op jit(solution)/shard_map/ppermute | solution.py:429
  66.0 0.0 collective-permute-done.14.refs_3_
  66.0 1.3 %collective-permute-start.18 = (bf16[2,2,128,128]{3,2,1,0:T(8,128)(2,1)S(1)}, bf16[2,2,128,128]{3,2,1,0:T(8,128)(2,1)S(1)}, u32[]{:S(2)}, u32[]{:S(2)}) collective-permute-start(bf16[2,2,128,128]{3,2,1,0:T(8,128)(2,1)S(1)} %get-tuple-element.74), channel_id=1, source_target_pairs={{12,0},{14,2},{13,1},{15,3},{28,16},{30,18},{29,17},{31,19}} | collective-permute-start | bytes 393224 | tf_op jit(solution)/shard_map/ppermute | solution.py:429
  67.4 4.0 %collective-permute-done.20.refs_9_ = bf16[2,2,128,128]{3,2,1,0:T(8,128)(2,1)S(1)} collective-permute-done((bf16[2,2,128,128]{3,2,1,0:T(8,128)(2,1)S(1)}, bf16[2,2,128,128]{3,2,1,0:T(8,128)(2,1)S(1)}, u32[]{:S(2)}, u32[]{:S(2)}) %collective-permute-start.20) | collective-permute-done | bytes 131104 | tf_op jit(solution)/shard_map/ppermute | solution.py:429
  71.4 0.9 %collective-permute-start.17 = (bf16[2,128,128]{2,1,0:T(8,128)(2,1)S(1)}, bf16[2,128,128]{2,1,0:T(8,128)(2,1)S(1)}, u32[]{:S(2)}, u32[]{:S(2)}) collective-permute-start(bf16[2,128,128]{2,1,0:T(8,128)(2,1)S(1)} %fusion), channel_id=1, source_target_pairs={{0,2},{2,0},{4,6},{6,4},{8,10},{10,8},{12,14},{14,12},{1,3},{3,1},... | collective-permute-start | bytes 196616 | tf_op jit(solution)/shard_map/ppermute | solution.py:429
  72.3 3.5 %collective-permute-done.19.refs_8_ = bf16[2,2,128,128]{3,2,1,0:T(8,128)(2,1)S(1)} collective-permute-done((bf16[2,2,128,128]{3,2,1,0:T(8,128)(2,1)S(1)}, bf16[2,2,128,128]{3,2,1,0:T(8,128)(2,1)S(1)}, u32[]{:S(2)}, u32[]{:S(2)}) %collective-permute-start.19) | collective-permute-done | bytes 131104 | tf_op jit(solution)/shard_map/ppermute | solution.py:429
  75.8 0.0 collective-permute-done.18.refs_7_
  75.8 1.6 %collective-permute-start.21 = (bf16[2,128,128]{2,1,0:T(8,128)(2,1)S(1)}, bf16[2,128,128]{2,1,0:T(8,128)(2,1)S(1)}, u32[]{:S(2)}, u32[]{:S(2)}) collective-permute-start(bf16[2,128,128]{2,1,0:T(8,128)(2,1)S(1)} %fusion.1), channel_id=1, source_target_pairs={{0,2},{2,0},{4,6},{6,4},{8,10},{10,8},{12,14},{14,12},{1,3},{3,1},... | collective-permute-start | bytes 196616 | tf_op jit(solution)/shard_map/ppermute | solution.py:429
  77.4 0.0 collective-permute-done.12.refs_2_
  77.4 0.7 copy-done.17
  78.1 0.7 copy-done.18
  78.7 2.1 %join_queries.1 = bf16[128,2560]{1,0:T(8,128)(2,1)} custom-call(s32[1]{0:T(128)} %bitcast.own_ref.refs_0_, bf16[128,640]{1,0:T(8,128)(2,1)} %copy-done.2, bf16[128,640]{1,0:T(8,128)(2,1)} %copy-done.3, bf16[128,640]{1,0:T(8,128)(2,1)} %copy-done.17, bf16[128,640]{1,0:T(8,128)(2,1)} %copy-done.18), custom_call_target="tpu_custom_call" | custom-call | bytes 1310720 | tf_op jit(solution)/shard_map/join_queries/pallas_call | solution.py:382
  80.8 0.0 collective-permute-done.17.refs_0_
  80.8 0.6 copy-done.20
  81.4 0.6 copy-done.21
  82.1 2.1 %join_keys.1 = (bf16[128,512]{1,0:T(8,128)(2,1)}, bf16[128,512]{1,0:T(8,128)(2,1)}) custom-call(s32[1]{0:T(128)} %bitcast.own_ref.refs_0_, bf16[2,128,128]{2,1,0:T(8,128)(2,1)} %copy-done.20, bf16[2,128,128]{2,1,0:T(8,128)(2,1)} %copy-done.21, bf16[2,2,128,128]{3,2,1,0:T(8,128)(2,1)} %copy-done, bf16[2,2,128,128]{3,2,1,0:T(8,128)(2,1)} %copy-done.13, ...), custom_call_target="tpu_custom_call" | custom-call | bytes 524288 | tf_op jit(solution)/shard_map/join_keys/pallas_call | solution.py:416
  (40 shorter events, 0.2 us)
Async XLA Ops:
  2.4 13.1 %collective-permute-start.3 = (bf16[2,2,128,128]{3,2,1,0:T(8,128)(2,1)}, bf16[2,2,128,128]{3,2,1,0:T(8,128)(2,1)S(1)}, u32[]{:S(2)}, u32[]{:S(2)}) collective-permute-start(bf16[2,2,128,128]{3,2,1,0:T(8,128)(2,1)} %get-tuple-element.45), channel_id=1, source_target_pairs={{0,2},{2,0},{4,6},{6,4},{8,10},{10,8},{12,14},{14,12},{1,3},{3,1},... | collective-permute-start | bytes 393224 | tf_op jit(solution)/shard_map/ppermute | solution.py:429
  5.4 3.9 %collective-permute-start = (f32[8,256]{1,0:T(8,128)}, f32[8,256]{1,0:T(8,128)S(1)}, u32[]{:S(2)}, u32[]{:S(2)}) collective-permute-start(f32[8,256]{1,0:T(8,128)} %get-tuple-element.42), channel_id=1, source_target_pairs={{0,2},{2,0},{4,6},{6,4},{8,10},{10,8},{12,14},{14,12},{1,3},{3,1},... | collective-permute-start | bytes 24584 | tf_op jit(solution)/shard_map/ppermute | solution.py:429
  9.9 5.5 %collective-permute-start.1 = (f32[8,256]{1,0:T(8,128)S(1)}, f32[8,256]{1,0:T(8,128)S(1)}, u32[]{:S(2)}, u32[]{:S(2)}) collective-permute-start(f32[8,256]{1,0:T(8,128)S(1)} %add.34), channel_id=1, source_target_pairs={{4,0},{6,2},{8,4},{10,6},{12,8},{14,10},{5,1},{7,3},{9,5},{11,7},{... | collective-permute-start | bytes 24584 | tf_op jit(solution)/shard_map/ppermute | solution.py:429
  13.9 26.6 %copy-start.5 = (bf16[2,5,128,128]{3,2,1,0:T(8,128)(2,1)S(1)}, bf16[2,5,128,128]{3,2,1,0:T(8,128)(2,1)}, u32[]{:S(2)}) copy-start(bf16[2,5,128,128]{3,2,1,0:T(8,128)(2,1)} %get-tuple-element.47.refs_4_) | copy-start | bytes 983044
  15.5 12.9 %copy-start.22 = (f32[8,256]{1,0:T(8,128)}, f32[8,256]{1,0:T(8,128)S(1)}, u32[]{:S(2)}) copy-start(f32[8,256]{1,0:T(8,128)S(1)} %add.35.near_ref) | copy-start | bytes 24580
  15.5 0.7 copy-start.19
  17.8 20.4 %collective-permute-start.4 = (bf16[2,5,128,128]{3,2,1,0:T(8,128)(2,1)}, bf16[2,5,128,128]{3,2,1,0:T(8,128)(2,1)S(1)}, u32[]{:S(2)}, u32[]{:S(2)}) collective-permute-start(bf16[2,5,128,128]{3,2,1,0:T(8,128)(2,1)} %get-tuple-element.52), channel_id=1, source_target_pairs={{0,2},{2,0},{4,6},{6,4},{8,10},{10,8},{12,14},{14,12},{1,3},{3,1},... | collective-permute-start | bytes 983048 | tf_op jit(solution)/shard_map/ppermute | solution.py:429
  19.6 19.2 %collective-permute-start.5 = (bf16[2,2,128,128]{3,2,1,0:T(8,128)(2,1)}, bf16[2,2,128,128]{3,2,1,0:T(8,128)(2,1)S(1)}, u32[]{:S(2)}, u32[]{:S(2)}) collective-permute-start(bf16[2,2,128,128]{3,2,1,0:T(8,128)(2,1)} %get-tuple-element.51.refs_6_), channel_id=1, source_target_pairs={{0,4},{2,6},{4,8},{6,10},{8,12},{10,14},{1,5},{3,7},{5,9},{7,11},{... | collective-permute-start | bytes 393224 | tf_op jit(solution)/shard_map/ppermute | solution.py:429
  23.0 15.7 %collective-permute-start.6 = (bf16[2,2,128,128]{3,2,1,0:T(8,128)(2,1)}, bf16[2,2,128,128]{3,2,1,0:T(8,128)(2,1)S(1)}, u32[]{:S(2)}, u32[]{:S(2)}) collective-permute-start(bf16[2,2,128,128]{3,2,1,0:T(8,128)(2,1)} %get-tuple-element.51.refs_6_), channel_id=1, source_target_pairs={{0,8},{2,10},{4,12},{6,14},{1,9},{3,11},{5,13},{7,15},{16,24},{18,... | collective-permute-start | bytes 393224 | tf_op jit(solution)/shard_map/ppermute | solution.py:429
  27.0 11.7 %collective-permute-start.7 = (bf16[2,2,128,128]{3,2,1,0:T(8,128)(2,1)}, bf16[2,2,128,128]{3,2,1,0:T(8,128)(2,1)S(1)}, u32[]{:S(2)}, u32[]{:S(2)}) collective-permute-start(bf16[2,2,128,128]{3,2,1,0:T(8,128)(2,1)} %get-tuple-element.51.refs_6_), channel_id=1, source_target_pairs={{0,12},{2,14},{1,13},{3,15},{16,28},{18,30},{17,29},{19,31}} | collective-permute-start | bytes 393224 | tf_op jit(solution)/shard_map/ppermute | solution.py:429
  28.3 6.4 %collective-permute-start.2 = (f32[8,256]{1,0:T(8,128)S(1)}, f32[8,256]{1,0:T(8,128)S(1)}, u32[]{:S(2)}, u32[]{:S(2)}) collective-permute-start(f32[8,256]{1,0:T(8,128)S(1)} %add.35.near_ref), channel_id=1, source_target_pairs={{8,0},{10,2},{12,4},{14,6},{9,1},{11,3},{13,5},{15,7},{24,16},{26,... | collective-permute-start | bytes 24584 | tf_op jit(solution)/shard_map/ppermute | solution.py:429
  34.8 0.6 copy-start.23
  38.2 18.4 %collective-permute-start.8 = (bf16[2,5,128,128]{3,2,1,0:T(8,128)(2,1)}, bf16[2,5,128,128]{3,2,1,0:T(8,128)(2,1)S(1)}, u32[]{:S(2)}, u32[]{:S(2)}) collective-permute-start(bf16[2,5,128,128]{3,2,1,0:T(8,128)(2,1)} %get-tuple-element.59), channel_id=1, source_target_pairs={{0,2},{2,0},{4,6},{6,4},{8,10},{10,8},{12,14},{14,12},{1,3},{3,1},... | collective-permute-start | bytes 983048 | tf_op jit(solution)/shard_map/ppermute | solution.py:429
  38.8 12.1 %collective-permute-start.10 = (bf16[2,2,128,128]{3,2,1,0:T(8,128)(2,1)}, bf16[2,2,128,128]{3,2,1,0:T(8,128)(2,1)S(1)}, u32[]{:S(2)}, u32[]{:S(2)}) collective-permute-start(bf16[2,2,128,128]{3,2,1,0:T(8,128)(2,1)} %get-tuple-element.62.refs_6_), channel_id=1, source_target_pairs={{0,8},{2,10},{4,12},{6,14},{1,9},{3,11},{5,13},{7,15},{16,24},{18,... | collective-permute-start | bytes 393224 | tf_op jit(solution)/shard_map/ppermute | solution.py:429
  40.4 0.7 copy-start.8
  41.1 0.9 %copy-start.7 = (bf16[2,2,128,128]{3,2,1,0:T(8,128)(2,1)S(1)}, bf16[2,2,128,128]{3,2,1,0:T(8,128)(2,1)}, u32[]{:S(2)}) copy-start(bf16[2,2,128,128]{3,2,1,0:T(8,128)(2,1)} %get-tuple-element.51.refs_6_) | copy-start | bytes 393220
  42.0 1.1 %copy-start.9 = (f32[2,640,128]{2,1,0:T(8,128)S(1)}, f32[2,640,128]{2,1,0:T(8,128)}, u32[]{:S(2)}) copy-start(f32[2,640,128]{2,1,0:T(8,128)} %get-tuple-element.44.refs_3_) | copy-start | bytes 1966084
  43.1 0.9 %copy-start.10 = (f32[2,128,128]{2,1,0:T(8,128)S(1)}, f32[2,128,128]{2,1,0:T(8,128)}, u32[]{:S(2)}) copy-start(f32[2,128,128]{2,1,0:T(8,128)} %get-tuple-element.43.refs_2_) | copy-start | bytes 393220
  44.0 5.1 %copy-start.6 = (bf16[2,2,128,128]{3,2,1,0:T(8,128)(2,1)S(1)}, bf16[2,2,128,128]{3,2,1,0:T(8,128)(2,1)}, u32[]{:S(2)}) copy-start(bf16[2,2,128,128]{3,2,1,0:T(8,128)(2,1)} %get-tuple-element.62.refs_6_) | copy-start | bytes 393220
  44.0 12.6 %copy-start.4 = (bf16[2,5,128,128]{3,2,1,0:T(8,128)(2,1)S(1)}, bf16[2,5,128,128]{3,2,1,0:T(8,128)(2,1)}, u32[]{:S(2)}) copy-start(bf16[2,5,128,128]{3,2,1,0:T(8,128)(2,1)} %get-tuple-element.57.refs_4_) | copy-start | bytes 983044
  48.4 0.7 copy-start.2
  49.1 18.2 %copy-start = (bf16[2,2,128,128]{3,2,1,0:T(8,128)(2,1)}, bf16[2,2,128,128]{3,2,1,0:T(8,128)(2,1)S(1)}, u32[]{:S(2)}) copy-start(bf16[2,2,128,128]{3,2,1,0:T(8,128)(2,1)S(1)} %get-tuple-element.68.refs_2_) | copy-start | bytes 393220
  49.1 5.0 %collective-permute-start.9 = (bf16[2,2,128,128]{3,2,1,0:T(8,128)(2,1)S(1)}, bf16[2,2,128,128]{3,2,1,0:T(8,128)(2,1)S(1)}, u32[]{:S(2)}, u32[]{:S(2)}) collective-permute-start(bf16[2,2,128,128]{3,2,1,0:T(8,128)(2,1)S(1)} %copy-done.6), channel_id=1, source_target_pairs={{0,4},{2,6},{4,8},{6,10},{8,12},{10,14},{1,5},{3,7},{5,9},{7,11},{... | collective-permute-start | bytes 393224 | tf_op jit(solution)/shard_map/ppermute | solution.py:429
  50.8 4.6 %collective-permute-start.11 = (bf16[2,2,128,128]{3,2,1,0:T(8,128)(2,1)S(1)}, bf16[2,2,128,128]{3,2,1,0:T(8,128)(2,1)S(1)}, u32[]{:S(2)}, u32[]{:S(2)}) collective-permute-start(bf16[2,2,128,128]{3,2,1,0:T(8,128)(2,1)S(1)} %collective-permute-done.10.refs_8_), channel_id=1, source_target_pairs={{8,12},{10,14},{9,13},{11,15},{24,28},{26,30},{25,29},{27,31}} | collective-permute-start | bytes 393224 | tf_op jit(solution)/shard_map/ppermute | solution.py:429
  51.5 10.6 %collective-permute-start.16 = (bf16[2,2,128,128]{3,2,1,0:T(8,128)(2,1)S(1)}, bf16[2,2,128,128]{3,2,1,0:T(8,128)(2,1)S(1)}, u32[]{:S(2)}, u32[]{:S(2)}) collective-permute-start(bf16[2,2,128,128]{3,2,1,0:T(8,128)(2,1)S(1)} %get-tuple-element.71), channel_id=1, source_target_pairs={{4,0},{6,2},{8,4},{10,6},{12,8},{14,10},{5,1},{7,3},{9,5},{11,7},{... | collective-permute-start | bytes 393224 | tf_op jit(solution)/shard_map/ppermute | solution.py:429
  52.8 11.9 %collective-permute-start.15 = (bf16[2,2,128,128]{3,2,1,0:T(8,128)(2,1)S(1)}, bf16[2,2,128,128]{3,2,1,0:T(8,128)(2,1)S(1)}, u32[]{:S(2)}, u32[]{:S(2)}) collective-permute-start(bf16[2,2,128,128]{3,2,1,0:T(8,128)(2,1)S(1)} %get-tuple-element.70), channel_id=1, source_target_pairs={{8,0},{10,2},{12,4},{14,6},{9,1},{11,3},{13,5},{15,7},{24,16},{26,... | collective-permute-start | bytes 393224 | tf_op jit(solution)/shard_map/ppermute | solution.py:429
  54.1 11.9 %collective-permute-start.14 = (bf16[2,2,128,128]{3,2,1,0:T(8,128)(2,1)S(1)}, bf16[2,2,128,128]{3,2,1,0:T(8,128)(2,1)S(1)}, u32[]{:S(2)}, u32[]{:S(2)}) collective-permute-start(bf16[2,2,128,128]{3,2,1,0:T(8,128)(2,1)S(1)} %get-tuple-element.69), channel_id=1, source_target_pairs={{12,0},{14,2},{13,1},{15,3},{28,16},{30,18},{29,17},{31,19}} | collective-permute-start | bytes 393224 | tf_op jit(solution)/shard_map/ppermute | solution.py:429
  55.4 22.0 %collective-permute-start.12 = (bf16[128,640]{1,0:T(8,128)(2,1)S(1)}, bf16[128,640]{1,0:T(8,128)(2,1)S(1)}, u32[]{:S(2)}, u32[]{:S(2)}) collective-permute-start(bf16[128,640]{1,0:T(8,128)(2,1)S(1)} %get-tuple-element.65), channel_id=1, source_target_pairs={{0,2},{2,0},{4,6},{6,4},{8,10},{10,8},{12,14},{14,12},{1,3},{3,1},... | collective-permute-start | bytes 491528 | tf_op jit(solution)/shard_map/ppermute | solution.py:429
  61.0 6.3 %copy-start.3 = (bf16[128,640]{1,0:T(8,128)(2,1)}, bf16[128,640]{1,0:T(8,128)(2,1)S(1)}, u32[]{:S(2)}) copy-start(bf16[128,640]{1,0:T(8,128)(2,1)S(1)} %get-tuple-element.64.refs_1_) | copy-start | bytes 491524
  61.0 14.7 %copy-start.1 = (bf16[2,2,128,128]{3,2,1,0:T(8,128)(2,1)}, bf16[2,2,128,128]{3,2,1,0:T(8,128)(2,1)S(1)}, u32[]{:S(2)}) copy-start(bf16[2,2,128,128]{3,2,1,0:T(8,128)(2,1)S(1)} %get-tuple-element.73.refs_6_) | copy-start | bytes 393220
  61.0 16.4 %collective-permute-start.13 = (bf16[128,640]{1,0:T(8,128)(2,1)S(1)}, bf16[128,640]{1,0:T(8,128)(2,1)S(1)}, u32[]{:S(2)}, u32[]{:S(2)}) collective-permute-start(bf16[128,640]{1,0:T(8,128)(2,1)S(1)} %get-tuple-element.66), channel_id=1, source_target_pairs={{0,2},{2,0},{4,6},{6,4},{8,10},{10,8},{12,14},{14,12},{1,3},{3,1},... | collective-permute-start | bytes 491528 | tf_op jit(solution)/shard_map/ppermute | solution.py:429
  62.1 18.7 %copy-start.11 = (bf16[2,2,128,128]{3,2,1,0:T(8,128)(2,1)}, bf16[2,2,128,128]{3,2,1,0:T(8,128)(2,1)S(1)}, u32[]{:S(2)}) copy-start(bf16[2,2,128,128]{3,2,1,0:T(8,128)(2,1)S(1)} %collective-permute-done.16.refs_5_) | copy-start | bytes 393220
  62.1 9.3 %collective-permute-start.20 = (bf16[2,2,128,128]{3,2,1,0:T(8,128)(2,1)S(1)}, bf16[2,2,128,128]{3,2,1,0:T(8,128)(2,1)S(1)}, u32[]{:S(2)}, u32[]{:S(2)}) collective-permute-start(bf16[2,2,128,128]{3,2,1,0:T(8,128)(2,1)S(1)} %get-tuple-element.76), channel_id=1, source_target_pairs={{4,0},{6,2},{8,4},{10,6},{12,8},{14,10},{5,1},{7,3},{9,5},{11,7},{... | collective-permute-start | bytes 393224 | tf_op jit(solution)/shard_map/ppermute | solution.py:429
  64.7 16.1 %copy-start.12 = (bf16[2,2,128,128]{3,2,1,0:T(8,128)(2,1)}, bf16[2,2,128,128]{3,2,1,0:T(8,128)(2,1)S(1)}, u32[]{:S(2)}) copy-start(bf16[2,2,128,128]{3,2,1,0:T(8,128)(2,1)S(1)} %collective-permute-done.15.refs_4_) | copy-start | bytes 393220
  64.7 11.1 %collective-permute-start.19 = (bf16[2,2,128,128]{3,2,1,0:T(8,128)(2,1)S(1)}, bf16[2,2,128,128]{3,2,1,0:T(8,128)(2,1)S(1)}, u32[]{:S(2)}, u32[]{:S(2)}) collective-permute-start(bf16[2,2,128,128]{3,2,1,0:T(8,128)(2,1)S(1)} %get-tuple-element.75), channel_id=1, source_target_pairs={{8,0},{10,2},{12,4},{14,6},{9,1},{11,3},{13,5},{15,7},{24,16},{26,... | collective-permute-start | bytes 393224 | tf_op jit(solution)/shard_map/ppermute | solution.py:429
  66.0 14.8 %copy-start.13 = (bf16[2,2,128,128]{3,2,1,0:T(8,128)(2,1)}, bf16[2,2,128,128]{3,2,1,0:T(8,128)(2,1)S(1)}, u32[]{:S(2)}) copy-start(bf16[2,2,128,128]{3,2,1,0:T(8,128)(2,1)S(1)} %collective-permute-done.14.refs_3_) | copy-start | bytes 393220
  66.0 9.8 %collective-permute-start.18 = (bf16[2,2,128,128]{3,2,1,0:T(8,128)(2,1)S(1)}, bf16[2,2,128,128]{3,2,1,0:T(8,128)(2,1)S(1)}, u32[]{:S(2)}, u32[]{:S(2)}) collective-permute-start(bf16[2,2,128,128]{3,2,1,0:T(8,128)(2,1)S(1)} %get-tuple-element.74), channel_id=1, source_target_pairs={{12,0},{14,2},{13,1},{15,3},{28,16},{30,18},{29,17},{31,19}} | collective-permute-start | bytes 393224 | tf_op jit(solution)/shard_map/ppermute | solution.py:429
  71.4 9.4 %copy-start.14 = (bf16[2,2,128,128]{3,2,1,0:T(8,128)(2,1)}, bf16[2,2,128,128]{3,2,1,0:T(8,128)(2,1)S(1)}, u32[]{:S(2)}) copy-start(bf16[2,2,128,128]{3,2,1,0:T(8,128)(2,1)S(1)} %collective-permute-done.20.refs_9_) | copy-start | bytes 393220
  71.4 9.4 %collective-permute-start.17 = (bf16[2,128,128]{2,1,0:T(8,128)(2,1)S(1)}, bf16[2,128,128]{2,1,0:T(8,128)(2,1)S(1)}, u32[]{:S(2)}, u32[]{:S(2)}) collective-permute-start(bf16[2,128,128]{2,1,0:T(8,128)(2,1)S(1)} %fusion), channel_id=1, source_target_pairs={{0,2},{2,0},{4,6},{6,4},{8,10},{10,8},{12,14},{14,12},{1,3},{3,1},... | collective-permute-start | bytes 196616 | tf_op jit(solution)/shard_map/ppermute | solution.py:429
  75.8 5.0 %copy-start.15 = (bf16[2,2,128,128]{3,2,1,0:T(8,128)(2,1)}, bf16[2,2,128,128]{3,2,1,0:T(8,128)(2,1)S(1)}, u32[]{:S(2)}) copy-start(bf16[2,2,128,128]{3,2,1,0:T(8,128)(2,1)S(1)} %collective-permute-done.19.refs_8_) | copy-start | bytes 393220
  75.8 5.0 %copy-start.16 = (bf16[2,2,128,128]{3,2,1,0:T(8,128)(2,1)}, bf16[2,2,128,128]{3,2,1,0:T(8,128)(2,1)S(1)}, u32[]{:S(2)}) copy-start(bf16[2,2,128,128]{3,2,1,0:T(8,128)(2,1)S(1)} %collective-permute-done.18.refs_7_) | copy-start | bytes 393220
  75.8 5.0 %collective-permute-start.21 = (bf16[2,128,128]{2,1,0:T(8,128)(2,1)S(1)}, bf16[2,128,128]{2,1,0:T(8,128)(2,1)S(1)}, u32[]{:S(2)}, u32[]{:S(2)}) collective-permute-start(bf16[2,128,128]{2,1,0:T(8,128)(2,1)S(1)} %fusion.1), channel_id=1, source_target_pairs={{0,2},{2,0},{4,6},{6,4},{8,10},{10,8},{12,14},{14,12},{1,3},{3,1},... | collective-permute-start | bytes 196616 | tf_op jit(solution)/shard_map/ppermute | solution.py:429
  77.4 0.7 copy-start.17
  78.1 0.7 copy-start.18
  80.8 0.6 copy-start.20
  81.4 0.6 copy-start.21

commit v5 on v4

--- a/solution.py
+++ b/solution.py
@@ -13,7 +13,9 @@
 BETA = 0.1
 LAMBDA_SEG = 0.7
 PAIRED_GROUPS = 8
+TERM_ROWS = 16
 LOG2E = math.log2(math.e)
+SMALL = pltpu.CompilerParams(vmem_limit_bytes=8 * 1024 * 1024)
 
 
 def lookup(table_values, lookup_ids):
@@ -44,9 +46,17 @@
     return deltas, firsts
 
 
+def split_float(value):
+    parts = []
+    for _ in range(3):
+        part = value.astype(jnp.bfloat16)
+        parts.append(part)
+        value = value - part.astype(jnp.float32)
+    return parts
+
+
 def pack_kernel(
     log_rate,
-    parts,
     own_ref,
     lengths_ref,
     k_ref,
@@ -55,18 +65,14 @@
     logprobs_ref,
     ref_logprobs_ref,
     values_ref,
-    *out_refs,
+    kept_ref,
+    terms_ref,
+    given_ref=None,
 ):
-    terms_ref = out_refs[-1]
     own = own_ref[0]
-    heads = k_ref.shape[1] // HD // parts
-    for step, out_ref in enumerate(out_refs[:-1]):
-        part = lax.rem(own + step, parts)
-        for h in range(heads):
-            columns = pl.ds(pl.multiple_of((part * heads + h) * HD, HD), HD)
-            out_ref[h, 0] = k_ref[:, columns]
-            out_ref[h, 1] = v_ref[:, columns]
     length = k_ref.shape[0]
+    heads = kept_ref.shape[0]
+    parts = k_ref.shape[1] // HD // heads
     deltas, firsts = token_terms(
         log_rate,
         lengths_ref[own],
@@ -78,6 +84,21 @@
     mine = lax.broadcasted_iota(jnp.int32, (terms_ref.shape[0], length), 0) == own
     terms_ref[:, :length] = jnp.where(mine, deltas, 0.0)
     terms_ref[:, length:] = jnp.where(mine, firsts, 0.0)
+    for step in range(parts):
+        part = lax.rem(own + step, parts)
+        for h in range(heads):
+            columns = pl.ds(pl.multiple_of((part * heads + h) * HD, HD), HD)
+            for plane, ref in enumerate((k_ref, v_ref)):
+                if step == 0:
+                    kept_ref[h, plane] = ref[:, columns]
+                else:
+                    first = (h * 2 + plane) * length
+                    given_ref[first : first + length, :] = ref[:, columns]
+    if parts == 2:
+        first = 2 * heads * length
+        rows = [part.astype(jnp.float32) for x in (deltas, firsts) for part in split_float(x)]
+        rows.append(jnp.zeros((TERM_ROWS - len(rows), HD), jnp.float32))
+        given_ref[first : first + TERM_ROWS, :] = jnp.concatenate(rows).astype(jnp.bfloat16)
 
 
 def pack(own, lengths, k, v, token_rows, parts, log_rate):
@@ -85,16 +106,22 @@
     smem = pl.BlockSpec(memory_space=pltpu.SMEM)
     vmem = pl.BlockSpec(memory_space=pltpu.VMEM)
     heads = width // HD // parts
-    block = jax.ShapeDtypeStruct((heads, 2, length, HD), k.dtype)
-    terms = jax.ShapeDtypeStruct((lengths.shape[0], 2 * length), jnp.float32)
+    out_shape = [
+        jax.ShapeDtypeStruct((heads, 2, length, HD), k.dtype),
+        jax.ShapeDtypeStruct((lengths.shape[0], 2 * length), jnp.float32),
+    ]
+    if parts == 2:
+        assert length == HD
+        out_shape.append(jax.ShapeDtypeStruct((2 * heads * length + TERM_ROWS, HD), k.dtype))
     return pl.pallas_call(
-        functools.partial(pack_kernel, log_rate, parts),
-        out_shape=(block,) * parts + (terms,),
+        functools.partial(pack_kernel, log_rate),
+        out_shape=out_shape,
         in_specs=[smem] * 2 + [vmem] * 6,
-        out_specs=(vmem,) * (parts + 1),
+        out_specs=[vmem] * len(out_shape),
         cost_estimate=pl.CostEstimate(
             flops=length * 100, bytes_accessed=8 * length * width, transcendentals=length
         ),
+        compiler_params=SMALL,
         name="pack_keys_values",
     )(own, lengths, k, v, *token_rows)
 
@@ -125,28 +152,44 @@
         in_specs=[smem, vmem, vmem],
         out_specs=(vmem,) * (parts * chunks),
         cost_estimate=pl.CostEstimate(flops=0, bytes_accessed=8 * length * width, transcendentals=0),
+        compiler_params=SMALL,
         name="pack_queries",
     )(own, q, direction)
     return [outs[step * chunks : (step + 1) * chunks] for step in range(parts)]
 
 
-def join_blocks_kernel(mine_ref, other_ref, *out_refs):
-    for chunk, out_ref in enumerate(out_refs):
-        out_ref[0] = mine_ref[chunk]
-        out_ref[1] = other_ref[chunk]
-
-
-def join_blocks(mine, other):
+def join_blocks_kernel(own_ref, terms_ref, mine_ref, other_ref, all_terms_ref, *out_refs):
+    heads, _, length, _ = mine_ref.shape
+    for h, out_ref in enumerate(out_refs):
+        out_ref[0] = mine_ref[h]
+        for plane in range(2):
+            first = (h * 2 + plane) * length
+            out_ref[1, plane] = other_ref[first : first + length, :]
+    tail = other_ref[2 * heads * length :, :].astype(jnp.float32)
+    own = own_ref[0]
+    other = own + 1 - 2 * lax.rem(own, 2)
+    mine = lax.broadcasted_iota(jnp.int32, (terms_ref.shape[0], length), 0) == other
+    for i in range(2):
+        columns = slice(i * length, (i + 1) * length)
+        row = tail[3 * i : 3 * i + 1] + tail[3 * i + 1 : 3 * i + 2] + tail[3 * i + 2 : 3 * i + 3]
+        all_terms_ref[:, columns] = terms_ref[:, columns] + jnp.where(mine, row, 0.0)
+
+
+def join_blocks(own, terms, mine, other):
     chunks = mine.shape[0]
+    smem = pl.BlockSpec(memory_space=pltpu.SMEM)
     vmem = pl.BlockSpec(memory_space=pltpu.VMEM)
-    return pl.pallas_call(
+    block = jax.ShapeDtypeStruct((2,) + mine.shape[1:], mine.dtype)
+    outs = pl.pallas_call(
         join_blocks_kernel,
-        out_shape=(jax.ShapeDtypeStruct((2,) + mine.shape[1:], mine.dtype),) * chunks,
-        in_specs=[vmem] * 2,
-        out_specs=(vmem,) * chunks,
+        out_shape=(jax.ShapeDtypeStruct(terms.shape, terms.dtype),) + (block,) * chunks,
+        in_specs=[smem] + [vmem] * 3,
+        out_specs=(vmem,) * (chunks + 1),
         cost_estimate=pl.CostEstimate(flops=0, bytes_accessed=8 * mine.size, transcendentals=0),
+        compiler_params=SMALL,
         name="join_blocks",
-    )(mine, other)
+    )(own, terms, mine, other)
+    return outs[0], outs[1:]
 
 
 def prepare_kernel(
@@ -252,6 +295,7 @@
             bytes_accessed=4 * (DEPTH + 1) * segs * length * length,
             transcendentals=length * length,
         ),
+        compiler_params=SMALL,
         name="prepare_advantages",
     )(own, parents, lengths, parents[None], lengths[None], near, far)
 
@@ -352,7 +396,7 @@
             pltpu.VMEM((keys, width), jnp.bfloat16),
             pltpu.VMEM((steps * segs, 2, length, HD), jnp.float32),
         ],
-        compiler_params=pltpu.CompilerParams(vmem_limit_bytes=40 * 1024 * 1024),
+        compiler_params=pltpu.CompilerParams(vmem_limit_bytes=16 * 1024 * 1024),
         cost_estimate=pl.CostEstimate(
             flops=5 * 2 * keys * length * width * segs,
             bytes_accessed=8 * 1024 * 1024,
@@ -387,6 +431,7 @@
         cost_estimate=pl.CostEstimate(
             flops=0, bytes_accessed=4 * length * width * len(dq_list), transcendentals=0
         ),
+        compiler_params=SMALL,
         name="join_queries",
     )(own, *dq_list)
 
@@ -421,6 +466,7 @@
         cost_estimate=pl.CostEstimate(
             flops=0, bytes_accessed=16 * length * HD * chunks, transcendentals=0
         ),
+        compiler_params=SMALL,
         name="join_keys",
     )(own, *others, *flat)
 
@@ -441,14 +487,13 @@
     down = {d: [(i, i - 2 * d) for i in range(2 * d, groups)] for d in (1, 2, 3)}
     forward = [(i, i + 2) for i in range(4, groups - 2)]
 
-    kept, given, terms = pack(own, lengths, key_vectors, value_vectors, token_rows, 2, log_rate)
-    terms = terms + permute(terms, swap)
+    kept, terms, given = pack(own, lengths, key_vectors, value_vectors, token_rows, 2, log_rate)
     taken = permute(given, swap)
     kept_q, given_q = pack_queries(own, after(queries, given), direction, 2, chunks)
-    terms = terms + permute(terms, down[1])
-    near = join_blocks(kept, after(taken, terms))
+    terms, near = join_blocks(own, terms, kept, taken)
     blocks = [[near[0]] + [permute(near[0], up[d]) for d in (3, 2, 1)][::-1]]
     taken_q = [permute(after(given_q[0], near[0]), swap)]
+    terms = terms + permute(terms, down[1])
     row, advantages, bias = prepare(
         own, parents, lengths, terms, permute(terms, down[2]), 2, log_rate
     )

time: 84.8 us -> 74.8 us (0.88)
  Pallas kernels: 22 us -> 13.7 us
  local copies, waits for them, and re-layouts: 8.04 us -> 5.31 us
  starting transfers between devices: 32.9 us -> 34.1 us
    pallas_call x2, Pallas kernels: 3.46 us -> 0.72 us  [the longest x1 0.7 us: pack(): pl.pallas_call(functools.partial(pack_kernel, log_rate), out_shape=out_sh...]
    unnamed x48 -> x20, local copies, waits for them, and re-layouts: 8.04 us -> 5.31 us
    pallas_call x1, Pallas kernels: 2.63 us -> 0.23 us  [pack_queries(): pl.pallas_call(functools.partial(pack_queries_kernel, parts), out_shape=(...]
    pallas_call x1, Pallas kernels: 2.09 us -> 0.77 us  [join_keys(): pl.pallas_call(functools.partial(join_keys_kernel, chunks), out_shape=(ou...]
    ppermute x22 -> x21, starting transfers between devices: 32.9 us -> 34.1 us  [permute(): return lax.ppermute(array, 'seg', pairs)]
    pallas_call x1, Pallas kernels: 2.06 us -> 0.91 us  [join_queries(): pl.pallas_call(functools.partial(join_queries_kernel, len(dq_list) // 2),...]
    ppermute x22 -> x21, waiting for transfers between devices: 19.5 us -> 20.3 us  [permute(): return lax.ppermute(array, 'seg', pairs)]
  transfers between devices with their start and end apart: 22 -> 21, of which waited for: 6 -> 6; matrix products, arithmetic and copies ran while one was open for 1% -> 0% of each run, Pallas kernels for 19% -> 16%
where the time goes in v5:
time: 74.8 us; the launch traced here: 74.3 us
  starting transfers between devices  34.1 us (46%)
  waiting for transfers between devices  20.3 us (27%)
  Pallas kernels  13.7 us (18%)
  local copies, waits for them, and re-layouts  5.31 us (7%)
  between operations  0.89 us (1%)
    ppermute x21, starting transfers between devices, permute(): return lax.ppermute(array, 'seg', pairs)  34.1 us
    ppermute x21, waiting for transfers between devices, permute(): return lax.ppermute(array, 'seg', pairs)  20.3 us
    pallas_call x2, Pallas kernels, attend(): pl.pallas_call(functools.partial(attend_kernel, DEPTH, segs), out_shape=o...  8.86 us
    unnamed x20, local copies, waits for them, and re-layouts  5.31 us
    pallas_call x1, Pallas kernels, prepare(): pl.pallas_call(functools.partial(prepare_kernel, log_rate, DEPTH, segs),...  2.21 us
  transfers between devices with their start and end apart: 21, of which 6 were waited for; matrix products, arithmetic and copies ran while one was open for 0% of the time, Pallas kernels for 16%

profile of v5, /device:TPU:0, one launch (start us, length us, event | category | flops | bytes accessed | tf_op | source)
XLA Modules:
  0.0 74.3 jit_solution(10628756418443177844)
XLA Ops:
  0.6 0.0 copy-start.7
  0.6 0.0 copy-start.8
  0.7 0.0 copy-start.4
  0.7 0.0 copy-start.5
  0.7 0.0 copy-start.6
  0.7 0.6 copy-done.7
  1.3 0.0 copy-done.8
  1.3 0.0 copy-done.4
  1.3 0.0 copy-done.5
  1.3 0.0 copy-done.6
  1.4 0.9 %copy-done.2 = bf16[128,512]{1,0:T(8,128)(2,1)S(1)} copy-done((bf16[128,512]{1,0:T(8,128)(2,1)S(1)}, bf16[128,512]{1,0:T(8,128)(2,1)}, u32[]{:S(2)}) %copy-start.2) | copy-done | bytes 131096
  2.3 0.9 %copy-done.3 = bf16[128,512]{1,0:T(8,128)(2,1)S(1)} copy-done((bf16[128,512]{1,0:T(8,128)(2,1)S(1)}, bf16[128,512]{1,0:T(8,128)(2,1)}, u32[]{:S(2)}) %copy-start.3) | copy-done | bytes 131096
  3.2 0.7 pack_keys_values.1
  3.9 3.0 %collective-permute-start = (bf16[528,128]{1,0:T(8,128)(2,1)S(1)}, bf16[528,128]{1,0:T(8,128)(2,1)S(1)}, u32[]{:S(2)}, u32[]{:S(2)}) collective-permute-start(bf16[528,128]{1,0:T(8,128)(2,1)S(1)} %get-tuple-element.44), channel_id=1, source_target_pairs={{0,2},{2,0},{4,6},{6,4},{8,10},{10,8},{12,14},{14,12},{1,3},{3,1},... | collective-permute-start | bytes 405512 | tf_op jit(solution)/shard_map/ppermute | solution.py:475
  6.8 1.1 %copy-done = bf16[128,2560]{1,0:T(8,128)(2,1)S(1)} copy-done((bf16[128,2560]{1,0:T(8,128)(2,1)S(1)}, bf16[128,2560]{1,0:T(8,128)(2,1)}, u32[]{:S(2)}) %copy-start) | copy-done | bytes 655384
  7.9 1.1 %copy-done.1 = bf16[128,2560]{1,0:T(8,128)(2,1)S(1)} copy-done((bf16[128,2560]{1,0:T(8,128)(2,1)S(1)}, bf16[128,2560]{1,0:T(8,128)(2,1)}, u32[]{:S(2)}) %copy-start.1) | copy-done | bytes 655384
  9.0 0.2 pack_queries.1
  9.3 1.2 %collective-permute-done.other_ref = bf16[528,128]{1,0:T(8,128)(2,1)S(1)} collective-permute-done((bf16[528,128]{1,0:T(8,128)(2,1)S(1)}, bf16[528,128]{1,0:T(8,128)(2,1)S(1)}, u32[]{:S(2)}, u32[]{:S(2)}) %collective-permute-start) | collective-permute-done | bytes 135200 | tf_op jit(solution)/shard_map/ppermute | solution.py:475
  10.4 1.8 %collective-permute-start.3 = (bf16[2,5,128,128]{3,2,1,0:T(8,128)(2,1)S(1)}, bf16[2,5,128,128]{3,2,1,0:T(8,128)(2,1)S(1)}, u32[]{:S(2)}, u32[]{:S(2)}) collective-permute-start(bf16[2,5,128,128]{3,2,1,0:T(8,128)(2,1)S(1)} %get-tuple-element.52), channel_id=1, source_target_pairs={{0,2},{2,0},{4,6},{6,4},{8,10},{10,8},{12,14},{14,12},{1,3},{3,1},... | collective-permute-start | bytes 983048 | tf_op jit(solution)/shard_map/ppermute | solution.py:475
  12.3 3.5 %collective-permute-start.4 = (bf16[2,2,128,128]{3,2,1,0:T(8,128)(2,1)S(1)}, bf16[2,2,128,128]{3,2,1,0:T(8,128)(2,1)S(1)}, u32[]{:S(2)}, u32[]{:S(2)}) collective-permute-start(bf16[2,2,128,128]{3,2,1,0:T(8,128)(2,1)S(1)} %get-tuple-element.51.refs_6_), channel_id=1, source_target_pairs={{0,4},{2,6},{4,8},{6,10},{8,12},{10,14},{1,5},{3,7},{5,9},{7,11},{... | collective-permute-start | bytes 393224 | tf_op jit(solution)/shard_map/ppermute | solution.py:475
  15.7 4.5 %collective-permute-start.5 = (bf16[2,2,128,128]{3,2,1,0:T(8,128)(2,1)S(1)}, bf16[2,2,128,128]{3,2,1,0:T(8,128)(2,1)S(1)}, u32[]{:S(2)}, u32[]{:S(2)}) collective-permute-start(bf16[2,2,128,128]{3,2,1,0:T(8,128)(2,1)S(1)} %get-tuple-element.51.refs_6_), channel_id=1, source_target_pairs={{0,8},{2,10},{4,12},{6,14},{1,9},{3,11},{5,13},{7,15},{16,24},{18,... | collective-permute-start | bytes 393224 | tf_op jit(solution)/shard_map/ppermute | solution.py:475
  20.2 1.3 %collective-permute-start.6 = (bf16[2,2,128,128]{3,2,1,0:T(8,128)(2,1)S(1)}, bf16[2,2,128,128]{3,2,1,0:T(8,128)(2,1)S(1)}, u32[]{:S(2)}, u32[]{:S(2)}) collective-permute-start(bf16[2,2,128,128]{3,2,1,0:T(8,128)(2,1)S(1)} %get-tuple-element.51.refs_6_), channel_id=1, source_target_pairs={{0,12},{2,14},{1,13},{3,15},{16,28},{18,30},{17,29},{19,31}} | collective-permute-start | bytes 393224 | tf_op jit(solution)/shard_map/ppermute | solution.py:475
  21.5 1.3 %collective-permute-start.1 = (f32[8,256]{1,0:T(8,128)S(1)}, f32[8,256]{1,0:T(8,128)S(1)}, u32[]{:S(2)}, u32[]{:S(2)}) collective-permute-start(f32[8,256]{1,0:T(8,128)S(1)} %get-tuple-element.45), channel_id=1, source_target_pairs={{4,0},{6,2},{8,4},{10,6},{12,8},{14,10},{5,1},{7,3},{9,5},{11,7},{... | collective-permute-start | bytes 24584 | tf_op jit(solution)/shard_map/ppermute | solution.py:475
  22.8 4.2 %collective-permute-done.1 = f32[8,256]{1,0:T(8,128)S(1)} collective-permute-done((f32[8,256]{1,0:T(8,128)S(1)}, f32[8,256]{1,0:T(8,128)S(1)}, u32[]{:S(2)}, u32[]{:S(2)}) %collective-permute-start.1) | collective-permute-done | bytes 8224 | tf_op jit(solution)/shard_map/ppermute | solution.py:475
  27.1 1.3 %collective-permute-start.2 = (f32[8,256]{1,0:T(8,128)S(1)}, f32[8,256]{1,0:T(8,128)S(1)}, u32[]{:S(2)}, u32[]{:S(2)}) collective-permute-start(f32[8,256]{1,0:T(8,128)S(1)} %add.31.near_ref), channel_id=1, source_target_pairs={{8,0},{10,2},{12,4},{14,6},{9,1},{11,3},{13,5},{15,7},{24,16},{26,... | collective-permute-start | bytes 24584 | tf_op jit(solution)/shard_map/ppermute | solution.py:475
  28.4 5.1 %collective-permute-done.2.far_ref = f32[8,256]{1,0:T(8,128)S(1)} collective-permute-done((f32[8,256]{1,0:T(8,128)S(1)}, f32[8,256]{1,0:T(8,128)S(1)}, u32[]{:S(2)}, u32[]{:S(2)}) %collective-permute-start.2) | collective-permute-done | bytes 8224 | tf_op jit(solution)/shard_map/ppermute | solution.py:475
  33.5 0.7 copy-done.9
  34.2 2.2 %prepare_advantages.1 = (f32[1,128]{1,0:T(1,128)}, f32[2,128,128]{2,1,0:T(8,128)S(1)}, f32[2,640,128]{2,1,0:T(8,128)S(1)}) custom-call(s32[1]{0:T(128)} %bitcast.own_ref.refs_0_, s32[8]{0:T(128)S(1)} %copy-done.9, s32[8]{0:T(128)S(1)} %copy-done.8, s32[1,8]{1,0:T(1,128)S(1)} %bitcast.17, s32[1,8]{1,0:T(1,128)S(1)} %bitcast.16, f32[8,256]{1,0:T(8,128)S(1)} %add.31.near_ref, ...), custom_call_target="tpu_custom_call" | custom-call | flops 3276800 | bytes 786432 | tf_op jit(solution)/shard_map/prepare_advantages/pallas_call | solution.py:284
  36.4 0.0 collective-permute-done.3.refs_5_
  36.4 0.5 collective-permute-start.7
  36.9 0.0 collective-permute-done.4.refs_7_
  36.9 0.0 collective-permute-done.5.refs_8_
  36.9 0.0 collective-permute-done.6.refs_9_
  36.9 1.7 %collective-permute-start.9 = (bf16[2,2,128,128]{3,2,1,0:T(8,128)(2,1)S(1)}, bf16[2,2,128,128]{3,2,1,0:T(8,128)(2,1)S(1)}, u32[]{:S(2)}, u32[]{:S(2)}) collective-permute-start(bf16[2,2,128,128]{3,2,1,0:T(8,128)(2,1)S(1)} %get-tuple-element.62.refs_6_), channel_id=1, source_target_pairs={{0,8},{2,10},{4,12},{6,14},{1,9},{3,11},{5,13},{7,15},{16,24},{18,... | collective-permute-start | bytes 393224 | tf_op jit(solution)/shard_map/ppermute | solution.py:475
  38.6 4.4 %tree_attention_backward.2 = (bf16[128,640]{1,0:T(8,128)(2,1)S(1)}, bf16[128,640]{1,0:T(8,128)(2,1)S(1)}, bf16[2,2,128,128]{3,2,1,0:T(8,128)(2,1)S(1)}, bf16[2,2...) custom-call(s32[1]{0:T(128)} %bitcast.own_ref.refs_0_, ...), custom_call_target="tpu_custom_call" | custom-call | flops 1048576000 | bytes 8388608 | tf_op jit(solution)/shard_map/tree_attention_backward/pallas_call | solution.py:388
  43.1 1.7 %collective-permute-start.8 = (bf16[2,2,128,128]{3,2,1,0:T(8,128)(2,1)S(1)}, bf16[2,2,128,128]{3,2,1,0:T(8,128)(2,1)S(1)}, u32[]{:S(2)}, u32[]{:S(2)}) collective-permute-start(bf16[2,2,128,128]{3,2,1,0:T(8,128)(2,1)S(1)} %get-tuple-element.62.refs_6_), channel_id=1, source_target_pairs={{0,4},{2,6},{4,8},{6,10},{8,12},{10,14},{1,5},{3,7},{5,9},{7,11},{... | collective-permute-start | bytes 393224 | tf_op jit(solution)/shard_map/ppermute | solution.py:475
  44.7 0.0 collective-permute-done.9.refs_8_
  44.7 0.7 collective-permute-start.10
  45.4 1.3 %collective-permute-start.15 = (bf16[2,2,128,128]{3,2,1,0:T(8,128)(2,1)S(1)}, bf16[2,2,128,128]{3,2,1,0:T(8,128)(2,1)S(1)}, u32[]{:S(2)}, u32[]{:S(2)}) collective-permute-start(bf16[2,2,128,128]{3,2,1,0:T(8,128)(2,1)S(1)} %get-tuple-element.71), channel_id=1, source_target_pairs={{4,0},{6,2},{8,4},{10,6},{12,8},{14,10},{5,1},{7,3},{9,5},{11,7},{... | collective-permute-start | bytes 393224 | tf_op jit(solution)/shard_map/ppermute | solution.py:475
  46.7 1.3 %collective-permute-start.14 = (bf16[2,2,128,128]{3,2,1,0:T(8,128)(2,1)S(1)}, bf16[2,2,128,128]{3,2,1,0:T(8,128)(2,1)S(1)}, u32[]{:S(2)}, u32[]{:S(2)}) collective-permute-start(bf16[2,2,128,128]{3,2,1,0:T(8,128)(2,1)S(1)} %get-tuple-element.70), channel_id=1, source_target_pairs={{8,0},{10,2},{12,4},{14,6},{9,1},{11,3},{13,5},{15,7},{24,16},{26,... | collective-permute-start | bytes 393224 | tf_op jit(solution)/shard_map/ppermute | solution.py:475
  48.0 0.0 collective-permute-done.8.refs_7_
  48.0 1.3 %collective-permute-start.13 = (bf16[2,2,128,128]{3,2,1,0:T(8,128)(2,1)S(1)}, bf16[2,2,128,128]{3,2,1,0:T(8,128)(2,1)S(1)}, u32[]{:S(2)}, u32[]{:S(2)}) collective-permute-start(bf16[2,2,128,128]{3,2,1,0:T(8,128)(2,1)S(1)} %get-tuple-element.69), channel_id=1, source_target_pairs={{12,0},{14,2},{13,1},{15,3},{28,16},{30,18},{29,17},{31,19}} | collective-permute-start | bytes 393224 | tf_op jit(solution)/shard_map/ppermute | solution.py:475
  49.3 0.0 collective-permute-done.10.refs_9_
  49.3 1.6 %collective-permute-start.11 = (bf16[128,640]{1,0:T(8,128)(2,1)S(1)}, bf16[128,640]{1,0:T(8,128)(2,1)S(1)}, u32[]{:S(2)}, u32[]{:S(2)}) collective-permute-start(bf16[128,640]{1,0:T(8,128)(2,1)S(1)} %get-tuple-element.65), channel_id=1, source_target_pairs={{0,2},{2,0},{4,6},{6,4},{8,10},{10,8},{12,14},{14,12},{1,3},{3,1},... | collective-permute-start | bytes 491528 | tf_op jit(solution)/shard_map/ppermute | solution.py:475
  50.9 0.0 collective-permute-done.7.refs_5_
  50.9 4.4 %tree_attention_backward.3 = (bf16[128,640]{1,0:T(8,128)(2,1)S(1)}, bf16[128,640]{1,0:T(8,128)(2,1)S(1)}, bf16[2,2,128,128]{3,2,1,0:T(8,128)(2,1)S(1)}, bf16[2,2...) custom-call(s32[1]{0:T(128)} %bitcast.own_ref.refs_0_, ...), custom_call_target="tpu_custom_call" | custom-call | flops 1048576000 | bytes 8388608 | tf_op jit(solution)/shard_map/tree_attention_backward/pallas_call | solution.py:388
  55.3 0.6 collective-permute-start.12
  55.9 0.0 collective-permute-done.15.refs_5_
  55.9 1.3 %collective-permute-start.19 = (bf16[2,2,128,128]{3,2,1,0:T(8,128)(2,1)S(1)}, bf16[2,2,128,128]{3,2,1,0:T(8,128)(2,1)S(1)}, u32[]{:S(2)}, u32[]{:S(2)}) collective-permute-start(bf16[2,2,128,128]{3,2,1,0:T(8,128)(2,1)S(1)} %get-tuple-element.76), channel_id=1, source_target_pairs={{4,0},{6,2},{8,4},{10,6},{12,8},{14,10},{5,1},{7,3},{9,5},{11,7},{... | collective-permute-start | bytes 393224 | tf_op jit(solution)/shard_map/ppermute | solution.py:475
  57.2 0.0 collective-permute-done.14.refs_4_
  57.2 1.3 %collective-permute-start.18 = (bf16[2,2,128,128]{3,2,1,0:T(8,128)(2,1)S(1)}, bf16[2,2,128,128]{3,2,1,0:T(8,128)(2,1)S(1)}, u32[]{:S(2)}, u32[]{:S(2)}) collective-permute-start(bf16[2,2,128,128]{3,2,1,0:T(8,128)(2,1)S(1)} %get-tuple-element.75), channel_id=1, source_target_pairs={{8,0},{10,2},{12,4},{14,6},{9,1},{11,3},{13,5},{15,7},{24,16},{26,... | collective-permute-start | bytes 393224 | tf_op jit(solution)/shard_map/ppermute | solution.py:475
  58.5 0.0 collective-permute-done.13.refs_3_
  58.5 1.3 %collective-permute-start.17 = (bf16[2,2,128,128]{3,2,1,0:T(8,128)(2,1)S(1)}, bf16[2,2,128,128]{3,2,1,0:T(8,128)(2,1)S(1)}, u32[]{:S(2)}, u32[]{:S(2)}) collective-permute-start(bf16[2,2,128,128]{3,2,1,0:T(8,128)(2,1)S(1)} %get-tuple-element.74), channel_id=1, source_target_pairs={{12,0},{14,2},{13,1},{15,3},{28,16},{30,18},{29,17},{31,19}} | collective-permute-start | bytes 393224 | tf_op jit(solution)/shard_map/ppermute | solution.py:475
  59.9 5.1 %collective-permute-done.19.refs_9_ = bf16[2,2,128,128]{3,2,1,0:T(8,128)(2,1)S(1)} collective-permute-done((bf16[2,2,128,128]{3,2,1,0:T(8,128)(2,1)S(1)}, bf16[2,2,128,128]{3,2,1,0:T(8,128)(2,1)S(1)}, u32[]{:S(2)}, u32[]{:S(2)}) %collective-permute-start.19) | collective-permute-done | bytes 131104 | tf_op jit(solution)/shard_map/ppermute | solution.py:475
  65.0 1.5 %collective-permute-start.16 = (bf16[2,128,128]{2,1,0:T(8,128)(2,1)S(1)}, bf16[2,128,128]{2,1,0:T(8,128)(2,1)S(1)}, u32[]{:S(2)}, u32[]{:S(2)}) collective-permute-start(bf16[2,128,128]{2,1,0:T(8,128)(2,1)S(1)} %fusion), channel_id=1, source_target_pairs={{0,2},{2,0},{4,6},{6,4},{8,10},{10,8},{12,14},{14,12},{1,3},{3,1},... | collective-permute-start | bytes 196616 | tf_op jit(solution)/shard_map/ppermute | solution.py:475
  66.5 2.7 %collective-permute-done.18.refs_8_ = bf16[2,2,128,128]{3,2,1,0:T(8,128)(2,1)S(1)} collective-permute-done((bf16[2,2,128,128]{3,2,1,0:T(8,128)(2,1)S(1)}, bf16[2,2,128,128]{3,2,1,0:T(8,128)(2,1)S(1)}, u32[]{:S(2)}, u32[]{:S(2)}) %collective-permute-start.18) | collective-permute-done | bytes 131104 | tf_op jit(solution)/shard_map/ppermute | solution.py:475
  69.2 0.0 collective-permute-done.17.refs_7_
  69.2 1.6 %collective-permute-start.20 = (bf16[2,128,128]{2,1,0:T(8,128)(2,1)S(1)}, bf16[2,128,128]{2,1,0:T(8,128)(2,1)S(1)}, u32[]{:S(2)}, u32[]{:S(2)}) collective-permute-start(bf16[2,128,128]{2,1,0:T(8,128)(2,1)S(1)} %fusion.1), channel_id=1, source_target_pairs={{0,2},{2,0},{4,6},{6,4},{8,10},{10,8},{12,14},{14,12},{1,3},{3,1},... | collective-permute-start | bytes 196616 | tf_op jit(solution)/shard_map/ppermute | solution.py:475
  70.8 0.0 collective-permute-done.11.refs_2_
  70.8 0.0 collective-permute-done.12.refs_3_
  70.8 0.9 %join_queries.1 = bf16[128,2560]{1,0:T(8,128)(2,1)} custom-call(s32[1]{0:T(128)} %bitcast.own_ref.refs_0_, bf16[128,640]{1,0:T(8,128)(2,1)S(1)} %get-tuple-element.56.refs_0_, bf16[128,640]{1,0:T(8,128)(2,1)S(1)} %get-tuple-element.64.refs_1_, bf16[128,640]{1,0:T(8,128)(2,1)S(1)} %collective-permute-done.11.refs_2_, ...), custom_call_target="tpu_custom_call" | custom-call | bytes 1310720 | tf_op jit(solution)/shard_map/join_queries/pallas_call | solution.py:426
  71.7 0.0 collective-permute-done.16.refs_0_
  71.7 1.9 %collective-permute-done.20.refs_1_ = bf16[2,128,128]{2,1,0:T(8,128)(2,1)S(1)} collective-permute-done((bf16[2,128,128]{2,1,0:T(8,128)(2,1)S(1)}, bf16[2,128,128]{2,1,0:T(8,128)(2,1)S(1)}, u32[]{:S(2)}, u32[]{:S(2)}) %collective-permute-start.20) | collective-permute-done | bytes 65568 | tf_op jit(solution)/shard_map/ppermute | solution.py:475
  73.6 0.8 %join_keys.1 = (bf16[128,512]{1,0:T(8,128)(2,1)}, bf16[128,512]{1,0:T(8,128)(2,1)}) custom-call(s32[1]{0:T(128)} %bitcast.own_ref.refs_0_, bf16[2,128,128]{2,1,0:T(8,128)(2,1)S(1)} %collective-permute-done.16.refs_0_, bf16[2,128,128]{2,1,0:T(8,128)(2,1)S(1)} %collective-permute-done.20.refs_1_, bf16[2,2,128,128]{3,2,1,0:T(8,128)(2,1)S(1)} %get-tuple-element.68.refs_2_, ...), custom_call_target="tpu_custom_call" | custom-call | bytes 524288 | tf_op jit(solution)/shard_map/join_keys/pallas_call | solution.py:461
  (9 shorter events, 0.1 us)
Async XLA Ops:
  0.6 0.7 copy-start.7
  0.6 0.7 copy-start.8
  0.7 0.7 copy-start.4
  0.7 0.7 copy-start.5
  0.7 0.7 copy-start.6
  1.4 0.9 %copy-start.2 = (bf16[128,512]{1,0:T(8,128)(2,1)S(1)}, bf16[128,512]{1,0:T(8,128)(2,1)}, u32[]{:S(2)}) copy-start(bf16[128,512]{1,0:T(8,128)(2,1)} %k_ref.1) | copy-start | bytes 393220
  2.3 0.9 %copy-start.3 = (bf16[128,512]{1,0:T(8,128)(2,1)S(1)}, bf16[128,512]{1,0:T(8,128)(2,1)}, u32[]{:S(2)}) copy-start(bf16[128,512]{1,0:T(8,128)(2,1)} %v_ref.1) | copy-start | bytes 393220
  3.9 6.6 %collective-permute-start = (bf16[528,128]{1,0:T(8,128)(2,1)S(1)}, bf16[528,128]{1,0:T(8,128)(2,1)S(1)}, u32[]{:S(2)}, u32[]{:S(2)}) collective-permute-start(bf16[528,128]{1,0:T(8,128)(2,1)S(1)} %get-tuple-element.44), channel_id=1, source_target_pairs={{0,2},{2,0},{4,6},{6,4},{8,10},{10,8},{12,14},{14,12},{1,3},{3,1},... | collective-permute-start | bytes 405512 | tf_op jit(solution)/shard_map/ppermute | solution.py:475
  6.8 1.1 %copy-start = (bf16[128,2560]{1,0:T(8,128)(2,1)S(1)}, bf16[128,2560]{1,0:T(8,128)(2,1)}, u32[]{:S(2)}) copy-start(bf16[128,2560]{1,0:T(8,128)(2,1)} %q_ref) | copy-start | bytes 1966084
  7.9 1.1 %copy-start.1 = (bf16[128,2560]{1,0:T(8,128)(2,1)S(1)}, bf16[128,2560]{1,0:T(8,128)(2,1)}, u32[]{:S(2)}) copy-start(bf16[128,2560]{1,0:T(8,128)(2,1)} %dir_ref.1) | copy-start | bytes 1966084
  10.4 25.9 %collective-permute-start.3 = (bf16[2,5,128,128]{3,2,1,0:T(8,128)(2,1)S(1)}, bf16[2,5,128,128]{3,2,1,0:T(8,128)(2,1)S(1)}, u32[]{:S(2)}, u32[]{:S(2)}) collective-permute-start(bf16[2,5,128,128]{3,2,1,0:T(8,128)(2,1)S(1)} %get-tuple-element.52), channel_id=1, source_target_pairs={{0,2},{2,0},{4,6},{6,4},{8,10},{10,8},{12,14},{14,12},{1,3},{3,1},... | collective-permute-start | bytes 983048 | tf_op jit(solution)/shard_map/ppermute | solution.py:475
  12.3 24.7 %collective-permute-start.4 = (bf16[2,2,128,128]{3,2,1,0:T(8,128)(2,1)S(1)}, bf16[2,2,128,128]{3,2,1,0:T(8,128)(2,1)S(1)}, u32[]{:S(2)}, u32[]{:S(2)}) collective-permute-start(bf16[2,2,128,128]{3,2,1,0:T(8,128)(2,1)S(1)} %get-tuple-element.51.refs_6_), channel_id=1, source_target_pairs={{0,4},{2,6},{4,8},{6,10},{8,12},{10,14},{1,5},{3,7},{5,9},{7,11},{... | collective-permute-start | bytes 393224 | tf_op jit(solution)/shard_map/ppermute | solution.py:475
  15.7 21.2 %collective-permute-start.5 = (bf16[2,2,128,128]{3,2,1,0:T(8,128)(2,1)S(1)}, bf16[2,2,128,128]{3,2,1,0:T(8,128)(2,1)S(1)}, u32[]{:S(2)}, u32[]{:S(2)}) collective-permute-start(bf16[2,2,128,128]{3,2,1,0:T(8,128)(2,1)S(1)} %get-tuple-element.51.refs_6_), channel_id=1, source_target_pairs={{0,8},{2,10},{4,12},{6,14},{1,9},{3,11},{5,13},{7,15},{16,24},{18,... | collective-permute-start | bytes 393224 | tf_op jit(solution)/shard_map/ppermute | solution.py:475
  20.2 16.7 %collective-permute-start.6 = (bf16[2,2,128,128]{3,2,1,0:T(8,128)(2,1)S(1)}, bf16[2,2,128,128]{3,2,1,0:T(8,128)(2,1)S(1)}, u32[]{:S(2)}, u32[]{:S(2)}) collective-permute-start(bf16[2,2,128,128]{3,2,1,0:T(8,128)(2,1)S(1)} %get-tuple-element.51.refs_6_), channel_id=1, source_target_pairs={{0,12},{2,14},{1,13},{3,15},{16,28},{18,30},{17,29},{19,31}} | collective-permute-start | bytes 393224 | tf_op jit(solution)/shard_map/ppermute | solution.py:475
  21.5 5.5 %collective-permute-start.1 = (f32[8,256]{1,0:T(8,128)S(1)}, f32[8,256]{1,0:T(8,128)S(1)}, u32[]{:S(2)}, u32[]{:S(2)}) collective-permute-start(f32[8,256]{1,0:T(8,128)S(1)} %get-tuple-element.45), channel_id=1, source_target_pairs={{4,0},{6,2},{8,4},{10,6},{12,8},{14,10},{5,1},{7,3},{9,5},{11,7},{... | collective-permute-start | bytes 24584 | tf_op jit(solution)/shard_map/ppermute | solution.py:475
  27.1 6.4 %collective-permute-start.2 = (f32[8,256]{1,0:T(8,128)S(1)}, f32[8,256]{1,0:T(8,128)S(1)}, u32[]{:S(2)}, u32[]{:S(2)}) collective-permute-start(f32[8,256]{1,0:T(8,128)S(1)} %add.31.near_ref), channel_id=1, source_target_pairs={{8,0},{10,2},{12,4},{14,6},{9,1},{11,3},{13,5},{15,7},{24,16},{26,... | collective-permute-start | bytes 24584 | tf_op jit(solution)/shard_map/ppermute | solution.py:475
  33.5 0.7 copy-start.9
  36.4 14.5 %collective-permute-start.7 = (bf16[2,5,128,128]{3,2,1,0:T(8,128)(2,1)S(1)}, bf16[2,5,128,128]{3,2,1,0:T(8,128)(2,1)S(1)}, u32[]{:S(2)}, u32[]{:S(2)}) collective-permute-start(bf16[2,5,128,128]{3,2,1,0:T(8,128)(2,1)S(1)} %get-tuple-element.59), channel_id=1, source_target_pairs={{0,2},{2,0},{4,6},{6,4},{8,10},{10,8},{12,14},{14,12},{1,3},{3,1},... | collective-permute-start | bytes 983048 | tf_op jit(solution)/shard_map/ppermute | solution.py:475
  36.9 7.8 %collective-permute-start.9 = (bf16[2,2,128,128]{3,2,1,0:T(8,128)(2,1)S(1)}, bf16[2,2,128,128]{3,2,1,0:T(8,128)(2,1)S(1)}, u32[]{:S(2)}, u32[]{:S(2)}) collective-permute-start(bf16[2,2,128,128]{3,2,1,0:T(8,128)(2,1)S(1)} %get-tuple-element.62.refs_6_), channel_id=1, source_target_pairs={{0,8},{2,10},{4,12},{6,14},{1,9},{3,11},{5,13},{7,15},{16,24},{18,... | collective-permute-start | bytes 393224 | tf_op jit(solution)/shard_map/ppermute | solution.py:475
  43.1 5.0 %collective-permute-start.8 = (bf16[2,2,128,128]{3,2,1,0:T(8,128)(2,1)S(1)}, bf16[2,2,128,128]{3,2,1,0:T(8,128)(2,1)S(1)}, u32[]{:S(2)}, u32[]{:S(2)}) collective-permute-start(bf16[2,2,128,128]{3,2,1,0:T(8,128)(2,1)S(1)} %get-tuple-element.62.refs_6_), channel_id=1, source_target_pairs={{0,4},{2,6},{4,8},{6,10},{8,12},{10,14},{1,5},{3,7},{5,9},{7,11},{... | collective-permute-start | bytes 393224 | tf_op jit(solution)/shard_map/ppermute | solution.py:475
  44.7 4.6 %collective-permute-start.10 = (bf16[2,2,128,128]{3,2,1,0:T(8,128)(2,1)S(1)}, bf16[2,2,128,128]{3,2,1,0:T(8,128)(2,1)S(1)}, u32[]{:S(2)}, u32[]{:S(2)}) collective-permute-start(bf16[2,2,128,128]{3,2,1,0:T(8,128)(2,1)S(1)} %collective-permute-done.9.refs_8_), channel_id=1, source_target_pairs={{8,12},{10,14},{9,13},{11,15},{24,28},{26,30},{25,29},{27,31}} | collective-permute-start | bytes 393224 | tf_op jit(solution)/shard_map/ppermute | solution.py:475
  45.4 10.5 %collective-permute-start.15 = (bf16[2,2,128,128]{3,2,1,0:T(8,128)(2,1)S(1)}, bf16[2,2,128,128]{3,2,1,0:T(8,128)(2,1)S(1)}, u32[]{:S(2)}, u32[]{:S(2)}) collective-permute-start(bf16[2,2,128,128]{3,2,1,0:T(8,128)(2,1)S(1)} %get-tuple-element.71), channel_id=1, source_target_pairs={{4,0},{6,2},{8,4},{10,6},{12,8},{14,10},{5,1},{7,3},{9,5},{11,7},{... | collective-permute-start | bytes 393224 | tf_op jit(solution)/shard_map/ppermute | solution.py:475
  46.7 10.5 %collective-permute-start.14 = (bf16[2,2,128,128]{3,2,1,0:T(8,128)(2,1)S(1)}, bf16[2,2,128,128]{3,2,1,0:T(8,128)(2,1)S(1)}, u32[]{:S(2)}, u32[]{:S(2)}) collective-permute-start(bf16[2,2,128,128]{3,2,1,0:T(8,128)(2,1)S(1)} %get-tuple-element.70), channel_id=1, source_target_pairs={{8,0},{10,2},{12,4},{14,6},{9,1},{11,3},{13,5},{15,7},{24,16},{26,... | collective-permute-start | bytes 393224 | tf_op jit(solution)/shard_map/ppermute | solution.py:475
  48.0 10.5 %collective-permute-start.13 = (bf16[2,2,128,128]{3,2,1,0:T(8,128)(2,1)S(1)}, bf16[2,2,128,128]{3,2,1,0:T(8,128)(2,1)S(1)}, u32[]{:S(2)}, u32[]{:S(2)}) collective-permute-start(bf16[2,2,128,128]{3,2,1,0:T(8,128)(2,1)S(1)} %get-tuple-element.69), channel_id=1, source_target_pairs={{12,0},{14,2},{13,1},{15,3},{28,16},{30,18},{29,17},{31,19}} | collective-permute-start | bytes 393224 | tf_op jit(solution)/shard_map/ppermute | solution.py:475
  49.3 21.5 %collective-permute-start.11 = (bf16[128,640]{1,0:T(8,128)(2,1)S(1)}, bf16[128,640]{1,0:T(8,128)(2,1)S(1)}, u32[]{:S(2)}, u32[]{:S(2)}) collective-permute-start(bf16[128,640]{1,0:T(8,128)(2,1)S(1)} %get-tuple-element.65), channel_id=1, source_target_pairs={{0,2},{2,0},{4,6},{6,4},{8,10},{10,8},{12,14},{14,12},{1,3},{3,1},... | collective-permute-start | bytes 491528 | tf_op jit(solution)/shard_map/ppermute | solution.py:475
  55.3 15.5 %collective-permute-start.12 = (bf16[128,640]{1,0:T(8,128)(2,1)S(1)}, bf16[128,640]{1,0:T(8,128)(2,1)S(1)}, u32[]{:S(2)}, u32[]{:S(2)}) collective-permute-start(bf16[128,640]{1,0:T(8,128)(2,1)S(1)} %get-tuple-element.66), channel_id=1, source_target_pairs={{0,2},{2,0},{4,6},{6,4},{8,10},{10,8},{12,14},{14,12},{1,3},{3,1},... | collective-permute-start | bytes 491528 | tf_op jit(solution)/shard_map/ppermute | solution.py:475
  55.9 9.0 %collective-permute-start.19 = (bf16[2,2,128,128]{3,2,1,0:T(8,128)(2,1)S(1)}, bf16[2,2,128,128]{3,2,1,0:T(8,128)(2,1)S(1)}, u32[]{:S(2)}, u32[]{:S(2)}) collective-permute-start(bf16[2,2,128,128]{3,2,1,0:T(8,128)(2,1)S(1)} %get-tuple-element.76), channel_id=1, source_target_pairs={{4,0},{6,2},{8,4},{10,6},{12,8},{14,10},{5,1},{7,3},{9,5},{11,7},{... | collective-permute-start | bytes 393224 | tf_op jit(solution)/shard_map/ppermute | solution.py:475
  57.2 12.0 %collective-permute-start.18 = (bf16[2,2,128,128]{3,2,1,0:T(8,128)(2,1)S(1)}, bf16[2,2,128,128]{3,2,1,0:T(8,128)(2,1)S(1)}, u32[]{:S(2)}, u32[]{:S(2)}) collective-permute-start(bf16[2,2,128,128]{3,2,1,0:T(8,128)(2,1)S(1)} %get-tuple-element.75), channel_id=1, source_target_pairs={{8,0},{10,2},{12,4},{14,6},{9,1},{11,3},{13,5},{15,7},{24,16},{26,... | collective-permute-start | bytes 393224 | tf_op jit(solution)/shard_map/ppermute | solution.py:475
  58.5 10.7 %collective-permute-start.17 = (bf16[2,2,128,128]{3,2,1,0:T(8,128)(2,1)S(1)}, bf16[2,2,128,128]{3,2,1,0:T(8,128)(2,1)S(1)}, u32[]{:S(2)}, u32[]{:S(2)}) collective-permute-start(bf16[2,2,128,128]{3,2,1,0:T(8,128)(2,1)S(1)} %get-tuple-element.74), channel_id=1, source_target_pairs={{12,0},{14,2},{13,1},{15,3},{28,16},{30,18},{29,17},{31,19}} | collective-permute-start | bytes 393224 | tf_op jit(solution)/shard_map/ppermute | solution.py:475
  65.0 6.7 %collective-permute-start.16 = (bf16[2,128,128]{2,1,0:T(8,128)(2,1)S(1)}, bf16[2,128,128]{2,1,0:T(8,128)(2,1)S(1)}, u32[]{:S(2)}, u32[]{:S(2)}) collective-permute-start(bf16[2,128,128]{2,1,0:T(8,128)(2,1)S(1)} %fusion), channel_id=1, source_target_pairs={{0,2},{2,0},{4,6},{6,4},{8,10},{10,8},{12,14},{14,12},{1,3},{3,1},... | collective-permute-start | bytes 196616 | tf_op jit(solution)/shard_map/ppermute | solution.py:475
  69.2 4.3 %collective-permute-start.20 = (bf16[2,128,128]{2,1,0:T(8,128)(2,1)S(1)}, bf16[2,128,128]{2,1,0:T(8,128)(2,1)S(1)}, u32[]{:S(2)}, u32[]{:S(2)}) collective-permute-start(bf16[2,128,128]{2,1,0:T(8,128)(2,1)S(1)} %fusion.1), channel_id=1, source_target_pairs={{0,2},{2,0},{4,6},{6,4},{8,10},{10,8},{12,14},{14,12},{1,3},{3,1},... | collective-permute-start | bytes 196616 | tf_op jit(solution)/shard_map/ppermute | solution.py:475

commit v6 on v4

v6 whole, which is shorter than its diff:
```python
import functools
import math

import jax
import jax.numpy as jnp
from jax import lax
from jax.experimental import pallas as pl
from jax.experimental.pallas import tpu as pltpu
from jax.sharding import PartitionSpec as P

HD = 128
DEPTH = 5
BETA = 0.1
LAMBDA_SEG = 0.7
PAIRED_GROUPS = 8
TERM_ROWS = 16
LOG2E = math.log2(math.e)
SMALL = pltpu.CompilerParams(vmem_limit_bytes=8 * 1024 * 1024)


def lookup(table_values, lookup_ids):
    matches = lookup_ids[..., None] == jnp.arange(table_values.shape[0], dtype=jnp.int32)
    return jnp.sum(jnp.where(matches, table_values, 0), axis=-1)


def ancestors(parents, count):
    current = jnp.arange(parents.shape[0], dtype=jnp.int32)
    chain_list = []
    for depth_step in range(count):
        parent_ids = lookup(parents, current)
        current = jnp.where(current >= 0, parent_ids, -1)
        chain_list.append(current)
    return jnp.stack(chain_list, axis=1)


def token_terms(log_rate, own_len, rewards, logprobs, ref_logprobs, values):
    positions = lax.broadcasted_iota(jnp.int32, rewards.shape, 1)
    later = jnp.concatenate([values[:, 1:], values[:, :1]], axis=1)
    later = jnp.where(positions + 1 < own_len, later, 0.0)
    deltas = jnp.where(
        positions < own_len, rewards - BETA * (logprobs - ref_logprobs) + later - values, 0.0
    )
    powers = jnp.exp(positions.astype(jnp.float32) * log_rate)
    first_local = jnp.sum(deltas * powers, axis=1, keepdims=True)
    firsts = jnp.where(positions == 0, first_local, jnp.where(positions == 1, values[:, :1], 0.0))
    return deltas, firsts


def split_float(value):
    parts = []
    for _ in range(3):
        part = value.astype(jnp.bfloat16)
        parts.append(part)
        value = value - part.astype(jnp.float32)
    return parts


def pack_kernel(
    log_rate,
    lengths_ref,
    k_ref,
    v_ref,
    rewards_ref,
    logprobs_ref,
    ref_logprobs_ref,
    values_ref,
    *refs,
):
    out_refs, sems = refs[:-1], refs[-1]
    own = lax.axis_index("seg")
    length = k_ref.shape[0]
    parts = len(out_refs)
    heads = k_ref.shape[1] // HD // parts
    copies = []
    for step in range(parts):
        part = lax.rem(own + step, parts)
        for h in range(heads):
            columns = pl.ds(pl.multiple_of((part * heads + h) * HD, HD), HD)
            for plane, ref in enumerate((k_ref, v_ref)):
                rows = pl.ds((h * 2 + plane) * length, length)
                copies.append(
                    pltpu.make_async_copy(
                        ref.at[:, columns], out_refs[step].at[rows, :], sems.at[len(copies)]
                    )
                )
    for copy in copies:
        copy.start()
    terms = token_terms(
        log_rate,
        lengths_ref[own],
        rewards_ref[...],
        logprobs_ref[...],
        ref_logprobs_ref[...],
        values_ref[...],
    )
    rows = [part.astype(jnp.float32) for x in terms for part in split_float(x)]
    rows.append(jnp.zeros((TERM_ROWS - len(rows), HD), jnp.float32))
    rows = jnp.concatenate(rows).astype(jnp.bfloat16)
    for out_ref in out_refs:
        out_ref[2 * heads * length :, :] = rows
    for copy in copies:
        copy.wait()


def pack(lengths, k, v, token_rows, parts, log_rate):
    length, width = k.shape
    smem = pl.BlockSpec(memory_space=pltpu.SMEM)
    vmem = pl.BlockSpec(memory_space=pltpu.VMEM)
    hbm = pl.BlockSpec(memory_space=pltpu.HBM)
    heads = width // HD // parts
    assert length == HD
    block = jax.ShapeDtypeStruct((2 * heads * length + TERM_ROWS, HD), k.dtype)
    return pl.pallas_call(
        functools.partial(pack_kernel, log_rate),
        out_shape=(block,) * parts,
        in_specs=[smem, hbm, hbm] + [vmem] * 4,
        out_specs=(vmem,) * parts,
        scratch_shapes=[pltpu.SemaphoreType.DMA((2 * heads * parts,))],
        cost_estimate=pl.CostEstimate(
            flops=length * 100, bytes_accessed=8 * length * width, transcendentals=length
        ),
        name="pack_keys_values",
    )(lengths, k, v, *token_rows)


def pack_queries_kernel(parts, q_ref, dir_ref, *out_refs):
    own = lax.axis_index("seg")
    chunks = len(out_refs) // parts
    heads = out_refs[0].shape[1]
    for index, out_ref in enumerate(out_refs):
        step, chunk = divmod(index, chunks)
        part = lax.rem(own + step, parts)
        for h in range(heads):
            column = (part * chunks + chunk) * heads + h
            columns = pl.ds(pl.multiple_of(column * HD, HD), HD)
            out_ref[0, h] = q_ref[:, columns]
            out_ref[1, h] = dir_ref[:, columns]


def pack_queries(q, direction, parts, chunks):
    length, width = q.shape
    vmem = pl.BlockSpec(memory_space=pltpu.VMEM)
    block = jax.ShapeDtypeStruct((2, width // HD // parts // chunks, length, HD), q.dtype)
    outs = pl.pallas_call(
        functools.partial(pack_queries_kernel, parts),
        out_shape=(block,) * (parts * chunks),
        in_specs=[vmem, vmem],
        out_specs=(vmem,) * (parts * chunks),
        cost_estimate=pl.CostEstimate(flops=0, bytes_accessed=8 * length * width, transcendentals=0),
        compiler_params=SMALL,
        name="pack_queries",
    )(q, direction)
    return [outs[step * chunks : (step + 1) * chunks] for step in range(parts)]


def parent_of(segment, parents_s):
    known = parents_s[jnp.maximum(segment, 0)]
    return jnp.where(segment >= 0, known, -1).astype(jnp.int32)


def segment_of(own, segs, i):
    part = lax.rem(own, segs)
    return own - part + lax.rem(part + i, segs)


def mask_kernel(depth, parents_s, lengths_s, bias_ref):
    segs, _, length = bias_ref.shape
    own = lax.axis_index("seg")
    u_id = lax.broadcasted_iota(jnp.int32, (length, length), 0)
    t_id = lax.broadcasted_iota(jnp.int32, (length, length), 1)
    for i in range(segs):
        ancestor = segment_of(own, segs, i)
        for slot in range(depth):
            if slot > 0:
                ancestor = parent_of(ancestor, parents_s)
            slot_len = jnp.where(ancestor >= 0, lengths_s[jnp.maximum(ancestor, 0)], 0)
            seen = u_id < slot_len
            if slot == 0:
                seen = jnp.logical_and(seen, u_id <= t_id)
            bias_ref[i, slot * length : (slot + 1) * length, :] = jnp.where(seen, 0.0, -1e30)


def masks(parents, lengths, length, segs):
    smem = pl.BlockSpec(memory_space=pltpu.SMEM)
    return pl.pallas_call(
        functools.partial(mask_kernel, DEPTH),
        out_shape=jax.ShapeDtypeStruct((segs, DEPTH * length, length), jnp.float32),
        in_specs=[smem] * 2,
        out_specs=pl.BlockSpec(memory_space=pltpu.VMEM),
        cost_estimate=pl.CostEstimate(
            flops=8 * DEPTH * segs * length * length,
            bytes_accessed=4 * DEPTH * segs * length * length,
            transcendentals=0,
        ),
        compiler_params=SMALL,
        name="masks",
    )(parents, lengths)


def advantage_kernel(log_rate, depth, segs, parents_s, lengths_s, *refs):
    term_refs, (row_ref, adv_ref) = refs[:-2], refs[-2:]
    length = row_ref.shape[1]
    count = parents_s.shape[0]
    own = lax.axis_index("seg")

    seg_col = lax.broadcasted_iota(jnp.int32, (count, 1), 0)
    if len(term_refs) == 1:
        deltas, firsts = term_refs[0][:, :length], term_refs[0][:, length:]
    else:
        part, pair, pairs = lax.rem(own, segs), own // segs, count // segs
        deltas = firsts = jnp.zeros((count, length), jnp.float32)
        for index, ref in enumerate(term_refs):
            step, side = divmod(index, segs)
            seg = lax.rem(pair - step + pairs, pairs) * segs + lax.rem(part + side, segs)
            tail = ref[ref.shape[0] - TERM_ROWS :, :].astype(jnp.float32)
            deltas = deltas + jnp.where(seg_col == seg, tail[0:1] + tail[1:2] + tail[2:3], 0.0)
            firsts = firsts + jnp.where(seg_col == seg, tail[3:4] + tail[4:5] + tail[5:6], 0.0)

    row_id = lax.broadcasted_iota(jnp.int32, (count, count), 0)
    col_id = lax.broadcasted_iota(jnp.int32, (count, count), 1)
    eye = row_id == col_id

    def to_row(col):
        return jnp.sum(jnp.where(eye, col, 0.0), axis=0, keepdims=True)

    parent_row = jnp.full((1, count), -1, jnp.int32)
    lens_col = jnp.zeros((count, 1), jnp.int32)
    for seg in range(count):
        parent_row = jnp.where(col_id[:1] == seg, parents_s[seg], parent_row)
        lens_col = jnp.where(seg_col == seg, lengths_s[seg], lens_col)
    lens_col = lens_col.astype(jnp.float32)
    children = (parent_row == row_id).astype(jnp.float32)
    weights = children / jnp.maximum(jnp.sum(children, axis=1, keepdims=True), 1.0)
    first_local, first_value = firsts[:, 0:1], firsts[:, 1:2]
    later_value = jnp.sum(weights * to_row(first_value), axis=1, keepdims=True)
    base_term = first_local + jnp.exp((lens_col - 1.0) * log_rate) * later_value
    factor = jnp.exp(lens_col * log_rate)
    head = base_term
    for _ in range(depth):
        head = base_term + factor * jnp.sum(weights * to_row(head), axis=1, keepdims=True)
    later_head = jnp.sum(weights * to_row(head), axis=1, keepdims=True)

    t_id = lax.broadcasted_iota(jnp.int32, (length, length), 0)
    j_id = lax.broadcasted_iota(jnp.int32, (length, length), 1)
    offset = (j_id - t_id).astype(jnp.float32)
    discount = jnp.where(offset >= 0, jnp.exp(offset * log_rate), 0.0)
    t_col = lax.broadcasted_iota(jnp.int32, (length, 1), 0)
    for i in range(segs):
        seg = segment_of(own, segs, i)
        seg_len = lengths_s[seg]
        mine = seg_col == seg
        my_value = jnp.sum(jnp.where(mine, later_value, 0.0), axis=0, keepdims=True)
        my_head = jnp.sum(jnp.where(mine, later_head, 0.0), axis=0, keepdims=True)
        my_deltas = jnp.sum(jnp.where(mine, deltas, 0.0), axis=0, keepdims=True)
        local_sum = jnp.sum(discount * my_deltas, axis=1, keepdims=True)
        left = (seg_len - t_col).astype(jnp.float32)
        advantage = jnp.where(
            t_col < seg_len,
            local_sum
            + jnp.exp((left - 1.0) * log_rate) * my_value
            + jnp.exp(left * log_rate) * my_head,
            0.0,
        )
        if i == 0:
            row_ref[...] = jnp.sum(jnp.where(t_id == j_id, advantage, 0.0), axis=0, keepdims=True)
        adv_ref[i] = jnp.broadcast_to(advantage, (length, HD))


def advantages_of(parents, lengths, terms, length, segs, log_rate):
    smem = pl.BlockSpec(memory_space=pltpu.SMEM)
    vmem = pl.BlockSpec(memory_space=pltpu.VMEM)
    return pl.pallas_call(
        functools.partial(advantage_kernel, log_rate, DEPTH, segs),
        out_shape=(
            jax.ShapeDtypeStruct((1, length), jnp.float32),
            jax.ShapeDtypeStruct((segs, length, HD), jnp.float32),
        ),
        in_specs=[smem] * 2 + [vmem] * len(terms),
        out_specs=(vmem,) * 2,
        cost_estimate=pl.CostEstimate(
            flops=200 * length * length,
            bytes_accessed=8 * segs * length * length,
            transcendentals=length * length,
        ),
        compiler_params=SMALL,
        name="advantages",
    )(parents, lengths, *terms)


def attend_kernel(depth, chunk, segs, sources, group_size, *refs):
    parents_s, adv_ref, bias_ref = refs[:3]
    query_refs, kv_refs = refs[3 : 3 + segs], refs[3 + segs : 3 + segs + sources]
    kv_scr, p_scr, ds_scr, acc_scr = refs[-4:]
    refs = refs[3 + segs + sources : -4]
    steps = sources // segs
    dkv_refs, dq_refs = refs[-steps:], refs[-steps - segs : -steps]

    length = query_refs[0].shape[2]
    own = lax.axis_index("seg")
    for source in range(sources):
        for plane in range(2):
            rows = slice((2 * chunk + plane) * length, (2 * chunk + plane + 1) * length)
            kv_scr[source, plane] = kv_refs[source][rows, :]
    acc_scr[...] = jnp.zeros_like(acc_scr)

    scale = HD**-0.5
    contract_last = (((1,), (1,)), ((), ()))
    contract_first = (((0,), (0,)), ((), ()))
    for i in range(segs):
        ancestor = segment_of(own, segs, i)
        part = lax.rem(own, segs)
        chosen = []
        for slot in range(depth):
            if slot > 0:
                ancestor = parent_of(ancestor, parents_s)
            if segs == 1:
                chosen.append(slot)
            else:
                known = jnp.maximum(ancestor, 0)
                step = (own - part) // segs - known // segs
                turn = lax.rem(lax.rem(known, segs) - part + segs, segs)
                chosen.append(jnp.where(ancestor >= 0, step * segs + turn, 0))
        q_list = [query_refs[i][0, j] for j in range(group_size)]
        dir_list = [query_refs[i][1, j] for j in range(group_size)]
        do_list = [(adv_ref[i] * d.astype(jnp.float32)).astype(jnp.bfloat16) for d in dir_list]
        k_all = jnp.concatenate([kv_scr[s, 0] for s in chosen], axis=0)
        v_all = jnp.concatenate([kv_scr[s, 1] for s in chosen], axis=0)
        for j in range(group_size):
            columns = slice(j * length, (j + 1) * length)
            scores = lax.dot_general(
                k_all, q_list[j], contract_last, preferred_element_type=jnp.float32
            )
            scores = scores * (scale * LOG2E) + bias_ref[i]
            top = jnp.max(scores, axis=0, keepdims=True)
            unnorm = jnp.exp2(scores - top)
            prob = unnorm * (1.0 / jnp.sum(unnorm, axis=0, keepdims=True))
            prob_low = prob.astype(jnp.bfloat16)
            dprob = lax.dot_general(
                v_all, do_list[j], contract_last, preferred_element_type=jnp.float32
            )
            row_dot = jnp.sum(prob_low.astype(jnp.float32) * dprob, axis=0, keepdims=True)
            dscore = (prob * (dprob - row_dot)).astype(jnp.bfloat16)
            p_scr[:, columns] = prob_low
            ds_scr[:, columns] = dscore
        dscore_all = ds_scr[...]
        dq_t = lax.dot_general(
            k_all, dscore_all, contract_first, preferred_element_type=jnp.float32
        )
        for j in range(group_size):
            dq = jnp.transpose(dq_t[:, j * length : (j + 1) * length]) * scale
            dq_refs[i][:, j * HD : (j + 1) * HD] = dq.astype(jnp.bfloat16)
        q_all = jnp.concatenate(q_list, axis=0)
        do_all = jnp.concatenate(do_list, axis=0)
        dk_all = jnp.dot(dscore_all, q_all, preferred_element_type=jnp.float32) * scale
        dv_all = jnp.dot(p_scr[...], do_all, preferred_element_type=jnp.float32)
        for slot, s in enumerate(chosen):
            rows = slice(slot * length, (slot + 1) * length)
            acc_scr[s, 0] += dk_all[rows]
            acc_scr[s, 1] += dv_all[rows]
    for step in range(steps):
        for i in range(segs):
            dkv_refs[step][i] = acc_scr[step * segs + i].astype(jnp.bfloat16)


def attend(parents, advantages, bias, query_list, kv_list, chunk):
    segs, length = advantages.shape[:2]
    sources = len(kv_list)
    steps = sources // segs
    group_size = query_list[0].shape[1]
    width = group_size * HD
    keys = DEPTH * length
    smem = pl.BlockSpec(memory_space=pltpu.SMEM)
    vmem = pl.BlockSpec(memory_space=pltpu.VMEM)
    out_shape = [jax.ShapeDtypeStruct((length, width), jnp.bfloat16)] * segs
    out_shape += [jax.ShapeDtypeStruct((segs, 2, length, HD), jnp.bfloat16)] * steps
    outs = pl.pallas_call(
        functools.partial(attend_kernel, DEPTH, chunk, segs, sources, group_size),
        out_shape=out_shape,
        in_specs=[smem] + [vmem] * (2 + segs + sources),
        out_specs=[vmem] * len(out_shape),
        scratch_shapes=[
            pltpu.VMEM((sources, 2, length, HD), jnp.bfloat16),
            pltpu.VMEM((keys, width), jnp.bfloat16),
            pltpu.VMEM((keys, width), jnp.bfloat16),
            pltpu.VMEM((sources, 2, length, HD), jnp.float32),
        ],
        compiler_params=pltpu.CompilerParams(vmem_limit_bytes=16 * 1024 * 1024),
        cost_estimate=pl.CostEstimate(
            flops=5 * 2 * keys * length * width * segs,
            bytes_accessed=8 * 1024 * 1024,
            transcendentals=keys * width * segs,
        ),
        name="tree_attention_backward",
    )(parents, advantages, bias, *query_list, *kv_list)
    return outs[:segs], outs[segs:]


def join_queries_kernel(*refs):
    part = lax.rem(lax.axis_index("seg"), 2)
    refs, dq_ref = refs[:-1], refs[-1]
    chunks = len(refs) // 2
    width = refs[0].shape[1]
    for index, ref in enumerate(refs):
        side, chunk = divmod(index, chunks)
        where = part if side == 0 else 1 - part
        column = pl.multiple_of((where * chunks + chunk) * width, HD)
        dq_ref[:, pl.ds(column, width)] = ref[...]


def join_queries(own_list, other_list):
    chunks = len(own_list)
    length, width = own_list[0].shape
    vmem = pl.BlockSpec(memory_space=pltpu.VMEM)
    return pl.pallas_call(
        join_queries_kernel,
        out_shape=jax.ShapeDtypeStruct((length, 2 * chunks * width), jnp.bfloat16),
        in_specs=[vmem] * (2 * chunks),
        out_specs=vmem,
        cost_estimate=pl.CostEstimate(
            flops=0, bytes_accessed=8 * length * width * chunks, transcendentals=0
        ),
        compiler_params=SMALL,
        name="join_queries",
    )(*own_list, *other_list)


def join_keys_kernel(chunks, *refs):
    part = lax.rem(lax.axis_index("seg"), 2)
    other_refs, sum_refs = refs[:chunks], refs[chunks:-2]
    many = len(sum_refs) // chunks
    dk_ref, dv_ref = refs[-2:]
    for chunk in range(chunks):
        here = pl.ds(pl.multiple_of((part * chunks + chunk) * HD, HD), HD)
        there = pl.ds(pl.multiple_of(((1 - part) * chunks + chunk) * HD, HD), HD)
        for plane, out_ref in enumerate((dk_ref, dv_ref)):
            blocks = [ref[0, plane] for ref in sum_refs[chunk * many : (chunk + 1) * many]]
            total = sum(block.astype(jnp.float32) for block in blocks)
            out_ref[:, here] = total.astype(jnp.bfloat16)
            out_ref[:, there] = other_refs[chunk][plane]


def join_keys(others, summands):
    chunks = len(others)
    length = others[0].shape[1]
    vmem = pl.BlockSpec(memory_space=pltpu.VMEM)
    flat = [block for blocks in summands for block in blocks]
    out = jax.ShapeDtypeStruct((length, 2 * chunks * HD), jnp.bfloat16)
    return pl.pallas_call(
        functools.partial(join_keys_kernel, chunks),
        out_shape=(out, out),
        in_specs=[vmem] * (chunks + len(flat)),
        out_specs=(vmem, vmem),
        cost_estimate=pl.CostEstimate(
            flops=0, bytes_accessed=16 * length * HD * chunks, transcendentals=0
        ),
        compiler_params=SMALL,
        name="join_keys",
    )(*others, *flat)


def permute(array, pairs):
    return lax.ppermute(array, "seg", pairs)


def after(array, *earlier):
    return lax.optimization_barrier((array, *earlier))[0]


def paired_body(queries, direction, key_vectors, value_vectors, token_rows, parents, lengths, log_rate):
    groups = lax.axis_size("seg")
    length = queries.shape[0]
    chunks = key_vectors.shape[1] // HD // 2
    swap = [(i, i ^ 1) for i in range(groups)]
    steps = range(1, groups // 2)
    up = {d: [(i, (i + 2 * d) % groups) for i in range(groups)] for d in steps}
    down = {d: [(i, (i - 2 * d) % groups) for i in range(groups)] for d in steps}

    kept, given = pack(lengths, key_vectors, value_vectors, token_rows, 2, log_rate)
    taken = permute(given, swap)
    kept_far = [permute(kept, up[d]) for d in steps]
    kept_q, given_q = pack_queries(after(queries, kept), direction, 2, chunks)
    bias = masks(parents, lengths, length, 2)
    gated, *given_q = lax.optimization_barrier((taken, *given_q, *kept_far, bias))[: 1 + chunks]
    taken_q = [permute(block, swap) for block in given_q]
    taken_far = [permute(gated, up[d]) for d in steps]
    blocks = [kept, taken]
    for pair in zip(kept_far, taken_far):
        blocks += pair
    row, advantages = advantages_of(parents, lengths, blocks, length, 2, log_rate)

    dq_own, dq_back, dkv_list = [], [], []
    for chunk in range(chunks):
        query_list = [kept_q[chunk], taken_q[chunk]]
        dq, dkv = attend(parents, advantages, bias, query_list, blocks, chunk)
        dq_own.append(dq[0])
        dq_back.append(dq[1])
        dkv_list.append(dkv)

    summands = []
    for dkv in dkv_list:
        arrived = [permute(dkv[d], down[d]) for d in steps[::-1]]
        summands.append([after(dkv[0], dq_own[-1])] + arrived)
    dq_back = [permute(block, swap) for block in dq_back]
    others = []
    for blocks in summands:
        total = sum(block[1].astype(jnp.float32) for block in blocks)
        others.append(permute(total.astype(jnp.bfloat16), swap))
    grad_q = join_queries(dq_own, dq_back)
    grad_k, grad_v = join_keys(others, summands)
    return grad_q, grad_k, grad_v, row[0]


def fetch_rows(spread, wanted):
    routed = jnp.take(spread, jnp.maximum(wanted, 0), axis=0)
    return lax.all_to_all(routed, "seg", split_axis=0, concat_axis=2, tiled=True)


def return_rows(grad_rows, wanted, total_segs):
    returned = lax.all_to_all(grad_rows, "seg", split_axis=2, concat_axis=0, tiled=True)
    piece_len = returned.shape[2]
    feature_len = returned.shape[3]
    routed_ids = wanted.reshape(-1)
    targets = jnp.where(routed_ids >= 0, routed_ids, total_segs)
    summed = jax.ops.segment_sum(
        returned.reshape(-1, piece_len * feature_len).astype(jnp.float32),
        targets,
        num_segments=total_segs + 1,
    )[:total_segs]
    return lax.all_to_all(
        summed.reshape(total_segs, piece_len, feature_len),
        "seg",
        split_axis=0,
        concat_axis=1,
        tiled=True,
    )


def routed_body(queries, direction, key_vectors, value_vectors, token_rows, parents, lengths, log_rate):
    total_segs = parents.shape[0]
    length, width = key_vectors.shape
    heads = width // HD
    own = lax.axis_index("seg")
    own_len = lax.dynamic_slice_in_dim(lengths, own, 1)[0]
    terms = jnp.concatenate(token_terms(log_rate, own_len, *token_rows), axis=1)
    terms = lax.all_gather(terms, "seg", axis=0, tiled=True)
    row, advantages = advantages_of(parents, lengths, [terms], length, 1, log_rate)
    bias = masks(parents, lengths, length, 1)
    flat = jnp.concatenate([key_vectors, value_vectors], axis=1)[None]
    spread = lax.all_to_all(flat, "seg", split_axis=1, concat_axis=0, tiled=True)
    chains = ancestors(parents, DEPTH - 1)
    arrived = fetch_rows(spread, chains)[0]
    slot_kv = jnp.concatenate([flat, arrived]).reshape(DEPTH, length, 2, heads, HD)
    slot_kv = jnp.transpose(slot_kv, (0, 3, 2, 1, 4)).reshape(DEPTH, -1, HD)
    kv_list = [slot_kv[slot] for slot in range(DEPTH)]
    (kept_q,) = pack_queries(queries, direction, 1, heads)
    dq_list, dkv_list = [], []
    for head in range(heads):
        dq, dkv = attend(parents, advantages, bias, [kept_q[head]], kv_list, head)
        dq_list.append(dq[0])
        dkv_list.append(jnp.concatenate(dkv))
    rows = jnp.transpose(jnp.stack(dkv_list), (1, 3, 2, 0, 4)).reshape(1, DEPTH, length, -1)
    summed = return_rows(rows[:, 1:], chains, total_segs)[0] + rows[0, 0].astype(jnp.float32)
    grad_keys = summed[:, :width].astype(jnp.bfloat16)
    grad_values = summed[:, width:].astype(jnp.bfloat16)
    return jnp.concatenate(dq_list, axis=1), grad_keys, grad_values, row[0]


def body(
    queries,
    key_vectors,
    value_vectors,
    direction,
    rewards,
    logprobs,
    ref_logprobs,
    value_est,
    parents,
    seg_lengths,
):
    groups = lax.axis_size("seg")
    assert parents.shape[0] == groups
    log_rate = math.log(LAMBDA_SEG) / rewards.shape[0]
    token_rows = [rewards[None], logprobs[None], ref_logprobs[None], value_est[None]]
    plan = paired_body if groups == PAIRED_GROUPS else routed_body
    return plan(
        queries, direction, key_vectors, value_vectors, token_rows, parents, seg_lengths, log_rate
    )


def solution(mesh):
    in_specs = (
        P(("grp", "seg"), "tp"),
        P(("grp", "seg"), "tp"),
        P(("grp", "seg"), "tp"),
        P(("grp", "seg"), "tp"),
        P(("grp", "seg")),
        P(("grp", "seg")),
        P(("grp", "seg")),
        P(("grp", "seg")),
        P("grp"),
        P("grp"),
    )
    out_specs = (
        P(("grp", "seg"), "tp"),
        P(("grp", "seg"), "tp"),
        P(("grp", "seg"), "tp"),
        P(("grp", "seg")),
    )
    return jax.shard_map(body, mesh=mesh, in_specs=in_specs, out_specs=out_specs, check_vma=False)
```

time: 84.8 us -> 70.8 us (0.83)
  Pallas kernels: 22 us -> 16.1 us
  local copies, waits for them, and re-layouts: 8.04 us -> 2.19 us
  starting transfers between devices: 32.9 us -> 30.8 us
    unnamed x48 -> x10, local copies, waits for them, and re-layouts: 8.04 us -> 2.19 us
    pallas_call x1, Pallas kernels: 2.63 us -> 0.23 us  [pack_queries(): pl.pallas_call(functools.partial(pack_queries_kernel, parts), out_shape=(...]
    pallas_call x6, Pallas kernels: 17.2 us -> 15.1 us  [the longest x2 8.91 us: attend(): pl.pallas_call(functools.partial(attend_kernel, DEPTH, chunk, segs, sourc...]
    ppermute x22 -> x19, starting transfers between devices: 32.9 us -> 30.8 us  [permute(): return lax.ppermute(array, 'seg', pairs)]
    pallas_call x1, Pallas kernels: 2.09 us -> 0.77 us  [join_keys(): pl.pallas_call(functools.partial(join_keys_kernel, chunks), out_shape=(ou...]
    ppermute x22 -> x19, waiting for transfers between devices: 19.5 us -> 20.3 us  [permute(): return lax.ppermute(array, 'seg', pairs)]
  transfers between devices with their start and end apart: 22 -> 19, of which waited for: 6 -> 8; matrix products, arithmetic and copies ran while one was open for 1% -> 0% of each run, Pallas kernels for 19% -> 18%
where the time goes in v6:
time: 70.8 us; the launch traced here: 70.3 us
  starting transfers between devices  30.8 us (44%)
  waiting for transfers between devices  20.3 us (29%)
  Pallas kernels  16.1 us (23%)
  local copies, waits for them, and re-layouts  2.19 us (3%)
  between operations  0.75 us (1%)
    ppermute x19, starting transfers between devices, permute(): return lax.ppermute(array, 'seg', pairs)  30.8 us
    ppermute x19, waiting for transfers between devices, permute(): return lax.ppermute(array, 'seg', pairs)  20.3 us
    pallas_call x2, Pallas kernels, attend(): pl.pallas_call(functools.partial(attend_kernel, DEPTH, chunk, segs, sourc...  8.91 us
    pallas_call x1, Pallas kernels, pack(): pl.pallas_call(functools.partial(pack_kernel, log_rate), out_shape=(block...  2.46 us
    pallas_call x1, Pallas kernels, advantages_of(): pl.pallas_call(functools.partial(advantage_kernel, log_rate, DEPTH, segs)...  2.21 us
    unnamed x10, local copies, waits for them, and re-layouts  2.19 us
  transfers between devices with their start and end apart: 19, of which 8 were waited for; matrix products, arithmetic and copies ran while one was open for 0% of the time, Pallas kernels for 18%

profile of v6, /device:TPU:0, one launch (start us, length us, event | category | flops | bytes accessed | tf_op | source)
XLA Modules:
  0.0 70.3 jit_solution(4378270223936212294)
XLA Ops:
  0.6 2.5 %pack_keys_values.1 = (bf16[528,128]{1,0:T(8,128)(2,1)}, bf16[528,128]{1,0:T(8,128)(2,1)}) custom-call(s32[8]{0:T(128)} %lengths_s.3, bf16[128,512]{1,0:T(8,128)(2,1)} %k_ref.1, bf16[128,512]{1,0:T(8,128)(2,1)} %v_ref.1, f32[1,128]{1,0:T(1,128)} %bitcast.9, f32[1,128]{1,0:T(1,128)} %bitcast.10, f32[1,128]{1,0:T(1,128)} %bitcast.11, f32[1,128]{1,0:T(1,128)} %bitcast.12), custom_call_target="tpu_custom_call" | custom-call | flops 12800 | bytes 524288 | tf_op jit(solution)/shard_map/pack_keys_values/pallas_call | solution.py:113
  3.1 3.0 %collective-permute-start = (bf16[528,128]{1,0:T(8,128)(2,1)}, bf16[528,128]{1,0:T(8,128)(2,1)S(1)}, u32[]{:S(2)}, u32[]{:S(2)}) collective-permute-start(bf16[528,128]{1,0:T(8,128)(2,1)} %get-tuple-element.33), channel_id=1, source_target_pairs={{0,2},{2,0},{4,6},{6,4},{8,10},{10,8},{12,14},{14,12},{1,3},{3,1},... | collective-permute-start | bytes 405512 | tf_op jit(solution)/shard_map/ppermute | solution.py:462
  6.1 0.0 copy-start.3
  6.1 0.0 copy-start.4
  6.1 3.6 %collective-permute-start.3 = (bf16[528,128]{1,0:T(8,128)(2,1)}, bf16[528,128]{1,0:T(8,128)(2,1)S(1)}, u32[]{:S(2)}, u32[]{:S(2)}) collective-permute-start(bf16[528,128]{1,0:T(8,128)(2,1)} %get-tuple-element.32.refs_0_.refs_5_), channel_id=1, source_target_pairs={{0,12},{2,14},{4,0},{6,2},{8,4},{10,6},{12,8},{14,10},{1,13},{3,15... | collective-permute-start | bytes 405512 | tf_op jit(solution)/shard_map/ppermute | solution.py:462
  9.7 0.0 collective-permute-start.2
  9.7 1.0 %collective-permute-start.1 = (bf16[528,128]{1,0:T(8,128)(2,1)}, bf16[528,128]{1,0:T(8,128)(2,1)S(1)}, u32[]{:S(2)}, u32[]{:S(2)}) collective-permute-start(bf16[528,128]{1,0:T(8,128)(2,1)} %get-tuple-element.32.refs_0_.refs_5_), channel_id=1, source_target_pairs={{0,4},{2,6},{4,8},{6,10},{8,12},{10,14},{12,0},{14,2},{1,5},{3,7},... | collective-permute-start | bytes 405512 | tf_op jit(solution)/shard_map/ppermute | solution.py:462
  10.7 0.0 copy-start
  10.7 1.1 %copy-done = bf16[128,2560]{1,0:T(8,128)(2,1)S(1)} copy-done((bf16[128,2560]{1,0:T(8,128)(2,1)S(1)}, bf16[128,2560]{1,0:T(8,128)(2,1)}, u32[]{:S(2)}) %copy-start) | copy-done | bytes 655384
  11.8 0.0 copy-start.1
  11.8 1.1 %copy-done.1 = bf16[128,2560]{1,0:T(8,128)(2,1)S(1)} copy-done((bf16[128,2560]{1,0:T(8,128)(2,1)S(1)}, bf16[128,2560]{1,0:T(8,128)(2,1)}, u32[]{:S(2)}) %copy-start.1) | copy-done | bytes 655384
  12.9 0.2 pack_queries.1
  13.1 0.0 copy-done.3
  13.1 0.0 copy-done.4
  13.2 0.0 copy-start.2
  13.2 0.6 masks.1.refs_2_
  13.8 0.0 collective-permute-done.refs_1_.refs_6_
  13.8 0.3 collective-permute-done.3.refs_6_.refs_11_
  14.1 7.0 %collective-permute-done.2.refs_4_.refs_9_ = bf16[528,128]{1,0:T(8,128)(2,1)S(1)} collective-permute-done((bf16[528,128]{1,0:T(8,128)(2,1)}, bf16[528,128]{1,0:T(8,128)(2,1)S(1)}, u32[]{:S(2)}, u32[]{:S(2)}) %collective-permute-start.2) | collective-permute-done | bytes 135200 | tf_op jit(solution)/shard_map/ppermute | solution.py:462
  21.1 0.0 collective-permute-done.1.refs_2_.refs_7_
  21.1 0.5 collective-permute-start.7
  21.6 1.5 %collective-permute-start.8 = (bf16[2,5,128,128]{3,2,1,0:T(8,128)(2,1)S(1)}, bf16[2,5,128,128]{3,2,1,0:T(8,128)(2,1)S(1)}, u32[]{:S(2)}, u32[]{:S(2)}) collective-permute-start(bf16[2,5,128,128]{3,2,1,0:T(8,128)(2,1)S(1)} %get-tuple-element.43), channel_id=1, source_target_pairs={{0,2},{2,0},{4,6},{6,4},{8,10},{10,8},{12,14},{14,12},{1,3},{3,1},... | collective-permute-start | bytes 983048 | tf_op jit(solution)/shard_map/ppermute | solution.py:462
  23.1 1.6 %collective-permute-start.6 = (bf16[528,128]{1,0:T(8,128)(2,1)S(1)}, bf16[528,128]{1,0:T(8,128)(2,1)S(1)}, u32[]{:S(2)}, u32[]{:S(2)}) collective-permute-start(bf16[528,128]{1,0:T(8,128)(2,1)S(1)} %collective-permute-done.refs_1_.refs_6_), channel_id=1, source_target_pairs={{0,12},{2,14},{4,0},{6,2},{8,4},{10,6},{12,8},{14,10},{1,13},{3,15... | collective-permute-start | bytes 405512 | tf_op jit(solution)/shard_map/ppermute | solution.py:462
  24.7 1.1 %collective-permute-start.5 = (bf16[528,128]{1,0:T(8,128)(2,1)S(1)}, bf16[528,128]{1,0:T(8,128)(2,1)S(1)}, u32[]{:S(2)}, u32[]{:S(2)}) collective-permute-start(bf16[528,128]{1,0:T(8,128)(2,1)S(1)} %collective-permute-done.refs_1_.refs_6_), channel_id=1, source_target_pairs={{0,8},{2,10},{4,12},{6,14},{8,0},{10,2},{12,4},{14,6},{1,9},{3,11}... | collective-permute-start | bytes 405512 | tf_op jit(solution)/shard_map/ppermute | solution.py:462
  25.9 2.0 %collective-permute-start.4 = (bf16[528,128]{1,0:T(8,128)(2,1)S(1)}, bf16[528,128]{1,0:T(8,128)(2,1)S(1)}, u32[]{:S(2)}, u32[]{:S(2)}) collective-permute-start(bf16[528,128]{1,0:T(8,128)(2,1)S(1)} %collective-permute-done.refs_1_.refs_6_), channel_id=1, source_target_pairs={{0,4},{2,6},{4,8},{6,10},{8,12},{10,14},{12,0},{14,2},{1,5},{3,7},... | collective-permute-start | bytes 405512 | tf_op jit(solution)/shard_map/ppermute | solution.py:462
  27.9 1.2 %collective-permute-done.6.refs_7_.refs_12_ = bf16[528,128]{1,0:T(8,128)(2,1)S(1)} collective-permute-done((bf16[528,128]{1,0:T(8,128)(2,1)S(1)}, bf16[528,128]{1,0:T(8,128)(2,1)S(1)}, u32[]{:S(2)}, u32[]{:S(2)}) %collective-permute-start.6) | collective-permute-done | bytes 135200 | tf_op jit(solution)/shard_map/ppermute | solution.py:462
  29.1 7.9 %collective-permute-done.5.refs_5_.refs_10_ = bf16[528,128]{1,0:T(8,128)(2,1)S(1)} collective-permute-done((bf16[528,128]{1,0:T(8,128)(2,1)S(1)}, bf16[528,128]{1,0:T(8,128)(2,1)S(1)}, u32[]{:S(2)}, u32[]{:S(2)}) %collective-permute-start.5) | collective-permute-done | bytes 135200 | tf_op jit(solution)/shard_map/ppermute | solution.py:462
  37.0 0.0 collective-permute-done.4.refs_3_.refs_8_
  37.0 0.0 copy-done.2
  37.0 2.2 %advantages.1 = (f32[1,128]{1,0:T(1,128)}, f32[2,128,128]{2,1,0:T(8,128)S(1)}) custom-call(s32[8]{0:T(128)S(1)} %copy-done.4, s32[8]{0:T(128)S(1)} %copy-done.3, bf16[528,128]{1,0:T(8,128)(2,1)S(1)} %copy-done.2, bf16[528,128]{1,0:T(8,128)(2,1)S(1)} %collective-permute-done.refs_1_.refs_6_, bf16[528,128]{1,0:T(8,128)(2,1)S(1)} %collective-permute-done.1.refs_2_.refs_7_, ...), custom_call_target="tpu_custom_call" | custom-call | flops 3276800 | bytes 262144 | tf_op jit(solution)/shard_map/advantages/pallas_call | solution.py:272
  39.2 0.0 collective-permute-done.7.refs_4_
  39.2 4.5 %tree_attention_backward.2 = (bf16[128,640]{1,0:T(8,128)(2,1)S(1)}, bf16[128,640]{1,0:T(8,128)(2,1)S(1)}, bf16[2,2,128,128]{3,2,1,0:T(8,128)(2,1)S(1)}, bf16[2,2...) custom-call(s32[8]{0:T(128)S(1)} %copy-done.4, ...), custom_call_target="tpu_custom_call" | custom-call | flops 1048576000 | bytes 8388608 | tf_op jit(solution)/shard_map/tree_attention_backward/pallas_call | solution.py:376
  43.6 0.1 collective-permute-start.11
  43.7 1.3 %collective-permute-start.12 = (bf16[2,2,128,128]{3,2,1,0:T(8,128)(2,1)S(1)}, bf16[2,2,128,128]{3,2,1,0:T(8,128)(2,1)S(1)}, u32[]{:S(2)}, u32[]{:S(2)}) collective-permute-start(bf16[2,2,128,128]{3,2,1,0:T(8,128)(2,1)S(1)} %get-tuple-element.50), channel_id=1, source_target_pairs={{0,8},{2,10},{4,12},{6,14},{8,0},{10,2},{12,4},{14,6},{1,9},{3,11}... | collective-permute-start | bytes 393224 | tf_op jit(solution)/shard_map/ppermute | solution.py:462
  45.0 2.8 %collective-permute-start.13 = (bf16[2,2,128,128]{3,2,1,0:T(8,128)(2,1)S(1)}, bf16[2,2,128,128]{3,2,1,0:T(8,128)(2,1)S(1)}, u32[]{:S(2)}, u32[]{:S(2)}) collective-permute-start(bf16[2,2,128,128]{3,2,1,0:T(8,128)(2,1)S(1)} %get-tuple-element.51), channel_id=1, source_target_pairs={{0,12},{2,14},{4,0},{6,2},{8,4},{10,6},{12,8},{14,10},{1,13},{3,15... | collective-permute-start | bytes 393224 | tf_op jit(solution)/shard_map/ppermute | solution.py:462
  47.9 0.5 collective-permute-start.9
  48.4 0.0 collective-permute-done.8.refs_4_
  48.4 4.5 %tree_attention_backward.3 = (bf16[128,640]{1,0:T(8,128)(2,1)S(1)}, bf16[128,640]{1,0:T(8,128)(2,1)S(1)}, bf16[2,2,128,128]{3,2,1,0:T(8,128)(2,1)S(1)}, bf16[2,2...) custom-call(s32[8]{0:T(128)S(1)} %copy-done.4, ...), custom_call_target="tpu_custom_call" | custom-call | flops 1048576000 | bytes 8388608 | tf_op jit(solution)/shard_map/tree_attention_backward/pallas_call | solution.py:376
  52.8 0.3 collective-permute-start.15
  53.1 0.0 collective-permute-done.11.refs_3_
  53.1 4.9 %collective-permute-start.16 = (bf16[2,2,128,128]{3,2,1,0:T(8,128)(2,1)S(1)}, bf16[2,2,128,128]{3,2,1,0:T(8,128)(2,1)S(1)}, u32[]{:S(2)}, u32[]{:S(2)}) collective-permute-start(bf16[2,2,128,128]{3,2,1,0:T(8,128)(2,1)S(1)} %get-tuple-element.55), channel_id=1, source_target_pairs={{0,8},{2,10},{4,12},{6,14},{8,0},{10,2},{12,4},{14,6},{1,9},{3,11}... | collective-permute-start | bytes 393224 | tf_op jit(solution)/shard_map/ppermute | solution.py:462
  58.1 0.0 collective-permute-done.12.refs_4_
  58.1 3.7 %collective-permute-start.17 = (bf16[2,2,128,128]{3,2,1,0:T(8,128)(2,1)S(1)}, bf16[2,2,128,128]{3,2,1,0:T(8,128)(2,1)S(1)}, u32[]{:S(2)}, u32[]{:S(2)}) collective-permute-start(bf16[2,2,128,128]{3,2,1,0:T(8,128)(2,1)S(1)} %get-tuple-element.56), channel_id=1, source_target_pairs={{0,12},{2,14},{4,0},{6,2},{8,4},{10,6},{12,8},{14,10},{1,13},{3,15... | collective-permute-start | bytes 393224 | tf_op jit(solution)/shard_map/ppermute | solution.py:462
  61.8 0.0 collective-permute-done.13.refs_5_
  61.8 0.5 collective-permute-start.10
  62.3 0.0 collective-permute-done.15.refs_7_
  62.3 1.6 %collective-permute-start.14 = (bf16[2,128,128]{2,1,0:T(8,128)(2,1)S(1)}, bf16[2,128,128]{2,1,0:T(8,128)(2,1)S(1)}, u32[]{:S(2)}, u32[]{:S(2)}) collective-permute-start(bf16[2,128,128]{2,1,0:T(8,128)(2,1)S(1)} %fusion), channel_id=1, source_target_pairs={{0,2},{2,0},{4,6},{6,4},{8,10},{10,8},{12,14},{14,12},{1,3},{3,1},... | collective-permute-start | bytes 196616 | tf_op jit(solution)/shard_map/ppermute | solution.py:462
  63.9 0.8 %collective-permute-done.16.refs_8_ = bf16[2,2,128,128]{3,2,1,0:T(8,128)(2,1)S(1)} collective-permute-done((bf16[2,2,128,128]{3,2,1,0:T(8,128)(2,1)S(1)}, bf16[2,2,128,128]{3,2,1,0:T(8,128)(2,1)S(1)}, u32[]{:S(2)}, u32[]{:S(2)}) %collective-permute-start.16) | collective-permute-done | bytes 131104 | tf_op jit(solution)/shard_map/ppermute | solution.py:462
  64.7 0.4 collective-permute-done.17.refs_9_
  65.2 0.7 collective-permute-start.18
  65.8 0.0 collective-permute-done.9.refs_2_
  65.8 2.0 %collective-permute-done.10.refs_3_ = bf16[128,640]{1,0:T(8,128)(2,1)S(1)} collective-permute-done((bf16[128,640]{1,0:T(8,128)(2,1)S(1)}, bf16[128,640]{1,0:T(8,128)(2,1)S(1)}, u32[]{:S(2)}, u32[]{:S(2)}) %collective-permute-start.10) | collective-permute-done | bytes 163872 | tf_op jit(solution)/shard_map/ppermute | solution.py:462
  67.8 0.9 %join_queries.1 = bf16[128,2560]{1,0:T(8,128)(2,1)} custom-call(bf16[128,640]{1,0:T(8,128)(2,1)S(1)} %get-tuple-element.41.refs_0_, bf16[128,640]{1,0:T(8,128)(2,1)S(1)} %get-tuple-element.44.refs_1_, bf16[128,640]{1,0:T(8,128)(2,1)S(1)} %collective-permute-done.9.refs_2_, bf16[128,640]{1,0:T(8,128)(2,1)S(1)} %collective-permute-done.10.refs_3_), custom_call_target="tpu_custom_call" | custom-call | bytes 1310720 | tf_op jit(solution)/shard_map/join_queries/pallas_call | solution.py:414
  68.7 0.0 collective-permute-done.14.refs_0_
  68.7 0.8 %collective-permute-done.18.refs_1_ = bf16[2,128,128]{2,1,0:T(8,128)(2,1)S(1)} collective-permute-done((bf16[2,128,128]{2,1,0:T(8,128)(2,1)S(1)}, bf16[2,128,128]{2,1,0:T(8,128)(2,1)S(1)}, u32[]{:S(2)}, u32[]{:S(2)}) %collective-permute-start.18) | collective-permute-done | bytes 65568 | tf_op jit(solution)/shard_map/ppermute | solution.py:462
  69.5 0.8 %join_keys.1 = (bf16[128,512]{1,0:T(8,128)(2,1)}, bf16[128,512]{1,0:T(8,128)(2,1)}) custom-call(bf16[2,128,128]{2,1,0:T(8,128)(2,1)S(1)} %collective-permute-done.14.refs_0_, bf16[2,128,128]{2,1,0:T(8,128)(2,1)S(1)} %collective-permute-done.18.refs_1_, bf16[2,2,128,128]{3,2,1,0:T(8,128)(2,1)S(1)} %get-tuple-element.48.refs_2_, ...), custom_call_target="tpu_custom_call" | custom-call | bytes 524288 | tf_op jit(solution)/shard_map/join_keys/pallas_call | solution.py:448
  (2 shorter events, 0.1 us)
Async XLA Ops:
  3.1 10.7 %collective-permute-start = (bf16[528,128]{1,0:T(8,128)(2,1)}, bf16[528,128]{1,0:T(8,128)(2,1)S(1)}, u32[]{:S(2)}, u32[]{:S(2)}) collective-permute-start(bf16[528,128]{1,0:T(8,128)(2,1)} %get-tuple-element.33), channel_id=1, source_target_pairs={{0,2},{2,0},{4,6},{6,4},{8,10},{10,8},{12,14},{14,12},{1,3},{3,1},... | collective-permute-start | bytes 405512 | tf_op jit(solution)/shard_map/ppermute | solution.py:462
  6.1 7.0 %copy-start.3 = (s32[8]{0:T(128)S(1)}, s32[8]{0:T(128)}, u32[]{:S(2)}) copy-start(s32[8]{0:T(128)} %lengths_s.3) | copy-start | bytes 100
  6.1 7.0 %copy-start.4 = (s32[8]{0:T(128)S(1)}, s32[8]{0:T(128)}, u32[]{:S(2)}) copy-start(s32[8]{0:T(128)} %refs_0_.3) | copy-start | bytes 100
  6.1 7.9 %collective-permute-start.3 = (bf16[528,128]{1,0:T(8,128)(2,1)}, bf16[528,128]{1,0:T(8,128)(2,1)S(1)}, u32[]{:S(2)}, u32[]{:S(2)}) collective-permute-start(bf16[528,128]{1,0:T(8,128)(2,1)} %get-tuple-element.32.refs_0_.refs_5_), channel_id=1, source_target_pairs={{0,12},{2,14},{4,0},{6,2},{8,4},{10,6},{12,8},{14,10},{1,13},{3,15... | collective-permute-start | bytes 405512 | tf_op jit(solution)/shard_map/ppermute | solution.py:462
  9.7 11.4 %collective-permute-start.2 = (bf16[528,128]{1,0:T(8,128)(2,1)}, bf16[528,128]{1,0:T(8,128)(2,1)S(1)}, u32[]{:S(2)}, u32[]{:S(2)}) collective-permute-start(bf16[528,128]{1,0:T(8,128)(2,1)} %get-tuple-element.32.refs_0_.refs_5_), channel_id=1, source_target_pairs={{0,8},{2,10},{4,12},{6,14},{8,0},{10,2},{12,4},{14,6},{1,9},{3,11}... | collective-permute-start | bytes 405512 | tf_op jit(solution)/shard_map/ppermute | solution.py:462
  9.7 11.4 %collective-permute-start.1 = (bf16[528,128]{1,0:T(8,128)(2,1)}, bf16[528,128]{1,0:T(8,128)(2,1)S(1)}, u32[]{:S(2)}, u32[]{:S(2)}) collective-permute-start(bf16[528,128]{1,0:T(8,128)(2,1)} %get-tuple-element.32.refs_0_.refs_5_), channel_id=1, source_target_pairs={{0,4},{2,6},{4,8},{6,10},{8,12},{10,14},{12,0},{14,2},{1,5},{3,7},... | collective-permute-start | bytes 405512 | tf_op jit(solution)/shard_map/ppermute | solution.py:462
  10.7 1.1 %copy-start = (bf16[128,2560]{1,0:T(8,128)(2,1)S(1)}, bf16[128,2560]{1,0:T(8,128)(2,1)}, u32[]{:S(2)}) copy-start(bf16[128,2560]{1,0:T(8,128)(2,1)} %q_ref) | copy-start | bytes 1966084
  11.8 1.1 %copy-start.1 = (bf16[128,2560]{1,0:T(8,128)(2,1)S(1)}, bf16[128,2560]{1,0:T(8,128)(2,1)}, u32[]{:S(2)}) copy-start(bf16[128,2560]{1,0:T(8,128)(2,1)} %dir_ref.1) | copy-start | bytes 1966084
  13.2 23.8 %copy-start.2 = (bf16[528,128]{1,0:T(8,128)(2,1)S(1)}, bf16[528,128]{1,0:T(8,128)(2,1)}, u32[]{:S(2)}) copy-start(bf16[528,128]{1,0:T(8,128)(2,1)} %get-tuple-element.32.refs_0_.refs_5_) | copy-start | bytes 405508
  21.1 18.1 %collective-permute-start.7 = (bf16[2,5,128,128]{3,2,1,0:T(8,128)(2,1)S(1)}, bf16[2,5,128,128]{3,2,1,0:T(8,128)(2,1)S(1)}, u32[]{:S(2)}, u32[]{:S(2)}) collective-permute-start(bf16[2,5,128,128]{3,2,1,0:T(8,128)(2,1)S(1)} %get-tuple-element.40), channel_id=1, source_target_pairs={{0,2},{2,0},{4,6},{6,4},{8,10},{10,8},{12,14},{14,12},{1,3},{3,1},... | collective-permute-start | bytes 983048 | tf_op jit(solution)/shard_map/ppermute | solution.py:462
  21.6 26.8 %collective-permute-start.8 = (bf16[2,5,128,128]{3,2,1,0:T(8,128)(2,1)S(1)}, bf16[2,5,128,128]{3,2,1,0:T(8,128)(2,1)S(1)}, u32[]{:S(2)}, u32[]{:S(2)}) collective-permute-start(bf16[2,5,128,128]{3,2,1,0:T(8,128)(2,1)S(1)} %get-tuple-element.43), channel_id=1, source_target_pairs={{0,2},{2,0},{4,6},{6,4},{8,10},{10,8},{12,14},{14,12},{1,3},{3,1},... | collective-permute-start | bytes 983048 | tf_op jit(solution)/shard_map/ppermute | solution.py:462
  23.1 6.0 %collective-permute-start.6 = (bf16[528,128]{1,0:T(8,128)(2,1)S(1)}, bf16[528,128]{1,0:T(8,128)(2,1)S(1)}, u32[]{:S(2)}, u32[]{:S(2)}) collective-permute-start(bf16[528,128]{1,0:T(8,128)(2,1)S(1)} %collective-permute-done.refs_1_.refs_6_), channel_id=1, source_target_pairs={{0,12},{2,14},{4,0},{6,2},{8,4},{10,6},{12,8},{14,10},{1,13},{3,15... | collective-permute-start | bytes 405512 | tf_op jit(solution)/shard_map/ppermute | solution.py:462
  24.7 12.2 %collective-permute-start.5 = (bf16[528,128]{1,0:T(8,128)(2,1)S(1)}, bf16[528,128]{1,0:T(8,128)(2,1)S(1)}, u32[]{:S(2)}, u32[]{:S(2)}) collective-permute-start(bf16[528,128]{1,0:T(8,128)(2,1)S(1)} %collective-permute-done.refs_1_.refs_6_), channel_id=1, source_target_pairs={{0,8},{2,10},{4,12},{6,14},{8,0},{10,2},{12,4},{14,6},{1,9},{3,11}... | collective-permute-start | bytes 405512 | tf_op jit(solution)/shard_map/ppermute | solution.py:462
  25.9 11.1 %collective-permute-start.4 = (bf16[528,128]{1,0:T(8,128)(2,1)S(1)}, bf16[528,128]{1,0:T(8,128)(2,1)S(1)}, u32[]{:S(2)}, u32[]{:S(2)}) collective-permute-start(bf16[528,128]{1,0:T(8,128)(2,1)S(1)} %collective-permute-done.refs_1_.refs_6_), channel_id=1, source_target_pairs={{0,4},{2,6},{4,8},{6,10},{8,12},{10,14},{12,0},{14,2},{1,5},{3,7},... | collective-permute-start | bytes 405512 | tf_op jit(solution)/shard_map/ppermute | solution.py:462
  43.6 9.5 %collective-permute-start.11 = (bf16[2,2,128,128]{3,2,1,0:T(8,128)(2,1)S(1)}, bf16[2,2,128,128]{3,2,1,0:T(8,128)(2,1)S(1)}, u32[]{:S(2)}, u32[]{:S(2)}) collective-permute-start(bf16[2,2,128,128]{3,2,1,0:T(8,128)(2,1)S(1)} %get-tuple-element.49), channel_id=1, source_target_pairs={{0,4},{2,6},{4,8},{6,10},{8,12},{10,14},{12,0},{14,2},{1,5},{3,7},... | collective-permute-start | bytes 393224 | tf_op jit(solution)/shard_map/ppermute | solution.py:462
  43.7 14.4 %collective-permute-start.12 = (bf16[2,2,128,128]{3,2,1,0:T(8,128)(2,1)S(1)}, bf16[2,2,128,128]{3,2,1,0:T(8,128)(2,1)S(1)}, u32[]{:S(2)}, u32[]{:S(2)}) collective-permute-start(bf16[2,2,128,128]{3,2,1,0:T(8,128)(2,1)S(1)} %get-tuple-element.50), channel_id=1, source_target_pairs={{0,8},{2,10},{4,12},{6,14},{8,0},{10,2},{12,4},{14,6},{1,9},{3,11}... | collective-permute-start | bytes 393224 | tf_op jit(solution)/shard_map/ppermute | solution.py:462
  45.0 16.8 %collective-permute-start.13 = (bf16[2,2,128,128]{3,2,1,0:T(8,128)(2,1)S(1)}, bf16[2,2,128,128]{3,2,1,0:T(8,128)(2,1)S(1)}, u32[]{:S(2)}, u32[]{:S(2)}) collective-permute-start(bf16[2,2,128,128]{3,2,1,0:T(8,128)(2,1)S(1)} %get-tuple-element.51), channel_id=1, source_target_pairs={{0,12},{2,14},{4,0},{6,2},{8,4},{10,6},{12,8},{14,10},{1,13},{3,15... | collective-permute-start | bytes 393224 | tf_op jit(solution)/shard_map/ppermute | solution.py:462
  47.9 18.0 %collective-permute-start.9 = (bf16[128,640]{1,0:T(8,128)(2,1)S(1)}, bf16[128,640]{1,0:T(8,128)(2,1)S(1)}, u32[]{:S(2)}, u32[]{:S(2)}) collective-permute-start(bf16[128,640]{1,0:T(8,128)(2,1)S(1)} %get-tuple-element.45), channel_id=1, source_target_pairs={{0,2},{2,0},{4,6},{6,4},{8,10},{10,8},{12,14},{14,12},{1,3},{3,1},... | collective-permute-start | bytes 491528 | tf_op jit(solution)/shard_map/ppermute | solution.py:462
  52.8 9.4 %collective-permute-start.15 = (bf16[2,2,128,128]{3,2,1,0:T(8,128)(2,1)S(1)}, bf16[2,2,128,128]{3,2,1,0:T(8,128)(2,1)S(1)}, u32[]{:S(2)}, u32[]{:S(2)}) collective-permute-start(bf16[2,2,128,128]{3,2,1,0:T(8,128)(2,1)S(1)} %get-tuple-element.54), channel_id=1, source_target_pairs={{0,4},{2,6},{4,8},{6,10},{8,12},{10,14},{12,0},{14,2},{1,5},{3,7},... | collective-permute-start | bytes 393224 | tf_op jit(solution)/shard_map/ppermute | solution.py:462
  53.1 11.6 %collective-permute-start.16 = (bf16[2,2,128,128]{3,2,1,0:T(8,128)(2,1)S(1)}, bf16[2,2,128,128]{3,2,1,0:T(8,128)(2,1)S(1)}, u32[]{:S(2)}, u32[]{:S(2)}) collective-permute-start(bf16[2,2,128,128]{3,2,1,0:T(8,128)(2,1)S(1)} %get-tuple-element.55), channel_id=1, source_target_pairs={{0,8},{2,10},{4,12},{6,14},{8,0},{10,2},{12,4},{14,6},{1,9},{3,11}... | collective-permute-start | bytes 393224 | tf_op jit(solution)/shard_map/ppermute | solution.py:462
  58.1 7.1 %collective-permute-start.17 = (bf16[2,2,128,128]{3,2,1,0:T(8,128)(2,1)S(1)}, bf16[2,2,128,128]{3,2,1,0:T(8,128)(2,1)S(1)}, u32[]{:S(2)}, u32[]{:S(2)}) collective-permute-start(bf16[2,2,128,128]{3,2,1,0:T(8,128)(2,1)S(1)} %get-tuple-element.56), channel_id=1, source_target_pairs={{0,12},{2,14},{4,0},{6,2},{8,4},{10,6},{12,8},{14,10},{1,13},{3,15... | collective-permute-start | bytes 393224 | tf_op jit(solution)/shard_map/ppermute | solution.py:462
  61.8 6.0 %collective-permute-start.10 = (bf16[128,640]{1,0:T(8,128)(2,1)S(1)}, bf16[128,640]{1,0:T(8,128)(2,1)S(1)}, u32[]{:S(2)}, u32[]{:S(2)}) collective-permute-start(bf16[128,640]{1,0:T(8,128)(2,1)S(1)} %get-tuple-element.46), channel_id=1, source_target_pairs={{0,2},{2,0},{4,6},{6,4},{8,10},{10,8},{12,14},{14,12},{1,3},{3,1},... | collective-permute-start | bytes 491528 | tf_op jit(solution)/shard_map/ppermute | solution.py:462
  62.3 6.4 %collective-permute-start.14 = (bf16[2,128,128]{2,1,0:T(8,128)(2,1)S(1)}, bf16[2,128,128]{2,1,0:T(8,128)(2,1)S(1)}, u32[]{:S(2)}, u32[]{:S(2)}) collective-permute-start(bf16[2,128,128]{2,1,0:T(8,128)(2,1)S(1)} %fusion), channel_id=1, source_target_pairs={{0,2},{2,0},{4,6},{6,4},{8,10},{10,8},{12,14},{14,12},{1,3},{3,1},... | collective-permute-start | bytes 196616 | tf_op jit(solution)/shard_map/ppermute | solution.py:462
  65.2 4.3 %collective-permute-start.18 = (bf16[2,128,128]{2,1,0:T(8,128)(2,1)S(1)}, bf16[2,128,128]{2,1,0:T(8,128)(2,1)S(1)}, u32[]{:S(2)}, u32[]{:S(2)}) collective-permute-start(bf16[2,128,128]{2,1,0:T(8,128)(2,1)S(1)} %fusion.1), channel_id=1, source_target_pairs={{0,2},{2,0},{4,6},{6,4},{8,10},{10,8},{12,14},{14,12},{1,3},{3,1},... | collective-permute-start | bytes 196616 | tf_op jit(solution)/shard_map/ppermute | solution.py:462

commit v7 on v6

--- a/solution.py
+++ b/solution.py
@@ -64,27 +64,12 @@
     logprobs_ref,
     ref_logprobs_ref,
     values_ref,
-    *refs,
+    *out_refs,
 ):
-    out_refs, sems = refs[:-1], refs[-1]
     own = lax.axis_index("seg")
     length = k_ref.shape[0]
     parts = len(out_refs)
     heads = k_ref.shape[1] // HD // parts
-    copies = []
-    for step in range(parts):
-        part = lax.rem(own + step, parts)
-        for h in range(heads):
-            columns = pl.ds(pl.multiple_of((part * heads + h) * HD, HD), HD)
-            for plane, ref in enumerate((k_ref, v_ref)):
-                rows = pl.ds((h * 2 + plane) * length, length)
-                copies.append(
-                    pltpu.make_async_copy(
-                        ref.at[:, columns], out_refs[step].at[rows, :], sems.at[len(copies)]
-                    )
-                )
-    for copy in copies:
-        copy.start()
     terms = token_terms(
         log_rate,
         lengths_ref[own],
@@ -93,29 +78,31 @@
         ref_logprobs_ref[...],
         values_ref[...],
     )
-    rows = [part.astype(jnp.float32) for x in terms for part in split_float(x)]
-    rows.append(jnp.zeros((TERM_ROWS - len(rows), HD), jnp.float32))
-    rows = jnp.concatenate(rows).astype(jnp.bfloat16)
-    for out_ref in out_refs:
-        out_ref[2 * heads * length :, :] = rows
-    for copy in copies:
-        copy.wait()
+    tail = [part.astype(jnp.float32) for x in terms for part in split_float(x)]
+    tail.append(jnp.zeros((TERM_ROWS - len(tail), HD), jnp.float32))
+    tail = jnp.concatenate(tail).astype(jnp.bfloat16)
+    for step, out_ref in enumerate(out_refs):
+        part = lax.rem(own + step, parts)
+        for h in range(heads):
+            columns = pl.ds(pl.multiple_of((part * heads + h) * HD, HD), HD)
+            for plane, ref in enumerate((k_ref, v_ref)):
+                first = (h * 2 + plane) * length
+                out_ref[first : first + length, :] = ref[:, columns]
+        out_ref[2 * heads * length :, :] = tail
 
 
 def pack(lengths, k, v, token_rows, parts, log_rate):
     length, width = k.shape
     smem = pl.BlockSpec(memory_space=pltpu.SMEM)
     vmem = pl.BlockSpec(memory_space=pltpu.VMEM)
-    hbm = pl.BlockSpec(memory_space=pltpu.HBM)
     heads = width // HD // parts
     assert length == HD
     block = jax.ShapeDtypeStruct((2 * heads * length + TERM_ROWS, HD), k.dtype)
     return pl.pallas_call(
         functools.partial(pack_kernel, log_rate),
         out_shape=(block,) * parts,
-        in_specs=[smem, hbm, hbm] + [vmem] * 4,
+        in_specs=[smem] + [vmem] * 6,
         out_specs=(vmem,) * parts,
-        scratch_shapes=[pltpu.SemaphoreType.DMA((2 * heads * parts,))],
         cost_estimate=pl.CostEstimate(
             flops=length * 100, bytes_accessed=8 * length * width, transcendentals=length
         ),
@@ -163,13 +150,69 @@
     return own - part + lax.rem(part + i, segs)
 
 
-def mask_kernel(depth, parents_s, lengths_s, bias_ref):
+def read_terms(ref):
+    if ref.dtype == jnp.float32:
+        length = ref.shape[1] // 2
+        return ref[:, :length], ref[:, length:]
+    tail = ref[ref.shape[0] - TERM_ROWS :, :].astype(jnp.float32)
+    return tail[0:1] + tail[1:2] + tail[2:3], tail[3:4] + tail[4:5] + tail[5:6]
+
+
+def prepare_kernel(log_rate, depth, parents_s, lengths_s, *refs):
+    term_refs, (bias_ref, columns_ref, weights_ref) = refs[:-3], refs[-3:]
     segs, _, length = bias_ref.shape
+    count = parents_s.shape[0]
     own = lax.axis_index("seg")
+
+    row_id = lax.broadcasted_iota(jnp.int32, (count, count), 0)
+    col_id = lax.broadcasted_iota(jnp.int32, (count, count), 1)
+    seg_col = lax.broadcasted_iota(jnp.int32, (count, 1), 0)
+
+    def to_col(row):
+        return jnp.sum(jnp.where(row_id == col_id, row, 0.0), axis=1, keepdims=True)
+
+    parent_row = jnp.full((1, count), -1, jnp.int32)
+    lens_col = jnp.zeros((count, 1), jnp.int32)
+    for seg in range(count):
+        parent_row = jnp.where(col_id[:1] == seg, parents_s[seg], parent_row)
+        lens_col = jnp.where(seg_col == seg, lengths_s[seg], lens_col)
+    lens_col = lens_col.astype(jnp.float32)
+    children = (parent_row == row_id).astype(jnp.float32)
+    tree = children / jnp.maximum(jnp.sum(children, axis=1, keepdims=True), 1.0)
+    factor = jnp.exp(lens_col * log_rate)
+    last_factor = jnp.exp((lens_col - 1.0) * log_rate)
+
     u_id = lax.broadcasted_iota(jnp.int32, (length, length), 0)
     t_id = lax.broadcasted_iota(jnp.int32, (length, length), 1)
+    offset = (t_id - u_id).astype(jnp.float32)
+    discount = jnp.where(offset >= 0, jnp.exp(offset * log_rate), 0.0)
+    t_col = lax.broadcasted_iota(jnp.int32, (length, 1), 0)
+    lane = lax.broadcasted_iota(jnp.int32, (count, HD), 1)
     for i in range(segs):
-        ancestor = segment_of(own, segs, i)
+        seg = segment_of(own, segs, i)
+        seg_len = lengths_s[seg]
+        deltas, _ = read_terms(term_refs[i])
+        live = t_col < seg_len
+        left = (seg_len - t_col).astype(jnp.float32)
+        columns = (
+            jnp.sum(discount * deltas, axis=1, keepdims=True),
+            jnp.exp((left - 1.0) * log_rate),
+            jnp.exp(left * log_rate),
+        )
+        for index, column in enumerate(columns):
+            column = jnp.where(live, column, 0.0)
+            columns_ref[i, index] = jnp.broadcast_to(column, (length, HD))
+
+        row = jnp.sum(jnp.where(row_id == seg, tree, 0.0), axis=0, keepdims=True)
+        value_col = col = total = to_col(row)
+        for _ in range(depth):
+            col = to_col(jnp.sum(col * factor * tree, axis=0, keepdims=True))
+            total = total + col
+        through = to_col(jnp.sum(total * last_factor * tree, axis=0, keepdims=True))
+        weights_ref[i, 0] = jnp.where(lane == 1, value_col, 0.0)
+        weights_ref[i, 1] = jnp.where(lane == 0, total, jnp.where(lane == 1, through, 0.0))
+
+        ancestor = seg
         for slot in range(depth):
             if slot > 0:
                 ancestor = parent_of(ancestor, parents_s)
@@ -180,111 +223,76 @@
             bias_ref[i, slot * length : (slot + 1) * length, :] = jnp.where(seen, 0.0, -1e30)
 
 
-def masks(parents, lengths, length, segs):
+def prepare(parents, lengths, terms, length, log_rate):
     smem = pl.BlockSpec(memory_space=pltpu.SMEM)
+    vmem = pl.BlockSpec(memory_space=pltpu.VMEM)
+    segs, count = len(terms), parents.shape[0]
     return pl.pallas_call(
-        functools.partial(mask_kernel, DEPTH),
-        out_shape=jax.ShapeDtypeStruct((segs, DEPTH * length, length), jnp.float32),
-        in_specs=[smem] * 2,
-        out_specs=pl.BlockSpec(memory_space=pltpu.VMEM),
+        functools.partial(prepare_kernel, log_rate, DEPTH),
+        out_shape=(
+            jax.ShapeDtypeStruct((segs, DEPTH * length, length), jnp.float32),
+            jax.ShapeDtypeStruct((segs, 3, length, HD), jnp.float32),
+            jax.ShapeDtypeStruct((segs, 2, count, HD), jnp.float32),
+        ),
+        in_specs=[smem] * 2 + [vmem] * len(terms),
+        out_specs=(vmem,) * 3,
         cost_estimate=pl.CostEstimate(
-            flops=8 * DEPTH * segs * length * length,
+            flops=20 * DEPTH * segs * length * length,
             bytes_accessed=4 * DEPTH * segs * length * length,
-            transcendentals=0,
+            transcendentals=length * length,
         ),
         compiler_params=SMALL,
-        name="masks",
-    )(parents, lengths)
-
-
-def advantage_kernel(log_rate, depth, segs, parents_s, lengths_s, *refs):
+        name="prepare",
+    )(parents, lengths, *terms)
+
+
+def advantage_kernel(columns_ref, weights_ref, *refs):
     term_refs, (row_ref, adv_ref) = refs[:-2], refs[-2:]
-    length = row_ref.shape[1]
-    count = parents_s.shape[0]
-    own = lax.axis_index("seg")
-
-    seg_col = lax.broadcasted_iota(jnp.int32, (count, 1), 0)
+    segs, _, length, _ = columns_ref.shape
+    count = weights_ref.shape[2]
     if len(term_refs) == 1:
-        deltas, firsts = term_refs[0][:, :length], term_refs[0][:, length:]
+        firsts = read_terms(term_refs[0])[1]
     else:
+        own = lax.axis_index("seg")
         part, pair, pairs = lax.rem(own, segs), own // segs, count // segs
-        deltas = firsts = jnp.zeros((count, length), jnp.float32)
+        seg_id = lax.broadcasted_iota(jnp.int32, (count, length), 0)
+        firsts = jnp.zeros((count, length), jnp.float32)
         for index, ref in enumerate(term_refs):
             step, side = divmod(index, segs)
             seg = lax.rem(pair - step + pairs, pairs) * segs + lax.rem(part + side, segs)
-            tail = ref[ref.shape[0] - TERM_ROWS :, :].astype(jnp.float32)
-            deltas = deltas + jnp.where(seg_col == seg, tail[0:1] + tail[1:2] + tail[2:3], 0.0)
-            firsts = firsts + jnp.where(seg_col == seg, tail[3:4] + tail[4:5] + tail[5:6], 0.0)
-
-    row_id = lax.broadcasted_iota(jnp.int32, (count, count), 0)
-    col_id = lax.broadcasted_iota(jnp.int32, (count, count), 1)
-    eye = row_id == col_id
-
-    def to_row(col):
-        return jnp.sum(jnp.where(eye, col, 0.0), axis=0, keepdims=True)
-
-    parent_row = jnp.full((1, count), -1, jnp.int32)
-    lens_col = jnp.zeros((count, 1), jnp.int32)
-    for seg in range(count):
-        parent_row = jnp.where(col_id[:1] == seg, parents_s[seg], parent_row)
-        lens_col = jnp.where(seg_col == seg, lengths_s[seg], lens_col)
-    lens_col = lens_col.astype(jnp.float32)
-    children = (parent_row == row_id).astype(jnp.float32)
-    weights = children / jnp.maximum(jnp.sum(children, axis=1, keepdims=True), 1.0)
-    first_local, first_value = firsts[:, 0:1], firsts[:, 1:2]
-    later_value = jnp.sum(weights * to_row(first_value), axis=1, keepdims=True)
-    base_term = first_local + jnp.exp((lens_col - 1.0) * log_rate) * later_value
-    factor = jnp.exp(lens_col * log_rate)
-    head = base_term
-    for _ in range(depth):
-        head = base_term + factor * jnp.sum(weights * to_row(head), axis=1, keepdims=True)
-    later_head = jnp.sum(weights * to_row(head), axis=1, keepdims=True)
-
-    t_id = lax.broadcasted_iota(jnp.int32, (length, length), 0)
-    j_id = lax.broadcasted_iota(jnp.int32, (length, length), 1)
-    offset = (j_id - t_id).astype(jnp.float32)
-    discount = jnp.where(offset >= 0, jnp.exp(offset * log_rate), 0.0)
-    t_col = lax.broadcasted_iota(jnp.int32, (length, 1), 0)
+            firsts = jnp.where(seg_id == seg, read_terms(ref)[1], firsts)
     for i in range(segs):
-        seg = segment_of(own, segs, i)
-        seg_len = lengths_s[seg]
-        mine = seg_col == seg
-        my_value = jnp.sum(jnp.where(mine, later_value, 0.0), axis=0, keepdims=True)
-        my_head = jnp.sum(jnp.where(mine, later_head, 0.0), axis=0, keepdims=True)
-        my_deltas = jnp.sum(jnp.where(mine, deltas, 0.0), axis=0, keepdims=True)
-        local_sum = jnp.sum(discount * my_deltas, axis=1, keepdims=True)
-        left = (seg_len - t_col).astype(jnp.float32)
-        advantage = jnp.where(
-            t_col < seg_len,
-            local_sum
-            + jnp.exp((left - 1.0) * log_rate) * my_value
-            + jnp.exp(left * log_rate) * my_head,
-            0.0,
+        later_value = jnp.sum(weights_ref[i, 0] * firsts, axis=(0, 1), keepdims=True)
+        later_head = jnp.sum(weights_ref[i, 1] * firsts, axis=(0, 1), keepdims=True)
+        advantage = (
+            columns_ref[i, 0] + columns_ref[i, 1] * later_value + columns_ref[i, 2] * later_head
         )
+        adv_ref[i] = advantage
         if i == 0:
-            row_ref[...] = jnp.sum(jnp.where(t_id == j_id, advantage, 0.0), axis=0, keepdims=True)
-        adv_ref[i] = jnp.broadcast_to(advantage, (length, HD))
-
-
-def advantages_of(parents, lengths, terms, length, segs, log_rate):
-    smem = pl.BlockSpec(memory_space=pltpu.SMEM)
+            row_id = lax.broadcasted_iota(jnp.int32, advantage.shape, 0)
+            col_id = lax.broadcasted_iota(jnp.int32, advantage.shape, 1)
+            row_ref[...] = jnp.sum(
+                jnp.where(row_id == col_id, advantage, 0.0), axis=0, keepdims=True
+            )
+
+
+def advantages_of(columns, weights, terms):
     vmem = pl.BlockSpec(memory_space=pltpu.VMEM)
+    segs, _, length, _ = columns.shape
     return pl.pallas_call(
-        functools.partial(advantage_kernel, log_rate, DEPTH, segs),
+        advantage_kernel,
         out_shape=(
             jax.ShapeDtypeStruct((1, length), jnp.float32),
             jax.ShapeDtypeStruct((segs, length, HD), jnp.float32),
         ),
-        in_specs=[smem] * 2 + [vmem] * len(terms),
+        in_specs=[vmem] * (2 + len(terms)),
         out_specs=(vmem,) * 2,
         cost_estimate=pl.CostEstimate(
-            flops=200 * length * length,
-            bytes_accessed=8 * segs * length * length,
-            transcendentals=length * length,
+            flops=10 * segs * length * HD, bytes_accessed=16 * segs * length * HD, transcendentals=0
         ),
         compiler_params=SMALL,
         name="advantages",
-    )(parents, lengths, *terms)
+    )(columns, weights, *terms)
 
 
 def attend_kernel(depth, chunk, segs, sources, group_size, *refs):
@@ -471,22 +479,26 @@
     length = queries.shape[0]
     chunks = key_vectors.shape[1] // HD // 2
     swap = [(i, i ^ 1) for i in range(groups)]
+    climb = [(i, (i + 2) % groups) for i in range(groups)]
     steps = range(1, groups // 2)
-    up = {d: [(i, (i + 2 * d) % groups) for i in range(groups)] for d in steps}
     down = {d: [(i, (i - 2 * d) % groups) for i in range(groups)] for d in steps}
 
     kept, given = pack(lengths, key_vectors, value_vectors, token_rows, 2, log_rate)
     taken = permute(given, swap)
-    kept_far = [permute(kept, up[d]) for d in steps]
+    chain = [kept, permute(kept, climb)]
+    other = [after(taken, chain[1])]
     kept_q, given_q = pack_queries(after(queries, kept), direction, 2, chunks)
-    bias = masks(parents, lengths, length, 2)
-    gated, *given_q = lax.optimization_barrier((taken, *given_q, *kept_far, bias))[: 1 + chunks]
-    taken_q = [permute(block, swap) for block in given_q]
-    taken_far = [permute(gated, up[d]) for d in steps]
-    blocks = [kept, taken]
-    for pair in zip(kept_far, taken_far):
-        blocks += pair
-    row, advantages = advantages_of(parents, lengths, blocks, length, 2, log_rate)
+    taken_q = [permute(after(given_q[0], *other), swap)]
+    bias, columns, weights = prepare(parents, lengths, [kept, other[0]], length, log_rate)
+    for step in steps:
+        if step + 1 in steps:
+            chain.append(permute(chain[-1], climb))
+        gate = [bias, taken_q[0]] if step == 1 else []
+        other.append(after(permute(other[-1], climb), chain[-1], *gate))
+    for block in given_q[1:]:
+        taken_q.append(permute(after(block, taken_q[-1]), swap))
+    blocks = [block for pair in zip(chain, other) for block in pair]
+    row, advantages = advantages_of(columns, weights, blocks)
 
     dq_own, dq_back, dkv_list = [], [], []
     for chunk in range(chunks):
@@ -542,9 +554,9 @@
     own = lax.axis_index("seg")
     own_len = lax.dynamic_slice_in_dim(lengths, own, 1)[0]
     terms = jnp.concatenate(token_terms(log_rate, own_len, *token_rows), axis=1)
+    bias, columns, weights = prepare(parents, lengths, [terms], length, log_rate)
     terms = lax.all_gather(terms, "seg", axis=0, tiled=True)
-    row, advantages = advantages_of(parents, lengths, [terms], length, 1, log_rate)
-    bias = masks(parents, lengths, length, 1)
+    row, advantages = advantages_of(columns, weights, [terms])
     flat = jnp.concatenate([key_vectors, value_vectors], axis=1)[None]
     spread = lax.all_to_all(flat, "seg", split_axis=1, concat_axis=0, tiled=True)
     chains = ancestors(parents, DEPTH - 1)

time: 70.8 us -> 66.3 us (0.936)
  starting transfers between devices: 30.8 us -> 21.1 us
  waiting for transfers between devices: 20.3 us -> 27.3 us
  Pallas kernels: 16.1 us -> 14.6 us
    ppermute x19, starting transfers between devices: 30.8 us -> 21.1 us  [permute(): return lax.ppermute(array, 'seg', pairs)]
    ppermute x19, waiting for transfers between devices: 20.3 us -> 27.3 us  [permute(): return lax.ppermute(array, 'seg', pairs)]
    pallas_call x2, Pallas kernels: 2.82 us -> 1.93 us  [the longest x1 1.23 us: prepare(): pl.pallas_call(functools.partial(prepare_kernel, log_rate, DEPTH), out_sh...]
  transfers between devices with their start and end apart: 19 -> 19, of which waited for: 8 -> 9; matrix products, arithmetic and copies ran while one was open for 0% -> 0% of each run, Pallas kernels for 18% -> 18%
where the time goes in v7:
time: 66.3 us; the launch traced here: 66.1 us
  waiting for transfers between devices  27.3 us (41%)
  starting transfers between devices  21.1 us (32%)
  Pallas kernels  14.6 us (22%)
  local copies, waits for them, and re-layouts  2.19 us (3%)
  between operations  0.72 us (1%)
    ppermute x19, waiting for transfers between devices, permute(): return lax.ppermute(array, 'seg', pairs)  27.3 us
    ppermute x19, starting transfers between devices, permute(): return lax.ppermute(array, 'seg', pairs)  21.1 us
    pallas_call x2, Pallas kernels, attend(): pl.pallas_call(functools.partial(attend_kernel, DEPTH, chunk, segs, sourc...  8.93 us
    unnamed x10, local copies, waits for them, and re-layouts  2.19 us
    pallas_call x1, Pallas kernels, pack(): pl.pallas_call(functools.partial(pack_kernel, log_rate), out_shape=(block...  1.86 us
  transfers between devices with their start and end apart: 19, of which 9 were waited for; matrix products, arithmetic and copies ran while one was open for 0% of the time, Pallas kernels for 18%

profile of v7, /device:TPU:0, one launch (start us, length us, event | category | flops | bytes accessed | tf_op | source)
XLA Modules:
  0.0 66.1 jit_solution(11247666886367799888)
XLA Ops:
  0.6 1.9 %pack_keys_values.1 = (bf16[528,128]{1,0:T(8,128)(2,1)}, bf16[528,128]{1,0:T(8,128)(2,1)}) custom-call(s32[8]{0:T(128)} %lengths_s.1, bf16[128,512]{1,0:T(8,128)(2,1)} %k_ref.1, bf16[128,512]{1,0:T(8,128)(2,1)} %v_ref.1, f32[1,128]{1,0:T(1,128)} %bitcast.9, f32[1,128]{1,0:T(1,128)} %bitcast.10, f32[1,128]{1,0:T(1,128)} %bitcast.11, f32[1,128]{1,0:T(1,128)} %bitcast.12), custom_call_target="tpu_custom_call" | custom-call | flops 12800 | bytes 524288 | tf_op jit(solution)/shard_map/pack_keys_values/pallas_call | solution.py:101
  2.5 2.9 %collective-permute-start = (bf16[528,128]{1,0:T(8,128)(2,1)}, bf16[528,128]{1,0:T(8,128)(2,1)S(1)}, u32[]{:S(2)}, u32[]{:S(2)}) collective-permute-start(bf16[528,128]{1,0:T(8,128)(2,1)} %get-tuple-element.39), channel_id=1, source_target_pairs={{0,2},{2,0},{4,6},{6,4},{8,10},{10,8},{12,14},{14,12},{1,3},{3,1},... | collective-permute-start | bytes 405512 | tf_op jit(solution)/shard_map/ppermute | solution.py:470
  5.4 1.6 %collective-permute-start.1 = (bf16[528,128]{1,0:T(8,128)(2,1)}, bf16[528,128]{1,0:T(8,128)(2,1)S(1)}, u32[]{:S(2)}, u32[]{:S(2)}) collective-permute-start(bf16[528,128]{1,0:T(8,128)(2,1)} %get-tuple-element.38.refs_0_.refs_5_), channel_id=1, source_target_pairs={{0,4},{2,6},{4,8},{6,10},{8,12},{10,14},{12,0},{14,2},{1,5},{3,7},... | collective-permute-start | bytes 405512 | tf_op jit(solution)/shard_map/ppermute | solution.py:470
  7.0 0.0 copy-start
  7.0 1.1 %copy-done = bf16[128,2560]{1,0:T(8,128)(2,1)S(1)} copy-done((bf16[128,2560]{1,0:T(8,128)(2,1)S(1)}, bf16[128,2560]{1,0:T(8,128)(2,1)}, u32[]{:S(2)}) %copy-start) | copy-done | bytes 655384
  8.1 0.0 copy-start.1
  8.1 1.1 %copy-done.1 = bf16[128,2560]{1,0:T(8,128)(2,1)S(1)} copy-done((bf16[128,2560]{1,0:T(8,128)(2,1)S(1)}, bf16[128,2560]{1,0:T(8,128)(2,1)}, u32[]{:S(2)}) %copy-start.1) | copy-done | bytes 655384
  9.2 0.0 copy-start.2
  9.2 0.2 pack_queries.1
  9.4 0.0 copy-start.3
  9.4 0.0 copy-start.4
  9.4 0.0 collective-permute-done.refs_1_.refs_6_
  9.5 3.1 %collective-permute-done.1.refs_2_.refs_7_ = bf16[528,128]{1,0:T(8,128)(2,1)S(1)} collective-permute-done((bf16[528,128]{1,0:T(8,128)(2,1)}, bf16[528,128]{1,0:T(8,128)(2,1)S(1)}, u32[]{:S(2)}, u32[]{:S(2)}) %collective-permute-start.1) | collective-permute-done | bytes 135200 | tf_op jit(solution)/shard_map/ppermute | solution.py:470
  12.5 0.5 collective-permute-start.4
  13.1 0.0 collective-permute-start.3
  13.1 1.3 %collective-permute-start.2 = (bf16[528,128]{1,0:T(8,128)(2,1)S(1)}, bf16[528,128]{1,0:T(8,128)(2,1)S(1)}, u32[]{:S(2)}, u32[]{:S(2)}) collective-permute-start(bf16[528,128]{1,0:T(8,128)(2,1)S(1)} %collective-permute-done.refs_1_.refs_6_), channel_id=1, source_target_pairs={{0,4},{2,6},{4,8},{6,10},{8,12},{10,14},{12,0},{14,2},{1,5},{3,7},... | collective-permute-start | bytes 405512 | tf_op jit(solution)/shard_map/ppermute | solution.py:470
  14.4 0.0 copy-done.2
  14.4 0.0 copy-done.3
  14.4 0.0 copy-done.4
  14.4 1.2 %prepare.1 = (f32[2,640,128]{2,1,0:T(8,128)S(1)}, f32[2,3,128,128]{3,2,1,0:T(8,128)S(1)}, f32[2,2,8,128]{3,2,1,0:T(8,128)S(1)}) custom-call(s32[8]{0:T(128)S(1)} %copy-done.4, s32[8]{0:T(128)S(1)} %copy-done.3, bf16[528,128]{1,0:T(8,128)(2,1)S(1)} %copy-done.2, bf16[528,128]{1,0:T(8,128)(2,1)S(1)} %collective-permute-done.refs_1_.refs_6_), custom_call_target="tpu_custom_call" | custom-call | flops 3276800 | bytes 655360 | tf_op jit(solution)/shard_map/prepare/pallas_call | solution.py:230
  15.6 4.9 %collective-permute-done.3.refs_4_.refs_9_ = bf16[528,128]{1,0:T(8,128)(2,1)S(1)} collective-permute-done((bf16[528,128]{1,0:T(8,128)(2,1)S(1)}, bf16[528,128]{1,0:T(8,128)(2,1)S(1)}, u32[]{:S(2)}, u32[]{:S(2)}) %collective-permute-start.3) | collective-permute-done | bytes 135200 | tf_op jit(solution)/shard_map/ppermute | solution.py:470
  20.5 0.0 collective-permute-start.6
  20.5 1.5 %collective-permute-done.2.refs_3_.refs_8_ = bf16[528,128]{1,0:T(8,128)(2,1)S(1)} collective-permute-done((bf16[528,128]{1,0:T(8,128)(2,1)S(1)}, bf16[528,128]{1,0:T(8,128)(2,1)S(1)}, u32[]{:S(2)}, u32[]{:S(2)}) %collective-permute-start.2) | collective-permute-done | bytes 135200 | tf_op jit(solution)/shard_map/ppermute | solution.py:470
  22.0 0.0 collective-permute-done.4.refs_4_
  22.0 0.0 collective-permute-start.5
  22.0 1.2 %collective-permute-start.8 = (bf16[2,5,128,128]{3,2,1,0:T(8,128)(2,1)S(1)}, bf16[2,5,128,128]{3,2,1,0:T(8,128)(2,1)S(1)}, u32[]{:S(2)}, u32[]{:S(2)}) collective-permute-start(bf16[2,5,128,128]{3,2,1,0:T(8,128)(2,1)S(1)} %get-tuple-element.55), channel_id=1, source_target_pairs={{0,2},{2,0},{4,6},{6,4},{8,10},{10,8},{12,14},{14,12},{1,3},{3,1},... | collective-permute-start | bytes 983048 | tf_op jit(solution)/shard_map/ppermute | solution.py:470
  23.3 4.0 %collective-permute-done.6.refs_6_.refs_11_ = bf16[528,128]{1,0:T(8,128)(2,1)S(1)} collective-permute-done((bf16[528,128]{1,0:T(8,128)(2,1)S(1)}, bf16[528,128]{1,0:T(8,128)(2,1)S(1)}, u32[]{:S(2)}, u32[]{:S(2)}) %collective-permute-start.6) | collective-permute-done | bytes 135200 | tf_op jit(solution)/shard_map/ppermute | solution.py:470
  27.3 1.5 %collective-permute-done.5.refs_5_.refs_10_ = bf16[528,128]{1,0:T(8,128)(2,1)S(1)} collective-permute-done((bf16[528,128]{1,0:T(8,128)(2,1)S(1)}, bf16[528,128]{1,0:T(8,128)(2,1)S(1)}, u32[]{:S(2)}, u32[]{:S(2)}) %collective-permute-start.5) | collective-permute-done | bytes 135200 | tf_op jit(solution)/shard_map/ppermute | solution.py:470
  28.8 0.0 collective-permute-start.7
  28.8 6.8 %collective-permute-done.7.refs_7_.refs_12_ = bf16[528,128]{1,0:T(8,128)(2,1)S(1)} collective-permute-done((bf16[528,128]{1,0:T(8,128)(2,1)S(1)}, bf16[528,128]{1,0:T(8,128)(2,1)S(1)}, u32[]{:S(2)}, u32[]{:S(2)}) %collective-permute-start.7) | collective-permute-done | bytes 135200 | tf_op jit(solution)/shard_map/ppermute | solution.py:470
  35.6 0.7 %advantages.1 = (f32[1,128]{1,0:T(1,128)}, f32[2,128,128]{2,1,0:T(8,128)S(1)}) custom-call(f32[2,3,128,128]{3,2,1,0:T(8,128)S(1)} %get-tuple-element.41.columns_ref, f32[2,2,8,128]{3,2,1,0:T(8,128)S(1)} %get-tuple-element.42.weights_ref, bf16[528,128]{1,0:T(8,128)(2,1)S(1)} %copy-done.2, bf16[528,128]{1,0:T(8,128)(2,1)S(1)} %collective-permute-done.refs_1_.refs_6_, ...), custom_call_target="tpu_custom_call" | custom-call | flops 327680 | bytes 524288 | tf_op jit(solution)/shard_map/advantages/pallas_call | solution.py:282
  36.3 4.5 %tree_attention_backward.2 = (bf16[128,640]{1,0:T(8,128)(2,1)S(1)}, bf16[128,640]{1,0:T(8,128)(2,1)S(1)}, bf16[2,2,128,128]{3,2,1,0:T(8,128)(2,1)S(1)}, bf16[2,2...) custom-call(s32[8]{0:T(128)S(1)} %copy-done.4, ...), custom_call_target="tpu_custom_call" | custom-call | flops 1048576000 | bytes 8388608 | tf_op jit(solution)/shard_map/tree_attention_backward/pallas_call | solution.py:384
  40.8 0.1 collective-permute-start.11
  40.9 0.4 collective-permute-start.12
  41.3 3.4 %collective-permute-start.13 = (bf16[2,2,128,128]{3,2,1,0:T(8,128)(2,1)S(1)}, bf16[2,2,128,128]{3,2,1,0:T(8,128)(2,1)S(1)}, u32[]{:S(2)}, u32[]{:S(2)}) collective-permute-start(bf16[2,2,128,128]{3,2,1,0:T(8,128)(2,1)S(1)} %get-tuple-element.63), channel_id=1, source_target_pairs={{0,12},{2,14},{4,0},{6,2},{8,4},{10,6},{12,8},{14,10},{1,13},{3,15... | collective-permute-start | bytes 393224 | tf_op jit(solution)/shard_map/ppermute | solution.py:470
  44.7 1.2 %collective-permute-start.9 = (bf16[128,640]{1,0:T(8,128)(2,1)S(1)}, bf16[128,640]{1,0:T(8,128)(2,1)S(1)}, u32[]{:S(2)}, u32[]{:S(2)}) collective-permute-start(bf16[128,640]{1,0:T(8,128)(2,1)S(1)} %get-tuple-element.57), channel_id=1, source_target_pairs={{0,2},{2,0},{4,6},{6,4},{8,10},{10,8},{12,14},{14,12},{1,3},{3,1},... | collective-permute-start | bytes 491528 | tf_op jit(solution)/shard_map/ppermute | solution.py:470
  45.9 0.0 collective-permute-done.8.refs_4_
  45.9 4.5 %tree_attention_backward.3 = (bf16[128,640]{1,0:T(8,128)(2,1)S(1)}, bf16[128,640]{1,0:T(8,128)(2,1)S(1)}, bf16[2,2,128,128]{3,2,1,0:T(8,128)(2,1)S(1)}, bf16[2,2...) custom-call(s32[8]{0:T(128)S(1)} %copy-done.4, ...), custom_call_target="tpu_custom_call" | custom-call | flops 1048576000 | bytes 8388608 | tf_op jit(solution)/shard_map/tree_attention_backward/pallas_call | solution.py:384
  50.4 0.6 collective-permute-start.15
  51.0 0.0 collective-permute-done.11.refs_3_
  51.0 1.5 %collective-permute-start.16 = (bf16[2,2,128,128]{3,2,1,0:T(8,128)(2,1)S(1)}, bf16[2,2,128,128]{3,2,1,0:T(8,128)(2,1)S(1)}, u32[]{:S(2)}, u32[]{:S(2)}) collective-permute-start(bf16[2,2,128,128]{3,2,1,0:T(8,128)(2,1)S(1)} %get-tuple-element.67), channel_id=1, source_target_pairs={{0,8},{2,10},{4,12},{6,14},{8,0},{10,2},{12,4},{14,6},{1,9},{3,11}... | collective-permute-start | bytes 393224 | tf_op jit(solution)/shard_map/ppermute | solution.py:470
  52.6 0.0 collective-permute-done.12.refs_4_
  52.6 3.1 %collective-permute-start.17 = (bf16[2,2,128,128]{3,2,1,0:T(8,128)(2,1)S(1)}, bf16[2,2,128,128]{3,2,1,0:T(8,128)(2,1)S(1)}, u32[]{:S(2)}, u32[]{:S(2)}) collective-permute-start(bf16[2,2,128,128]{3,2,1,0:T(8,128)(2,1)S(1)} %get-tuple-element.68), channel_id=1, source_target_pairs={{0,12},{2,14},{4,0},{6,2},{8,4},{10,6},{12,8},{14,10},{1,13},{3,15... | collective-permute-start | bytes 393224 | tf_op jit(solution)/shard_map/ppermute | solution.py:470
  55.7 0.0 collective-permute-done.13.refs_5_
  55.7 1.1 %collective-permute-start.10 = (bf16[128,640]{1,0:T(8,128)(2,1)S(1)}, bf16[128,640]{1,0:T(8,128)(2,1)S(1)}, u32[]{:S(2)}, u32[]{:S(2)}) collective-permute-start(bf16[128,640]{1,0:T(8,128)(2,1)S(1)} %get-tuple-element.58), channel_id=1, source_target_pairs={{0,2},{2,0},{4,6},{6,4},{8,10},{10,8},{12,14},{14,12},{1,3},{3,1},... | collective-permute-start | bytes 491528 | tf_op jit(solution)/shard_map/ppermute | solution.py:470
  56.8 0.6 collective-permute-done.15.refs_7_
  57.4 0.8 %collective-permute-start.14 = (bf16[2,128,128]{2,1,0:T(8,128)(2,1)S(1)}, bf16[2,128,128]{2,1,0:T(8,128)(2,1)S(1)}, u32[]{:S(2)}, u32[]{:S(2)}) collective-permute-start(bf16[2,128,128]{2,1,0:T(8,128)(2,1)S(1)} %fusion), channel_id=1, source_target_pairs={{0,2},{2,0},{4,6},{6,4},{8,10},{10,8},{12,14},{14,12},{1,3},{3,1},... | collective-permute-start | bytes 196616 | tf_op jit(solution)/shard_map/ppermute | solution.py:470
  58.2 2.7 %collective-permute-done.16.refs_8_ = bf16[2,2,128,128]{3,2,1,0:T(8,128)(2,1)S(1)} collective-permute-done((bf16[2,2,128,128]{3,2,1,0:T(8,128)(2,1)S(1)}, bf16[2,2,128,128]{3,2,1,0:T(8,128)(2,1)S(1)}, u32[]{:S(2)}, u32[]{:S(2)}) %collective-permute-start.16) | collective-permute-done | bytes 131104 | tf_op jit(solution)/shard_map/ppermute | solution.py:470
  60.9 0.0 collective-permute-done.17.refs_9_
  61.0 1.3 %collective-permute-start.18 = (bf16[2,128,128]{2,1,0:T(8,128)(2,1)S(1)}, bf16[2,128,128]{2,1,0:T(8,128)(2,1)S(1)}, u32[]{:S(2)}, u32[]{:S(2)}) collective-permute-start(bf16[2,128,128]{2,1,0:T(8,128)(2,1)S(1)} %fusion.1), channel_id=1, source_target_pairs={{0,2},{2,0},{4,6},{6,4},{8,10},{10,8},{12,14},{14,12},{1,3},{3,1},... | collective-permute-start | bytes 196616 | tf_op jit(solution)/shard_map/ppermute | solution.py:470
  62.2 0.0 collective-permute-done.9.refs_2_
  62.2 0.0 collective-permute-done.10.refs_3_
  62.2 0.9 %join_queries.1 = bf16[128,2560]{1,0:T(8,128)(2,1)} custom-call(bf16[128,640]{1,0:T(8,128)(2,1)S(1)} %get-tuple-element.52.refs_0_, bf16[128,640]{1,0:T(8,128)(2,1)S(1)} %get-tuple-element.56.refs_1_, bf16[128,640]{1,0:T(8,128)(2,1)S(1)} %collective-permute-done.9.refs_2_, bf16[128,640]{1,0:T(8,128)(2,1)S(1)} %collective-permute-done.10.refs_3_), custom_call_target="tpu_custom_call" | custom-call | bytes 1310720 | tf_op jit(solution)/shard_map/join_queries/pallas_call | solution.py:422
  63.2 0.0 collective-permute-done.14.refs_0_
  63.2 2.1 %collective-permute-done.18.refs_1_ = bf16[2,128,128]{2,1,0:T(8,128)(2,1)S(1)} collective-permute-done((bf16[2,128,128]{2,1,0:T(8,128)(2,1)S(1)}, bf16[2,128,128]{2,1,0:T(8,128)(2,1)S(1)}, u32[]{:S(2)}, u32[]{:S(2)}) %collective-permute-start.18) | collective-permute-done | bytes 65568 | tf_op jit(solution)/shard_map/ppermute | solution.py:470
  65.3 0.8 %join_keys.1 = (bf16[128,512]{1,0:T(8,128)(2,1)}, bf16[128,512]{1,0:T(8,128)(2,1)}) custom-call(bf16[2,128,128]{2,1,0:T(8,128)(2,1)S(1)} %collective-permute-done.14.refs_0_, bf16[2,128,128]{2,1,0:T(8,128)(2,1)S(1)} %collective-permute-done.18.refs_1_, bf16[2,2,128,128]{3,2,1,0:T(8,128)(2,1)S(1)} %get-tuple-element.60.refs_2_, ...), custom_call_target="tpu_custom_call" | custom-call | bytes 524288 | tf_op jit(solution)/shard_map/join_keys/pallas_call | solution.py:456
  (2 shorter events, 0.1 us)
Async XLA Ops:
  2.5 7.0 %collective-permute-start = (bf16[528,128]{1,0:T(8,128)(2,1)}, bf16[528,128]{1,0:T(8,128)(2,1)S(1)}, u32[]{:S(2)}, u32[]{:S(2)}) collective-permute-start(bf16[528,128]{1,0:T(8,128)(2,1)} %get-tuple-element.39), channel_id=1, source_target_pairs={{0,2},{2,0},{4,6},{6,4},{8,10},{10,8},{12,14},{14,12},{1,3},{3,1},... | collective-permute-start | bytes 405512 | tf_op jit(solution)/shard_map/ppermute | solution.py:470
  5.4 7.1 %collective-permute-start.1 = (bf16[528,128]{1,0:T(8,128)(2,1)}, bf16[528,128]{1,0:T(8,128)(2,1)S(1)}, u32[]{:S(2)}, u32[]{:S(2)}) collective-permute-start(bf16[528,128]{1,0:T(8,128)(2,1)} %get-tuple-element.38.refs_0_.refs_5_), channel_id=1, source_target_pairs={{0,4},{2,6},{4,8},{6,10},{8,12},{10,14},{12,0},{14,2},{1,5},{3,7},... | collective-permute-start | bytes 405512 | tf_op jit(solution)/shard_map/ppermute | solution.py:470
  7.0 1.1 %copy-start = (bf16[128,2560]{1,0:T(8,128)(2,1)S(1)}, bf16[128,2560]{1,0:T(8,128)(2,1)}, u32[]{:S(2)}) copy-start(bf16[128,2560]{1,0:T(8,128)(2,1)} %q_ref) | copy-start | bytes 1966084
  8.1 1.1 %copy-start.1 = (bf16[128,2560]{1,0:T(8,128)(2,1)S(1)}, bf16[128,2560]{1,0:T(8,128)(2,1)}, u32[]{:S(2)}) copy-start(bf16[128,2560]{1,0:T(8,128)(2,1)} %dir_ref.1) | copy-start | bytes 1966084
  9.2 5.2 %copy-start.2 = (bf16[528,128]{1,0:T(8,128)(2,1)S(1)}, bf16[528,128]{1,0:T(8,128)(2,1)}, u32[]{:S(2)}) copy-start(bf16[528,128]{1,0:T(8,128)(2,1)} %get-tuple-element.38.refs_0_.refs_5_) | copy-start | bytes 405508
  9.4 5.0 %copy-start.3 = (s32[8]{0:T(128)S(1)}, s32[8]{0:T(128)}, u32[]{:S(2)}) copy-start(s32[8]{0:T(128)} %lengths_s.1) | copy-start | bytes 100
  9.4 4.9 %copy-start.4 = (s32[8]{0:T(128)S(1)}, s32[8]{0:T(128)}, u32[]{:S(2)}) copy-start(s32[8]{0:T(128)} %refs_0_.3) | copy-start | bytes 100
  12.5 9.5 %collective-permute-start.4 = (bf16[2,5,128,128]{3,2,1,0:T(8,128)(2,1)S(1)}, bf16[2,5,128,128]{3,2,1,0:T(8,128)(2,1)S(1)}, u32[]{:S(2)}, u32[]{:S(2)}) collective-permute-start(bf16[2,5,128,128]{3,2,1,0:T(8,128)(2,1)S(1)} %get-tuple-element.46), channel_id=1, source_target_pairs={{0,2},{2,0},{4,6},{6,4},{8,10},{10,8},{12,14},{14,12},{1,3},{3,1},... | collective-permute-start | bytes 983048 | tf_op jit(solution)/shard_map/ppermute | solution.py:470
  13.1 7.4 %collective-permute-start.3 = (bf16[528,128]{1,0:T(8,128)(2,1)S(1)}, bf16[528,128]{1,0:T(8,128)(2,1)S(1)}, u32[]{:S(2)}, u32[]{:S(2)}) collective-permute-start(bf16[528,128]{1,0:T(8,128)(2,1)S(1)} %collective-permute-done.1.refs_2_.refs_7_), channel_id=1, source_target_pairs={{0,4},{2,6},{4,8},{6,10},{8,12},{10,14},{12,0},{14,2},{1,5},{3,7},... | collective-permute-start | bytes 405512 | tf_op jit(solution)/shard_map/ppermute | solution.py:470
  13.1 8.9 %collective-permute-start.2 = (bf16[528,128]{1,0:T(8,128)(2,1)S(1)}, bf16[528,128]{1,0:T(8,128)(2,1)S(1)}, u32[]{:S(2)}, u32[]{:S(2)}) collective-permute-start(bf16[528,128]{1,0:T(8,128)(2,1)S(1)} %collective-permute-done.refs_1_.refs_6_), channel_id=1, source_target_pairs={{0,4},{2,6},{4,8},{6,10},{8,12},{10,14},{12,0},{14,2},{1,5},{3,7},... | collective-permute-start | bytes 405512 | tf_op jit(solution)/shard_map/ppermute | solution.py:470
  20.5 6.8 %collective-permute-start.6 = (bf16[528,128]{1,0:T(8,128)(2,1)S(1)}, bf16[528,128]{1,0:T(8,128)(2,1)S(1)}, u32[]{:S(2)}, u32[]{:S(2)}) collective-permute-start(bf16[528,128]{1,0:T(8,128)(2,1)S(1)} %collective-permute-done.3.refs_4_.refs_9_), channel_id=1, source_target_pairs={{0,4},{2,6},{4,8},{6,10},{8,12},{10,14},{12,0},{14,2},{1,5},{3,7},... | collective-permute-start | bytes 405512 | tf_op jit(solution)/shard_map/ppermute | solution.py:470
  22.0 6.8 %collective-permute-start.5 = (bf16[528,128]{1,0:T(8,128)(2,1)S(1)}, bf16[528,128]{1,0:T(8,128)(2,1)S(1)}, u32[]{:S(2)}, u32[]{:S(2)}) collective-permute-start(bf16[528,128]{1,0:T(8,128)(2,1)S(1)} %collective-permute-done.2.refs_3_.refs_8_), channel_id=1, source_target_pairs={{0,4},{2,6},{4,8},{6,10},{8,12},{10,14},{12,0},{14,2},{1,5},{3,7},... | collective-permute-start | bytes 405512 | tf_op jit(solution)/shard_map/ppermute | solution.py:470
  22.0 23.9 %collective-permute-start.8 = (bf16[2,5,128,128]{3,2,1,0:T(8,128)(2,1)S(1)}, bf16[2,5,128,128]{3,2,1,0:T(8,128)(2,1)S(1)}, u32[]{:S(2)}, u32[]{:S(2)}) collective-permute-start(bf16[2,5,128,128]{3,2,1,0:T(8,128)(2,1)S(1)} %get-tuple-element.55), channel_id=1, source_target_pairs={{0,2},{2,0},{4,6},{6,4},{8,10},{10,8},{12,14},{14,12},{1,3},{3,1},... | collective-permute-start | bytes 983048 | tf_op jit(solution)/shard_map/ppermute | solution.py:470
  28.8 6.8 %collective-permute-start.7 = (bf16[528,128]{1,0:T(8,128)(2,1)S(1)}, bf16[528,128]{1,0:T(8,128)(2,1)S(1)}, u32[]{:S(2)}, u32[]{:S(2)}) collective-permute-start(bf16[528,128]{1,0:T(8,128)(2,1)S(1)} %collective-permute-done.5.refs_5_.refs_10_), channel_id=1, source_target_pairs={{0,4},{2,6},{4,8},{6,10},{8,12},{10,14},{12,0},{14,2},{1,5},{3,7},... | collective-permute-start | bytes 405512 | tf_op jit(solution)/shard_map/ppermute | solution.py:470
  40.8 10.2 %collective-permute-start.11 = (bf16[2,2,128,128]{3,2,1,0:T(8,128)(2,1)S(1)}, bf16[2,2,128,128]{3,2,1,0:T(8,128)(2,1)S(1)}, u32[]{:S(2)}, u32[]{:S(2)}) collective-permute-start(bf16[2,2,128,128]{3,2,1,0:T(8,128)(2,1)S(1)} %get-tuple-element.61), channel_id=1, source_target_pairs={{0,4},{2,6},{4,8},{6,10},{8,12},{10,14},{12,0},{14,2},{1,5},{3,7},... | collective-permute-start | bytes 393224 | tf_op jit(solution)/shard_map/ppermute | solution.py:470
  40.9 11.7 %collective-permute-start.12 = (bf16[2,2,128,128]{3,2,1,0:T(8,128)(2,1)S(1)}, bf16[2,2,128,128]{3,2,1,0:T(8,128)(2,1)S(1)}, u32[]{:S(2)}, u32[]{:S(2)}) collective-permute-start(bf16[2,2,128,128]{3,2,1,0:T(8,128)(2,1)S(1)} %get-tuple-element.62), channel_id=1, source_target_pairs={{0,8},{2,10},{4,12},{6,14},{8,0},{10,2},{12,4},{14,6},{1,9},{3,11}... | collective-permute-start | bytes 393224 | tf_op jit(solution)/shard_map/ppermute | solution.py:470
  41.3 14.4 %collective-permute-start.13 = (bf16[2,2,128,128]{3,2,1,0:T(8,128)(2,1)S(1)}, bf16[2,2,128,128]{3,2,1,0:T(8,128)(2,1)S(1)}, u32[]{:S(2)}, u32[]{:S(2)}) collective-permute-start(bf16[2,2,128,128]{3,2,1,0:T(8,128)(2,1)S(1)} %get-tuple-element.63), channel_id=1, source_target_pairs={{0,12},{2,14},{4,0},{6,2},{8,4},{10,6},{12,8},{14,10},{1,13},{3,15... | collective-permute-start | bytes 393224 | tf_op jit(solution)/shard_map/ppermute | solution.py:470
  44.7 17.6 %collective-permute-start.9 = (bf16[128,640]{1,0:T(8,128)(2,1)S(1)}, bf16[128,640]{1,0:T(8,128)(2,1)S(1)}, u32[]{:S(2)}, u32[]{:S(2)}) collective-permute-start(bf16[128,640]{1,0:T(8,128)(2,1)S(1)} %get-tuple-element.57), channel_id=1, source_target_pairs={{0,2},{2,0},{4,6},{6,4},{8,10},{10,8},{12,14},{14,12},{1,3},{3,1},... | collective-permute-start | bytes 491528 | tf_op jit(solution)/shard_map/ppermute | solution.py:470
  50.4 7.0 %collective-permute-start.15 = (bf16[2,2,128,128]{3,2,1,0:T(8,128)(2,1)S(1)}, bf16[2,2,128,128]{3,2,1,0:T(8,128)(2,1)S(1)}, u32[]{:S(2)}, u32[]{:S(2)}) collective-permute-start(bf16[2,2,128,128]{3,2,1,0:T(8,128)(2,1)S(1)} %get-tuple-element.66), channel_id=1, source_target_pairs={{0,4},{2,6},{4,8},{6,10},{8,12},{10,14},{12,0},{14,2},{1,5},{3,7},... | collective-permute-start | bytes 393224 | tf_op jit(solution)/shard_map/ppermute | solution.py:470
  51.0 9.9 %collective-permute-start.16 = (bf16[2,2,128,128]{3,2,1,0:T(8,128)(2,1)S(1)}, bf16[2,2,128,128]{3,2,1,0:T(8,128)(2,1)S(1)}, u32[]{:S(2)}, u32[]{:S(2)}) collective-permute-start(bf16[2,2,128,128]{3,2,1,0:T(8,128)(2,1)S(1)} %get-tuple-element.67), channel_id=1, source_target_pairs={{0,8},{2,10},{4,12},{6,14},{8,0},{10,2},{12,4},{14,6},{1,9},{3,11}... | collective-permute-start | bytes 393224 | tf_op jit(solution)/shard_map/ppermute | solution.py:470
  52.6 8.3 %collective-permute-start.17 = (bf16[2,2,128,128]{3,2,1,0:T(8,128)(2,1)S(1)}, bf16[2,2,128,128]{3,2,1,0:T(8,128)(2,1)S(1)}, u32[]{:S(2)}, u32[]{:S(2)}) collective-permute-start(bf16[2,2,128,128]{3,2,1,0:T(8,128)(2,1)S(1)} %get-tuple-element.68), channel_id=1, source_target_pairs={{0,12},{2,14},{4,0},{6,2},{8,4},{10,6},{12,8},{14,10},{1,13},{3,15... | collective-permute-start | bytes 393224 | tf_op jit(solution)/shard_map/ppermute | solution.py:470
  55.7 6.6 %collective-permute-start.10 = (bf16[128,640]{1,0:T(8,128)(2,1)S(1)}, bf16[128,640]{1,0:T(8,128)(2,1)S(1)}, u32[]{:S(2)}, u32[]{:S(2)}) collective-permute-start(bf16[128,640]{1,0:T(8,128)(2,1)S(1)} %get-tuple-element.58), channel_id=1, source_target_pairs={{0,2},{2,0},{4,6},{6,4},{8,10},{10,8},{12,14},{14,12},{1,3},{3,1},... | collective-permute-start | bytes 491528 | tf_op jit(solution)/shard_map/ppermute | solution.py:470
  57.4 5.7 %collective-permute-start.14 = (bf16[2,128,128]{2,1,0:T(8,128)(2,1)S(1)}, bf16[2,128,128]{2,1,0:T(8,128)(2,1)S(1)}, u32[]{:S(2)}, u32[]{:S(2)}) collective-permute-start(bf16[2,128,128]{2,1,0:T(8,128)(2,1)S(1)} %fusion), channel_id=1, source_target_pairs={{0,2},{2,0},{4,6},{6,4},{8,10},{10,8},{12,14},{14,12},{1,3},{3,1},... | collective-permute-start | bytes 196616 | tf_op jit(solution)/shard_map/ppermute | solution.py:470
  61.0 4.3 %collective-permute-start.18 = (bf16[2,128,128]{2,1,0:T(8,128)(2,1)S(1)}, bf16[2,128,128]{2,1,0:T(8,128)(2,1)S(1)}, u32[]{:S(2)}, u32[]{:S(2)}) collective-permute-start(bf16[2,128,128]{2,1,0:T(8,128)(2,1)S(1)} %fusion.1), channel_id=1, source_target_pairs={{0,2},{2,0},{4,6},{6,4},{8,10},{10,8},{12,14},{14,12},{1,3},{3,1},... | collective-permute-start | bytes 196616 | tf_op jit(solution)/shard_map/ppermute | solution.py:470

commit v8 on v7

--- a/solution.py
+++ b/solution.py
@@ -159,10 +159,11 @@
 
 
 def prepare_kernel(log_rate, depth, parents_s, lengths_s, *refs):
-    term_refs, (bias_ref, columns_ref, weights_ref) = refs[:-3], refs[-3:]
+    term_refs, (bias_ref, columns_ref, weights_ref, firsts_ref) = refs[:-4], refs[-4:]
     segs, _, length = bias_ref.shape
     count = parents_s.shape[0]
     own = lax.axis_index("seg")
+    firsts_ref[...] = jnp.zeros_like(firsts_ref)
 
     row_id = lax.broadcasted_iota(jnp.int32, (count, count), 0)
     col_id = lax.broadcasted_iota(jnp.int32, (count, count), 1)
@@ -191,7 +192,8 @@
     for i in range(segs):
         seg = segment_of(own, segs, i)
         seg_len = lengths_s[seg]
-        deltas, _ = read_terms(term_refs[i])
+        deltas, firsts = read_terms(term_refs[i])
+        firsts_ref[...] += jnp.where(seg_col == seg, firsts, 0.0)
         live = t_col < seg_len
         left = (seg_len - t_col).astype(jnp.float32)
         columns = (
@@ -233,9 +235,10 @@
             jax.ShapeDtypeStruct((segs, DEPTH * length, length), jnp.float32),
             jax.ShapeDtypeStruct((segs, 3, length, HD), jnp.float32),
             jax.ShapeDtypeStruct((segs, 2, count, HD), jnp.float32),
+            jax.ShapeDtypeStruct((count, length), jnp.float32),
         ),
         in_specs=[smem] * 2 + [vmem] * len(terms),
-        out_specs=(vmem,) * 3,
+        out_specs=(vmem,) * 4,
         cost_estimate=pl.CostEstimate(
             flops=20 * DEPTH * segs * length * length,
             bytes_accessed=4 * DEPTH * segs * length * length,
@@ -246,22 +249,9 @@
     )(parents, lengths, *terms)
 
 
-def advantage_kernel(columns_ref, weights_ref, *refs):
-    term_refs, (row_ref, adv_ref) = refs[:-2], refs[-2:]
-    segs, _, length, _ = columns_ref.shape
-    count = weights_ref.shape[2]
-    if len(term_refs) == 1:
-        firsts = read_terms(term_refs[0])[1]
-    else:
-        own = lax.axis_index("seg")
-        part, pair, pairs = lax.rem(own, segs), own // segs, count // segs
-        seg_id = lax.broadcasted_iota(jnp.int32, (count, length), 0)
-        firsts = jnp.zeros((count, length), jnp.float32)
-        for index, ref in enumerate(term_refs):
-            step, side = divmod(index, segs)
-            seg = lax.rem(pair - step + pairs, pairs) * segs + lax.rem(part + side, segs)
-            firsts = jnp.where(seg_id == seg, read_terms(ref)[1], firsts)
-    for i in range(segs):
+def advantage_kernel(columns_ref, weights_ref, near_ref, far_ref, row_ref, adv_ref):
+    firsts = near_ref[...] + far_ref[...]
+    for i in range(columns_ref.shape[0]):
         later_value = jnp.sum(weights_ref[i, 0] * firsts, axis=(0, 1), keepdims=True)
         later_head = jnp.sum(weights_ref[i, 1] * firsts, axis=(0, 1), keepdims=True)
         advantage = (
@@ -276,7 +266,7 @@
             )
 
 
-def advantages_of(columns, weights, terms):
+def advantages_of(columns, weights, near, far):
     vmem = pl.BlockSpec(memory_space=pltpu.VMEM)
     segs, _, length, _ = columns.shape
     return pl.pallas_call(
@@ -285,14 +275,14 @@
             jax.ShapeDtypeStruct((1, length), jnp.float32),
             jax.ShapeDtypeStruct((segs, length, HD), jnp.float32),
         ),
-        in_specs=[vmem] * (2 + len(terms)),
+        in_specs=[vmem] * 4,
         out_specs=(vmem,) * 2,
         cost_estimate=pl.CostEstimate(
             flops=10 * segs * length * HD, bytes_accessed=16 * segs * length * HD, transcendentals=0
         ),
         compiler_params=SMALL,
         name="advantages",
-    )(columns, weights, *terms)
+    )(columns, weights, near, far)
 
 
 def attend_kernel(depth, chunk, segs, sources, group_size, *refs):
@@ -478,27 +468,30 @@
     groups = lax.axis_size("seg")
     length = queries.shape[0]
     chunks = key_vectors.shape[1] // HD // 2
+    steps = range(1, groups // 2)
     swap = [(i, i ^ 1) for i in range(groups)]
-    climb = [(i, (i + 2) % groups) for i in range(groups)]
-    steps = range(1, groups // 2)
-    down = {d: [(i, (i - 2 * d) % groups) for i in range(groups)] for d in steps}
+    down = {d: [(i, i - 2 * d) for i in range(2 * d, groups)] for d in steps}
+
+    def climb(block, step):
+        return permute(block, [(i, i + 2) for i in range(2 * step - 2, groups - 2)])
 
     kept, given = pack(lengths, key_vectors, value_vectors, token_rows, 2, log_rate)
     taken = permute(given, swap)
-    chain = [kept, permute(kept, climb)]
+    chain = [kept, climb(kept, 1)]
     other = [after(taken, chain[1])]
     kept_q, given_q = pack_queries(after(queries, kept), direction, 2, chunks)
+    bias, columns, weights, firsts = prepare(parents, lengths, [kept, taken], length, log_rate)
+    firsts = firsts + permute(firsts, down[1])
+    row, advantages = advantages_of(columns, weights, firsts, permute(firsts, down[2]))
     taken_q = [permute(after(given_q[0], *other), swap)]
-    bias, columns, weights = prepare(parents, lengths, [kept, other[0]], length, log_rate)
     for step in steps:
         if step + 1 in steps:
-            chain.append(permute(chain[-1], climb))
-        gate = [bias, taken_q[0]] if step == 1 else []
-        other.append(after(permute(other[-1], climb), chain[-1], *gate))
+            chain.append(climb(chain[-1], step + 1))
+        gate = {1: [firsts, taken_q[0]], 2: [advantages]}.get(step, [])
+        other.append(after(climb(other[-1], step), chain[-1], *gate))
     for block in given_q[1:]:
         taken_q.append(permute(after(block, taken_q[-1]), swap))
     blocks = [block for pair in zip(chain, other) for block in pair]
-    row, advantages = advantages_of(columns, weights, blocks)
 
     dq_own, dq_back, dkv_list = [], [], []
     for chunk in range(chunks):
@@ -554,9 +547,11 @@
     own = lax.axis_index("seg")
     own_len = lax.dynamic_slice_in_dim(lengths, own, 1)[0]
     terms = jnp.concatenate(token_terms(log_rate, own_len, *token_rows), axis=1)
-    bias, columns, weights = prepare(parents, lengths, [terms], length, log_rate)
-    terms = lax.all_gather(terms, "seg", axis=0, tiled=True)
-    row, advantages = advantages_of(columns, weights, [terms])
+    bias, columns, weights, firsts = prepare(parents, lengths, [terms], length, log_rate)
+    firsts = lax.all_gather(
+        lax.dynamic_slice_in_dim(firsts, own, 1), "seg", axis=0, tiled=True
+    )
+    row, advantages = advantages_of(columns, weights, firsts, jnp.zeros_like(firsts))
     flat = jnp.concatenate([key_vectors, value_vectors], axis=1)[None]
     spread = lax.all_to_all(flat, "seg", split_axis=1, concat_axis=0, tiled=True)
     chains = ancestors(parents, DEPTH - 1)

time: 66.3 us -> 73.9 us (1.11)
  starting transfers between devices: 21.1 us -> 31.2 us
  waiting for transfers between devices: 27.3 us -> 24.4 us
    ppermute x19 -> x21, starting transfers between devices: 21.1 us -> 31.2 us  [permute(): return lax.ppermute(array, 'seg', pairs)]
    ppermute x19 -> x21, waiting for transfers between devices: 27.3 us -> 24.4 us  [permute(): return lax.ppermute(array, 'seg', pairs)]
  transfers between devices with their start and end apart: 19 -> 21, of which waited for: 9 -> 8; matrix products, arithmetic and copies ran while one was open for 0% -> 0% of each run, Pallas kernels for 18% -> 16%
where the time goes in v8:
time: 73.9 us; the launch traced here: 73.4 us
  starting transfers between devices  31.2 us (42%)
  waiting for transfers between devices  24.4 us (33%)
  Pallas kernels  14.6 us (20%)
  local copies, waits for them, and re-layouts  2.19 us (3%)
  between operations  0.89 us (1%)
    ppermute x21, starting transfers between devices, permute(): return lax.ppermute(array, 'seg', pairs)  31.2 us
    ppermute x21, waiting for transfers between devices, permute(): return lax.ppermute(array, 'seg', pairs)  24.4 us
    pallas_call x2, Pallas kernels, attend(): pl.pallas_call(functools.partial(attend_kernel, DEPTH, chunk, segs, sourc...  8.88 us
    unnamed x10, local copies, waits for them, and re-layouts  2.19 us
    pallas_call x1, Pallas kernels, pack(): pl.pallas_call(functools.partial(pack_kernel, log_rate), out_shape=(block...  1.86 us
  transfers between devices with their start and end apart: 21, of which 8 were waited for; matrix products, arithmetic and copies ran while one was open for 0% of the time, Pallas kernels for 16%

profile of v8, /device:TPU:0, one launch (start us, length us, event | category | flops | bytes accessed | tf_op | source)
XLA Modules:
  0.0 73.4 jit_solution(16929458225049324880)
XLA Ops:
  0.6 1.9 %pack_keys_values.1 = (bf16[528,128]{1,0:T(8,128)(2,1)}, bf16[528,128]{1,0:T(8,128)(2,1)}) custom-call(s32[8]{0:T(128)} %lengths_s.1, bf16[128,512]{1,0:T(8,128)(2,1)} %k_ref.1, bf16[128,512]{1,0:T(8,128)(2,1)} %v_ref.1, f32[1,128]{1,0:T(1,128)} %bitcast.9, f32[1,128]{1,0:T(1,128)} %bitcast.10, f32[1,128]{1,0:T(1,128)} %bitcast.11, f32[1,128]{1,0:T(1,128)} %bitcast.12), custom_call_target="tpu_custom_call" | custom-call | flops 12800 | bytes 524288 | tf_op jit(solution)/shard_map/pack_keys_values/pallas_call | solution.py:101
  2.5 2.9 %collective-permute-start = (bf16[528,128]{1,0:T(8,128)(2,1)}, bf16[528,128]{1,0:T(8,128)(2,1)S(1)}, u32[]{:S(2)}, u32[]{:S(2)}) collective-permute-start(bf16[528,128]{1,0:T(8,128)(2,1)} %get-tuple-element.40), channel_id=1, source_target_pairs={{0,2},{2,0},{4,6},{6,4},{8,10},{10,8},{12,14},{14,12},{1,3},{3,1},... | collective-permute-start | bytes 405512 | tf_op jit(solution)/shard_map/ppermute | solution.py:460
  5.4 3.5 %collective-permute-start.3 = (bf16[528,128]{1,0:T(8,128)(2,1)}, bf16[528,128]{1,0:T(8,128)(2,1)S(1)}, u32[]{:S(2)}, u32[]{:S(2)}) collective-permute-start(bf16[528,128]{1,0:T(8,128)(2,1)} %get-tuple-element.39.refs_0_.refs_5_), channel_id=1, source_target_pairs={{0,4},{2,6},{4,8},{6,10},{8,12},{10,14},{1,5},{3,7},{5,9},{7,11},{... | collective-permute-start | bytes 405512 | tf_op jit(solution)/shard_map/ppermute | solution.py:460
  8.9 0.0 copy-start
  8.9 1.1 %copy-done = bf16[128,2560]{1,0:T(8,128)(2,1)S(1)} copy-done((bf16[128,2560]{1,0:T(8,128)(2,1)S(1)}, bf16[128,2560]{1,0:T(8,128)(2,1)}, u32[]{:S(2)}) %copy-start) | copy-done | bytes 655384
  10.0 0.0 copy-start.1
  10.0 1.1 %copy-done.1 = bf16[128,2560]{1,0:T(8,128)(2,1)S(1)} copy-done((bf16[128,2560]{1,0:T(8,128)(2,1)S(1)}, bf16[128,2560]{1,0:T(8,128)(2,1)}, u32[]{:S(2)}) %copy-start.1) | copy-done | bytes 655384
  11.1 0.0 copy-start.2
  11.1 0.2 pack_queries.1
  11.3 0.0 copy-start.3
  11.3 0.0 copy-start.4
  11.4 0.0 collective-permute-done.refs_1_.refs_6_
  11.4 0.4 collective-permute-done.3.refs_7_
  11.8 0.5 collective-permute-start.4
  12.3 0.7 collective-permute-start.6
  13.0 7.1 %collective-permute-start.5 = (bf16[528,128]{1,0:T(8,128)(2,1)S(1)}, bf16[528,128]{1,0:T(8,128)(2,1)S(1)}, u32[]{:S(2)}, u32[]{:S(2)}) collective-permute-start(bf16[528,128]{1,0:T(8,128)(2,1)S(1)} %collective-permute-done.refs_1_.refs_6_), channel_id=1, source_target_pairs={{0,4},{2,6},{4,8},{6,10},{8,12},{10,14},{1,5},{3,7},{5,9},{7,11},{... | collective-permute-start | bytes 405512 | tf_op jit(solution)/shard_map/ppermute | solution.py:460
  20.1 0.0 copy-done.2
  20.1 0.0 copy-done.3
  20.1 0.0 copy-done.4
  20.1 1.2 %prepare.1 = (f32[2,640,128]{2,1,0:T(8,128)S(1)}, f32[2,3,128,128]{3,2,1,0:T(8,128)S(1)}, f32[2,2,8,128]{3,2,1,0:T(8,128)S(1)}, f32[8,128]{1,0:T(8,128)S(1)}) custom-call(s32[8]{0:T(128)S(1)} %copy-done.4, s32[8]{0:T(128)S(1)} %copy-done.3, bf16[528,128]{1,0:T(8,128)(2,1)S(1)} %copy-done.2, bf16[528,128]{1,0:T(8,128)(2,1)S(1)} %collective-permute-done.refs_1_.refs_6_), custom_call_target="tpu_custom_call" | custom-call | flops 3276800 | bytes 655360 | tf_op jit(solution)/shard_map/prepare/pallas_call | solution.py:232
  21.3 1.3 %collective-permute-start.1 = (f32[8,128]{1,0:T(8,128)S(1)}, f32[8,128]{1,0:T(8,128)S(1)}, u32[]{:S(2)}, u32[]{:S(2)}) collective-permute-start(f32[8,128]{1,0:T(8,128)S(1)} %get-tuple-element.43), channel_id=1, source_target_pairs={{4,0},{6,2},{8,4},{10,6},{12,8},{14,10},{5,1},{7,3},{9,5},{11,7},{... | collective-permute-start | bytes 12296 | tf_op jit(solution)/shard_map/ppermute | solution.py:460
  22.6 4.2 %collective-permute-done.1 = f32[8,128]{1,0:T(8,128)S(1)} collective-permute-done((f32[8,128]{1,0:T(8,128)S(1)}, f32[8,128]{1,0:T(8,128)S(1)}, u32[]{:S(2)}, u32[]{:S(2)}) %collective-permute-start.1) | collective-permute-done | bytes 4128 | tf_op jit(solution)/shard_map/ppermute | solution.py:460
  26.8 0.0 collective-permute-done.6.refs_9_
  26.8 0.7 collective-permute-start.8
  27.5 0.0 collective-permute-done.5.refs_8_
  27.5 0.0 collective-permute-done.4.refs_4_
  27.5 0.7 collective-permute-start.7
  28.2 1.6 %collective-permute-start.10 = (bf16[2,5,128,128]{3,2,1,0:T(8,128)(2,1)S(1)}, bf16[2,5,128,128]{3,2,1,0:T(8,128)(2,1)S(1)}, u32[]{:S(2)}, u32[]{:S(2)}) collective-permute-start(bf16[2,5,128,128]{3,2,1,0:T(8,128)(2,1)S(1)} %get-tuple-element.57), channel_id=1, source_target_pairs={{0,2},{2,0},{4,6},{6,4},{8,10},{10,8},{12,14},{14,12},{1,3},{3,1},... | collective-permute-start | bytes 983048 | tf_op jit(solution)/shard_map/ppermute | solution.py:460
  29.8 1.3 %collective-permute-start.2 = (f32[8,128]{1,0:T(8,128)S(1)}, f32[8,128]{1,0:T(8,128)S(1)}, u32[]{:S(2)}, u32[]{:S(2)}) collective-permute-start(f32[8,128]{1,0:T(8,128)S(1)} %add.31.near_ref), channel_id=1, source_target_pairs={{8,0},{10,2},{12,4},{14,6},{9,1},{11,3},{13,5},{15,7},{24,16},{26,... | collective-permute-start | bytes 12296 | tf_op jit(solution)/shard_map/ppermute | solution.py:460
  31.1 5.1 %collective-permute-done.2.far_ref = f32[8,128]{1,0:T(8,128)S(1)} collective-permute-done((f32[8,128]{1,0:T(8,128)S(1)}, f32[8,128]{1,0:T(8,128)S(1)}, u32[]{:S(2)}, u32[]{:S(2)}) %collective-permute-start.2) | collective-permute-done | bytes 4128 | tf_op jit(solution)/shard_map/ppermute | solution.py:460
  36.2 0.7 advantages.1
  36.8 0.0 collective-permute-done.8.refs_11_
  36.8 0.0 collective-permute-done.7.refs_10_
  36.8 0.7 collective-permute-start.9
  37.5 0.0 collective-permute-done.9.refs_12_
  37.5 4.5 %tree_attention_backward.2 = (bf16[128,640]{1,0:T(8,128)(2,1)S(1)}, bf16[128,640]{1,0:T(8,128)(2,1)S(1)}, bf16[2,2,128,128]{3,2,1,0:T(8,128)(2,1)S(1)}, bf16[2,2...) custom-call(s32[8]{0:T(128)S(1)} %copy-done.4, ...), custom_call_target="tpu_custom_call" | custom-call | flops 1048576000 | bytes 8388608 | tf_op jit(solution)/shard_map/tree_attention_backward/pallas_call | solution.py:374
  42.0 1.3 %collective-permute-start.13 = (bf16[2,2,128,128]{3,2,1,0:T(8,128)(2,1)S(1)}, bf16[2,2,128,128]{3,2,1,0:T(8,128)(2,1)S(1)}, u32[]{:S(2)}, u32[]{:S(2)}) collective-permute-start(bf16[2,2,128,128]{3,2,1,0:T(8,128)(2,1)S(1)} %get-tuple-element.63), channel_id=1, source_target_pairs={{12,0},{14,2},{13,1},{15,3},{28,16},{30,18},{29,17},{31,19}} | collective-permute-start | bytes 393224 | tf_op jit(solution)/shard_map/ppermute | solution.py:460
  43.3 1.3 %collective-permute-start.14 = (bf16[2,2,128,128]{3,2,1,0:T(8,128)(2,1)S(1)}, bf16[2,2,128,128]{3,2,1,0:T(8,128)(2,1)S(1)}, u32[]{:S(2)}, u32[]{:S(2)}) collective-permute-start(bf16[2,2,128,128]{3,2,1,0:T(8,128)(2,1)S(1)} %get-tuple-element.64), channel_id=1, source_target_pairs={{8,0},{10,2},{12,4},{14,6},{9,1},{11,3},{13,5},{15,7},{24,16},{26,... | collective-permute-start | bytes 393224 | tf_op jit(solution)/shard_map/ppermute | solution.py:460
  44.6 1.3 %collective-permute-start.15 = (bf16[2,2,128,128]{3,2,1,0:T(8,128)(2,1)S(1)}, bf16[2,2,128,128]{3,2,1,0:T(8,128)(2,1)S(1)}, u32[]{:S(2)}, u32[]{:S(2)}) collective-permute-start(bf16[2,2,128,128]{3,2,1,0:T(8,128)(2,1)S(1)} %get-tuple-element.65), channel_id=1, source_target_pairs={{4,0},{6,2},{8,4},{10,6},{12,8},{14,10},{5,1},{7,3},{9,5},{11,7},{... | collective-permute-start | bytes 393224 | tf_op jit(solution)/shard_map/ppermute | solution.py:460
  45.9 0.6 collective-permute-start.11
  46.5 0.0 collective-permute-done.10.refs_4_
  46.5 4.4 %tree_attention_backward.3 = (bf16[128,640]{1,0:T(8,128)(2,1)S(1)}, bf16[128,640]{1,0:T(8,128)(2,1)S(1)}, bf16[2,2,128,128]{3,2,1,0:T(8,128)(2,1)S(1)}, bf16[2,2...) custom-call(s32[8]{0:T(128)S(1)} %copy-done.4, ...), custom_call_target="tpu_custom_call" | custom-call | flops 1048576000 | bytes 8388608 | tf_op jit(solution)/shard_map/tree_attention_backward/pallas_call | solution.py:374
  50.9 1.3 %collective-permute-start.17 = (bf16[2,2,128,128]{3,2,1,0:T(8,128)(2,1)S(1)}, bf16[2,2,128,128]{3,2,1,0:T(8,128)(2,1)S(1)}, u32[]{:S(2)}, u32[]{:S(2)}) collective-permute-start(bf16[2,2,128,128]{3,2,1,0:T(8,128)(2,1)S(1)} %get-tuple-element.68), channel_id=1, source_target_pairs={{12,0},{14,2},{13,1},{15,3},{28,16},{30,18},{29,17},{31,19}} | collective-permute-start | bytes 393224 | tf_op jit(solution)/shard_map/ppermute | solution.py:460
  52.2 3.3 %collective-permute-done.13.refs_3_ = bf16[2,2,128,128]{3,2,1,0:T(8,128)(2,1)S(1)} collective-permute-done((bf16[2,2,128,128]{3,2,1,0:T(8,128)(2,1)S(1)}, bf16[2,2,128,128]{3,2,1,0:T(8,128)(2,1)S(1)}, u32[]{:S(2)}, u32[]{:S(2)}) %collective-permute-start.13) | collective-permute-done | bytes 131104 | tf_op jit(solution)/shard_map/ppermute | solution.py:460
  55.5 1.3 %collective-permute-start.18 = (bf16[2,2,128,128]{3,2,1,0:T(8,128)(2,1)S(1)}, bf16[2,2,128,128]{3,2,1,0:T(8,128)(2,1)S(1)}, u32[]{:S(2)}, u32[]{:S(2)}) collective-permute-start(bf16[2,2,128,128]{3,2,1,0:T(8,128)(2,1)S(1)} %get-tuple-element.69), channel_id=1, source_target_pairs={{8,0},{10,2},{12,4},{14,6},{9,1},{11,3},{13,5},{15,7},{24,16},{26,... | collective-permute-start | bytes 393224 | tf_op jit(solution)/shard_map/ppermute | solution.py:460
  56.8 1.1 %collective-permute-done.14.refs_4_ = bf16[2,2,128,128]{3,2,1,0:T(8,128)(2,1)S(1)} collective-permute-done((bf16[2,2,128,128]{3,2,1,0:T(8,128)(2,1)S(1)}, bf16[2,2,128,128]{3,2,1,0:T(8,128)(2,1)S(1)}, u32[]{:S(2)}, u32[]{:S(2)}) %collective-permute-start.14) | collective-permute-done | bytes 131104 | tf_op jit(solution)/shard_map/ppermute | solution.py:460
  57.9 1.3 %collective-permute-start.19 = (bf16[2,2,128,128]{3,2,1,0:T(8,128)(2,1)S(1)}, bf16[2,2,128,128]{3,2,1,0:T(8,128)(2,1)S(1)}, u32[]{:S(2)}, u32[]{:S(2)}) collective-permute-start(bf16[2,2,128,128]{3,2,1,0:T(8,128)(2,1)S(1)} %get-tuple-element.70), channel_id=1, source_target_pairs={{4,0},{6,2},{8,4},{10,6},{12,8},{14,10},{5,1},{7,3},{9,5},{11,7},{... | collective-permute-start | bytes 393224 | tf_op jit(solution)/shard_map/ppermute | solution.py:460
  59.2 0.0 collective-permute-done.15.refs_5_
  59.2 0.1 collective-permute-start.12
  59.3 5.2 %collective-permute-done.17.refs_7_ = bf16[2,2,128,128]{3,2,1,0:T(8,128)(2,1)S(1)} collective-permute-done((bf16[2,2,128,128]{3,2,1,0:T(8,128)(2,1)S(1)}, bf16[2,2,128,128]{3,2,1,0:T(8,128)(2,1)S(1)}, u32[]{:S(2)}, u32[]{:S(2)}) %collective-permute-start.17) | collective-permute-done | bytes 131104 | tf_op jit(solution)/shard_map/ppermute | solution.py:460
  64.6 1.4 %collective-permute-start.16 = (bf16[2,128,128]{2,1,0:T(8,128)(2,1)S(1)}, bf16[2,128,128]{2,1,0:T(8,128)(2,1)S(1)}, u32[]{:S(2)}, u32[]{:S(2)}) collective-permute-start(bf16[2,128,128]{2,1,0:T(8,128)(2,1)S(1)} %fusion), channel_id=1, source_target_pairs={{0,2},{2,0},{4,6},{6,4},{8,10},{10,8},{12,14},{14,12},{1,3},{3,1},... | collective-permute-start | bytes 196616 | tf_op jit(solution)/shard_map/ppermute | solution.py:460
  66.0 2.2 %collective-permute-done.18.refs_8_ = bf16[2,2,128,128]{3,2,1,0:T(8,128)(2,1)S(1)} collective-permute-done((bf16[2,2,128,128]{3,2,1,0:T(8,128)(2,1)S(1)}, bf16[2,2,128,128]{3,2,1,0:T(8,128)(2,1)S(1)}, u32[]{:S(2)}, u32[]{:S(2)}) %collective-permute-start.18) | collective-permute-done | bytes 131104 | tf_op jit(solution)/shard_map/ppermute | solution.py:460
  68.2 0.0 collective-permute-done.19.refs_9_
  68.3 0.6 collective-permute-start.20
  68.9 0.0 collective-permute-done.11.refs_2_
  68.9 0.0 collective-permute-done.12.refs_3_
  68.9 0.9 %join_queries.1 = bf16[128,2560]{1,0:T(8,128)(2,1)} custom-call(bf16[128,640]{1,0:T(8,128)(2,1)S(1)} %get-tuple-element.54.refs_0_, bf16[128,640]{1,0:T(8,128)(2,1)S(1)} %get-tuple-element.58.refs_1_, bf16[128,640]{1,0:T(8,128)(2,1)S(1)} %collective-permute-done.11.refs_2_, bf16[128,640]{1,0:T(8,128)(2,1)S(1)} %collective-permute-done.12.refs_3_), custom_call_target="tpu_custom_call" | custom-call | bytes 1310720 | tf_op jit(solution)/shard_map/join_queries/pallas_call | solution.py:412
  69.8 0.0 collective-permute-done.16.refs_0_
  69.8 2.8 %collective-permute-done.20.refs_1_ = bf16[2,128,128]{2,1,0:T(8,128)(2,1)S(1)} collective-permute-done((bf16[2,128,128]{2,1,0:T(8,128)(2,1)S(1)}, bf16[2,128,128]{2,1,0:T(8,128)(2,1)S(1)}, u32[]{:S(2)}, u32[]{:S(2)}) %collective-permute-start.20) | collective-permute-done | bytes 65568 | tf_op jit(solution)/shard_map/ppermute | solution.py:460
  72.6 0.8 %join_keys.1 = (bf16[128,512]{1,0:T(8,128)(2,1)}, bf16[128,512]{1,0:T(8,128)(2,1)}) custom-call(bf16[2,128,128]{2,1,0:T(8,128)(2,1)S(1)} %collective-permute-done.16.refs_0_, bf16[2,128,128]{2,1,0:T(8,128)(2,1)S(1)} %collective-permute-done.20.refs_1_, bf16[2,2,128,128]{3,2,1,0:T(8,128)(2,1)S(1)} %get-tuple-element.62.refs_2_, ...), custom_call_target="tpu_custom_call" | custom-call | bytes 524288 | tf_op jit(solution)/shard_map/join_keys/pallas_call | solution.py:446
  (3 shorter events, 0.1 us)
Async XLA Ops:
  2.5 8.9 %collective-permute-start = (bf16[528,128]{1,0:T(8,128)(2,1)}, bf16[528,128]{1,0:T(8,128)(2,1)S(1)}, u32[]{:S(2)}, u32[]{:S(2)}) collective-permute-start(bf16[528,128]{1,0:T(8,128)(2,1)} %get-tuple-element.40), channel_id=1, source_target_pairs={{0,2},{2,0},{4,6},{6,4},{8,10},{10,8},{12,14},{14,12},{1,3},{3,1},... | collective-permute-start | bytes 405512 | tf_op jit(solution)/shard_map/ppermute | solution.py:460
  5.4 6.3 %collective-permute-start.3 = (bf16[528,128]{1,0:T(8,128)(2,1)}, bf16[528,128]{1,0:T(8,128)(2,1)S(1)}, u32[]{:S(2)}, u32[]{:S(2)}) collective-permute-start(bf16[528,128]{1,0:T(8,128)(2,1)} %get-tuple-element.39.refs_0_.refs_5_), channel_id=1, source_target_pairs={{0,4},{2,6},{4,8},{6,10},{8,12},{10,14},{1,5},{3,7},{5,9},{7,11},{... | collective-permute-start | bytes 405512 | tf_op jit(solution)/shard_map/ppermute | solution.py:460
  8.9 1.1 %copy-start = (bf16[128,2560]{1,0:T(8,128)(2,1)S(1)}, bf16[128,2560]{1,0:T(8,128)(2,1)}, u32[]{:S(2)}) copy-start(bf16[128,2560]{1,0:T(8,128)(2,1)} %q_ref) | copy-start | bytes 1966084
  10.0 1.1 %copy-start.1 = (bf16[128,2560]{1,0:T(8,128)(2,1)S(1)}, bf16[128,2560]{1,0:T(8,128)(2,1)}, u32[]{:S(2)}) copy-start(bf16[128,2560]{1,0:T(8,128)(2,1)} %dir_ref.1) | copy-start | bytes 1966084
  11.1 9.0 %copy-start.2 = (bf16[528,128]{1,0:T(8,128)(2,1)S(1)}, bf16[528,128]{1,0:T(8,128)(2,1)}, u32[]{:S(2)}) copy-start(bf16[528,128]{1,0:T(8,128)(2,1)} %get-tuple-element.39.refs_0_.refs_5_) | copy-start | bytes 405508
  11.3 8.8 %copy-start.3 = (s32[8]{0:T(128)S(1)}, s32[8]{0:T(128)}, u32[]{:S(2)}) copy-start(s32[8]{0:T(128)} %lengths_s.1) | copy-start | bytes 100
  11.3 8.8 %copy-start.4 = (s32[8]{0:T(128)S(1)}, s32[8]{0:T(128)}, u32[]{:S(2)}) copy-start(s32[8]{0:T(128)} %refs_0_.3) | copy-start | bytes 100
  11.8 15.8 %collective-permute-start.4 = (bf16[2,5,128,128]{3,2,1,0:T(8,128)(2,1)S(1)}, bf16[2,5,128,128]{3,2,1,0:T(8,128)(2,1)S(1)}, u32[]{:S(2)}, u32[]{:S(2)}) collective-permute-start(bf16[2,5,128,128]{3,2,1,0:T(8,128)(2,1)S(1)} %get-tuple-element.50), channel_id=1, source_target_pairs={{0,2},{2,0},{4,6},{6,4},{8,10},{10,8},{12,14},{14,12},{1,3},{3,1},... | collective-permute-start | bytes 983048 | tf_op jit(solution)/shard_map/ppermute | solution.py:460
  12.3 14.5 %collective-permute-start.6 = (bf16[528,128]{1,0:T(8,128)(2,1)S(1)}, bf16[528,128]{1,0:T(8,128)(2,1)S(1)}, u32[]{:S(2)}, u32[]{:S(2)}) collective-permute-start(bf16[528,128]{1,0:T(8,128)(2,1)S(1)} %collective-permute-done.3.refs_7_), channel_id=1, source_target_pairs={{4,8},{6,10},{8,12},{10,14},{5,9},{7,11},{9,13},{11,15},{20,24},{2... | collective-permute-start | bytes 405512 | tf_op jit(solution)/shard_map/ppermute | solution.py:460
  13.0 14.5 %collective-permute-start.5 = (bf16[528,128]{1,0:T(8,128)(2,1)S(1)}, bf16[528,128]{1,0:T(8,128)(2,1)S(1)}, u32[]{:S(2)}, u32[]{:S(2)}) collective-permute-start(bf16[528,128]{1,0:T(8,128)(2,1)S(1)} %collective-permute-done.refs_1_.refs_6_), channel_id=1, source_target_pairs={{0,4},{2,6},{4,8},{6,10},{8,12},{10,14},{1,5},{3,7},{5,9},{7,11},{... | collective-permute-start | bytes 405512 | tf_op jit(solution)/shard_map/ppermute | solution.py:460
  21.3 5.5 %collective-permute-start.1 = (f32[8,128]{1,0:T(8,128)S(1)}, f32[8,128]{1,0:T(8,128)S(1)}, u32[]{:S(2)}, u32[]{:S(2)}) collective-permute-start(f32[8,128]{1,0:T(8,128)S(1)} %get-tuple-element.43), channel_id=1, source_target_pairs={{4,0},{6,2},{8,4},{10,6},{12,8},{14,10},{5,1},{7,3},{9,5},{11,7},{... | collective-permute-start | bytes 12296 | tf_op jit(solution)/shard_map/ppermute | solution.py:460
  26.8 10.0 %collective-permute-start.8 = (bf16[528,128]{1,0:T(8,128)(2,1)S(1)}, bf16[528,128]{1,0:T(8,128)(2,1)S(1)}, u32[]{:S(2)}, u32[]{:S(2)}) collective-permute-start(bf16[528,128]{1,0:T(8,128)(2,1)S(1)} %collective-permute-done.6.refs_9_), channel_id=1, source_target_pairs={{8,12},{10,14},{9,13},{11,15},{24,28},{26,30},{25,29},{27,31}} | collective-permute-start | bytes 405512 | tf_op jit(solution)/shard_map/ppermute | solution.py:460
  27.5 9.3 %collective-permute-start.7 = (bf16[528,128]{1,0:T(8,128)(2,1)S(1)}, bf16[528,128]{1,0:T(8,128)(2,1)S(1)}, u32[]{:S(2)}, u32[]{:S(2)}) collective-permute-start(bf16[528,128]{1,0:T(8,128)(2,1)S(1)} %collective-permute-done.5.refs_8_), channel_id=1, source_target_pairs={{4,8},{6,10},{8,12},{10,14},{5,9},{7,11},{9,13},{11,15},{20,24},{2... | collective-permute-start | bytes 405512 | tf_op jit(solution)/shard_map/ppermute | solution.py:460
  28.2 18.3 %collective-permute-start.10 = (bf16[2,5,128,128]{3,2,1,0:T(8,128)(2,1)S(1)}, bf16[2,5,128,128]{3,2,1,0:T(8,128)(2,1)S(1)}, u32[]{:S(2)}, u32[]{:S(2)}) collective-permute-start(bf16[2,5,128,128]{3,2,1,0:T(8,128)(2,1)S(1)} %get-tuple-element.57), channel_id=1, source_target_pairs={{0,2},{2,0},{4,6},{6,4},{8,10},{10,8},{12,14},{14,12},{1,3},{3,1},... | collective-permute-start | bytes 983048 | tf_op jit(solution)/shard_map/ppermute | solution.py:460
  29.8 6.4 %collective-permute-start.2 = (f32[8,128]{1,0:T(8,128)S(1)}, f32[8,128]{1,0:T(8,128)S(1)}, u32[]{:S(2)}, u32[]{:S(2)}) collective-permute-start(f32[8,128]{1,0:T(8,128)S(1)} %add.31.near_ref), channel_id=1, source_target_pairs={{8,0},{10,2},{12,4},{14,6},{9,1},{11,3},{13,5},{15,7},{24,16},{26,... | collective-permute-start | bytes 12296 | tf_op jit(solution)/shard_map/ppermute | solution.py:460
  36.8 0.7 collective-permute-start.9
  42.0 13.6 %collective-permute-start.13 = (bf16[2,2,128,128]{3,2,1,0:T(8,128)(2,1)S(1)}, bf16[2,2,128,128]{3,2,1,0:T(8,128)(2,1)S(1)}, u32[]{:S(2)}, u32[]{:S(2)}) collective-permute-start(bf16[2,2,128,128]{3,2,1,0:T(8,128)(2,1)S(1)} %get-tuple-element.63), channel_id=1, source_target_pairs={{12,0},{14,2},{13,1},{15,3},{28,16},{30,18},{29,17},{31,19}} | collective-permute-start | bytes 393224 | tf_op jit(solution)/shard_map/ppermute | solution.py:460
  43.3 14.6 %collective-permute-start.14 = (bf16[2,2,128,128]{3,2,1,0:T(8,128)(2,1)S(1)}, bf16[2,2,128,128]{3,2,1,0:T(8,128)(2,1)S(1)}, u32[]{:S(2)}, u32[]{:S(2)}) collective-permute-start(bf16[2,2,128,128]{3,2,1,0:T(8,128)(2,1)S(1)} %get-tuple-element.64), channel_id=1, source_target_pairs={{8,0},{10,2},{12,4},{14,6},{9,1},{11,3},{13,5},{15,7},{24,16},{26,... | collective-permute-start | bytes 393224 | tf_op jit(solution)/shard_map/ppermute | solution.py:460
  44.6 14.6 %collective-permute-start.15 = (bf16[2,2,128,128]{3,2,1,0:T(8,128)(2,1)S(1)}, bf16[2,2,128,128]{3,2,1,0:T(8,128)(2,1)S(1)}, u32[]{:S(2)}, u32[]{:S(2)}) collective-permute-start(bf16[2,2,128,128]{3,2,1,0:T(8,128)(2,1)S(1)} %get-tuple-element.65), channel_id=1, source_target_pairs={{4,0},{6,2},{8,4},{10,6},{12,8},{14,10},{5,1},{7,3},{9,5},{11,7},{... | collective-permute-start | bytes 393224 | tf_op jit(solution)/shard_map/ppermute | solution.py:460
  45.9 23.0 %collective-permute-start.11 = (bf16[128,640]{1,0:T(8,128)(2,1)S(1)}, bf16[128,640]{1,0:T(8,128)(2,1)S(1)}, u32[]{:S(2)}, u32[]{:S(2)}) collective-permute-start(bf16[128,640]{1,0:T(8,128)(2,1)S(1)} %get-tuple-element.59), channel_id=1, source_target_pairs={{0,2},{2,0},{4,6},{6,4},{8,10},{10,8},{12,14},{14,12},{1,3},{3,1},... | collective-permute-start | bytes 491528 | tf_op jit(solution)/shard_map/ppermute | solution.py:460
  50.9 13.7 %collective-permute-start.17 = (bf16[2,2,128,128]{3,2,1,0:T(8,128)(2,1)S(1)}, bf16[2,2,128,128]{3,2,1,0:T(8,128)(2,1)S(1)}, u32[]{:S(2)}, u32[]{:S(2)}) collective-permute-start(bf16[2,2,128,128]{3,2,1,0:T(8,128)(2,1)S(1)} %get-tuple-element.68), channel_id=1, source_target_pairs={{12,0},{14,2},{13,1},{15,3},{28,16},{30,18},{29,17},{31,19}} | collective-permute-start | bytes 393224 | tf_op jit(solution)/shard_map/ppermute | solution.py:460
  55.5 12.7 %collective-permute-start.18 = (bf16[2,2,128,128]{3,2,1,0:T(8,128)(2,1)S(1)}, bf16[2,2,128,128]{3,2,1,0:T(8,128)(2,1)S(1)}, u32[]{:S(2)}, u32[]{:S(2)}) collective-permute-start(bf16[2,2,128,128]{3,2,1,0:T(8,128)(2,1)S(1)} %get-tuple-element.69), channel_id=1, source_target_pairs={{8,0},{10,2},{12,4},{14,6},{9,1},{11,3},{13,5},{15,7},{24,16},{26,... | collective-permute-start | bytes 393224 | tf_op jit(solution)/shard_map/ppermute | solution.py:460
  57.9 10.3 %collective-permute-start.19 = (bf16[2,2,128,128]{3,2,1,0:T(8,128)(2,1)S(1)}, bf16[2,2,128,128]{3,2,1,0:T(8,128)(2,1)S(1)}, u32[]{:S(2)}, u32[]{:S(2)}) collective-permute-start(bf16[2,2,128,128]{3,2,1,0:T(8,128)(2,1)S(1)} %get-tuple-element.70), channel_id=1, source_target_pairs={{4,0},{6,2},{8,4},{10,6},{12,8},{14,10},{5,1},{7,3},{9,5},{11,7},{... | collective-permute-start | bytes 393224 | tf_op jit(solution)/shard_map/ppermute | solution.py:460
  59.2 9.7 %collective-permute-start.12 = (bf16[128,640]{1,0:T(8,128)(2,1)S(1)}, bf16[128,640]{1,0:T(8,128)(2,1)S(1)}, u32[]{:S(2)}, u32[]{:S(2)}) collective-permute-start(bf16[128,640]{1,0:T(8,128)(2,1)S(1)} %get-tuple-element.60), channel_id=1, source_target_pairs={{0,2},{2,0},{4,6},{6,4},{8,10},{10,8},{12,14},{14,12},{1,3},{3,1},... | collective-permute-start | bytes 491528 | tf_op jit(solution)/shard_map/ppermute | solution.py:460
  64.6 5.2 %collective-permute-start.16 = (bf16[2,128,128]{2,1,0:T(8,128)(2,1)S(1)}, bf16[2,128,128]{2,1,0:T(8,128)(2,1)S(1)}, u32[]{:S(2)}, u32[]{:S(2)}) collective-permute-start(bf16[2,128,128]{2,1,0:T(8,128)(2,1)S(1)} %fusion), channel_id=1, source_target_pairs={{0,2},{2,0},{4,6},{6,4},{8,10},{10,8},{12,14},{14,12},{1,3},{3,1},... | collective-permute-start | bytes 196616 | tf_op jit(solution)/shard_map/ppermute | solution.py:460
  68.3 4.3 %collective-permute-start.20 = (bf16[2,128,128]{2,1,0:T(8,128)(2,1)S(1)}, bf16[2,128,128]{2,1,0:T(8,128)(2,1)S(1)}, u32[]{:S(2)}, u32[]{:S(2)}) collective-permute-start(bf16[2,128,128]{2,1,0:T(8,128)(2,1)S(1)} %fusion.1), channel_id=1, source_target_pairs={{0,2},{2,0},{4,6},{6,4},{8,10},{10,8},{12,14},{14,12},{1,3},{3,1},... | collective-permute-start | bytes 196616 | tf_op jit(solution)/shard_map/ppermute | solution.py:460

commit v9 on v7

--- a/solution.py
+++ b/solution.py
@@ -145,6 +145,10 @@
     return jnp.where(segment >= 0, known, -1).astype(jnp.int32)
 
 
+def ring_place(pair):
+    return jnp.where(pair >= 2, 5 - pair, pair)
+
+
 def segment_of(own, segs, i):
     part = lax.rem(own, segs)
     return own - part + lax.rem(part + i, segs)
@@ -259,7 +263,8 @@
         firsts = jnp.zeros((count, length), jnp.float32)
         for index, ref in enumerate(term_refs):
             step, side = divmod(index, segs)
-            seg = lax.rem(pair - step + pairs, pairs) * segs + lax.rem(part + side, segs)
+            place = lax.rem(ring_place(pair) - step + pairs, pairs)
+            seg = ring_place(place) * segs + lax.rem(part + side, segs)
             firsts = jnp.where(seg_id == seg, read_terms(ref)[1], firsts)
     for i in range(segs):
         later_value = jnp.sum(weights_ref[i, 0] * firsts, axis=(0, 1), keepdims=True)
@@ -325,7 +330,8 @@
                 chosen.append(slot)
             else:
                 known = jnp.maximum(ancestor, 0)
-                step = (own - part) // segs - known // segs
+                step = ring_place((own - part) // segs) - ring_place(known // segs)
+                step = lax.rem(step + sources // segs, sources // segs)
                 turn = lax.rem(lax.rem(known, segs) - part + segs, segs)
                 chosen.append(jnp.where(ancestor >= 0, step * segs + turn, 0))
         q_list = [query_refs[i][0, j] for j in range(group_size)]
@@ -333,19 +339,22 @@
         do_list = [(adv_ref[i] * d.astype(jnp.float32)).astype(jnp.bfloat16) for d in dir_list]
         k_all = jnp.concatenate([kv_scr[s, 0] for s in chosen], axis=0)
         v_all = jnp.concatenate([kv_scr[s, 1] for s in chosen], axis=0)
+        q_all = jnp.concatenate(q_list, axis=0)
+        do_all = jnp.concatenate(do_list, axis=0)
+        all_scores = lax.dot_general(
+            k_all, q_all, contract_last, preferred_element_type=jnp.float32
+        )
+        all_dprob = lax.dot_general(
+            v_all, do_all, contract_last, preferred_element_type=jnp.float32
+        )
         for j in range(group_size):
             columns = slice(j * length, (j + 1) * length)
-            scores = lax.dot_general(
-                k_all, q_list[j], contract_last, preferred_element_type=jnp.float32
-            )
-            scores = scores * (scale * LOG2E) + bias_ref[i]
+            scores = all_scores[:, columns] * (scale * LOG2E) + bias_ref[i]
             top = jnp.max(scores, axis=0, keepdims=True)
             unnorm = jnp.exp2(scores - top)
             prob = unnorm * (1.0 / jnp.sum(unnorm, axis=0, keepdims=True))
             prob_low = prob.astype(jnp.bfloat16)
-            dprob = lax.dot_general(
-                v_all, do_list[j], contract_last, preferred_element_type=jnp.float32
-            )
+            dprob = all_dprob[:, columns]
             row_dot = jnp.sum(prob_low.astype(jnp.float32) * dprob, axis=0, keepdims=True)
             dscore = (prob * (dprob - row_dot)).astype(jnp.bfloat16)
             p_scr[:, columns] = prob_low
@@ -357,8 +366,6 @@
         for j in range(group_size):
             dq = jnp.transpose(dq_t[:, j * length : (j + 1) * length]) * scale
             dq_refs[i][:, j * HD : (j + 1) * HD] = dq.astype(jnp.bfloat16)
-        q_all = jnp.concatenate(q_list, axis=0)
-        do_all = jnp.concatenate(do_list, axis=0)
         dk_all = jnp.dot(dscore_all, q_all, preferred_element_type=jnp.float32) * scale
         dv_all = jnp.dot(p_scr[...], do_all, preferred_element_type=jnp.float32)
         for slot, s in enumerate(chosen):
@@ -479,9 +486,18 @@
     length = queries.shape[0]
     chunks = key_vectors.shape[1] // HD // 2
     swap = [(i, i ^ 1) for i in range(groups)]
-    climb = [(i, (i + 2) % groups) for i in range(groups)]
     steps = range(1, groups // 2)
-    down = {d: [(i, (i - 2 * d) % groups) for i in range(groups)] for d in steps}
+    ring = [0, 1, 3, 2]
+
+    def turn(distance):
+        pairs = []
+        for place, pair in enumerate(ring):
+            target = ring[(place + distance) % len(ring)]
+            pairs += [(2 * pair + x, 2 * target + x) for x in range(2)]
+        return pairs
+
+    climb = turn(1)
+    down = {d: turn(-d) for d in steps}
 
     kept, given = pack(lengths, key_vectors, value_vectors, token_rows, 2, log_rate)
     taken = permute(given, swap)

time: 66.3 us -> 64.8 us (0.977)
  waiting for transfers between devices: 27.3 us -> 15.7 us
  starting transfers between devices: 21.1 us -> 31.4 us
    ppermute x19, waiting for transfers between devices: 27.3 us -> 15.7 us  [permute(): return lax.ppermute(array, 'seg', pairs)]
    ppermute x19, starting transfers between devices: 21.1 us -> 31.4 us  [permute(): return lax.ppermute(array, 'seg', pairs)]
where the time goes in v9:
time: 64.8 us; the launch traced here: 64.6 us
  starting transfers between devices  31.4 us (48%)
  waiting for transfers between devices  15.7 us (24%)
  Pallas kernels  14.6 us (23%)
  local copies, waits for them, and re-layouts  2.19 us (3%)
  between operations  0.72 us (1%)
    ppermute x19, starting transfers between devices, permute(): return lax.ppermute(array, 'seg', pairs)  31.4 us
    ppermute x19, waiting for transfers between devices, permute(): return lax.ppermute(array, 'seg', pairs)  15.7 us
    pallas_call x2, Pallas kernels, attend(): pl.pallas_call(functools.partial(attend_kernel, DEPTH, chunk, segs, sourc...  8.85 us
    unnamed x10, local copies, waits for them, and re-layouts  2.19 us
    pallas_call x1, Pallas kernels, pack(): pl.pallas_call(functools.partial(pack_kernel, log_rate), out_shape=(block...  1.86 us
  transfers between devices with their start and end apart: 19, of which 9 were waited for; matrix products, arithmetic and copies ran while one was open for 0% of the time, Pallas kernels for 18%

profile of v9, /device:TPU:0, one launch (start us, length us, event | category | flops | bytes accessed | tf_op | source)
XLA Modules:
  0.0 64.6 jit_solution(10358318315507150305)
XLA Ops:
  0.6 1.9 %pack_keys_values.1 = (bf16[528,128]{1,0:T(8,128)(2,1)}, bf16[528,128]{1,0:T(8,128)(2,1)}) custom-call(s32[8]{0:T(128)} %lengths_s.1, bf16[128,512]{1,0:T(8,128)(2,1)} %k_ref.1, bf16[128,512]{1,0:T(8,128)(2,1)} %v_ref.1, f32[1,128]{1,0:T(1,128)} %bitcast.9, f32[1,128]{1,0:T(1,128)} %bitcast.10, f32[1,128]{1,0:T(1,128)} %bitcast.11, f32[1,128]{1,0:T(1,128)} %bitcast.12), custom_call_target="tpu_custom_call" | custom-call | flops 12800 | bytes 524288 | tf_op jit(solution)/shard_map/pack_keys_values/pallas_call | solution.py:101
  2.5 2.9 %collective-permute-start = (bf16[528,128]{1,0:T(8,128)(2,1)}, bf16[528,128]{1,0:T(8,128)(2,1)S(1)}, u32[]{:S(2)}, u32[]{:S(2)}) collective-permute-start(bf16[528,128]{1,0:T(8,128)(2,1)} %get-tuple-element.39), channel_id=1, source_target_pairs={{0,2},{2,0},{4,6},{6,4},{8,10},{10,8},{12,14},{14,12},{1,3},{3,1},... | collective-permute-start | bytes 405512 | tf_op jit(solution)/shard_map/ppermute | solution.py:477
  5.4 1.6 %collective-permute-start.1 = (bf16[528,128]{1,0:T(8,128)(2,1)}, bf16[528,128]{1,0:T(8,128)(2,1)S(1)}, u32[]{:S(2)}, u32[]{:S(2)}) collective-permute-start(bf16[528,128]{1,0:T(8,128)(2,1)} %get-tuple-element.38.refs_0_.refs_5_), channel_id=1, source_target_pairs={{0,4},{2,6},{4,12},{6,14},{12,8},{14,10},{8,0},{10,2},{1,5},{3,7},... | collective-permute-start | bytes 405512 | tf_op jit(solution)/shard_map/ppermute | solution.py:477
  7.0 0.0 copy-start
  7.0 1.1 %copy-done = bf16[128,2560]{1,0:T(8,128)(2,1)S(1)} copy-done((bf16[128,2560]{1,0:T(8,128)(2,1)S(1)}, bf16[128,2560]{1,0:T(8,128)(2,1)}, u32[]{:S(2)}) %copy-start) | copy-done | bytes 655384
  8.1 0.0 copy-start.1
  8.1 1.1 %copy-done.1 = bf16[128,2560]{1,0:T(8,128)(2,1)S(1)} copy-done((bf16[128,2560]{1,0:T(8,128)(2,1)S(1)}, bf16[128,2560]{1,0:T(8,128)(2,1)}, u32[]{:S(2)}) %copy-start.1) | copy-done | bytes 655384
  9.2 0.0 copy-start.2
  9.2 0.2 pack_queries.1
  9.4 0.0 copy-start.3
  9.4 0.0 copy-start.4
  9.4 0.0 collective-permute-done.refs_1_.refs_6_
  9.5 2.1 %collective-permute-done.1.refs_2_.refs_7_ = bf16[528,128]{1,0:T(8,128)(2,1)S(1)} collective-permute-done((bf16[528,128]{1,0:T(8,128)(2,1)}, bf16[528,128]{1,0:T(8,128)(2,1)S(1)}, u32[]{:S(2)}, u32[]{:S(2)}) %collective-permute-start.1) | collective-permute-done | bytes 135200 | tf_op jit(solution)/shard_map/ppermute | solution.py:477
  11.6 0.5 collective-permute-start.4
  12.1 0.9 %collective-permute-start.3 = (bf16[528,128]{1,0:T(8,128)(2,1)S(1)}, bf16[528,128]{1,0:T(8,128)(2,1)S(1)}, u32[]{:S(2)}, u32[]{:S(2)}) collective-permute-start(bf16[528,128]{1,0:T(8,128)(2,1)S(1)} %collective-permute-done.1.refs_2_.refs_7_), channel_id=1, source_target_pairs={{0,4},{2,6},{4,12},{6,14},{12,8},{14,10},{8,0},{10,2},{1,5},{3,7},... | collective-permute-start | bytes 405512 | tf_op jit(solution)/shard_map/ppermute | solution.py:477
  13.0 3.3 %collective-permute-start.2 = (bf16[528,128]{1,0:T(8,128)(2,1)S(1)}, bf16[528,128]{1,0:T(8,128)(2,1)S(1)}, u32[]{:S(2)}, u32[]{:S(2)}) collective-permute-start(bf16[528,128]{1,0:T(8,128)(2,1)S(1)} %collective-permute-done.refs_1_.refs_6_), channel_id=1, source_target_pairs={{0,4},{2,6},{4,12},{6,14},{12,8},{14,10},{8,0},{10,2},{1,5},{3,7},... | collective-permute-start | bytes 405512 | tf_op jit(solution)/shard_map/ppermute | solution.py:477
  16.3 0.0 copy-done.2
  16.3 0.0 copy-done.3
  16.3 0.0 copy-done.4
  16.3 1.2 %prepare.1 = (f32[2,640,128]{2,1,0:T(8,128)S(1)}, f32[2,3,128,128]{3,2,1,0:T(8,128)S(1)}, f32[2,2,8,128]{3,2,1,0:T(8,128)S(1)}) custom-call(s32[8]{0:T(128)S(1)} %copy-done.4, s32[8]{0:T(128)S(1)} %copy-done.3, bf16[528,128]{1,0:T(8,128)(2,1)S(1)} %copy-done.2, bf16[528,128]{1,0:T(8,128)(2,1)S(1)} %collective-permute-done.refs_1_.refs_6_), custom_call_target="tpu_custom_call" | custom-call | flops 3276800 | bytes 655360 | tf_op jit(solution)/shard_map/prepare/pallas_call | solution.py:234
  17.5 1.1 %collective-permute-done.3.refs_4_.refs_9_ = bf16[528,128]{1,0:T(8,128)(2,1)S(1)} collective-permute-done((bf16[528,128]{1,0:T(8,128)(2,1)S(1)}, bf16[528,128]{1,0:T(8,128)(2,1)S(1)}, u32[]{:S(2)}, u32[]{:S(2)}) %collective-permute-start.3) | collective-permute-done | bytes 135200 | tf_op jit(solution)/shard_map/ppermute | solution.py:477
  18.6 0.8 %collective-permute-start.6 = (bf16[528,128]{1,0:T(8,128)(2,1)S(1)}, bf16[528,128]{1,0:T(8,128)(2,1)S(1)}, u32[]{:S(2)}, u32[]{:S(2)}) collective-permute-start(bf16[528,128]{1,0:T(8,128)(2,1)S(1)} %collective-permute-done.3.refs_4_.refs_9_), channel_id=1, source_target_pairs={{0,4},{2,6},{4,12},{6,14},{12,8},{14,10},{8,0},{10,2},{1,5},{3,7},... | collective-permute-start | bytes 405512 | tf_op jit(solution)/shard_map/ppermute | solution.py:477
  19.3 1.6 %collective-permute-done.2.refs_3_.refs_8_ = bf16[528,128]{1,0:T(8,128)(2,1)S(1)} collective-permute-done((bf16[528,128]{1,0:T(8,128)(2,1)S(1)}, bf16[528,128]{1,0:T(8,128)(2,1)S(1)}, u32[]{:S(2)}, u32[]{:S(2)}) %collective-permute-start.2) | collective-permute-done | bytes 135200 | tf_op jit(solution)/shard_map/ppermute | solution.py:477
  21.0 0.0 collective-permute-done.4.refs_4_
  21.0 1.5 %collective-permute-start.5 = (bf16[528,128]{1,0:T(8,128)(2,1)S(1)}, bf16[528,128]{1,0:T(8,128)(2,1)S(1)}, u32[]{:S(2)}, u32[]{:S(2)}) collective-permute-start(bf16[528,128]{1,0:T(8,128)(2,1)S(1)} %collective-permute-done.2.refs_3_.refs_8_), channel_id=1, source_target_pairs={{0,4},{2,6},{4,12},{6,14},{12,8},{14,10},{8,0},{10,2},{1,5},{3,7},... | collective-permute-start | bytes 405512 | tf_op jit(solution)/shard_map/ppermute | solution.py:477
  22.5 1.5 %collective-permute-start.8 = (bf16[2,5,128,128]{3,2,1,0:T(8,128)(2,1)S(1)}, bf16[2,5,128,128]{3,2,1,0:T(8,128)(2,1)S(1)}, u32[]{:S(2)}, u32[]{:S(2)}) collective-permute-start(bf16[2,5,128,128]{3,2,1,0:T(8,128)(2,1)S(1)} %get-tuple-element.55), channel_id=1, source_target_pairs={{0,2},{2,0},{4,6},{6,4},{8,10},{10,8},{12,14},{14,12},{1,3},{3,1},... | collective-permute-start | bytes 983048 | tf_op jit(solution)/shard_map/ppermute | solution.py:477
  24.0 0.5 collective-permute-done.6.refs_6_.refs_11_
  24.5 3.1 %collective-permute-done.5.refs_5_.refs_10_ = bf16[528,128]{1,0:T(8,128)(2,1)S(1)} collective-permute-done((bf16[528,128]{1,0:T(8,128)(2,1)S(1)}, bf16[528,128]{1,0:T(8,128)(2,1)S(1)}, u32[]{:S(2)}, u32[]{:S(2)}) %collective-permute-start.5) | collective-permute-done | bytes 135200 | tf_op jit(solution)/shard_map/ppermute | solution.py:477
  27.6 0.2 collective-permute-start.7
  27.9 5.7 %collective-permute-done.7.refs_7_.refs_12_ = bf16[528,128]{1,0:T(8,128)(2,1)S(1)} collective-permute-done((bf16[528,128]{1,0:T(8,128)(2,1)S(1)}, bf16[528,128]{1,0:T(8,128)(2,1)S(1)}, u32[]{:S(2)}, u32[]{:S(2)}) %collective-permute-start.7) | collective-permute-done | bytes 135200 | tf_op jit(solution)/shard_map/ppermute | solution.py:477
  33.5 0.7 %advantages.1 = (f32[1,128]{1,0:T(1,128)}, f32[2,128,128]{2,1,0:T(8,128)S(1)}) custom-call(f32[2,3,128,128]{3,2,1,0:T(8,128)S(1)} %get-tuple-element.41.columns_ref, f32[2,2,8,128]{3,2,1,0:T(8,128)S(1)} %get-tuple-element.42.weights_ref, bf16[528,128]{1,0:T(8,128)(2,1)S(1)} %copy-done.2, bf16[528,128]{1,0:T(8,128)(2,1)S(1)} %collective-permute-done.refs_1_.refs_6_, ...), custom_call_target="tpu_custom_call" | custom-call | flops 327680 | bytes 524288 | tf_op jit(solution)/shard_map/advantages/pallas_call | solution.py:287
  34.2 4.4 %tree_attention_backward.2 = (bf16[128,640]{1,0:T(8,128)(2,1)S(1)}, bf16[128,640]{1,0:T(8,128)(2,1)S(1)}, bf16[2,2,128,128]{3,2,1,0:T(8,128)(2,1)S(1)}, bf16[2,2...) custom-call(s32[8]{0:T(128)S(1)} %copy-done.4, ...), custom_call_target="tpu_custom_call" | custom-call | flops 1048576000 | bytes 8388608 | tf_op jit(solution)/shard_map/tree_attention_backward/pallas_call | solution.py:391
  38.7 0.3 collective-permute-start.11
  39.0 2.9 %collective-permute-start.12 = (bf16[2,2,128,128]{3,2,1,0:T(8,128)(2,1)S(1)}, bf16[2,2,128,128]{3,2,1,0:T(8,128)(2,1)S(1)}, u32[]{:S(2)}, u32[]{:S(2)}) collective-permute-start(bf16[2,2,128,128]{3,2,1,0:T(8,128)(2,1)S(1)} %get-tuple-element.62), channel_id=1, source_target_pairs={{0,12},{2,14},{4,8},{6,10},{12,0},{14,2},{8,4},{10,6},{1,13},{3,15... | collective-permute-start | bytes 393224 | tf_op jit(solution)/shard_map/ppermute | solution.py:477
  41.9 1.9 %collective-permute-start.13 = (bf16[2,2,128,128]{3,2,1,0:T(8,128)(2,1)S(1)}, bf16[2,2,128,128]{3,2,1,0:T(8,128)(2,1)S(1)}, u32[]{:S(2)}, u32[]{:S(2)}) collective-permute-start(bf16[2,2,128,128]{3,2,1,0:T(8,128)(2,1)S(1)} %get-tuple-element.63), channel_id=1, source_target_pairs={{0,8},{2,10},{4,0},{6,2},{12,4},{14,6},{8,12},{10,14},{1,9},{3,11}... | collective-permute-start | bytes 393224 | tf_op jit(solution)/shard_map/ppermute | solution.py:477
  43.8 1.5 %collective-permute-start.9 = (bf16[128,640]{1,0:T(8,128)(2,1)S(1)}, bf16[128,640]{1,0:T(8,128)(2,1)S(1)}, u32[]{:S(2)}, u32[]{:S(2)}) collective-permute-start(bf16[128,640]{1,0:T(8,128)(2,1)S(1)} %get-tuple-element.57), channel_id=1, source_target_pairs={{0,2},{2,0},{4,6},{6,4},{8,10},{10,8},{12,14},{14,12},{1,3},{3,1},... | collective-permute-start | bytes 491528 | tf_op jit(solution)/shard_map/ppermute | solution.py:477
  45.3 0.0 collective-permute-done.8.refs_4_
  45.3 4.4 %tree_attention_backward.3 = (bf16[128,640]{1,0:T(8,128)(2,1)S(1)}, bf16[128,640]{1,0:T(8,128)(2,1)S(1)}, bf16[2,2,128,128]{3,2,1,0:T(8,128)(2,1)S(1)}, bf16[2,2...) custom-call(s32[8]{0:T(128)S(1)} %copy-done.4, ...), custom_call_target="tpu_custom_call" | custom-call | flops 1048576000 | bytes 8388608 | tf_op jit(solution)/shard_map/tree_attention_backward/pallas_call | solution.py:391
  49.7 0.1 collective-permute-start.15
  49.9 0.0 collective-permute-done.11.refs_3_
  49.9 1.4 %collective-permute-start.16 = (bf16[2,2,128,128]{3,2,1,0:T(8,128)(2,1)S(1)}, bf16[2,2,128,128]{3,2,1,0:T(8,128)(2,1)S(1)}, u32[]{:S(2)}, u32[]{:S(2)}) collective-permute-start(bf16[2,2,128,128]{3,2,1,0:T(8,128)(2,1)S(1)} %get-tuple-element.67), channel_id=1, source_target_pairs={{0,12},{2,14},{4,8},{6,10},{12,0},{14,2},{8,4},{10,6},{1,13},{3,15... | collective-permute-start | bytes 393224 | tf_op jit(solution)/shard_map/ppermute | solution.py:477
  51.2 0.0 collective-permute-done.12.refs_4_
  51.2 4.2 %collective-permute-start.17 = (bf16[2,2,128,128]{3,2,1,0:T(8,128)(2,1)S(1)}, bf16[2,2,128,128]{3,2,1,0:T(8,128)(2,1)S(1)}, u32[]{:S(2)}, u32[]{:S(2)}) collective-permute-start(bf16[2,2,128,128]{3,2,1,0:T(8,128)(2,1)S(1)} %get-tuple-element.68), channel_id=1, source_target_pairs={{0,8},{2,10},{4,0},{6,2},{12,4},{14,6},{8,12},{10,14},{1,9},{3,11}... | collective-permute-start | bytes 393224 | tf_op jit(solution)/shard_map/ppermute | solution.py:477
  55.5 0.0 collective-permute-done.13.refs_5_
  55.5 3.3 %collective-permute-start.10 = (bf16[128,640]{1,0:T(8,128)(2,1)S(1)}, bf16[128,640]{1,0:T(8,128)(2,1)S(1)}, u32[]{:S(2)}, u32[]{:S(2)}) collective-permute-start(bf16[128,640]{1,0:T(8,128)(2,1)S(1)} %get-tuple-element.58), channel_id=1, source_target_pairs={{0,2},{2,0},{4,6},{6,4},{8,10},{10,8},{12,14},{14,12},{1,3},{3,1},... | collective-permute-start | bytes 491528 | tf_op jit(solution)/shard_map/ppermute | solution.py:477
  58.8 0.0 collective-permute-done.15.refs_7_
  58.8 0.2 collective-permute-start.14
  59.0 0.0 collective-permute-done.16.refs_8_
  59.1 0.0 collective-permute-done.17.refs_9_
  59.1 2.3 %collective-permute-start.18 = (bf16[2,128,128]{2,1,0:T(8,128)(2,1)S(1)}, bf16[2,128,128]{2,1,0:T(8,128)(2,1)S(1)}, u32[]{:S(2)}, u32[]{:S(2)}) collective-permute-start(bf16[2,128,128]{2,1,0:T(8,128)(2,1)S(1)} %fusion.1), channel_id=1, source_target_pairs={{0,2},{2,0},{4,6},{6,4},{8,10},{10,8},{12,14},{14,12},{1,3},{3,1},... | collective-permute-start | bytes 196616 | tf_op jit(solution)/shard_map/ppermute | solution.py:477
  61.4 0.0 collective-permute-done.9.refs_2_
  61.4 0.7 %collective-permute-done.10.refs_3_ = bf16[128,640]{1,0:T(8,128)(2,1)S(1)} collective-permute-done((bf16[128,640]{1,0:T(8,128)(2,1)S(1)}, bf16[128,640]{1,0:T(8,128)(2,1)S(1)}, u32[]{:S(2)}, u32[]{:S(2)}) %collective-permute-start.10) | collective-permute-done | bytes 163872 | tf_op jit(solution)/shard_map/ppermute | solution.py:477
  62.1 0.9 %join_queries.1 = bf16[128,2560]{1,0:T(8,128)(2,1)} custom-call(bf16[128,640]{1,0:T(8,128)(2,1)S(1)} %get-tuple-element.52.refs_0_, bf16[128,640]{1,0:T(8,128)(2,1)S(1)} %get-tuple-element.56.refs_1_, bf16[128,640]{1,0:T(8,128)(2,1)S(1)} %collective-permute-done.9.refs_2_, bf16[128,640]{1,0:T(8,128)(2,1)S(1)} %collective-permute-done.10.refs_3_), custom_call_target="tpu_custom_call" | custom-call | bytes 1310720 | tf_op jit(solution)/shard_map/join_queries/pallas_call | solution.py:429
  63.0 0.2 collective-permute-done.14.refs_0_
  63.1 0.7 %collective-permute-done.18.refs_1_ = bf16[2,128,128]{2,1,0:T(8,128)(2,1)S(1)} collective-permute-done((bf16[2,128,128]{2,1,0:T(8,128)(2,1)S(1)}, bf16[2,128,128]{2,1,0:T(8,128)(2,1)S(1)}, u32[]{:S(2)}, u32[]{:S(2)}) %collective-permute-start.18) | collective-permute-done | bytes 65568 | tf_op jit(solution)/shard_map/ppermute | solution.py:477
  63.8 0.8 %join_keys.1 = (bf16[128,512]{1,0:T(8,128)(2,1)}, bf16[128,512]{1,0:T(8,128)(2,1)}) custom-call(bf16[2,128,128]{2,1,0:T(8,128)(2,1)S(1)} %collective-permute-done.14.refs_0_, bf16[2,128,128]{2,1,0:T(8,128)(2,1)S(1)} %collective-permute-done.18.refs_1_, bf16[2,2,128,128]{3,2,1,0:T(8,128)(2,1)S(1)} %get-tuple-element.60.refs_2_, ...), custom_call_target="tpu_custom_call" | custom-call | bytes 524288 | tf_op jit(solution)/shard_map/join_keys/pallas_call | solution.py:463
  (2 shorter events, 0.1 us)
Async XLA Ops:
  2.5 7.0 %collective-permute-start = (bf16[528,128]{1,0:T(8,128)(2,1)}, bf16[528,128]{1,0:T(8,128)(2,1)S(1)}, u32[]{:S(2)}, u32[]{:S(2)}) collective-permute-start(bf16[528,128]{1,0:T(8,128)(2,1)} %get-tuple-element.39), channel_id=1, source_target_pairs={{0,2},{2,0},{4,6},{6,4},{8,10},{10,8},{12,14},{14,12},{1,3},{3,1},... | collective-permute-start | bytes 405512 | tf_op jit(solution)/shard_map/ppermute | solution.py:477
  5.4 6.2 %collective-permute-start.1 = (bf16[528,128]{1,0:T(8,128)(2,1)}, bf16[528,128]{1,0:T(8,128)(2,1)S(1)}, u32[]{:S(2)}, u32[]{:S(2)}) collective-permute-start(bf16[528,128]{1,0:T(8,128)(2,1)} %get-tuple-element.38.refs_0_.refs_5_), channel_id=1, source_target_pairs={{0,4},{2,6},{4,12},{6,14},{12,8},{14,10},{8,0},{10,2},{1,5},{3,7},... | collective-permute-start | bytes 405512 | tf_op jit(solution)/shard_map/ppermute | solution.py:477
  7.0 1.1 %copy-start = (bf16[128,2560]{1,0:T(8,128)(2,1)S(1)}, bf16[128,2560]{1,0:T(8,128)(2,1)}, u32[]{:S(2)}) copy-start(bf16[128,2560]{1,0:T(8,128)(2,1)} %q_ref) | copy-start | bytes 1966084
  8.1 1.1 %copy-start.1 = (bf16[128,2560]{1,0:T(8,128)(2,1)S(1)}, bf16[128,2560]{1,0:T(8,128)(2,1)}, u32[]{:S(2)}) copy-start(bf16[128,2560]{1,0:T(8,128)(2,1)} %dir_ref.1) | copy-start | bytes 1966084
  9.2 7.1 %copy-start.2 = (bf16[528,128]{1,0:T(8,128)(2,1)S(1)}, bf16[528,128]{1,0:T(8,128)(2,1)}, u32[]{:S(2)}) copy-start(bf16[528,128]{1,0:T(8,128)(2,1)} %get-tuple-element.38.refs_0_.refs_5_) | copy-start | bytes 405508
  9.4 6.9 %copy-start.3 = (s32[8]{0:T(128)S(1)}, s32[8]{0:T(128)}, u32[]{:S(2)}) copy-start(s32[8]{0:T(128)} %lengths_s.1) | copy-start | bytes 100
  9.4 6.9 %copy-start.4 = (s32[8]{0:T(128)S(1)}, s32[8]{0:T(128)}, u32[]{:S(2)}) copy-start(s32[8]{0:T(128)} %refs_0_.3) | copy-start | bytes 100
  11.6 9.4 %collective-permute-start.4 = (bf16[2,5,128,128]{3,2,1,0:T(8,128)(2,1)S(1)}, bf16[2,5,128,128]{3,2,1,0:T(8,128)(2,1)S(1)}, u32[]{:S(2)}, u32[]{:S(2)}) collective-permute-start(bf16[2,5,128,128]{3,2,1,0:T(8,128)(2,1)S(1)} %get-tuple-element.46), channel_id=1, source_target_pairs={{0,2},{2,0},{4,6},{6,4},{8,10},{10,8},{12,14},{14,12},{1,3},{3,1},... | collective-permute-start | bytes 983048 | tf_op jit(solution)/shard_map/ppermute | solution.py:477
  12.1 6.5 %collective-permute-start.3 = (bf16[528,128]{1,0:T(8,128)(2,1)S(1)}, bf16[528,128]{1,0:T(8,128)(2,1)S(1)}, u32[]{:S(2)}, u32[]{:S(2)}) collective-permute-start(bf16[528,128]{1,0:T(8,128)(2,1)S(1)} %collective-permute-done.1.refs_2_.refs_7_), channel_id=1, source_target_pairs={{0,4},{2,6},{4,12},{6,14},{12,8},{14,10},{8,0},{10,2},{1,5},{3,7},... | collective-permute-start | bytes 405512 | tf_op jit(solution)/shard_map/ppermute | solution.py:477
  13.0 8.0 %collective-permute-start.2 = (bf16[528,128]{1,0:T(8,128)(2,1)S(1)}, bf16[528,128]{1,0:T(8,128)(2,1)S(1)}, u32[]{:S(2)}, u32[]{:S(2)}) collective-permute-start(bf16[528,128]{1,0:T(8,128)(2,1)S(1)} %collective-permute-done.refs_1_.refs_6_), channel_id=1, source_target_pairs={{0,4},{2,6},{4,12},{6,14},{12,8},{14,10},{8,0},{10,2},{1,5},{3,7},... | collective-permute-start | bytes 405512 | tf_op jit(solution)/shard_map/ppermute | solution.py:477
  18.6 5.9 %collective-permute-start.6 = (bf16[528,128]{1,0:T(8,128)(2,1)S(1)}, bf16[528,128]{1,0:T(8,128)(2,1)S(1)}, u32[]{:S(2)}, u32[]{:S(2)}) collective-permute-start(bf16[528,128]{1,0:T(8,128)(2,1)S(1)} %collective-permute-done.3.refs_4_.refs_9_), channel_id=1, source_target_pairs={{0,4},{2,6},{4,12},{6,14},{12,8},{14,10},{8,0},{10,2},{1,5},{3,7},... | collective-permute-start | bytes 405512 | tf_op jit(solution)/shard_map/ppermute | solution.py:477
  21.0 6.6 %collective-permute-start.5 = (bf16[528,128]{1,0:T(8,128)(2,1)S(1)}, bf16[528,128]{1,0:T(8,128)(2,1)S(1)}, u32[]{:S(2)}, u32[]{:S(2)}) collective-permute-start(bf16[528,128]{1,0:T(8,128)(2,1)S(1)} %collective-permute-done.2.refs_3_.refs_8_), channel_id=1, source_target_pairs={{0,4},{2,6},{4,12},{6,14},{12,8},{14,10},{8,0},{10,2},{1,5},{3,7},... | collective-permute-start | bytes 405512 | tf_op jit(solution)/shard_map/ppermute | solution.py:477
  22.5 22.8 %collective-permute-start.8 = (bf16[2,5,128,128]{3,2,1,0:T(8,128)(2,1)S(1)}, bf16[2,5,128,128]{3,2,1,0:T(8,128)(2,1)S(1)}, u32[]{:S(2)}, u32[]{:S(2)}) collective-permute-start(bf16[2,5,128,128]{3,2,1,0:T(8,128)(2,1)S(1)} %get-tuple-element.55), channel_id=1, source_target_pairs={{0,2},{2,0},{4,6},{6,4},{8,10},{10,8},{12,14},{14,12},{1,3},{3,1},... | collective-permute-start | bytes 983048 | tf_op jit(solution)/shard_map/ppermute | solution.py:477
  27.6 5.9 %collective-permute-start.7 = (bf16[528,128]{1,0:T(8,128)(2,1)S(1)}, bf16[528,128]{1,0:T(8,128)(2,1)S(1)}, u32[]{:S(2)}, u32[]{:S(2)}) collective-permute-start(bf16[528,128]{1,0:T(8,128)(2,1)S(1)} %collective-permute-done.5.refs_5_.refs_10_), channel_id=1, source_target_pairs={{0,4},{2,6},{4,12},{6,14},{12,8},{14,10},{8,0},{10,2},{1,5},{3,7},... | collective-permute-start | bytes 405512 | tf_op jit(solution)/shard_map/ppermute | solution.py:477
  38.7 11.2 %collective-permute-start.11 = (bf16[2,2,128,128]{3,2,1,0:T(8,128)(2,1)S(1)}, bf16[2,2,128,128]{3,2,1,0:T(8,128)(2,1)S(1)}, u32[]{:S(2)}, u32[]{:S(2)}) collective-permute-start(bf16[2,2,128,128]{3,2,1,0:T(8,128)(2,1)S(1)} %get-tuple-element.61), channel_id=1, source_target_pairs={{0,4},{2,6},{4,12},{6,14},{12,8},{14,10},{8,0},{10,2},{1,5},{3,7},... | collective-permute-start | bytes 393224 | tf_op jit(solution)/shard_map/ppermute | solution.py:477
  39.0 12.3 %collective-permute-start.12 = (bf16[2,2,128,128]{3,2,1,0:T(8,128)(2,1)S(1)}, bf16[2,2,128,128]{3,2,1,0:T(8,128)(2,1)S(1)}, u32[]{:S(2)}, u32[]{:S(2)}) collective-permute-start(bf16[2,2,128,128]{3,2,1,0:T(8,128)(2,1)S(1)} %get-tuple-element.62), channel_id=1, source_target_pairs={{0,12},{2,14},{4,8},{6,10},{12,0},{14,2},{8,4},{10,6},{1,13},{3,15... | collective-permute-start | bytes 393224 | tf_op jit(solution)/shard_map/ppermute | solution.py:477
  41.9 13.6 %collective-permute-start.13 = (bf16[2,2,128,128]{3,2,1,0:T(8,128)(2,1)S(1)}, bf16[2,2,128,128]{3,2,1,0:T(8,128)(2,1)S(1)}, u32[]{:S(2)}, u32[]{:S(2)}) collective-permute-start(bf16[2,2,128,128]{3,2,1,0:T(8,128)(2,1)S(1)} %get-tuple-element.63), channel_id=1, source_target_pairs={{0,8},{2,10},{4,0},{6,2},{12,4},{14,6},{8,12},{10,14},{1,9},{3,11}... | collective-permute-start | bytes 393224 | tf_op jit(solution)/shard_map/ppermute | solution.py:477
  43.8 17.6 %collective-permute-start.9 = (bf16[128,640]{1,0:T(8,128)(2,1)S(1)}, bf16[128,640]{1,0:T(8,128)(2,1)S(1)}, u32[]{:S(2)}, u32[]{:S(2)}) collective-permute-start(bf16[128,640]{1,0:T(8,128)(2,1)S(1)} %get-tuple-element.57), channel_id=1, source_target_pairs={{0,2},{2,0},{4,6},{6,4},{8,10},{10,8},{12,14},{14,12},{1,3},{3,1},... | collective-permute-start | bytes 491528 | tf_op jit(solution)/shard_map/ppermute | solution.py:477
  49.7 9.1 %collective-permute-start.15 = (bf16[2,2,128,128]{3,2,1,0:T(8,128)(2,1)S(1)}, bf16[2,2,128,128]{3,2,1,0:T(8,128)(2,1)S(1)}, u32[]{:S(2)}, u32[]{:S(2)}) collective-permute-start(bf16[2,2,128,128]{3,2,1,0:T(8,128)(2,1)S(1)} %get-tuple-element.66), channel_id=1, source_target_pairs={{0,4},{2,6},{4,12},{6,14},{12,8},{14,10},{8,0},{10,2},{1,5},{3,7},... | collective-permute-start | bytes 393224 | tf_op jit(solution)/shard_map/ppermute | solution.py:477
  49.9 9.2 %collective-permute-start.16 = (bf16[2,2,128,128]{3,2,1,0:T(8,128)(2,1)S(1)}, bf16[2,2,128,128]{3,2,1,0:T(8,128)(2,1)S(1)}, u32[]{:S(2)}, u32[]{:S(2)}) collective-permute-start(bf16[2,2,128,128]{3,2,1,0:T(8,128)(2,1)S(1)} %get-tuple-element.67), channel_id=1, source_target_pairs={{0,12},{2,14},{4,8},{6,10},{12,0},{14,2},{8,4},{10,6},{1,13},{3,15... | collective-permute-start | bytes 393224 | tf_op jit(solution)/shard_map/ppermute | solution.py:477
  51.2 7.8 %collective-permute-start.17 = (bf16[2,2,128,128]{3,2,1,0:T(8,128)(2,1)S(1)}, bf16[2,2,128,128]{3,2,1,0:T(8,128)(2,1)S(1)}, u32[]{:S(2)}, u32[]{:S(2)}) collective-permute-start(bf16[2,2,128,128]{3,2,1,0:T(8,128)(2,1)S(1)} %get-tuple-element.68), channel_id=1, source_target_pairs={{0,8},{2,10},{4,0},{6,2},{12,4},{14,6},{8,12},{10,14},{1,9},{3,11}... | collective-permute-start | bytes 393224 | tf_op jit(solution)/shard_map/ppermute | solution.py:477
  55.5 6.6 %collective-permute-start.10 = (bf16[128,640]{1,0:T(8,128)(2,1)S(1)}, bf16[128,640]{1,0:T(8,128)(2,1)S(1)}, u32[]{:S(2)}, u32[]{:S(2)}) collective-permute-start(bf16[128,640]{1,0:T(8,128)(2,1)S(1)} %get-tuple-element.58), channel_id=1, source_target_pairs={{0,2},{2,0},{4,6},{6,4},{8,10},{10,8},{12,14},{14,12},{1,3},{3,1},... | collective-permute-start | bytes 491528 | tf_op jit(solution)/shard_map/ppermute | solution.py:477
  58.8 4.3 %collective-permute-start.14 = (bf16[2,128,128]{2,1,0:T(8,128)(2,1)S(1)}, bf16[2,128,128]{2,1,0:T(8,128)(2,1)S(1)}, u32[]{:S(2)}, u32[]{:S(2)}) collective-permute-start(bf16[2,128,128]{2,1,0:T(8,128)(2,1)S(1)} %fusion), channel_id=1, source_target_pairs={{0,2},{2,0},{4,6},{6,4},{8,10},{10,8},{12,14},{14,12},{1,3},{3,1},... | collective-permute-start | bytes 196616 | tf_op jit(solution)/shard_map/ppermute | solution.py:477
  59.1 4.7 %collective-permute-start.18 = (bf16[2,128,128]{2,1,0:T(8,128)(2,1)S(1)}, bf16[2,128,128]{2,1,0:T(8,128)(2,1)S(1)}, u32[]{:S(2)}, u32[]{:S(2)}) collective-permute-start(bf16[2,128,128]{2,1,0:T(8,128)(2,1)S(1)} %fusion.1), channel_id=1, source_target_pairs={{0,2},{2,0},{4,6},{6,4},{8,10},{10,8},{12,14},{14,12},{1,3},{3,1},... | collective-permute-start | bytes 196616 | tf_op jit(solution)/shard_map/ppermute | solution.py:477

commit v10 on v9

--- a/solution.py
+++ b/solution.py
@@ -57,6 +57,7 @@
 
 def pack_kernel(
     log_rate,
+    parts,
     lengths_ref,
     k_ref,
     v_ref,
@@ -68,8 +69,7 @@
 ):
     own = lax.axis_index("seg")
     length = k_ref.shape[0]
-    parts = len(out_refs)
-    heads = k_ref.shape[1] // HD // parts
+    heads = len(out_refs) // parts
     terms = token_terms(
         log_rate,
         lengths_ref[own],
@@ -81,14 +81,14 @@
     tail = [part.astype(jnp.float32) for x in terms for part in split_float(x)]
     tail.append(jnp.zeros((TERM_ROWS - len(tail), HD), jnp.float32))
     tail = jnp.concatenate(tail).astype(jnp.bfloat16)
-    for step, out_ref in enumerate(out_refs):
+    for index, out_ref in enumerate(out_refs):
+        step, h = divmod(index, heads)
         part = lax.rem(own + step, parts)
-        for h in range(heads):
-            columns = pl.ds(pl.multiple_of((part * heads + h) * HD, HD), HD)
-            for plane, ref in enumerate((k_ref, v_ref)):
-                first = (h * 2 + plane) * length
-                out_ref[first : first + length, :] = ref[:, columns]
-        out_ref[2 * heads * length :, :] = tail
+        columns = pl.ds(pl.multiple_of((part * heads + h) * HD, HD), HD)
+        out_ref[:length, :] = k_ref[:, columns]
+        out_ref[length : 2 * length, :] = v_ref[:, columns]
+        if h == 0:
+            out_ref[2 * length :, :] = tail
 
 
 def pack(lengths, k, v, token_rows, parts, log_rate):
@@ -97,17 +97,40 @@
     vmem = pl.BlockSpec(memory_space=pltpu.VMEM)
     heads = width // HD // parts
     assert length == HD
-    block = jax.ShapeDtypeStruct((2 * heads * length + TERM_ROWS, HD), k.dtype)
-    return pl.pallas_call(
-        functools.partial(pack_kernel, log_rate),
-        out_shape=(block,) * parts,
+    blocks = [
+        jax.ShapeDtypeStruct((2 * length + (TERM_ROWS if h == 0 else 0), HD), k.dtype)
+        for h in range(heads)
+    ]
+    outs = pl.pallas_call(
+        functools.partial(pack_kernel, log_rate, parts),
+        out_shape=blocks * parts,
         in_specs=[smem] + [vmem] * 6,
-        out_specs=(vmem,) * parts,
+        out_specs=[vmem] * (heads * parts),
         cost_estimate=pl.CostEstimate(
             flops=length * 100, bytes_accessed=8 * length * width, transcendentals=length
         ),
         name="pack_keys_values",
     )(lengths, k, v, *token_rows)
+    return [outs[step * heads : (step + 1) * heads] for step in range(parts)]
+
+
+def join_blocks_kernel(mine_ref, other_ref, out_ref):
+    rows = mine_ref.shape[0]
+    out_ref[:rows, :] = mine_ref[...]
+    out_ref[rows:, :] = other_ref[...]
+
+
+def join_blocks(mine, other):
+    vmem = pl.BlockSpec(memory_space=pltpu.VMEM)
+    return pl.pallas_call(
+        join_blocks_kernel,
+        out_shape=jax.ShapeDtypeStruct((2 * mine.shape[0], HD), mine.dtype),
+        in_specs=[vmem] * 2,
+        out_specs=vmem,
+        cost_estimate=pl.CostEstimate(flops=0, bytes_accessed=8 * mine.size, transcendentals=0),
+        compiler_params=SMALL,
+        name="join_blocks",
+    )(mine, other)
 
 
 def pack_queries_kernel(parts, q_ref, dir_ref, *out_refs):
@@ -154,11 +177,11 @@
     return own - part + lax.rem(part + i, segs)
 
 
-def read_terms(ref):
+def read_terms(ref, end=None):
     if ref.dtype == jnp.float32:
         length = ref.shape[1] // 2
         return ref[:, :length], ref[:, length:]
-    tail = ref[ref.shape[0] - TERM_ROWS :, :].astype(jnp.float32)
+    tail = ref[end - TERM_ROWS : end, :].astype(jnp.float32)
     return tail[0:1] + tail[1:2] + tail[2:3], tail[3:4] + tail[4:5] + tail[5:6]
 
 
@@ -195,7 +218,7 @@
     for i in range(segs):
         seg = segment_of(own, segs, i)
         seg_len = lengths_s[seg]
-        deltas, _ = read_terms(term_refs[i])
+        deltas, _ = read_terms(term_refs[i], term_refs[i].shape[0])
         live = t_col < seg_len
         left = (seg_len - t_col).astype(jnp.float32)
         columns = (
@@ -261,11 +284,12 @@
         part, pair, pairs = lax.rem(own, segs), own // segs, count // segs
         seg_id = lax.broadcasted_iota(jnp.int32, (count, length), 0)
         firsts = jnp.zeros((count, length), jnp.float32)
-        for index, ref in enumerate(term_refs):
-            step, side = divmod(index, segs)
+        for step, ref in enumerate(term_refs):
             place = lax.rem(ring_place(pair) - step + pairs, pairs)
-            seg = ring_place(place) * segs + lax.rem(part + side, segs)
-            firsts = jnp.where(seg_id == seg, read_terms(ref)[1], firsts)
+            for side in range(segs):
+                seg = ring_place(place) * segs + lax.rem(part + side, segs)
+                end = (side + 1) * (ref.shape[0] // segs)
+                firsts = jnp.where(seg_id == seg, read_terms(ref, end)[1], firsts)
     for i in range(segs):
         later_value = jnp.sum(weights_ref[i, 0] * firsts, axis=(0, 1), keepdims=True)
         later_head = jnp.sum(weights_ref[i, 1] * firsts, axis=(0, 1), keepdims=True)
@@ -300,20 +324,20 @@
     )(columns, weights, *terms)
 
 
-def attend_kernel(depth, chunk, segs, sources, group_size, *refs):
+def attend_kernel(depth, segs, steps, group_size, *refs):
     parents_s, adv_ref, bias_ref = refs[:3]
-    query_refs, kv_refs = refs[3 : 3 + segs], refs[3 + segs : 3 + segs + sources]
+    query_refs, kv_refs = refs[3 : 3 + segs], refs[3 + segs : 3 + segs + steps]
     kv_scr, p_scr, ds_scr, acc_scr = refs[-4:]
-    refs = refs[3 + segs + sources : -4]
-    steps = sources // segs
+    refs = refs[3 + segs + steps : -4]
     dkv_refs, dq_refs = refs[-steps:], refs[-steps - segs : -steps]
 
     length = query_refs[0].shape[2]
     own = lax.axis_index("seg")
-    for source in range(sources):
+    for source in range(steps * segs):
+        step, side = divmod(source, segs)
         for plane in range(2):
-            rows = slice((2 * chunk + plane) * length, (2 * chunk + plane + 1) * length)
-            kv_scr[source, plane] = kv_refs[source][rows, :]
+            first = side * (kv_refs[step].shape[0] // segs) + plane * length
+            kv_scr[source, plane] = kv_refs[step][first : first + length, :]
     acc_scr[...] = jnp.zeros_like(acc_scr)
 
     scale = HD**-0.5
@@ -331,7 +355,7 @@
             else:
                 known = jnp.maximum(ancestor, 0)
                 step = ring_place((own - part) // segs) - ring_place(known // segs)
-                step = lax.rem(step + sources // segs, sources // segs)
+                step = lax.rem(step + steps, steps)
                 turn = lax.rem(lax.rem(known, segs) - part + segs, segs)
                 chosen.append(jnp.where(ancestor >= 0, step * segs + turn, 0))
         q_list = [query_refs[i][0, j] for j in range(group_size)]
@@ -377,10 +401,10 @@
             dkv_refs[step][i] = acc_scr[step * segs + i].astype(jnp.bfloat16)
 
 
-def attend(parents, advantages, bias, query_list, kv_list, chunk):
+def attend(parents, advantages, bias, query_list, kv_list):
     segs, length = advantages.shape[:2]
-    sources = len(kv_list)
-    steps = sources // segs
+    steps = len(kv_list)
+    sources = steps * segs
     group_size = query_list[0].shape[1]
     width = group_size * HD
     keys = DEPTH * length
@@ -389,9 +413,9 @@
     out_shape = [jax.ShapeDtypeStruct((length, width), jnp.bfloat16)] * segs
     out_shape += [jax.ShapeDtypeStruct((segs, 2, length, HD), jnp.bfloat16)] * steps
     outs = pl.pallas_call(
-        functools.partial(attend_kernel, DEPTH, chunk, segs, sources, group_size),
+        functools.partial(attend_kernel, DEPTH, segs, steps, group_size),
         out_shape=out_shape,
-        in_specs=[smem] + [vmem] * (2 + segs + sources),
+        in_specs=[smem] + [vmem] * (2 + segs + steps),
         out_specs=[vmem] * len(out_shape),
         scratch_shapes=[
             pltpu.VMEM((sources, 2, length, HD), jnp.bfloat16),
@@ -500,26 +524,28 @@
     down = {d: turn(-d) for d in steps}
 
     kept, given = pack(lengths, key_vectors, value_vectors, token_rows, 2, log_rate)
-    taken = permute(given, swap)
-    chain = [kept, permute(kept, climb)]
-    other = [after(taken, chain[1])]
-    kept_q, given_q = pack_queries(after(queries, kept), direction, 2, chunks)
-    taken_q = [permute(after(given_q[0], *other), swap)]
-    bias, columns, weights = prepare(parents, lengths, [kept, other[0]], length, log_rate)
-    for step in steps:
-        if step + 1 in steps:
-            chain.append(permute(chain[-1], climb))
-        gate = [bias, taken_q[0]] if step == 1 else []
-        other.append(after(permute(other[-1], climb), chain[-1], *gate))
-    for block in given_q[1:]:
-        taken_q.append(permute(after(block, taken_q[-1]), swap))
-    blocks = [block for pair in zip(chain, other) for block in pair]
-    row, advantages = advantages_of(columns, weights, blocks)
+    taken = [permute(block, swap) for block in given]
+    kept_q, given_q = pack_queries(after(queries, kept[0]), direction, 2, chunks)
+    bias, columns, weights = prepare(parents, lengths, [kept[0], taken[0]], length, log_rate)
+    near = [
+        join_blocks(mine, after(other, *kept_q) if chunk == 0 else other)
+        for chunk, (mine, other) in enumerate(zip(kept, taken))
+    ]
+    chain = [near[0]]
+    for gate in ([], near[1:], [bias]):
+        chain.append(permute(after(chain[-1], *gate), climb))
+    chains = [chain]
+    taken_q = [permute(after(given_q[0], chain[1]), swap)]
+    for chunk in range(1, chunks):
+        block, query_block = lax.optimization_barrier((near[chunk], given_q[chunk], bias, chain[-1]))[:2]
+        chains.append([block] + [permute(block, turn(d)) for d in steps])
+        taken_q.append(permute(query_block, swap))
+    row, advantages = advantages_of(columns, weights, chains[0])
 
     dq_own, dq_back, dkv_list = [], [], []
     for chunk in range(chunks):
         query_list = [kept_q[chunk], taken_q[chunk]]
-        dq, dkv = attend(parents, advantages, bias, query_list, blocks, chunk)
+        dq, dkv = attend(parents, advantages, bias, query_list, chains[chunk])
         dq_own.append(dq[0])
         dq_back.append(dq[1])
         dkv_list.append(dkv)
@@ -578,12 +604,12 @@
     chains = ancestors(parents, DEPTH - 1)
     arrived = fetch_rows(spread, chains)[0]
     slot_kv = jnp.concatenate([flat, arrived]).reshape(DEPTH, length, 2, heads, HD)
-    slot_kv = jnp.transpose(slot_kv, (0, 3, 2, 1, 4)).reshape(DEPTH, -1, HD)
-    kv_list = [slot_kv[slot] for slot in range(DEPTH)]
+    slot_kv = jnp.transpose(slot_kv, (0, 3, 2, 1, 4)).reshape(DEPTH, heads, 2 * length, HD)
     (kept_q,) = pack_queries(queries, direction, 1, heads)
     dq_list, dkv_list = [], []
     for head in range(heads):
-        dq, dkv = attend(parents, advantages, bias, [kept_q[head]], kv_list, head)
+        kv_list = [slot_kv[slot, head] for slot in range(DEPTH)]
+        dq, dkv = attend(parents, advantages, bias, [kept_q[head]], kv_list)
         dq_list.append(dq[0])
         dkv_list.append(jnp.concatenate(dkv))
     rows = jnp.transpose(jnp.stack(dkv_list), (1, 3, 2, 0, 4)).reshape(1, DEPTH, length, -1)

time: 64.8 us -> 67.6 us (1.043)
  starting transfers between devices: 31.4 us -> 35.2 us
  waiting for transfers between devices: 15.7 us -> 14.1 us
    ppermute x19 -> x20, starting transfers between devices: 31.4 us -> 35.2 us  [permute(): return lax.ppermute(array, 'seg', pairs)]
    ppermute x19 -> x20, waiting for transfers between devices: 15.7 us -> 14.1 us  [permute(): return lax.ppermute(array, 'seg', pairs)]
    unnamed x10 -> x14, local copies, waits for them, and re-layouts: 2.19 us -> 2.75 us
    pallas_call x3 -> x5, Pallas kernels: 10.7 us -> 10.7 us  [the longest x2 8.84 us: attend(): pl.pallas_call(functools.partial(attend_kernel, DEPTH, segs, steps, group...]
  transfers between devices with their start and end apart: 19 -> 20, of which waited for: 9 -> 10; matrix products, arithmetic and copies ran while one was open for 0% -> 0% of each run, Pallas kernels for 18% -> 18%
where the time goes in v10:
time: 67.6 us; the launch traced here: 67.4 us
  starting transfers between devices  35.2 us (52%)
  Pallas kernels  14.5 us (21%)
  waiting for transfers between devices  14.1 us (21%)
  local copies, waits for them, and re-layouts  2.75 us (4%)
  between operations  0.71 us (1%)
    ppermute x20, starting transfers between devices, permute(): return lax.ppermute(array, 'seg', pairs)  35.2 us
    ppermute x20, waiting for transfers between devices, permute(): return lax.ppermute(array, 'seg', pairs)  14.1 us
    pallas_call x2, Pallas kernels, attend(): pl.pallas_call(functools.partial(attend_kernel, DEPTH, segs, steps, group...  8.84 us
    unnamed x14, local copies, waits for them, and re-layouts  2.75 us
    pallas_call x1, Pallas kernels, pack(): pl.pallas_call(functools.partial(pack_kernel, log_rate, parts), out_shape...  1.81 us
  transfers between devices with their start and end apart: 20, of which 10 were waited for; matrix products, arithmetic and copies ran while one was open for 0% of the time, Pallas kernels for 18%

profile of v10, /device:TPU:0, one launch (start us, length us, event | category | flops | bytes accessed | tf_op | source)
XLA Modules:
  0.0 67.4 jit_solution(6682652426257038651)
XLA Ops:
  0.6 1.8 %pack_keys_values.1 = (bf16[272,128]{1,0:T(8,128)(2,1)}, bf16[256,128]{1,0:T(8,128)(2,1)}, bf16[272,128]{1,0:T(8,128)(2,1)}, bf16[256,128]{1,0:T(8,128)(2,1)}) custom-call(s32[8]{0:T(128)} %lengths_s.1, bf16[128,512]{1,0:T(8,128)(2,1)} %k_ref.1, bf16[128,512]{1,0:T(8,128)(2,1)} %v_ref.1, f32[1,128]{1,0:T(1,128)} %bitcast.9, f32[1,128]{1,0:T(1,128)} %bitcast.10, ...), custom_call_target="tpu_custom_call" | custom-call | flops 12800 | bytes 524288 | tf_op jit(solution)/shard_map/pack_keys_values/pallas_call | solution.py:104
  2.4 2.9 %collective-permute-start = (bf16[272,128]{1,0:T(8,128)(2,1)}, bf16[272,128]{1,0:T(8,128)(2,1)S(1)}, u32[]{:S(2)}, u32[]{:S(2)}) collective-permute-start(bf16[272,128]{1,0:T(8,128)(2,1)} %get-tuple-element.41), channel_id=1, source_target_pairs={{0,2},{2,0},{4,6},{6,4},{8,10},{10,8},{12,14},{14,12},{1,3},{3,1},... | collective-permute-start | bytes 208904 | tf_op jit(solution)/shard_map/ppermute | solution.py:501
  5.4 0.0 copy-start
  5.4 1.1 %copy-done = bf16[128,2560]{1,0:T(8,128)(2,1)S(1)} copy-done((bf16[128,2560]{1,0:T(8,128)(2,1)S(1)}, bf16[128,2560]{1,0:T(8,128)(2,1)}, u32[]{:S(2)}) %copy-start) | copy-done | bytes 655384
  6.5 0.0 copy-start.1
  6.5 1.1 %copy-done.1 = bf16[128,2560]{1,0:T(8,128)(2,1)S(1)} copy-done((bf16[128,2560]{1,0:T(8,128)(2,1)S(1)}, bf16[128,2560]{1,0:T(8,128)(2,1)}, u32[]{:S(2)}) %copy-start.1) | copy-done | bytes 655384
  7.6 0.0 copy-start.2
  7.6 0.2 pack_queries.1
  7.8 0.1 collective-permute-done.refs_1_.other_ref
  7.9 0.6 copy-done.2
  8.4 0.0 copy-start.6
  8.4 0.0 copy-start.3
  8.5 1.6 %collective-permute-start.1 = (bf16[544,128]{1,0:T(8,128)(2,1)S(1)}, bf16[544,128]{1,0:T(8,128)(2,1)S(1)}, u32[]{:S(2)}, u32[]{:S(2)}) collective-permute-start(bf16[544,128]{1,0:T(8,128)(2,1)S(1)} %join_blocks.2.refs_0_.refs_5_), channel_id=1, source_target_pairs={{0,4},{2,6},{4,12},{6,14},{12,8},{14,10},{8,0},{10,2},{1,5},{3,7},... | collective-permute-start | bytes 417800 | tf_op jit(solution)/shard_map/ppermute | solution.py:501
  10.1 0.0 copy-done.6
  10.1 1.5 %collective-permute-start.2 = (bf16[256,128]{1,0:T(8,128)(2,1)S(1)}, bf16[256,128]{1,0:T(8,128)(2,1)S(1)}, u32[]{:S(2)}, u32[]{:S(2)}) collective-permute-start(bf16[256,128]{1,0:T(8,128)(2,1)S(1)} %copy-done.6), channel_id=1, source_target_pairs={{0,2},{2,0},{4,6},{6,4},{8,10},{10,8},{12,14},{14,12},{1,3},{3,1},... | collective-permute-start | bytes 196616 | tf_op jit(solution)/shard_map/ppermute | solution.py:501
  11.6 2.8 %collective-permute-done.2.other_ref = bf16[256,128]{1,0:T(8,128)(2,1)S(1)} collective-permute-done((bf16[256,128]{1,0:T(8,128)(2,1)S(1)}, bf16[256,128]{1,0:T(8,128)(2,1)S(1)}, u32[]{:S(2)}, u32[]{:S(2)}) %collective-permute-start.2) | collective-permute-done | bytes 65568 | tf_op jit(solution)/shard_map/ppermute | solution.py:501
  14.4 0.0 copy-done.3
  14.4 0.0 copy-start.4
  14.4 0.0 copy-start.5
  14.4 0.2 collective-permute-done.1.refs_1_.refs_6_
  14.5 2.5 %collective-permute-start.3 = (bf16[544,128]{1,0:T(8,128)(2,1)S(1)}, bf16[544,128]{1,0:T(8,128)(2,1)S(1)}, u32[]{:S(2)}, u32[]{:S(2)}) collective-permute-start(bf16[544,128]{1,0:T(8,128)(2,1)S(1)} %collective-permute-done.1.refs_1_.refs_6_), channel_id=1, source_target_pairs={{0,4},{2,6},{4,12},{6,14},{12,8},{14,10},{8,0},{10,2},{1,5},{3,7},... | collective-permute-start | bytes 417800 | tf_op jit(solution)/shard_map/ppermute | solution.py:501
  17.0 0.0 copy-done.4
  17.0 0.0 copy-done.5
  17.0 1.2 %prepare.1 = (f32[2,640,128]{2,1,0:T(8,128)S(1)}, f32[2,3,128,128]{3,2,1,0:T(8,128)S(1)}, f32[2,2,8,128]{3,2,1,0:T(8,128)S(1)}) custom-call(s32[8]{0:T(128)S(1)} %copy-done.5, s32[8]{0:T(128)S(1)} %copy-done.4, bf16[272,128]{1,0:T(8,128)(2,1)S(1)} %copy-done.2, bf16[272,128]{1,0:T(8,128)(2,1)S(1)} %collective-permute-done.refs_1_.other_ref), custom_call_target="tpu_custom_call" | custom-call | flops 3276800 | bytes 655360 | tf_op jit(solution)/shard_map/prepare/pallas_call | solution.py:257
  18.3 2.2 %collective-permute-done.3.refs_2_.refs_7_ = bf16[544,128]{1,0:T(8,128)(2,1)S(1)} collective-permute-done((bf16[544,128]{1,0:T(8,128)(2,1)S(1)}, bf16[544,128]{1,0:T(8,128)(2,1)S(1)}, u32[]{:S(2)}, u32[]{:S(2)}) %collective-permute-start.3) | collective-permute-done | bytes 139296 | tf_op jit(solution)/shard_map/ppermute | solution.py:501
  20.5 1.7 %collective-permute-start.4 = (bf16[544,128]{1,0:T(8,128)(2,1)S(1)}, bf16[544,128]{1,0:T(8,128)(2,1)S(1)}, u32[]{:S(2)}, u32[]{:S(2)}) collective-permute-start(bf16[544,128]{1,0:T(8,128)(2,1)S(1)} %collective-permute-done.3.refs_2_.refs_7_), channel_id=1, source_target_pairs={{0,4},{2,6},{4,12},{6,14},{12,8},{14,10},{8,0},{10,2},{1,5},{3,7},... | collective-permute-start | bytes 417800 | tf_op jit(solution)/shard_map/ppermute | solution.py:501
  22.2 2.4 %collective-permute-start.5 = (bf16[2,5,128,128]{3,2,1,0:T(8,128)(2,1)S(1)}, bf16[2,5,128,128]{3,2,1,0:T(8,128)(2,1)S(1)}, u32[]{:S(2)}, u32[]{:S(2)}) collective-permute-start(bf16[2,5,128,128]{3,2,1,0:T(8,128)(2,1)S(1)} %get-tuple-element.55), channel_id=1, source_target_pairs={{0,2},{2,0},{4,6},{6,4},{8,10},{10,8},{12,14},{14,12},{1,3},{3,1},... | collective-permute-start | bytes 983048 | tf_op jit(solution)/shard_map/ppermute | solution.py:501
  24.6 1.8 %collective-permute-done.4.refs_3_.refs_8_ = bf16[544,128]{1,0:T(8,128)(2,1)S(1)} collective-permute-done((bf16[544,128]{1,0:T(8,128)(2,1)S(1)}, bf16[544,128]{1,0:T(8,128)(2,1)S(1)}, u32[]{:S(2)}, u32[]{:S(2)}) %collective-permute-start.4) | collective-permute-done | bytes 139296 | tf_op jit(solution)/shard_map/ppermute | solution.py:501
  26.5 2.2 %collective-permute-start.6 = (bf16[2,5,128,128]{3,2,1,0:T(8,128)(2,1)S(1)}, bf16[2,5,128,128]{3,2,1,0:T(8,128)(2,1)S(1)}, u32[]{:S(2)}, u32[]{:S(2)}) collective-permute-start(bf16[2,5,128,128]{3,2,1,0:T(8,128)(2,1)S(1)} %get-tuple-element.58), channel_id=1, source_target_pairs={{0,2},{2,0},{4,6},{6,4},{8,10},{10,8},{12,14},{14,12},{1,3},{3,1},... | collective-permute-start | bytes 983048 | tf_op jit(solution)/shard_map/ppermute | solution.py:501
  28.6 2.5 %collective-permute-start.7 = (bf16[512,128]{1,0:T(8,128)(2,1)S(1)}, bf16[512,128]{1,0:T(8,128)(2,1)S(1)}, u32[]{:S(2)}, u32[]{:S(2)}) collective-permute-start(bf16[512,128]{1,0:T(8,128)(2,1)S(1)} %join_blocks.3.refs_5_), channel_id=1, source_target_pairs={{0,4},{2,6},{4,12},{6,14},{12,8},{14,10},{8,0},{10,2},{1,5},{3,7},... | collective-permute-start | bytes 393224 | tf_op jit(solution)/shard_map/ppermute | solution.py:501
  31.1 0.4 collective-permute-start.8
  31.5 2.0 %collective-permute-start.9 = (bf16[512,128]{1,0:T(8,128)(2,1)S(1)}, bf16[512,128]{1,0:T(8,128)(2,1)S(1)}, u32[]{:S(2)}, u32[]{:S(2)}) collective-permute-start(bf16[512,128]{1,0:T(8,128)(2,1)S(1)} %join_blocks.3.refs_5_), channel_id=1, source_target_pairs={{0,8},{2,10},{4,0},{6,2},{12,4},{14,6},{8,12},{10,14},{1,9},{3,11}... | collective-permute-start | bytes 393224 | tf_op jit(solution)/shard_map/ppermute | solution.py:501
  33.5 0.7 %advantages.1 = (f32[1,128]{1,0:T(1,128)}, f32[2,128,128]{2,1,0:T(8,128)S(1)}) custom-call(f32[2,3,128,128]{3,2,1,0:T(8,128)S(1)} %get-tuple-element.42.columns_ref, f32[2,2,8,128]{3,2,1,0:T(8,128)S(1)} %get-tuple-element.43.weights_ref, bf16[544,128]{1,0:T(8,128)(2,1)S(1)} %join_blocks.2.refs_0_.refs_5_, ...), custom_call_target="tpu_custom_call" | custom-call | flops 327680 | bytes 524288 | tf_op jit(solution)/shard_map/advantages/pallas_call | solution.py:311
  34.2 0.0 collective-permute-done.5.refs_4_
  34.2 4.4 %tree_attention_backward.2 = (bf16[128,640]{1,0:T(8,128)(2,1)S(1)}, bf16[128,640]{1,0:T(8,128)(2,1)S(1)}, bf16[2,2,128,128]{3,2,1,0:T(8,128)(2,1)S(1)}, bf16[2,2...) custom-call(s32[8]{0:T(128)S(1)} %copy-done.5, ...), custom_call_target="tpu_custom_call" | custom-call | flops 1048576000 | bytes 8388608 | tf_op jit(solution)/shard_map/tree_attention_backward/pallas_call | solution.py:415
  38.7 2.0 %collective-permute-start.14 = (bf16[2,2,128,128]{3,2,1,0:T(8,128)(2,1)S(1)}, bf16[2,2,128,128]{3,2,1,0:T(8,128)(2,1)S(1)}, u32[]{:S(2)}, u32[]{:S(2)}) collective-permute-start(bf16[2,2,128,128]{3,2,1,0:T(8,128)(2,1)S(1)} %get-tuple-element.67), channel_id=1, source_target_pairs={{0,8},{2,10},{4,0},{6,2},{12,4},{14,6},{8,12},{10,14},{1,9},{3,11}... | collective-permute-start | bytes 393224 | tf_op jit(solution)/shard_map/ppermute | solution.py:501
  40.7 0.0 collective-permute-done.7.refs_6_
  40.7 1.2 %collective-permute-start.13 = (bf16[2,2,128,128]{3,2,1,0:T(8,128)(2,1)S(1)}, bf16[2,2,128,128]{3,2,1,0:T(8,128)(2,1)S(1)}, u32[]{:S(2)}, u32[]{:S(2)}) collective-permute-start(bf16[2,2,128,128]{3,2,1,0:T(8,128)(2,1)S(1)} %get-tuple-element.66), channel_id=1, source_target_pairs={{0,12},{2,14},{4,8},{6,10},{12,0},{14,2},{8,4},{10,6},{1,13},{3,15... | collective-permute-start | bytes 393224 | tf_op jit(solution)/shard_map/ppermute | solution.py:501
  41.9 0.0 collective-permute-done.8.refs_7_
  41.9 1.0 %collective-permute-start.12 = (bf16[2,2,128,128]{3,2,1,0:T(8,128)(2,1)S(1)}, bf16[2,2,128,128]{3,2,1,0:T(8,128)(2,1)S(1)}, u32[]{:S(2)}, u32[]{:S(2)}) collective-permute-start(bf16[2,2,128,128]{3,2,1,0:T(8,128)(2,1)S(1)} %get-tuple-element.65), channel_id=1, source_target_pairs={{0,4},{2,6},{4,12},{6,14},{12,8},{14,10},{8,0},{10,2},{1,5},{3,7},... | collective-permute-start | bytes 393224 | tf_op jit(solution)/shard_map/ppermute | solution.py:501
  42.9 0.0 collective-permute-done.9.refs_8_
  42.9 3.5 %collective-permute-start.10 = (bf16[128,640]{1,0:T(8,128)(2,1)S(1)}, bf16[128,640]{1,0:T(8,128)(2,1)S(1)}, u32[]{:S(2)}, u32[]{:S(2)}) collective-permute-start(bf16[128,640]{1,0:T(8,128)(2,1)S(1)} %get-tuple-element.61), channel_id=1, source_target_pairs={{0,2},{2,0},{4,6},{6,4},{8,10},{10,8},{12,14},{14,12},{1,3},{3,1},... | collective-permute-start | bytes 491528 | tf_op jit(solution)/shard_map/ppermute | solution.py:501
  46.4 0.0 collective-permute-done.6.refs_4_
  46.4 4.4 %tree_attention_backward.3 = (bf16[128,640]{1,0:T(8,128)(2,1)S(1)}, bf16[128,640]{1,0:T(8,128)(2,1)S(1)}, bf16[2,2,128,128]{3,2,1,0:T(8,128)(2,1)S(1)}, bf16[2,2...) custom-call(s32[8]{0:T(128)S(1)} %copy-done.5, ...), custom_call_target="tpu_custom_call" | custom-call | flops 1048576000 | bytes 8388608 | tf_op jit(solution)/shard_map/tree_attention_backward/pallas_call | solution.py:415
  50.8 0.1 collective-permute-start.11
  50.9 0.0 collective-permute-done.14.refs_5_
  50.9 2.0 %collective-permute-start.18 = (bf16[2,2,128,128]{3,2,1,0:T(8,128)(2,1)S(1)}, bf16[2,2,128,128]{3,2,1,0:T(8,128)(2,1)S(1)}, u32[]{:S(2)}, u32[]{:S(2)}) collective-permute-start(bf16[2,2,128,128]{3,2,1,0:T(8,128)(2,1)S(1)} %get-tuple-element.72), channel_id=1, source_target_pairs={{0,8},{2,10},{4,0},{6,2},{12,4},{14,6},{8,12},{10,14},{1,9},{3,11}... | collective-permute-start | bytes 393224 | tf_op jit(solution)/shard_map/ppermute | solution.py:501
  52.9 0.0 collective-permute-done.13.refs_4_
  52.9 1.5 %collective-permute-start.17 = (bf16[2,2,128,128]{3,2,1,0:T(8,128)(2,1)S(1)}, bf16[2,2,128,128]{3,2,1,0:T(8,128)(2,1)S(1)}, u32[]{:S(2)}, u32[]{:S(2)}) collective-permute-start(bf16[2,2,128,128]{3,2,1,0:T(8,128)(2,1)S(1)} %get-tuple-element.71), channel_id=1, source_target_pairs={{0,12},{2,14},{4,8},{6,10},{12,0},{14,2},{8,4},{10,6},{1,13},{3,15... | collective-permute-start | bytes 393224 | tf_op jit(solution)/shard_map/ppermute | solution.py:501
  54.4 0.3 collective-permute-done.12.refs_3_
  54.7 0.7 %collective-permute-start.16 = (bf16[2,2,128,128]{3,2,1,0:T(8,128)(2,1)S(1)}, bf16[2,2,128,128]{3,2,1,0:T(8,128)(2,1)S(1)}, u32[]{:S(2)}, u32[]{:S(2)}) collective-permute-start(bf16[2,2,128,128]{3,2,1,0:T(8,128)(2,1)S(1)} %get-tuple-element.70), channel_id=1, source_target_pairs={{0,4},{2,6},{4,12},{6,14},{12,8},{14,10},{8,0},{10,2},{1,5},{3,7},... | collective-permute-start | bytes 393224 | tf_op jit(solution)/shard_map/ppermute | solution.py:501
  55.5 1.7 %collective-permute-done.18.refs_9_ = bf16[2,2,128,128]{3,2,1,0:T(8,128)(2,1)S(1)} collective-permute-done((bf16[2,2,128,128]{3,2,1,0:T(8,128)(2,1)S(1)}, bf16[2,2,128,128]{3,2,1,0:T(8,128)(2,1)S(1)}, u32[]{:S(2)}, u32[]{:S(2)}) %collective-permute-start.18) | collective-permute-done | bytes 131104 | tf_op jit(solution)/shard_map/ppermute | solution.py:501
  57.2 1.4 %collective-permute-start.15 = (bf16[2,128,128]{2,1,0:T(8,128)(2,1)S(1)}, bf16[2,128,128]{2,1,0:T(8,128)(2,1)S(1)}, u32[]{:S(2)}, u32[]{:S(2)}) collective-permute-start(bf16[2,128,128]{2,1,0:T(8,128)(2,1)S(1)} %fusion), channel_id=1, source_target_pairs={{0,2},{2,0},{4,6},{6,4},{8,10},{10,8},{12,14},{14,12},{1,3},{3,1},... | collective-permute-start | bytes 196616 | tf_op jit(solution)/shard_map/ppermute | solution.py:501
  58.7 1.3 %collective-permute-done.17.refs_8_ = bf16[2,2,128,128]{3,2,1,0:T(8,128)(2,1)S(1)} collective-permute-done((bf16[2,2,128,128]{3,2,1,0:T(8,128)(2,1)S(1)}, bf16[2,2,128,128]{3,2,1,0:T(8,128)(2,1)S(1)}, u32[]{:S(2)}, u32[]{:S(2)}) %collective-permute-start.17) | collective-permute-done | bytes 131104 | tf_op jit(solution)/shard_map/ppermute | solution.py:501
  60.0 2.2 %collective-permute-done.16.refs_7_ = bf16[2,2,128,128]{3,2,1,0:T(8,128)(2,1)S(1)} collective-permute-done((bf16[2,2,128,128]{3,2,1,0:T(8,128)(2,1)S(1)}, bf16[2,2,128,128]{3,2,1,0:T(8,128)(2,1)S(1)}, u32[]{:S(2)}, u32[]{:S(2)}) %collective-permute-start.16) | collective-permute-done | bytes 131104 | tf_op jit(solution)/shard_map/ppermute | solution.py:501
  62.3 2.0 %collective-permute-start.19 = (bf16[2,128,128]{2,1,0:T(8,128)(2,1)S(1)}, bf16[2,128,128]{2,1,0:T(8,128)(2,1)S(1)}, u32[]{:S(2)}, u32[]{:S(2)}) collective-permute-start(bf16[2,128,128]{2,1,0:T(8,128)(2,1)S(1)} %fusion.1), channel_id=1, source_target_pairs={{0,2},{2,0},{4,6},{6,4},{8,10},{10,8},{12,14},{14,12},{1,3},{3,1},... | collective-permute-start | bytes 196616 | tf_op jit(solution)/shard_map/ppermute | solution.py:501
  64.2 0.0 collective-permute-done.10.refs_2_
  64.2 0.0 collective-permute-done.11.refs_3_
  64.3 0.9 %join_queries.1 = bf16[128,2560]{1,0:T(8,128)(2,1)} custom-call(bf16[128,640]{1,0:T(8,128)(2,1)S(1)} %get-tuple-element.56.refs_0_, bf16[128,640]{1,0:T(8,128)(2,1)S(1)} %get-tuple-element.60.refs_1_, bf16[128,640]{1,0:T(8,128)(2,1)S(1)} %collective-permute-done.10.refs_2_, bf16[128,640]{1,0:T(8,128)(2,1)S(1)} %collective-permute-done.11.refs_3_), custom_call_target="tpu_custom_call" | custom-call | bytes 1310720 | tf_op jit(solution)/shard_map/join_queries/pallas_call | solution.py:453
  65.2 0.0 collective-permute-done.15.refs_0_
  65.2 1.4 %collective-permute-done.19.refs_1_ = bf16[2,128,128]{2,1,0:T(8,128)(2,1)S(1)} collective-permute-done((bf16[2,128,128]{2,1,0:T(8,128)(2,1)S(1)}, bf16[2,128,128]{2,1,0:T(8,128)(2,1)S(1)}, u32[]{:S(2)}, u32[]{:S(2)}) %collective-permute-start.19) | collective-permute-done | bytes 65568 | tf_op jit(solution)/shard_map/ppermute | solution.py:501
  66.6 0.8 %join_keys.1 = (bf16[128,512]{1,0:T(8,128)(2,1)}, bf16[128,512]{1,0:T(8,128)(2,1)}) custom-call(bf16[2,128,128]{2,1,0:T(8,128)(2,1)S(1)} %collective-permute-done.15.refs_0_, bf16[2,128,128]{2,1,0:T(8,128)(2,1)S(1)} %collective-permute-done.19.refs_1_, bf16[2,2,128,128]{3,2,1,0:T(8,128)(2,1)S(1)} %get-tuple-element.64.refs_2_, ...), custom_call_target="tpu_custom_call" | custom-call | bytes 524288 | tf_op jit(solution)/shard_map/join_keys/pallas_call | solution.py:487
  (4 shorter events, 0.1 us)
Async XLA Ops:
  2.4 5.4 %collective-permute-start = (bf16[272,128]{1,0:T(8,128)(2,1)}, bf16[272,128]{1,0:T(8,128)(2,1)S(1)}, u32[]{:S(2)}, u32[]{:S(2)}) collective-permute-start(bf16[272,128]{1,0:T(8,128)(2,1)} %get-tuple-element.41), channel_id=1, source_target_pairs={{0,2},{2,0},{4,6},{6,4},{8,10},{10,8},{12,14},{14,12},{1,3},{3,1},... | collective-permute-start | bytes 208904 | tf_op jit(solution)/shard_map/ppermute | solution.py:501
  5.4 1.1 %copy-start = (bf16[128,2560]{1,0:T(8,128)(2,1)S(1)}, bf16[128,2560]{1,0:T(8,128)(2,1)}, u32[]{:S(2)}) copy-start(bf16[128,2560]{1,0:T(8,128)(2,1)} %q_ref) | copy-start | bytes 1966084
  6.5 1.1 %copy-start.1 = (bf16[128,2560]{1,0:T(8,128)(2,1)S(1)}, bf16[128,2560]{1,0:T(8,128)(2,1)}, u32[]{:S(2)}) copy-start(bf16[128,2560]{1,0:T(8,128)(2,1)} %dir_ref.1) | copy-start | bytes 1966084
  7.6 0.9 %copy-start.2 = (bf16[272,128]{1,0:T(8,128)(2,1)S(1)}, bf16[272,128]{1,0:T(8,128)(2,1)}, u32[]{:S(2)}) copy-start(bf16[272,128]{1,0:T(8,128)(2,1)} %get-tuple-element.40.refs_0_.mine_ref) | copy-start | bytes 208900
  8.4 1.6 %copy-start.6 = (bf16[256,128]{1,0:T(8,128)(2,1)S(1)}, bf16[256,128]{1,0:T(8,128)(2,1)}, u32[]{:S(2)}) copy-start(bf16[256,128]{1,0:T(8,128)(2,1)} %get-tuple-element.49) | copy-start | bytes 196612
  8.4 5.9 %copy-start.3 = (bf16[256,128]{1,0:T(8,128)(2,1)S(1)}, bf16[256,128]{1,0:T(8,128)(2,1)}, u32[]{:S(2)}) copy-start(bf16[256,128]{1,0:T(8,128)(2,1)} %get-tuple-element.48.mine_ref) | copy-start | bytes 196612
  8.5 6.1 %collective-permute-start.1 = (bf16[544,128]{1,0:T(8,128)(2,1)S(1)}, bf16[544,128]{1,0:T(8,128)(2,1)S(1)}, u32[]{:S(2)}, u32[]{:S(2)}) collective-permute-start(bf16[544,128]{1,0:T(8,128)(2,1)S(1)} %join_blocks.2.refs_0_.refs_5_), channel_id=1, source_target_pairs={{0,4},{2,6},{4,12},{6,14},{12,8},{14,10},{8,0},{10,2},{1,5},{3,7},... | collective-permute-start | bytes 417800 | tf_op jit(solution)/shard_map/ppermute | solution.py:501
  10.1 4.3 %collective-permute-start.2 = (bf16[256,128]{1,0:T(8,128)(2,1)S(1)}, bf16[256,128]{1,0:T(8,128)(2,1)S(1)}, u32[]{:S(2)}, u32[]{:S(2)}) collective-permute-start(bf16[256,128]{1,0:T(8,128)(2,1)S(1)} %copy-done.6), channel_id=1, source_target_pairs={{0,2},{2,0},{4,6},{6,4},{8,10},{10,8},{12,14},{14,12},{1,3},{3,1},... | collective-permute-start | bytes 196616 | tf_op jit(solution)/shard_map/ppermute | solution.py:501
  14.4 2.7 %copy-start.4 = (s32[8]{0:T(128)S(1)}, s32[8]{0:T(128)}, u32[]{:S(2)}) copy-start(s32[8]{0:T(128)} %lengths_s.1) | copy-start | bytes 100
  14.4 2.7 %copy-start.5 = (s32[8]{0:T(128)S(1)}, s32[8]{0:T(128)}, u32[]{:S(2)}) copy-start(s32[8]{0:T(128)} %refs_0_.3) | copy-start | bytes 100
  14.5 6.0 %collective-permute-start.3 = (bf16[544,128]{1,0:T(8,128)(2,1)S(1)}, bf16[544,128]{1,0:T(8,128)(2,1)S(1)}, u32[]{:S(2)}, u32[]{:S(2)}) collective-permute-start(bf16[544,128]{1,0:T(8,128)(2,1)S(1)} %collective-permute-done.1.refs_1_.refs_6_), channel_id=1, source_target_pairs={{0,4},{2,6},{4,12},{6,14},{12,8},{14,10},{8,0},{10,2},{1,5},{3,7},... | collective-permute-start | bytes 417800 | tf_op jit(solution)/shard_map/ppermute | solution.py:501
  20.5 6.0 %collective-permute-start.4 = (bf16[544,128]{1,0:T(8,128)(2,1)S(1)}, bf16[544,128]{1,0:T(8,128)(2,1)S(1)}, u32[]{:S(2)}, u32[]{:S(2)}) collective-permute-start(bf16[544,128]{1,0:T(8,128)(2,1)S(1)} %collective-permute-done.3.refs_2_.refs_7_), channel_id=1, source_target_pairs={{0,4},{2,6},{4,12},{6,14},{12,8},{14,10},{8,0},{10,2},{1,5},{3,7},... | collective-permute-start | bytes 417800 | tf_op jit(solution)/shard_map/ppermute | solution.py:501
  22.2 12.0 %collective-permute-start.5 = (bf16[2,5,128,128]{3,2,1,0:T(8,128)(2,1)S(1)}, bf16[2,5,128,128]{3,2,1,0:T(8,128)(2,1)S(1)}, u32[]{:S(2)}, u32[]{:S(2)}) collective-permute-start(bf16[2,5,128,128]{3,2,1,0:T(8,128)(2,1)S(1)} %get-tuple-element.55), channel_id=1, source_target_pairs={{0,2},{2,0},{4,6},{6,4},{8,10},{10,8},{12,14},{14,12},{1,3},{3,1},... | collective-permute-start | bytes 983048 | tf_op jit(solution)/shard_map/ppermute | solution.py:501
  26.5 19.9 %collective-permute-start.6 = (bf16[2,5,128,128]{3,2,1,0:T(8,128)(2,1)S(1)}, bf16[2,5,128,128]{3,2,1,0:T(8,128)(2,1)S(1)}, u32[]{:S(2)}, u32[]{:S(2)}) collective-permute-start(bf16[2,5,128,128]{3,2,1,0:T(8,128)(2,1)S(1)} %get-tuple-element.58), channel_id=1, source_target_pairs={{0,2},{2,0},{4,6},{6,4},{8,10},{10,8},{12,14},{14,12},{1,3},{3,1},... | collective-permute-start | bytes 983048 | tf_op jit(solution)/shard_map/ppermute | solution.py:501
  28.6 12.1 %collective-permute-start.7 = (bf16[512,128]{1,0:T(8,128)(2,1)S(1)}, bf16[512,128]{1,0:T(8,128)(2,1)S(1)}, u32[]{:S(2)}, u32[]{:S(2)}) collective-permute-start(bf16[512,128]{1,0:T(8,128)(2,1)S(1)} %join_blocks.3.refs_5_), channel_id=1, source_target_pairs={{0,4},{2,6},{4,12},{6,14},{12,8},{14,10},{8,0},{10,2},{1,5},{3,7},... | collective-permute-start | bytes 393224 | tf_op jit(solution)/shard_map/ppermute | solution.py:501
  31.1 10.7 %collective-permute-start.8 = (bf16[512,128]{1,0:T(8,128)(2,1)S(1)}, bf16[512,128]{1,0:T(8,128)(2,1)S(1)}, u32[]{:S(2)}, u32[]{:S(2)}) collective-permute-start(bf16[512,128]{1,0:T(8,128)(2,1)S(1)} %join_blocks.3.refs_5_), channel_id=1, source_target_pairs={{0,12},{2,14},{4,8},{6,10},{12,0},{14,2},{8,4},{10,6},{1,13},{3,15... | collective-permute-start | bytes 393224 | tf_op jit(solution)/shard_map/ppermute | solution.py:501
  31.5 11.4 %collective-permute-start.9 = (bf16[512,128]{1,0:T(8,128)(2,1)S(1)}, bf16[512,128]{1,0:T(8,128)(2,1)S(1)}, u32[]{:S(2)}, u32[]{:S(2)}) collective-permute-start(bf16[512,128]{1,0:T(8,128)(2,1)S(1)} %join_blocks.3.refs_5_), channel_id=1, source_target_pairs={{0,8},{2,10},{4,0},{6,2},{12,4},{14,6},{8,12},{10,14},{1,9},{3,11}... | collective-permute-start | bytes 393224 | tf_op jit(solution)/shard_map/ppermute | solution.py:501
  38.7 12.2 %collective-permute-start.14 = (bf16[2,2,128,128]{3,2,1,0:T(8,128)(2,1)S(1)}, bf16[2,2,128,128]{3,2,1,0:T(8,128)(2,1)S(1)}, u32[]{:S(2)}, u32[]{:S(2)}) collective-permute-start(bf16[2,2,128,128]{3,2,1,0:T(8,128)(2,1)S(1)} %get-tuple-element.67), channel_id=1, source_target_pairs={{0,8},{2,10},{4,0},{6,2},{12,4},{14,6},{8,12},{10,14},{1,9},{3,11}... | collective-permute-start | bytes 393224 | tf_op jit(solution)/shard_map/ppermute | solution.py:501
  40.7 12.2 %collective-permute-start.13 = (bf16[2,2,128,128]{3,2,1,0:T(8,128)(2,1)S(1)}, bf16[2,2,128,128]{3,2,1,0:T(8,128)(2,1)S(1)}, u32[]{:S(2)}, u32[]{:S(2)}) collective-permute-start(bf16[2,2,128,128]{3,2,1,0:T(8,128)(2,1)S(1)} %get-tuple-element.66), channel_id=1, source_target_pairs={{0,12},{2,14},{4,8},{6,10},{12,0},{14,2},{8,4},{10,6},{1,13},{3,15... | collective-permute-start | bytes 393224 | tf_op jit(solution)/shard_map/ppermute | solution.py:501
  41.9 12.9 %collective-permute-start.12 = (bf16[2,2,128,128]{3,2,1,0:T(8,128)(2,1)S(1)}, bf16[2,2,128,128]{3,2,1,0:T(8,128)(2,1)S(1)}, u32[]{:S(2)}, u32[]{:S(2)}) collective-permute-start(bf16[2,2,128,128]{3,2,1,0:T(8,128)(2,1)S(1)} %get-tuple-element.65), channel_id=1, source_target_pairs={{0,4},{2,6},{4,12},{6,14},{12,8},{14,10},{8,0},{10,2},{1,5},{3,7},... | collective-permute-start | bytes 393224 | tf_op jit(solution)/shard_map/ppermute | solution.py:501
  42.9 21.4 %collective-permute-start.10 = (bf16[128,640]{1,0:T(8,128)(2,1)S(1)}, bf16[128,640]{1,0:T(8,128)(2,1)S(1)}, u32[]{:S(2)}, u32[]{:S(2)}) collective-permute-start(bf16[128,640]{1,0:T(8,128)(2,1)S(1)} %get-tuple-element.61), channel_id=1, source_target_pairs={{0,2},{2,0},{4,6},{6,4},{8,10},{10,8},{12,14},{14,12},{1,3},{3,1},... | collective-permute-start | bytes 491528 | tf_op jit(solution)/shard_map/ppermute | solution.py:501
  50.8 13.5 %collective-permute-start.11 = (bf16[128,640]{1,0:T(8,128)(2,1)S(1)}, bf16[128,640]{1,0:T(8,128)(2,1)S(1)}, u32[]{:S(2)}, u32[]{:S(2)}) collective-permute-start(bf16[128,640]{1,0:T(8,128)(2,1)S(1)} %get-tuple-element.62), channel_id=1, source_target_pairs={{0,2},{2,0},{4,6},{6,4},{8,10},{10,8},{12,14},{14,12},{1,3},{3,1},... | collective-permute-start | bytes 491528 | tf_op jit(solution)/shard_map/ppermute | solution.py:501
  50.9 6.3 %collective-permute-start.18 = (bf16[2,2,128,128]{3,2,1,0:T(8,128)(2,1)S(1)}, bf16[2,2,128,128]{3,2,1,0:T(8,128)(2,1)S(1)}, u32[]{:S(2)}, u32[]{:S(2)}) collective-permute-start(bf16[2,2,128,128]{3,2,1,0:T(8,128)(2,1)S(1)} %get-tuple-element.72), channel_id=1, source_target_pairs={{0,8},{2,10},{4,0},{6,2},{12,4},{14,6},{8,12},{10,14},{1,9},{3,11}... | collective-permute-start | bytes 393224 | tf_op jit(solution)/shard_map/ppermute | solution.py:501
  52.9 7.1 %collective-permute-start.17 = (bf16[2,2,128,128]{3,2,1,0:T(8,128)(2,1)S(1)}, bf16[2,2,128,128]{3,2,1,0:T(8,128)(2,1)S(1)}, u32[]{:S(2)}, u32[]{:S(2)}) collective-permute-start(bf16[2,2,128,128]{3,2,1,0:T(8,128)(2,1)S(1)} %get-tuple-element.71), channel_id=1, source_target_pairs={{0,12},{2,14},{4,8},{6,10},{12,0},{14,2},{8,4},{10,6},{1,13},{3,15... | collective-permute-start | bytes 393224 | tf_op jit(solution)/shard_map/ppermute | solution.py:501
  54.7 7.5 %collective-permute-start.16 = (bf16[2,2,128,128]{3,2,1,0:T(8,128)(2,1)S(1)}, bf16[2,2,128,128]{3,2,1,0:T(8,128)(2,1)S(1)}, u32[]{:S(2)}, u32[]{:S(2)}) collective-permute-start(bf16[2,2,128,128]{3,2,1,0:T(8,128)(2,1)S(1)} %get-tuple-element.70), channel_id=1, source_target_pairs={{0,4},{2,6},{4,12},{6,14},{12,8},{14,10},{8,0},{10,2},{1,5},{3,7},... | collective-permute-start | bytes 393224 | tf_op jit(solution)/shard_map/ppermute | solution.py:501
  57.2 8.0 %collective-permute-start.15 = (bf16[2,128,128]{2,1,0:T(8,128)(2,1)S(1)}, bf16[2,128,128]{2,1,0:T(8,128)(2,1)S(1)}, u32[]{:S(2)}, u32[]{:S(2)}) collective-permute-start(bf16[2,128,128]{2,1,0:T(8,128)(2,1)S(1)} %fusion), channel_id=1, source_target_pairs={{0,2},{2,0},{4,6},{6,4},{8,10},{10,8},{12,14},{14,12},{1,3},{3,1},... | collective-permute-start | bytes 196616 | tf_op jit(solution)/shard_map/ppermute | solution.py:501
  62.3 4.3 %collective-permute-start.19 = (bf16[2,128,128]{2,1,0:T(8,128)(2,1)S(1)}, bf16[2,128,128]{2,1,0:T(8,128)(2,1)S(1)}, u32[]{:S(2)}, u32[]{:S(2)}) collective-permute-start(bf16[2,128,128]{2,1,0:T(8,128)(2,1)S(1)} %fusion.1), channel_id=1, source_target_pairs={{0,2},{2,0},{4,6},{6,4},{8,10},{10,8},{12,14},{14,12},{1,3},{3,1},... | collective-permute-start | bytes 196616 | tf_op jit(solution)/shard_map/ppermute | solution.py:501

commit v11 on v9

--- a/solution.py
+++ b/solution.py
@@ -306,7 +306,7 @@
     kv_scr, p_scr, ds_scr, acc_scr = refs[-4:]
     refs = refs[3 + segs + sources : -4]
     steps = sources // segs
-    dkv_refs, dq_refs = refs[-steps:], refs[-steps - segs : -steps]
+    dkv_ref, dq_refs = refs[-1], refs[:segs]
 
     length = query_refs[0].shape[2]
     own = lax.axis_index("seg")
@@ -373,8 +373,12 @@
             acc_scr[s, 0] += dk_all[rows]
             acc_scr[s, 1] += dv_all[rows]
     for step in range(steps):
+        target = step
+        if segs > 1:
+            place = ring_place(own // segs) - step + steps
+            target = ring_place(lax.rem(place, steps))
         for i in range(segs):
-            dkv_refs[step][i] = acc_scr[step * segs + i].astype(jnp.bfloat16)
+            dkv_ref[target, i] = acc_scr[step * segs + i].astype(jnp.bfloat16)
 
 
 def attend(parents, advantages, bias, query_list, kv_list, chunk):
@@ -387,7 +391,7 @@
     smem = pl.BlockSpec(memory_space=pltpu.SMEM)
     vmem = pl.BlockSpec(memory_space=pltpu.VMEM)
     out_shape = [jax.ShapeDtypeStruct((length, width), jnp.bfloat16)] * segs
-    out_shape += [jax.ShapeDtypeStruct((segs, 2, length, HD), jnp.bfloat16)] * steps
+    out_shape.append(jax.ShapeDtypeStruct((steps, segs, 2, length, HD), jnp.bfloat16))
     outs = pl.pallas_call(
         functools.partial(attend_kernel, DEPTH, chunk, segs, sources, group_size),
         out_shape=out_shape,
@@ -407,7 +411,7 @@
         ),
         name="tree_attention_backward",
     )(parents, advantages, bias, *query_list, *kv_list)
-    return outs[:segs], outs[segs:]
+    return outs[:segs], outs[segs]
 
 
 def join_queries_kernel(*refs):
@@ -442,13 +446,12 @@
 def join_keys_kernel(chunks, *refs):
     part = lax.rem(lax.axis_index("seg"), 2)
     other_refs, sum_refs = refs[:chunks], refs[chunks:-2]
-    many = len(sum_refs) // chunks
     dk_ref, dv_ref = refs[-2:]
     for chunk in range(chunks):
         here = pl.ds(pl.multiple_of((part * chunks + chunk) * HD, HD), HD)
         there = pl.ds(pl.multiple_of(((1 - part) * chunks + chunk) * HD, HD), HD)
         for plane, out_ref in enumerate((dk_ref, dv_ref)):
-            blocks = [ref[0, plane] for ref in sum_refs[chunk * many : (chunk + 1) * many]]
+            blocks = [sum_refs[chunk][pair, 0, plane] for pair in range(sum_refs[chunk].shape[0])]
             total = sum(block.astype(jnp.float32) for block in blocks)
             out_ref[:, here] = total.astype(jnp.bfloat16)
             out_ref[:, there] = other_refs[chunk][plane]
@@ -458,19 +461,18 @@
     chunks = len(others)
     length = others[0].shape[1]
     vmem = pl.BlockSpec(memory_space=pltpu.VMEM)
-    flat = [block for blocks in summands for block in blocks]
     out = jax.ShapeDtypeStruct((length, 2 * chunks * HD), jnp.bfloat16)
     return pl.pallas_call(
         functools.partial(join_keys_kernel, chunks),
         out_shape=(out, out),
-        in_specs=[vmem] * (chunks + len(flat)),
+        in_specs=[vmem] * (2 * chunks),
         out_specs=(vmem, vmem),
         cost_estimate=pl.CostEstimate(
             flops=0, bytes_accessed=16 * length * HD * chunks, transcendentals=0
         ),
         compiler_params=SMALL,
         name="join_keys",
-    )(*others, *flat)
+    )(*others, *summands)
 
 
 def permute(array, pairs):
@@ -497,7 +499,6 @@
         return pairs
 
     climb = turn(1)
-    down = {d: turn(-d) for d in steps}
 
     kept, given = pack(lengths, key_vectors, value_vectors, token_rows, 2, log_rate)
     taken = permute(given, swap)
@@ -524,14 +525,16 @@
         dq_back.append(dq[1])
         dkv_list.append(dkv)
 
-    summands = []
-    for dkv in dkv_list:
-        arrived = [permute(dkv[d], down[d]) for d in steps[::-1]]
-        summands.append([after(dkv[0], dq_own[-1])] + arrived)
-    dq_back = [permute(block, swap) for block in dq_back]
+    last = dq_own[-1]
+    columns_of = [list(range(x, groups, 2)) for x in range(2)]
+    summands = [
+        after(lax.all_to_all(dkv, "seg", 0, 0, axis_index_groups=columns_of, tiled=True), last)
+        for dkv in dkv_list
+    ]
+    dq_back = [permute(after(block, last), swap) for block in dq_back]
     others = []
     for blocks in summands:
-        total = sum(block[1].astype(jnp.float32) for block in blocks)
+        total = sum(blocks[pair, 1].astype(jnp.float32) for pair in range(len(ring)))
         others.append(permute(total.astype(jnp.bfloat16), swap))
     grad_q = join_queries(dq_own, dq_back)
     grad_k, grad_v = join_keys(others, summands)
@@ -585,7 +588,7 @@
     for head in range(heads):
         dq, dkv = attend(parents, advantages, bias, [kept_q[head]], kv_list, head)
         dq_list.append(dq[0])
-        dkv_list.append(jnp.concatenate(dkv))
+        dkv_list.append(dkv[:, 0])
     rows = jnp.transpose(jnp.stack(dkv_list), (1, 3, 2, 0, 4)).reshape(1, DEPTH, length, -1)
     summed = return_rows(rows[:, 1:], chains, total_segs)[0] + rows[0, 0].astype(jnp.float32)
     grad_keys = summed[:, :width].astype(jnp.bfloat16)

time: 64.8 us -> 77.9 us (1.20)
  waiting for transfers between devices: 15.7 us -> 29.7 us
  starting transfers between devices: 31.4 us -> 27.8 us
  Pallas kernels: 14.6 us -> 16.1 us
  local copies, waits for them, and re-layouts: 2.19 us -> 3.1 us
    ppermute x19 -> x13, starting transfers between devices: 31.4 us -> 18.3 us  [permute(): return lax.ppermute(array, 'seg', pairs)]
    all_to_all x0 -> x2, starting transfers between devices: none -> 9.43 us  [paired_body(): lax.all_to_all(dkv, 'seg', 0, 0, axis_index_groups=columns_of, tiled=True)]
    ppermute x19 -> x13, waiting for transfers between devices: 15.7 us -> 23.1 us  [permute(): return lax.ppermute(array, 'seg', pairs)]
    all_to_all x0 -> x2, waiting for transfers between devices: none -> 6.67 us  [paired_body(): lax.all_to_all(dkv, 'seg', 0, 0, axis_index_groups=columns_of, tiled=True)]
    pallas_call x2, Pallas kernels: 8.85 us -> 10.4 us  [attend(): pl.pallas_call(functools.partial(attend_kernel, DEPTH, chunk, segs, sourc...]
    unnamed x10 -> x14, local copies, waits for them, and re-layouts: 2.19 us -> 3.1 us
  transfers between devices with their start and end apart: 19 -> 15, of which waited for: 9 -> 9; matrix products, arithmetic and copies ran while one was open for 0% -> 0% of each run, Pallas kernels for 18% -> 10%
where the time goes in v11:
time: 77.9 us; the launch traced here: 77.5 us
  waiting for transfers between devices  29.7 us (38%)
  starting transfers between devices  27.8 us (36%)
  Pallas kernels  16.1 us (21%)
  local copies, waits for them, and re-layouts  3.1 us (4%)
    ppermute x13, waiting for transfers between devices, permute(): return lax.ppermute(array, 'seg', pairs)  23.1 us
    ppermute x13, starting transfers between devices, permute(): return lax.ppermute(array, 'seg', pairs)  18.3 us
    pallas_call x2, Pallas kernels, attend(): pl.pallas_call(functools.partial(attend_kernel, DEPTH, chunk, segs, sourc...  10.4 us
    all_to_all x2, starting transfers between devices, paired_body(): lax.all_to_all(dkv, 'seg', 0, 0, axis_index_groups=columns_of, tiled=True)  9.43 us
    all_to_all x2, waiting for transfers between devices, paired_body(): lax.all_to_all(dkv, 'seg', 0, 0, axis_index_groups=columns_of, tiled=True)  6.67 us
    unnamed x14, local copies, waits for them, and re-layouts  3.1 us
    pallas_call x1, Pallas kernels, pack(): pl.pallas_call(functools.partial(pack_kernel, log_rate), out_shape=(block...  1.86 us
  transfers between devices with their start and end apart: 15, of which 9 were waited for; matrix products, arithmetic and copies ran while one was open for 0% of the time, Pallas kernels for 10%

profile of v11, /device:TPU:0, one launch (start us, length us, event | category | flops | bytes accessed | tf_op | source)
XLA Modules:
  0.0 77.5 jit_solution(16844195244053601321)
XLA Ops:
  0.6 1.9 %pack_keys_values.1 = (bf16[528,128]{1,0:T(8,128)(2,1)}, bf16[528,128]{1,0:T(8,128)(2,1)}) custom-call(s32[8]{0:T(128)} %lengths_s.1, bf16[128,512]{1,0:T(8,128)(2,1)} %k_ref.1, bf16[128,512]{1,0:T(8,128)(2,1)} %v_ref.1, f32[1,128]{1,0:T(1,128)} %bitcast.9, f32[1,128]{1,0:T(1,128)} %bitcast.10, f32[1,128]{1,0:T(1,128)} %bitcast.11, f32[1,128]{1,0:T(1,128)} %bitcast.12), custom_call_target="tpu_custom_call" | custom-call | flops 12800 | bytes 524288 | tf_op jit(solution)/shard_map/pack_keys_values/pallas_call | solution.py:101
  2.5 2.9 %collective-permute-start = (bf16[528,128]{1,0:T(8,128)(2,1)}, bf16[528,128]{1,0:T(8,128)(2,1)S(1)}, u32[]{:S(2)}, u32[]{:S(2)}) collective-permute-start(bf16[528,128]{1,0:T(8,128)(2,1)} %get-tuple-element.35), channel_id=1, source_target_pairs={{0,2},{2,0},{4,6},{6,4},{8,10},{10,8},{12,14},{14,12},{1,3},{3,1},... | collective-permute-start | bytes 405512 | tf_op jit(solution)/shard_map/ppermute | solution.py:479
  5.4 1.6 %collective-permute-start.1 = (bf16[528,128]{1,0:T(8,128)(2,1)}, bf16[528,128]{1,0:T(8,128)(2,1)S(1)}, u32[]{:S(2)}, u32[]{:S(2)}) collective-permute-start(bf16[528,128]{1,0:T(8,128)(2,1)} %get-tuple-element.34.refs_0_.refs_5_), channel_id=1, source_target_pairs={{0,4},{2,6},{4,12},{6,14},{12,8},{14,10},{8,0},{10,2},{1,5},{3,7},... | collective-permute-start | bytes 405512 | tf_op jit(solution)/shard_map/ppermute | solution.py:479
  7.0 0.0 copy-start
  7.0 1.1 %copy-done = bf16[128,2560]{1,0:T(8,128)(2,1)S(1)} copy-done((bf16[128,2560]{1,0:T(8,128)(2,1)S(1)}, bf16[128,2560]{1,0:T(8,128)(2,1)}, u32[]{:S(2)}) %copy-start) | copy-done | bytes 655384
  8.1 0.0 copy-start.1
  8.1 1.1 %copy-done.1 = bf16[128,2560]{1,0:T(8,128)(2,1)S(1)} copy-done((bf16[128,2560]{1,0:T(8,128)(2,1)S(1)}, bf16[128,2560]{1,0:T(8,128)(2,1)}, u32[]{:S(2)}) %copy-start.1) | copy-done | bytes 655384
  9.2 0.0 copy-start.2
  9.2 0.2 pack_queries.1
  9.4 0.0 copy-start.3
  9.4 0.0 copy-start.4
  9.4 0.0 collective-permute-done.refs_1_.refs_6_
  9.5 2.1 %collective-permute-done.1.refs_2_.refs_7_ = bf16[528,128]{1,0:T(8,128)(2,1)S(1)} collective-permute-done((bf16[528,128]{1,0:T(8,128)(2,1)}, bf16[528,128]{1,0:T(8,128)(2,1)S(1)}, u32[]{:S(2)}, u32[]{:S(2)}) %collective-permute-start.1) | collective-permute-done | bytes 135200 | tf_op jit(solution)/shard_map/ppermute | solution.py:479
  11.6 0.5 collective-permute-start.4
  12.1 0.9 %collective-permute-start.3 = (bf16[528,128]{1,0:T(8,128)(2,1)S(1)}, bf16[528,128]{1,0:T(8,128)(2,1)S(1)}, u32[]{:S(2)}, u32[]{:S(2)}) collective-permute-start(bf16[528,128]{1,0:T(8,128)(2,1)S(1)} %collective-permute-done.1.refs_2_.refs_7_), channel_id=1, source_target_pairs={{0,4},{2,6},{4,12},{6,14},{12,8},{14,10},{8,0},{10,2},{1,5},{3,7},... | collective-permute-start | bytes 405512 | tf_op jit(solution)/shard_map/ppermute | solution.py:479
  13.0 3.3 %collective-permute-start.2 = (bf16[528,128]{1,0:T(8,128)(2,1)S(1)}, bf16[528,128]{1,0:T(8,128)(2,1)S(1)}, u32[]{:S(2)}, u32[]{:S(2)}) collective-permute-start(bf16[528,128]{1,0:T(8,128)(2,1)S(1)} %collective-permute-done.refs_1_.refs_6_), channel_id=1, source_target_pairs={{0,4},{2,6},{4,12},{6,14},{12,8},{14,10},{8,0},{10,2},{1,5},{3,7},... | collective-permute-start | bytes 405512 | tf_op jit(solution)/shard_map/ppermute | solution.py:479
  16.3 0.0 copy-done.2
  16.3 0.0 copy-done.3
  16.3 0.0 copy-done.4
  16.3 1.2 %prepare.1 = (f32[2,640,128]{2,1,0:T(8,128)S(1)}, f32[2,3,128,128]{3,2,1,0:T(8,128)S(1)}, f32[2,2,8,128]{3,2,1,0:T(8,128)S(1)}) custom-call(s32[8]{0:T(128)S(1)} %copy-done.4, s32[8]{0:T(128)S(1)} %copy-done.3, bf16[528,128]{1,0:T(8,128)(2,1)S(1)} %copy-done.2, bf16[528,128]{1,0:T(8,128)(2,1)S(1)} %collective-permute-done.refs_1_.refs_6_), custom_call_target="tpu_custom_call" | custom-call | flops 3276800 | bytes 655360 | tf_op jit(solution)/shard_map/prepare/pallas_call | solution.py:234
  17.5 1.1 %collective-permute-done.3.refs_4_.refs_9_ = bf16[528,128]{1,0:T(8,128)(2,1)S(1)} collective-permute-done((bf16[528,128]{1,0:T(8,128)(2,1)S(1)}, bf16[528,128]{1,0:T(8,128)(2,1)S(1)}, u32[]{:S(2)}, u32[]{:S(2)}) %collective-permute-start.3) | collective-permute-done | bytes 135200 | tf_op jit(solution)/shard_map/ppermute | solution.py:479
  18.6 0.8 collective-permute-start.6
  19.3 1.6 %collective-permute-done.2.refs_3_.refs_8_ = bf16[528,128]{1,0:T(8,128)(2,1)S(1)} collective-permute-done((bf16[528,128]{1,0:T(8,128)(2,1)S(1)}, bf16[528,128]{1,0:T(8,128)(2,1)S(1)}, u32[]{:S(2)}, u32[]{:S(2)}) %collective-permute-start.2) | collective-permute-done | bytes 135200 | tf_op jit(solution)/shard_map/ppermute | solution.py:479
  21.0 0.0 collective-permute-done.4.refs_4_
  21.0 1.5 %collective-permute-start.5 = (bf16[528,128]{1,0:T(8,128)(2,1)S(1)}, bf16[528,128]{1,0:T(8,128)(2,1)S(1)}, u32[]{:S(2)}, u32[]{:S(2)}) collective-permute-start(bf16[528,128]{1,0:T(8,128)(2,1)S(1)} %collective-permute-done.2.refs_3_.refs_8_), channel_id=1, source_target_pairs={{0,4},{2,6},{4,12},{6,14},{12,8},{14,10},{8,0},{10,2},{1,5},{3,7},... | collective-permute-start | bytes 405512 | tf_op jit(solution)/shard_map/ppermute | solution.py:479
  22.5 2.0 %collective-permute-done.6.refs_6_.refs_11_ = bf16[528,128]{1,0:T(8,128)(2,1)S(1)} collective-permute-done((bf16[528,128]{1,0:T(8,128)(2,1)S(1)}, bf16[528,128]{1,0:T(8,128)(2,1)S(1)}, u32[]{:S(2)}, u32[]{:S(2)}) %collective-permute-start.6) | collective-permute-done | bytes 135200 | tf_op jit(solution)/shard_map/ppermute | solution.py:479
  24.5 3.1 %collective-permute-done.5.refs_5_.refs_10_ = bf16[528,128]{1,0:T(8,128)(2,1)S(1)} collective-permute-done((bf16[528,128]{1,0:T(8,128)(2,1)S(1)}, bf16[528,128]{1,0:T(8,128)(2,1)S(1)}, u32[]{:S(2)}, u32[]{:S(2)}) %collective-permute-start.5) | collective-permute-done | bytes 135200 | tf_op jit(solution)/shard_map/ppermute | solution.py:479
  27.6 0.2 collective-permute-start.7
  27.9 5.7 %collective-permute-done.7.refs_7_.refs_12_ = bf16[528,128]{1,0:T(8,128)(2,1)S(1)} collective-permute-done((bf16[528,128]{1,0:T(8,128)(2,1)S(1)}, bf16[528,128]{1,0:T(8,128)(2,1)S(1)}, u32[]{:S(2)}, u32[]{:S(2)}) %collective-permute-start.7) | collective-permute-done | bytes 135200 | tf_op jit(solution)/shard_map/ppermute | solution.py:479
  33.5 0.7 advantages.1
  34.2 0.0 copy-start.5
  34.2 5.2 %tree_attention_backward.2 = (bf16[128,640]{1,0:T(8,128)(2,1)S(1)}, bf16[128,640]{1,0:T(8,128)(2,1)S(1)}, bf16[4,2,2,128,128]{4,3,2,1,0:T(8,128)(2,1)}) custom-call(s32[8]{0:T(128)S(1)} %copy-done.4, f32[2,128,128]{2,1,0:T(8,128)S(1)} %get-tuple-element.46.refs_1_, f32[2,640,128]{2,1,0:T(8,128)S(1)} %get-tuple-element.39.refs_2_, ...), custom_call_target="tpu_custom_call" | custom-call | flops 1048576000 | bytes 8388608 | tf_op jit(solution)/shard_map/tree_attention_backward/pallas_call | solution.py:395
  39.4 0.0 copy-done.5
  39.4 4.3 %all-to-all-start = ((bf16[4,2,2,128,128]{4,3,2,1,0:T(8,128)(2,1)}), bf16[4,2,2,128,128]{4,3,2,1,0:T(8,128)(2,1)S(1)}, u32[]{:S(2)}, u32[]{:S(2)}) async-start(bf16[4,2,2,128,128]{4,3,2,1,0:T(8,128)(2,1)} %get-tuple-element.57), calls=%async_computation | async-start | bytes 1048576 | tf_op jit(solution)/shard_map/all_to_all | solution.py:531
  43.8 1.5 %collective-permute-start.8 = (bf16[2,5,128,128]{3,2,1,0:T(8,128)(2,1)S(1)}, bf16[2,5,128,128]{3,2,1,0:T(8,128)(2,1)S(1)}, u32[]{:S(2)}, u32[]{:S(2)}) collective-permute-start(bf16[2,5,128,128]{3,2,1,0:T(8,128)(2,1)S(1)} %get-tuple-element.51), channel_id=1, source_target_pairs={{0,2},{2,0},{4,6},{6,4},{8,10},{10,8},{12,14},{14,12},{1,3},{3,1},... | collective-permute-start | bytes 983048 | tf_op jit(solution)/shard_map/ppermute | solution.py:479
  45.2 5.6 %collective-permute-done.8.refs_4_ = bf16[2,5,128,128]{3,2,1,0:T(8,128)(2,1)S(1)} collective-permute-done((bf16[2,5,128,128]{3,2,1,0:T(8,128)(2,1)S(1)}, bf16[2,5,128,128]{3,2,1,0:T(8,128)(2,1)S(1)}, u32[]{:S(2)}, u32[]{:S(2)}) %collective-permute-start.8) | collective-permute-done | bytes 327712 | tf_op jit(solution)/shard_map/ppermute | solution.py:479
  50.8 0.0 copy-start.6
  50.8 0.9 %copy-done.6 = f32[2,128,128]{2,1,0:T(8,128)S(1)} copy-done((f32[2,128,128]{2,1,0:T(8,128)S(1)}, f32[2,128,128]{2,1,0:T(8,128)}, u32[]{:S(2)}) %copy-start.6) | copy-done | bytes 131096
  51.7 5.2 %tree_attention_backward.3 = (bf16[128,640]{1,0:T(8,128)(2,1)S(1)}, bf16[128,640]{1,0:T(8,128)(2,1)S(1)}, bf16[4,2,2,128,128]{4,3,2,1,0:T(8,128)(2,1)}) custom-call(s32[8]{0:T(128)S(1)} %copy-done.4, f32[2,128,128]{2,1,0:T(8,128)S(1)} %copy-done.6, f32[2,640,128]{2,1,0:T(8,128)S(1)} %get-tuple-element.39.refs_2_, ...), custom_call_target="tpu_custom_call" | custom-call | flops 1048576000 | bytes 8388608 | tf_op jit(solution)/shard_map/tree_attention_backward/pallas_call | solution.py:395
  57.0 0.0 all-to-all-done.refs_2_
  57.0 5.1 %all-to-all-start.1 = ((bf16[4,2,2,128,128]{4,3,2,1,0:T(8,128)(2,1)}), bf16[4,2,2,128,128]{4,3,2,1,0:T(8,128)(2,1)S(1)}, u32[]{:S(2)}, u32[]{:S(2)}) async-start(bf16[4,2,2,128,128]{4,3,2,1,0:T(8,128)(2,1)} %get-tuple-element.59), calls=%async_computation.1 | async-start | bytes 1048576 | tf_op jit(solution)/shard_map/all_to_all | solution.py:531
  62.1 1.5 %collective-permute-start.9 = (bf16[128,640]{1,0:T(8,128)(2,1)S(1)}, bf16[128,640]{1,0:T(8,128)(2,1)S(1)}, u32[]{:S(2)}, u32[]{:S(2)}) collective-permute-start(bf16[128,640]{1,0:T(8,128)(2,1)S(1)} %get-tuple-element.54), channel_id=1, source_target_pairs={{0,2},{2,0},{4,6},{6,4},{8,10},{10,8},{12,14},{14,12},{1,3},{3,1},... | collective-permute-start | bytes 491528 | tf_op jit(solution)/shard_map/ppermute | solution.py:479
  63.6 0.5 collective-permute-start.10
  64.1 1.6 %collective-permute-start.11 = (bf16[2,128,128]{2,1,0:T(8,128)(2,1)S(1)}, bf16[2,128,128]{2,1,0:T(8,128)(2,1)S(1)}, u32[]{:S(2)}, u32[]{:S(2)}) collective-permute-start(bf16[2,128,128]{2,1,0:T(8,128)(2,1)S(1)} %fusion), channel_id=1, source_target_pairs={{0,2},{2,0},{4,6},{6,4},{8,10},{10,8},{12,14},{14,12},{1,3},{3,1},... | collective-permute-start | bytes 196616 | tf_op jit(solution)/shard_map/ppermute | solution.py:479
  65.7 6.7 %all-to-all-done.1.refs_3_ = bf16[4,2,2,128,128]{4,3,2,1,0:T(8,128)(2,1)S(1)} async-done(((bf16[4,2,2,128,128]{4,3,2,1,0:T(8,128)(2,1)}), bf16[4,2,2,128,128]{4,3,2,1,0:T(8,128)(2,1)S(1)}, u32[]{:S(2)}, u32[]{:S(2)}) %all-to-all-start.1) | async-done | bytes 524320 | tf_op jit(solution)/shard_map/all_to_all | solution.py:531
  72.4 1.6 %collective-permute-start.12 = (bf16[2,128,128]{2,1,0:T(8,128)(2,1)S(1)}, bf16[2,128,128]{2,1,0:T(8,128)(2,1)S(1)}, u32[]{:S(2)}, u32[]{:S(2)}) collective-permute-start(bf16[2,128,128]{2,1,0:T(8,128)(2,1)S(1)} %fusion.1), channel_id=1, source_target_pairs={{0,2},{2,0},{4,6},{6,4},{8,10},{10,8},{12,14},{14,12},{1,3},{3,1},... | collective-permute-start | bytes 196616 | tf_op jit(solution)/shard_map/ppermute | solution.py:479
  74.0 0.0 collective-permute-done.9.refs_2_
  74.0 0.0 collective-permute-done.10.refs_3_
  74.0 0.9 %join_queries.1 = bf16[128,2560]{1,0:T(8,128)(2,1)} custom-call(bf16[128,640]{1,0:T(8,128)(2,1)S(1)} %get-tuple-element.48.refs_0_, bf16[128,640]{1,0:T(8,128)(2,1)S(1)} %get-tuple-element.52.refs_1_, bf16[128,640]{1,0:T(8,128)(2,1)S(1)} %collective-permute-done.9.refs_2_, bf16[128,640]{1,0:T(8,128)(2,1)S(1)} %collective-permute-done.10.refs_3_), custom_call_target="tpu_custom_call" | custom-call | bytes 1310720 | tf_op jit(solution)/shard_map/join_queries/pallas_call | solution.py:433
  74.9 0.0 collective-permute-done.11.refs_0_
  74.9 1.9 %collective-permute-done.12.refs_1_ = bf16[2,128,128]{2,1,0:T(8,128)(2,1)S(1)} collective-permute-done((bf16[2,128,128]{2,1,0:T(8,128)(2,1)S(1)}, bf16[2,128,128]{2,1,0:T(8,128)(2,1)S(1)}, u32[]{:S(2)}, u32[]{:S(2)}) %collective-permute-start.12) | collective-permute-done | bytes 65568 | tf_op jit(solution)/shard_map/ppermute | solution.py:479
  76.7 0.8 join_keys.1
  (2 shorter events, 0.1 us)
Async XLA Ops:
  2.5 7.0 %collective-permute-start = (bf16[528,128]{1,0:T(8,128)(2,1)}, bf16[528,128]{1,0:T(8,128)(2,1)S(1)}, u32[]{:S(2)}, u32[]{:S(2)}) collective-permute-start(bf16[528,128]{1,0:T(8,128)(2,1)} %get-tuple-element.35), channel_id=1, source_target_pairs={{0,2},{2,0},{4,6},{6,4},{8,10},{10,8},{12,14},{14,12},{1,3},{3,1},... | collective-permute-start | bytes 405512 | tf_op jit(solution)/shard_map/ppermute | solution.py:479
  5.4 6.2 %collective-permute-start.1 = (bf16[528,128]{1,0:T(8,128)(2,1)}, bf16[528,128]{1,0:T(8,128)(2,1)S(1)}, u32[]{:S(2)}, u32[]{:S(2)}) collective-permute-start(bf16[528,128]{1,0:T(8,128)(2,1)} %get-tuple-element.34.refs_0_.refs_5_), channel_id=1, source_target_pairs={{0,4},{2,6},{4,12},{6,14},{12,8},{14,10},{8,0},{10,2},{1,5},{3,7},... | collective-permute-start | bytes 405512 | tf_op jit(solution)/shard_map/ppermute | solution.py:479
  7.0 1.1 %copy-start = (bf16[128,2560]{1,0:T(8,128)(2,1)S(1)}, bf16[128,2560]{1,0:T(8,128)(2,1)}, u32[]{:S(2)}) copy-start(bf16[128,2560]{1,0:T(8,128)(2,1)} %q_ref) | copy-start | bytes 1966084
  8.1 1.1 %copy-start.1 = (bf16[128,2560]{1,0:T(8,128)(2,1)S(1)}, bf16[128,2560]{1,0:T(8,128)(2,1)}, u32[]{:S(2)}) copy-start(bf16[128,2560]{1,0:T(8,128)(2,1)} %dir_ref.1) | copy-start | bytes 1966084
  9.2 7.1 %copy-start.2 = (bf16[528,128]{1,0:T(8,128)(2,1)S(1)}, bf16[528,128]{1,0:T(8,128)(2,1)}, u32[]{:S(2)}) copy-start(bf16[528,128]{1,0:T(8,128)(2,1)} %get-tuple-element.34.refs_0_.refs_5_) | copy-start | bytes 405508
  9.4 6.9 %copy-start.3 = (s32[8]{0:T(128)S(1)}, s32[8]{0:T(128)}, u32[]{:S(2)}) copy-start(s32[8]{0:T(128)} %lengths_s.1) | copy-start | bytes 100
  9.4 6.9 %copy-start.4 = (s32[8]{0:T(128)S(1)}, s32[8]{0:T(128)}, u32[]{:S(2)}) copy-start(s32[8]{0:T(128)} %refs_0_.3) | copy-start | bytes 100
  11.6 9.4 %collective-permute-start.4 = (bf16[2,5,128,128]{3,2,1,0:T(8,128)(2,1)S(1)}, bf16[2,5,128,128]{3,2,1,0:T(8,128)(2,1)S(1)}, u32[]{:S(2)}, u32[]{:S(2)}) collective-permute-start(bf16[2,5,128,128]{3,2,1,0:T(8,128)(2,1)S(1)} %get-tuple-element.42), channel_id=1, source_target_pairs={{0,2},{2,0},{4,6},{6,4},{8,10},{10,8},{12,14},{14,12},{1,3},{3,1},... | collective-permute-start | bytes 983048 | tf_op jit(solution)/shard_map/ppermute | solution.py:479
  12.1 6.5 %collective-permute-start.3 = (bf16[528,128]{1,0:T(8,128)(2,1)S(1)}, bf16[528,128]{1,0:T(8,128)(2,1)S(1)}, u32[]{:S(2)}, u32[]{:S(2)}) collective-permute-start(bf16[528,128]{1,0:T(8,128)(2,1)S(1)} %collective-permute-done.1.refs_2_.refs_7_), channel_id=1, source_target_pairs={{0,4},{2,6},{4,12},{6,14},{12,8},{14,10},{8,0},{10,2},{1,5},{3,7},... | collective-permute-start | bytes 405512 | tf_op jit(solution)/shard_map/ppermute | solution.py:479
  13.0 8.0 %collective-permute-start.2 = (bf16[528,128]{1,0:T(8,128)(2,1)S(1)}, bf16[528,128]{1,0:T(8,128)(2,1)S(1)}, u32[]{:S(2)}, u32[]{:S(2)}) collective-permute-start(bf16[528,128]{1,0:T(8,128)(2,1)S(1)} %collective-permute-done.refs_1_.refs_6_), channel_id=1, source_target_pairs={{0,4},{2,6},{4,12},{6,14},{12,8},{14,10},{8,0},{10,2},{1,5},{3,7},... | collective-permute-start | bytes 405512 | tf_op jit(solution)/shard_map/ppermute | solution.py:479
  18.6 5.9 %collective-permute-start.6 = (bf16[528,128]{1,0:T(8,128)(2,1)S(1)}, bf16[528,128]{1,0:T(8,128)(2,1)S(1)}, u32[]{:S(2)}, u32[]{:S(2)}) collective-permute-start(bf16[528,128]{1,0:T(8,128)(2,1)S(1)} %collective-permute-done.3.refs_4_.refs_9_), channel_id=1, source_target_pairs={{0,4},{2,6},{4,12},{6,14},{12,8},{14,10},{8,0},{10,2},{1,5},{3,7},... | collective-permute-start | bytes 405512 | tf_op jit(solution)/shard_map/ppermute | solution.py:479
  21.0 6.6 %collective-permute-start.5 = (bf16[528,128]{1,0:T(8,128)(2,1)S(1)}, bf16[528,128]{1,0:T(8,128)(2,1)S(1)}, u32[]{:S(2)}, u32[]{:S(2)}) collective-permute-start(bf16[528,128]{1,0:T(8,128)(2,1)S(1)} %collective-permute-done.2.refs_3_.refs_8_), channel_id=1, source_target_pairs={{0,4},{2,6},{4,12},{6,14},{12,8},{14,10},{8,0},{10,2},{1,5},{3,7},... | collective-permute-start | bytes 405512 | tf_op jit(solution)/shard_map/ppermute | solution.py:479
  27.6 5.9 %collective-permute-start.7 = (bf16[528,128]{1,0:T(8,128)(2,1)S(1)}, bf16[528,128]{1,0:T(8,128)(2,1)S(1)}, u32[]{:S(2)}, u32[]{:S(2)}) collective-permute-start(bf16[528,128]{1,0:T(8,128)(2,1)S(1)} %collective-permute-done.5.refs_5_.refs_10_), channel_id=1, source_target_pairs={{0,4},{2,6},{4,12},{6,14},{12,8},{14,10},{8,0},{10,2},{1,5},{3,7},... | collective-permute-start | bytes 405512 | tf_op jit(solution)/shard_map/ppermute | solution.py:479
  34.2 5.2 %copy-start.5 = (f32[2,128,128]{2,1,0:T(8,128)}, f32[2,128,128]{2,1,0:T(8,128)S(1)}, u32[]{:S(2)}) copy-start(f32[2,128,128]{2,1,0:T(8,128)S(1)} %get-tuple-element.46.refs_1_) | copy-start | bytes 393220
  39.4 17.6 %all-to-all-start = ((bf16[4,2,2,128,128]{4,3,2,1,0:T(8,128)(2,1)}), bf16[4,2,2,128,128]{4,3,2,1,0:T(8,128)(2,1)S(1)}, u32[]{:S(2)}, u32[]{:S(2)}) async-start(bf16[4,2,2,128,128]{4,3,2,1,0:T(8,128)(2,1)} %get-tuple-element.57), calls=%async_computation | async-start | bytes 1048576 | tf_op jit(solution)/shard_map/all_to_all | solution.py:531
  43.8 7.1 %collective-permute-start.8 = (bf16[2,5,128,128]{3,2,1,0:T(8,128)(2,1)S(1)}, bf16[2,5,128,128]{3,2,1,0:T(8,128)(2,1)S(1)}, u32[]{:S(2)}, u32[]{:S(2)}) collective-permute-start(bf16[2,5,128,128]{3,2,1,0:T(8,128)(2,1)S(1)} %get-tuple-element.51), channel_id=1, source_target_pairs={{0,2},{2,0},{4,6},{6,4},{8,10},{10,8},{12,14},{14,12},{1,3},{3,1},... | collective-permute-start | bytes 983048 | tf_op jit(solution)/shard_map/ppermute | solution.py:479
  50.8 0.9 %copy-start.6 = (f32[2,128,128]{2,1,0:T(8,128)S(1)}, f32[2,128,128]{2,1,0:T(8,128)}, u32[]{:S(2)}) copy-start(f32[2,128,128]{2,1,0:T(8,128)} %copy-done.5) | copy-start | bytes 393220
  57.0 15.4 %all-to-all-start.1 = ((bf16[4,2,2,128,128]{4,3,2,1,0:T(8,128)(2,1)}), bf16[4,2,2,128,128]{4,3,2,1,0:T(8,128)(2,1)S(1)}, u32[]{:S(2)}, u32[]{:S(2)}) async-start(bf16[4,2,2,128,128]{4,3,2,1,0:T(8,128)(2,1)} %get-tuple-element.59), calls=%async_computation.1 | async-start | bytes 1048576 | tf_op jit(solution)/shard_map/all_to_all | solution.py:531
  62.1 11.9 %collective-permute-start.9 = (bf16[128,640]{1,0:T(8,128)(2,1)S(1)}, bf16[128,640]{1,0:T(8,128)(2,1)S(1)}, u32[]{:S(2)}, u32[]{:S(2)}) collective-permute-start(bf16[128,640]{1,0:T(8,128)(2,1)S(1)} %get-tuple-element.54), channel_id=1, source_target_pairs={{0,2},{2,0},{4,6},{6,4},{8,10},{10,8},{12,14},{14,12},{1,3},{3,1},... | collective-permute-start | bytes 491528 | tf_op jit(solution)/shard_map/ppermute | solution.py:479
  63.6 10.4 %collective-permute-start.10 = (bf16[128,640]{1,0:T(8,128)(2,1)S(1)}, bf16[128,640]{1,0:T(8,128)(2,1)S(1)}, u32[]{:S(2)}, u32[]{:S(2)}) collective-permute-start(bf16[128,640]{1,0:T(8,128)(2,1)S(1)} %get-tuple-element.56), channel_id=1, source_target_pairs={{0,2},{2,0},{4,6},{6,4},{8,10},{10,8},{12,14},{14,12},{1,3},{3,1},... | collective-permute-start | bytes 491528 | tf_op jit(solution)/shard_map/ppermute | solution.py:479
  64.1 10.7 %collective-permute-start.11 = (bf16[2,128,128]{2,1,0:T(8,128)(2,1)S(1)}, bf16[2,128,128]{2,1,0:T(8,128)(2,1)S(1)}, u32[]{:S(2)}, u32[]{:S(2)}) collective-permute-start(bf16[2,128,128]{2,1,0:T(8,128)(2,1)S(1)} %fusion), channel_id=1, source_target_pairs={{0,2},{2,0},{4,6},{6,4},{8,10},{10,8},{12,14},{14,12},{1,3},{3,1},... | collective-permute-start | bytes 196616 | tf_op jit(solution)/shard_map/ppermute | solution.py:479
  72.4 4.3 %collective-permute-start.12 = (bf16[2,128,128]{2,1,0:T(8,128)(2,1)S(1)}, bf16[2,128,128]{2,1,0:T(8,128)(2,1)S(1)}, u32[]{:S(2)}, u32[]{:S(2)}) collective-permute-start(bf16[2,128,128]{2,1,0:T(8,128)(2,1)S(1)} %fusion.1), channel_id=1, source_target_pairs={{0,2},{2,0},{4,6},{6,4},{8,10},{10,8},{12,14},{14,12},{1,3},{3,1},... | collective-permute-start | bytes 196616 | tf_op jit(solution)/shard_map/ppermute | solution.py:479

commit v12 on v9

--- a/solution.py
+++ b/solution.py
@@ -145,10 +145,6 @@
     return jnp.where(segment >= 0, known, -1).astype(jnp.int32)
 
 
-def ring_place(pair):
-    return jnp.where(pair >= 2, 5 - pair, pair)
-
-
 def segment_of(own, segs, i):
     part = lax.rem(own, segs)
     return own - part + lax.rem(part + i, segs)
@@ -258,13 +254,12 @@
         firsts = read_terms(term_refs[0])[1]
     else:
         own = lax.axis_index("seg")
-        part, pair, pairs = lax.rem(own, segs), own // segs, count // segs
+        part, pair = lax.rem(own, segs), own // segs
         seg_id = lax.broadcasted_iota(jnp.int32, (count, length), 0)
         firsts = jnp.zeros((count, length), jnp.float32)
         for index, ref in enumerate(term_refs):
             step, side = divmod(index, segs)
-            place = lax.rem(ring_place(pair) - step + pairs, pairs)
-            seg = ring_place(place) * segs + lax.rem(part + side, segs)
+            seg = (pair ^ step) * segs + lax.rem(part + side, segs)
             firsts = jnp.where(seg_id == seg, read_terms(ref)[1], firsts)
     for i in range(segs):
         later_value = jnp.sum(weights_ref[i, 0] * firsts, axis=(0, 1), keepdims=True)
@@ -330,8 +325,7 @@
                 chosen.append(slot)
             else:
                 known = jnp.maximum(ancestor, 0)
-                step = ring_place((own - part) // segs) - ring_place(known // segs)
-                step = lax.rem(step + sources // segs, sources // segs)
+                step = (own // segs) ^ (known // segs)
                 turn = lax.rem(lax.rem(known, segs) - part + segs, segs)
                 chosen.append(jnp.where(ancestor >= 0, step * segs + turn, 0))
         q_list = [query_refs[i][0, j] for j in range(group_size)]
@@ -487,32 +481,22 @@
     chunks = key_vectors.shape[1] // HD // 2
     swap = [(i, i ^ 1) for i in range(groups)]
     steps = range(1, groups // 2)
-    ring = [0, 1, 3, 2]
-
-    def turn(distance):
-        pairs = []
-        for place, pair in enumerate(ring):
-            target = ring[(place + distance) % len(ring)]
-            pairs += [(2 * pair + x, 2 * target + x) for x in range(2)]
-        return pairs
-
-    climb = turn(1)
-    down = {d: turn(-d) for d in steps}
+    meet = {bits: [(i, i ^ (2 * bits)) for i in range(groups)] for bits in steps}
 
     kept, given = pack(lengths, key_vectors, value_vectors, token_rows, 2, log_rate)
     taken = permute(given, swap)
-    chain = [kept, permute(kept, climb)]
-    other = [after(taken, chain[1])]
+    kept_two, kept_one = permute(kept, meet[2]), permute(kept, meet[1])
     kept_q, given_q = pack_queries(after(queries, kept), direction, 2, chunks)
-    taken_q = [permute(after(given_q[0], *other), swap)]
-    bias, columns, weights = prepare(parents, lengths, [kept, other[0]], length, log_rate)
-    for step in steps:
-        if step + 1 in steps:
-            chain.append(permute(chain[-1], climb))
-        gate = [bias, taken_q[0]] if step == 1 else []
-        other.append(after(permute(other[-1], climb), chain[-1], *gate))
+    gated = after(taken, kept_two, kept_one)
+    taken_two, taken_one = permute(gated, meet[2]), permute(gated, meet[1])
+    kept_three = permute(kept_two, meet[1])
+    bias, columns, weights = prepare(parents, lengths, [kept, taken], length, log_rate)
+    taken_q = [permute(after(given_q[0], gated), swap)]
+    taken_three = permute(after(taken_two, taken_one, kept_three, bias, taken_q[0]), meet[1])
     for block in given_q[1:]:
-        taken_q.append(permute(after(block, taken_q[-1]), swap))
+        taken_q.append(permute(after(block, taken_three), swap))
+    chain = [kept, kept_one, kept_two, kept_three]
+    other = [taken, taken_one, taken_two, taken_three]
     blocks = [block for pair in zip(chain, other) for block in pair]
     row, advantages = advantages_of(columns, weights, blocks)
 
@@ -526,9 +510,9 @@
 
     summands = []
     for dkv in dkv_list:
-        arrived = [permute(dkv[d], down[d]) for d in steps[::-1]]
+        arrived = [permute(dkv[bits], meet[bits]) for bits in steps[::-1]]
         summands.append([after(dkv[0], dq_own[-1])] + arrived)
-    dq_back = [permute(block, swap) for block in dq_back]
+    dq_back = [permute(after(block, dq_own[-1]), swap) for block in dq_back]
     others = []
     for blocks in summands:
         total = sum(block[1].astype(jnp.float32) for block in blocks)

time: 64.8 us -> 67.6 us (1.043)
  waiting for transfers between devices: 15.7 us -> 23.4 us
  starting transfers between devices: 31.4 us -> 26.5 us
    ppermute x19, waiting for transfers between devices: 15.7 us -> 23.4 us  [permute(): return lax.ppermute(array, 'seg', pairs)]
    ppermute x19, starting transfers between devices: 31.4 us -> 26.5 us  [permute(): return lax.ppermute(array, 'seg', pairs)]
  transfers between devices with their start and end apart: 19 -> 19, of which waited for: 9 -> 10; matrix products, arithmetic and copies ran while one was open for 0% -> 0% of each run, Pallas kernels for 18% -> 18%
where the time goes in v12:
time: 67.6 us; the launch traced here: 67.4 us
  starting transfers between devices  26.5 us (39%)
  waiting for transfers between devices  23.4 us (35%)
  Pallas kernels  14.5 us (21%)
  local copies, waits for them, and re-layouts  2.19 us (3%)
  between operations  0.72 us (1%)
    ppermute x19, starting transfers between devices, permute(): return lax.ppermute(array, 'seg', pairs)  26.5 us
    ppermute x19, waiting for transfers between devices, permute(): return lax.ppermute(array, 'seg', pairs)  23.4 us
    pallas_call x2, Pallas kernels, attend(): pl.pallas_call(functools.partial(attend_kernel, DEPTH, chunk, segs, sourc...  8.85 us
    unnamed x10, local copies, waits for them, and re-layouts  2.19 us
    pallas_call x1, Pallas kernels, pack(): pl.pallas_call(functools.partial(pack_kernel, log_rate), out_shape=(block...  1.86 us
  transfers between devices with their start and end apart: 19, of which 10 were waited for; matrix products, arithmetic and copies ran while one was open for 0% of the time, Pallas kernels for 18%

profile of v12, /device:TPU:0, one launch (start us, length us, event | category | flops | bytes accessed | tf_op | source)
XLA Modules:
  0.0 67.4 jit_solution(10557836865789489177)
XLA Ops:
  0.6 1.9 %pack_keys_values.1 = (bf16[528,128]{1,0:T(8,128)(2,1)}, bf16[528,128]{1,0:T(8,128)(2,1)}) custom-call(s32[8]{0:T(128)} %lengths_s.1, bf16[128,512]{1,0:T(8,128)(2,1)} %k_ref.1, bf16[128,512]{1,0:T(8,128)(2,1)} %v_ref.1, f32[1,128]{1,0:T(1,128)} %bitcast.9, f32[1,128]{1,0:T(1,128)} %bitcast.10, f32[1,128]{1,0:T(1,128)} %bitcast.11, f32[1,128]{1,0:T(1,128)} %bitcast.12), custom_call_target="tpu_custom_call" | custom-call | flops 12800 | bytes 524288 | tf_op jit(solution)/shard_map/pack_keys_values/pallas_call | solution.py:101
  2.5 2.9 %collective-permute-start = (bf16[528,128]{1,0:T(8,128)(2,1)}, bf16[528,128]{1,0:T(8,128)(2,1)S(1)}, u32[]{:S(2)}, u32[]{:S(2)}) collective-permute-start(bf16[528,128]{1,0:T(8,128)(2,1)} %get-tuple-element.39), channel_id=1, source_target_pairs={{0,2},{2,0},{4,6},{6,4},{8,10},{10,8},{12,14},{14,12},{1,3},{3,1},... | collective-permute-start | bytes 405512 | tf_op jit(solution)/shard_map/ppermute | solution.py:471
  5.4 2.6 %collective-permute-start.2 = (bf16[528,128]{1,0:T(8,128)(2,1)}, bf16[528,128]{1,0:T(8,128)(2,1)S(1)}, u32[]{:S(2)}, u32[]{:S(2)}) collective-permute-start(bf16[528,128]{1,0:T(8,128)(2,1)} %get-tuple-element.38.refs_0_.refs_5_), channel_id=1, source_target_pairs={{0,8},{2,10},{4,12},{6,14},{8,0},{10,2},{12,4},{14,6},{1,9},{3,11}... | collective-permute-start | bytes 405512 | tf_op jit(solution)/shard_map/ppermute | solution.py:471
  8.0 1.6 %collective-permute-start.1 = (bf16[528,128]{1,0:T(8,128)(2,1)}, bf16[528,128]{1,0:T(8,128)(2,1)S(1)}, u32[]{:S(2)}, u32[]{:S(2)}) collective-permute-start(bf16[528,128]{1,0:T(8,128)(2,1)} %get-tuple-element.38.refs_0_.refs_5_), channel_id=1, source_target_pairs={{0,4},{2,6},{4,0},{6,2},{8,12},{10,14},{12,8},{14,10},{1,5},{3,7},... | collective-permute-start | bytes 405512 | tf_op jit(solution)/shard_map/ppermute | solution.py:471
  9.6 0.0 copy-start
  9.6 1.1 %copy-done = bf16[128,2560]{1,0:T(8,128)(2,1)S(1)} copy-done((bf16[128,2560]{1,0:T(8,128)(2,1)S(1)}, bf16[128,2560]{1,0:T(8,128)(2,1)}, u32[]{:S(2)}) %copy-start) | copy-done | bytes 655384
  10.7 0.0 copy-start.1
  10.7 1.1 %copy-done.1 = bf16[128,2560]{1,0:T(8,128)(2,1)S(1)} copy-done((bf16[128,2560]{1,0:T(8,128)(2,1)S(1)}, bf16[128,2560]{1,0:T(8,128)(2,1)}, u32[]{:S(2)}) %copy-start.1) | copy-done | bytes 655384
  11.8 0.0 copy-start.2
  11.8 0.2 pack_queries.1
  12.0 0.0 copy-start.3
  12.0 0.0 copy-start.4
  12.0 0.0 collective-permute-done.refs_1_.refs_6_
  12.0 2.5 %collective-permute-done.2.refs_4_.refs_9_ = bf16[528,128]{1,0:T(8,128)(2,1)S(1)} collective-permute-done((bf16[528,128]{1,0:T(8,128)(2,1)}, bf16[528,128]{1,0:T(8,128)(2,1)S(1)}, u32[]{:S(2)}, u32[]{:S(2)}) %collective-permute-start.2) | collective-permute-done | bytes 135200 | tf_op jit(solution)/shard_map/ppermute | solution.py:471
  14.6 0.2 collective-permute-done.1.refs_2_.refs_7_
  14.8 0.5 collective-permute-start.6
  15.3 1.4 %collective-permute-start.5 = (bf16[528,128]{1,0:T(8,128)(2,1)S(1)}, bf16[528,128]{1,0:T(8,128)(2,1)S(1)}, u32[]{:S(2)}, u32[]{:S(2)}) collective-permute-start(bf16[528,128]{1,0:T(8,128)(2,1)S(1)} %collective-permute-done.2.refs_4_.refs_9_), channel_id=1, source_target_pairs={{0,4},{2,6},{4,0},{6,2},{8,12},{10,14},{12,8},{14,10},{1,5},{3,7},... | collective-permute-start | bytes 405512 | tf_op jit(solution)/shard_map/ppermute | solution.py:471
  16.7 2.4 %collective-permute-start.4 = (bf16[528,128]{1,0:T(8,128)(2,1)S(1)}, bf16[528,128]{1,0:T(8,128)(2,1)S(1)}, u32[]{:S(2)}, u32[]{:S(2)}) collective-permute-start(bf16[528,128]{1,0:T(8,128)(2,1)S(1)} %collective-permute-done.refs_1_.refs_6_), channel_id=1, source_target_pairs={{0,8},{2,10},{4,12},{6,14},{8,0},{10,2},{12,4},{14,6},{1,9},{3,11}... | collective-permute-start | bytes 405512 | tf_op jit(solution)/shard_map/ppermute | solution.py:471
  19.1 0.0 collective-permute-start.3
  19.1 0.0 copy-done.2
  19.1 0.0 copy-done.3
  19.1 0.0 copy-done.4
  19.1 1.2 %prepare.1 = (f32[2,640,128]{2,1,0:T(8,128)S(1)}, f32[2,3,128,128]{3,2,1,0:T(8,128)S(1)}, f32[2,2,8,128]{3,2,1,0:T(8,128)S(1)}) custom-call(s32[8]{0:T(128)S(1)} %copy-done.4, s32[8]{0:T(128)S(1)} %copy-done.3, bf16[528,128]{1,0:T(8,128)(2,1)S(1)} %copy-done.2, bf16[528,128]{1,0:T(8,128)(2,1)S(1)} %collective-permute-done.refs_1_.refs_6_), custom_call_target="tpu_custom_call" | custom-call | flops 3276800 | bytes 655360 | tf_op jit(solution)/shard_map/prepare/pallas_call | solution.py:230
  20.3 3.1 %collective-permute-done.5.refs_6_.refs_11_ = bf16[528,128]{1,0:T(8,128)(2,1)S(1)} collective-permute-done((bf16[528,128]{1,0:T(8,128)(2,1)S(1)}, bf16[528,128]{1,0:T(8,128)(2,1)S(1)}, u32[]{:S(2)}, u32[]{:S(2)}) %collective-permute-start.5) | collective-permute-done | bytes 135200 | tf_op jit(solution)/shard_map/ppermute | solution.py:471
  23.5 1.6 %collective-permute-done.4.refs_5_.refs_10_ = bf16[528,128]{1,0:T(8,128)(2,1)S(1)} collective-permute-done((bf16[528,128]{1,0:T(8,128)(2,1)S(1)}, bf16[528,128]{1,0:T(8,128)(2,1)S(1)}, u32[]{:S(2)}, u32[]{:S(2)}) %collective-permute-start.4) | collective-permute-done | bytes 135200 | tf_op jit(solution)/shard_map/ppermute | solution.py:471
  25.0 1.0 %collective-permute-done.3.refs_3_.refs_8_ = bf16[528,128]{1,0:T(8,128)(2,1)S(1)} collective-permute-done((bf16[528,128]{1,0:T(8,128)(2,1)S(1)}, bf16[528,128]{1,0:T(8,128)(2,1)S(1)}, u32[]{:S(2)}, u32[]{:S(2)}) %collective-permute-start.3) | collective-permute-done | bytes 135200 | tf_op jit(solution)/shard_map/ppermute | solution.py:471
  26.1 0.0 collective-permute-done.6.refs_4_
  26.1 1.4 %collective-permute-start.7 = (bf16[528,128]{1,0:T(8,128)(2,1)S(1)}, bf16[528,128]{1,0:T(8,128)(2,1)S(1)}, u32[]{:S(2)}, u32[]{:S(2)}) collective-permute-start(bf16[528,128]{1,0:T(8,128)(2,1)S(1)} %collective-permute-done.4.refs_5_.refs_10_), channel_id=1, source_target_pairs={{0,4},{2,6},{4,0},{6,2},{8,12},{10,14},{12,8},{14,10},{1,5},{3,7},... | collective-permute-start | bytes 405512 | tf_op jit(solution)/shard_map/ppermute | solution.py:471
  27.5 3.6 %collective-permute-done.7.refs_7_.refs_12_ = bf16[528,128]{1,0:T(8,128)(2,1)S(1)} collective-permute-done((bf16[528,128]{1,0:T(8,128)(2,1)S(1)}, bf16[528,128]{1,0:T(8,128)(2,1)S(1)}, u32[]{:S(2)}, u32[]{:S(2)}) %collective-permute-start.7) | collective-permute-done | bytes 135200 | tf_op jit(solution)/shard_map/ppermute | solution.py:471
  31.1 1.5 %collective-permute-start.8 = (bf16[2,5,128,128]{3,2,1,0:T(8,128)(2,1)S(1)}, bf16[2,5,128,128]{3,2,1,0:T(8,128)(2,1)S(1)}, u32[]{:S(2)}, u32[]{:S(2)}) collective-permute-start(bf16[2,5,128,128]{3,2,1,0:T(8,128)(2,1)S(1)} %get-tuple-element.53), channel_id=1, source_target_pairs={{0,2},{2,0},{4,6},{6,4},{8,10},{10,8},{12,14},{14,12},{1,3},{3,1},... | collective-permute-start | bytes 983048 | tf_op jit(solution)/shard_map/ppermute | solution.py:471
  32.6 0.7 %advantages.1 = (f32[1,128]{1,0:T(1,128)}, f32[2,128,128]{2,1,0:T(8,128)S(1)}) custom-call(f32[2,3,128,128]{3,2,1,0:T(8,128)S(1)} %get-tuple-element.40.columns_ref, f32[2,2,8,128]{3,2,1,0:T(8,128)S(1)} %get-tuple-element.41.weights_ref, bf16[528,128]{1,0:T(8,128)(2,1)S(1)} %copy-done.2, bf16[528,128]{1,0:T(8,128)(2,1)S(1)} %collective-permute-done.refs_1_.refs_6_, ...), custom_call_target="tpu_custom_call" | custom-call | flops 327680 | bytes 524288 | tf_op jit(solution)/shard_map/advantages/pallas_call | solution.py:282
  33.3 4.4 %tree_attention_backward.2 = (bf16[128,640]{1,0:T(8,128)(2,1)S(1)}, bf16[128,640]{1,0:T(8,128)(2,1)S(1)}, bf16[2,2,128,128]{3,2,1,0:T(8,128)(2,1)S(1)}, bf16[2,2...) custom-call(s32[8]{0:T(128)S(1)} %copy-done.4, ...), custom_call_target="tpu_custom_call" | custom-call | flops 1048576000 | bytes 8388608 | tf_op jit(solution)/shard_map/tree_attention_backward/pallas_call | solution.py:385
  37.8 3.5 %collective-permute-start.11 = (bf16[2,2,128,128]{3,2,1,0:T(8,128)(2,1)S(1)}, bf16[2,2,128,128]{3,2,1,0:T(8,128)(2,1)S(1)}, u32[]{:S(2)}, u32[]{:S(2)}) collective-permute-start(bf16[2,2,128,128]{3,2,1,0:T(8,128)(2,1)S(1)} %get-tuple-element.61), channel_id=1, source_target_pairs={{0,12},{2,14},{4,8},{6,10},{8,4},{10,6},{12,0},{14,2},{1,13},{3,15... | collective-permute-start | bytes 393224 | tf_op jit(solution)/shard_map/ppermute | solution.py:471
  41.2 0.0 collective-permute-start.12
  41.2 1.0 %collective-permute-start.13 = (bf16[2,2,128,128]{3,2,1,0:T(8,128)(2,1)S(1)}, bf16[2,2,128,128]{3,2,1,0:T(8,128)(2,1)S(1)}, u32[]{:S(2)}, u32[]{:S(2)}) collective-permute-start(bf16[2,2,128,128]{3,2,1,0:T(8,128)(2,1)S(1)} %get-tuple-element.63), channel_id=1, source_target_pairs={{0,4},{2,6},{4,0},{6,2},{8,12},{10,14},{12,8},{14,10},{1,5},{3,7},... | collective-permute-start | bytes 393224 | tf_op jit(solution)/shard_map/ppermute | solution.py:471
  42.2 0.0 collective-permute-done.8.refs_4_
  42.2 4.4 %tree_attention_backward.3 = (bf16[128,640]{1,0:T(8,128)(2,1)S(1)}, bf16[128,640]{1,0:T(8,128)(2,1)S(1)}, bf16[2,2,128,128]{3,2,1,0:T(8,128)(2,1)S(1)}, bf16[2,2...) custom-call(s32[8]{0:T(128)S(1)} %copy-done.4, ...), custom_call_target="tpu_custom_call" | custom-call | flops 1048576000 | bytes 8388608 | tf_op jit(solution)/shard_map/tree_attention_backward/pallas_call | solution.py:385
  46.6 3.5 %collective-permute-start.15 = (bf16[2,2,128,128]{3,2,1,0:T(8,128)(2,1)S(1)}, bf16[2,2,128,128]{3,2,1,0:T(8,128)(2,1)S(1)}, u32[]{:S(2)}, u32[]{:S(2)}) collective-permute-start(bf16[2,2,128,128]{3,2,1,0:T(8,128)(2,1)S(1)} %get-tuple-element.66), channel_id=1, source_target_pairs={{0,12},{2,14},{4,8},{6,10},{8,4},{10,6},{12,0},{14,2},{1,13},{3,15... | collective-permute-start | bytes 393224 | tf_op jit(solution)/shard_map/ppermute | solution.py:471
  50.1 0.0 collective-permute-start.16
  50.1 0.0 collective-permute-done.11.refs_3_
  50.1 1.0 %collective-permute-start.17 = (bf16[2,2,128,128]{3,2,1,0:T(8,128)(2,1)S(1)}, bf16[2,2,128,128]{3,2,1,0:T(8,128)(2,1)S(1)}, u32[]{:S(2)}, u32[]{:S(2)}) collective-permute-start(bf16[2,2,128,128]{3,2,1,0:T(8,128)(2,1)S(1)} %get-tuple-element.68), channel_id=1, source_target_pairs={{0,4},{2,6},{4,0},{6,2},{8,12},{10,14},{12,8},{14,10},{1,5},{3,7},... | collective-permute-start | bytes 393224 | tf_op jit(solution)/shard_map/ppermute | solution.py:471
  51.1 6.0 %collective-permute-done.12.refs_4_ = bf16[2,2,128,128]{3,2,1,0:T(8,128)(2,1)S(1)} collective-permute-done((bf16[2,2,128,128]{3,2,1,0:T(8,128)(2,1)S(1)}, bf16[2,2,128,128]{3,2,1,0:T(8,128)(2,1)S(1)}, u32[]{:S(2)}, u32[]{:S(2)}) %collective-permute-start.12) | collective-permute-done | bytes 131104 | tf_op jit(solution)/shard_map/ppermute | solution.py:471
  57.1 0.0 collective-permute-done.13.refs_5_
  57.2 0.6 collective-permute-start.14
  57.8 1.5 %collective-permute-start.9 = (bf16[128,640]{1,0:T(8,128)(2,1)S(1)}, bf16[128,640]{1,0:T(8,128)(2,1)S(1)}, u32[]{:S(2)}, u32[]{:S(2)}) collective-permute-start(bf16[128,640]{1,0:T(8,128)(2,1)S(1)} %get-tuple-element.56), channel_id=1, source_target_pairs={{0,2},{2,0},{4,6},{6,4},{8,10},{10,8},{12,14},{14,12},{1,3},{3,1},... | collective-permute-start | bytes 491528 | tf_op jit(solution)/shard_map/ppermute | solution.py:471
  59.3 0.0 collective-permute-done.15.refs_7_
  59.3 0.5 collective-permute-start.10
  59.8 1.6 %collective-permute-done.16.refs_8_ = bf16[2,2,128,128]{3,2,1,0:T(8,128)(2,1)S(1)} collective-permute-done((bf16[2,2,128,128]{3,2,1,0:T(8,128)(2,1)S(1)}, bf16[2,2,128,128]{3,2,1,0:T(8,128)(2,1)S(1)}, u32[]{:S(2)}, u32[]{:S(2)}) %collective-permute-start.16) | collective-permute-done | bytes 131104 | tf_op jit(solution)/shard_map/ppermute | solution.py:471
  61.4 0.0 collective-permute-done.17.refs_9_
  61.4 0.6 collective-permute-start.18
  62.0 1.5 %collective-permute-done.9.refs_2_ = bf16[128,640]{1,0:T(8,128)(2,1)S(1)} collective-permute-done((bf16[128,640]{1,0:T(8,128)(2,1)S(1)}, bf16[128,640]{1,0:T(8,128)(2,1)S(1)}, u32[]{:S(2)}, u32[]{:S(2)}) %collective-permute-start.9) | collective-permute-done | bytes 163872 | tf_op jit(solution)/shard_map/ppermute | solution.py:471
  63.5 2.2 %collective-permute-done.10.refs_3_ = bf16[128,640]{1,0:T(8,128)(2,1)S(1)} collective-permute-done((bf16[128,640]{1,0:T(8,128)(2,1)S(1)}, bf16[128,640]{1,0:T(8,128)(2,1)S(1)}, u32[]{:S(2)}, u32[]{:S(2)}) %collective-permute-start.10) | collective-permute-done | bytes 163872 | tf_op jit(solution)/shard_map/ppermute | solution.py:471
  65.7 0.9 %join_queries.1 = bf16[128,2560]{1,0:T(8,128)(2,1)} custom-call(bf16[128,640]{1,0:T(8,128)(2,1)S(1)} %get-tuple-element.50.refs_0_, bf16[128,640]{1,0:T(8,128)(2,1)S(1)} %get-tuple-element.54.refs_1_, bf16[128,640]{1,0:T(8,128)(2,1)S(1)} %collective-permute-done.9.refs_2_, bf16[128,640]{1,0:T(8,128)(2,1)S(1)} %collective-permute-done.10.refs_3_), custom_call_target="tpu_custom_call" | custom-call | bytes 1310720 | tf_op jit(solution)/shard_map/join_queries/pallas_call | solution.py:423
  66.6 0.0 collective-permute-done.14.refs_0_
  66.6 0.0 collective-permute-done.18.refs_1_
  66.6 0.8 %join_keys.1 = (bf16[128,512]{1,0:T(8,128)(2,1)}, bf16[128,512]{1,0:T(8,128)(2,1)}) custom-call(bf16[2,128,128]{2,1,0:T(8,128)(2,1)S(1)} %collective-permute-done.14.refs_0_, bf16[2,128,128]{2,1,0:T(8,128)(2,1)S(1)} %collective-permute-done.18.refs_1_, bf16[2,2,128,128]{3,2,1,0:T(8,128)(2,1)S(1)} %get-tuple-element.60.refs_2_, ...), custom_call_target="tpu_custom_call" | custom-call | bytes 524288 | tf_op jit(solution)/shard_map/join_keys/pallas_call | solution.py:457
  (2 shorter events, 0.1 us)
Async XLA Ops:
  2.5 9.6 %collective-permute-start = (bf16[528,128]{1,0:T(8,128)(2,1)}, bf16[528,128]{1,0:T(8,128)(2,1)S(1)}, u32[]{:S(2)}, u32[]{:S(2)}) collective-permute-start(bf16[528,128]{1,0:T(8,128)(2,1)} %get-tuple-element.39), channel_id=1, source_target_pairs={{0,2},{2,0},{4,6},{6,4},{8,10},{10,8},{12,14},{14,12},{1,3},{3,1},... | collective-permute-start | bytes 405512 | tf_op jit(solution)/shard_map/ppermute | solution.py:471
  5.4 9.2 %collective-permute-start.2 = (bf16[528,128]{1,0:T(8,128)(2,1)}, bf16[528,128]{1,0:T(8,128)(2,1)S(1)}, u32[]{:S(2)}, u32[]{:S(2)}) collective-permute-start(bf16[528,128]{1,0:T(8,128)(2,1)} %get-tuple-element.38.refs_0_.refs_5_), channel_id=1, source_target_pairs={{0,8},{2,10},{4,12},{6,14},{8,0},{10,2},{12,4},{14,6},{1,9},{3,11}... | collective-permute-start | bytes 405512 | tf_op jit(solution)/shard_map/ppermute | solution.py:471
  8.0 6.8 %collective-permute-start.1 = (bf16[528,128]{1,0:T(8,128)(2,1)}, bf16[528,128]{1,0:T(8,128)(2,1)S(1)}, u32[]{:S(2)}, u32[]{:S(2)}) collective-permute-start(bf16[528,128]{1,0:T(8,128)(2,1)} %get-tuple-element.38.refs_0_.refs_5_), channel_id=1, source_target_pairs={{0,4},{2,6},{4,0},{6,2},{8,12},{10,14},{12,8},{14,10},{1,5},{3,7},... | collective-permute-start | bytes 405512 | tf_op jit(solution)/shard_map/ppermute | solution.py:471
  9.6 1.1 %copy-start = (bf16[128,2560]{1,0:T(8,128)(2,1)S(1)}, bf16[128,2560]{1,0:T(8,128)(2,1)}, u32[]{:S(2)}) copy-start(bf16[128,2560]{1,0:T(8,128)(2,1)} %q_ref) | copy-start | bytes 1966084
  10.7 1.1 %copy-start.1 = (bf16[128,2560]{1,0:T(8,128)(2,1)S(1)}, bf16[128,2560]{1,0:T(8,128)(2,1)}, u32[]{:S(2)}) copy-start(bf16[128,2560]{1,0:T(8,128)(2,1)} %dir_ref.1) | copy-start | bytes 1966084
  11.8 7.3 %copy-start.2 = (bf16[528,128]{1,0:T(8,128)(2,1)S(1)}, bf16[528,128]{1,0:T(8,128)(2,1)}, u32[]{:S(2)}) copy-start(bf16[528,128]{1,0:T(8,128)(2,1)} %get-tuple-element.38.refs_0_.refs_5_) | copy-start | bytes 405508
  12.0 7.1 %copy-start.3 = (s32[8]{0:T(128)S(1)}, s32[8]{0:T(128)}, u32[]{:S(2)}) copy-start(s32[8]{0:T(128)} %lengths_s.1) | copy-start | bytes 100
  12.0 7.1 %copy-start.4 = (s32[8]{0:T(128)S(1)}, s32[8]{0:T(128)}, u32[]{:S(2)}) copy-start(s32[8]{0:T(128)} %refs_0_.3) | copy-start | bytes 100
  14.8 11.3 %collective-permute-start.6 = (bf16[2,5,128,128]{3,2,1,0:T(8,128)(2,1)S(1)}, bf16[2,5,128,128]{3,2,1,0:T(8,128)(2,1)S(1)}, u32[]{:S(2)}, u32[]{:S(2)}) collective-permute-start(bf16[2,5,128,128]{3,2,1,0:T(8,128)(2,1)S(1)} %get-tuple-element.46), channel_id=1, source_target_pairs={{0,2},{2,0},{4,6},{6,4},{8,10},{10,8},{12,14},{14,12},{1,3},{3,1},... | collective-permute-start | bytes 983048 | tf_op jit(solution)/shard_map/ppermute | solution.py:471
  15.3 8.2 %collective-permute-start.5 = (bf16[528,128]{1,0:T(8,128)(2,1)S(1)}, bf16[528,128]{1,0:T(8,128)(2,1)S(1)}, u32[]{:S(2)}, u32[]{:S(2)}) collective-permute-start(bf16[528,128]{1,0:T(8,128)(2,1)S(1)} %collective-permute-done.2.refs_4_.refs_9_), channel_id=1, source_target_pairs={{0,4},{2,6},{4,0},{6,2},{8,12},{10,14},{12,8},{14,10},{1,5},{3,7},... | collective-permute-start | bytes 405512 | tf_op jit(solution)/shard_map/ppermute | solution.py:471
  16.7 8.3 %collective-permute-start.4 = (bf16[528,128]{1,0:T(8,128)(2,1)S(1)}, bf16[528,128]{1,0:T(8,128)(2,1)S(1)}, u32[]{:S(2)}, u32[]{:S(2)}) collective-permute-start(bf16[528,128]{1,0:T(8,128)(2,1)S(1)} %collective-permute-done.refs_1_.refs_6_), channel_id=1, source_target_pairs={{0,8},{2,10},{4,12},{6,14},{8,0},{10,2},{12,4},{14,6},{1,9},{3,11}... | collective-permute-start | bytes 405512 | tf_op jit(solution)/shard_map/ppermute | solution.py:471
  19.1 7.0 %collective-permute-start.3 = (bf16[528,128]{1,0:T(8,128)(2,1)S(1)}, bf16[528,128]{1,0:T(8,128)(2,1)S(1)}, u32[]{:S(2)}, u32[]{:S(2)}) collective-permute-start(bf16[528,128]{1,0:T(8,128)(2,1)S(1)} %collective-permute-done.refs_1_.refs_6_), channel_id=1, source_target_pairs={{0,4},{2,6},{4,0},{6,2},{8,12},{10,14},{12,8},{14,10},{1,5},{3,7},... | collective-permute-start | bytes 405512 | tf_op jit(solution)/shard_map/ppermute | solution.py:471
  26.1 5.0 %collective-permute-start.7 = (bf16[528,128]{1,0:T(8,128)(2,1)S(1)}, bf16[528,128]{1,0:T(8,128)(2,1)S(1)}, u32[]{:S(2)}, u32[]{:S(2)}) collective-permute-start(bf16[528,128]{1,0:T(8,128)(2,1)S(1)} %collective-permute-done.4.refs_5_.refs_10_), channel_id=1, source_target_pairs={{0,4},{2,6},{4,0},{6,2},{8,12},{10,14},{12,8},{14,10},{1,5},{3,7},... | collective-permute-start | bytes 405512 | tf_op jit(solution)/shard_map/ppermute | solution.py:471
  31.1 11.1 %collective-permute-start.8 = (bf16[2,5,128,128]{3,2,1,0:T(8,128)(2,1)S(1)}, bf16[2,5,128,128]{3,2,1,0:T(8,128)(2,1)S(1)}, u32[]{:S(2)}, u32[]{:S(2)}) collective-permute-start(bf16[2,5,128,128]{3,2,1,0:T(8,128)(2,1)S(1)} %get-tuple-element.53), channel_id=1, source_target_pairs={{0,2},{2,0},{4,6},{6,4},{8,10},{10,8},{12,14},{14,12},{1,3},{3,1},... | collective-permute-start | bytes 983048 | tf_op jit(solution)/shard_map/ppermute | solution.py:471
  37.8 12.3 %collective-permute-start.11 = (bf16[2,2,128,128]{3,2,1,0:T(8,128)(2,1)S(1)}, bf16[2,2,128,128]{3,2,1,0:T(8,128)(2,1)S(1)}, u32[]{:S(2)}, u32[]{:S(2)}) collective-permute-start(bf16[2,2,128,128]{3,2,1,0:T(8,128)(2,1)S(1)} %get-tuple-element.61), channel_id=1, source_target_pairs={{0,12},{2,14},{4,8},{6,10},{8,4},{10,6},{12,0},{14,2},{1,13},{3,15... | collective-permute-start | bytes 393224 | tf_op jit(solution)/shard_map/ppermute | solution.py:471
  41.2 15.9 %collective-permute-start.12 = (bf16[2,2,128,128]{3,2,1,0:T(8,128)(2,1)S(1)}, bf16[2,2,128,128]{3,2,1,0:T(8,128)(2,1)S(1)}, u32[]{:S(2)}, u32[]{:S(2)}) collective-permute-start(bf16[2,2,128,128]{3,2,1,0:T(8,128)(2,1)S(1)} %get-tuple-element.62), channel_id=1, source_target_pairs={{0,8},{2,10},{4,12},{6,14},{8,0},{10,2},{12,4},{14,6},{1,9},{3,11}... | collective-permute-start | bytes 393224 | tf_op jit(solution)/shard_map/ppermute | solution.py:471
  41.2 15.9 %collective-permute-start.13 = (bf16[2,2,128,128]{3,2,1,0:T(8,128)(2,1)S(1)}, bf16[2,2,128,128]{3,2,1,0:T(8,128)(2,1)S(1)}, u32[]{:S(2)}, u32[]{:S(2)}) collective-permute-start(bf16[2,2,128,128]{3,2,1,0:T(8,128)(2,1)S(1)} %get-tuple-element.63), channel_id=1, source_target_pairs={{0,4},{2,6},{4,0},{6,2},{8,12},{10,14},{12,8},{14,10},{1,5},{3,7},... | collective-permute-start | bytes 393224 | tf_op jit(solution)/shard_map/ppermute | solution.py:471
  46.6 12.6 %collective-permute-start.15 = (bf16[2,2,128,128]{3,2,1,0:T(8,128)(2,1)S(1)}, bf16[2,2,128,128]{3,2,1,0:T(8,128)(2,1)S(1)}, u32[]{:S(2)}, u32[]{:S(2)}) collective-permute-start(bf16[2,2,128,128]{3,2,1,0:T(8,128)(2,1)S(1)} %get-tuple-element.66), channel_id=1, source_target_pairs={{0,12},{2,14},{4,8},{6,10},{8,4},{10,6},{12,0},{14,2},{1,13},{3,15... | collective-permute-start | bytes 393224 | tf_op jit(solution)/shard_map/ppermute | solution.py:471
  50.1 11.3 %collective-permute-start.16 = (bf16[2,2,128,128]{3,2,1,0:T(8,128)(2,1)S(1)}, bf16[2,2,128,128]{3,2,1,0:T(8,128)(2,1)S(1)}, u32[]{:S(2)}, u32[]{:S(2)}) collective-permute-start(bf16[2,2,128,128]{3,2,1,0:T(8,128)(2,1)S(1)} %get-tuple-element.67), channel_id=1, source_target_pairs={{0,8},{2,10},{4,12},{6,14},{8,0},{10,2},{12,4},{14,6},{1,9},{3,11}... | collective-permute-start | bytes 393224 | tf_op jit(solution)/shard_map/ppermute | solution.py:471
  50.1 11.3 %collective-permute-start.17 = (bf16[2,2,128,128]{3,2,1,0:T(8,128)(2,1)S(1)}, bf16[2,2,128,128]{3,2,1,0:T(8,128)(2,1)S(1)}, u32[]{:S(2)}, u32[]{:S(2)}) collective-permute-start(bf16[2,2,128,128]{3,2,1,0:T(8,128)(2,1)S(1)} %get-tuple-element.68), channel_id=1, source_target_pairs={{0,4},{2,6},{4,0},{6,2},{8,12},{10,14},{12,8},{14,10},{1,5},{3,7},... | collective-permute-start | bytes 393224 | tf_op jit(solution)/shard_map/ppermute | solution.py:471
  57.2 9.5 %collective-permute-start.14 = (bf16[2,128,128]{2,1,0:T(8,128)(2,1)S(1)}, bf16[2,128,128]{2,1,0:T(8,128)(2,1)S(1)}, u32[]{:S(2)}, u32[]{:S(2)}) collective-permute-start(bf16[2,128,128]{2,1,0:T(8,128)(2,1)S(1)} %fusion), channel_id=1, source_target_pairs={{0,2},{2,0},{4,6},{6,4},{8,10},{10,8},{12,14},{14,12},{1,3},{3,1},... | collective-permute-start | bytes 196616 | tf_op jit(solution)/shard_map/ppermute | solution.py:471
  57.8 5.8 %collective-permute-start.9 = (bf16[128,640]{1,0:T(8,128)(2,1)S(1)}, bf16[128,640]{1,0:T(8,128)(2,1)S(1)}, u32[]{:S(2)}, u32[]{:S(2)}) collective-permute-start(bf16[128,640]{1,0:T(8,128)(2,1)S(1)} %get-tuple-element.56), channel_id=1, source_target_pairs={{0,2},{2,0},{4,6},{6,4},{8,10},{10,8},{12,14},{14,12},{1,3},{3,1},... | collective-permute-start | bytes 491528 | tf_op jit(solution)/shard_map/ppermute | solution.py:471
  59.3 6.4 %collective-permute-start.10 = (bf16[128,640]{1,0:T(8,128)(2,1)S(1)}, bf16[128,640]{1,0:T(8,128)(2,1)S(1)}, u32[]{:S(2)}, u32[]{:S(2)}) collective-permute-start(bf16[128,640]{1,0:T(8,128)(2,1)S(1)} %get-tuple-element.58), channel_id=1, source_target_pairs={{0,2},{2,0},{4,6},{6,4},{8,10},{10,8},{12,14},{14,12},{1,3},{3,1},... | collective-permute-start | bytes 491528 | tf_op jit(solution)/shard_map/ppermute | solution.py:471
  61.4 5.2 %collective-permute-start.18 = (bf16[2,128,128]{2,1,0:T(8,128)(2,1)S(1)}, bf16[2,128,128]{2,1,0:T(8,128)(2,1)S(1)}, u32[]{:S(2)}, u32[]{:S(2)}) collective-permute-start(bf16[2,128,128]{2,1,0:T(8,128)(2,1)S(1)} %fusion.1), channel_id=1, source_target_pairs={{0,2},{2,0},{4,6},{6,4},{8,10},{10,8},{12,14},{14,12},{1,3},{3,1},... | collective-permute-start | bytes 196616 | tf_op jit(solution)/shard_map/ppermute | solution.py:471

commit v13 on v10

--- a/solution.py
+++ b/solution.py
@@ -168,10 +168,6 @@
     return jnp.where(segment >= 0, known, -1).astype(jnp.int32)
 
 
-def ring_place(pair):
-    return jnp.where(pair >= 2, 5 - pair, pair)
-
-
 def segment_of(own, segs, i):
     part = lax.rem(own, segs)
     return own - part + lax.rem(part + i, segs)
@@ -281,13 +277,12 @@
         firsts = read_terms(term_refs[0])[1]
     else:
         own = lax.axis_index("seg")
-        part, pair, pairs = lax.rem(own, segs), own // segs, count // segs
+        part, pair = lax.rem(own, segs), own // segs
         seg_id = lax.broadcasted_iota(jnp.int32, (count, length), 0)
         firsts = jnp.zeros((count, length), jnp.float32)
         for step, ref in enumerate(term_refs):
-            place = lax.rem(ring_place(pair) - step + pairs, pairs)
             for side in range(segs):
-                seg = ring_place(place) * segs + lax.rem(part + side, segs)
+                seg = (pair ^ step) * segs + lax.rem(part + side, segs)
                 end = (side + 1) * (ref.shape[0] // segs)
                 firsts = jnp.where(seg_id == seg, read_terms(ref, end)[1], firsts)
     for i in range(segs):
@@ -354,8 +349,7 @@
                 chosen.append(slot)
             else:
                 known = jnp.maximum(ancestor, 0)
-                step = ring_place((own - part) // segs) - ring_place(known // segs)
-                step = lax.rem(step + steps, steps)
+                step = (own // segs) ^ (known // segs)
                 turn = lax.rem(lax.rem(known, segs) - part + segs, segs)
                 chosen.append(jnp.where(ancestor >= 0, step * segs + turn, 0))
         q_list = [query_refs[i][0, j] for j in range(group_size)]
@@ -511,50 +505,38 @@
     chunks = key_vectors.shape[1] // HD // 2
     swap = [(i, i ^ 1) for i in range(groups)]
     steps = range(1, groups // 2)
-    ring = [0, 1, 3, 2]
-
-    def turn(distance):
-        pairs = []
-        for place, pair in enumerate(ring):
-            target = ring[(place + distance) % len(ring)]
-            pairs += [(2 * pair + x, 2 * target + x) for x in range(2)]
-        return pairs
-
-    climb = turn(1)
-    down = {d: turn(-d) for d in steps}
+    meet = {bits: [(i, i ^ (2 * bits)) for i in range(groups)] for bits in steps}
 
     kept, given = pack(lengths, key_vectors, value_vectors, token_rows, 2, log_rate)
     taken = [permute(block, swap) for block in given]
     kept_q, given_q = pack_queries(after(queries, kept[0]), direction, 2, chunks)
     bias, columns, weights = prepare(parents, lengths, [kept[0], taken[0]], length, log_rate)
-    near = [
-        join_blocks(mine, after(other, *kept_q) if chunk == 0 else other)
-        for chunk, (mine, other) in enumerate(zip(kept, taken))
-    ]
-    chain = [near[0]]
-    for gate in ([], near[1:], [bias]):
-        chain.append(permute(after(chain[-1], *gate), climb))
-    chains = [chain]
-    taken_q = [permute(after(given_q[0], chain[1]), swap)]
-    for chunk in range(1, chunks):
-        block, query_block = lax.optimization_barrier((near[chunk], given_q[chunk], bias, chain[-1]))[:2]
-        chains.append([block] + [permute(block, turn(d)) for d in steps])
-        taken_q.append(permute(query_block, swap))
+    near = [join_blocks(kept[0], after(taken[0], *kept_q)), join_blocks(kept[1], taken[1])]
+    two, one = permute(near[0], meet[2]), permute(near[0], meet[1])
+    three = permute(after(two, one, near[1], bias), meet[1])
+    chains = [[near[0], one, two, three]]
+    taken_q = [permute(after(given_q[0], near[0], near[1]), swap)]
+    block = after(near[1], two, one, taken_q[0])
+    two, one = permute(block, meet[2]), permute(block, meet[1])
+    taken_q.append(permute(after(given_q[1], three), swap))
     row, advantages = advantages_of(columns, weights, chains[0])
 
     dq_own, dq_back, dkv_list = [], [], []
     for chunk in range(chunks):
         query_list = [kept_q[chunk], taken_q[chunk]]
         dq, dkv = attend(parents, advantages, bias, query_list, chains[chunk])
+        if chunk == 0:
+            three = permute(after(two, dq[0]), meet[1])
+            chains.append([block, one, two, three])
         dq_own.append(dq[0])
         dq_back.append(dq[1])
         dkv_list.append(dkv)
 
     summands = []
     for dkv in dkv_list:
-        arrived = [permute(dkv[d], down[d]) for d in steps[::-1]]
+        arrived = [permute(dkv[bits], meet[bits]) for bits in steps[::-1]]
         summands.append([after(dkv[0], dq_own[-1])] + arrived)
-    dq_back = [permute(block, swap) for block in dq_back]
+    dq_back = [permute(after(block, dq_own[-1]), swap) for block in dq_back]
     others = []
     for blocks in summands:
         total = sum(block[1].astype(jnp.float32) for block in blocks)

time: 67.6 us -> 62.1 us (0.919)
  starting transfers between devices: 35.2 us -> 28.5 us
  waiting for transfers between devices: 14.1 us -> 15.4 us
    ppermute x20, starting transfers between devices: 35.2 us -> 28.5 us  [permute(): return lax.ppermute(array, 'seg', pairs)]
    ppermute x20, waiting for transfers between devices: 14.1 us -> 15.4 us  [permute(): return lax.ppermute(array, 'seg', pairs)]
    unnamed x14 -> x12, local copies, waits for them, and re-layouts: 2.75 us -> 2.62 us
  transfers between devices with their start and end apart: 20 -> 20, of which waited for: 10 -> 7; matrix products, arithmetic and copies ran while one was open for 0% -> 0% of each run, Pallas kernels for 18% -> 19%
where the time goes in v13:
time: 62.1 us; the launch traced here: 61.8 us
  starting transfers between devices  28.5 us (46%)
  waiting for transfers between devices  15.4 us (25%)
  Pallas kernels  14.5 us (23%)
  local copies, waits for them, and re-layouts  2.62 us (4%)
  between operations  0.72 us (1%)
    ppermute x20, starting transfers between devices, permute(): return lax.ppermute(array, 'seg', pairs)  28.5 us
    ppermute x20, waiting for transfers between devices, permute(): return lax.ppermute(array, 'seg', pairs)  15.4 us
    pallas_call x2, Pallas kernels, attend(): pl.pallas_call(functools.partial(attend_kernel, DEPTH, segs, steps, group...  8.85 us
    unnamed x12, local copies, waits for them, and re-layouts  2.62 us
    pallas_call x1, Pallas kernels, pack(): pl.pallas_call(functools.partial(pack_kernel, log_rate, parts), out_shape...  1.81 us
  transfers between devices with their start and end apart: 20, of which 7 were waited for; matrix products, arithmetic and copies ran while one was open for 0% of the time, Pallas kernels for 19%

profile of v13, /device:TPU:0, one launch (start us, length us, event | category | flops | bytes accessed | tf_op | source)
XLA Modules:
  0.0 61.8 jit_solution(1370471009676554098)
XLA Ops:
  0.6 1.8 %pack_keys_values.1 = (bf16[272,128]{1,0:T(8,128)(2,1)}, bf16[256,128]{1,0:T(8,128)(2,1)}, bf16[272,128]{1,0:T(8,128)(2,1)}, bf16[256,128]{1,0:T(8,128)(2,1)}) custom-call(s32[8]{0:T(128)} %lengths_s.1, bf16[128,512]{1,0:T(8,128)(2,1)} %k_ref.1, bf16[128,512]{1,0:T(8,128)(2,1)} %v_ref.1, f32[1,128]{1,0:T(1,128)} %bitcast.9, f32[1,128]{1,0:T(1,128)} %bitcast.10, ...), custom_call_target="tpu_custom_call" | custom-call | flops 12800 | bytes 524288 | tf_op jit(solution)/shard_map/pack_keys_values/pallas_call | solution.py:104
  2.4 2.9 %collective-permute-start = (bf16[272,128]{1,0:T(8,128)(2,1)}, bf16[272,128]{1,0:T(8,128)(2,1)S(1)}, u32[]{:S(2)}, u32[]{:S(2)}) collective-permute-start(bf16[272,128]{1,0:T(8,128)(2,1)} %get-tuple-element.43), channel_id=1, source_target_pairs={{0,2},{2,0},{4,6},{6,4},{8,10},{10,8},{12,14},{14,12},{1,3},{3,1},... | collective-permute-start | bytes 208904 | tf_op jit(solution)/shard_map/ppermute | solution.py:495
  5.4 0.1 collective-permute-start.3
  5.5 0.0 copy-start
  5.5 1.1 %copy-done = bf16[128,2560]{1,0:T(8,128)(2,1)S(1)} copy-done((bf16[128,2560]{1,0:T(8,128)(2,1)S(1)}, bf16[128,2560]{1,0:T(8,128)(2,1)}, u32[]{:S(2)}) %copy-start) | copy-done | bytes 655384
  6.5 0.0 copy-start.1
  6.5 1.1 %copy-done.1 = bf16[128,2560]{1,0:T(8,128)(2,1)S(1)} copy-done((bf16[128,2560]{1,0:T(8,128)(2,1)S(1)}, bf16[128,2560]{1,0:T(8,128)(2,1)}, u32[]{:S(2)}) %copy-start.1) | copy-done | bytes 655384
  7.6 0.0 copy-start.2
  7.6 0.2 pack_queries.1
  7.9 0.2 collective-permute-done.refs_1_.other_ref
  8.1 0.4 copy-done.2
  8.5 0.0 copy-start.3
  8.5 2.2 %collective-permute-start.1 = (bf16[544,128]{1,0:T(8,128)(2,1)S(1)}, bf16[544,128]{1,0:T(8,128)(2,1)S(1)}, u32[]{:S(2)}, u32[]{:S(2)}) collective-permute-start(bf16[544,128]{1,0:T(8,128)(2,1)S(1)} %join_blocks.2.refs_0_.refs_5_), channel_id=1, source_target_pairs={{0,4},{2,6},{4,0},{6,2},{8,12},{10,14},{12,8},{14,10},{1,5},{3,7},... | collective-permute-start | bytes 417800 | tf_op jit(solution)/shard_map/ppermute | solution.py:495
  10.7 2.6 %collective-permute-start.2 = (bf16[544,128]{1,0:T(8,128)(2,1)S(1)}, bf16[544,128]{1,0:T(8,128)(2,1)S(1)}, u32[]{:S(2)}, u32[]{:S(2)}) collective-permute-start(bf16[544,128]{1,0:T(8,128)(2,1)S(1)} %join_blocks.2.refs_0_.refs_5_), channel_id=1, source_target_pairs={{0,8},{2,10},{4,12},{6,14},{8,0},{10,2},{12,4},{14,6},{1,9},{3,11}... | collective-permute-start | bytes 417800 | tf_op jit(solution)/shard_map/ppermute | solution.py:495
  13.3 0.0 collective-permute-done.3.other_ref
  13.3 0.0 copy-done.3
  13.4 0.0 copy-start.4
  13.4 0.0 copy-start.5
  13.4 1.4 %collective-permute-start.5 = (bf16[2,5,128,128]{3,2,1,0:T(8,128)(2,1)S(1)}, bf16[2,5,128,128]{3,2,1,0:T(8,128)(2,1)S(1)}, u32[]{:S(2)}, u32[]{:S(2)}) collective-permute-start(bf16[2,5,128,128]{3,2,1,0:T(8,128)(2,1)S(1)} %get-tuple-element.56), channel_id=1, source_target_pairs={{0,2},{2,0},{4,6},{6,4},{8,10},{10,8},{12,14},{14,12},{1,3},{3,1},... | collective-permute-start | bytes 983048 | tf_op jit(solution)/shard_map/ppermute | solution.py:495
  14.8 0.0 copy-done.4
  14.8 0.0 copy-done.5
  14.8 1.2 %prepare.1 = (f32[2,640,128]{2,1,0:T(8,128)S(1)}, f32[2,3,128,128]{3,2,1,0:T(8,128)S(1)}, f32[2,2,8,128]{3,2,1,0:T(8,128)S(1)}) custom-call(s32[8]{0:T(128)S(1)} %copy-done.5, s32[8]{0:T(128)S(1)} %copy-done.4, bf16[272,128]{1,0:T(8,128)(2,1)S(1)} %copy-done.2, bf16[272,128]{1,0:T(8,128)(2,1)S(1)} %collective-permute-done.refs_1_.other_ref), custom_call_target="tpu_custom_call" | custom-call | flops 3276800 | bytes 655360 | tf_op jit(solution)/shard_map/prepare/pallas_call | solution.py:253
  16.1 0.0 collective-permute-done.1.refs_1_.refs_6_
  16.1 3.2 %collective-permute-done.2.refs_2_.refs_7_ = bf16[544,128]{1,0:T(8,128)(2,1)S(1)} collective-permute-done((bf16[544,128]{1,0:T(8,128)(2,1)S(1)}, bf16[544,128]{1,0:T(8,128)(2,1)S(1)}, u32[]{:S(2)}, u32[]{:S(2)}) %collective-permute-start.2) | collective-permute-done | bytes 139296 | tf_op jit(solution)/shard_map/ppermute | solution.py:495
  19.2 0.2 collective-permute-start.4
  19.5 4.8 %collective-permute-done.4.refs_3_.refs_8_ = bf16[544,128]{1,0:T(8,128)(2,1)S(1)} collective-permute-done((bf16[544,128]{1,0:T(8,128)(2,1)S(1)}, bf16[544,128]{1,0:T(8,128)(2,1)S(1)}, u32[]{:S(2)}, u32[]{:S(2)}) %collective-permute-start.4) | collective-permute-done | bytes 139296 | tf_op jit(solution)/shard_map/ppermute | solution.py:495
  24.3 2.6 %collective-permute-start.6 = (bf16[2,5,128,128]{3,2,1,0:T(8,128)(2,1)S(1)}, bf16[2,5,128,128]{3,2,1,0:T(8,128)(2,1)S(1)}, u32[]{:S(2)}, u32[]{:S(2)}) collective-permute-start(bf16[2,5,128,128]{3,2,1,0:T(8,128)(2,1)S(1)} %get-tuple-element.59), channel_id=1, source_target_pairs={{0,2},{2,0},{4,6},{6,4},{8,10},{10,8},{12,14},{14,12},{1,3},{3,1},... | collective-permute-start | bytes 983048 | tf_op jit(solution)/shard_map/ppermute | solution.py:495
  26.9 0.0 collective-permute-done.5.refs_4_
  26.9 0.0 collective-permute-start.8
  26.9 0.7 %advantages.1 = (f32[1,128]{1,0:T(1,128)}, f32[2,128,128]{2,1,0:T(8,128)S(1)}) custom-call(f32[2,3,128,128]{3,2,1,0:T(8,128)S(1)} %get-tuple-element.44.columns_ref, f32[2,2,8,128]{3,2,1,0:T(8,128)S(1)} %get-tuple-element.45.weights_ref, bf16[544,128]{1,0:T(8,128)(2,1)S(1)} %join_blocks.2.refs_0_.refs_5_, ...), custom_call_target="tpu_custom_call" | custom-call | flops 327680 | bytes 524288 | tf_op jit(solution)/shard_map/advantages/pallas_call | solution.py:306
  27.6 2.0 %collective-permute-start.7 = (bf16[512,128]{1,0:T(8,128)(2,1)S(1)}, bf16[512,128]{1,0:T(8,128)(2,1)S(1)}, u32[]{:S(2)}, u32[]{:S(2)}) collective-permute-start(bf16[512,128]{1,0:T(8,128)(2,1)S(1)} %join_blocks.3.refs_5_), channel_id=1, source_target_pairs={{0,4},{2,6},{4,0},{6,2},{8,12},{10,14},{12,8},{14,10},{1,5},{3,7},... | collective-permute-start | bytes 393224 | tf_op jit(solution)/shard_map/ppermute | solution.py:495
  29.5 4.4 %tree_attention_backward.2 = (bf16[128,640]{1,0:T(8,128)(2,1)S(1)}, bf16[128,640]{1,0:T(8,128)(2,1)S(1)}, bf16[2,2,128,128]{3,2,1,0:T(8,128)(2,1)S(1)}, bf16[2,2...) custom-call(s32[8]{0:T(128)S(1)} %copy-done.5, ...), custom_call_target="tpu_custom_call" | custom-call | flops 1048576000 | bytes 8388608 | tf_op jit(solution)/shard_map/tree_attention_backward/pallas_call | solution.py:409
  33.9 0.0 collective-permute-done.8.refs_7_
  33.9 0.1 collective-permute-start.9
  34.1 2.4 %collective-permute-start.12 = (bf16[2,2,128,128]{3,2,1,0:T(8,128)(2,1)S(1)}, bf16[2,2,128,128]{3,2,1,0:T(8,128)(2,1)S(1)}, u32[]{:S(2)}, u32[]{:S(2)}) collective-permute-start(bf16[2,2,128,128]{3,2,1,0:T(8,128)(2,1)S(1)} %get-tuple-element.69), channel_id=1, source_target_pairs={{0,12},{2,14},{4,8},{6,10},{8,4},{10,6},{12,0},{14,2},{1,13},{3,15... | collective-permute-start | bytes 393224 | tf_op jit(solution)/shard_map/ppermute | solution.py:495
  36.5 1.0 %collective-permute-start.13 = (bf16[2,2,128,128]{3,2,1,0:T(8,128)(2,1)S(1)}, bf16[2,2,128,128]{3,2,1,0:T(8,128)(2,1)S(1)}, u32[]{:S(2)}, u32[]{:S(2)}) collective-permute-start(bf16[2,2,128,128]{3,2,1,0:T(8,128)(2,1)S(1)} %get-tuple-element.70), channel_id=1, source_target_pairs={{0,8},{2,10},{4,12},{6,14},{8,0},{10,2},{12,4},{14,6},{1,9},{3,11}... | collective-permute-start | bytes 393224 | tf_op jit(solution)/shard_map/ppermute | solution.py:495
  37.5 0.0 collective-permute-done.7.refs_6_
  37.5 1.0 %collective-permute-start.14 = (bf16[2,2,128,128]{3,2,1,0:T(8,128)(2,1)S(1)}, bf16[2,2,128,128]{3,2,1,0:T(8,128)(2,1)S(1)}, u32[]{:S(2)}, u32[]{:S(2)}) collective-permute-start(bf16[2,2,128,128]{3,2,1,0:T(8,128)(2,1)S(1)} %get-tuple-element.71), channel_id=1, source_target_pairs={{0,4},{2,6},{4,0},{6,2},{8,12},{10,14},{12,8},{14,10},{1,5},{3,7},... | collective-permute-start | bytes 393224 | tf_op jit(solution)/shard_map/ppermute | solution.py:495
  38.5 2.5 %collective-permute-done.9.refs_8_ = bf16[512,128]{1,0:T(8,128)(2,1)S(1)} collective-permute-done((bf16[512,128]{1,0:T(8,128)(2,1)S(1)}, bf16[512,128]{1,0:T(8,128)(2,1)S(1)}, u32[]{:S(2)}, u32[]{:S(2)}) %collective-permute-start.9) | collective-permute-done | bytes 131104 | tf_op jit(solution)/shard_map/ppermute | solution.py:495
  41.0 0.0 collective-permute-done.6.refs_4_
  41.0 4.4 %tree_attention_backward.3 = (bf16[128,640]{1,0:T(8,128)(2,1)S(1)}, bf16[128,640]{1,0:T(8,128)(2,1)S(1)}, bf16[2,2,128,128]{3,2,1,0:T(8,128)(2,1)S(1)}, bf16[2,2...) custom-call(s32[8]{0:T(128)S(1)} %copy-done.5, ...), custom_call_target="tpu_custom_call" | custom-call | flops 1048576000 | bytes 8388608 | tf_op jit(solution)/shard_map/tree_attention_backward/pallas_call | solution.py:409
  45.5 2.4 %collective-permute-start.16 = (bf16[2,2,128,128]{3,2,1,0:T(8,128)(2,1)S(1)}, bf16[2,2,128,128]{3,2,1,0:T(8,128)(2,1)S(1)}, u32[]{:S(2)}, u32[]{:S(2)}) collective-permute-start(bf16[2,2,128,128]{3,2,1,0:T(8,128)(2,1)S(1)} %get-tuple-element.74), channel_id=1, source_target_pairs={{0,12},{2,14},{4,8},{6,10},{8,4},{10,6},{12,0},{14,2},{1,13},{3,15... | collective-permute-start | bytes 393224 | tf_op jit(solution)/shard_map/ppermute | solution.py:495
  47.9 0.0 collective-permute-start.17
  47.9 0.0 collective-permute-done.12.refs_3_
  47.9 2.0 %collective-permute-start.18 = (bf16[2,2,128,128]{3,2,1,0:T(8,128)(2,1)S(1)}, bf16[2,2,128,128]{3,2,1,0:T(8,128)(2,1)S(1)}, u32[]{:S(2)}, u32[]{:S(2)}) collective-permute-start(bf16[2,2,128,128]{3,2,1,0:T(8,128)(2,1)S(1)} %get-tuple-element.76), channel_id=1, source_target_pairs={{0,4},{2,6},{4,0},{6,2},{8,12},{10,14},{12,8},{14,10},{1,5},{3,7},... | collective-permute-start | bytes 393224 | tf_op jit(solution)/shard_map/ppermute | solution.py:495
  49.9 0.0 collective-permute-done.13.refs_4_
  49.9 0.0 collective-permute-done.14.refs_5_
  50.0 2.4 %collective-permute-start.15 = (bf16[2,128,128]{2,1,0:T(8,128)(2,1)S(1)}, bf16[2,128,128]{2,1,0:T(8,128)(2,1)S(1)}, u32[]{:S(2)}, u32[]{:S(2)}) collective-permute-start(bf16[2,128,128]{2,1,0:T(8,128)(2,1)S(1)} %fusion), channel_id=1, source_target_pairs={{0,2},{2,0},{4,6},{6,4},{8,10},{10,8},{12,14},{14,12},{1,3},{3,1},... | collective-permute-start | bytes 196616 | tf_op jit(solution)/shard_map/ppermute | solution.py:495
  52.4 0.1 collective-permute-start.11
  52.4 0.0 collective-permute-done.16.refs_7_
  52.5 2.3 %collective-permute-start.10 = (bf16[128,640]{1,0:T(8,128)(2,1)S(1)}, bf16[128,640]{1,0:T(8,128)(2,1)S(1)}, u32[]{:S(2)}, u32[]{:S(2)}) collective-permute-start(bf16[128,640]{1,0:T(8,128)(2,1)S(1)} %get-tuple-element.64), channel_id=1, source_target_pairs={{0,2},{2,0},{4,6},{6,4},{8,10},{10,8},{12,14},{14,12},{1,3},{3,1},... | collective-permute-start | bytes 491528 | tf_op jit(solution)/shard_map/ppermute | solution.py:495
  54.8 1.6 %collective-permute-done.17.refs_8_ = bf16[2,2,128,128]{3,2,1,0:T(8,128)(2,1)S(1)} collective-permute-done((bf16[2,2,128,128]{3,2,1,0:T(8,128)(2,1)S(1)}, bf16[2,2,128,128]{3,2,1,0:T(8,128)(2,1)S(1)}, u32[]{:S(2)}, u32[]{:S(2)}) %collective-permute-start.17) | collective-permute-done | bytes 131104 | tf_op jit(solution)/shard_map/ppermute | solution.py:495
  56.4 0.0 collective-permute-done.18.refs_9_
  56.4 0.7 %collective-permute-start.19 = (bf16[2,128,128]{2,1,0:T(8,128)(2,1)S(1)}, bf16[2,128,128]{2,1,0:T(8,128)(2,1)S(1)}, u32[]{:S(2)}, u32[]{:S(2)}) collective-permute-start(bf16[2,128,128]{2,1,0:T(8,128)(2,1)S(1)} %fusion.1), channel_id=1, source_target_pairs={{0,2},{2,0},{4,6},{6,4},{8,10},{10,8},{12,14},{14,12},{1,3},{3,1},... | collective-permute-start | bytes 196616 | tf_op jit(solution)/shard_map/ppermute | solution.py:495
  57.1 0.6 collective-permute-done.11.refs_3_
  57.7 2.5 %collective-permute-done.10.refs_2_ = bf16[128,640]{1,0:T(8,128)(2,1)S(1)} collective-permute-done((bf16[128,640]{1,0:T(8,128)(2,1)S(1)}, bf16[128,640]{1,0:T(8,128)(2,1)S(1)}, u32[]{:S(2)}, u32[]{:S(2)}) %collective-permute-start.10) | collective-permute-done | bytes 163872 | tf_op jit(solution)/shard_map/ppermute | solution.py:495
  60.1 0.9 %join_queries.1 = bf16[128,2560]{1,0:T(8,128)(2,1)} custom-call(bf16[128,640]{1,0:T(8,128)(2,1)S(1)} %get-tuple-element.57.refs_0_, bf16[128,640]{1,0:T(8,128)(2,1)S(1)} %get-tuple-element.62.refs_1_, bf16[128,640]{1,0:T(8,128)(2,1)S(1)} %collective-permute-done.10.refs_2_, bf16[128,640]{1,0:T(8,128)(2,1)S(1)} %collective-permute-done.11.refs_3_), custom_call_target="tpu_custom_call" | custom-call | bytes 1310720 | tf_op jit(solution)/shard_map/join_queries/pallas_call | solution.py:447
  61.1 0.0 collective-permute-done.15.refs_0_
  61.1 0.0 collective-permute-done.19.refs_1_
  61.1 0.8 %join_keys.1 = (bf16[128,512]{1,0:T(8,128)(2,1)}, bf16[128,512]{1,0:T(8,128)(2,1)}) custom-call(bf16[2,128,128]{2,1,0:T(8,128)(2,1)S(1)} %collective-permute-done.15.refs_0_, bf16[2,128,128]{2,1,0:T(8,128)(2,1)S(1)} %collective-permute-done.19.refs_1_, bf16[2,2,128,128]{3,2,1,0:T(8,128)(2,1)S(1)} %get-tuple-element.68.refs_2_, ...), custom_call_target="tpu_custom_call" | custom-call | bytes 524288 | tf_op jit(solution)/shard_map/join_keys/pallas_call | solution.py:481
  (4 shorter events, 0.1 us)
Async XLA Ops:
  2.4 5.6 %collective-permute-start = (bf16[272,128]{1,0:T(8,128)(2,1)}, bf16[272,128]{1,0:T(8,128)(2,1)S(1)}, u32[]{:S(2)}, u32[]{:S(2)}) collective-permute-start(bf16[272,128]{1,0:T(8,128)(2,1)} %get-tuple-element.43), channel_id=1, source_target_pairs={{0,2},{2,0},{4,6},{6,4},{8,10},{10,8},{12,14},{14,12},{1,3},{3,1},... | collective-permute-start | bytes 208904 | tf_op jit(solution)/shard_map/ppermute | solution.py:495
  5.4 8.0 %collective-permute-start.3 = (bf16[256,128]{1,0:T(8,128)(2,1)}, bf16[256,128]{1,0:T(8,128)(2,1)S(1)}, u32[]{:S(2)}, u32[]{:S(2)}) collective-permute-start(bf16[256,128]{1,0:T(8,128)(2,1)} %get-tuple-element.51), channel_id=1, source_target_pairs={{0,2},{2,0},{4,6},{6,4},{8,10},{10,8},{12,14},{14,12},{1,3},{3,1},... | collective-permute-start | bytes 196616 | tf_op jit(solution)/shard_map/ppermute | solution.py:495
  5.5 1.1 %copy-start = (bf16[128,2560]{1,0:T(8,128)(2,1)S(1)}, bf16[128,2560]{1,0:T(8,128)(2,1)}, u32[]{:S(2)}) copy-start(bf16[128,2560]{1,0:T(8,128)(2,1)} %q_ref) | copy-start | bytes 1966084
  6.5 1.1 %copy-start.1 = (bf16[128,2560]{1,0:T(8,128)(2,1)S(1)}, bf16[128,2560]{1,0:T(8,128)(2,1)}, u32[]{:S(2)}) copy-start(bf16[128,2560]{1,0:T(8,128)(2,1)} %dir_ref.1) | copy-start | bytes 1966084
  7.6 0.9 %copy-start.2 = (bf16[272,128]{1,0:T(8,128)(2,1)S(1)}, bf16[272,128]{1,0:T(8,128)(2,1)}, u32[]{:S(2)}) copy-start(bf16[272,128]{1,0:T(8,128)(2,1)} %get-tuple-element.42.refs_0_.mine_ref) | copy-start | bytes 208900
  8.5 4.8 %copy-start.3 = (bf16[256,128]{1,0:T(8,128)(2,1)S(1)}, bf16[256,128]{1,0:T(8,128)(2,1)}, u32[]{:S(2)}) copy-start(bf16[256,128]{1,0:T(8,128)(2,1)} %get-tuple-element.50.mine_ref) | copy-start | bytes 196612
  8.5 7.5 %collective-permute-start.1 = (bf16[544,128]{1,0:T(8,128)(2,1)S(1)}, bf16[544,128]{1,0:T(8,128)(2,1)S(1)}, u32[]{:S(2)}, u32[]{:S(2)}) collective-permute-start(bf16[544,128]{1,0:T(8,128)(2,1)S(1)} %join_blocks.2.refs_0_.refs_5_), channel_id=1, source_target_pairs={{0,4},{2,6},{4,0},{6,2},{8,12},{10,14},{12,8},{14,10},{1,5},{3,7},... | collective-permute-start | bytes 417800 | tf_op jit(solution)/shard_map/ppermute | solution.py:495
  10.7 8.5 %collective-permute-start.2 = (bf16[544,128]{1,0:T(8,128)(2,1)S(1)}, bf16[544,128]{1,0:T(8,128)(2,1)S(1)}, u32[]{:S(2)}, u32[]{:S(2)}) collective-permute-start(bf16[544,128]{1,0:T(8,128)(2,1)S(1)} %join_blocks.2.refs_0_.refs_5_), channel_id=1, source_target_pairs={{0,8},{2,10},{4,12},{6,14},{8,0},{10,2},{12,4},{14,6},{1,9},{3,11}... | collective-permute-start | bytes 417800 | tf_op jit(solution)/shard_map/ppermute | solution.py:495
  13.4 1.5 %copy-start.4 = (s32[8]{0:T(128)S(1)}, s32[8]{0:T(128)}, u32[]{:S(2)}) copy-start(s32[8]{0:T(128)} %lengths_s.1) | copy-start | bytes 100
  13.4 1.5 %copy-start.5 = (s32[8]{0:T(128)S(1)}, s32[8]{0:T(128)}, u32[]{:S(2)}) copy-start(s32[8]{0:T(128)} %refs_0_.3) | copy-start | bytes 100
  13.4 13.5 %collective-permute-start.5 = (bf16[2,5,128,128]{3,2,1,0:T(8,128)(2,1)S(1)}, bf16[2,5,128,128]{3,2,1,0:T(8,128)(2,1)S(1)}, u32[]{:S(2)}, u32[]{:S(2)}) collective-permute-start(bf16[2,5,128,128]{3,2,1,0:T(8,128)(2,1)S(1)} %get-tuple-element.56), channel_id=1, source_target_pairs={{0,2},{2,0},{4,6},{6,4},{8,10},{10,8},{12,14},{14,12},{1,3},{3,1},... | collective-permute-start | bytes 983048 | tf_op jit(solution)/shard_map/ppermute | solution.py:495
  19.2 5.1 %collective-permute-start.4 = (bf16[544,128]{1,0:T(8,128)(2,1)S(1)}, bf16[544,128]{1,0:T(8,128)(2,1)S(1)}, u32[]{:S(2)}, u32[]{:S(2)}) collective-permute-start(bf16[544,128]{1,0:T(8,128)(2,1)S(1)} %collective-permute-done.2.refs_2_.refs_7_), channel_id=1, source_target_pairs={{0,4},{2,6},{4,0},{6,2},{8,12},{10,14},{12,8},{14,10},{1,5},{3,7},... | collective-permute-start | bytes 417800 | tf_op jit(solution)/shard_map/ppermute | solution.py:495
  24.3 16.7 %collective-permute-start.6 = (bf16[2,5,128,128]{3,2,1,0:T(8,128)(2,1)S(1)}, bf16[2,5,128,128]{3,2,1,0:T(8,128)(2,1)S(1)}, u32[]{:S(2)}, u32[]{:S(2)}) collective-permute-start(bf16[2,5,128,128]{3,2,1,0:T(8,128)(2,1)S(1)} %get-tuple-element.59), channel_id=1, source_target_pairs={{0,2},{2,0},{4,6},{6,4},{8,10},{10,8},{12,14},{14,12},{1,3},{3,1},... | collective-permute-start | bytes 983048 | tf_op jit(solution)/shard_map/ppermute | solution.py:495
  26.9 7.1 %collective-permute-start.8 = (bf16[512,128]{1,0:T(8,128)(2,1)S(1)}, bf16[512,128]{1,0:T(8,128)(2,1)S(1)}, u32[]{:S(2)}, u32[]{:S(2)}) collective-permute-start(bf16[512,128]{1,0:T(8,128)(2,1)S(1)} %join_blocks.3.refs_5_), channel_id=1, source_target_pairs={{0,8},{2,10},{4,12},{6,14},{8,0},{10,2},{12,4},{14,6},{1,9},{3,11}... | collective-permute-start | bytes 393224 | tf_op jit(solution)/shard_map/ppermute | solution.py:495
  27.6 10.0 %collective-permute-start.7 = (bf16[512,128]{1,0:T(8,128)(2,1)S(1)}, bf16[512,128]{1,0:T(8,128)(2,1)S(1)}, u32[]{:S(2)}, u32[]{:S(2)}) collective-permute-start(bf16[512,128]{1,0:T(8,128)(2,1)S(1)} %join_blocks.3.refs_5_), channel_id=1, source_target_pairs={{0,4},{2,6},{4,0},{6,2},{8,12},{10,14},{12,8},{14,10},{1,5},{3,7},... | collective-permute-start | bytes 393224 | tf_op jit(solution)/shard_map/ppermute | solution.py:495
  33.9 7.1 %collective-permute-start.9 = (bf16[512,128]{1,0:T(8,128)(2,1)S(1)}, bf16[512,128]{1,0:T(8,128)(2,1)S(1)}, u32[]{:S(2)}, u32[]{:S(2)}) collective-permute-start(bf16[512,128]{1,0:T(8,128)(2,1)S(1)} %collective-permute-done.8.refs_7_), channel_id=1, source_target_pairs={{0,4},{2,6},{4,0},{6,2},{8,12},{10,14},{12,8},{14,10},{1,5},{3,7},... | collective-permute-start | bytes 393224 | tf_op jit(solution)/shard_map/ppermute | solution.py:495
  34.1 13.8 %collective-permute-start.12 = (bf16[2,2,128,128]{3,2,1,0:T(8,128)(2,1)S(1)}, bf16[2,2,128,128]{3,2,1,0:T(8,128)(2,1)S(1)}, u32[]{:S(2)}, u32[]{:S(2)}) collective-permute-start(bf16[2,2,128,128]{3,2,1,0:T(8,128)(2,1)S(1)} %get-tuple-element.69), channel_id=1, source_target_pairs={{0,12},{2,14},{4,8},{6,10},{8,4},{10,6},{12,0},{14,2},{1,13},{3,15... | collective-permute-start | bytes 393224 | tf_op jit(solution)/shard_map/ppermute | solution.py:495
  36.5 13.4 %collective-permute-start.13 = (bf16[2,2,128,128]{3,2,1,0:T(8,128)(2,1)S(1)}, bf16[2,2,128,128]{3,2,1,0:T(8,128)(2,1)S(1)}, u32[]{:S(2)}, u32[]{:S(2)}) collective-permute-start(bf16[2,2,128,128]{3,2,1,0:T(8,128)(2,1)S(1)} %get-tuple-element.70), channel_id=1, source_target_pairs={{0,8},{2,10},{4,12},{6,14},{8,0},{10,2},{12,4},{14,6},{1,9},{3,11}... | collective-permute-start | bytes 393224 | tf_op jit(solution)/shard_map/ppermute | solution.py:495
  37.5 12.4 %collective-permute-start.14 = (bf16[2,2,128,128]{3,2,1,0:T(8,128)(2,1)S(1)}, bf16[2,2,128,128]{3,2,1,0:T(8,128)(2,1)S(1)}, u32[]{:S(2)}, u32[]{:S(2)}) collective-permute-start(bf16[2,2,128,128]{3,2,1,0:T(8,128)(2,1)S(1)} %get-tuple-element.71), channel_id=1, source_target_pairs={{0,4},{2,6},{4,0},{6,2},{8,12},{10,14},{12,8},{14,10},{1,5},{3,7},... | collective-permute-start | bytes 393224 | tf_op jit(solution)/shard_map/ppermute | solution.py:495
  45.5 7.0 %collective-permute-start.16 = (bf16[2,2,128,128]{3,2,1,0:T(8,128)(2,1)S(1)}, bf16[2,2,128,128]{3,2,1,0:T(8,128)(2,1)S(1)}, u32[]{:S(2)}, u32[]{:S(2)}) collective-permute-start(bf16[2,2,128,128]{3,2,1,0:T(8,128)(2,1)S(1)} %get-tuple-element.74), channel_id=1, source_target_pairs={{0,12},{2,14},{4,8},{6,10},{8,4},{10,6},{12,0},{14,2},{1,13},{3,15... | collective-permute-start | bytes 393224 | tf_op jit(solution)/shard_map/ppermute | solution.py:495
  47.9 8.5 %collective-permute-start.17 = (bf16[2,2,128,128]{3,2,1,0:T(8,128)(2,1)S(1)}, bf16[2,2,128,128]{3,2,1,0:T(8,128)(2,1)S(1)}, u32[]{:S(2)}, u32[]{:S(2)}) collective-permute-start(bf16[2,2,128,128]{3,2,1,0:T(8,128)(2,1)S(1)} %get-tuple-element.75), channel_id=1, source_target_pairs={{0,8},{2,10},{4,12},{6,14},{8,0},{10,2},{12,4},{14,6},{1,9},{3,11}... | collective-permute-start | bytes 393224 | tf_op jit(solution)/shard_map/ppermute | solution.py:495
  47.9 8.5 %collective-permute-start.18 = (bf16[2,2,128,128]{3,2,1,0:T(8,128)(2,1)S(1)}, bf16[2,2,128,128]{3,2,1,0:T(8,128)(2,1)S(1)}, u32[]{:S(2)}, u32[]{:S(2)}) collective-permute-start(bf16[2,2,128,128]{3,2,1,0:T(8,128)(2,1)S(1)} %get-tuple-element.76), channel_id=1, source_target_pairs={{0,4},{2,6},{4,0},{6,2},{8,12},{10,14},{12,8},{14,10},{1,5},{3,7},... | collective-permute-start | bytes 393224 | tf_op jit(solution)/shard_map/ppermute | solution.py:495
  50.0 11.1 %collective-permute-start.15 = (bf16[2,128,128]{2,1,0:T(8,128)(2,1)S(1)}, bf16[2,128,128]{2,1,0:T(8,128)(2,1)S(1)}, u32[]{:S(2)}, u32[]{:S(2)}) collective-permute-start(bf16[2,128,128]{2,1,0:T(8,128)(2,1)S(1)} %fusion), channel_id=1, source_target_pairs={{0,2},{2,0},{4,6},{6,4},{8,10},{10,8},{12,14},{14,12},{1,3},{3,1},... | collective-permute-start | bytes 196616 | tf_op jit(solution)/shard_map/ppermute | solution.py:495
  52.4 5.3 %collective-permute-start.11 = (bf16[128,640]{1,0:T(8,128)(2,1)S(1)}, bf16[128,640]{1,0:T(8,128)(2,1)S(1)}, u32[]{:S(2)}, u32[]{:S(2)}) collective-permute-start(bf16[128,640]{1,0:T(8,128)(2,1)S(1)} %get-tuple-element.66), channel_id=1, source_target_pairs={{0,2},{2,0},{4,6},{6,4},{8,10},{10,8},{12,14},{14,12},{1,3},{3,1},... | collective-permute-start | bytes 491528 | tf_op jit(solution)/shard_map/ppermute | solution.py:495
  52.5 7.7 %collective-permute-start.10 = (bf16[128,640]{1,0:T(8,128)(2,1)S(1)}, bf16[128,640]{1,0:T(8,128)(2,1)S(1)}, u32[]{:S(2)}, u32[]{:S(2)}) collective-permute-start(bf16[128,640]{1,0:T(8,128)(2,1)S(1)} %get-tuple-element.64), channel_id=1, source_target_pairs={{0,2},{2,0},{4,6},{6,4},{8,10},{10,8},{12,14},{14,12},{1,3},{3,1},... | collective-permute-start | bytes 491528 | tf_op jit(solution)/shard_map/ppermute | solution.py:495
  56.4 4.6 %collective-permute-start.19 = (bf16[2,128,128]{2,1,0:T(8,128)(2,1)S(1)}, bf16[2,128,128]{2,1,0:T(8,128)(2,1)S(1)}, u32[]{:S(2)}, u32[]{:S(2)}) collective-permute-start(bf16[2,128,128]{2,1,0:T(8,128)(2,1)S(1)} %fusion.1), channel_id=1, source_target_pairs={{0,2},{2,0},{4,6},{6,4},{8,10},{10,8},{12,14},{14,12},{1,3},{3,1},... | collective-permute-start | bytes 196616 | tf_op jit(solution)/shard_map/ppermute | solution.py:495

commit v14 on v13

--- a/solution.py
+++ b/solution.py
@@ -516,9 +516,9 @@
     three = permute(after(two, one, near[1], bias), meet[1])
     chains = [[near[0], one, two, three]]
     taken_q = [permute(after(given_q[0], near[0], near[1]), swap)]
-    block = after(near[1], two, one, taken_q[0])
+    block = after(near[1], two, one)
     two, one = permute(block, meet[2]), permute(block, meet[1])
-    taken_q.append(permute(after(given_q[1], three), swap))
+    taken_q.append(permute(after(given_q[1], taken_q[0]), swap))
     row, advantages = advantages_of(columns, weights, chains[0])
 
     dq_own, dq_back, dkv_list = [], [], []
@@ -536,7 +536,7 @@
     for dkv in dkv_list:
         arrived = [permute(dkv[bits], meet[bits]) for bits in steps[::-1]]
         summands.append([after(dkv[0], dq_own[-1])] + arrived)
-    dq_back = [permute(after(block, dq_own[-1]), swap) for block in dq_back]
+    dq_back = [permute(block, swap) for block in dq_back]
     others = []
     for blocks in summands:
         total = sum(block[1].astype(jnp.float32) for block in blocks)

time: 62.1 us -> 63.4 us (1.021)
  waiting for transfers between devices: 15.4 us -> 20.5 us
  starting transfers between devices: 28.5 us -> 24.3 us
    ppermute x20, waiting for transfers between devices: 15.4 us -> 20.5 us  [permute(): return lax.ppermute(array, 'seg', pairs)]
    ppermute x20, starting transfers between devices: 28.5 us -> 24.3 us  [permute(): return lax.ppermute(array, 'seg', pairs)]
  transfers between devices with their start and end apart: 20 -> 20, of which waited for: 7 -> 10; matrix products, arithmetic and copies ran while one was open for 0% -> 0% of each run, Pallas kernels for 19% -> 19%
where the time goes in v14:
time: 63.4 us; the launch traced here: 63.1 us
  starting transfers between devices  24.3 us (38%)
  waiting for transfers between devices  20.5 us (32%)
  Pallas kernels  14.5 us (23%)
  local copies, waits for them, and re-layouts  3.05 us (5%)
  between operations  0.77 us (1%)
    ppermute x20, starting transfers between devices, permute(): return lax.ppermute(array, 'seg', pairs)  24.3 us
    ppermute x20, waiting for transfers between devices, permute(): return lax.ppermute(array, 'seg', pairs)  20.5 us
    pallas_call x2, Pallas kernels, attend(): pl.pallas_call(functools.partial(attend_kernel, DEPTH, segs, steps, group...  8.85 us
    unnamed x12, local copies, waits for them, and re-layouts  3.05 us
    pallas_call x1, Pallas kernels, pack(): pl.pallas_call(functools.partial(pack_kernel, log_rate, parts), out_shape...  1.81 us
  transfers between devices with their start and end apart: 20, of which 10 were waited for; matrix products, arithmetic and copies ran while one was open for 0% of the time, Pallas kernels for 19%

profile of v14, /device:TPU:0, one launch (start us, length us, event | category | flops | bytes accessed | tf_op | source)
XLA Modules:
  0.0 63.1 jit_solution(13526301510045003660)
XLA Ops:
  0.6 1.8 %pack_keys_values.1 = (bf16[272,128]{1,0:T(8,128)(2,1)}, bf16[256,128]{1,0:T(8,128)(2,1)}, bf16[272,128]{1,0:T(8,128)(2,1)}, bf16[256,128]{1,0:T(8,128)(2,1)}) custom-call(s32[8]{0:T(128)} %lengths_s.1, bf16[128,512]{1,0:T(8,128)(2,1)} %k_ref.1, bf16[128,512]{1,0:T(8,128)(2,1)} %v_ref.1, f32[1,128]{1,0:T(1,128)} %bitcast.9, f32[1,128]{1,0:T(1,128)} %bitcast.10, ...), custom_call_target="tpu_custom_call" | custom-call | flops 12800 | bytes 524288 | tf_op jit(solution)/shard_map/pack_keys_values/pallas_call | solution.py:104
  2.4 2.9 %collective-permute-start = (bf16[272,128]{1,0:T(8,128)(2,1)}, bf16[272,128]{1,0:T(8,128)(2,1)S(1)}, u32[]{:S(2)}, u32[]{:S(2)}) collective-permute-start(bf16[272,128]{1,0:T(8,128)(2,1)} %get-tuple-element.41), channel_id=1, source_target_pairs={{0,2},{2,0},{4,6},{6,4},{8,10},{10,8},{12,14},{14,12},{1,3},{3,1},... | collective-permute-start | bytes 208904 | tf_op jit(solution)/shard_map/ppermute | solution.py:495
  5.4 0.1 collective-permute-start.3
  5.5 0.0 copy-start
  5.5 1.1 %copy-done = bf16[128,2560]{1,0:T(8,128)(2,1)S(1)} copy-done((bf16[128,2560]{1,0:T(8,128)(2,1)S(1)}, bf16[128,2560]{1,0:T(8,128)(2,1)}, u32[]{:S(2)}) %copy-start) | copy-done | bytes 655384
  6.5 0.0 copy-start.1
  6.5 1.1 %copy-done.1 = bf16[128,2560]{1,0:T(8,128)(2,1)S(1)} copy-done((bf16[128,2560]{1,0:T(8,128)(2,1)S(1)}, bf16[128,2560]{1,0:T(8,128)(2,1)}, u32[]{:S(2)}) %copy-start.1) | copy-done | bytes 655384
  7.6 0.0 copy-start.3
  7.6 0.2 pack_queries.1
  7.9 2.0 %collective-permute-done.3.other_ref = bf16[256,128]{1,0:T(8,128)(2,1)S(1)} collective-permute-done((bf16[256,128]{1,0:T(8,128)(2,1)}, bf16[256,128]{1,0:T(8,128)(2,1)S(1)}, u32[]{:S(2)}, u32[]{:S(2)}) %collective-permute-start.3) | collective-permute-done | bytes 65568 | tf_op jit(solution)/shard_map/ppermute | solution.py:495
  9.9 0.0 copy-done.3
  9.9 0.0 copy-start.2
  9.9 0.0 collective-permute-done.refs_1_.other_ref
  9.9 0.9 %copy-done.2 = bf16[272,128]{1,0:T(8,128)(2,1)S(1)} copy-done((bf16[272,128]{1,0:T(8,128)(2,1)S(1)}, bf16[272,128]{1,0:T(8,128)(2,1)}, u32[]{:S(2)}) %copy-start.2) | copy-done | bytes 69656
  10.8 0.0 copy-start.4
  10.8 0.0 copy-start.5
  10.8 1.1 %collective-permute-start.5 = (bf16[2,5,128,128]{3,2,1,0:T(8,128)(2,1)S(1)}, bf16[2,5,128,128]{3,2,1,0:T(8,128)(2,1)S(1)}, u32[]{:S(2)}, u32[]{:S(2)}) collective-permute-start(bf16[2,5,128,128]{3,2,1,0:T(8,128)(2,1)S(1)} %get-tuple-element.54), channel_id=1, source_target_pairs={{0,2},{2,0},{4,6},{6,4},{8,10},{10,8},{12,14},{14,12},{1,3},{3,1},... | collective-permute-start | bytes 983048 | tf_op jit(solution)/shard_map/ppermute | solution.py:495
  11.9 1.6 %collective-permute-start.1 = (bf16[544,128]{1,0:T(8,128)(2,1)S(1)}, bf16[544,128]{1,0:T(8,128)(2,1)S(1)}, u32[]{:S(2)}, u32[]{:S(2)}) collective-permute-start(bf16[544,128]{1,0:T(8,128)(2,1)S(1)} %join_blocks.2.refs_0_.refs_5_), channel_id=1, source_target_pairs={{0,4},{2,6},{4,0},{6,2},{8,12},{10,14},{12,8},{14,10},{1,5},{3,7},... | collective-permute-start | bytes 417800 | tf_op jit(solution)/shard_map/ppermute | solution.py:495
  13.5 2.6 %collective-permute-start.2 = (bf16[544,128]{1,0:T(8,128)(2,1)S(1)}, bf16[544,128]{1,0:T(8,128)(2,1)S(1)}, u32[]{:S(2)}, u32[]{:S(2)}) collective-permute-start(bf16[544,128]{1,0:T(8,128)(2,1)S(1)} %join_blocks.2.refs_0_.refs_5_), channel_id=1, source_target_pairs={{0,8},{2,10},{4,12},{6,14},{8,0},{10,2},{12,4},{14,6},{1,9},{3,11}... | collective-permute-start | bytes 417800 | tf_op jit(solution)/shard_map/ppermute | solution.py:495
  16.1 0.0 copy-done.4
  16.1 0.0 copy-done.5
  16.1 1.2 %prepare.1 = (f32[2,640,128]{2,1,0:T(8,128)S(1)}, f32[2,3,128,128]{3,2,1,0:T(8,128)S(1)}, f32[2,2,8,128]{3,2,1,0:T(8,128)S(1)}) custom-call(s32[8]{0:T(128)S(1)} %copy-done.5, s32[8]{0:T(128)S(1)} %copy-done.4, bf16[272,128]{1,0:T(8,128)(2,1)S(1)} %copy-done.2, bf16[272,128]{1,0:T(8,128)(2,1)S(1)} %collective-permute-done.refs_1_.other_ref), custom_call_target="tpu_custom_call" | custom-call | flops 3276800 | bytes 655360 | tf_op jit(solution)/shard_map/prepare/pallas_call | solution.py:253
  17.3 1.5 %collective-permute-done.1.refs_1_.refs_6_ = bf16[544,128]{1,0:T(8,128)(2,1)S(1)} collective-permute-done((bf16[544,128]{1,0:T(8,128)(2,1)S(1)}, bf16[544,128]{1,0:T(8,128)(2,1)S(1)}, u32[]{:S(2)}, u32[]{:S(2)}) %collective-permute-start.1) | collective-permute-done | bytes 139296 | tf_op jit(solution)/shard_map/ppermute | solution.py:495
  18.8 2.7 %collective-permute-done.2.refs_2_.refs_7_ = bf16[544,128]{1,0:T(8,128)(2,1)S(1)} collective-permute-done((bf16[544,128]{1,0:T(8,128)(2,1)S(1)}, bf16[544,128]{1,0:T(8,128)(2,1)S(1)}, u32[]{:S(2)}, u32[]{:S(2)}) %collective-permute-start.2) | collective-permute-done | bytes 139296 | tf_op jit(solution)/shard_map/ppermute | solution.py:495
  21.5 0.4 collective-permute-start.4
  21.8 0.0 collective-permute-done.5.refs_4_
  21.8 1.3 %collective-permute-start.6 = (bf16[2,5,128,128]{3,2,1,0:T(8,128)(2,1)S(1)}, bf16[2,5,128,128]{3,2,1,0:T(8,128)(2,1)S(1)}, u32[]{:S(2)}, u32[]{:S(2)}) collective-permute-start(bf16[2,5,128,128]{3,2,1,0:T(8,128)(2,1)S(1)} %get-tuple-element.57), channel_id=1, source_target_pairs={{0,2},{2,0},{4,6},{6,4},{8,10},{10,8},{12,14},{14,12},{1,3},{3,1},... | collective-permute-start | bytes 983048 | tf_op jit(solution)/shard_map/ppermute | solution.py:495
  23.2 2.7 %collective-permute-start.8 = (bf16[512,128]{1,0:T(8,128)(2,1)S(1)}, bf16[512,128]{1,0:T(8,128)(2,1)S(1)}, u32[]{:S(2)}, u32[]{:S(2)}) collective-permute-start(bf16[512,128]{1,0:T(8,128)(2,1)S(1)} %join_blocks.3.refs_5_), channel_id=1, source_target_pairs={{0,8},{2,10},{4,12},{6,14},{8,0},{10,2},{12,4},{14,6},{1,9},{3,11}... | collective-permute-start | bytes 393224 | tf_op jit(solution)/shard_map/ppermute | solution.py:495
  25.9 0.0 collective-permute-start.7
  25.9 3.6 %collective-permute-done.4.refs_3_.refs_8_ = bf16[544,128]{1,0:T(8,128)(2,1)S(1)} collective-permute-done((bf16[544,128]{1,0:T(8,128)(2,1)S(1)}, bf16[544,128]{1,0:T(8,128)(2,1)S(1)}, u32[]{:S(2)}, u32[]{:S(2)}) %collective-permute-start.4) | collective-permute-done | bytes 139296 | tf_op jit(solution)/shard_map/ppermute | solution.py:495
  29.5 0.7 %advantages.1 = (f32[1,128]{1,0:T(1,128)}, f32[2,128,128]{2,1,0:T(8,128)S(1)}) custom-call(f32[2,3,128,128]{3,2,1,0:T(8,128)S(1)} %get-tuple-element.42.columns_ref, f32[2,2,8,128]{3,2,1,0:T(8,128)S(1)} %get-tuple-element.43.weights_ref, bf16[544,128]{1,0:T(8,128)(2,1)S(1)} %join_blocks.2.refs_0_.refs_5_, ...), custom_call_target="tpu_custom_call" | custom-call | flops 327680 | bytes 524288 | tf_op jit(solution)/shard_map/advantages/pallas_call | solution.py:306
  30.2 4.4 %tree_attention_backward.2 = (bf16[128,640]{1,0:T(8,128)(2,1)S(1)}, bf16[128,640]{1,0:T(8,128)(2,1)S(1)}, bf16[2,2,128,128]{3,2,1,0:T(8,128)(2,1)S(1)}, bf16[2,2...) custom-call(s32[8]{0:T(128)S(1)} %copy-done.5, ...), custom_call_target="tpu_custom_call" | custom-call | flops 1048576000 | bytes 8388608 | tf_op jit(solution)/shard_map/tree_attention_backward/pallas_call | solution.py:409
  34.6 0.0 collective-permute-done.8.refs_7_
  34.6 0.1 collective-permute-start.9
  34.7 2.3 %collective-permute-start.12 = (bf16[2,2,128,128]{3,2,1,0:T(8,128)(2,1)S(1)}, bf16[2,2,128,128]{3,2,1,0:T(8,128)(2,1)S(1)}, u32[]{:S(2)}, u32[]{:S(2)}) collective-permute-start(bf16[2,2,128,128]{3,2,1,0:T(8,128)(2,1)S(1)} %get-tuple-element.65), channel_id=1, source_target_pairs={{0,12},{2,14},{4,8},{6,10},{8,4},{10,6},{12,0},{14,2},{1,13},{3,15... | collective-permute-start | bytes 393224 | tf_op jit(solution)/shard_map/ppermute | solution.py:495
  37.1 1.1 %collective-permute-start.13 = (bf16[2,2,128,128]{3,2,1,0:T(8,128)(2,1)S(1)}, bf16[2,2,128,128]{3,2,1,0:T(8,128)(2,1)S(1)}, u32[]{:S(2)}, u32[]{:S(2)}) collective-permute-start(bf16[2,2,128,128]{3,2,1,0:T(8,128)(2,1)S(1)} %get-tuple-element.66), channel_id=1, source_target_pairs={{0,8},{2,10},{4,12},{6,14},{8,0},{10,2},{12,4},{14,6},{1,9},{3,11}... | collective-permute-start | bytes 393224 | tf_op jit(solution)/shard_map/ppermute | solution.py:495
  38.2 0.0 collective-permute-done.7.refs_6_
  38.2 1.0 %collective-permute-start.14 = (bf16[2,2,128,128]{3,2,1,0:T(8,128)(2,1)S(1)}, bf16[2,2,128,128]{3,2,1,0:T(8,128)(2,1)S(1)}, u32[]{:S(2)}, u32[]{:S(2)}) collective-permute-start(bf16[2,2,128,128]{3,2,1,0:T(8,128)(2,1)S(1)} %get-tuple-element.67), channel_id=1, source_target_pairs={{0,4},{2,6},{4,0},{6,2},{8,12},{10,14},{12,8},{14,10},{1,5},{3,7},... | collective-permute-start | bytes 393224 | tf_op jit(solution)/shard_map/ppermute | solution.py:495
  39.2 0.5 collective-permute-done.9.refs_8_
  39.7 0.8 %collective-permute-start.10 = (bf16[128,640]{1,0:T(8,128)(2,1)S(1)}, bf16[128,640]{1,0:T(8,128)(2,1)S(1)}, u32[]{:S(2)}, u32[]{:S(2)}) collective-permute-start(bf16[128,640]{1,0:T(8,128)(2,1)S(1)} %get-tuple-element.61), channel_id=1, source_target_pairs={{0,2},{2,0},{4,6},{6,4},{8,10},{10,8},{12,14},{14,12},{1,3},{3,1},... | collective-permute-start | bytes 491528 | tf_op jit(solution)/shard_map/ppermute | solution.py:495
  40.5 0.0 collective-permute-done.6.refs_4_
  40.5 4.4 %tree_attention_backward.3 = (bf16[128,640]{1,0:T(8,128)(2,1)S(1)}, bf16[128,640]{1,0:T(8,128)(2,1)S(1)}, bf16[2,2,128,128]{3,2,1,0:T(8,128)(2,1)S(1)}, bf16[2,2...) custom-call(s32[8]{0:T(128)S(1)} %copy-done.5, ...), custom_call_target="tpu_custom_call" | custom-call | flops 1048576000 | bytes 8388608 | tf_op jit(solution)/shard_map/tree_attention_backward/pallas_call | solution.py:409
  44.9 2.7 %collective-permute-start.16 = (bf16[2,2,128,128]{3,2,1,0:T(8,128)(2,1)S(1)}, bf16[2,2,128,128]{3,2,1,0:T(8,128)(2,1)S(1)}, u32[]{:S(2)}, u32[]{:S(2)}) collective-permute-start(bf16[2,2,128,128]{3,2,1,0:T(8,128)(2,1)S(1)} %get-tuple-element.70), channel_id=1, source_target_pairs={{0,12},{2,14},{4,8},{6,10},{8,4},{10,6},{12,0},{14,2},{1,13},{3,15... | collective-permute-start | bytes 393224 | tf_op jit(solution)/shard_map/ppermute | solution.py:495
  47.6 0.0 collective-permute-done.12.refs_3_
  47.6 1.4 %collective-permute-start.17 = (bf16[2,2,128,128]{3,2,1,0:T(8,128)(2,1)S(1)}, bf16[2,2,128,128]{3,2,1,0:T(8,128)(2,1)S(1)}, u32[]{:S(2)}, u32[]{:S(2)}) collective-permute-start(bf16[2,2,128,128]{3,2,1,0:T(8,128)(2,1)S(1)} %get-tuple-element.71), channel_id=1, source_target_pairs={{0,8},{2,10},{4,12},{6,14},{8,0},{10,2},{12,4},{14,6},{1,9},{3,11}... | collective-permute-start | bytes 393224 | tf_op jit(solution)/shard_map/ppermute | solution.py:495
  49.0 2.8 %collective-permute-done.13.refs_4_ = bf16[2,2,128,128]{3,2,1,0:T(8,128)(2,1)S(1)} collective-permute-done((bf16[2,2,128,128]{3,2,1,0:T(8,128)(2,1)S(1)}, bf16[2,2,128,128]{3,2,1,0:T(8,128)(2,1)S(1)}, u32[]{:S(2)}, u32[]{:S(2)}) %collective-permute-start.13) | collective-permute-done | bytes 131104 | tf_op jit(solution)/shard_map/ppermute | solution.py:495
  51.9 0.0 collective-permute-start.18
  51.9 0.0 collective-permute-done.14.refs_5_
  51.9 0.1 collective-permute-start.15
  52.0 0.0 collective-permute-done.16.refs_7_
  52.0 2.0 %collective-permute-start.11 = (bf16[128,640]{1,0:T(8,128)(2,1)S(1)}, bf16[128,640]{1,0:T(8,128)(2,1)S(1)}, u32[]{:S(2)}, u32[]{:S(2)}) collective-permute-start(bf16[128,640]{1,0:T(8,128)(2,1)S(1)} %get-tuple-element.62), channel_id=1, source_target_pairs={{0,2},{2,0},{4,6},{6,4},{8,10},{10,8},{12,14},{14,12},{1,3},{3,1},... | collective-permute-start | bytes 491528 | tf_op jit(solution)/shard_map/ppermute | solution.py:495
  54.0 2.7 %collective-permute-done.17.refs_8_ = bf16[2,2,128,128]{3,2,1,0:T(8,128)(2,1)S(1)} collective-permute-done((bf16[2,2,128,128]{3,2,1,0:T(8,128)(2,1)S(1)}, bf16[2,2,128,128]{3,2,1,0:T(8,128)(2,1)S(1)}, u32[]{:S(2)}, u32[]{:S(2)}) %collective-permute-start.17) | collective-permute-done | bytes 131104 | tf_op jit(solution)/shard_map/ppermute | solution.py:495
  56.7 1.3 %collective-permute-done.18.refs_9_ = bf16[2,2,128,128]{3,2,1,0:T(8,128)(2,1)S(1)} collective-permute-done((bf16[2,2,128,128]{3,2,1,0:T(8,128)(2,1)S(1)}, bf16[2,2,128,128]{3,2,1,0:T(8,128)(2,1)S(1)}, u32[]{:S(2)}, u32[]{:S(2)}) %collective-permute-start.18) | collective-permute-done | bytes 131104 | tf_op jit(solution)/shard_map/ppermute | solution.py:495
  58.0 0.1 collective-permute-start.19
  58.1 0.0 collective-permute-done.10.refs_2_
  58.1 0.6 collective-permute-done.11.refs_3_
  58.7 0.9 %join_queries.1 = bf16[128,2560]{1,0:T(8,128)(2,1)} custom-call(bf16[128,640]{1,0:T(8,128)(2,1)S(1)} %get-tuple-element.55.refs_0_, bf16[128,640]{1,0:T(8,128)(2,1)S(1)} %get-tuple-element.60.refs_1_, bf16[128,640]{1,0:T(8,128)(2,1)S(1)} %collective-permute-done.10.refs_2_, bf16[128,640]{1,0:T(8,128)(2,1)S(1)} %collective-permute-done.11.refs_3_), custom_call_target="tpu_custom_call" | custom-call | bytes 1310720 | tf_op jit(solution)/shard_map/join_queries/pallas_call | solution.py:447
  59.6 0.0 collective-permute-done.15.refs_0_
  59.6 2.7 %collective-permute-done.19.refs_1_ = bf16[2,128,128]{2,1,0:T(8,128)(2,1)S(1)} collective-permute-done((bf16[2,128,128]{2,1,0:T(8,128)(2,1)S(1)}, bf16[2,128,128]{2,1,0:T(8,128)(2,1)S(1)}, u32[]{:S(2)}, u32[]{:S(2)}) %collective-permute-start.19) | collective-permute-done | bytes 65568 | tf_op jit(solution)/shard_map/ppermute | solution.py:495
  62.4 0.8 %join_keys.1 = (bf16[128,512]{1,0:T(8,128)(2,1)}, bf16[128,512]{1,0:T(8,128)(2,1)}) custom-call(bf16[2,128,128]{2,1,0:T(8,128)(2,1)S(1)} %collective-permute-done.15.refs_0_, bf16[2,128,128]{2,1,0:T(8,128)(2,1)S(1)} %collective-permute-done.19.refs_1_, bf16[2,2,128,128]{3,2,1,0:T(8,128)(2,1)S(1)} %get-tuple-element.64.refs_2_, ...), custom_call_target="tpu_custom_call" | custom-call | bytes 524288 | tf_op jit(solution)/shard_map/join_keys/pallas_call | solution.py:481
  (4 shorter events, 0.1 us)
Async XLA Ops:
  2.4 7.4 %collective-permute-start = (bf16[272,128]{1,0:T(8,128)(2,1)}, bf16[272,128]{1,0:T(8,128)(2,1)S(1)}, u32[]{:S(2)}, u32[]{:S(2)}) collective-permute-start(bf16[272,128]{1,0:T(8,128)(2,1)} %get-tuple-element.41), channel_id=1, source_target_pairs={{0,2},{2,0},{4,6},{6,4},{8,10},{10,8},{12,14},{14,12},{1,3},{3,1},... | collective-permute-start | bytes 208904 | tf_op jit(solution)/shard_map/ppermute | solution.py:495
  5.4 4.5 %collective-permute-start.3 = (bf16[256,128]{1,0:T(8,128)(2,1)}, bf16[256,128]{1,0:T(8,128)(2,1)S(1)}, u32[]{:S(2)}, u32[]{:S(2)}) collective-permute-start(bf16[256,128]{1,0:T(8,128)(2,1)} %get-tuple-element.49), channel_id=1, source_target_pairs={{0,2},{2,0},{4,6},{6,4},{8,10},{10,8},{12,14},{14,12},{1,3},{3,1},... | collective-permute-start | bytes 196616 | tf_op jit(solution)/shard_map/ppermute | solution.py:495
  5.5 1.1 %copy-start = (bf16[128,2560]{1,0:T(8,128)(2,1)S(1)}, bf16[128,2560]{1,0:T(8,128)(2,1)}, u32[]{:S(2)}) copy-start(bf16[128,2560]{1,0:T(8,128)(2,1)} %q_ref) | copy-start | bytes 1966084
  6.5 1.1 %copy-start.1 = (bf16[128,2560]{1,0:T(8,128)(2,1)S(1)}, bf16[128,2560]{1,0:T(8,128)(2,1)}, u32[]{:S(2)}) copy-start(bf16[128,2560]{1,0:T(8,128)(2,1)} %dir_ref.1) | copy-start | bytes 1966084
  7.6 2.2 %copy-start.3 = (bf16[256,128]{1,0:T(8,128)(2,1)S(1)}, bf16[256,128]{1,0:T(8,128)(2,1)}, u32[]{:S(2)}) copy-start(bf16[256,128]{1,0:T(8,128)(2,1)} %get-tuple-element.48.mine_ref) | copy-start | bytes 196612
  9.9 0.9 %copy-start.2 = (bf16[272,128]{1,0:T(8,128)(2,1)S(1)}, bf16[272,128]{1,0:T(8,128)(2,1)}, u32[]{:S(2)}) copy-start(bf16[272,128]{1,0:T(8,128)(2,1)} %get-tuple-element.40.refs_0_.mine_ref) | copy-start | bytes 208900
  10.8 5.3 %copy-start.4 = (s32[8]{0:T(128)S(1)}, s32[8]{0:T(128)}, u32[]{:S(2)}) copy-start(s32[8]{0:T(128)} %lengths_s.1) | copy-start | bytes 100
  10.8 5.3 %copy-start.5 = (s32[8]{0:T(128)S(1)}, s32[8]{0:T(128)}, u32[]{:S(2)}) copy-start(s32[8]{0:T(128)} %refs_0_.3) | copy-start | bytes 100
  10.8 11.1 %collective-permute-start.5 = (bf16[2,5,128,128]{3,2,1,0:T(8,128)(2,1)S(1)}, bf16[2,5,128,128]{3,2,1,0:T(8,128)(2,1)S(1)}, u32[]{:S(2)}, u32[]{:S(2)}) collective-permute-start(bf16[2,5,128,128]{3,2,1,0:T(8,128)(2,1)S(1)} %get-tuple-element.54), channel_id=1, source_target_pairs={{0,2},{2,0},{4,6},{6,4},{8,10},{10,8},{12,14},{14,12},{1,3},{3,1},... | collective-permute-start | bytes 983048 | tf_op jit(solution)/shard_map/ppermute | solution.py:495
  11.9 6.9 %collective-permute-start.1 = (bf16[544,128]{1,0:T(8,128)(2,1)S(1)}, bf16[544,128]{1,0:T(8,128)(2,1)S(1)}, u32[]{:S(2)}, u32[]{:S(2)}) collective-permute-start(bf16[544,128]{1,0:T(8,128)(2,1)S(1)} %join_blocks.2.refs_0_.refs_5_), channel_id=1, source_target_pairs={{0,4},{2,6},{4,0},{6,2},{8,12},{10,14},{12,8},{14,10},{1,5},{3,7},... | collective-permute-start | bytes 417800 | tf_op jit(solution)/shard_map/ppermute | solution.py:495
  13.5 8.0 %collective-permute-start.2 = (bf16[544,128]{1,0:T(8,128)(2,1)S(1)}, bf16[544,128]{1,0:T(8,128)(2,1)S(1)}, u32[]{:S(2)}, u32[]{:S(2)}) collective-permute-start(bf16[544,128]{1,0:T(8,128)(2,1)S(1)} %join_blocks.2.refs_0_.refs_5_), channel_id=1, source_target_pairs={{0,8},{2,10},{4,12},{6,14},{8,0},{10,2},{12,4},{14,6},{1,9},{3,11}... | collective-permute-start | bytes 417800 | tf_op jit(solution)/shard_map/ppermute | solution.py:495
  21.5 8.0 %collective-permute-start.4 = (bf16[544,128]{1,0:T(8,128)(2,1)S(1)}, bf16[544,128]{1,0:T(8,128)(2,1)S(1)}, u32[]{:S(2)}, u32[]{:S(2)}) collective-permute-start(bf16[544,128]{1,0:T(8,128)(2,1)S(1)} %collective-permute-done.2.refs_2_.refs_7_), channel_id=1, source_target_pairs={{0,4},{2,6},{4,0},{6,2},{8,12},{10,14},{12,8},{14,10},{1,5},{3,7},... | collective-permute-start | bytes 417800 | tf_op jit(solution)/shard_map/ppermute | solution.py:495
  21.8 18.6 %collective-permute-start.6 = (bf16[2,5,128,128]{3,2,1,0:T(8,128)(2,1)S(1)}, bf16[2,5,128,128]{3,2,1,0:T(8,128)(2,1)S(1)}, u32[]{:S(2)}, u32[]{:S(2)}) collective-permute-start(bf16[2,5,128,128]{3,2,1,0:T(8,128)(2,1)S(1)} %get-tuple-element.57), channel_id=1, source_target_pairs={{0,2},{2,0},{4,6},{6,4},{8,10},{10,8},{12,14},{14,12},{1,3},{3,1},... | collective-permute-start | bytes 983048 | tf_op jit(solution)/shard_map/ppermute | solution.py:495
  23.2 11.4 %collective-permute-start.8 = (bf16[512,128]{1,0:T(8,128)(2,1)S(1)}, bf16[512,128]{1,0:T(8,128)(2,1)S(1)}, u32[]{:S(2)}, u32[]{:S(2)}) collective-permute-start(bf16[512,128]{1,0:T(8,128)(2,1)S(1)} %join_blocks.3.refs_5_), channel_id=1, source_target_pairs={{0,8},{2,10},{4,12},{6,14},{8,0},{10,2},{12,4},{14,6},{1,9},{3,11}... | collective-permute-start | bytes 393224 | tf_op jit(solution)/shard_map/ppermute | solution.py:495
  25.9 12.3 %collective-permute-start.7 = (bf16[512,128]{1,0:T(8,128)(2,1)S(1)}, bf16[512,128]{1,0:T(8,128)(2,1)S(1)}, u32[]{:S(2)}, u32[]{:S(2)}) collective-permute-start(bf16[512,128]{1,0:T(8,128)(2,1)S(1)} %join_blocks.3.refs_5_), channel_id=1, source_target_pairs={{0,4},{2,6},{4,0},{6,2},{8,12},{10,14},{12,8},{14,10},{1,5},{3,7},... | collective-permute-start | bytes 393224 | tf_op jit(solution)/shard_map/ppermute | solution.py:495
  34.6 5.0 %collective-permute-start.9 = (bf16[512,128]{1,0:T(8,128)(2,1)S(1)}, bf16[512,128]{1,0:T(8,128)(2,1)S(1)}, u32[]{:S(2)}, u32[]{:S(2)}) collective-permute-start(bf16[512,128]{1,0:T(8,128)(2,1)S(1)} %collective-permute-done.8.refs_7_), channel_id=1, source_target_pairs={{0,4},{2,6},{4,0},{6,2},{8,12},{10,14},{12,8},{14,10},{1,5},{3,7},... | collective-permute-start | bytes 393224 | tf_op jit(solution)/shard_map/ppermute | solution.py:495
  34.7 12.9 %collective-permute-start.12 = (bf16[2,2,128,128]{3,2,1,0:T(8,128)(2,1)S(1)}, bf16[2,2,128,128]{3,2,1,0:T(8,128)(2,1)S(1)}, u32[]{:S(2)}, u32[]{:S(2)}) collective-permute-start(bf16[2,2,128,128]{3,2,1,0:T(8,128)(2,1)S(1)} %get-tuple-element.65), channel_id=1, source_target_pairs={{0,12},{2,14},{4,8},{6,10},{8,4},{10,6},{12,0},{14,2},{1,13},{3,15... | collective-permute-start | bytes 393224 | tf_op jit(solution)/shard_map/ppermute | solution.py:495
  37.1 14.8 %collective-permute-start.13 = (bf16[2,2,128,128]{3,2,1,0:T(8,128)(2,1)S(1)}, bf16[2,2,128,128]{3,2,1,0:T(8,128)(2,1)S(1)}, u32[]{:S(2)}, u32[]{:S(2)}) collective-permute-start(bf16[2,2,128,128]{3,2,1,0:T(8,128)(2,1)S(1)} %get-tuple-element.66), channel_id=1, source_target_pairs={{0,8},{2,10},{4,12},{6,14},{8,0},{10,2},{12,4},{14,6},{1,9},{3,11}... | collective-permute-start | bytes 393224 | tf_op jit(solution)/shard_map/ppermute | solution.py:495
  38.2 13.7 %collective-permute-start.14 = (bf16[2,2,128,128]{3,2,1,0:T(8,128)(2,1)S(1)}, bf16[2,2,128,128]{3,2,1,0:T(8,128)(2,1)S(1)}, u32[]{:S(2)}, u32[]{:S(2)}) collective-permute-start(bf16[2,2,128,128]{3,2,1,0:T(8,128)(2,1)S(1)} %get-tuple-element.67), channel_id=1, source_target_pairs={{0,4},{2,6},{4,0},{6,2},{8,12},{10,14},{12,8},{14,10},{1,5},{3,7},... | collective-permute-start | bytes 393224 | tf_op jit(solution)/shard_map/ppermute | solution.py:495
  39.7 18.4 %collective-permute-start.10 = (bf16[128,640]{1,0:T(8,128)(2,1)S(1)}, bf16[128,640]{1,0:T(8,128)(2,1)S(1)}, u32[]{:S(2)}, u32[]{:S(2)}) collective-permute-start(bf16[128,640]{1,0:T(8,128)(2,1)S(1)} %get-tuple-element.61), channel_id=1, source_target_pairs={{0,2},{2,0},{4,6},{6,4},{8,10},{10,8},{12,14},{14,12},{1,3},{3,1},... | collective-permute-start | bytes 491528 | tf_op jit(solution)/shard_map/ppermute | solution.py:495
  44.9 7.1 %collective-permute-start.16 = (bf16[2,2,128,128]{3,2,1,0:T(8,128)(2,1)S(1)}, bf16[2,2,128,128]{3,2,1,0:T(8,128)(2,1)S(1)}, u32[]{:S(2)}, u32[]{:S(2)}) collective-permute-start(bf16[2,2,128,128]{3,2,1,0:T(8,128)(2,1)S(1)} %get-tuple-element.70), channel_id=1, source_target_pairs={{0,12},{2,14},{4,8},{6,10},{8,4},{10,6},{12,0},{14,2},{1,13},{3,15... | collective-permute-start | bytes 393224 | tf_op jit(solution)/shard_map/ppermute | solution.py:495
  47.6 9.1 %collective-permute-start.17 = (bf16[2,2,128,128]{3,2,1,0:T(8,128)(2,1)S(1)}, bf16[2,2,128,128]{3,2,1,0:T(8,128)(2,1)S(1)}, u32[]{:S(2)}, u32[]{:S(2)}) collective-permute-start(bf16[2,2,128,128]{3,2,1,0:T(8,128)(2,1)S(1)} %get-tuple-element.71), channel_id=1, source_target_pairs={{0,8},{2,10},{4,12},{6,14},{8,0},{10,2},{12,4},{14,6},{1,9},{3,11}... | collective-permute-start | bytes 393224 | tf_op jit(solution)/shard_map/ppermute | solution.py:495
  51.9 6.1 %collective-permute-start.18 = (bf16[2,2,128,128]{3,2,1,0:T(8,128)(2,1)S(1)}, bf16[2,2,128,128]{3,2,1,0:T(8,128)(2,1)S(1)}, u32[]{:S(2)}, u32[]{:S(2)}) collective-permute-start(bf16[2,2,128,128]{3,2,1,0:T(8,128)(2,1)S(1)} %get-tuple-element.72), channel_id=1, source_target_pairs={{0,4},{2,6},{4,0},{6,2},{8,12},{10,14},{12,8},{14,10},{1,5},{3,7},... | collective-permute-start | bytes 393224 | tf_op jit(solution)/shard_map/ppermute | solution.py:495
  51.9 7.7 %collective-permute-start.15 = (bf16[2,128,128]{2,1,0:T(8,128)(2,1)S(1)}, bf16[2,128,128]{2,1,0:T(8,128)(2,1)S(1)}, u32[]{:S(2)}, u32[]{:S(2)}) collective-permute-start(bf16[2,128,128]{2,1,0:T(8,128)(2,1)S(1)} %fusion), channel_id=1, source_target_pairs={{0,2},{2,0},{4,6},{6,4},{8,10},{10,8},{12,14},{14,12},{1,3},{3,1},... | collective-permute-start | bytes 196616 | tf_op jit(solution)/shard_map/ppermute | solution.py:495
  52.0 6.7 %collective-permute-start.11 = (bf16[128,640]{1,0:T(8,128)(2,1)S(1)}, bf16[128,640]{1,0:T(8,128)(2,1)S(1)}, u32[]{:S(2)}, u32[]{:S(2)}) collective-permute-start(bf16[128,640]{1,0:T(8,128)(2,1)S(1)} %get-tuple-element.62), channel_id=1, source_target_pairs={{0,2},{2,0},{4,6},{6,4},{8,10},{10,8},{12,14},{14,12},{1,3},{3,1},... | collective-permute-start | bytes 491528 | tf_op jit(solution)/shard_map/ppermute | solution.py:495
  58.0 4.3 %collective-permute-start.19 = (bf16[2,128,128]{2,1,0:T(8,128)(2,1)S(1)}, bf16[2,128,128]{2,1,0:T(8,128)(2,1)S(1)}, u32[]{:S(2)}, u32[]{:S(2)}) collective-permute-start(bf16[2,128,128]{2,1,0:T(8,128)(2,1)S(1)} %fusion.1), channel_id=1, source_target_pairs={{0,2},{2,0},{4,6},{6,4},{8,10},{10,8},{12,14},{14,12},{1,3},{3,1},... | collective-permute-start | bytes 196616 | tf_op jit(solution)/shard_map/ppermute | solution.py:495

commit v15 on v14

--- a/solution.py
+++ b/solution.py
@@ -240,10 +240,12 @@
             if slot > 0:
                 ancestor = parent_of(ancestor, parents_s)
             slot_len = jnp.where(ancestor >= 0, lengths_s[jnp.maximum(ancestor, 0)], 0)
-            seen = u_id < slot_len
+            hidden = jnp.logical_and(t_id == 0, u_id >= slot_len)
             if slot == 0:
-                seen = jnp.logical_and(seen, u_id <= t_id)
-            bias_ref[i, slot * length : (slot + 1) * length, :] = jnp.where(seen, 0.0, -1e30)
+                hidden = jnp.logical_or(hidden, jnp.logical_and(t_id > 0, t_id == u_id))
+            bias_ref[i, slot * length : (slot + 1) * length, :] = jnp.where(
+                hidden, 1.0, 0.0
+            ).astype(jnp.bfloat16)
 
 
 def prepare(parents, lengths, terms, length, log_rate):
@@ -253,7 +255,7 @@
     return pl.pallas_call(
         functools.partial(prepare_kernel, log_rate, DEPTH),
         out_shape=(
-            jax.ShapeDtypeStruct((segs, DEPTH * length, length), jnp.float32),
+            jax.ShapeDtypeStruct((segs, DEPTH * length, length), jnp.bfloat16),
             jax.ShapeDtypeStruct((segs, 3, length, HD), jnp.float32),
             jax.ShapeDtypeStruct((segs, 2, count, HD), jnp.float32),
         ),
@@ -319,12 +321,12 @@
     )(columns, weights, *terms)
 
 
-def attend_kernel(depth, segs, steps, group_size, *refs):
+def attend_kernel(depth, segs, steps, group_size, folded, *refs):
     parents_s, adv_ref, bias_ref = refs[:3]
     query_refs, kv_refs = refs[3 : 3 + segs], refs[3 + segs : 3 + segs + steps]
     kv_scr, p_scr, ds_scr, acc_scr = refs[-4:]
     refs = refs[3 + segs + steps : -4]
-    dkv_refs, dq_refs = refs[-steps:], refs[-steps - segs : -steps]
+    dq_refs, dkv_refs = refs[:segs], refs[segs:]
 
     length = query_refs[0].shape[2]
     own = lax.axis_index("seg")
@@ -335,6 +337,10 @@
             kv_scr[source, plane] = kv_refs[step][first : first + length, :]
     acc_scr[...] = jnp.zeros_like(acc_scr)
 
+    query_id = lax.broadcasted_iota(jnp.int32, (length, length), 0)
+    key_id = lax.broadcasted_iota(jnp.int32, (length, length), 1)
+    hides = jnp.logical_or(key_id == 0, key_id > query_id)
+    hides = jnp.where(hides, -1e30, 0.0).astype(jnp.bfloat16)
     scale = HD**-0.5
     contract_last = (((1,), (1,)), ((), ()))
     contract_first = (((0,), (0,)), ((), ()))
@@ -360,23 +366,25 @@
         q_all = jnp.concatenate(q_list, axis=0)
         do_all = jnp.concatenate(do_list, axis=0)
         all_scores = lax.dot_general(
-            k_all, q_all, contract_last, preferred_element_type=jnp.float32
+            jnp.concatenate([k_all, bias_ref[i]], axis=1),
+            jnp.concatenate([q_all, jnp.concatenate([hides] * group_size, axis=0)], axis=1),
+            contract_last,
+            preferred_element_type=jnp.float32,
         )
         all_dprob = lax.dot_general(
             v_all, do_all, contract_last, preferred_element_type=jnp.float32
         )
         for j in range(group_size):
             columns = slice(j * length, (j + 1) * length)
-            scores = all_scores[:, columns] * (scale * LOG2E) + bias_ref[i]
+            scores = all_scores[:, columns]
+            dprob = all_dprob[:, columns]
             top = jnp.max(scores, axis=0, keepdims=True)
-            unnorm = jnp.exp2(scores - top)
-            prob = unnorm * (1.0 / jnp.sum(unnorm, axis=0, keepdims=True))
-            prob_low = prob.astype(jnp.bfloat16)
-            dprob = all_dprob[:, columns]
-            row_dot = jnp.sum(prob_low.astype(jnp.float32) * dprob, axis=0, keepdims=True)
-            dscore = (prob * (dprob - row_dot)).astype(jnp.bfloat16)
-            p_scr[:, columns] = prob_low
-            ds_scr[:, columns] = dscore
+            unnorm = jnp.exp2((scores - top) * (scale * LOG2E))
+            inverse = 1.0 / jnp.sum(unnorm, axis=0, keepdims=True)
+            row_dot = jnp.sum(unnorm * dprob, axis=0, keepdims=True) * inverse
+            prob = unnorm * inverse
+            p_scr[:, columns] = prob.astype(jnp.bfloat16)
+            ds_scr[:, columns] = (prob * (dprob - row_dot)).astype(jnp.bfloat16)
         dscore_all = ds_scr[...]
         dq_t = lax.dot_general(
             k_all, dscore_all, contract_first, preferred_element_type=jnp.float32
@@ -391,11 +399,14 @@
             acc_scr[s, 0] += dk_all[rows]
             acc_scr[s, 1] += dv_all[rows]
     for step in range(steps):
+        ref, first = dkv_refs[step % len(dkv_refs)], 0
+        if folded:
+            ref, first = dkv_refs[(0, 2, 1, 2)[step]], (0, 0, 0, segs)[step]
         for i in range(segs):
-            dkv_refs[step][i] = acc_scr[step * segs + i].astype(jnp.bfloat16)
-
-
-def attend(parents, advantages, bias, query_list, kv_list):
+            ref[first + i] = acc_scr[step * segs + i].astype(jnp.bfloat16)
+
+
+def attend(parents, advantages, bias, query_list, kv_list, folded=False):
     segs, length = advantages.shape[:2]
     steps = len(kv_list)
     sources = steps * segs
@@ -405,9 +416,12 @@
     smem = pl.BlockSpec(memory_space=pltpu.SMEM)
     vmem = pl.BlockSpec(memory_space=pltpu.VMEM)
     out_shape = [jax.ShapeDtypeStruct((length, width), jnp.bfloat16)] * segs
-    out_shape += [jax.ShapeDtypeStruct((segs, 2, length, HD), jnp.bfloat16)] * steps
+    counts = [1, 1, 2] if folded else [1] * steps
+    out_shape += [
+        jax.ShapeDtypeStruct((many * segs, 2, length, HD), jnp.bfloat16) for many in counts
+    ]
     outs = pl.pallas_call(
-        functools.partial(attend_kernel, DEPTH, segs, steps, group_size),
+        functools.partial(attend_kernel, DEPTH, segs, steps, group_size, folded),
         out_shape=out_shape,
         in_specs=[smem] + [vmem] * (2 + segs + steps),
         out_specs=[vmem] * len(out_shape),
@@ -457,16 +471,15 @@
     )(*own_list, *other_list)
 
 
-def join_keys_kernel(chunks, *refs):
+def join_keys_kernel(chunks, ends, *refs):
     part = lax.rem(lax.axis_index("seg"), 2)
     other_refs, sum_refs = refs[:chunks], refs[chunks:-2]
-    many = len(sum_refs) // chunks
     dk_ref, dv_ref = refs[-2:]
     for chunk in range(chunks):
         here = pl.ds(pl.multiple_of((part * chunks + chunk) * HD, HD), HD)
         there = pl.ds(pl.multiple_of(((1 - part) * chunks + chunk) * HD, HD), HD)
         for plane, out_ref in enumerate((dk_ref, dv_ref)):
-            blocks = [ref[0, plane] for ref in sum_refs[chunk * many : (chunk + 1) * many]]
+            blocks = [ref[0, plane] for ref in sum_refs[ends[chunk] : ends[chunk + 1]]]
             total = sum(block.astype(jnp.float32) for block in blocks)
             out_ref[:, here] = total.astype(jnp.bfloat16)
             out_ref[:, there] = other_refs[chunk][plane]
@@ -477,9 +490,10 @@
     length = others[0].shape[1]
     vmem = pl.BlockSpec(memory_space=pltpu.VMEM)
     flat = [block for blocks in summands for block in blocks]
+    ends = [sum(len(blocks) for blocks in summands[:chunk]) for chunk in range(chunks + 1)]
     out = jax.ShapeDtypeStruct((length, 2 * chunks * HD), jnp.bfloat16)
     return pl.pallas_call(
-        functools.partial(join_keys_kernel, chunks),
+        functools.partial(join_keys_kernel, chunks, ends),
         out_shape=(out, out),
         in_specs=[vmem] * (chunks + len(flat)),
         out_specs=(vmem, vmem),
@@ -524,18 +538,20 @@
     dq_own, dq_back, dkv_list = [], [], []
     for chunk in range(chunks):
         query_list = [kept_q[chunk], taken_q[chunk]]
-        dq, dkv = attend(parents, advantages, bias, query_list, chains[chunk])
+        dq, dkv = attend(parents, advantages, bias, query_list, chains[chunk], folded=chunk == 0)
         if chunk == 0:
-            three = permute(after(two, dq[0]), meet[1])
+            three = permute(after(two, one, dq[0]), meet[1])
             chains.append([block, one, two, three])
         dq_own.append(dq[0])
         dq_back.append(dq[1])
         dkv_list.append(dkv)
 
-    summands = []
-    for dkv in dkv_list:
-        arrived = [permute(dkv[bits], meet[bits]) for bits in steps[::-1]]
-        summands.append([after(dkv[0], dq_own[-1])] + arrived)
+    mine, further, folded = dkv_list[0]
+    met = after(permute(after(folded, chains[1][3]), meet[1]), dq_own[-1])
+    further = (further.astype(jnp.float32) + met[2:].astype(jnp.float32)).astype(jnp.bfloat16)
+    summands = [[mine, met, permute(further, meet[2])]]
+    last = lax.optimization_barrier((*dkv_list[1], further))[:-1]
+    summands.append([last[0]] + [permute(last[bits], meet[bits]) for bits in steps[::-1]])
     dq_back = [permute(block, swap) for block in dq_back]
     others = []
     for blocks in summands:

time: 63.4 us -> 70.1 us (1.11)
  waiting for transfers between devices: 20.5 us -> 27.1 us
    ppermute x20 -> x19, waiting for transfers between devices: 20.5 us -> 27.1 us  [permute(): return lax.ppermute(array, 'seg', pairs)]
    ppermute x20 -> x19, starting transfers between devices: 24.3 us -> 24.2 us  [permute(): return lax.ppermute(array, 'seg', pairs)]
  transfers between devices with their start and end apart: 20 -> 19, of which waited for: 10 -> 10; matrix products, arithmetic and copies ran while one was open for 0% -> 0% of each run, Pallas kernels for 19% -> 17%
where the time goes in v15:
time: 70.1 us; the launch traced here: 69.8 us
  waiting for transfers between devices  27.1 us (39%)
  starting transfers between devices  24.2 us (35%)
  Pallas kernels  14.7 us (21%)
  local copies, waits for them, and re-layouts  3.05 us (4%)
  between operations  0.74 us (1%)
    ppermute x19, waiting for transfers between devices, permute(): return lax.ppermute(array, 'seg', pairs)  27.1 us
    ppermute x19, starting transfers between devices, permute(): return lax.ppermute(array, 'seg', pairs)  24.2 us
    pallas_call x2, Pallas kernels, attend(): pl.pallas_call(functools.partial(attend_kernel, DEPTH, segs, steps, group...  8.96 us
    unnamed x12, local copies, waits for them, and re-layouts  3.05 us
    pallas_call x1, Pallas kernels, pack(): pl.pallas_call(functools.partial(pack_kernel, log_rate, parts), out_shape...  1.81 us
  transfers between devices with their start and end apart: 19, of which 10 were waited for; matrix products, arithmetic and copies ran while one was open for 0% of the time, Pallas kernels for 17%

profile of v15, /device:TPU:0, one launch (start us, length us, event | category | flops | bytes accessed | tf_op | source)
XLA Modules:
  0.0 69.8 jit_solution(17790157852885146962)
XLA Ops:
  0.6 1.8 %pack_keys_values.1 = (bf16[272,128]{1,0:T(8,128)(2,1)}, bf16[256,128]{1,0:T(8,128)(2,1)}, bf16[272,128]{1,0:T(8,128)(2,1)}, bf16[256,128]{1,0:T(8,128)(2,1)}) custom-call(s32[8]{0:T(128)} %lengths_s.1, bf16[128,512]{1,0:T(8,128)(2,1)} %k_ref.1, bf16[128,512]{1,0:T(8,128)(2,1)} %v_ref.1, f32[1,128]{1,0:T(1,128)} %bitcast.9, f32[1,128]{1,0:T(1,128)} %bitcast.10, ...), custom_call_target="tpu_custom_call" | custom-call | flops 12800 | bytes 524288 | tf_op jit(solution)/shard_map/pack_keys_values/pallas_call | solution.py:104
  2.4 2.9 %collective-permute-start = (bf16[272,128]{1,0:T(8,128)(2,1)}, bf16[272,128]{1,0:T(8,128)(2,1)S(1)}, u32[]{:S(2)}, u32[]{:S(2)}) collective-permute-start(bf16[272,128]{1,0:T(8,128)(2,1)} %get-tuple-element.44), channel_id=1, source_target_pairs={{0,2},{2,0},{4,6},{6,4},{8,10},{10,8},{12,14},{14,12},{1,3},{3,1},... | collective-permute-start | bytes 208904 | tf_op jit(solution)/shard_map/ppermute | solution.py:509
  5.4 0.1 collective-permute-start.3
  5.5 0.0 copy-start
  5.5 1.1 %copy-done = bf16[128,2560]{1,0:T(8,128)(2,1)S(1)} copy-done((bf16[128,2560]{1,0:T(8,128)(2,1)S(1)}, bf16[128,2560]{1,0:T(8,128)(2,1)}, u32[]{:S(2)}) %copy-start) | copy-done | bytes 655384
  6.5 0.0 copy-start.1
  6.5 1.1 %copy-done.1 = bf16[128,2560]{1,0:T(8,128)(2,1)S(1)} copy-done((bf16[128,2560]{1,0:T(8,128)(2,1)S(1)}, bf16[128,2560]{1,0:T(8,128)(2,1)}, u32[]{:S(2)}) %copy-start.1) | copy-done | bytes 655384
  7.6 0.0 copy-start.3
  7.6 0.2 pack_queries.1
  7.9 2.0 %collective-permute-done.3.other_ref = bf16[256,128]{1,0:T(8,128)(2,1)S(1)} collective-permute-done((bf16[256,128]{1,0:T(8,128)(2,1)}, bf16[256,128]{1,0:T(8,128)(2,1)S(1)}, u32[]{:S(2)}, u32[]{:S(2)}) %collective-permute-start.3) | collective-permute-done | bytes 65568 | tf_op jit(solution)/shard_map/ppermute | solution.py:509
  9.9 0.0 copy-done.3
  9.9 0.0 copy-start.2
  9.9 0.0 collective-permute-done.refs_1_.other_ref
  9.9 0.9 %copy-done.2 = bf16[272,128]{1,0:T(8,128)(2,1)S(1)} copy-done((bf16[272,128]{1,0:T(8,128)(2,1)S(1)}, bf16[272,128]{1,0:T(8,128)(2,1)}, u32[]{:S(2)}) %copy-start.2) | copy-done | bytes 69656
  10.8 0.0 copy-start.4
  10.8 0.0 copy-start.5
  10.8 1.1 %collective-permute-start.5 = (bf16[2,5,128,128]{3,2,1,0:T(8,128)(2,1)S(1)}, bf16[2,5,128,128]{3,2,1,0:T(8,128)(2,1)S(1)}, u32[]{:S(2)}, u32[]{:S(2)}) collective-permute-start(bf16[2,5,128,128]{3,2,1,0:T(8,128)(2,1)S(1)} %get-tuple-element.57), channel_id=1, source_target_pairs={{0,2},{2,0},{4,6},{6,4},{8,10},{10,8},{12,14},{14,12},{1,3},{3,1},... | collective-permute-start | bytes 983048 | tf_op jit(solution)/shard_map/ppermute | solution.py:509
  11.9 1.6 %collective-permute-start.1 = (bf16[544,128]{1,0:T(8,128)(2,1)S(1)}, bf16[544,128]{1,0:T(8,128)(2,1)S(1)}, u32[]{:S(2)}, u32[]{:S(2)}) collective-permute-start(bf16[544,128]{1,0:T(8,128)(2,1)S(1)} %join_blocks.2.refs_0_.refs_5_), channel_id=1, source_target_pairs={{0,4},{2,6},{4,0},{6,2},{8,12},{10,14},{12,8},{14,10},{1,5},{3,7},... | collective-permute-start | bytes 417800 | tf_op jit(solution)/shard_map/ppermute | solution.py:509
  13.5 2.6 %collective-permute-start.2 = (bf16[544,128]{1,0:T(8,128)(2,1)S(1)}, bf16[544,128]{1,0:T(8,128)(2,1)S(1)}, u32[]{:S(2)}, u32[]{:S(2)}) collective-permute-start(bf16[544,128]{1,0:T(8,128)(2,1)S(1)} %join_blocks.2.refs_0_.refs_5_), channel_id=1, source_target_pairs={{0,8},{2,10},{4,12},{6,14},{8,0},{10,2},{12,4},{14,6},{1,9},{3,11}... | collective-permute-start | bytes 417800 | tf_op jit(solution)/shard_map/ppermute | solution.py:509
  16.1 0.0 copy-done.4
  16.1 0.0 copy-done.5
  16.1 1.3 %prepare.1 = (bf16[2,640,128]{2,1,0:T(8,128)(2,1)S(1)}, f32[2,3,128,128]{3,2,1,0:T(8,128)S(1)}, f32[2,2,8,128]{3,2,1,0:T(8,128)S(1)}) custom-call(s32[8]{0:T(128)S(1)} %copy-done.5, s32[8]{0:T(128)S(1)} %copy-done.4, bf16[272,128]{1,0:T(8,128)(2,1)S(1)} %copy-done.2, bf16[272,128]{1,0:T(8,128)(2,1)S(1)} %collective-permute-done.refs_1_.other_ref), custom_call_target="tpu_custom_call" | custom-call | flops 3276800 | bytes 655360 | tf_op jit(solution)/shard_map/prepare/pallas_call | solution.py:255
  17.4 1.4 %collective-permute-done.1.refs_1_.refs_6_ = bf16[544,128]{1,0:T(8,128)(2,1)S(1)} collective-permute-done((bf16[544,128]{1,0:T(8,128)(2,1)S(1)}, bf16[544,128]{1,0:T(8,128)(2,1)S(1)}, u32[]{:S(2)}, u32[]{:S(2)}) %collective-permute-start.1) | collective-permute-done | bytes 139296 | tf_op jit(solution)/shard_map/ppermute | solution.py:509
  18.8 2.7 %collective-permute-done.2.refs_2_.refs_7_ = bf16[544,128]{1,0:T(8,128)(2,1)S(1)} collective-permute-done((bf16[544,128]{1,0:T(8,128)(2,1)S(1)}, bf16[544,128]{1,0:T(8,128)(2,1)S(1)}, u32[]{:S(2)}, u32[]{:S(2)}) %collective-permute-start.2) | collective-permute-done | bytes 139296 | tf_op jit(solution)/shard_map/ppermute | solution.py:509
  21.5 0.4 collective-permute-start.4
  21.8 1.7 %collective-permute-start.7 = (bf16[512,128]{1,0:T(8,128)(2,1)S(1)}, bf16[512,128]{1,0:T(8,128)(2,1)S(1)}, u32[]{:S(2)}, u32[]{:S(2)}) collective-permute-start(bf16[512,128]{1,0:T(8,128)(2,1)S(1)} %join_blocks.3.refs_5_), channel_id=1, source_target_pairs={{0,4},{2,6},{4,0},{6,2},{8,12},{10,14},{12,8},{14,10},{1,5},{3,7},... | collective-permute-start | bytes 393224 | tf_op jit(solution)/shard_map/ppermute | solution.py:509
  23.5 1.3 %collective-permute-start.8 = (bf16[512,128]{1,0:T(8,128)(2,1)S(1)}, bf16[512,128]{1,0:T(8,128)(2,1)S(1)}, u32[]{:S(2)}, u32[]{:S(2)}) collective-permute-start(bf16[512,128]{1,0:T(8,128)(2,1)S(1)} %join_blocks.3.refs_5_), channel_id=1, source_target_pairs={{0,8},{2,10},{4,12},{6,14},{8,0},{10,2},{12,4},{14,6},{1,9},{3,11}... | collective-permute-start | bytes 393224 | tf_op jit(solution)/shard_map/ppermute | solution.py:509
  24.8 1.7 %collective-permute-done.4.refs_3_.refs_8_ = bf16[544,128]{1,0:T(8,128)(2,1)S(1)} collective-permute-done((bf16[544,128]{1,0:T(8,128)(2,1)S(1)}, bf16[544,128]{1,0:T(8,128)(2,1)S(1)}, u32[]{:S(2)}, u32[]{:S(2)}) %collective-permute-start.4) | collective-permute-done | bytes 139296 | tf_op jit(solution)/shard_map/ppermute | solution.py:509
  26.5 0.7 advantages.1
  27.2 0.0 collective-permute-done.5.refs_4_
  27.2 1.4 %collective-permute-start.6 = (bf16[2,5,128,128]{3,2,1,0:T(8,128)(2,1)S(1)}, bf16[2,5,128,128]{3,2,1,0:T(8,128)(2,1)S(1)}, u32[]{:S(2)}, u32[]{:S(2)}) collective-permute-start(bf16[2,5,128,128]{3,2,1,0:T(8,128)(2,1)S(1)} %get-tuple-element.60), channel_id=1, source_target_pairs={{0,2},{2,0},{4,6},{6,4},{8,10},{10,8},{12,14},{14,12},{1,3},{3,1},... | collective-permute-start | bytes 983048 | tf_op jit(solution)/shard_map/ppermute | solution.py:509
  28.6 4.5 %tree_attention_backward.2 = (bf16[128,640]{1,0:T(8,128)(2,1)S(1)}, bf16[128,640]{1,0:T(8,128)(2,1)S(1)}, bf16[2,2,128,128]{3,2,1,0:T(8,128)(2,1)S(1)}, bf16[2,2...) custom-call(s32[8]{0:T(128)S(1)} %copy-done.5, f32[2,128,128]{2,1,0:T(8,128)S(1)} %get-tuple-element.55.refs_1_, ...), custom_call_target="tpu_custom_call" | custom-call | flops 1048576000 | bytes 8388608 | tf_op jit(solution)/shard_map/tree_attention_backward/pallas_call | solution.py:423
  33.1 0.0 collective-permute-done.7.refs_6_
  33.1 0.0 collective-permute-done.8.refs_7_
  33.1 1.5 %collective-permute-start.9 = (bf16[512,128]{1,0:T(8,128)(2,1)S(1)}, bf16[512,128]{1,0:T(8,128)(2,1)S(1)}, u32[]{:S(2)}, u32[]{:S(2)}) collective-permute-start(bf16[512,128]{1,0:T(8,128)(2,1)S(1)} %collective-permute-done.8.refs_7_), channel_id=1, source_target_pairs={{0,4},{2,6},{4,0},{6,2},{8,12},{10,14},{12,8},{14,10},{1,5},{3,7},... | collective-permute-start | bytes 393224 | tf_op jit(solution)/shard_map/ppermute | solution.py:509
  34.6 4.8 %collective-permute-done.9.refs_8_ = bf16[512,128]{1,0:T(8,128)(2,1)S(1)} collective-permute-done((bf16[512,128]{1,0:T(8,128)(2,1)S(1)}, bf16[512,128]{1,0:T(8,128)(2,1)S(1)}, u32[]{:S(2)}, u32[]{:S(2)}) %collective-permute-start.9) | collective-permute-done | bytes 131104 | tf_op jit(solution)/shard_map/ppermute | solution.py:509
  39.4 1.3 %collective-permute-start.12 = (bf16[4,2,128,128]{3,2,1,0:T(8,128)(2,1)S(1)}, bf16[4,2,128,128]{3,2,1,0:T(8,128)(2,1)S(1)}, u32[]{:S(2)}, u32[]{:S(2)}) collective-permute-start(bf16[4,2,128,128]{3,2,1,0:T(8,128)(2,1)S(1)} %get-tuple-element.68), channel_id=1, source_target_pairs={{0,4},{2,6},{4,0},{6,2},{8,12},{10,14},{12,8},{14,10},{1,5},{3,7},... | collective-permute-start | bytes 786440 | tf_op jit(solution)/shard_map/ppermute | solution.py:509
  40.7 0.0 collective-permute-done.6.refs_4_
  40.7 4.5 %tree_attention_backward.3 = (bf16[128,640]{1,0:T(8,128)(2,1)S(1)}, bf16[128,640]{1,0:T(8,128)(2,1)S(1)}, bf16[2,2,128,128]{3,2,1,0:T(8,128)(2,1)S(1)}, bf16[2,2...) custom-call(s32[8]{0:T(128)S(1)} %copy-done.5, ...), custom_call_target="tpu_custom_call" | custom-call | flops 1048576000 | bytes 8388608 | tf_op jit(solution)/shard_map/tree_attention_backward/pallas_call | solution.py:423
  45.2 6.2 %collective-permute-done.12.refs_3_ = bf16[4,2,128,128]{3,2,1,0:T(8,128)(2,1)S(1)} collective-permute-done((bf16[4,2,128,128]{3,2,1,0:T(8,128)(2,1)S(1)}, bf16[4,2,128,128]{3,2,1,0:T(8,128)(2,1)S(1)}, u32[]{:S(2)}, u32[]{:S(2)}) %collective-permute-start.12) | collective-permute-done | bytes 262176 | tf_op jit(solution)/shard_map/ppermute | solution.py:509
  51.5 2.0 %collective-permute-start.15 = (bf16[2,2,128,128]{3,2,1,0:T(8,128)(2,1)S(1)}, bf16[2,2,128,128]{3,2,1,0:T(8,128)(2,1)S(1)}, u32[]{:S(2)}, u32[]{:S(2)}) collective-permute-start(bf16[2,2,128,128]{3,2,1,0:T(8,128)(2,1)S(1)} %get-tuple-element.76), channel_id=1, source_target_pairs={{0,12},{2,14},{4,8},{6,10},{8,4},{10,6},{12,0},{14,2},{1,13},{3,15... | collective-permute-start | bytes 393224 | tf_op jit(solution)/shard_map/ppermute | solution.py:509
  53.4 0.0 collective-permute-start.16
  53.5 2.5 %collective-permute-start.17 = (bf16[2,2,128,128]{3,2,1,0:T(8,128)(2,1)S(1)}, bf16[2,2,128,128]{3,2,1,0:T(8,128)(2,1)S(1)}, u32[]{:S(2)}, u32[]{:S(2)}) collective-permute-start(bf16[2,2,128,128]{3,2,1,0:T(8,128)(2,1)S(1)} %get-tuple-element.78), channel_id=1, source_target_pairs={{0,4},{2,6},{4,0},{6,2},{8,12},{10,14},{12,8},{14,10},{1,5},{3,7},... | collective-permute-start | bytes 393224 | tf_op jit(solution)/shard_map/ppermute | solution.py:509
  55.9 0.8 %collective-permute-start.10 = (bf16[128,640]{1,0:T(8,128)(2,1)S(1)}, bf16[128,640]{1,0:T(8,128)(2,1)S(1)}, u32[]{:S(2)}, u32[]{:S(2)}) collective-permute-start(bf16[128,640]{1,0:T(8,128)(2,1)S(1)} %get-tuple-element.64), channel_id=1, source_target_pairs={{0,2},{2,0},{4,6},{6,4},{8,10},{10,8},{12,14},{14,12},{1,3},{3,1},... | collective-permute-start | bytes 491528 | tf_op jit(solution)/shard_map/ppermute | solution.py:509
  56.7 1.3 %collective-permute-start.11 = (bf16[128,640]{1,0:T(8,128)(2,1)S(1)}, bf16[128,640]{1,0:T(8,128)(2,1)S(1)}, u32[]{:S(2)}, u32[]{:S(2)}) collective-permute-start(bf16[128,640]{1,0:T(8,128)(2,1)S(1)} %get-tuple-element.65), channel_id=1, source_target_pairs={{0,2},{2,0},{4,6},{6,4},{8,10},{10,8},{12,14},{14,12},{1,3},{3,1},... | collective-permute-start | bytes 491528 | tf_op jit(solution)/shard_map/ppermute | solution.py:509
  57.9 0.5 collective-permute-done.15.refs_6_
  58.4 0.0 collective-permute-start.13
  58.4 2.7 %collective-permute-done.16.refs_7_ = bf16[2,2,128,128]{3,2,1,0:T(8,128)(2,1)S(1)} collective-permute-done((bf16[2,2,128,128]{3,2,1,0:T(8,128)(2,1)S(1)}, bf16[2,2,128,128]{3,2,1,0:T(8,128)(2,1)S(1)}, u32[]{:S(2)}, u32[]{:S(2)}) %collective-permute-start.16) | collective-permute-done | bytes 131104 | tf_op jit(solution)/shard_map/ppermute | solution.py:509
  61.1 0.0 collective-permute-done.17.refs_8_
  61.1 0.8 %collective-permute-start.18 = (bf16[2,128,128]{2,1,0:T(8,128)(2,1)S(1)}, bf16[2,128,128]{2,1,0:T(8,128)(2,1)S(1)}, u32[]{:S(2)}, u32[]{:S(2)}) collective-permute-start(bf16[2,128,128]{2,1,0:T(8,128)(2,1)S(1)} %fusion.1), channel_id=1, source_target_pairs={{0,2},{2,0},{4,6},{6,4},{8,10},{10,8},{12,14},{14,12},{1,3},{3,1},... | collective-permute-start | bytes 196616 | tf_op jit(solution)/shard_map/ppermute | solution.py:509
  62.0 2.7 %collective-permute-done.13.refs_4_ = bf16[2,2,128,128]{3,2,1,0:T(8,128)(2,1)S(1)} collective-permute-done((bf16[2,2,128,128]{3,2,1,0:T(8,128)(2,1)S(1)}, bf16[2,2,128,128]{3,2,1,0:T(8,128)(2,1)S(1)}, u32[]{:S(2)}, u32[]{:S(2)}) %collective-permute-start.13) | collective-permute-done | bytes 131104 | tf_op jit(solution)/shard_map/ppermute | solution.py:509
  64.7 1.1 %collective-permute-start.14 = (bf16[2,128,128]{2,1,0:T(8,128)(2,1)S(1)}, bf16[2,128,128]{2,1,0:T(8,128)(2,1)S(1)}, u32[]{:S(2)}, u32[]{:S(2)}) collective-permute-start(bf16[2,128,128]{2,1,0:T(8,128)(2,1)S(1)} %fusion), channel_id=1, source_target_pairs={{0,2},{2,0},{4,6},{6,4},{8,10},{10,8},{12,14},{14,12},{1,3},{3,1},... | collective-permute-start | bytes 196616 | tf_op jit(solution)/shard_map/ppermute | solution.py:509
  65.8 0.0 collective-permute-done.10.refs_2_
  65.8 0.0 collective-permute-done.11.refs_3_
  65.8 0.9 %join_queries.1 = bf16[128,2560]{1,0:T(8,128)(2,1)} custom-call(bf16[128,640]{1,0:T(8,128)(2,1)S(1)} %get-tuple-element.58.refs_0_, bf16[128,640]{1,0:T(8,128)(2,1)S(1)} %get-tuple-element.63.refs_1_, bf16[128,640]{1,0:T(8,128)(2,1)S(1)} %collective-permute-done.10.refs_2_, bf16[128,640]{1,0:T(8,128)(2,1)S(1)} %collective-permute-done.11.refs_3_), custom_call_target="tpu_custom_call" | custom-call | bytes 1310720 | tf_op jit(solution)/shard_map/join_queries/pallas_call | solution.py:461
  66.7 0.0 collective-permute-done.18.refs_1_
  66.8 2.3 %collective-permute-done.14.refs_0_ = bf16[2,128,128]{2,1,0:T(8,128)(2,1)S(1)} collective-permute-done((bf16[2,128,128]{2,1,0:T(8,128)(2,1)S(1)}, bf16[2,128,128]{2,1,0:T(8,128)(2,1)S(1)}, u32[]{:S(2)}, u32[]{:S(2)}) %collective-permute-start.14) | collective-permute-done | bytes 65568 | tf_op jit(solution)/shard_map/ppermute | solution.py:509
  69.1 0.8 %join_keys.1 = (bf16[128,512]{1,0:T(8,128)(2,1)}, bf16[128,512]{1,0:T(8,128)(2,1)}) custom-call(bf16[2,128,128]{2,1,0:T(8,128)(2,1)S(1)} %collective-permute-done.14.refs_0_, bf16[2,128,128]{2,1,0:T(8,128)(2,1)S(1)} %collective-permute-done.18.refs_1_, bf16[2,2,128,128]{3,2,1,0:T(8,128)(2,1)S(1)} %get-tuple-element.66.refs_2_, ...), custom_call_target="tpu_custom_call" | custom-call | bytes 524288 | tf_op jit(solution)/shard_map/join_keys/pallas_call | solution.py:495
  (5 shorter events, 0.1 us)
Async XLA Ops:
  2.4 7.4 %collective-permute-start = (bf16[272,128]{1,0:T(8,128)(2,1)}, bf16[272,128]{1,0:T(8,128)(2,1)S(1)}, u32[]{:S(2)}, u32[]{:S(2)}) collective-permute-start(bf16[272,128]{1,0:T(8,128)(2,1)} %get-tuple-element.44), channel_id=1, source_target_pairs={{0,2},{2,0},{4,6},{6,4},{8,10},{10,8},{12,14},{14,12},{1,3},{3,1},... | collective-permute-start | bytes 208904 | tf_op jit(solution)/shard_map/ppermute | solution.py:509
  5.4 4.5 %collective-permute-start.3 = (bf16[256,128]{1,0:T(8,128)(2,1)}, bf16[256,128]{1,0:T(8,128)(2,1)S(1)}, u32[]{:S(2)}, u32[]{:S(2)}) collective-permute-start(bf16[256,128]{1,0:T(8,128)(2,1)} %get-tuple-element.52), channel_id=1, source_target_pairs={{0,2},{2,0},{4,6},{6,4},{8,10},{10,8},{12,14},{14,12},{1,3},{3,1},... | collective-permute-start | bytes 196616 | tf_op jit(solution)/shard_map/ppermute | solution.py:509
  5.5 1.1 %copy-start = (bf16[128,2560]{1,0:T(8,128)(2,1)S(1)}, bf16[128,2560]{1,0:T(8,128)(2,1)}, u32[]{:S(2)}) copy-start(bf16[128,2560]{1,0:T(8,128)(2,1)} %q_ref) | copy-start | bytes 1966084
  6.5 1.1 %copy-start.1 = (bf16[128,2560]{1,0:T(8,128)(2,1)S(1)}, bf16[128,2560]{1,0:T(8,128)(2,1)}, u32[]{:S(2)}) copy-start(bf16[128,2560]{1,0:T(8,128)(2,1)} %dir_ref.1) | copy-start | bytes 1966084
  7.6 2.2 %copy-start.3 = (bf16[256,128]{1,0:T(8,128)(2,1)S(1)}, bf16[256,128]{1,0:T(8,128)(2,1)}, u32[]{:S(2)}) copy-start(bf16[256,128]{1,0:T(8,128)(2,1)} %get-tuple-element.51.mine_ref) | copy-start | bytes 196612
  9.9 0.9 %copy-start.2 = (bf16[272,128]{1,0:T(8,128)(2,1)S(1)}, bf16[272,128]{1,0:T(8,128)(2,1)}, u32[]{:S(2)}) copy-start(bf16[272,128]{1,0:T(8,128)(2,1)} %get-tuple-element.43.refs_0_.mine_ref) | copy-start | bytes 208900
  10.8 5.3 %copy-start.4 = (s32[8]{0:T(128)S(1)}, s32[8]{0:T(128)}, u32[]{:S(2)}) copy-start(s32[8]{0:T(128)} %lengths_s.1) | copy-start | bytes 100
  10.8 5.3 %copy-start.5 = (s32[8]{0:T(128)S(1)}, s32[8]{0:T(128)}, u32[]{:S(2)}) copy-start(s32[8]{0:T(128)} %refs_0_.3) | copy-start | bytes 100
  10.8 16.4 %collective-permute-start.5 = (bf16[2,5,128,128]{3,2,1,0:T(8,128)(2,1)S(1)}, bf16[2,5,128,128]{3,2,1,0:T(8,128)(2,1)S(1)}, u32[]{:S(2)}, u32[]{:S(2)}) collective-permute-start(bf16[2,5,128,128]{3,2,1,0:T(8,128)(2,1)S(1)} %get-tuple-element.57), channel_id=1, source_target_pairs={{0,2},{2,0},{4,6},{6,4},{8,10},{10,8},{12,14},{14,12},{1,3},{3,1},... | collective-permute-start | bytes 983048 | tf_op jit(solution)/shard_map/ppermute | solution.py:509
  11.9 6.9 %collective-permute-start.1 = (bf16[544,128]{1,0:T(8,128)(2,1)S(1)}, bf16[544,128]{1,0:T(8,128)(2,1)S(1)}, u32[]{:S(2)}, u32[]{:S(2)}) collective-permute-start(bf16[544,128]{1,0:T(8,128)(2,1)S(1)} %join_blocks.2.refs_0_.refs_5_), channel_id=1, source_target_pairs={{0,4},{2,6},{4,0},{6,2},{8,12},{10,14},{12,8},{14,10},{1,5},{3,7},... | collective-permute-start | bytes 417800 | tf_op jit(solution)/shard_map/ppermute | solution.py:509
  13.5 8.0 %collective-permute-start.2 = (bf16[544,128]{1,0:T(8,128)(2,1)S(1)}, bf16[544,128]{1,0:T(8,128)(2,1)S(1)}, u32[]{:S(2)}, u32[]{:S(2)}) collective-permute-start(bf16[544,128]{1,0:T(8,128)(2,1)S(1)} %join_blocks.2.refs_0_.refs_5_), channel_id=1, source_target_pairs={{0,8},{2,10},{4,12},{6,14},{8,0},{10,2},{12,4},{14,6},{1,9},{3,11}... | collective-permute-start | bytes 417800 | tf_op jit(solution)/shard_map/ppermute | solution.py:509
  21.5 5.1 %collective-permute-start.4 = (bf16[544,128]{1,0:T(8,128)(2,1)S(1)}, bf16[544,128]{1,0:T(8,128)(2,1)S(1)}, u32[]{:S(2)}, u32[]{:S(2)}) collective-permute-start(bf16[544,128]{1,0:T(8,128)(2,1)S(1)} %collective-permute-done.2.refs_2_.refs_7_), channel_id=1, source_target_pairs={{0,4},{2,6},{4,0},{6,2},{8,12},{10,14},{12,8},{14,10},{1,5},{3,7},... | collective-permute-start | bytes 417800 | tf_op jit(solution)/shard_map/ppermute | solution.py:509
  21.8 11.2 %collective-permute-start.7 = (bf16[512,128]{1,0:T(8,128)(2,1)S(1)}, bf16[512,128]{1,0:T(8,128)(2,1)S(1)}, u32[]{:S(2)}, u32[]{:S(2)}) collective-permute-start(bf16[512,128]{1,0:T(8,128)(2,1)S(1)} %join_blocks.3.refs_5_), channel_id=1, source_target_pairs={{0,4},{2,6},{4,0},{6,2},{8,12},{10,14},{12,8},{14,10},{1,5},{3,7},... | collective-permute-start | bytes 393224 | tf_op jit(solution)/shard_map/ppermute | solution.py:509
  23.5 9.6 %collective-permute-start.8 = (bf16[512,128]{1,0:T(8,128)(2,1)S(1)}, bf16[512,128]{1,0:T(8,128)(2,1)S(1)}, u32[]{:S(2)}, u32[]{:S(2)}) collective-permute-start(bf16[512,128]{1,0:T(8,128)(2,1)S(1)} %join_blocks.3.refs_5_), channel_id=1, source_target_pairs={{0,8},{2,10},{4,12},{6,14},{8,0},{10,2},{12,4},{14,6},{1,9},{3,11}... | collective-permute-start | bytes 393224 | tf_op jit(solution)/shard_map/ppermute | solution.py:509
  27.2 13.5 %collective-permute-start.6 = (bf16[2,5,128,128]{3,2,1,0:T(8,128)(2,1)S(1)}, bf16[2,5,128,128]{3,2,1,0:T(8,128)(2,1)S(1)}, u32[]{:S(2)}, u32[]{:S(2)}) collective-permute-start(bf16[2,5,128,128]{3,2,1,0:T(8,128)(2,1)S(1)} %get-tuple-element.60), channel_id=1, source_target_pairs={{0,2},{2,0},{4,6},{6,4},{8,10},{10,8},{12,14},{14,12},{1,3},{3,1},... | collective-permute-start | bytes 983048 | tf_op jit(solution)/shard_map/ppermute | solution.py:509
  33.1 6.3 %collective-permute-start.9 = (bf16[512,128]{1,0:T(8,128)(2,1)S(1)}, bf16[512,128]{1,0:T(8,128)(2,1)S(1)}, u32[]{:S(2)}, u32[]{:S(2)}) collective-permute-start(bf16[512,128]{1,0:T(8,128)(2,1)S(1)} %collective-permute-done.8.refs_7_), channel_id=1, source_target_pairs={{0,4},{2,6},{4,0},{6,2},{8,12},{10,14},{12,8},{14,10},{1,5},{3,7},... | collective-permute-start | bytes 393224 | tf_op jit(solution)/shard_map/ppermute | solution.py:509
  39.4 12.0 %collective-permute-start.12 = (bf16[4,2,128,128]{3,2,1,0:T(8,128)(2,1)S(1)}, bf16[4,2,128,128]{3,2,1,0:T(8,128)(2,1)S(1)}, u32[]{:S(2)}, u32[]{:S(2)}) collective-permute-start(bf16[4,2,128,128]{3,2,1,0:T(8,128)(2,1)S(1)} %get-tuple-element.68), channel_id=1, source_target_pairs={{0,4},{2,6},{4,0},{6,2},{8,12},{10,14},{12,8},{14,10},{1,5},{3,7},... | collective-permute-start | bytes 786440 | tf_op jit(solution)/shard_map/ppermute | solution.py:509
  51.5 7.0 %collective-permute-start.15 = (bf16[2,2,128,128]{3,2,1,0:T(8,128)(2,1)S(1)}, bf16[2,2,128,128]{3,2,1,0:T(8,128)(2,1)S(1)}, u32[]{:S(2)}, u32[]{:S(2)}) collective-permute-start(bf16[2,2,128,128]{3,2,1,0:T(8,128)(2,1)S(1)} %get-tuple-element.76), channel_id=1, source_target_pairs={{0,12},{2,14},{4,8},{6,10},{8,4},{10,6},{12,0},{14,2},{1,13},{3,15... | collective-permute-start | bytes 393224 | tf_op jit(solution)/shard_map/ppermute | solution.py:509
  53.4 7.7 %collective-permute-start.16 = (bf16[2,2,128,128]{3,2,1,0:T(8,128)(2,1)S(1)}, bf16[2,2,128,128]{3,2,1,0:T(8,128)(2,1)S(1)}, u32[]{:S(2)}, u32[]{:S(2)}) collective-permute-start(bf16[2,2,128,128]{3,2,1,0:T(8,128)(2,1)S(1)} %get-tuple-element.77), channel_id=1, source_target_pairs={{0,8},{2,10},{4,12},{6,14},{8,0},{10,2},{12,4},{14,6},{1,9},{3,11}... | collective-permute-start | bytes 393224 | tf_op jit(solution)/shard_map/ppermute | solution.py:509
  53.5 7.7 %collective-permute-start.17 = (bf16[2,2,128,128]{3,2,1,0:T(8,128)(2,1)S(1)}, bf16[2,2,128,128]{3,2,1,0:T(8,128)(2,1)S(1)}, u32[]{:S(2)}, u32[]{:S(2)}) collective-permute-start(bf16[2,2,128,128]{3,2,1,0:T(8,128)(2,1)S(1)} %get-tuple-element.78), channel_id=1, source_target_pairs={{0,4},{2,6},{4,0},{6,2},{8,12},{10,14},{12,8},{14,10},{1,5},{3,7},... | collective-permute-start | bytes 393224 | tf_op jit(solution)/shard_map/ppermute | solution.py:509
  55.9 9.9 %collective-permute-start.10 = (bf16[128,640]{1,0:T(8,128)(2,1)S(1)}, bf16[128,640]{1,0:T(8,128)(2,1)S(1)}, u32[]{:S(2)}, u32[]{:S(2)}) collective-permute-start(bf16[128,640]{1,0:T(8,128)(2,1)S(1)} %get-tuple-element.64), channel_id=1, source_target_pairs={{0,2},{2,0},{4,6},{6,4},{8,10},{10,8},{12,14},{14,12},{1,3},{3,1},... | collective-permute-start | bytes 491528 | tf_op jit(solution)/shard_map/ppermute | solution.py:509
  56.7 9.1 %collective-permute-start.11 = (bf16[128,640]{1,0:T(8,128)(2,1)S(1)}, bf16[128,640]{1,0:T(8,128)(2,1)S(1)}, u32[]{:S(2)}, u32[]{:S(2)}) collective-permute-start(bf16[128,640]{1,0:T(8,128)(2,1)S(1)} %get-tuple-element.65), channel_id=1, source_target_pairs={{0,2},{2,0},{4,6},{6,4},{8,10},{10,8},{12,14},{14,12},{1,3},{3,1},... | collective-permute-start | bytes 491528 | tf_op jit(solution)/shard_map/ppermute | solution.py:509
  58.4 6.3 %collective-permute-start.13 = (bf16[2,2,128,128]{3,2,1,0:T(8,128)(2,1)S(1)}, bf16[2,2,128,128]{3,2,1,0:T(8,128)(2,1)S(1)}, u32[]{:S(2)}, u32[]{:S(2)}) collective-permute-start(bf16[2,2,128,128]{3,2,1,0:T(8,128)(2,1)S(1)} %add_convert_fusion), channel_id=1, source_target_pairs={{0,8},{2,10},{4,12},{6,14},{8,0},{10,2},{12,4},{14,6},{1,9},{3,11}... | collective-permute-start | bytes 393224 | tf_op jit(solution)/shard_map/ppermute | solution.py:509
  61.1 5.6 %collective-permute-start.18 = (bf16[2,128,128]{2,1,0:T(8,128)(2,1)S(1)}, bf16[2,128,128]{2,1,0:T(8,128)(2,1)S(1)}, u32[]{:S(2)}, u32[]{:S(2)}) collective-permute-start(bf16[2,128,128]{2,1,0:T(8,128)(2,1)S(1)} %fusion.1), channel_id=1, source_target_pairs={{0,2},{2,0},{4,6},{6,4},{8,10},{10,8},{12,14},{14,12},{1,3},{3,1},... | collective-permute-start | bytes 196616 | tf_op jit(solution)/shard_map/ppermute | solution.py:509
  64.7 4.3 %collective-permute-start.14 = (bf16[2,128,128]{2,1,0:T(8,128)(2,1)S(1)}, bf16[2,128,128]{2,1,0:T(8,128)(2,1)S(1)}, u32[]{:S(2)}, u32[]{:S(2)}) collective-permute-start(bf16[2,128,128]{2,1,0:T(8,128)(2,1)S(1)} %fusion), channel_id=1, source_target_pairs={{0,2},{2,0},{4,6},{6,4},{8,10},{10,8},{12,14},{14,12},{1,3},{3,1},... | collective-permute-start | bytes 196616 | tf_op jit(solution)/shard_map/ppermute | solution.py:509

commit v16 on v14

--- a/solution.py
+++ b/solution.py
@@ -322,8 +322,8 @@
 def attend_kernel(depth, segs, steps, group_size, *refs):
     parents_s, adv_ref, bias_ref = refs[:3]
     query_refs, kv_refs = refs[3 : 3 + segs], refs[3 + segs : 3 + segs + steps]
-    kv_scr, p_scr, ds_scr, acc_scr = refs[-4:]
-    refs = refs[3 + segs + steps : -4]
+    kv_scr, both_scr, acc_scr = refs[-3:]
+    refs = refs[3 + segs + steps : -3]
     dkv_refs, dq_refs = refs[-steps:], refs[-steps - segs : -steps]
 
     length = query_refs[0].shape[2]
@@ -336,6 +336,7 @@
     acc_scr[...] = jnp.zeros_like(acc_scr)
 
     scale = HD**-0.5
+    half = group_size * length
     contract_last = (((1,), (1,)), ((), ()))
     contract_first = (((0,), (0,)), ((), ()))
     for i in range(segs):
@@ -357,35 +358,45 @@
         do_list = [(adv_ref[i] * d.astype(jnp.float32)).astype(jnp.bfloat16) for d in dir_list]
         k_all = jnp.concatenate([kv_scr[s, 0] for s in chosen], axis=0)
         v_all = jnp.concatenate([kv_scr[s, 1] for s in chosen], axis=0)
-        q_all = jnp.concatenate(q_list, axis=0)
-        do_all = jnp.concatenate(do_list, axis=0)
-        all_scores = lax.dot_general(
-            k_all, q_all, contract_last, preferred_element_type=jnp.float32
-        )
-        all_dprob = lax.dot_general(
-            v_all, do_all, contract_last, preferred_element_type=jnp.float32
+        zeros = jnp.zeros((length, HD), jnp.bfloat16)
+        right = []
+        for q, grad_out in zip(q_list, do_list):
+            right.append(jnp.concatenate([q, zeros], axis=1))
+            right.append(jnp.concatenate([zeros, grad_out], axis=1))
+        products = lax.dot_general(
+            jnp.concatenate([k_all, v_all], axis=1),
+            jnp.concatenate(right, axis=0),
+            contract_last,
+            preferred_element_type=jnp.float32,
         )
         for j in range(group_size):
             columns = slice(j * length, (j + 1) * length)
-            scores = all_scores[:, columns] * (scale * LOG2E) + bias_ref[i]
+            first = 2 * j * length
+            scores = products[:, first : first + length] * (scale * LOG2E) + bias_ref[i]
             top = jnp.max(scores, axis=0, keepdims=True)
             unnorm = jnp.exp2(scores - top)
             prob = unnorm * (1.0 / jnp.sum(unnorm, axis=0, keepdims=True))
             prob_low = prob.astype(jnp.bfloat16)
-            dprob = all_dprob[:, columns]
+            dprob = products[:, first + length : first + 2 * length]
             row_dot = jnp.sum(prob_low.astype(jnp.float32) * dprob, axis=0, keepdims=True)
             dscore = (prob * (dprob - row_dot)).astype(jnp.bfloat16)
-            p_scr[:, columns] = prob_low
-            ds_scr[:, columns] = dscore
-        dscore_all = ds_scr[...]
+            both_scr[:, columns] = prob_low
+            both_scr[:, slice(columns.start + half, columns.stop + half)] = dscore
+        dscore_all = both_scr[:, half:]
         dq_t = lax.dot_general(
             k_all, dscore_all, contract_first, preferred_element_type=jnp.float32
         )
         for j in range(group_size):
             dq = jnp.transpose(dq_t[:, j * length : (j + 1) * length]) * scale
             dq_refs[i][:, j * HD : (j + 1) * HD] = dq.astype(jnp.bfloat16)
-        dk_all = jnp.dot(dscore_all, q_all, preferred_element_type=jnp.float32) * scale
-        dv_all = jnp.dot(p_scr[...], do_all, preferred_element_type=jnp.float32)
+        left = jnp.concatenate(do_list + [jnp.zeros((half, HD), jnp.bfloat16)], axis=0)
+        other = jnp.concatenate([jnp.zeros((half, HD), jnp.bfloat16)] + q_list, axis=0)
+        grads = jnp.dot(
+            both_scr[...],
+            jnp.concatenate([left, other], axis=1),
+            preferred_element_type=jnp.float32,
+        )
+        dv_all, dk_all = grads[:, :HD], grads[:, HD:] * scale
         for slot, s in enumerate(chosen):
             rows = slice(slot * length, (slot + 1) * length)
             acc_scr[s, 0] += dk_all[rows]
@@ -413,8 +424,7 @@
         out_specs=[vmem] * len(out_shape),
         scratch_shapes=[
             pltpu.VMEM((sources, 2, length, HD), jnp.bfloat16),
-            pltpu.VMEM((keys, width), jnp.bfloat16),
-            pltpu.VMEM((keys, width), jnp.bfloat16),
+            pltpu.VMEM((keys, 2 * group_size * length), jnp.bfloat16),
             pltpu.VMEM((sources, 2, length, HD), jnp.float32),
         ],
         compiler_params=pltpu.CompilerParams(vmem_limit_bytes=16 * 1024 * 1024),

time: 63.4 us -> 63.2 us (level)
  Pallas kernels: 14.5 us -> 16.3 us
  waiting for transfers between devices: 20.5 us -> 18.9 us
    pallas_call x2, Pallas kernels: 8.85 us -> 10.6 us  [attend(): pl.pallas_call(functools.partial(attend_kernel, DEPTH, segs, steps, group...]
    ppermute x20, waiting for transfers between devices: 20.5 us -> 18.9 us  [permute(): return lax.ppermute(array, 'seg', pairs)]
  transfers between devices with their start and end apart: 20 -> 20, of which waited for: 10 -> 11; matrix products, arithmetic and copies ran while one was open for 0% -> 0% of each run, Pallas kernels for 19% -> 22%
where the time goes in v16:
time: 63.2 us; the launch traced here: 62.9 us
  starting transfers between devices  23.8 us (38%)
  waiting for transfers between devices  18.9 us (30%)
  Pallas kernels  16.3 us (26%)
  local copies, waits for them, and re-layouts  3.05 us (5%)
  between operations  0.74 us (1%)
    ppermute x20, starting transfers between devices, permute(): return lax.ppermute(array, 'seg', pairs)  23.8 us
    ppermute x20, waiting for transfers between devices, permute(): return lax.ppermute(array, 'seg', pairs)  18.9 us
    pallas_call x2, Pallas kernels, attend(): pl.pallas_call(functools.partial(attend_kernel, DEPTH, segs, steps, group...  10.6 us
    unnamed x12, local copies, waits for them, and re-layouts  3.05 us
    pallas_call x1, Pallas kernels, pack(): pl.pallas_call(functools.partial(pack_kernel, log_rate, parts), out_shape...  1.81 us
  transfers between devices with their start and end apart: 20, of which 11 were waited for; matrix products, arithmetic and copies ran while one was open for 0% of the time, Pallas kernels for 22%

profile of v16, /device:TPU:0, one launch (start us, length us, event | category | flops | bytes accessed | tf_op | source)
XLA Modules:
  0.0 62.9 jit_solution(13566844477420519689)
XLA Ops:
  0.6 1.8 %pack_keys_values.1 = (bf16[272,128]{1,0:T(8,128)(2,1)}, bf16[256,128]{1,0:T(8,128)(2,1)}, bf16[272,128]{1,0:T(8,128)(2,1)}, bf16[256,128]{1,0:T(8,128)(2,1)}) custom-call(s32[8]{0:T(128)} %lengths_s.1, bf16[128,512]{1,0:T(8,128)(2,1)} %k_ref.1, bf16[128,512]{1,0:T(8,128)(2,1)} %v_ref.1, f32[1,128]{1,0:T(1,128)} %bitcast.9, f32[1,128]{1,0:T(1,128)} %bitcast.10, ...), custom_call_target="tpu_custom_call" | custom-call | flops 12800 | bytes 524288 | tf_op jit(solution)/shard_map/pack_keys_values/pallas_call | solution.py:104
  2.4 2.9 %collective-permute-start = (bf16[272,128]{1,0:T(8,128)(2,1)}, bf16[272,128]{1,0:T(8,128)(2,1)S(1)}, u32[]{:S(2)}, u32[]{:S(2)}) collective-permute-start(bf16[272,128]{1,0:T(8,128)(2,1)} %get-tuple-element.41), channel_id=1, source_target_pairs={{0,2},{2,0},{4,6},{6,4},{8,10},{10,8},{12,14},{14,12},{1,3},{3,1},... | collective-permute-start | bytes 208904 | tf_op jit(solution)/shard_map/ppermute | solution.py:505
  5.4 0.1 collective-permute-start.3
  5.5 0.0 copy-start
  5.5 1.1 %copy-done = bf16[128,2560]{1,0:T(8,128)(2,1)S(1)} copy-done((bf16[128,2560]{1,0:T(8,128)(2,1)S(1)}, bf16[128,2560]{1,0:T(8,128)(2,1)}, u32[]{:S(2)}) %copy-start) | copy-done | bytes 655384
  6.5 0.0 copy-start.1
  6.5 1.1 %copy-done.1 = bf16[128,2560]{1,0:T(8,128)(2,1)S(1)} copy-done((bf16[128,2560]{1,0:T(8,128)(2,1)S(1)}, bf16[128,2560]{1,0:T(8,128)(2,1)}, u32[]{:S(2)}) %copy-start.1) | copy-done | bytes 655384
  7.6 0.0 copy-start.3
  7.6 0.2 pack_queries.1
  7.9 2.0 %collective-permute-done.3.other_ref = bf16[256,128]{1,0:T(8,128)(2,1)S(1)} collective-permute-done((bf16[256,128]{1,0:T(8,128)(2,1)}, bf16[256,128]{1,0:T(8,128)(2,1)S(1)}, u32[]{:S(2)}, u32[]{:S(2)}) %collective-permute-start.3) | collective-permute-done | bytes 65568 | tf_op jit(solution)/shard_map/ppermute | solution.py:505
  9.9 0.0 copy-done.3
  9.9 0.0 copy-start.2
  9.9 0.0 collective-permute-done.refs_1_.other_ref
  9.9 0.9 %copy-done.2 = bf16[272,128]{1,0:T(8,128)(2,1)S(1)} copy-done((bf16[272,128]{1,0:T(8,128)(2,1)S(1)}, bf16[272,128]{1,0:T(8,128)(2,1)}, u32[]{:S(2)}) %copy-start.2) | copy-done | bytes 69656
  10.8 0.0 copy-start.4
  10.8 0.0 copy-start.5
  10.8 1.1 %collective-permute-start.5 = (bf16[2,5,128,128]{3,2,1,0:T(8,128)(2,1)S(1)}, bf16[2,5,128,128]{3,2,1,0:T(8,128)(2,1)S(1)}, u32[]{:S(2)}, u32[]{:S(2)}) collective-permute-start(bf16[2,5,128,128]{3,2,1,0:T(8,128)(2,1)S(1)} %get-tuple-element.54), channel_id=1, source_target_pairs={{0,2},{2,0},{4,6},{6,4},{8,10},{10,8},{12,14},{14,12},{1,3},{3,1},... | collective-permute-start | bytes 983048 | tf_op jit(solution)/shard_map/ppermute | solution.py:505
  11.9 1.6 %collective-permute-start.1 = (bf16[544,128]{1,0:T(8,128)(2,1)S(1)}, bf16[544,128]{1,0:T(8,128)(2,1)S(1)}, u32[]{:S(2)}, u32[]{:S(2)}) collective-permute-start(bf16[544,128]{1,0:T(8,128)(2,1)S(1)} %join_blocks.2.refs_0_.refs_5_), channel_id=1, source_target_pairs={{0,4},{2,6},{4,0},{6,2},{8,12},{10,14},{12,8},{14,10},{1,5},{3,7},... | collective-permute-start | bytes 417800 | tf_op jit(solution)/shard_map/ppermute | solution.py:505
  13.5 2.6 %collective-permute-start.2 = (bf16[544,128]{1,0:T(8,128)(2,1)S(1)}, bf16[544,128]{1,0:T(8,128)(2,1)S(1)}, u32[]{:S(2)}, u32[]{:S(2)}) collective-permute-start(bf16[544,128]{1,0:T(8,128)(2,1)S(1)} %join_blocks.2.refs_0_.refs_5_), channel_id=1, source_target_pairs={{0,8},{2,10},{4,12},{6,14},{8,0},{10,2},{12,4},{14,6},{1,9},{3,11}... | collective-permute-start | bytes 417800 | tf_op jit(solution)/shard_map/ppermute | solution.py:505
  16.1 0.0 copy-done.4
  16.1 0.0 copy-done.5
  16.1 1.2 %prepare.1 = (f32[2,640,128]{2,1,0:T(8,128)S(1)}, f32[2,3,128,128]{3,2,1,0:T(8,128)S(1)}, f32[2,2,8,128]{3,2,1,0:T(8,128)S(1)}) custom-call(s32[8]{0:T(128)S(1)} %copy-done.5, s32[8]{0:T(128)S(1)} %copy-done.4, bf16[272,128]{1,0:T(8,128)(2,1)S(1)} %copy-done.2, bf16[272,128]{1,0:T(8,128)(2,1)S(1)} %collective-permute-done.refs_1_.other_ref), custom_call_target="tpu_custom_call" | custom-call | flops 3276800 | bytes 655360 | tf_op jit(solution)/shard_map/prepare/pallas_call | solution.py:253
  17.3 1.5 %collective-permute-done.1.refs_1_.refs_6_ = bf16[544,128]{1,0:T(8,128)(2,1)S(1)} collective-permute-done((bf16[544,128]{1,0:T(8,128)(2,1)S(1)}, bf16[544,128]{1,0:T(8,128)(2,1)S(1)}, u32[]{:S(2)}, u32[]{:S(2)}) %collective-permute-start.1) | collective-permute-done | bytes 139296 | tf_op jit(solution)/shard_map/ppermute | solution.py:505
  18.8 2.7 %collective-permute-done.2.refs_2_.refs_7_ = bf16[544,128]{1,0:T(8,128)(2,1)S(1)} collective-permute-done((bf16[544,128]{1,0:T(8,128)(2,1)S(1)}, bf16[544,128]{1,0:T(8,128)(2,1)S(1)}, u32[]{:S(2)}, u32[]{:S(2)}) %collective-permute-start.2) | collective-permute-done | bytes 139296 | tf_op jit(solution)/shard_map/ppermute | solution.py:505
  21.5 0.4 collective-permute-start.4
  21.8 0.0 collective-permute-done.5.refs_4_
  21.8 1.3 %collective-permute-start.6 = (bf16[2,5,128,128]{3,2,1,0:T(8,128)(2,1)S(1)}, bf16[2,5,128,128]{3,2,1,0:T(8,128)(2,1)S(1)}, u32[]{:S(2)}, u32[]{:S(2)}) collective-permute-start(bf16[2,5,128,128]{3,2,1,0:T(8,128)(2,1)S(1)} %get-tuple-element.57), channel_id=1, source_target_pairs={{0,2},{2,0},{4,6},{6,4},{8,10},{10,8},{12,14},{14,12},{1,3},{3,1},... | collective-permute-start | bytes 983048 | tf_op jit(solution)/shard_map/ppermute | solution.py:505
  23.2 2.7 %collective-permute-start.8 = (bf16[512,128]{1,0:T(8,128)(2,1)S(1)}, bf16[512,128]{1,0:T(8,128)(2,1)S(1)}, u32[]{:S(2)}, u32[]{:S(2)}) collective-permute-start(bf16[512,128]{1,0:T(8,128)(2,1)S(1)} %join_blocks.3.refs_5_), channel_id=1, source_target_pairs={{0,8},{2,10},{4,12},{6,14},{8,0},{10,2},{12,4},{14,6},{1,9},{3,11}... | collective-permute-start | bytes 393224 | tf_op jit(solution)/shard_map/ppermute | solution.py:505
  25.9 0.0 collective-permute-start.7
  25.9 3.6 %collective-permute-done.4.refs_3_.refs_8_ = bf16[544,128]{1,0:T(8,128)(2,1)S(1)} collective-permute-done((bf16[544,128]{1,0:T(8,128)(2,1)S(1)}, bf16[544,128]{1,0:T(8,128)(2,1)S(1)}, u32[]{:S(2)}, u32[]{:S(2)}) %collective-permute-start.4) | collective-permute-done | bytes 139296 | tf_op jit(solution)/shard_map/ppermute | solution.py:505
  29.5 0.7 %advantages.1 = (f32[1,128]{1,0:T(1,128)}, f32[2,128,128]{2,1,0:T(8,128)S(1)}) custom-call(f32[2,3,128,128]{3,2,1,0:T(8,128)S(1)} %get-tuple-element.42.columns_ref, f32[2,2,8,128]{3,2,1,0:T(8,128)S(1)} %get-tuple-element.43.weights_ref, bf16[544,128]{1,0:T(8,128)(2,1)S(1)} %join_blocks.2.refs_0_.refs_5_, ...), custom_call_target="tpu_custom_call" | custom-call | flops 327680 | bytes 524288 | tf_op jit(solution)/shard_map/advantages/pallas_call | solution.py:306
  30.2 5.3 %tree_attention_backward.2 = (bf16[128,640]{1,0:T(8,128)(2,1)S(1)}, bf16[128,640]{1,0:T(8,128)(2,1)S(1)}, bf16[2,2,128,128]{3,2,1,0:T(8,128)(2,1)S(1)}, bf16[2,2...) custom-call(s32[8]{0:T(128)S(1)} %copy-done.5, ...), custom_call_target="tpu_custom_call" | custom-call | flops 1048576000 | bytes 8388608 | tf_op jit(solution)/shard_map/tree_attention_backward/pallas_call | solution.py:420
  35.5 0.0 collective-permute-done.8.refs_7_
  35.5 0.1 collective-permute-start.9
  35.6 2.3 %collective-permute-start.12 = (bf16[2,2,128,128]{3,2,1,0:T(8,128)(2,1)S(1)}, bf16[2,2,128,128]{3,2,1,0:T(8,128)(2,1)S(1)}, u32[]{:S(2)}, u32[]{:S(2)}) collective-permute-start(bf16[2,2,128,128]{3,2,1,0:T(8,128)(2,1)S(1)} %get-tuple-element.65), channel_id=1, source_target_pairs={{0,12},{2,14},{4,8},{6,10},{8,4},{10,6},{12,0},{14,2},{1,13},{3,15... | collective-permute-start | bytes 393224 | tf_op jit(solution)/shard_map/ppermute | solution.py:505
  38.0 1.1 %collective-permute-start.13 = (bf16[2,2,128,128]{3,2,1,0:T(8,128)(2,1)S(1)}, bf16[2,2,128,128]{3,2,1,0:T(8,128)(2,1)S(1)}, u32[]{:S(2)}, u32[]{:S(2)}) collective-permute-start(bf16[2,2,128,128]{3,2,1,0:T(8,128)(2,1)S(1)} %get-tuple-element.66), channel_id=1, source_target_pairs={{0,8},{2,10},{4,12},{6,14},{8,0},{10,2},{12,4},{14,6},{1,9},{3,11}... | collective-permute-start | bytes 393224 | tf_op jit(solution)/shard_map/ppermute | solution.py:505
  39.1 0.0 collective-permute-done.7.refs_6_
  39.1 1.0 %collective-permute-start.14 = (bf16[2,2,128,128]{3,2,1,0:T(8,128)(2,1)S(1)}, bf16[2,2,128,128]{3,2,1,0:T(8,128)(2,1)S(1)}, u32[]{:S(2)}, u32[]{:S(2)}) collective-permute-start(bf16[2,2,128,128]{3,2,1,0:T(8,128)(2,1)S(1)} %get-tuple-element.67), channel_id=1, source_target_pairs={{0,4},{2,6},{4,0},{6,2},{8,12},{10,14},{12,8},{14,10},{1,5},{3,7},... | collective-permute-start | bytes 393224 | tf_op jit(solution)/shard_map/ppermute | solution.py:505
  40.1 0.5 collective-permute-done.9.refs_8_
  40.6 0.8 %collective-permute-start.10 = (bf16[128,640]{1,0:T(8,128)(2,1)S(1)}, bf16[128,640]{1,0:T(8,128)(2,1)S(1)}, u32[]{:S(2)}, u32[]{:S(2)}) collective-permute-start(bf16[128,640]{1,0:T(8,128)(2,1)S(1)} %get-tuple-element.61), channel_id=1, source_target_pairs={{0,2},{2,0},{4,6},{6,4},{8,10},{10,8},{12,14},{14,12},{1,3},{3,1},... | collective-permute-start | bytes 491528 | tf_op jit(solution)/shard_map/ppermute | solution.py:505
  41.4 0.0 collective-permute-done.6.refs_4_
  41.4 5.3 %tree_attention_backward.3 = (bf16[128,640]{1,0:T(8,128)(2,1)S(1)}, bf16[128,640]{1,0:T(8,128)(2,1)S(1)}, bf16[2,2,128,128]{3,2,1,0:T(8,128)(2,1)S(1)}, bf16[2,2...) custom-call(s32[8]{0:T(128)S(1)} %copy-done.5, ...), custom_call_target="tpu_custom_call" | custom-call | flops 1048576000 | bytes 8388608 | tf_op jit(solution)/shard_map/tree_attention_backward/pallas_call | solution.py:420
  46.7 2.7 %collective-permute-start.16 = (bf16[2,2,128,128]{3,2,1,0:T(8,128)(2,1)S(1)}, bf16[2,2,128,128]{3,2,1,0:T(8,128)(2,1)S(1)}, u32[]{:S(2)}, u32[]{:S(2)}) collective-permute-start(bf16[2,2,128,128]{3,2,1,0:T(8,128)(2,1)S(1)} %get-tuple-element.70), channel_id=1, source_target_pairs={{0,12},{2,14},{4,8},{6,10},{8,4},{10,6},{12,0},{14,2},{1,13},{3,15... | collective-permute-start | bytes 393224 | tf_op jit(solution)/shard_map/ppermute | solution.py:505
  49.4 0.0 collective-permute-done.12.refs_3_
  49.4 0.5 collective-permute-start.17
  49.9 1.4 %collective-permute-done.13.refs_4_ = bf16[2,2,128,128]{3,2,1,0:T(8,128)(2,1)S(1)} collective-permute-done((bf16[2,2,128,128]{3,2,1,0:T(8,128)(2,1)S(1)}, bf16[2,2,128,128]{3,2,1,0:T(8,128)(2,1)S(1)}, u32[]{:S(2)}, u32[]{:S(2)}) %collective-permute-start.13) | collective-permute-done | bytes 131104 | tf_op jit(solution)/shard_map/ppermute | solution.py:505
  51.3 0.0 collective-permute-start.18
  51.3 0.0 collective-permute-done.14.refs_5_
  51.3 1.2 %collective-permute-start.15 = (bf16[2,128,128]{2,1,0:T(8,128)(2,1)S(1)}, bf16[2,128,128]{2,1,0:T(8,128)(2,1)S(1)}, u32[]{:S(2)}, u32[]{:S(2)}) collective-permute-start(bf16[2,128,128]{2,1,0:T(8,128)(2,1)S(1)} %fusion), channel_id=1, source_target_pairs={{0,2},{2,0},{4,6},{6,4},{8,10},{10,8},{12,14},{14,12},{1,3},{3,1},... | collective-permute-start | bytes 196616 | tf_op jit(solution)/shard_map/ppermute | solution.py:505
  52.5 1.1 %collective-permute-done.16.refs_7_ = bf16[2,2,128,128]{3,2,1,0:T(8,128)(2,1)S(1)} collective-permute-done((bf16[2,2,128,128]{3,2,1,0:T(8,128)(2,1)S(1)}, bf16[2,2,128,128]{3,2,1,0:T(8,128)(2,1)S(1)}, u32[]{:S(2)}, u32[]{:S(2)}) %collective-permute-start.16) | collective-permute-done | bytes 131104 | tf_op jit(solution)/shard_map/ppermute | solution.py:505
  53.6 1.2 %collective-permute-start.11 = (bf16[128,640]{1,0:T(8,128)(2,1)S(1)}, bf16[128,640]{1,0:T(8,128)(2,1)S(1)}, u32[]{:S(2)}, u32[]{:S(2)}) collective-permute-start(bf16[128,640]{1,0:T(8,128)(2,1)S(1)} %get-tuple-element.62), channel_id=1, source_target_pairs={{0,2},{2,0},{4,6},{6,4},{8,10},{10,8},{12,14},{14,12},{1,3},{3,1},... | collective-permute-start | bytes 491528 | tf_op jit(solution)/shard_map/ppermute | solution.py:505
  54.9 2.7 %collective-permute-done.17.refs_8_ = bf16[2,2,128,128]{3,2,1,0:T(8,128)(2,1)S(1)} collective-permute-done((bf16[2,2,128,128]{3,2,1,0:T(8,128)(2,1)S(1)}, bf16[2,2,128,128]{3,2,1,0:T(8,128)(2,1)S(1)}, u32[]{:S(2)}, u32[]{:S(2)}) %collective-permute-start.17) | collective-permute-done | bytes 131104 | tf_op jit(solution)/shard_map/ppermute | solution.py:505
  57.6 0.2 collective-permute-done.18.refs_9_
  57.8 0.3 collective-permute-start.19
  58.1 0.0 collective-permute-done.10.refs_2_
  58.1 1.6 %collective-permute-done.11.refs_3_ = bf16[128,640]{1,0:T(8,128)(2,1)S(1)} collective-permute-done((bf16[128,640]{1,0:T(8,128)(2,1)S(1)}, bf16[128,640]{1,0:T(8,128)(2,1)S(1)}, u32[]{:S(2)}, u32[]{:S(2)}) %collective-permute-start.11) | collective-permute-done | bytes 163872 | tf_op jit(solution)/shard_map/ppermute | solution.py:505
  59.7 0.9 %join_queries.1 = bf16[128,2560]{1,0:T(8,128)(2,1)} custom-call(bf16[128,640]{1,0:T(8,128)(2,1)S(1)} %get-tuple-element.55.refs_0_, bf16[128,640]{1,0:T(8,128)(2,1)S(1)} %get-tuple-element.60.refs_1_, bf16[128,640]{1,0:T(8,128)(2,1)S(1)} %collective-permute-done.10.refs_2_, bf16[128,640]{1,0:T(8,128)(2,1)S(1)} %collective-permute-done.11.refs_3_), custom_call_target="tpu_custom_call" | custom-call | bytes 1310720 | tf_op jit(solution)/shard_map/join_queries/pallas_call | solution.py:457
  60.6 0.0 collective-permute-done.15.refs_0_
  60.6 1.5 %collective-permute-done.19.refs_1_ = bf16[2,128,128]{2,1,0:T(8,128)(2,1)S(1)} collective-permute-done((bf16[2,128,128]{2,1,0:T(8,128)(2,1)S(1)}, bf16[2,128,128]{2,1,0:T(8,128)(2,1)S(1)}, u32[]{:S(2)}, u32[]{:S(2)}) %collective-permute-start.19) | collective-permute-done | bytes 65568 | tf_op jit(solution)/shard_map/ppermute | solution.py:505
  62.1 0.8 %join_keys.1 = (bf16[128,512]{1,0:T(8,128)(2,1)}, bf16[128,512]{1,0:T(8,128)(2,1)}) custom-call(bf16[2,128,128]{2,1,0:T(8,128)(2,1)S(1)} %collective-permute-done.15.refs_0_, bf16[2,128,128]{2,1,0:T(8,128)(2,1)S(1)} %collective-permute-done.19.refs_1_, bf16[2,2,128,128]{3,2,1,0:T(8,128)(2,1)S(1)} %get-tuple-element.64.refs_2_, ...), custom_call_target="tpu_custom_call" | custom-call | bytes 524288 | tf_op jit(solution)/shard_map/join_keys/pallas_call | solution.py:491
  (4 shorter events, 0.1 us)
Async XLA Ops:
  2.4 7.4 %collective-permute-start = (bf16[272,128]{1,0:T(8,128)(2,1)}, bf16[272,128]{1,0:T(8,128)(2,1)S(1)}, u32[]{:S(2)}, u32[]{:S(2)}) collective-permute-start(bf16[272,128]{1,0:T(8,128)(2,1)} %get-tuple-element.41), channel_id=1, source_target_pairs={{0,2},{2,0},{4,6},{6,4},{8,10},{10,8},{12,14},{14,12},{1,3},{3,1},... | collective-permute-start | bytes 208904 | tf_op jit(solution)/shard_map/ppermute | solution.py:505
  5.4 4.5 %collective-permute-start.3 = (bf16[256,128]{1,0:T(8,128)(2,1)}, bf16[256,128]{1,0:T(8,128)(2,1)S(1)}, u32[]{:S(2)}, u32[]{:S(2)}) collective-permute-start(bf16[256,128]{1,0:T(8,128)(2,1)} %get-tuple-element.49), channel_id=1, source_target_pairs={{0,2},{2,0},{4,6},{6,4},{8,10},{10,8},{12,14},{14,12},{1,3},{3,1},... | collective-permute-start | bytes 196616 | tf_op jit(solution)/shard_map/ppermute | solution.py:505
  5.5 1.1 %copy-start = (bf16[128,2560]{1,0:T(8,128)(2,1)S(1)}, bf16[128,2560]{1,0:T(8,128)(2,1)}, u32[]{:S(2)}) copy-start(bf16[128,2560]{1,0:T(8,128)(2,1)} %q_ref) | copy-start | bytes 1966084
  6.5 1.1 %copy-start.1 = (bf16[128,2560]{1,0:T(8,128)(2,1)S(1)}, bf16[128,2560]{1,0:T(8,128)(2,1)}, u32[]{:S(2)}) copy-start(bf16[128,2560]{1,0:T(8,128)(2,1)} %dir_ref.1) | copy-start | bytes 1966084
  7.6 2.2 %copy-start.3 = (bf16[256,128]{1,0:T(8,128)(2,1)S(1)}, bf16[256,128]{1,0:T(8,128)(2,1)}, u32[]{:S(2)}) copy-start(bf16[256,128]{1,0:T(8,128)(2,1)} %get-tuple-element.48.mine_ref) | copy-start | bytes 196612
  9.9 0.9 %copy-start.2 = (bf16[272,128]{1,0:T(8,128)(2,1)S(1)}, bf16[272,128]{1,0:T(8,128)(2,1)}, u32[]{:S(2)}) copy-start(bf16[272,128]{1,0:T(8,128)(2,1)} %get-tuple-element.40.refs_0_.mine_ref) | copy-start | bytes 208900
  10.8 5.3 %copy-start.4 = (s32[8]{0:T(128)S(1)}, s32[8]{0:T(128)}, u32[]{:S(2)}) copy-start(s32[8]{0:T(128)} %lengths_s.1) | copy-start | bytes 100
  10.8 5.3 %copy-start.5 = (s32[8]{0:T(128)S(1)}, s32[8]{0:T(128)}, u32[]{:S(2)}) copy-start(s32[8]{0:T(128)} %refs_0_.3) | copy-start | bytes 100
  10.8 11.1 %collective-permute-start.5 = (bf16[2,5,128,128]{3,2,1,0:T(8,128)(2,1)S(1)}, bf16[2,5,128,128]{3,2,1,0:T(8,128)(2,1)S(1)}, u32[]{:S(2)}, u32[]{:S(2)}) collective-permute-start(bf16[2,5,128,128]{3,2,1,0:T(8,128)(2,1)S(1)} %get-tuple-element.54), channel_id=1, source_target_pairs={{0,2},{2,0},{4,6},{6,4},{8,10},{10,8},{12,14},{14,12},{1,3},{3,1},... | collective-permute-start | bytes 983048 | tf_op jit(solution)/shard_map/ppermute | solution.py:505
  11.9 6.9 %collective-permute-start.1 = (bf16[544,128]{1,0:T(8,128)(2,1)S(1)}, bf16[544,128]{1,0:T(8,128)(2,1)S(1)}, u32[]{:S(2)}, u32[]{:S(2)}) collective-permute-start(bf16[544,128]{1,0:T(8,128)(2,1)S(1)} %join_blocks.2.refs_0_.refs_5_), channel_id=1, source_target_pairs={{0,4},{2,6},{4,0},{6,2},{8,12},{10,14},{12,8},{14,10},{1,5},{3,7},... | collective-permute-start | bytes 417800 | tf_op jit(solution)/shard_map/ppermute | solution.py:505
  13.5 8.0 %collective-permute-start.2 = (bf16[544,128]{1,0:T(8,128)(2,1)S(1)}, bf16[544,128]{1,0:T(8,128)(2,1)S(1)}, u32[]{:S(2)}, u32[]{:S(2)}) collective-permute-start(bf16[544,128]{1,0:T(8,128)(2,1)S(1)} %join_blocks.2.refs_0_.refs_5_), channel_id=1, source_target_pairs={{0,8},{2,10},{4,12},{6,14},{8,0},{10,2},{12,4},{14,6},{1,9},{3,11}... | collective-permute-start | bytes 417800 | tf_op jit(solution)/shard_map/ppermute | solution.py:505
  21.5 8.0 %collective-permute-start.4 = (bf16[544,128]{1,0:T(8,128)(2,1)S(1)}, bf16[544,128]{1,0:T(8,128)(2,1)S(1)}, u32[]{:S(2)}, u32[]{:S(2)}) collective-permute-start(bf16[544,128]{1,0:T(8,128)(2,1)S(1)} %collective-permute-done.2.refs_2_.refs_7_), channel_id=1, source_target_pairs={{0,4},{2,6},{4,0},{6,2},{8,12},{10,14},{12,8},{14,10},{1,5},{3,7},... | collective-permute-start | bytes 417800 | tf_op jit(solution)/shard_map/ppermute | solution.py:505
  21.8 19.5 %collective-permute-start.6 = (bf16[2,5,128,128]{3,2,1,0:T(8,128)(2,1)S(1)}, bf16[2,5,128,128]{3,2,1,0:T(8,128)(2,1)S(1)}, u32[]{:S(2)}, u32[]{:S(2)}) collective-permute-start(bf16[2,5,128,128]{3,2,1,0:T(8,128)(2,1)S(1)} %get-tuple-element.57), channel_id=1, source_target_pairs={{0,2},{2,0},{4,6},{6,4},{8,10},{10,8},{12,14},{14,12},{1,3},{3,1},... | collective-permute-start | bytes 983048 | tf_op jit(solution)/shard_map/ppermute | solution.py:505
  23.2 12.3 %collective-permute-start.8 = (bf16[512,128]{1,0:T(8,128)(2,1)S(1)}, bf16[512,128]{1,0:T(8,128)(2,1)S(1)}, u32[]{:S(2)}, u32[]{:S(2)}) collective-permute-start(bf16[512,128]{1,0:T(8,128)(2,1)S(1)} %join_blocks.3.refs_5_), channel_id=1, source_target_pairs={{0,8},{2,10},{4,12},{6,14},{8,0},{10,2},{12,4},{14,6},{1,9},{3,11}... | collective-permute-start | bytes 393224 | tf_op jit(solution)/shard_map/ppermute | solution.py:505
  25.9 13.2 %collective-permute-start.7 = (bf16[512,128]{1,0:T(8,128)(2,1)S(1)}, bf16[512,128]{1,0:T(8,128)(2,1)S(1)}, u32[]{:S(2)}, u32[]{:S(2)}) collective-permute-start(bf16[512,128]{1,0:T(8,128)(2,1)S(1)} %join_blocks.3.refs_5_), channel_id=1, source_target_pairs={{0,4},{2,6},{4,0},{6,2},{8,12},{10,14},{12,8},{14,10},{1,5},{3,7},... | collective-permute-start | bytes 393224 | tf_op jit(solution)/shard_map/ppermute | solution.py:505
  35.5 5.0 %collective-permute-start.9 = (bf16[512,128]{1,0:T(8,128)(2,1)S(1)}, bf16[512,128]{1,0:T(8,128)(2,1)S(1)}, u32[]{:S(2)}, u32[]{:S(2)}) collective-permute-start(bf16[512,128]{1,0:T(8,128)(2,1)S(1)} %collective-permute-done.8.refs_7_), channel_id=1, source_target_pairs={{0,4},{2,6},{4,0},{6,2},{8,12},{10,14},{12,8},{14,10},{1,5},{3,7},... | collective-permute-start | bytes 393224 | tf_op jit(solution)/shard_map/ppermute | solution.py:505
  35.6 13.8 %collective-permute-start.12 = (bf16[2,2,128,128]{3,2,1,0:T(8,128)(2,1)S(1)}, bf16[2,2,128,128]{3,2,1,0:T(8,128)(2,1)S(1)}, u32[]{:S(2)}, u32[]{:S(2)}) collective-permute-start(bf16[2,2,128,128]{3,2,1,0:T(8,128)(2,1)S(1)} %get-tuple-element.65), channel_id=1, source_target_pairs={{0,12},{2,14},{4,8},{6,10},{8,4},{10,6},{12,0},{14,2},{1,13},{3,15... | collective-permute-start | bytes 393224 | tf_op jit(solution)/shard_map/ppermute | solution.py:505
  38.0 13.3 %collective-permute-start.13 = (bf16[2,2,128,128]{3,2,1,0:T(8,128)(2,1)S(1)}, bf16[2,2,128,128]{3,2,1,0:T(8,128)(2,1)S(1)}, u32[]{:S(2)}, u32[]{:S(2)}) collective-permute-start(bf16[2,2,128,128]{3,2,1,0:T(8,128)(2,1)S(1)} %get-tuple-element.66), channel_id=1, source_target_pairs={{0,8},{2,10},{4,12},{6,14},{8,0},{10,2},{12,4},{14,6},{1,9},{3,11}... | collective-permute-start | bytes 393224 | tf_op jit(solution)/shard_map/ppermute | solution.py:505
  39.1 12.2 %collective-permute-start.14 = (bf16[2,2,128,128]{3,2,1,0:T(8,128)(2,1)S(1)}, bf16[2,2,128,128]{3,2,1,0:T(8,128)(2,1)S(1)}, u32[]{:S(2)}, u32[]{:S(2)}) collective-permute-start(bf16[2,2,128,128]{3,2,1,0:T(8,128)(2,1)S(1)} %get-tuple-element.67), channel_id=1, source_target_pairs={{0,4},{2,6},{4,0},{6,2},{8,12},{10,14},{12,8},{14,10},{1,5},{3,7},... | collective-permute-start | bytes 393224 | tf_op jit(solution)/shard_map/ppermute | solution.py:505
  40.6 17.5 %collective-permute-start.10 = (bf16[128,640]{1,0:T(8,128)(2,1)S(1)}, bf16[128,640]{1,0:T(8,128)(2,1)S(1)}, u32[]{:S(2)}, u32[]{:S(2)}) collective-permute-start(bf16[128,640]{1,0:T(8,128)(2,1)S(1)} %get-tuple-element.61), channel_id=1, source_target_pairs={{0,2},{2,0},{4,6},{6,4},{8,10},{10,8},{12,14},{14,12},{1,3},{3,1},... | collective-permute-start | bytes 491528 | tf_op jit(solution)/shard_map/ppermute | solution.py:505
  46.7 6.9 %collective-permute-start.16 = (bf16[2,2,128,128]{3,2,1,0:T(8,128)(2,1)S(1)}, bf16[2,2,128,128]{3,2,1,0:T(8,128)(2,1)S(1)}, u32[]{:S(2)}, u32[]{:S(2)}) collective-permute-start(bf16[2,2,128,128]{3,2,1,0:T(8,128)(2,1)S(1)} %get-tuple-element.70), channel_id=1, source_target_pairs={{0,12},{2,14},{4,8},{6,10},{8,4},{10,6},{12,0},{14,2},{1,13},{3,15... | collective-permute-start | bytes 393224 | tf_op jit(solution)/shard_map/ppermute | solution.py:505
  49.4 8.2 %collective-permute-start.17 = (bf16[2,2,128,128]{3,2,1,0:T(8,128)(2,1)S(1)}, bf16[2,2,128,128]{3,2,1,0:T(8,128)(2,1)S(1)}, u32[]{:S(2)}, u32[]{:S(2)}) collective-permute-start(bf16[2,2,128,128]{3,2,1,0:T(8,128)(2,1)S(1)} %get-tuple-element.71), channel_id=1, source_target_pairs={{0,8},{2,10},{4,12},{6,14},{8,0},{10,2},{12,4},{14,6},{1,9},{3,11}... | collective-permute-start | bytes 393224 | tf_op jit(solution)/shard_map/ppermute | solution.py:505
  51.3 6.5 %collective-permute-start.18 = (bf16[2,2,128,128]{3,2,1,0:T(8,128)(2,1)S(1)}, bf16[2,2,128,128]{3,2,1,0:T(8,128)(2,1)S(1)}, u32[]{:S(2)}, u32[]{:S(2)}) collective-permute-start(bf16[2,2,128,128]{3,2,1,0:T(8,128)(2,1)S(1)} %get-tuple-element.72), channel_id=1, source_target_pairs={{0,4},{2,6},{4,0},{6,2},{8,12},{10,14},{12,8},{14,10},{1,5},{3,7},... | collective-permute-start | bytes 393224 | tf_op jit(solution)/shard_map/ppermute | solution.py:505
  51.3 9.2 %collective-permute-start.15 = (bf16[2,128,128]{2,1,0:T(8,128)(2,1)S(1)}, bf16[2,128,128]{2,1,0:T(8,128)(2,1)S(1)}, u32[]{:S(2)}, u32[]{:S(2)}) collective-permute-start(bf16[2,128,128]{2,1,0:T(8,128)(2,1)S(1)} %fusion), channel_id=1, source_target_pairs={{0,2},{2,0},{4,6},{6,4},{8,10},{10,8},{12,14},{14,12},{1,3},{3,1},... | collective-permute-start | bytes 196616 | tf_op jit(solution)/shard_map/ppermute | solution.py:505
  53.6 6.0 %collective-permute-start.11 = (bf16[128,640]{1,0:T(8,128)(2,1)S(1)}, bf16[128,640]{1,0:T(8,128)(2,1)S(1)}, u32[]{:S(2)}, u32[]{:S(2)}) collective-permute-start(bf16[128,640]{1,0:T(8,128)(2,1)S(1)} %get-tuple-element.62), channel_id=1, source_target_pairs={{0,2},{2,0},{4,6},{6,4},{8,10},{10,8},{12,14},{14,12},{1,3},{3,1},... | collective-permute-start | bytes 491528 | tf_op jit(solution)/shard_map/ppermute | solution.py:505
  57.8 4.3 %collective-permute-start.19 = (bf16[2,128,128]{2,1,0:T(8,128)(2,1)S(1)}, bf16[2,128,128]{2,1,0:T(8,128)(2,1)S(1)}, u32[]{:S(2)}, u32[]{:S(2)}) collective-permute-start(bf16[2,128,128]{2,1,0:T(8,128)(2,1)S(1)} %fusion.1), channel_id=1, source_target_pairs={{0,2},{2,0},{4,6},{6,4},{8,10},{10,8},{12,14},{14,12},{1,3},{3,1},... | collective-permute-start | bytes 196616 | tf_op jit(solution)/shard_map/ppermute | solution.py:505

commit v17 on v14

--- a/solution.py
+++ b/solution.py
@@ -506,6 +506,7 @@
     swap = [(i, i ^ 1) for i in range(groups)]
     steps = range(1, groups // 2)
     meet = {bits: [(i, i ^ (2 * bits)) for i in range(groups)] for bits in steps}
+    home = {bits: [(i, j) for i, j in meet[bits] if j < i] for bits in steps}
 
     kept, given = pack(lengths, key_vectors, value_vectors, token_rows, 2, log_rate)
     taken = [permute(block, swap) for block in given]
@@ -534,7 +535,7 @@
 
     summands = []
     for dkv in dkv_list:
-        arrived = [permute(dkv[bits], meet[bits]) for bits in steps[::-1]]
+        arrived = [permute(dkv[bits], home[bits]) for bits in steps[::-1]]
         summands.append([after(dkv[0], dq_own[-1])] + arrived)
     dq_back = [permute(block, swap) for block in dq_back]
     others = []

time: 63.4 us -> 65.4 us (1.032)
  waiting for transfers between devices: 20.5 us -> 23 us
  starting transfers between devices: 24.3 us -> 23.5 us
    ppermute x20, waiting for transfers between devices: 20.5 us -> 23 us  [permute(): return lax.ppermute(array, 'seg', pairs)]
    ppermute x20, starting transfers between devices: 24.3 us -> 23.5 us  [permute(): return lax.ppermute(array, 'seg', pairs)]
  transfers between devices with their start and end apart: 20 -> 20, of which waited for: 10 -> 11; matrix products, arithmetic and copies ran while one was open for 0% -> 0% of each run, Pallas kernels for 19% -> 18%
where the time goes in v17:
time: 65.4 us; the launch traced here: 65 us
  starting transfers between devices  23.5 us (36%)
  waiting for transfers between devices  23 us (35%)
  Pallas kernels  14.5 us (22%)
  local copies, waits for them, and re-layouts  3.05 us (5%)
  between operations  0.8 us (1%)
    ppermute x20, starting transfers between devices, permute(): return lax.ppermute(array, 'seg', pairs)  23.5 us
    ppermute x20, waiting for transfers between devices, permute(): return lax.ppermute(array, 'seg', pairs)  23 us
    pallas_call x2, Pallas kernels, attend(): pl.pallas_call(functools.partial(attend_kernel, DEPTH, segs, steps, group...  8.86 us
    unnamed x12, local copies, waits for them, and re-layouts  3.05 us
    pallas_call x1, Pallas kernels, pack(): pl.pallas_call(functools.partial(pack_kernel, log_rate, parts), out_shape...  1.81 us
  transfers between devices with their start and end apart: 20, of which 11 were waited for; matrix products, arithmetic and copies ran while one was open for 0% of the time, Pallas kernels for 18%

profile of v17, /device:TPU:0, one launch (start us, length us, event | category | flops | bytes accessed | tf_op | source)
XLA Modules:
  0.0 65.0 jit_solution(11889561758690171432)
XLA Ops:
  0.6 1.8 %pack_keys_values.1 = (bf16[272,128]{1,0:T(8,128)(2,1)}, bf16[256,128]{1,0:T(8,128)(2,1)}, bf16[272,128]{1,0:T(8,128)(2,1)}, bf16[256,128]{1,0:T(8,128)(2,1)}) custom-call(s32[8]{0:T(128)} %lengths_s.1, bf16[128,512]{1,0:T(8,128)(2,1)} %k_ref.1, bf16[128,512]{1,0:T(8,128)(2,1)} %v_ref.1, f32[1,128]{1,0:T(1,128)} %bitcast.9, f32[1,128]{1,0:T(1,128)} %bitcast.10, ...), custom_call_target="tpu_custom_call" | custom-call | flops 12800 | bytes 524288 | tf_op jit(solution)/shard_map/pack_keys_values/pallas_call | solution.py:104
  2.4 2.9 %collective-permute-start = (bf16[272,128]{1,0:T(8,128)(2,1)}, bf16[272,128]{1,0:T(8,128)(2,1)S(1)}, u32[]{:S(2)}, u32[]{:S(2)}) collective-permute-start(bf16[272,128]{1,0:T(8,128)(2,1)} %get-tuple-element.41), channel_id=1, source_target_pairs={{0,2},{2,0},{4,6},{6,4},{8,10},{10,8},{12,14},{14,12},{1,3},{3,1},... | collective-permute-start | bytes 208904 | tf_op jit(solution)/shard_map/ppermute | solution.py:495
  5.4 0.1 collective-permute-start.3
  5.5 0.0 copy-start
  5.5 1.1 %copy-done = bf16[128,2560]{1,0:T(8,128)(2,1)S(1)} copy-done((bf16[128,2560]{1,0:T(8,128)(2,1)S(1)}, bf16[128,2560]{1,0:T(8,128)(2,1)}, u32[]{:S(2)}) %copy-start) | copy-done | bytes 655384
  6.5 0.0 copy-start.1
  6.5 1.1 %copy-done.1 = bf16[128,2560]{1,0:T(8,128)(2,1)S(1)} copy-done((bf16[128,2560]{1,0:T(8,128)(2,1)S(1)}, bf16[128,2560]{1,0:T(8,128)(2,1)}, u32[]{:S(2)}) %copy-start.1) | copy-done | bytes 655384
  7.6 0.0 copy-start.3
  7.6 0.2 pack_queries.1
  7.9 2.0 %collective-permute-done.3.other_ref = bf16[256,128]{1,0:T(8,128)(2,1)S(1)} collective-permute-done((bf16[256,128]{1,0:T(8,128)(2,1)}, bf16[256,128]{1,0:T(8,128)(2,1)S(1)}, u32[]{:S(2)}, u32[]{:S(2)}) %collective-permute-start.3) | collective-permute-done | bytes 65568 | tf_op jit(solution)/shard_map/ppermute | solution.py:495
  9.9 0.0 copy-done.3
  9.9 0.0 copy-start.2
  9.9 0.0 collective-permute-done.refs_1_.other_ref
  9.9 0.9 %copy-done.2 = bf16[272,128]{1,0:T(8,128)(2,1)S(1)} copy-done((bf16[272,128]{1,0:T(8,128)(2,1)S(1)}, bf16[272,128]{1,0:T(8,128)(2,1)}, u32[]{:S(2)}) %copy-start.2) | copy-done | bytes 69656
  10.8 0.0 copy-start.4
  10.8 0.0 copy-start.5
  10.8 1.1 %collective-permute-start.5 = (bf16[2,5,128,128]{3,2,1,0:T(8,128)(2,1)S(1)}, bf16[2,5,128,128]{3,2,1,0:T(8,128)(2,1)S(1)}, u32[]{:S(2)}, u32[]{:S(2)}) collective-permute-start(bf16[2,5,128,128]{3,2,1,0:T(8,128)(2,1)S(1)} %get-tuple-element.54), channel_id=1, source_target_pairs={{0,2},{2,0},{4,6},{6,4},{8,10},{10,8},{12,14},{14,12},{1,3},{3,1},... | collective-permute-start | bytes 983048 | tf_op jit(solution)/shard_map/ppermute | solution.py:495
  11.9 1.6 %collective-permute-start.1 = (bf16[544,128]{1,0:T(8,128)(2,1)S(1)}, bf16[544,128]{1,0:T(8,128)(2,1)S(1)}, u32[]{:S(2)}, u32[]{:S(2)}) collective-permute-start(bf16[544,128]{1,0:T(8,128)(2,1)S(1)} %join_blocks.2.refs_0_.refs_5_), channel_id=1, source_target_pairs={{0,4},{2,6},{4,0},{6,2},{8,12},{10,14},{12,8},{14,10},{1,5},{3,7},... | collective-permute-start | bytes 417800 | tf_op jit(solution)/shard_map/ppermute | solution.py:495
  13.5 2.6 %collective-permute-start.2 = (bf16[544,128]{1,0:T(8,128)(2,1)S(1)}, bf16[544,128]{1,0:T(8,128)(2,1)S(1)}, u32[]{:S(2)}, u32[]{:S(2)}) collective-permute-start(bf16[544,128]{1,0:T(8,128)(2,1)S(1)} %join_blocks.2.refs_0_.refs_5_), channel_id=1, source_target_pairs={{0,8},{2,10},{4,12},{6,14},{8,0},{10,2},{12,4},{14,6},{1,9},{3,11}... | collective-permute-start | bytes 417800 | tf_op jit(solution)/shard_map/ppermute | solution.py:495
  16.1 0.0 copy-done.4
  16.1 0.0 copy-done.5
  16.1 1.2 %prepare.1 = (f32[2,640,128]{2,1,0:T(8,128)S(1)}, f32[2,3,128,128]{3,2,1,0:T(8,128)S(1)}, f32[2,2,8,128]{3,2,1,0:T(8,128)S(1)}) custom-call(s32[8]{0:T(128)S(1)} %copy-done.5, s32[8]{0:T(128)S(1)} %copy-done.4, bf16[272,128]{1,0:T(8,128)(2,1)S(1)} %copy-done.2, bf16[272,128]{1,0:T(8,128)(2,1)S(1)} %collective-permute-done.refs_1_.other_ref), custom_call_target="tpu_custom_call" | custom-call | flops 3276800 | bytes 655360 | tf_op jit(solution)/shard_map/prepare/pallas_call | solution.py:253
  17.3 1.5 %collective-permute-done.1.refs_1_.refs_6_ = bf16[544,128]{1,0:T(8,128)(2,1)S(1)} collective-permute-done((bf16[544,128]{1,0:T(8,128)(2,1)S(1)}, bf16[544,128]{1,0:T(8,128)(2,1)S(1)}, u32[]{:S(2)}, u32[]{:S(2)}) %collective-permute-start.1) | collective-permute-done | bytes 139296 | tf_op jit(solution)/shard_map/ppermute | solution.py:495
  18.8 2.7 %collective-permute-done.2.refs_2_.refs_7_ = bf16[544,128]{1,0:T(8,128)(2,1)S(1)} collective-permute-done((bf16[544,128]{1,0:T(8,128)(2,1)S(1)}, bf16[544,128]{1,0:T(8,128)(2,1)S(1)}, u32[]{:S(2)}, u32[]{:S(2)}) %collective-permute-start.2) | collective-permute-done | bytes 139296 | tf_op jit(solution)/shard_map/ppermute | solution.py:495
  21.5 0.4 collective-permute-start.4
  21.8 0.0 collective-permute-done.5.refs_4_
  21.8 1.3 %collective-permute-start.6 = (bf16[2,5,128,128]{3,2,1,0:T(8,128)(2,1)S(1)}, bf16[2,5,128,128]{3,2,1,0:T(8,128)(2,1)S(1)}, u32[]{:S(2)}, u32[]{:S(2)}) collective-permute-start(bf16[2,5,128,128]{3,2,1,0:T(8,128)(2,1)S(1)} %get-tuple-element.57), channel_id=1, source_target_pairs={{0,2},{2,0},{4,6},{6,4},{8,10},{10,8},{12,14},{14,12},{1,3},{3,1},... | collective-permute-start | bytes 983048 | tf_op jit(solution)/shard_map/ppermute | solution.py:495
  23.2 2.7 %collective-permute-start.8 = (bf16[512,128]{1,0:T(8,128)(2,1)S(1)}, bf16[512,128]{1,0:T(8,128)(2,1)S(1)}, u32[]{:S(2)}, u32[]{:S(2)}) collective-permute-start(bf16[512,128]{1,0:T(8,128)(2,1)S(1)} %join_blocks.3.refs_5_), channel_id=1, source_target_pairs={{0,8},{2,10},{4,12},{6,14},{8,0},{10,2},{12,4},{14,6},{1,9},{3,11}... | collective-permute-start | bytes 393224 | tf_op jit(solution)/shard_map/ppermute | solution.py:495
  25.9 0.0 collective-permute-start.7
  25.9 3.6 %collective-permute-done.4.refs_3_.refs_8_ = bf16[544,128]{1,0:T(8,128)(2,1)S(1)} collective-permute-done((bf16[544,128]{1,0:T(8,128)(2,1)S(1)}, bf16[544,128]{1,0:T(8,128)(2,1)S(1)}, u32[]{:S(2)}, u32[]{:S(2)}) %collective-permute-start.4) | collective-permute-done | bytes 139296 | tf_op jit(solution)/shard_map/ppermute | solution.py:495
  29.5 0.7 %advantages.1 = (f32[1,128]{1,0:T(1,128)}, f32[2,128,128]{2,1,0:T(8,128)S(1)}) custom-call(f32[2,3,128,128]{3,2,1,0:T(8,128)S(1)} %get-tuple-element.42.columns_ref, f32[2,2,8,128]{3,2,1,0:T(8,128)S(1)} %get-tuple-element.43.weights_ref, bf16[544,128]{1,0:T(8,128)(2,1)S(1)} %join_blocks.2.refs_0_.refs_5_, ...), custom_call_target="tpu_custom_call" | custom-call | flops 327680 | bytes 524288 | tf_op jit(solution)/shard_map/advantages/pallas_call | solution.py:306
  30.2 4.4 %tree_attention_backward.2 = (bf16[128,640]{1,0:T(8,128)(2,1)S(1)}, bf16[128,640]{1,0:T(8,128)(2,1)S(1)}, bf16[2,2,128,128]{3,2,1,0:T(8,128)(2,1)S(1)}, bf16[2,2...) custom-call(s32[8]{0:T(128)S(1)} %copy-done.5, ...), custom_call_target="tpu_custom_call" | custom-call | flops 1048576000 | bytes 8388608 | tf_op jit(solution)/shard_map/tree_attention_backward/pallas_call | solution.py:409
  34.6 0.0 collective-permute-done.8.refs_7_
  34.6 0.1 collective-permute-start.9
  34.7 1.3 %collective-permute-start.12 = (bf16[2,2,128,128]{3,2,1,0:T(8,128)(2,1)S(1)}, bf16[2,2,128,128]{3,2,1,0:T(8,128)(2,1)S(1)}, u32[]{:S(2)}, u32[]{:S(2)}) collective-permute-start(bf16[2,2,128,128]{3,2,1,0:T(8,128)(2,1)S(1)} %get-tuple-element.65), channel_id=1, source_target_pairs={{8,4},{10,6},{12,0},{14,2},{9,5},{11,7},{13,1},{15,3},{24,20},{26,... | collective-permute-start | bytes 393224 | tf_op jit(solution)/shard_map/ppermute | solution.py:495
  36.0 1.3 %collective-permute-start.13 = (bf16[2,2,128,128]{3,2,1,0:T(8,128)(2,1)S(1)}, bf16[2,2,128,128]{3,2,1,0:T(8,128)(2,1)S(1)}, u32[]{:S(2)}, u32[]{:S(2)}) collective-permute-start(bf16[2,2,128,128]{3,2,1,0:T(8,128)(2,1)S(1)} %get-tuple-element.66), channel_id=1, source_target_pairs={{8,0},{10,2},{12,4},{14,6},{9,1},{11,3},{13,5},{15,7},{24,16},{26,... | collective-permute-start | bytes 393224 | tf_op jit(solution)/shard_map/ppermute | solution.py:495
  37.3 0.0 collective-permute-done.7.refs_6_
  37.3 1.3 %collective-permute-start.14 = (bf16[2,2,128,128]{3,2,1,0:T(8,128)(2,1)S(1)}, bf16[2,2,128,128]{3,2,1,0:T(8,128)(2,1)S(1)}, u32[]{:S(2)}, u32[]{:S(2)}) collective-permute-start(bf16[2,2,128,128]{3,2,1,0:T(8,128)(2,1)S(1)} %get-tuple-element.67), channel_id=1, source_target_pairs={{4,0},{6,2},{12,8},{14,10},{5,1},{7,3},{13,9},{15,11},{20,16},{22,... | collective-permute-start | bytes 393224 | tf_op jit(solution)/shard_map/ppermute | solution.py:495
  38.6 2.4 %collective-permute-done.9.refs_8_ = bf16[512,128]{1,0:T(8,128)(2,1)S(1)} collective-permute-done((bf16[512,128]{1,0:T(8,128)(2,1)S(1)}, bf16[512,128]{1,0:T(8,128)(2,1)S(1)}, u32[]{:S(2)}, u32[]{:S(2)}) %collective-permute-start.9) | collective-permute-done | bytes 131104 | tf_op jit(solution)/shard_map/ppermute | solution.py:495
  41.1 0.7 %collective-permute-start.10 = (bf16[128,640]{1,0:T(8,128)(2,1)S(1)}, bf16[128,640]{1,0:T(8,128)(2,1)S(1)}, u32[]{:S(2)}, u32[]{:S(2)}) collective-permute-start(bf16[128,640]{1,0:T(8,128)(2,1)S(1)} %get-tuple-element.61), channel_id=1, source_target_pairs={{0,2},{2,0},{4,6},{6,4},{8,10},{10,8},{12,14},{14,12},{1,3},{3,1},... | collective-permute-start | bytes 491528 | tf_op jit(solution)/shard_map/ppermute | solution.py:495
  41.7 0.0 collective-permute-done.6.refs_4_
  41.7 4.4 %tree_attention_backward.3 = (bf16[128,640]{1,0:T(8,128)(2,1)S(1)}, bf16[128,640]{1,0:T(8,128)(2,1)S(1)}, bf16[2,2,128,128]{3,2,1,0:T(8,128)(2,1)S(1)}, bf16[2,2...) custom-call(s32[8]{0:T(128)S(1)} %copy-done.5, ...), custom_call_target="tpu_custom_call" | custom-call | flops 1048576000 | bytes 8388608 | tf_op jit(solution)/shard_map/tree_attention_backward/pallas_call | solution.py:409
  46.2 1.3 %collective-permute-start.16 = (bf16[2,2,128,128]{3,2,1,0:T(8,128)(2,1)S(1)}, bf16[2,2,128,128]{3,2,1,0:T(8,128)(2,1)S(1)}, u32[]{:S(2)}, u32[]{:S(2)}) collective-permute-start(bf16[2,2,128,128]{3,2,1,0:T(8,128)(2,1)S(1)} %get-tuple-element.70), channel_id=1, source_target_pairs={{8,4},{10,6},{12,0},{14,2},{9,5},{11,7},{13,1},{15,3},{24,20},{26,... | collective-permute-start | bytes 393224 | tf_op jit(solution)/shard_map/ppermute | solution.py:495
  47.5 0.0 collective-permute-done.12.refs_3_
  47.5 1.3 %collective-permute-start.17 = (bf16[2,2,128,128]{3,2,1,0:T(8,128)(2,1)S(1)}, bf16[2,2,128,128]{3,2,1,0:T(8,128)(2,1)S(1)}, u32[]{:S(2)}, u32[]{:S(2)}) collective-permute-start(bf16[2,2,128,128]{3,2,1,0:T(8,128)(2,1)S(1)} %get-tuple-element.71), channel_id=1, source_target_pairs={{8,0},{10,2},{12,4},{14,6},{9,1},{11,3},{13,5},{15,7},{24,16},{26,... | collective-permute-start | bytes 393224 | tf_op jit(solution)/shard_map/ppermute | solution.py:495
  48.8 3.2 %collective-permute-done.13.refs_4_ = bf16[2,2,128,128]{3,2,1,0:T(8,128)(2,1)S(1)} collective-permute-done((bf16[2,2,128,128]{3,2,1,0:T(8,128)(2,1)S(1)}, bf16[2,2,128,128]{3,2,1,0:T(8,128)(2,1)S(1)}, u32[]{:S(2)}, u32[]{:S(2)}) %collective-permute-start.13) | collective-permute-done | bytes 131104 | tf_op jit(solution)/shard_map/ppermute | solution.py:495
  52.0 1.3 %collective-permute-start.18 = (bf16[2,2,128,128]{3,2,1,0:T(8,128)(2,1)S(1)}, bf16[2,2,128,128]{3,2,1,0:T(8,128)(2,1)S(1)}, u32[]{:S(2)}, u32[]{:S(2)}) collective-permute-start(bf16[2,2,128,128]{3,2,1,0:T(8,128)(2,1)S(1)} %get-tuple-element.72), channel_id=1, source_target_pairs={{4,0},{6,2},{12,8},{14,10},{5,1},{7,3},{13,9},{15,11},{20,16},{22,... | collective-permute-start | bytes 393224 | tf_op jit(solution)/shard_map/ppermute | solution.py:495
  53.2 0.0 collective-permute-done.14.refs_5_
  53.3 0.4 collective-permute-start.15
  53.7 1.2 %collective-permute-done.16.refs_7_ = bf16[2,2,128,128]{3,2,1,0:T(8,128)(2,1)S(1)} collective-permute-done((bf16[2,2,128,128]{3,2,1,0:T(8,128)(2,1)S(1)}, bf16[2,2,128,128]{3,2,1,0:T(8,128)(2,1)S(1)}, u32[]{:S(2)}, u32[]{:S(2)}) %collective-permute-start.16) | collective-permute-done | bytes 131104 | tf_op jit(solution)/shard_map/ppermute | solution.py:495
  54.9 1.4 %collective-permute-start.11 = (bf16[128,640]{1,0:T(8,128)(2,1)S(1)}, bf16[128,640]{1,0:T(8,128)(2,1)S(1)}, u32[]{:S(2)}, u32[]{:S(2)}) collective-permute-start(bf16[128,640]{1,0:T(8,128)(2,1)S(1)} %get-tuple-element.62), channel_id=1, source_target_pairs={{0,2},{2,0},{4,6},{6,4},{8,10},{10,8},{12,14},{14,12},{1,3},{3,1},... | collective-permute-start | bytes 491528 | tf_op jit(solution)/shard_map/ppermute | solution.py:495
  56.3 2.3 %collective-permute-done.17.refs_8_ = bf16[2,2,128,128]{3,2,1,0:T(8,128)(2,1)S(1)} collective-permute-done((bf16[2,2,128,128]{3,2,1,0:T(8,128)(2,1)S(1)}, bf16[2,2,128,128]{3,2,1,0:T(8,128)(2,1)S(1)}, u32[]{:S(2)}, u32[]{:S(2)}) %collective-permute-start.17) | collective-permute-done | bytes 131104 | tf_op jit(solution)/shard_map/ppermute | solution.py:495
  58.6 1.3 %collective-permute-done.18.refs_9_ = bf16[2,2,128,128]{3,2,1,0:T(8,128)(2,1)S(1)} collective-permute-done((bf16[2,2,128,128]{3,2,1,0:T(8,128)(2,1)S(1)}, bf16[2,2,128,128]{3,2,1,0:T(8,128)(2,1)S(1)}, u32[]{:S(2)}, u32[]{:S(2)}) %collective-permute-start.18) | collective-permute-done | bytes 131104 | tf_op jit(solution)/shard_map/ppermute | solution.py:495
  59.9 0.6 collective-permute-start.19
  60.5 0.0 collective-permute-done.10.refs_2_
  60.5 0.4 collective-permute-done.11.refs_3_
  61.0 0.9 %join_queries.1 = bf16[128,2560]{1,0:T(8,128)(2,1)} custom-call(bf16[128,640]{1,0:T(8,128)(2,1)S(1)} %get-tuple-element.55.refs_0_, bf16[128,640]{1,0:T(8,128)(2,1)S(1)} %get-tuple-element.60.refs_1_, bf16[128,640]{1,0:T(8,128)(2,1)S(1)} %collective-permute-done.10.refs_2_, bf16[128,640]{1,0:T(8,128)(2,1)S(1)} %collective-permute-done.11.refs_3_), custom_call_target="tpu_custom_call" | custom-call | bytes 1310720 | tf_op jit(solution)/shard_map/join_queries/pallas_call | solution.py:447
  61.9 0.0 collective-permute-done.15.refs_0_
  61.9 2.4 %collective-permute-done.19.refs_1_ = bf16[2,128,128]{2,1,0:T(8,128)(2,1)S(1)} collective-permute-done((bf16[2,128,128]{2,1,0:T(8,128)(2,1)S(1)}, bf16[2,128,128]{2,1,0:T(8,128)(2,1)S(1)}, u32[]{:S(2)}, u32[]{:S(2)}) %collective-permute-start.19) | collective-permute-done | bytes 65568 | tf_op jit(solution)/shard_map/ppermute | solution.py:495
  64.2 0.8 %join_keys.1 = (bf16[128,512]{1,0:T(8,128)(2,1)}, bf16[128,512]{1,0:T(8,128)(2,1)}) custom-call(bf16[2,128,128]{2,1,0:T(8,128)(2,1)S(1)} %collective-permute-done.15.refs_0_, bf16[2,128,128]{2,1,0:T(8,128)(2,1)S(1)} %collective-permute-done.19.refs_1_, bf16[2,2,128,128]{3,2,1,0:T(8,128)(2,1)S(1)} %get-tuple-element.64.refs_2_, ...), custom_call_target="tpu_custom_call" | custom-call | bytes 524288 | tf_op jit(solution)/shard_map/join_keys/pallas_call | solution.py:481
  (4 shorter events, 0.1 us)
Async XLA Ops:
  2.4 7.4 %collective-permute-start = (bf16[272,128]{1,0:T(8,128)(2,1)}, bf16[272,128]{1,0:T(8,128)(2,1)S(1)}, u32[]{:S(2)}, u32[]{:S(2)}) collective-permute-start(bf16[272,128]{1,0:T(8,128)(2,1)} %get-tuple-element.41), channel_id=1, source_target_pairs={{0,2},{2,0},{4,6},{6,4},{8,10},{10,8},{12,14},{14,12},{1,3},{3,1},... | collective-permute-start | bytes 208904 | tf_op jit(solution)/shard_map/ppermute | solution.py:495
  5.4 4.5 %collective-permute-start.3 = (bf16[256,128]{1,0:T(8,128)(2,1)}, bf16[256,128]{1,0:T(8,128)(2,1)S(1)}, u32[]{:S(2)}, u32[]{:S(2)}) collective-permute-start(bf16[256,128]{1,0:T(8,128)(2,1)} %get-tuple-element.49), channel_id=1, source_target_pairs={{0,2},{2,0},{4,6},{6,4},{8,10},{10,8},{12,14},{14,12},{1,3},{3,1},... | collective-permute-start | bytes 196616 | tf_op jit(solution)/shard_map/ppermute | solution.py:495
  5.5 1.1 %copy-start = (bf16[128,2560]{1,0:T(8,128)(2,1)S(1)}, bf16[128,2560]{1,0:T(8,128)(2,1)}, u32[]{:S(2)}) copy-start(bf16[128,2560]{1,0:T(8,128)(2,1)} %q_ref) | copy-start | bytes 1966084
  6.5 1.1 %copy-start.1 = (bf16[128,2560]{1,0:T(8,128)(2,1)S(1)}, bf16[128,2560]{1,0:T(8,128)(2,1)}, u32[]{:S(2)}) copy-start(bf16[128,2560]{1,0:T(8,128)(2,1)} %dir_ref.1) | copy-start | bytes 1966084
  7.6 2.2 %copy-start.3 = (bf16[256,128]{1,0:T(8,128)(2,1)S(1)}, bf16[256,128]{1,0:T(8,128)(2,1)}, u32[]{:S(2)}) copy-start(bf16[256,128]{1,0:T(8,128)(2,1)} %get-tuple-element.48.mine_ref) | copy-start | bytes 196612
  9.9 0.9 %copy-start.2 = (bf16[272,128]{1,0:T(8,128)(2,1)S(1)}, bf16[272,128]{1,0:T(8,128)(2,1)}, u32[]{:S(2)}) copy-start(bf16[272,128]{1,0:T(8,128)(2,1)} %get-tuple-element.40.refs_0_.mine_ref) | copy-start | bytes 208900
  10.8 5.3 %copy-start.4 = (s32[8]{0:T(128)S(1)}, s32[8]{0:T(128)}, u32[]{:S(2)}) copy-start(s32[8]{0:T(128)} %lengths_s.1) | copy-start | bytes 100
  10.8 5.3 %copy-start.5 = (s32[8]{0:T(128)S(1)}, s32[8]{0:T(128)}, u32[]{:S(2)}) copy-start(s32[8]{0:T(128)} %refs_0_.3) | copy-start | bytes 100
  10.8 11.1 %collective-permute-start.5 = (bf16[2,5,128,128]{3,2,1,0:T(8,128)(2,1)S(1)}, bf16[2,5,128,128]{3,2,1,0:T(8,128)(2,1)S(1)}, u32[]{:S(2)}, u32[]{:S(2)}) collective-permute-start(bf16[2,5,128,128]{3,2,1,0:T(8,128)(2,1)S(1)} %get-tuple-element.54), channel_id=1, source_target_pairs={{0,2},{2,0},{4,6},{6,4},{8,10},{10,8},{12,14},{14,12},{1,3},{3,1},... | collective-permute-start | bytes 983048 | tf_op jit(solution)/shard_map/ppermute | solution.py:495
  11.9 6.9 %collective-permute-start.1 = (bf16[544,128]{1,0:T(8,128)(2,1)S(1)}, bf16[544,128]{1,0:T(8,128)(2,1)S(1)}, u32[]{:S(2)}, u32[]{:S(2)}) collective-permute-start(bf16[544,128]{1,0:T(8,128)(2,1)S(1)} %join_blocks.2.refs_0_.refs_5_), channel_id=1, source_target_pairs={{0,4},{2,6},{4,0},{6,2},{8,12},{10,14},{12,8},{14,10},{1,5},{3,7},... | collective-permute-start | bytes 417800 | tf_op jit(solution)/shard_map/ppermute | solution.py:495
  13.5 8.0 %collective-permute-start.2 = (bf16[544,128]{1,0:T(8,128)(2,1)S(1)}, bf16[544,128]{1,0:T(8,128)(2,1)S(1)}, u32[]{:S(2)}, u32[]{:S(2)}) collective-permute-start(bf16[544,128]{1,0:T(8,128)(2,1)S(1)} %join_blocks.2.refs_0_.refs_5_), channel_id=1, source_target_pairs={{0,8},{2,10},{4,12},{6,14},{8,0},{10,2},{12,4},{14,6},{1,9},{3,11}... | collective-permute-start | bytes 417800 | tf_op jit(solution)/shard_map/ppermute | solution.py:495
  21.5 8.0 %collective-permute-start.4 = (bf16[544,128]{1,0:T(8,128)(2,1)S(1)}, bf16[544,128]{1,0:T(8,128)(2,1)S(1)}, u32[]{:S(2)}, u32[]{:S(2)}) collective-permute-start(bf16[544,128]{1,0:T(8,128)(2,1)S(1)} %collective-permute-done.2.refs_2_.refs_7_), channel_id=1, source_target_pairs={{0,4},{2,6},{4,0},{6,2},{8,12},{10,14},{12,8},{14,10},{1,5},{3,7},... | collective-permute-start | bytes 417800 | tf_op jit(solution)/shard_map/ppermute | solution.py:495
  21.8 19.9 %collective-permute-start.6 = (bf16[2,5,128,128]{3,2,1,0:T(8,128)(2,1)S(1)}, bf16[2,5,128,128]{3,2,1,0:T(8,128)(2,1)S(1)}, u32[]{:S(2)}, u32[]{:S(2)}) collective-permute-start(bf16[2,5,128,128]{3,2,1,0:T(8,128)(2,1)S(1)} %get-tuple-element.57), channel_id=1, source_target_pairs={{0,2},{2,0},{4,6},{6,4},{8,10},{10,8},{12,14},{14,12},{1,3},{3,1},... | collective-permute-start | bytes 983048 | tf_op jit(solution)/shard_map/ppermute | solution.py:495
  23.2 11.4 %collective-permute-start.8 = (bf16[512,128]{1,0:T(8,128)(2,1)S(1)}, bf16[512,128]{1,0:T(8,128)(2,1)S(1)}, u32[]{:S(2)}, u32[]{:S(2)}) collective-permute-start(bf16[512,128]{1,0:T(8,128)(2,1)S(1)} %join_blocks.3.refs_5_), channel_id=1, source_target_pairs={{0,8},{2,10},{4,12},{6,14},{8,0},{10,2},{12,4},{14,6},{1,9},{3,11}... | collective-permute-start | bytes 393224 | tf_op jit(solution)/shard_map/ppermute | solution.py:495
  25.9 11.5 %collective-permute-start.7 = (bf16[512,128]{1,0:T(8,128)(2,1)S(1)}, bf16[512,128]{1,0:T(8,128)(2,1)S(1)}, u32[]{:S(2)}, u32[]{:S(2)}) collective-permute-start(bf16[512,128]{1,0:T(8,128)(2,1)S(1)} %join_blocks.3.refs_5_), channel_id=1, source_target_pairs={{0,4},{2,6},{4,0},{6,2},{8,12},{10,14},{12,8},{14,10},{1,5},{3,7},... | collective-permute-start | bytes 393224 | tf_op jit(solution)/shard_map/ppermute | solution.py:495
  34.6 6.4 %collective-permute-start.9 = (bf16[512,128]{1,0:T(8,128)(2,1)S(1)}, bf16[512,128]{1,0:T(8,128)(2,1)S(1)}, u32[]{:S(2)}, u32[]{:S(2)}) collective-permute-start(bf16[512,128]{1,0:T(8,128)(2,1)S(1)} %collective-permute-done.8.refs_7_), channel_id=1, source_target_pairs={{0,4},{2,6},{4,0},{6,2},{8,12},{10,14},{12,8},{14,10},{1,5},{3,7},... | collective-permute-start | bytes 393224 | tf_op jit(solution)/shard_map/ppermute | solution.py:495
  34.7 12.8 %collective-permute-start.12 = (bf16[2,2,128,128]{3,2,1,0:T(8,128)(2,1)S(1)}, bf16[2,2,128,128]{3,2,1,0:T(8,128)(2,1)S(1)}, u32[]{:S(2)}, u32[]{:S(2)}) collective-permute-start(bf16[2,2,128,128]{3,2,1,0:T(8,128)(2,1)S(1)} %get-tuple-element.65), channel_id=1, source_target_pairs={{8,4},{10,6},{12,0},{14,2},{9,5},{11,7},{13,1},{15,3},{24,20},{26,... | collective-permute-start | bytes 393224 | tf_op jit(solution)/shard_map/ppermute | solution.py:495
  36.0 15.9 %collective-permute-start.13 = (bf16[2,2,128,128]{3,2,1,0:T(8,128)(2,1)S(1)}, bf16[2,2,128,128]{3,2,1,0:T(8,128)(2,1)S(1)}, u32[]{:S(2)}, u32[]{:S(2)}) collective-permute-start(bf16[2,2,128,128]{3,2,1,0:T(8,128)(2,1)S(1)} %get-tuple-element.66), channel_id=1, source_target_pairs={{8,0},{10,2},{12,4},{14,6},{9,1},{11,3},{13,5},{15,7},{24,16},{26,... | collective-permute-start | bytes 393224 | tf_op jit(solution)/shard_map/ppermute | solution.py:495
  37.3 15.9 %collective-permute-start.14 = (bf16[2,2,128,128]{3,2,1,0:T(8,128)(2,1)S(1)}, bf16[2,2,128,128]{3,2,1,0:T(8,128)(2,1)S(1)}, u32[]{:S(2)}, u32[]{:S(2)}) collective-permute-start(bf16[2,2,128,128]{3,2,1,0:T(8,128)(2,1)S(1)} %get-tuple-element.67), channel_id=1, source_target_pairs={{4,0},{6,2},{12,8},{14,10},{5,1},{7,3},{13,9},{15,11},{20,16},{22,... | collective-permute-start | bytes 393224 | tf_op jit(solution)/shard_map/ppermute | solution.py:495
  41.1 19.4 %collective-permute-start.10 = (bf16[128,640]{1,0:T(8,128)(2,1)S(1)}, bf16[128,640]{1,0:T(8,128)(2,1)S(1)}, u32[]{:S(2)}, u32[]{:S(2)}) collective-permute-start(bf16[128,640]{1,0:T(8,128)(2,1)S(1)} %get-tuple-element.61), channel_id=1, source_target_pairs={{0,2},{2,0},{4,6},{6,4},{8,10},{10,8},{12,14},{14,12},{1,3},{3,1},... | collective-permute-start | bytes 491528 | tf_op jit(solution)/shard_map/ppermute | solution.py:495
  46.2 8.8 %collective-permute-start.16 = (bf16[2,2,128,128]{3,2,1,0:T(8,128)(2,1)S(1)}, bf16[2,2,128,128]{3,2,1,0:T(8,128)(2,1)S(1)}, u32[]{:S(2)}, u32[]{:S(2)}) collective-permute-start(bf16[2,2,128,128]{3,2,1,0:T(8,128)(2,1)S(1)} %get-tuple-element.70), channel_id=1, source_target_pairs={{8,4},{10,6},{12,0},{14,2},{9,5},{11,7},{13,1},{15,3},{24,20},{26,... | collective-permute-start | bytes 393224 | tf_op jit(solution)/shard_map/ppermute | solution.py:495
  47.5 11.1 %collective-permute-start.17 = (bf16[2,2,128,128]{3,2,1,0:T(8,128)(2,1)S(1)}, bf16[2,2,128,128]{3,2,1,0:T(8,128)(2,1)S(1)}, u32[]{:S(2)}, u32[]{:S(2)}) collective-permute-start(bf16[2,2,128,128]{3,2,1,0:T(8,128)(2,1)S(1)} %get-tuple-element.71), channel_id=1, source_target_pairs={{8,0},{10,2},{12,4},{14,6},{9,1},{11,3},{13,5},{15,7},{24,16},{26,... | collective-permute-start | bytes 393224 | tf_op jit(solution)/shard_map/ppermute | solution.py:495
  52.0 7.9 %collective-permute-start.18 = (bf16[2,2,128,128]{3,2,1,0:T(8,128)(2,1)S(1)}, bf16[2,2,128,128]{3,2,1,0:T(8,128)(2,1)S(1)}, u32[]{:S(2)}, u32[]{:S(2)}) collective-permute-start(bf16[2,2,128,128]{3,2,1,0:T(8,128)(2,1)S(1)} %get-tuple-element.72), channel_id=1, source_target_pairs={{4,0},{6,2},{12,8},{14,10},{5,1},{7,3},{13,9},{15,11},{20,16},{22,... | collective-permute-start | bytes 393224 | tf_op jit(solution)/shard_map/ppermute | solution.py:495
  53.3 8.6 %collective-permute-start.15 = (bf16[2,128,128]{2,1,0:T(8,128)(2,1)S(1)}, bf16[2,128,128]{2,1,0:T(8,128)(2,1)S(1)}, u32[]{:S(2)}, u32[]{:S(2)}) collective-permute-start(bf16[2,128,128]{2,1,0:T(8,128)(2,1)S(1)} %fusion), channel_id=1, source_target_pairs={{0,2},{2,0},{4,6},{6,4},{8,10},{10,8},{12,14},{14,12},{1,3},{3,1},... | collective-permute-start | bytes 196616 | tf_op jit(solution)/shard_map/ppermute | solution.py:495
  54.9 6.0 %collective-permute-start.11 = (bf16[128,640]{1,0:T(8,128)(2,1)S(1)}, bf16[128,640]{1,0:T(8,128)(2,1)S(1)}, u32[]{:S(2)}, u32[]{:S(2)}) collective-permute-start(bf16[128,640]{1,0:T(8,128)(2,1)S(1)} %get-tuple-element.62), channel_id=1, source_target_pairs={{0,2},{2,0},{4,6},{6,4},{8,10},{10,8},{12,14},{14,12},{1,3},{3,1},... | collective-permute-start | bytes 491528 | tf_op jit(solution)/shard_map/ppermute | solution.py:495
  59.9 4.3 %collective-permute-start.19 = (bf16[2,128,128]{2,1,0:T(8,128)(2,1)S(1)}, bf16[2,128,128]{2,1,0:T(8,128)(2,1)S(1)}, u32[]{:S(2)}, u32[]{:S(2)}) collective-permute-start(bf16[2,128,128]{2,1,0:T(8,128)(2,1)S(1)} %fusion.1), channel_id=1, source_target_pairs={{0,2},{2,0},{4,6},{6,4},{8,10},{10,8},{12,14},{14,12},{1,3},{3,1},... | collective-permute-start | bytes 196616 | tf_op jit(solution)/shard_map/ppermute | solution.py:495

commit v18 on v13

--- a/solution.py
+++ b/solution.py
@@ -536,7 +536,7 @@
     for dkv in dkv_list:
         arrived = [permute(dkv[bits], meet[bits]) for bits in steps[::-1]]
         summands.append([after(dkv[0], dq_own[-1])] + arrived)
-    dq_back = [permute(after(block, dq_own[-1]), swap) for block in dq_back]
+    dq_back = [permute(block, swap) for block in dq_back]
     others = []
     for blocks in summands:
         total = sum(block[1].astype(jnp.float32) for block in blocks)

time: 62.1 us -> 63.2 us (1.018)
  waiting for transfers between devices: 15.4 us -> 19.2 us
  starting transfers between devices: 28.5 us -> 25.7 us
    ppermute x20, waiting for transfers between devices: 15.4 us -> 19.2 us  [permute(): return lax.ppermute(array, 'seg', pairs)]
    ppermute x20, starting transfers between devices: 28.5 us -> 25.7 us  [permute(): return lax.ppermute(array, 'seg', pairs)]
  transfers between devices with their start and end apart: 20 -> 20, of which waited for: 7 -> 8; matrix products, arithmetic and copies ran while one was open for 0% -> 0% of each run, Pallas kernels for 19% -> 19%
where the time goes in v18:
time: 63.2 us; the launch traced here: 62.9 us
  starting transfers between devices  25.7 us (41%)
  waiting for transfers between devices  19.2 us (30%)
  Pallas kernels  14.5 us (23%)
  local copies, waits for them, and re-layouts  2.62 us (4%)
  between operations  0.74 us (1%)
    ppermute x20, starting transfers between devices, permute(): return lax.ppermute(array, 'seg', pairs)  25.7 us
    ppermute x20, waiting for transfers between devices, permute(): return lax.ppermute(array, 'seg', pairs)  19.2 us
    pallas_call x2, Pallas kernels, attend(): pl.pallas_call(functools.partial(attend_kernel, DEPTH, segs, steps, group...  8.85 us
    unnamed x12, local copies, waits for them, and re-layouts  2.62 us
    pallas_call x1, Pallas kernels, pack(): pl.pallas_call(functools.partial(pack_kernel, log_rate, parts), out_shape...  1.81 us
  transfers between devices with their start and end apart: 20, of which 8 were waited for; matrix products, arithmetic and copies ran while one was open for 0% of the time, Pallas kernels for 19%

profile of v18, /device:TPU:0, one launch (start us, length us, event | category | flops | bytes accessed | tf_op | source)
XLA Modules:
  0.0 62.9 jit_solution(7383762706636944119)
XLA Ops:
  0.6 1.8 %pack_keys_values.1 = (bf16[272,128]{1,0:T(8,128)(2,1)}, bf16[256,128]{1,0:T(8,128)(2,1)}, bf16[272,128]{1,0:T(8,128)(2,1)}, bf16[256,128]{1,0:T(8,128)(2,1)}) custom-call(s32[8]{0:T(128)} %lengths_s.1, bf16[128,512]{1,0:T(8,128)(2,1)} %k_ref.1, bf16[128,512]{1,0:T(8,128)(2,1)} %v_ref.1, f32[1,128]{1,0:T(1,128)} %bitcast.9, f32[1,128]{1,0:T(1,128)} %bitcast.10, ...), custom_call_target="tpu_custom_call" | custom-call | flops 12800 | bytes 524288 | tf_op jit(solution)/shard_map/pack_keys_values/pallas_call | solution.py:104
  2.4 2.9 %collective-permute-start = (bf16[272,128]{1,0:T(8,128)(2,1)}, bf16[272,128]{1,0:T(8,128)(2,1)S(1)}, u32[]{:S(2)}, u32[]{:S(2)}) collective-permute-start(bf16[272,128]{1,0:T(8,128)(2,1)} %get-tuple-element.41), channel_id=1, source_target_pairs={{0,2},{2,0},{4,6},{6,4},{8,10},{10,8},{12,14},{14,12},{1,3},{3,1},... | collective-permute-start | bytes 208904 | tf_op jit(solution)/shard_map/ppermute | solution.py:495
  5.4 0.1 collective-permute-start.3
  5.5 0.0 copy-start
  5.5 1.1 %copy-done = bf16[128,2560]{1,0:T(8,128)(2,1)S(1)} copy-done((bf16[128,2560]{1,0:T(8,128)(2,1)S(1)}, bf16[128,2560]{1,0:T(8,128)(2,1)}, u32[]{:S(2)}) %copy-start) | copy-done | bytes 655384
  6.5 0.0 copy-start.1
  6.5 1.1 %copy-done.1 = bf16[128,2560]{1,0:T(8,128)(2,1)S(1)} copy-done((bf16[128,2560]{1,0:T(8,128)(2,1)S(1)}, bf16[128,2560]{1,0:T(8,128)(2,1)}, u32[]{:S(2)}) %copy-start.1) | copy-done | bytes 655384
  7.6 0.0 copy-start.2
  7.6 0.2 pack_queries.1
  7.9 0.2 collective-permute-done.refs_1_.other_ref
  8.1 0.4 copy-done.2
  8.5 0.0 copy-start.3
  8.5 2.2 %collective-permute-start.1 = (bf16[544,128]{1,0:T(8,128)(2,1)S(1)}, bf16[544,128]{1,0:T(8,128)(2,1)S(1)}, u32[]{:S(2)}, u32[]{:S(2)}) collective-permute-start(bf16[544,128]{1,0:T(8,128)(2,1)S(1)} %join_blocks.2.refs_0_.refs_5_), channel_id=1, source_target_pairs={{0,4},{2,6},{4,0},{6,2},{8,12},{10,14},{12,8},{14,10},{1,5},{3,7},... | collective-permute-start | bytes 417800 | tf_op jit(solution)/shard_map/ppermute | solution.py:495
  10.7 2.6 %collective-permute-start.2 = (bf16[544,128]{1,0:T(8,128)(2,1)S(1)}, bf16[544,128]{1,0:T(8,128)(2,1)S(1)}, u32[]{:S(2)}, u32[]{:S(2)}) collective-permute-start(bf16[544,128]{1,0:T(8,128)(2,1)S(1)} %join_blocks.2.refs_0_.refs_5_), channel_id=1, source_target_pairs={{0,8},{2,10},{4,12},{6,14},{8,0},{10,2},{12,4},{14,6},{1,9},{3,11}... | collective-permute-start | bytes 417800 | tf_op jit(solution)/shard_map/ppermute | solution.py:495
  13.3 0.0 collective-permute-done.3.other_ref
  13.3 0.0 copy-done.3
  13.4 0.0 copy-start.4
  13.4 0.0 copy-start.5
  13.4 1.4 %collective-permute-start.5 = (bf16[2,5,128,128]{3,2,1,0:T(8,128)(2,1)S(1)}, bf16[2,5,128,128]{3,2,1,0:T(8,128)(2,1)S(1)}, u32[]{:S(2)}, u32[]{:S(2)}) collective-permute-start(bf16[2,5,128,128]{3,2,1,0:T(8,128)(2,1)S(1)} %get-tuple-element.54), channel_id=1, source_target_pairs={{0,2},{2,0},{4,6},{6,4},{8,10},{10,8},{12,14},{14,12},{1,3},{3,1},... | collective-permute-start | bytes 983048 | tf_op jit(solution)/shard_map/ppermute | solution.py:495
  14.8 0.0 copy-done.4
  14.8 0.0 copy-done.5
  14.8 1.2 %prepare.1 = (f32[2,640,128]{2,1,0:T(8,128)S(1)}, f32[2,3,128,128]{3,2,1,0:T(8,128)S(1)}, f32[2,2,8,128]{3,2,1,0:T(8,128)S(1)}) custom-call(s32[8]{0:T(128)S(1)} %copy-done.5, s32[8]{0:T(128)S(1)} %copy-done.4, bf16[272,128]{1,0:T(8,128)(2,1)S(1)} %copy-done.2, bf16[272,128]{1,0:T(8,128)(2,1)S(1)} %collective-permute-done.refs_1_.other_ref), custom_call_target="tpu_custom_call" | custom-call | flops 3276800 | bytes 655360 | tf_op jit(solution)/shard_map/prepare/pallas_call | solution.py:253
  16.1 0.0 collective-permute-done.1.refs_1_.refs_6_
  16.1 3.2 %collective-permute-done.2.refs_2_.refs_7_ = bf16[544,128]{1,0:T(8,128)(2,1)S(1)} collective-permute-done((bf16[544,128]{1,0:T(8,128)(2,1)S(1)}, bf16[544,128]{1,0:T(8,128)(2,1)S(1)}, u32[]{:S(2)}, u32[]{:S(2)}) %collective-permute-start.2) | collective-permute-done | bytes 139296 | tf_op jit(solution)/shard_map/ppermute | solution.py:495
  19.2 0.2 collective-permute-start.4
  19.5 4.8 %collective-permute-done.4.refs_3_.refs_8_ = bf16[544,128]{1,0:T(8,128)(2,1)S(1)} collective-permute-done((bf16[544,128]{1,0:T(8,128)(2,1)S(1)}, bf16[544,128]{1,0:T(8,128)(2,1)S(1)}, u32[]{:S(2)}, u32[]{:S(2)}) %collective-permute-start.4) | collective-permute-done | bytes 139296 | tf_op jit(solution)/shard_map/ppermute | solution.py:495
  24.3 2.6 %collective-permute-start.6 = (bf16[2,5,128,128]{3,2,1,0:T(8,128)(2,1)S(1)}, bf16[2,5,128,128]{3,2,1,0:T(8,128)(2,1)S(1)}, u32[]{:S(2)}, u32[]{:S(2)}) collective-permute-start(bf16[2,5,128,128]{3,2,1,0:T(8,128)(2,1)S(1)} %get-tuple-element.57), channel_id=1, source_target_pairs={{0,2},{2,0},{4,6},{6,4},{8,10},{10,8},{12,14},{14,12},{1,3},{3,1},... | collective-permute-start | bytes 983048 | tf_op jit(solution)/shard_map/ppermute | solution.py:495
  26.9 0.0 collective-permute-done.5.refs_4_
  26.9 0.0 collective-permute-start.8
  26.9 0.7 %advantages.1 = (f32[1,128]{1,0:T(1,128)}, f32[2,128,128]{2,1,0:T(8,128)S(1)}) custom-call(f32[2,3,128,128]{3,2,1,0:T(8,128)S(1)} %get-tuple-element.42.columns_ref, f32[2,2,8,128]{3,2,1,0:T(8,128)S(1)} %get-tuple-element.43.weights_ref, bf16[544,128]{1,0:T(8,128)(2,1)S(1)} %join_blocks.2.refs_0_.refs_5_, ...), custom_call_target="tpu_custom_call" | custom-call | flops 327680 | bytes 524288 | tf_op jit(solution)/shard_map/advantages/pallas_call | solution.py:306
  27.6 2.0 %collective-permute-start.7 = (bf16[512,128]{1,0:T(8,128)(2,1)S(1)}, bf16[512,128]{1,0:T(8,128)(2,1)S(1)}, u32[]{:S(2)}, u32[]{:S(2)}) collective-permute-start(bf16[512,128]{1,0:T(8,128)(2,1)S(1)} %join_blocks.3.refs_5_), channel_id=1, source_target_pairs={{0,4},{2,6},{4,0},{6,2},{8,12},{10,14},{12,8},{14,10},{1,5},{3,7},... | collective-permute-start | bytes 393224 | tf_op jit(solution)/shard_map/ppermute | solution.py:495
  29.5 4.4 %tree_attention_backward.2 = (bf16[128,640]{1,0:T(8,128)(2,1)S(1)}, bf16[128,640]{1,0:T(8,128)(2,1)S(1)}, bf16[2,2,128,128]{3,2,1,0:T(8,128)(2,1)S(1)}, bf16[2,2...) custom-call(s32[8]{0:T(128)S(1)} %copy-done.5, ...), custom_call_target="tpu_custom_call" | custom-call | flops 1048576000 | bytes 8388608 | tf_op jit(solution)/shard_map/tree_attention_backward/pallas_call | solution.py:409
  33.9 0.0 collective-permute-done.8.refs_7_
  33.9 0.1 collective-permute-start.9
  34.1 2.0 %collective-permute-start.14 = (bf16[2,2,128,128]{3,2,1,0:T(8,128)(2,1)S(1)}, bf16[2,2,128,128]{3,2,1,0:T(8,128)(2,1)S(1)}, u32[]{:S(2)}, u32[]{:S(2)}) collective-permute-start(bf16[2,2,128,128]{3,2,1,0:T(8,128)(2,1)S(1)} %get-tuple-element.67), channel_id=1, source_target_pairs={{0,4},{2,6},{4,0},{6,2},{8,12},{10,14},{12,8},{14,10},{1,5},{3,7},... | collective-permute-start | bytes 393224 | tf_op jit(solution)/shard_map/ppermute | solution.py:495
  36.0 1.0 %collective-permute-start.13 = (bf16[2,2,128,128]{3,2,1,0:T(8,128)(2,1)S(1)}, bf16[2,2,128,128]{3,2,1,0:T(8,128)(2,1)S(1)}, u32[]{:S(2)}, u32[]{:S(2)}) collective-permute-start(bf16[2,2,128,128]{3,2,1,0:T(8,128)(2,1)S(1)} %get-tuple-element.66), channel_id=1, source_target_pairs={{0,8},{2,10},{4,12},{6,14},{8,0},{10,2},{12,4},{14,6},{1,9},{3,11}... | collective-permute-start | bytes 393224 | tf_op jit(solution)/shard_map/ppermute | solution.py:495
  37.1 0.0 collective-permute-done.7.refs_6_
  37.1 1.9 %collective-permute-start.12 = (bf16[2,2,128,128]{3,2,1,0:T(8,128)(2,1)S(1)}, bf16[2,2,128,128]{3,2,1,0:T(8,128)(2,1)S(1)}, u32[]{:S(2)}, u32[]{:S(2)}) collective-permute-start(bf16[2,2,128,128]{3,2,1,0:T(8,128)(2,1)S(1)} %get-tuple-element.65), channel_id=1, source_target_pairs={{0,12},{2,14},{4,8},{6,10},{8,4},{10,6},{12,0},{14,2},{1,13},{3,15... | collective-permute-start | bytes 393224 | tf_op jit(solution)/shard_map/ppermute | solution.py:495
  38.9 3.4 %collective-permute-done.9.refs_8_ = bf16[512,128]{1,0:T(8,128)(2,1)S(1)} collective-permute-done((bf16[512,128]{1,0:T(8,128)(2,1)S(1)}, bf16[512,128]{1,0:T(8,128)(2,1)S(1)}, u32[]{:S(2)}, u32[]{:S(2)}) %collective-permute-start.9) | collective-permute-done | bytes 131104 | tf_op jit(solution)/shard_map/ppermute | solution.py:495
  42.3 0.0 collective-permute-start.10
  42.4 0.0 collective-permute-done.6.refs_4_
  42.4 4.4 %tree_attention_backward.3 = (bf16[128,640]{1,0:T(8,128)(2,1)S(1)}, bf16[128,640]{1,0:T(8,128)(2,1)S(1)}, bf16[2,2,128,128]{3,2,1,0:T(8,128)(2,1)S(1)}, bf16[2,2...) custom-call(s32[8]{0:T(128)S(1)} %copy-done.5, ...), custom_call_target="tpu_custom_call" | custom-call | flops 1048576000 | bytes 8388608 | tf_op jit(solution)/shard_map/tree_attention_backward/pallas_call | solution.py:409
  46.8 2.1 %collective-permute-start.11 = (bf16[128,640]{1,0:T(8,128)(2,1)S(1)}, bf16[128,640]{1,0:T(8,128)(2,1)S(1)}, u32[]{:S(2)}, u32[]{:S(2)}) collective-permute-start(bf16[128,640]{1,0:T(8,128)(2,1)S(1)} %get-tuple-element.62), channel_id=1, source_target_pairs={{0,2},{2,0},{4,6},{6,4},{8,10},{10,8},{12,14},{14,12},{1,3},{3,1},... | collective-permute-start | bytes 491528 | tf_op jit(solution)/shard_map/ppermute | solution.py:495
  48.9 0.0 collective-permute-done.14.refs_5_
  48.9 0.0 collective-permute-start.18
  48.9 0.0 collective-permute-done.13.refs_4_
  48.9 0.1 collective-permute-start.17
  49.0 0.0 collective-permute-done.12.refs_3_
  49.0 4.3 %collective-permute-start.16 = (bf16[2,2,128,128]{3,2,1,0:T(8,128)(2,1)S(1)}, bf16[2,2,128,128]{3,2,1,0:T(8,128)(2,1)S(1)}, u32[]{:S(2)}, u32[]{:S(2)}) collective-permute-start(bf16[2,2,128,128]{3,2,1,0:T(8,128)(2,1)S(1)} %get-tuple-element.70), channel_id=1, source_target_pairs={{0,12},{2,14},{4,8},{6,10},{8,4},{10,6},{12,0},{14,2},{1,13},{3,15... | collective-permute-start | bytes 393224 | tf_op jit(solution)/shard_map/ppermute | solution.py:495
  53.3 1.9 %collective-permute-done.18.refs_9_ = bf16[2,2,128,128]{3,2,1,0:T(8,128)(2,1)S(1)} collective-permute-done((bf16[2,2,128,128]{3,2,1,0:T(8,128)(2,1)S(1)}, bf16[2,2,128,128]{3,2,1,0:T(8,128)(2,1)S(1)}, u32[]{:S(2)}, u32[]{:S(2)}) %collective-permute-start.18) | collective-permute-done | bytes 131104 | tf_op jit(solution)/shard_map/ppermute | solution.py:495
  55.2 0.1 collective-permute-start.15
  55.3 0.0 collective-permute-done.17.refs_8_
  55.3 2.4 %collective-permute-done.16.refs_7_ = bf16[2,2,128,128]{3,2,1,0:T(8,128)(2,1)S(1)} collective-permute-done((bf16[2,2,128,128]{3,2,1,0:T(8,128)(2,1)S(1)}, bf16[2,2,128,128]{3,2,1,0:T(8,128)(2,1)S(1)}, u32[]{:S(2)}, u32[]{:S(2)}) %collective-permute-start.16) | collective-permute-done | bytes 131104 | tf_op jit(solution)/shard_map/ppermute | solution.py:495
  57.8 0.2 collective-permute-start.19
  57.9 0.0 collective-permute-done.10.refs_2_
  57.9 0.0 collective-permute-done.11.refs_3_
  57.9 0.9 %join_queries.1 = bf16[128,2560]{1,0:T(8,128)(2,1)} custom-call(bf16[128,640]{1,0:T(8,128)(2,1)S(1)} %get-tuple-element.55.refs_0_, bf16[128,640]{1,0:T(8,128)(2,1)S(1)} %get-tuple-element.60.refs_1_, bf16[128,640]{1,0:T(8,128)(2,1)S(1)} %collective-permute-done.10.refs_2_, bf16[128,640]{1,0:T(8,128)(2,1)S(1)} %collective-permute-done.11.refs_3_), custom_call_target="tpu_custom_call" | custom-call | bytes 1310720 | tf_op jit(solution)/shard_map/join_queries/pallas_call | solution.py:447
  58.8 0.7 %collective-permute-done.15.refs_0_ = bf16[2,128,128]{2,1,0:T(8,128)(2,1)S(1)} collective-permute-done((bf16[2,128,128]{2,1,0:T(8,128)(2,1)S(1)}, bf16[2,128,128]{2,1,0:T(8,128)(2,1)S(1)}, u32[]{:S(2)}, u32[]{:S(2)}) %collective-permute-start.15) | collective-permute-done | bytes 65568 | tf_op jit(solution)/shard_map/ppermute | solution.py:495
  59.5 2.6 %collective-permute-done.19.refs_1_ = bf16[2,128,128]{2,1,0:T(8,128)(2,1)S(1)} collective-permute-done((bf16[2,128,128]{2,1,0:T(8,128)(2,1)S(1)}, bf16[2,128,128]{2,1,0:T(8,128)(2,1)S(1)}, u32[]{:S(2)}, u32[]{:S(2)}) %collective-permute-start.19) | collective-permute-done | bytes 65568 | tf_op jit(solution)/shard_map/ppermute | solution.py:495
  62.1 0.8 %join_keys.1 = (bf16[128,512]{1,0:T(8,128)(2,1)}, bf16[128,512]{1,0:T(8,128)(2,1)}) custom-call(bf16[2,128,128]{2,1,0:T(8,128)(2,1)S(1)} %collective-permute-done.15.refs_0_, bf16[2,128,128]{2,1,0:T(8,128)(2,1)S(1)} %collective-permute-done.19.refs_1_, bf16[2,2,128,128]{3,2,1,0:T(8,128)(2,1)S(1)} %get-tuple-element.64.refs_2_, ...), custom_call_target="tpu_custom_call" | custom-call | bytes 524288 | tf_op jit(solution)/shard_map/join_keys/pallas_call | solution.py:481
  (4 shorter events, 0.1 us)
Async XLA Ops:
  2.4 5.6 %collective-permute-start = (bf16[272,128]{1,0:T(8,128)(2,1)}, bf16[272,128]{1,0:T(8,128)(2,1)S(1)}, u32[]{:S(2)}, u32[]{:S(2)}) collective-permute-start(bf16[272,128]{1,0:T(8,128)(2,1)} %get-tuple-element.41), channel_id=1, source_target_pairs={{0,2},{2,0},{4,6},{6,4},{8,10},{10,8},{12,14},{14,12},{1,3},{3,1},... | collective-permute-start | bytes 208904 | tf_op jit(solution)/shard_map/ppermute | solution.py:495
  5.4 8.0 %collective-permute-start.3 = (bf16[256,128]{1,0:T(8,128)(2,1)}, bf16[256,128]{1,0:T(8,128)(2,1)S(1)}, u32[]{:S(2)}, u32[]{:S(2)}) collective-permute-start(bf16[256,128]{1,0:T(8,128)(2,1)} %get-tuple-element.49), channel_id=1, source_target_pairs={{0,2},{2,0},{4,6},{6,4},{8,10},{10,8},{12,14},{14,12},{1,3},{3,1},... | collective-permute-start | bytes 196616 | tf_op jit(solution)/shard_map/ppermute | solution.py:495
  5.5 1.1 %copy-start = (bf16[128,2560]{1,0:T(8,128)(2,1)S(1)}, bf16[128,2560]{1,0:T(8,128)(2,1)}, u32[]{:S(2)}) copy-start(bf16[128,2560]{1,0:T(8,128)(2,1)} %q_ref) | copy-start | bytes 1966084
  6.5 1.1 %copy-start.1 = (bf16[128,2560]{1,0:T(8,128)(2,1)S(1)}, bf16[128,2560]{1,0:T(8,128)(2,1)}, u32[]{:S(2)}) copy-start(bf16[128,2560]{1,0:T(8,128)(2,1)} %dir_ref.1) | copy-start | bytes 1966084
  7.6 0.9 %copy-start.2 = (bf16[272,128]{1,0:T(8,128)(2,1)S(1)}, bf16[272,128]{1,0:T(8,128)(2,1)}, u32[]{:S(2)}) copy-start(bf16[272,128]{1,0:T(8,128)(2,1)} %get-tuple-element.40.refs_0_.mine_ref) | copy-start | bytes 208900
  8.5 4.8 %copy-start.3 = (bf16[256,128]{1,0:T(8,128)(2,1)S(1)}, bf16[256,128]{1,0:T(8,128)(2,1)}, u32[]{:S(2)}) copy-start(bf16[256,128]{1,0:T(8,128)(2,1)} %get-tuple-element.48.mine_ref) | copy-start | bytes 196612
  8.5 7.5 %collective-permute-start.1 = (bf16[544,128]{1,0:T(8,128)(2,1)S(1)}, bf16[544,128]{1,0:T(8,128)(2,1)S(1)}, u32[]{:S(2)}, u32[]{:S(2)}) collective-permute-start(bf16[544,128]{1,0:T(8,128)(2,1)S(1)} %join_blocks.2.refs_0_.refs_5_), channel_id=1, source_target_pairs={{0,4},{2,6},{4,0},{6,2},{8,12},{10,14},{12,8},{14,10},{1,5},{3,7},... | collective-permute-start | bytes 417800 | tf_op jit(solution)/shard_map/ppermute | solution.py:495
  10.7 8.5 %collective-permute-start.2 = (bf16[544,128]{1,0:T(8,128)(2,1)S(1)}, bf16[544,128]{1,0:T(8,128)(2,1)S(1)}, u32[]{:S(2)}, u32[]{:S(2)}) collective-permute-start(bf16[544,128]{1,0:T(8,128)(2,1)S(1)} %join_blocks.2.refs_0_.refs_5_), channel_id=1, source_target_pairs={{0,8},{2,10},{4,12},{6,14},{8,0},{10,2},{12,4},{14,6},{1,9},{3,11}... | collective-permute-start | bytes 417800 | tf_op jit(solution)/shard_map/ppermute | solution.py:495
  13.4 1.5 %copy-start.4 = (s32[8]{0:T(128)S(1)}, s32[8]{0:T(128)}, u32[]{:S(2)}) copy-start(s32[8]{0:T(128)} %lengths_s.1) | copy-start | bytes 100
  13.4 1.5 %copy-start.5 = (s32[8]{0:T(128)S(1)}, s32[8]{0:T(128)}, u32[]{:S(2)}) copy-start(s32[8]{0:T(128)} %refs_0_.3) | copy-start | bytes 100
  13.4 13.5 %collective-permute-start.5 = (bf16[2,5,128,128]{3,2,1,0:T(8,128)(2,1)S(1)}, bf16[2,5,128,128]{3,2,1,0:T(8,128)(2,1)S(1)}, u32[]{:S(2)}, u32[]{:S(2)}) collective-permute-start(bf16[2,5,128,128]{3,2,1,0:T(8,128)(2,1)S(1)} %get-tuple-element.54), channel_id=1, source_target_pairs={{0,2},{2,0},{4,6},{6,4},{8,10},{10,8},{12,14},{14,12},{1,3},{3,1},... | collective-permute-start | bytes 983048 | tf_op jit(solution)/shard_map/ppermute | solution.py:495
  19.2 5.1 %collective-permute-start.4 = (bf16[544,128]{1,0:T(8,128)(2,1)S(1)}, bf16[544,128]{1,0:T(8,128)(2,1)S(1)}, u32[]{:S(2)}, u32[]{:S(2)}) collective-permute-start(bf16[544,128]{1,0:T(8,128)(2,1)S(1)} %collective-permute-done.2.refs_2_.refs_7_), channel_id=1, source_target_pairs={{0,4},{2,6},{4,0},{6,2},{8,12},{10,14},{12,8},{14,10},{1,5},{3,7},... | collective-permute-start | bytes 417800 | tf_op jit(solution)/shard_map/ppermute | solution.py:495
  24.3 18.1 %collective-permute-start.6 = (bf16[2,5,128,128]{3,2,1,0:T(8,128)(2,1)S(1)}, bf16[2,5,128,128]{3,2,1,0:T(8,128)(2,1)S(1)}, u32[]{:S(2)}, u32[]{:S(2)}) collective-permute-start(bf16[2,5,128,128]{3,2,1,0:T(8,128)(2,1)S(1)} %get-tuple-element.57), channel_id=1, source_target_pairs={{0,2},{2,0},{4,6},{6,4},{8,10},{10,8},{12,14},{14,12},{1,3},{3,1},... | collective-permute-start | bytes 983048 | tf_op jit(solution)/shard_map/ppermute | solution.py:495
  26.9 7.1 %collective-permute-start.8 = (bf16[512,128]{1,0:T(8,128)(2,1)S(1)}, bf16[512,128]{1,0:T(8,128)(2,1)S(1)}, u32[]{:S(2)}, u32[]{:S(2)}) collective-permute-start(bf16[512,128]{1,0:T(8,128)(2,1)S(1)} %join_blocks.3.refs_5_), channel_id=1, source_target_pairs={{0,8},{2,10},{4,12},{6,14},{8,0},{10,2},{12,4},{14,6},{1,9},{3,11}... | collective-permute-start | bytes 393224 | tf_op jit(solution)/shard_map/ppermute | solution.py:495
  27.6 9.5 %collective-permute-start.7 = (bf16[512,128]{1,0:T(8,128)(2,1)S(1)}, bf16[512,128]{1,0:T(8,128)(2,1)S(1)}, u32[]{:S(2)}, u32[]{:S(2)}) collective-permute-start(bf16[512,128]{1,0:T(8,128)(2,1)S(1)} %join_blocks.3.refs_5_), channel_id=1, source_target_pairs={{0,4},{2,6},{4,0},{6,2},{8,12},{10,14},{12,8},{14,10},{1,5},{3,7},... | collective-permute-start | bytes 393224 | tf_op jit(solution)/shard_map/ppermute | solution.py:495
  33.9 8.4 %collective-permute-start.9 = (bf16[512,128]{1,0:T(8,128)(2,1)S(1)}, bf16[512,128]{1,0:T(8,128)(2,1)S(1)}, u32[]{:S(2)}, u32[]{:S(2)}) collective-permute-start(bf16[512,128]{1,0:T(8,128)(2,1)S(1)} %collective-permute-done.8.refs_7_), channel_id=1, source_target_pairs={{0,4},{2,6},{4,0},{6,2},{8,12},{10,14},{12,8},{14,10},{1,5},{3,7},... | collective-permute-start | bytes 393224 | tf_op jit(solution)/shard_map/ppermute | solution.py:495
  34.1 14.8 %collective-permute-start.14 = (bf16[2,2,128,128]{3,2,1,0:T(8,128)(2,1)S(1)}, bf16[2,2,128,128]{3,2,1,0:T(8,128)(2,1)S(1)}, u32[]{:S(2)}, u32[]{:S(2)}) collective-permute-start(bf16[2,2,128,128]{3,2,1,0:T(8,128)(2,1)S(1)} %get-tuple-element.67), channel_id=1, source_target_pairs={{0,4},{2,6},{4,0},{6,2},{8,12},{10,14},{12,8},{14,10},{1,5},{3,7},... | collective-permute-start | bytes 393224 | tf_op jit(solution)/shard_map/ppermute | solution.py:495
  36.0 12.8 %collective-permute-start.13 = (bf16[2,2,128,128]{3,2,1,0:T(8,128)(2,1)S(1)}, bf16[2,2,128,128]{3,2,1,0:T(8,128)(2,1)S(1)}, u32[]{:S(2)}, u32[]{:S(2)}) collective-permute-start(bf16[2,2,128,128]{3,2,1,0:T(8,128)(2,1)S(1)} %get-tuple-element.66), channel_id=1, source_target_pairs={{0,8},{2,10},{4,12},{6,14},{8,0},{10,2},{12,4},{14,6},{1,9},{3,11}... | collective-permute-start | bytes 393224 | tf_op jit(solution)/shard_map/ppermute | solution.py:495
  37.1 11.9 %collective-permute-start.12 = (bf16[2,2,128,128]{3,2,1,0:T(8,128)(2,1)S(1)}, bf16[2,2,128,128]{3,2,1,0:T(8,128)(2,1)S(1)}, u32[]{:S(2)}, u32[]{:S(2)}) collective-permute-start(bf16[2,2,128,128]{3,2,1,0:T(8,128)(2,1)S(1)} %get-tuple-element.65), channel_id=1, source_target_pairs={{0,12},{2,14},{4,8},{6,10},{8,4},{10,6},{12,0},{14,2},{1,13},{3,15... | collective-permute-start | bytes 393224 | tf_op jit(solution)/shard_map/ppermute | solution.py:495
  42.3 15.6 %collective-permute-start.10 = (bf16[128,640]{1,0:T(8,128)(2,1)S(1)}, bf16[128,640]{1,0:T(8,128)(2,1)S(1)}, u32[]{:S(2)}, u32[]{:S(2)}) collective-permute-start(bf16[128,640]{1,0:T(8,128)(2,1)S(1)} %get-tuple-element.61), channel_id=1, source_target_pairs={{0,2},{2,0},{4,6},{6,4},{8,10},{10,8},{12,14},{14,12},{1,3},{3,1},... | collective-permute-start | bytes 491528 | tf_op jit(solution)/shard_map/ppermute | solution.py:495
  46.8 11.1 %collective-permute-start.11 = (bf16[128,640]{1,0:T(8,128)(2,1)S(1)}, bf16[128,640]{1,0:T(8,128)(2,1)S(1)}, u32[]{:S(2)}, u32[]{:S(2)}) collective-permute-start(bf16[128,640]{1,0:T(8,128)(2,1)S(1)} %get-tuple-element.62), channel_id=1, source_target_pairs={{0,2},{2,0},{4,6},{6,4},{8,10},{10,8},{12,14},{14,12},{1,3},{3,1},... | collective-permute-start | bytes 491528 | tf_op jit(solution)/shard_map/ppermute | solution.py:495
  48.9 6.4 %collective-permute-start.18 = (bf16[2,2,128,128]{3,2,1,0:T(8,128)(2,1)S(1)}, bf16[2,2,128,128]{3,2,1,0:T(8,128)(2,1)S(1)}, u32[]{:S(2)}, u32[]{:S(2)}) collective-permute-start(bf16[2,2,128,128]{3,2,1,0:T(8,128)(2,1)S(1)} %get-tuple-element.72), channel_id=1, source_target_pairs={{0,4},{2,6},{4,0},{6,2},{8,12},{10,14},{12,8},{14,10},{1,5},{3,7},... | collective-permute-start | bytes 393224 | tf_op jit(solution)/shard_map/ppermute | solution.py:495
  48.9 6.5 %collective-permute-start.17 = (bf16[2,2,128,128]{3,2,1,0:T(8,128)(2,1)S(1)}, bf16[2,2,128,128]{3,2,1,0:T(8,128)(2,1)S(1)}, u32[]{:S(2)}, u32[]{:S(2)}) collective-permute-start(bf16[2,2,128,128]{3,2,1,0:T(8,128)(2,1)S(1)} %get-tuple-element.71), channel_id=1, source_target_pairs={{0,8},{2,10},{4,12},{6,14},{8,0},{10,2},{12,4},{14,6},{1,9},{3,11}... | collective-permute-start | bytes 393224 | tf_op jit(solution)/shard_map/ppermute | solution.py:495
  49.0 8.7 %collective-permute-start.16 = (bf16[2,2,128,128]{3,2,1,0:T(8,128)(2,1)S(1)}, bf16[2,2,128,128]{3,2,1,0:T(8,128)(2,1)S(1)}, u32[]{:S(2)}, u32[]{:S(2)}) collective-permute-start(bf16[2,2,128,128]{3,2,1,0:T(8,128)(2,1)S(1)} %get-tuple-element.70), channel_id=1, source_target_pairs={{0,12},{2,14},{4,8},{6,10},{8,4},{10,6},{12,0},{14,2},{1,13},{3,15... | collective-permute-start | bytes 393224 | tf_op jit(solution)/shard_map/ppermute | solution.py:495
  55.2 4.3 %collective-permute-start.15 = (bf16[2,128,128]{2,1,0:T(8,128)(2,1)S(1)}, bf16[2,128,128]{2,1,0:T(8,128)(2,1)S(1)}, u32[]{:S(2)}, u32[]{:S(2)}) collective-permute-start(bf16[2,128,128]{2,1,0:T(8,128)(2,1)S(1)} %fusion), channel_id=1, source_target_pairs={{0,2},{2,0},{4,6},{6,4},{8,10},{10,8},{12,14},{14,12},{1,3},{3,1},... | collective-permute-start | bytes 196616 | tf_op jit(solution)/shard_map/ppermute | solution.py:495
  57.8 4.3 %collective-permute-start.19 = (bf16[2,128,128]{2,1,0:T(8,128)(2,1)S(1)}, bf16[2,128,128]{2,1,0:T(8,128)(2,1)S(1)}, u32[]{:S(2)}, u32[]{:S(2)}) collective-permute-start(bf16[2,128,128]{2,1,0:T(8,128)(2,1)S(1)} %fusion.1), channel_id=1, source_target_pairs={{0,2},{2,0},{4,6},{6,4},{8,10},{10,8},{12,14},{14,12},{1,3},{3,1},... | collective-permute-start | bytes 196616 | tf_op jit(solution)/shard_map/ppermute | solution.py:495

commit v19 on v14

--- a/solution.py
+++ b/solution.py
@@ -536,7 +536,7 @@
     for dkv in dkv_list:
         arrived = [permute(dkv[bits], meet[bits]) for bits in steps[::-1]]
         summands.append([after(dkv[0], dq_own[-1])] + arrived)
-    dq_back = [permute(block, swap) for block in dq_back]
+    dq_back = [permute(after(block, dq_own[-1]), swap) for block in dq_back]
     others = []
     for blocks in summands:
         total = sum(block[1].astype(jnp.float32) for block in blocks)

time: 63.4 us -> 63.4 us (level)
  starting transfers between devices: 24.3 us -> 25 us
  waiting for transfers between devices: 20.5 us -> 19.8 us
    ppermute x20, starting transfers between devices: 24.3 us -> 25 us  [permute(): return lax.ppermute(array, 'seg', pairs)]
    ppermute x20, waiting for transfers between devices: 20.5 us -> 19.8 us  [permute(): return lax.ppermute(array, 'seg', pairs)]
  transfers between devices with their start and end apart: 20 -> 20, of which waited for: 10 -> 9; matrix products, arithmetic and copies ran while one was open for 0% -> 0% of each run, Pallas kernels for 19% -> 19%
where the time goes in v19:
time: 63.4 us; the launch traced here: 63.2 us
  starting transfers between devices  25 us (39%)
  waiting for transfers between devices  19.8 us (31%)
  Pallas kernels  14.5 us (23%)
  local copies, waits for them, and re-layouts  3.05 us (5%)
  between operations  0.74 us (1%)
    ppermute x20, starting transfers between devices, permute(): return lax.ppermute(array, 'seg', pairs)  25 us
    ppermute x20, waiting for transfers between devices, permute(): return lax.ppermute(array, 'seg', pairs)  19.8 us
    pallas_call x2, Pallas kernels, attend(): pl.pallas_call(functools.partial(attend_kernel, DEPTH, segs, steps, group...  8.85 us
    unnamed x12, local copies, waits for them, and re-layouts  3.05 us
    pallas_call x1, Pallas kernels, pack(): pl.pallas_call(functools.partial(pack_kernel, log_rate, parts), out_shape...  1.81 us
  transfers between devices with their start and end apart: 20, of which 9 were waited for; matrix products, arithmetic and copies ran while one was open for 0% of the time, Pallas kernels for 19%

profile of v19, /device:TPU:0, one launch (start us, length us, event | category | flops | bytes accessed | tf_op | source)
XLA Modules:
  0.0 63.2 jit_solution(2151058612755642063)
XLA Ops:
  0.6 1.8 %pack_keys_values.1 = (bf16[272,128]{1,0:T(8,128)(2,1)}, bf16[256,128]{1,0:T(8,128)(2,1)}, bf16[272,128]{1,0:T(8,128)(2,1)}, bf16[256,128]{1,0:T(8,128)(2,1)}) custom-call(s32[8]{0:T(128)} %lengths_s.1, bf16[128,512]{1,0:T(8,128)(2,1)} %k_ref.1, bf16[128,512]{1,0:T(8,128)(2,1)} %v_ref.1, f32[1,128]{1,0:T(1,128)} %bitcast.9, f32[1,128]{1,0:T(1,128)} %bitcast.10, ...), custom_call_target="tpu_custom_call" | custom-call | flops 12800 | bytes 524288 | tf_op jit(solution)/shard_map/pack_keys_values/pallas_call | solution.py:104
  2.4 2.9 %collective-permute-start = (bf16[272,128]{1,0:T(8,128)(2,1)}, bf16[272,128]{1,0:T(8,128)(2,1)S(1)}, u32[]{:S(2)}, u32[]{:S(2)}) collective-permute-start(bf16[272,128]{1,0:T(8,128)(2,1)} %get-tuple-element.43), channel_id=1, source_target_pairs={{0,2},{2,0},{4,6},{6,4},{8,10},{10,8},{12,14},{14,12},{1,3},{3,1},... | collective-permute-start | bytes 208904 | tf_op jit(solution)/shard_map/ppermute | solution.py:495
  5.4 0.1 collective-permute-start.3
  5.5 0.0 copy-start
  5.5 1.1 %copy-done = bf16[128,2560]{1,0:T(8,128)(2,1)S(1)} copy-done((bf16[128,2560]{1,0:T(8,128)(2,1)S(1)}, bf16[128,2560]{1,0:T(8,128)(2,1)}, u32[]{:S(2)}) %copy-start) | copy-done | bytes 655384
  6.5 0.0 copy-start.1
  6.5 1.1 %copy-done.1 = bf16[128,2560]{1,0:T(8,128)(2,1)S(1)} copy-done((bf16[128,2560]{1,0:T(8,128)(2,1)S(1)}, bf16[128,2560]{1,0:T(8,128)(2,1)}, u32[]{:S(2)}) %copy-start.1) | copy-done | bytes 655384
  7.6 0.0 copy-start.3
  7.6 0.2 pack_queries.1
  7.9 2.0 %collective-permute-done.3.other_ref = bf16[256,128]{1,0:T(8,128)(2,1)S(1)} collective-permute-done((bf16[256,128]{1,0:T(8,128)(2,1)}, bf16[256,128]{1,0:T(8,128)(2,1)S(1)}, u32[]{:S(2)}, u32[]{:S(2)}) %collective-permute-start.3) | collective-permute-done | bytes 65568 | tf_op jit(solution)/shard_map/ppermute | solution.py:495
  9.9 0.0 copy-done.3
  9.9 0.0 copy-start.2
  9.9 0.0 collective-permute-done.refs_1_.other_ref
  9.9 0.9 %copy-done.2 = bf16[272,128]{1,0:T(8,128)(2,1)S(1)} copy-done((bf16[272,128]{1,0:T(8,128)(2,1)S(1)}, bf16[272,128]{1,0:T(8,128)(2,1)}, u32[]{:S(2)}) %copy-start.2) | copy-done | bytes 69656
  10.8 0.0 copy-start.4
  10.8 0.0 copy-start.5
  10.8 1.1 %collective-permute-start.5 = (bf16[2,5,128,128]{3,2,1,0:T(8,128)(2,1)S(1)}, bf16[2,5,128,128]{3,2,1,0:T(8,128)(2,1)S(1)}, u32[]{:S(2)}, u32[]{:S(2)}) collective-permute-start(bf16[2,5,128,128]{3,2,1,0:T(8,128)(2,1)S(1)} %get-tuple-element.56), channel_id=1, source_target_pairs={{0,2},{2,0},{4,6},{6,4},{8,10},{10,8},{12,14},{14,12},{1,3},{3,1},... | collective-permute-start | bytes 983048 | tf_op jit(solution)/shard_map/ppermute | solution.py:495
  11.9 1.6 %collective-permute-start.1 = (bf16[544,128]{1,0:T(8,128)(2,1)S(1)}, bf16[544,128]{1,0:T(8,128)(2,1)S(1)}, u32[]{:S(2)}, u32[]{:S(2)}) collective-permute-start(bf16[544,128]{1,0:T(8,128)(2,1)S(1)} %join_blocks.2.refs_0_.refs_5_), channel_id=1, source_target_pairs={{0,4},{2,6},{4,0},{6,2},{8,12},{10,14},{12,8},{14,10},{1,5},{3,7},... | collective-permute-start | bytes 417800 | tf_op jit(solution)/shard_map/ppermute | solution.py:495
  13.5 2.6 %collective-permute-start.2 = (bf16[544,128]{1,0:T(8,128)(2,1)S(1)}, bf16[544,128]{1,0:T(8,128)(2,1)S(1)}, u32[]{:S(2)}, u32[]{:S(2)}) collective-permute-start(bf16[544,128]{1,0:T(8,128)(2,1)S(1)} %join_blocks.2.refs_0_.refs_5_), channel_id=1, source_target_pairs={{0,8},{2,10},{4,12},{6,14},{8,0},{10,2},{12,4},{14,6},{1,9},{3,11}... | collective-permute-start | bytes 417800 | tf_op jit(solution)/shard_map/ppermute | solution.py:495
  16.1 0.0 copy-done.4
  16.1 0.0 copy-done.5
  16.1 1.2 %prepare.1 = (f32[2,640,128]{2,1,0:T(8,128)S(1)}, f32[2,3,128,128]{3,2,1,0:T(8,128)S(1)}, f32[2,2,8,128]{3,2,1,0:T(8,128)S(1)}) custom-call(s32[8]{0:T(128)S(1)} %copy-done.5, s32[8]{0:T(128)S(1)} %copy-done.4, bf16[272,128]{1,0:T(8,128)(2,1)S(1)} %copy-done.2, bf16[272,128]{1,0:T(8,128)(2,1)S(1)} %collective-permute-done.refs_1_.other_ref), custom_call_target="tpu_custom_call" | custom-call | flops 3276800 | bytes 655360 | tf_op jit(solution)/shard_map/prepare/pallas_call | solution.py:253
  17.3 1.5 %collective-permute-done.1.refs_1_.refs_6_ = bf16[544,128]{1,0:T(8,128)(2,1)S(1)} collective-permute-done((bf16[544,128]{1,0:T(8,128)(2,1)S(1)}, bf16[544,128]{1,0:T(8,128)(2,1)S(1)}, u32[]{:S(2)}, u32[]{:S(2)}) %collective-permute-start.1) | collective-permute-done | bytes 139296 | tf_op jit(solution)/shard_map/ppermute | solution.py:495
  18.8 2.7 %collective-permute-done.2.refs_2_.refs_7_ = bf16[544,128]{1,0:T(8,128)(2,1)S(1)} collective-permute-done((bf16[544,128]{1,0:T(8,128)(2,1)S(1)}, bf16[544,128]{1,0:T(8,128)(2,1)S(1)}, u32[]{:S(2)}, u32[]{:S(2)}) %collective-permute-start.2) | collective-permute-done | bytes 139296 | tf_op jit(solution)/shard_map/ppermute | solution.py:495
  21.5 0.4 collective-permute-start.4
  21.8 0.0 collective-permute-done.5.refs_4_
  21.8 1.3 %collective-permute-start.6 = (bf16[2,5,128,128]{3,2,1,0:T(8,128)(2,1)S(1)}, bf16[2,5,128,128]{3,2,1,0:T(8,128)(2,1)S(1)}, u32[]{:S(2)}, u32[]{:S(2)}) collective-permute-start(bf16[2,5,128,128]{3,2,1,0:T(8,128)(2,1)S(1)} %get-tuple-element.59), channel_id=1, source_target_pairs={{0,2},{2,0},{4,6},{6,4},{8,10},{10,8},{12,14},{14,12},{1,3},{3,1},... | collective-permute-start | bytes 983048 | tf_op jit(solution)/shard_map/ppermute | solution.py:495
  23.2 2.7 %collective-permute-start.8 = (bf16[512,128]{1,0:T(8,128)(2,1)S(1)}, bf16[512,128]{1,0:T(8,128)(2,1)S(1)}, u32[]{:S(2)}, u32[]{:S(2)}) collective-permute-start(bf16[512,128]{1,0:T(8,128)(2,1)S(1)} %join_blocks.3.refs_5_), channel_id=1, source_target_pairs={{0,8},{2,10},{4,12},{6,14},{8,0},{10,2},{12,4},{14,6},{1,9},{3,11}... | collective-permute-start | bytes 393224 | tf_op jit(solution)/shard_map/ppermute | solution.py:495
  25.9 0.0 collective-permute-start.7
  25.9 3.6 %collective-permute-done.4.refs_3_.refs_8_ = bf16[544,128]{1,0:T(8,128)(2,1)S(1)} collective-permute-done((bf16[544,128]{1,0:T(8,128)(2,1)S(1)}, bf16[544,128]{1,0:T(8,128)(2,1)S(1)}, u32[]{:S(2)}, u32[]{:S(2)}) %collective-permute-start.4) | collective-permute-done | bytes 139296 | tf_op jit(solution)/shard_map/ppermute | solution.py:495
  29.5 0.7 %advantages.1 = (f32[1,128]{1,0:T(1,128)}, f32[2,128,128]{2,1,0:T(8,128)S(1)}) custom-call(f32[2,3,128,128]{3,2,1,0:T(8,128)S(1)} %get-tuple-element.44.columns_ref, f32[2,2,8,128]{3,2,1,0:T(8,128)S(1)} %get-tuple-element.45.weights_ref, bf16[544,128]{1,0:T(8,128)(2,1)S(1)} %join_blocks.2.refs_0_.refs_5_, ...), custom_call_target="tpu_custom_call" | custom-call | flops 327680 | bytes 524288 | tf_op jit(solution)/shard_map/advantages/pallas_call | solution.py:306
  30.2 4.4 %tree_attention_backward.2 = (bf16[128,640]{1,0:T(8,128)(2,1)S(1)}, bf16[128,640]{1,0:T(8,128)(2,1)S(1)}, bf16[2,2,128,128]{3,2,1,0:T(8,128)(2,1)S(1)}, bf16[2,2...) custom-call(s32[8]{0:T(128)S(1)} %copy-done.5, ...), custom_call_target="tpu_custom_call" | custom-call | flops 1048576000 | bytes 8388608 | tf_op jit(solution)/shard_map/tree_attention_backward/pallas_call | solution.py:409
  34.6 0.0 collective-permute-done.8.refs_7_
  34.6 0.1 collective-permute-start.9
  34.7 2.3 %collective-permute-start.12 = (bf16[2,2,128,128]{3,2,1,0:T(8,128)(2,1)S(1)}, bf16[2,2,128,128]{3,2,1,0:T(8,128)(2,1)S(1)}, u32[]{:S(2)}, u32[]{:S(2)}) collective-permute-start(bf16[2,2,128,128]{3,2,1,0:T(8,128)(2,1)S(1)} %get-tuple-element.69), channel_id=1, source_target_pairs={{0,12},{2,14},{4,8},{6,10},{8,4},{10,6},{12,0},{14,2},{1,13},{3,15... | collective-permute-start | bytes 393224 | tf_op jit(solution)/shard_map/ppermute | solution.py:495
  37.1 1.1 %collective-permute-start.13 = (bf16[2,2,128,128]{3,2,1,0:T(8,128)(2,1)S(1)}, bf16[2,2,128,128]{3,2,1,0:T(8,128)(2,1)S(1)}, u32[]{:S(2)}, u32[]{:S(2)}) collective-permute-start(bf16[2,2,128,128]{3,2,1,0:T(8,128)(2,1)S(1)} %get-tuple-element.70), channel_id=1, source_target_pairs={{0,8},{2,10},{4,12},{6,14},{8,0},{10,2},{12,4},{14,6},{1,9},{3,11}... | collective-permute-start | bytes 393224 | tf_op jit(solution)/shard_map/ppermute | solution.py:495
  38.2 0.0 collective-permute-done.7.refs_6_
  38.2 1.0 %collective-permute-start.14 = (bf16[2,2,128,128]{3,2,1,0:T(8,128)(2,1)S(1)}, bf16[2,2,128,128]{3,2,1,0:T(8,128)(2,1)S(1)}, u32[]{:S(2)}, u32[]{:S(2)}) collective-permute-start(bf16[2,2,128,128]{3,2,1,0:T(8,128)(2,1)S(1)} %get-tuple-element.71), channel_id=1, source_target_pairs={{0,4},{2,6},{4,0},{6,2},{8,12},{10,14},{12,8},{14,10},{1,5},{3,7},... | collective-permute-start | bytes 393224 | tf_op jit(solution)/shard_map/ppermute | solution.py:495
  39.2 0.5 collective-permute-done.9.refs_8_
  39.7 0.0 collective-permute-done.6.refs_4_
  39.7 4.4 %tree_attention_backward.3 = (bf16[128,640]{1,0:T(8,128)(2,1)S(1)}, bf16[128,640]{1,0:T(8,128)(2,1)S(1)}, bf16[2,2,128,128]{3,2,1,0:T(8,128)(2,1)S(1)}, bf16[2,2...) custom-call(s32[8]{0:T(128)S(1)} %copy-done.5, ...), custom_call_target="tpu_custom_call" | custom-call | flops 1048576000 | bytes 8388608 | tf_op jit(solution)/shard_map/tree_attention_backward/pallas_call | solution.py:409
  44.1 2.3 %collective-permute-start.16 = (bf16[2,2,128,128]{3,2,1,0:T(8,128)(2,1)S(1)}, bf16[2,2,128,128]{3,2,1,0:T(8,128)(2,1)S(1)}, u32[]{:S(2)}, u32[]{:S(2)}) collective-permute-start(bf16[2,2,128,128]{3,2,1,0:T(8,128)(2,1)S(1)} %get-tuple-element.74), channel_id=1, source_target_pairs={{0,12},{2,14},{4,8},{6,10},{8,4},{10,6},{12,0},{14,2},{1,13},{3,15... | collective-permute-start | bytes 393224 | tf_op jit(solution)/shard_map/ppermute | solution.py:495
  46.5 0.0 collective-permute-start.17
  46.5 0.0 collective-permute-done.12.refs_3_
  46.5 2.1 %collective-permute-start.18 = (bf16[2,2,128,128]{3,2,1,0:T(8,128)(2,1)S(1)}, bf16[2,2,128,128]{3,2,1,0:T(8,128)(2,1)S(1)}, u32[]{:S(2)}, u32[]{:S(2)}) collective-permute-start(bf16[2,2,128,128]{3,2,1,0:T(8,128)(2,1)S(1)} %get-tuple-element.76), channel_id=1, source_target_pairs={{0,4},{2,6},{4,0},{6,2},{8,12},{10,14},{12,8},{14,10},{1,5},{3,7},... | collective-permute-start | bytes 393224 | tf_op jit(solution)/shard_map/ppermute | solution.py:495
  48.6 4.9 %collective-permute-done.13.refs_4_ = bf16[2,2,128,128]{3,2,1,0:T(8,128)(2,1)S(1)} collective-permute-done((bf16[2,2,128,128]{3,2,1,0:T(8,128)(2,1)S(1)}, bf16[2,2,128,128]{3,2,1,0:T(8,128)(2,1)S(1)}, u32[]{:S(2)}, u32[]{:S(2)}) %collective-permute-start.13) | collective-permute-done | bytes 131104 | tf_op jit(solution)/shard_map/ppermute | solution.py:495
  53.5 0.0 collective-permute-done.14.refs_5_
  53.6 0.1 collective-permute-start.15
  53.7 2.0 %collective-permute-start.11 = (bf16[128,640]{1,0:T(8,128)(2,1)S(1)}, bf16[128,640]{1,0:T(8,128)(2,1)S(1)}, u32[]{:S(2)}, u32[]{:S(2)}) collective-permute-start(bf16[128,640]{1,0:T(8,128)(2,1)S(1)} %get-tuple-element.66), channel_id=1, source_target_pairs={{0,2},{2,0},{4,6},{6,4},{8,10},{10,8},{12,14},{14,12},{1,3},{3,1},... | collective-permute-start | bytes 491528 | tf_op jit(solution)/shard_map/ppermute | solution.py:495
  55.7 0.0 collective-permute-done.16.refs_7_
  55.7 0.1 collective-permute-start.10
  55.7 0.8 %collective-permute-done.17.refs_8_ = bf16[2,2,128,128]{3,2,1,0:T(8,128)(2,1)S(1)} collective-permute-done((bf16[2,2,128,128]{3,2,1,0:T(8,128)(2,1)S(1)}, bf16[2,2,128,128]{3,2,1,0:T(8,128)(2,1)S(1)}, u32[]{:S(2)}, u32[]{:S(2)}) %collective-permute-start.17) | collective-permute-done | bytes 131104 | tf_op jit(solution)/shard_map/ppermute | solution.py:495
  56.6 0.0 collective-permute-done.18.refs_9_
  56.6 1.2 %collective-permute-start.19 = (bf16[2,128,128]{2,1,0:T(8,128)(2,1)S(1)}, bf16[2,128,128]{2,1,0:T(8,128)(2,1)S(1)}, u32[]{:S(2)}, u32[]{:S(2)}) collective-permute-start(bf16[2,128,128]{2,1,0:T(8,128)(2,1)S(1)} %fusion.1), channel_id=1, source_target_pairs={{0,2},{2,0},{4,6},{6,4},{8,10},{10,8},{12,14},{14,12},{1,3},{3,1},... | collective-permute-start | bytes 196616 | tf_op jit(solution)/shard_map/ppermute | solution.py:495
  57.8 1.9 %collective-permute-done.11.refs_3_ = bf16[128,640]{1,0:T(8,128)(2,1)S(1)} collective-permute-done((bf16[128,640]{1,0:T(8,128)(2,1)S(1)}, bf16[128,640]{1,0:T(8,128)(2,1)S(1)}, u32[]{:S(2)}, u32[]{:S(2)}) %collective-permute-start.11) | collective-permute-done | bytes 163872 | tf_op jit(solution)/shard_map/ppermute | solution.py:495
  59.7 1.8 %collective-permute-done.10.refs_2_ = bf16[128,640]{1,0:T(8,128)(2,1)S(1)} collective-permute-done((bf16[128,640]{1,0:T(8,128)(2,1)S(1)}, bf16[128,640]{1,0:T(8,128)(2,1)S(1)}, u32[]{:S(2)}, u32[]{:S(2)}) %collective-permute-start.10) | collective-permute-done | bytes 163872 | tf_op jit(solution)/shard_map/ppermute | solution.py:495
  61.5 0.9 %join_queries.1 = bf16[128,2560]{1,0:T(8,128)(2,1)} custom-call(bf16[128,640]{1,0:T(8,128)(2,1)S(1)} %get-tuple-element.57.refs_0_, bf16[128,640]{1,0:T(8,128)(2,1)S(1)} %get-tuple-element.62.refs_1_, bf16[128,640]{1,0:T(8,128)(2,1)S(1)} %collective-permute-done.10.refs_2_, bf16[128,640]{1,0:T(8,128)(2,1)S(1)} %collective-permute-done.11.refs_3_), custom_call_target="tpu_custom_call" | custom-call | bytes 1310720 | tf_op jit(solution)/shard_map/join_queries/pallas_call | solution.py:447
  62.4 0.0 collective-permute-done.15.refs_0_
  62.4 0.0 collective-permute-done.19.refs_1_
  62.4 0.8 %join_keys.1 = (bf16[128,512]{1,0:T(8,128)(2,1)}, bf16[128,512]{1,0:T(8,128)(2,1)}) custom-call(bf16[2,128,128]{2,1,0:T(8,128)(2,1)S(1)} %collective-permute-done.15.refs_0_, bf16[2,128,128]{2,1,0:T(8,128)(2,1)S(1)} %collective-permute-done.19.refs_1_, bf16[2,2,128,128]{3,2,1,0:T(8,128)(2,1)S(1)} %get-tuple-element.68.refs_2_, ...), custom_call_target="tpu_custom_call" | custom-call | bytes 524288 | tf_op jit(solution)/shard_map/join_keys/pallas_call | solution.py:481
  (4 shorter events, 0.1 us)
Async XLA Ops:
  2.4 7.4 %collective-permute-start = (bf16[272,128]{1,0:T(8,128)(2,1)}, bf16[272,128]{1,0:T(8,128)(2,1)S(1)}, u32[]{:S(2)}, u32[]{:S(2)}) collective-permute-start(bf16[272,128]{1,0:T(8,128)(2,1)} %get-tuple-element.43), channel_id=1, source_target_pairs={{0,2},{2,0},{4,6},{6,4},{8,10},{10,8},{12,14},{14,12},{1,3},{3,1},... | collective-permute-start | bytes 208904 | tf_op jit(solution)/shard_map/ppermute | solution.py:495
  5.4 4.5 %collective-permute-start.3 = (bf16[256,128]{1,0:T(8,128)(2,1)}, bf16[256,128]{1,0:T(8,128)(2,1)S(1)}, u32[]{:S(2)}, u32[]{:S(2)}) collective-permute-start(bf16[256,128]{1,0:T(8,128)(2,1)} %get-tuple-element.51), channel_id=1, source_target_pairs={{0,2},{2,0},{4,6},{6,4},{8,10},{10,8},{12,14},{14,12},{1,3},{3,1},... | collective-permute-start | bytes 196616 | tf_op jit(solution)/shard_map/ppermute | solution.py:495
  5.5 1.1 %copy-start = (bf16[128,2560]{1,0:T(8,128)(2,1)S(1)}, bf16[128,2560]{1,0:T(8,128)(2,1)}, u32[]{:S(2)}) copy-start(bf16[128,2560]{1,0:T(8,128)(2,1)} %q_ref) | copy-start | bytes 1966084
  6.5 1.1 %copy-start.1 = (bf16[128,2560]{1,0:T(8,128)(2,1)S(1)}, bf16[128,2560]{1,0:T(8,128)(2,1)}, u32[]{:S(2)}) copy-start(bf16[128,2560]{1,0:T(8,128)(2,1)} %dir_ref.1) | copy-start | bytes 1966084
  7.6 2.2 %copy-start.3 = (bf16[256,128]{1,0:T(8,128)(2,1)S(1)}, bf16[256,128]{1,0:T(8,128)(2,1)}, u32[]{:S(2)}) copy-start(bf16[256,128]{1,0:T(8,128)(2,1)} %get-tuple-element.50.mine_ref) | copy-start | bytes 196612
  9.9 0.9 %copy-start.2 = (bf16[272,128]{1,0:T(8,128)(2,1)S(1)}, bf16[272,128]{1,0:T(8,128)(2,1)}, u32[]{:S(2)}) copy-start(bf16[272,128]{1,0:T(8,128)(2,1)} %get-tuple-element.42.refs_0_.mine_ref) | copy-start | bytes 208900
  10.8 5.3 %copy-start.4 = (s32[8]{0:T(128)S(1)}, s32[8]{0:T(128)}, u32[]{:S(2)}) copy-start(s32[8]{0:T(128)} %lengths_s.1) | copy-start | bytes 100
  10.8 5.3 %copy-start.5 = (s32[8]{0:T(128)S(1)}, s32[8]{0:T(128)}, u32[]{:S(2)}) copy-start(s32[8]{0:T(128)} %refs_0_.3) | copy-start | bytes 100
  10.8 11.1 %collective-permute-start.5 = (bf16[2,5,128,128]{3,2,1,0:T(8,128)(2,1)S(1)}, bf16[2,5,128,128]{3,2,1,0:T(8,128)(2,1)S(1)}, u32[]{:S(2)}, u32[]{:S(2)}) collective-permute-start(bf16[2,5,128,128]{3,2,1,0:T(8,128)(2,1)S(1)} %get-tuple-element.56), channel_id=1, source_target_pairs={{0,2},{2,0},{4,6},{6,4},{8,10},{10,8},{12,14},{14,12},{1,3},{3,1},... | collective-permute-start | bytes 983048 | tf_op jit(solution)/shard_map/ppermute | solution.py:495
  11.9 6.9 %collective-permute-start.1 = (bf16[544,128]{1,0:T(8,128)(2,1)S(1)}, bf16[544,128]{1,0:T(8,128)(2,1)S(1)}, u32[]{:S(2)}, u32[]{:S(2)}) collective-permute-start(bf16[544,128]{1,0:T(8,128)(2,1)S(1)} %join_blocks.2.refs_0_.refs_5_), channel_id=1, source_target_pairs={{0,4},{2,6},{4,0},{6,2},{8,12},{10,14},{12,8},{14,10},{1,5},{3,7},... | collective-permute-start | bytes 417800 | tf_op jit(solution)/shard_map/ppermute | solution.py:495
  13.5 8.0 %collective-permute-start.2 = (bf16[544,128]{1,0:T(8,128)(2,1)S(1)}, bf16[544,128]{1,0:T(8,128)(2,1)S(1)}, u32[]{:S(2)}, u32[]{:S(2)}) collective-permute-start(bf16[544,128]{1,0:T(8,128)(2,1)S(1)} %join_blocks.2.refs_0_.refs_5_), channel_id=1, source_target_pairs={{0,8},{2,10},{4,12},{6,14},{8,0},{10,2},{12,4},{14,6},{1,9},{3,11}... | collective-permute-start | bytes 417800 | tf_op jit(solution)/shard_map/ppermute | solution.py:495
  21.5 8.0 %collective-permute-start.4 = (bf16[544,128]{1,0:T(8,128)(2,1)S(1)}, bf16[544,128]{1,0:T(8,128)(2,1)S(1)}, u32[]{:S(2)}, u32[]{:S(2)}) collective-permute-start(bf16[544,128]{1,0:T(8,128)(2,1)S(1)} %collective-permute-done.2.refs_2_.refs_7_), channel_id=1, source_target_pairs={{0,4},{2,6},{4,0},{6,2},{8,12},{10,14},{12,8},{14,10},{1,5},{3,7},... | collective-permute-start | bytes 417800 | tf_op jit(solution)/shard_map/ppermute | solution.py:495
  21.8 17.8 %collective-permute-start.6 = (bf16[2,5,128,128]{3,2,1,0:T(8,128)(2,1)S(1)}, bf16[2,5,128,128]{3,2,1,0:T(8,128)(2,1)S(1)}, u32[]{:S(2)}, u32[]{:S(2)}) collective-permute-start(bf16[2,5,128,128]{3,2,1,0:T(8,128)(2,1)S(1)} %get-tuple-element.59), channel_id=1, source_target_pairs={{0,2},{2,0},{4,6},{6,4},{8,10},{10,8},{12,14},{14,12},{1,3},{3,1},... | collective-permute-start | bytes 983048 | tf_op jit(solution)/shard_map/ppermute | solution.py:495
  23.2 11.4 %collective-permute-start.8 = (bf16[512,128]{1,0:T(8,128)(2,1)S(1)}, bf16[512,128]{1,0:T(8,128)(2,1)S(1)}, u32[]{:S(2)}, u32[]{:S(2)}) collective-permute-start(bf16[512,128]{1,0:T(8,128)(2,1)S(1)} %join_blocks.3.refs_5_), channel_id=1, source_target_pairs={{0,8},{2,10},{4,12},{6,14},{8,0},{10,2},{12,4},{14,6},{1,9},{3,11}... | collective-permute-start | bytes 393224 | tf_op jit(solution)/shard_map/ppermute | solution.py:495
  25.9 12.3 %collective-permute-start.7 = (bf16[512,128]{1,0:T(8,128)(2,1)S(1)}, bf16[512,128]{1,0:T(8,128)(2,1)S(1)}, u32[]{:S(2)}, u32[]{:S(2)}) collective-permute-start(bf16[512,128]{1,0:T(8,128)(2,1)S(1)} %join_blocks.3.refs_5_), channel_id=1, source_target_pairs={{0,4},{2,6},{4,0},{6,2},{8,12},{10,14},{12,8},{14,10},{1,5},{3,7},... | collective-permute-start | bytes 393224 | tf_op jit(solution)/shard_map/ppermute | solution.py:495
  34.6 5.0 %collective-permute-start.9 = (bf16[512,128]{1,0:T(8,128)(2,1)S(1)}, bf16[512,128]{1,0:T(8,128)(2,1)S(1)}, u32[]{:S(2)}, u32[]{:S(2)}) collective-permute-start(bf16[512,128]{1,0:T(8,128)(2,1)S(1)} %collective-permute-done.8.refs_7_), channel_id=1, source_target_pairs={{0,4},{2,6},{4,0},{6,2},{8,12},{10,14},{12,8},{14,10},{1,5},{3,7},... | collective-permute-start | bytes 393224 | tf_op jit(solution)/shard_map/ppermute | solution.py:495
  34.7 11.7 %collective-permute-start.12 = (bf16[2,2,128,128]{3,2,1,0:T(8,128)(2,1)S(1)}, bf16[2,2,128,128]{3,2,1,0:T(8,128)(2,1)S(1)}, u32[]{:S(2)}, u32[]{:S(2)}) collective-permute-start(bf16[2,2,128,128]{3,2,1,0:T(8,128)(2,1)S(1)} %get-tuple-element.69), channel_id=1, source_target_pairs={{0,12},{2,14},{4,8},{6,10},{8,4},{10,6},{12,0},{14,2},{1,13},{3,15... | collective-permute-start | bytes 393224 | tf_op jit(solution)/shard_map/ppermute | solution.py:495
  37.1 16.5 %collective-permute-start.13 = (bf16[2,2,128,128]{3,2,1,0:T(8,128)(2,1)S(1)}, bf16[2,2,128,128]{3,2,1,0:T(8,128)(2,1)S(1)}, u32[]{:S(2)}, u32[]{:S(2)}) collective-permute-start(bf16[2,2,128,128]{3,2,1,0:T(8,128)(2,1)S(1)} %get-tuple-element.70), channel_id=1, source_target_pairs={{0,8},{2,10},{4,12},{6,14},{8,0},{10,2},{12,4},{14,6},{1,9},{3,11}... | collective-permute-start | bytes 393224 | tf_op jit(solution)/shard_map/ppermute | solution.py:495
  38.2 15.3 %collective-permute-start.14 = (bf16[2,2,128,128]{3,2,1,0:T(8,128)(2,1)S(1)}, bf16[2,2,128,128]{3,2,1,0:T(8,128)(2,1)S(1)}, u32[]{:S(2)}, u32[]{:S(2)}) collective-permute-start(bf16[2,2,128,128]{3,2,1,0:T(8,128)(2,1)S(1)} %get-tuple-element.71), channel_id=1, source_target_pairs={{0,4},{2,6},{4,0},{6,2},{8,12},{10,14},{12,8},{14,10},{1,5},{3,7},... | collective-permute-start | bytes 393224 | tf_op jit(solution)/shard_map/ppermute | solution.py:495
  44.1 11.5 %collective-permute-start.16 = (bf16[2,2,128,128]{3,2,1,0:T(8,128)(2,1)S(1)}, bf16[2,2,128,128]{3,2,1,0:T(8,128)(2,1)S(1)}, u32[]{:S(2)}, u32[]{:S(2)}) collective-permute-start(bf16[2,2,128,128]{3,2,1,0:T(8,128)(2,1)S(1)} %get-tuple-element.74), channel_id=1, source_target_pairs={{0,12},{2,14},{4,8},{6,10},{8,4},{10,6},{12,0},{14,2},{1,13},{3,15... | collective-permute-start | bytes 393224 | tf_op jit(solution)/shard_map/ppermute | solution.py:495
  46.5 10.1 %collective-permute-start.17 = (bf16[2,2,128,128]{3,2,1,0:T(8,128)(2,1)S(1)}, bf16[2,2,128,128]{3,2,1,0:T(8,128)(2,1)S(1)}, u32[]{:S(2)}, u32[]{:S(2)}) collective-permute-start(bf16[2,2,128,128]{3,2,1,0:T(8,128)(2,1)S(1)} %get-tuple-element.75), channel_id=1, source_target_pairs={{0,8},{2,10},{4,12},{6,14},{8,0},{10,2},{12,4},{14,6},{1,9},{3,11}... | collective-permute-start | bytes 393224 | tf_op jit(solution)/shard_map/ppermute | solution.py:495
  46.5 10.1 %collective-permute-start.18 = (bf16[2,2,128,128]{3,2,1,0:T(8,128)(2,1)S(1)}, bf16[2,2,128,128]{3,2,1,0:T(8,128)(2,1)S(1)}, u32[]{:S(2)}, u32[]{:S(2)}) collective-permute-start(bf16[2,2,128,128]{3,2,1,0:T(8,128)(2,1)S(1)} %get-tuple-element.76), channel_id=1, source_target_pairs={{0,4},{2,6},{4,0},{6,2},{8,12},{10,14},{12,8},{14,10},{1,5},{3,7},... | collective-permute-start | bytes 393224 | tf_op jit(solution)/shard_map/ppermute | solution.py:495
  53.6 8.8 %collective-permute-start.15 = (bf16[2,128,128]{2,1,0:T(8,128)(2,1)S(1)}, bf16[2,128,128]{2,1,0:T(8,128)(2,1)S(1)}, u32[]{:S(2)}, u32[]{:S(2)}) collective-permute-start(bf16[2,128,128]{2,1,0:T(8,128)(2,1)S(1)} %fusion), channel_id=1, source_target_pairs={{0,2},{2,0},{4,6},{6,4},{8,10},{10,8},{12,14},{14,12},{1,3},{3,1},... | collective-permute-start | bytes 196616 | tf_op jit(solution)/shard_map/ppermute | solution.py:495
  53.7 6.0 %collective-permute-start.11 = (bf16[128,640]{1,0:T(8,128)(2,1)S(1)}, bf16[128,640]{1,0:T(8,128)(2,1)S(1)}, u32[]{:S(2)}, u32[]{:S(2)}) collective-permute-start(bf16[128,640]{1,0:T(8,128)(2,1)S(1)} %get-tuple-element.66), channel_id=1, source_target_pairs={{0,2},{2,0},{4,6},{6,4},{8,10},{10,8},{12,14},{14,12},{1,3},{3,1},... | collective-permute-start | bytes 491528 | tf_op jit(solution)/shard_map/ppermute | solution.py:495
  55.7 5.8 %collective-permute-start.10 = (bf16[128,640]{1,0:T(8,128)(2,1)S(1)}, bf16[128,640]{1,0:T(8,128)(2,1)S(1)}, u32[]{:S(2)}, u32[]{:S(2)}) collective-permute-start(bf16[128,640]{1,0:T(8,128)(2,1)S(1)} %get-tuple-element.64), channel_id=1, source_target_pairs={{0,2},{2,0},{4,6},{6,4},{8,10},{10,8},{12,14},{14,12},{1,3},{3,1},... | collective-permute-start | bytes 491528 | tf_op jit(solution)/shard_map/ppermute | solution.py:495
  56.6 5.8 %collective-permute-start.19 = (bf16[2,128,128]{2,1,0:T(8,128)(2,1)S(1)}, bf16[2,128,128]{2,1,0:T(8,128)(2,1)S(1)}, u32[]{:S(2)}, u32[]{:S(2)}) collective-permute-start(bf16[2,128,128]{2,1,0:T(8,128)(2,1)S(1)} %fusion.1), channel_id=1, source_target_pairs={{0,2},{2,0},{4,6},{6,4},{8,10},{10,8},{12,14},{14,12},{1,3},{3,1},... | collective-permute-start | bytes 196616 | tf_op jit(solution)/shard_map/ppermute | solution.py:495
